TPU v7x, 32 devices: a whole 2x2x4 slice. The times are simulated.
32 devices in a mesh: seq: 4 (over z), tp: 4 (over x, core), dp: 2 (over y).
Axes of the slice: x: 2, y: 2, z: 4, core: 2. Of those that a mesh axis runs over, the one named last changes fastest.
Arguments:
- query_gate: bfloat16 [2, 1024, 4096], P('dp', 'seq', 'tp'), may hold values from -6 to 6
- key_gate: bfloat16 [2, 1024, 4096], P('dp', 'seq', 'tp'), may hold values from -6 to 6
- value_input: bfloat16 [2, 1024, 4096], P('dp', 'seq', 'tp'), may hold values from -6 to 6
- filter_taps: bfloat16 [4096, 128], P('tp'), may hold values from -0.5 to 0.5
- skip_gain: float32 [4096], P('tp'), may hold values from -1 to 1
- out_weight: bfloat16 [4096, 4096], P('tp', 'dp'), may hold values from -0.09375 to 0.09375
- cotangent: bfloat16 [2, 1024, 4096], P('dp', 'seq', 'tp'), may hold values from -6 to 6
Outputs:
- grad_query: bfloat16 [2, 1024, 4096], P('dp', 'seq', 'tp')
- grad_key: bfloat16 [2, 1024, 4096], P('dp', 'seq', 'tp')
- grad_value: bfloat16 [2, 1024, 4096], P('dp', 'seq', 'tp')
- grad_filter: float32 [4096, 128], P('tp')
- grad_skip: float32 [4096], P('tp')
- grad_weight: float32 [4096, 4096], P(('seq', 'dp'), 'tp')
All inputs are finite; a program needn't handle non-finite values.
Results may differ from a plain program's by a relative error of at most 0.0095.
Values may be sent and summed in bfloat16 or wider, within the bound.
No kernel may reach another device: no remote copies, remote signals or barrier semaphores. Data moves between devices by JAX's collectives and lax.ppermute only.
A program may use at most 192 MiB of HBM per device.

v0:
```python
import math

import jax
import jax.numpy as jnp
from jax import lax
from jax.sharding import PartitionSpec as P

block_rows = 16


def shifted(block, axis, distance):
    devices = range(lax.axis_size(axis))
    route = [(i - distance, i) for i in devices if i - distance in devices]
    return lax.ppermute(block, axis, route)


def taps_matrix(vector, row_count, col_count):
    channels, width_all = vector.shape
    tiled = jnp.tile(vector, (1, row_count + 1))
    skewed = tiled[:, : row_count * (width_all - 1)].reshape(channels, row_count, width_all - 1)
    return skewed[:, :, row_count - 1 : row_count - 1 + col_count]


def forward_table(filter_taps):
    channels, tap_count = filter_taps.shape
    padding = jnp.zeros((channels, block_rows), filter_taps.dtype)
    vector = jnp.concatenate([padding, filter_taps[:, ::-1], padding], axis=1)
    return taps_matrix(vector, block_rows, tap_count + block_rows)


def backward_table(filter_taps):
    channels, tap_count = filter_taps.shape
    before = jnp.zeros((channels, block_rows - 1), filter_taps.dtype)
    after = jnp.zeros((channels, block_rows + 1), filter_taps.dtype)
    vector = jnp.concatenate([before, filter_taps, after], axis=1)
    return taps_matrix(vector, block_rows, tap_count + block_rows)


def windows(extended, length, tap_count):
    pieces = []
    for shift_index in range(tap_count // block_rows + 1):
        lower = shift_index * block_rows
        pieces.append(
            extended[lower : lower + length].reshape(
                length // block_rows, block_rows, extended.shape[1]
            )
        )
    return jnp.concatenate(pieces, axis=1)


def lag_sums(blocks, tap_count):
    channels, row_count, col_count = blocks.shape
    flattened = blocks.reshape(channels, row_count * col_count)
    padded = jnp.concatenate([flattened, jnp.zeros((channels, row_count), blocks.dtype)], axis=1)
    diagonal = padded.reshape(channels, row_count, col_count + 1)[:, :, 1 : tap_count + 1]
    return jnp.sum(diagonal, axis=1)[:, ::-1]


def per_device(query_gate, key_gate, value_input, filter_taps, skip_gain, out_weight, cotangent):
    queries = query_gate[0]
    key_rows = key_gate[0]
    value_rows = value_input[0]
    length, channels = queries.shape
    tap_count = filter_taps.shape[1]
    seq_count = lax.axis_size("seq")
    replica_count = lax.axis_size("dp")
    norm_factor = 1.0 / math.sqrt(length * seq_count * replica_count)
    mixed = (key_rows.astype(jnp.float32) * value_rows.astype(jnp.float32)).astype(jnp.bfloat16)
    tail_rows = mixed[length - (tap_count - 1) :]
    prior = shifted(tail_rows, "seq", 1)
    extended = jnp.concatenate([jnp.zeros((1, channels), jnp.bfloat16), prior, mixed], axis=0)
    forward_windows = windows(extended, length, tap_count)
    conv = jnp.einsum(
        "cab,ibc->iac",
        forward_table(filter_taps),
        forward_windows,
        preferred_element_type=jnp.float32,
    ).reshape(length, channels)
    state = conv + skip_gain[None, :] * mixed.astype(jnp.float32)
    gated = (queries.astype(jnp.float32) * state).astype(jnp.bfloat16)
    full_cot = lax.all_gather(cotangent[0], "tp", axis=1, tiled=True)
    selected = full_cot
    grad_gated = lax.dot_general(
        selected,
        lax.all_gather(out_weight, "dp", axis=1, tiled=True),
        (((1,), (1,)), ((), ())),
        preferred_element_type=jnp.float32,
    )
    grad_query = (grad_gated * state).astype(jnp.bfloat16)
    signal = (grad_gated * queries.astype(jnp.float32)).astype(jnp.bfloat16)
    head_rows = signal[: tap_count - 1]
    later = shifted(head_rows, "seq", -1)
    signal_ext = jnp.concatenate([signal, later, jnp.zeros((1, channels), jnp.bfloat16)], axis=0)
    back = jnp.einsum(
        "cab,ibc->iac",
        backward_table(filter_taps),
        windows(signal_ext, length, tap_count),
        preferred_element_type=jnp.float32,
    ).reshape(length, channels)
    back = back + skip_gain[None, :] * signal.astype(jnp.float32)
    grad_key = (back * value_rows.astype(jnp.float32)).astype(jnp.bfloat16)
    grad_value = (back * key_rows.astype(jnp.float32)).astype(jnp.bfloat16)
    signal_blocks = signal.reshape(length // block_rows, block_rows, channels)
    blocks = jnp.einsum(
        "iac,ibc->cab", signal_blocks, forward_windows, preferred_element_type=jnp.float32
    )
    skip_term = jnp.sum(signal.astype(jnp.float32) * mixed.astype(jnp.float32), axis=0)
    filter_sum, skip_sum = lax.psum((lag_sums(blocks, tap_count), skip_term), ("seq", "dp"))
    selected = full_cot
    grad_weight = lax.psum_scatter(
        lax.dot_general(
            selected, gated, (((0,), (0,)), ((), ())), preferred_element_type=jnp.float32
        ),
        ("seq", "dp"),
        scatter_dimension=0,
        tiled=True,
    )
    return (
        grad_query[None],
        grad_key[None],
        grad_value[None],
        filter_sum * norm_factor,
        skip_sum * norm_factor,
        grad_weight * norm_factor,
    )


def solution(mesh):
    return jax.shard_map(
        per_device,
        mesh=mesh,
        in_specs=(
            P("dp", "seq", "tp"),
            P("dp", "seq", "tp"),
            P("dp", "seq", "tp"),
            P("tp", None),
            P("tp"),
            P("tp", "dp"),
            P("dp", "seq", "tp"),
        ),
        out_specs=(
            P("dp", "seq", "tp"),
            P("dp", "seq", "tp"),
            P("dp", "seq", "tp"),
            P("tp", None),
            P("tp"),
            P(("seq", "dp"), "tp"),
        ),
        check_vma=False,
    )
```

profile of v0, /device:TPU:0, one launch (start us, length us, event | category | flops | bytes accessed | tf_op | source)
XLA Modules:
  0.0 812.7 jit_solution(5226510006126013183)
XLA Ops:
  16.3 4.9 reshape.123
  21.3 6.7 slice.135
  28.0 12.7 %copy.91 = bf16[1024,16,144]{2,1,0:T(8,128)(2,1)} copy(bf16[1024,16,144]{0,2,1:T(8,128)(2,1)} %slice.135) | data formatting | bytes 9437184
  40.7 99.8 %all-gather.4.cloned.1.call-done = bf16[1024,4096]{1,0:T(8,128)(2,1)} async-done(((bf16[1024,2048]{1,0:T(8,128)(2,1)}), bf16[1024,4096]{1,0:T(8,128)(2,1)}) %all-gather.4.cloned.1.call-update) | async-done | bytes 8388624 | tf_op jit(solution)/shard_map/all_gather | solution.py:85
  140.5 7.5 fusion.8
  164.1 6.8 slice.120
  170.8 12.5 %copy.90 = bf16[1024,16,144]{2,1,0:T(8,128)(2,1)} copy(bf16[1024,16,144]{0,2,1:T(8,128)(2,1)} %slice.120) | data formatting | bytes 9437184
  196.6 5.8 copy.75
  202.4 5.7 copy.76
  208.1 5.7 copy.77
  213.8 5.7 copy.78
  238.4 35.9 %concatenate.45 = bf16[16,144,1024]{1,0,2:T(8,128)(2,1)} concatenate(bf16[16,16,1024]{1,0,2:T(8,128)(2,1)} %copy.74, bf16[16,16,1024]{1,0,2:T(8,128)(2,1)} %copy.75, bf16[16,16,1024]{1,0,2:T(8,128)(2,1)} %copy.76, bf16[16,16,1024]{1,0,2:T(8,128)(2,1)} %copy.77, bf16[16,16,1024]{1,0,2:T(8,128)(2,1)} %copy.78, bf16[16,16,1024]{1,0,2:T(8,128)(2,1)} %copy.79, ...), dimensions={1} | concatenate | bytes 9437184 | tf_op jit(solution)/shard_map/concatenate | solution.py:48
  274.3 11.3 %convolution_bitcast_fusion.1 = f32[16,16,1024]{1,0,2:T(8,128)} fusion(bf16[16,144,1024]{1,0,2:T(8,128)(2,1)} %concatenate.45, bf16[1024,16,144]{2,1,0:T(8,128)(2,1)} %copy.91), kind=kOutput, calls=%fused_computation.2 | convolution fusion | flops 75497472 | bytes 10485760 | tf_op jit(solution)/shard_map/cab,ibc->iac/dot_general | solution.py:94
  285.6 5.1 copy.85
  292.6 5.7 copy.62
  298.3 5.7 copy.63
  304.0 5.8 copy.64
  309.8 5.7 copy.65
  315.5 5.9 copy.66
  321.4 5.7 copy.67
  336.6 35.9 %concatenate.41 = bf16[16,144,1024]{1,0,2:T(8,128)(2,1)} concatenate(bf16[16,16,1024]{1,0,2:T(8,128)(2,1)} %copy.62, bf16[16,16,1024]{1,0,2:T(8,128)(2,1)} %copy.63, bf16[16,16,1024]{1,0,2:T(8,128)(2,1)} %copy.64, bf16[16,16,1024]{1,0,2:T(8,128)(2,1)} %copy.65, bf16[16,16,1024]{1,0,2:T(8,128)(2,1)} %copy.66, bf16[16,16,1024]{1,0,2:T(8,128)(2,1)} %copy.67, ...), dimensions={1} | concatenate | bytes 9437184 | tf_op jit(solution)/shard_map/concatenate | solution.py:48
  372.5 9.9 %fusion.29 = f32[1024,16,144]{2,1,0:T(8,128)} fusion(bf16[16,16,1024]{1,0,2:T(8,128)(2,1)} %copy.74, bf16[16,144,1024]{1,0,2:T(8,128)(2,1)} %concatenate.41), kind=kOutput, calls=%fused_computation.75 | convolution fusion | flops 75497472 | bytes 14680064 | tf_op jit(solution)/shard_map/iac,ibc->cab/dot_general | solution.py:104
  382.4 11.3 %convolution_bitcast_fusion.2 = f32[16,16,1024]{1,0,2:T(8,128)} fusion(bf16[16,144,1024]{1,0,2:T(8,128)(2,1)} %concatenate.41, bf16[1024,16,144]{2,1,0:T(8,128)(2,1)} %copy.90), kind=kOutput, calls=%fused_computation.3 | convolution fusion | flops 75497472 | bytes 10485760 | tf_op jit(solution)/shard_map/cab,ibc->iac/dot_general | solution.py:73
  393.7 5.1 copy.73
  398.8 15.0 %copy.87 = f32[1024,16,144]{0,2,1:T(8,128)} copy(f32[1024,16,144]{2,1,0:T(8,128)} %fusion.29) | data formatting | bytes 18874368 | tf_op jit(solution)/shard_map/iac,ibc->cab/dot_general | solution.py:104
  413.8 9.3 %concatenate.47 = f32[1024,2320]{0,1:T(8,128)} pad(f32[1024,2304]{0,1:T(8,128)} %bitcast.90, f32[]{:T(128)} %constant.4.clone.1), padding=0_0x0_16 | pad | bytes 18939908 | tf_op jit(solution)/shard_map/concatenate | solution.py:54
  423.1 10.3 %reshape.126 = f32[1024,16,145]{0,2,1:T(8,128)} reshape(f32[1024,2320]{0,1:T(8,128)} %concatenate.47) | data formatting | bytes 19005440 | tf_op jit(solution)/shard_map/reshape | solution.py:55
  433.4 5.5 slice_reduce_fusion
  447.5 8.1 convolution_bitcast_fusion
  455.7 19.0 %psum.15 = f32[1024]{0:T(1024)S(1)} all-reduce(f32[1024]{0:T(1024)S(1)} %get-tuple-element.24), channel_id=1, replica_groups=mesh['seq'=4,'tp'=4,'dp'=2] {'seq','dp'}, use_global_device_ids=true, to_apply=%region_3.0 | all-reduce | flops 1024 | bytes 8192 | tf_op jit(solution)/shard_map/psum | solution.py:108
  475.3 40.7 %all-reduce.3.cloned.1.call-done = f32[1024,128]{0,1:T(8,128)} async-done(((f32[1024,128]{0,1:T(8,128)}), f32[1024,128]{0,1:T(8,128)}) %all-reduce.3.cloned.1.call-update) | async-done | bytes 524304 | tf_op jit(solution)/shard_map/psum | solution.py:108
  518.1 283.9 %reduce-scatter.2.cloned.1.call-done = f32[512,1024]{0,1:T(8,128)} async-done(((f32[4096,1024]{0,1:T(8,128)}), f32[512,1024]{0,1:T(8,128)}) %reduce-scatter.2.cloned.1.call-update) | async-done | bytes 2097168 | tf_op jit(solution)/shard_map/reduce_scatter | solution.py:110
  (61 shorter events, 83.5 us)
Async XLA Ops:
  7.2 5.2 copy-start.3
  7.2 33.5 %all-gather.6.cloned.1.call-start = ((), (), s32[]{:S(2)}) async-start(), calls=%async_computation.4 | async-start | bytes 2621440 | tf_op jit(solution)/shard_map/all_gather | solution.py:81
  7.9 132.6 %all-gather.4.cloned.1.call-start = ((), (), s32[]{:S(2)}) async-start(), calls=%async_computation.1 | async-start | bytes 12582912 | tf_op jit(solution)/shard_map/all_gather | solution.py:85
  8.7 507.3 %all-reduce.3.cloned.1.call-start = ((), (), s32[]{:S(2)}) async-start(), calls=%async_computation.2 | async-start | bytes 1048576 | tf_op jit(solution)/shard_map/psum | solution.py:108
  28.0 112.5 %copy-start = (bf16[1,256,1024]{2,1,0:T(8,128)(2,1)S(1)}, bf16[1,256,1024]{2,1,0:T(8,128)(2,1)}, u32[]{:S(2)}) copy-start(bf16[1,256,1024]{2,1,0:T(8,128)(2,1)} %param.9) | copy-start | bytes 1572868
  28.0 112.5 %copy-start.1 = (bf16[1,256,1024]{2,1,0:T(8,128)(2,1)S(1)}, bf16[1,256,1024]{2,1,0:T(8,128)(2,1)}, u32[]{:S(2)}) copy-start(bf16[1,256,1024]{2,1,0:T(8,128)(2,1)} %param.8) | copy-start | bytes 1572868
  28.0 112.5 %copy-start.4 = (bf16[1,256,1024]{2,1,0:T(8,128)(2,1)S(1)}, bf16[1,256,1024]{2,1,0:T(8,128)(2,1)}, u32[]{:S(2)}) copy-start(bf16[1,256,1024]{2,1,0:T(8,128)(2,1)} %param.7) | copy-start | bytes 1572868
  148.7 45.0 %collective-permute-start.1 = (bf16[127,1024]{1,0:T(8,128)(2,1)}, bf16[127,1024]{1,0:T(8,128)(2,1)}, u32[]{:S(2)}, u32[]{:S(2)}) collective-permute-start(bf16[127,1024]{1,0:T(8,128)(2,1)} %slice.121), channel_id=1, source_target_pairs={{8,0},{16,8},{24,16},{9,1},{17,9},{25,17},{10,2},{18,10},{26,18},{... | collective-permute-start | bytes 780296 | tf_op jit(solution)/shard_map/ppermute | solution.py:14
  188.9 101.8 %collective-permute-start = (bf16[127,1024]{1,0:T(8,128)(2,1)}, bf16[127,1024]{1,0:T(8,128)(2,1)S(1)}, u32[]{:S(2)}, u32[]{:S(2)}) collective-permute-start(bf16[127,1024]{1,0:T(8,128)(2,1)} %slice.106), channel_id=1, source_target_pairs={{0,8},{8,16},{16,24},{1,9},{9,17},{17,25},{2,10},{10,18},{18,26},{... | collective-permute-start | bytes 780296 | tf_op jit(solution)/shard_map/ppermute | solution.py:14
  433.4 10.6 %copy-start.5 = (f32[1024]{0:T(1024)S(1)}, f32[1024]{0:T(1024)}, u32[]{:S(2)}) copy-start(f32[1024]{0:T(1024)} %param.11) | copy-start | bytes 12292
  443.7 358.3 %reduce-scatter.2.cloned.1.call-start = ((), (), s32[]{:S(2)}) async-start(), calls=%async_computation.3 | async-start | bytes 18874368 | tf_op jit(solution)/shard_map/reduce_scatter | solution.py:110
  444.0 3.5 copy-start.2
Sparse Core Ops, SparseCore 0:
  9.6 25.2 all-gather.5
  36.4 104.0 all-gather.3
  443.8 72.1 all-reduce.2
  520.1 281.8 reduce-scatter.1
where the time goes:
time: 824 us; the launch traced here: 813 us
  waiting for transfers between devices  426 us (52%)
  local copies, waits for them, and re-layouts  281 us (34%)
  matrix products  48 us (6%)
  blocking collectives  19 us (2%)
  other arithmetic  18.1 us (2%)
  between operations  14.4 us (2%)
    reduce_scatter x1, waiting for transfers between devices, per_device(): lax.psum_scatter(lax.dot_general(selected, gated, (((0,), (0,)), ((), ())...  284 us
    all_gather x1, waiting for transfers between devices, per_device(): lax.all_gather(out_weight, 'dp', axis=1, tiled=True)  99.8 us
    reshape x17, local copies, waits for them, and re-layouts, windows(): extended[lower:lower + length]  90.6 us
    concatenate x2, local copies, waits for them, and re-layouts, windows(): return jnp.concatenate(pieces, axis=1)  71.8 us
    psum x1, waiting for transfers between devices, per_device(): lax.psum((lag_sums(blocks, tap_count), skip_term), ('seq', 'dp'))  40.7 us
    unnamed x16, local copies, waits for them, and re-layouts  28.1 us
    psum x1, blocking collectives, per_device(): lax.psum((lag_sums(blocks, tap_count), skip_term), ('seq', 'dp'))  19 us
  transfers between devices with their start and end apart: 6, of which 3 were waited for; matrix products, arithmetic and copies ran while one was open for 22% of the time, Pallas kernels for 0%

commit v1 on v0

v1 whole, which is shorter than its diff:
```python
import math

import jax
import jax.numpy as jnp
import numpy as np
from jax import lax
from jax.sharding import PartitionSpec as P

high = lax.Precision.HIGH


def analysis_table(size, positions):
    half = size // 2
    omega = 2.0 * np.pi * (np.arange(half) + 0.5) / size
    angle = omega[:, None] * np.asarray(positions)[None, :]
    return np.concatenate([np.cos(angle), -np.sin(angle)], axis=0).astype(np.float32)


def transform(table, rows):
    return jnp.dot(
        table, rows.astype(jnp.float32), precision=high, preferred_element_type=jnp.float32
    )


def spectrum_product(left, right, conjugate_right):
    half = left.shape[0] // 2
    left_re, left_im = left[:half], left[half:]
    right_re, right_im = right[:half], right[half:]
    if conjugate_right:
        right_im = -right_im
    return jnp.concatenate(
        [left_re * right_re - left_im * right_im, left_re * right_im + left_im * right_re], axis=0
    )


def swap_pairs(value, axis, distance):
    count = lax.axis_size(axis)
    return lax.ppermute(value, axis, [(i, i ^ distance) for i in range(count)])


def sum_over(value, axis):
    distance = 1
    while distance < lax.axis_size(axis):
        own = value.astype(jnp.bfloat16)
        other = swap_pairs(own, axis, distance)
        value = own.astype(jnp.float32) + other.astype(jnp.float32)
        distance *= 2
    return value


def per_device(query_gate, key_gate, value_input, filter_taps, skip_gain, out_weight, cotangent):
    f32, bf16 = jnp.float32, jnp.bfloat16
    queries, key_rows, value_rows, cot = (
        query_gate[0],
        key_gate[0],
        value_input[0],
        cotangent[0],
    )
    length, channels = queries.shape
    taps = filter_taps.shape[1]
    n_seq, n_tp, n_dp = lax.axis_size("seq"), lax.axis_size("tp"), lax.axis_size("dp")
    subs = n_tp // n_dp
    me_tp, me_dp = lax.axis_index("tp"), lax.axis_index("dp")
    me_half, me_sub = me_tp // subs, me_tp % subs
    size = length + taps
    norm_factor = 1.0 / math.sqrt(length * n_seq * n_dp)

    ext = analysis_table(size, np.arange(size))
    scale = 2.0 / size
    synth_fwd = np.ascontiguousarray(ext[:, taps:].T)
    synth_bwd = np.ascontiguousarray(ext[:, :length].T)
    synth_lag = np.ascontiguousarray(analysis_table(size, np.arange(taps) - taps).T)

    mixed = (key_rows.astype(f32) * value_rows.astype(f32)).astype(bf16)
    prior = lax.ppermute(mixed[length - taps :], "seq", [(i, i + 1) for i in range(n_seq - 1)])

    def tp_dp(half, sub, replica):
        return (half * subs + sub) * n_dp + replica

    rounds = []
    for turn in range(2):
        route = [
            (tp_dp(h, c, d), tp_dp(d ^ turn, c, h))
            for h in range(n_dp)
            for c in range(subs)
            for d in range(n_dp)
        ]
        rounds.append(lax.ppermute(cot, ("tp", "dp"), route))
    same = me_half == me_dp
    other_cot = jnp.where(same, rounds[1], rounds[0])
    own_cot = jnp.where(same, rounds[0], rounds[1])

    def project(pieces_of):
        total = None
        for shift in range(subs):
            if shift:
                route = [
                    (tp_dp(h, c, d), tp_dp(h, (c + shift) % subs, d))
                    for h in range(n_dp)
                    for c in range(subs)
                    for d in range(n_dp)
                ]
                piece = lax.ppermute(pieces_of, ("tp", "dp"), route)
            else:
                piece = pieces_of
            width = piece.shape[1]
            which = (me_sub - shift + subs) % subs
            block = lax.dynamic_slice_in_dim(out_weight, which * width, width, axis=1)
            part = lax.dot_general(
                piece, block, (((1,), (1,)), ((), ())), preferred_element_type=f32
            )
            total = part if total is None else total + part
        return total

    other_part = swap_pairs(project(other_cot).astype(bf16), "dp", 1)
    own_part = project(own_cot)

    filt = transform(analysis_table(size, np.arange(taps)), filter_taps.T)
    bias = jnp.concatenate(
        [
            jnp.broadcast_to(skip_gain[None], (size // 2, channels)),
            jnp.zeros((size // 2, channels), f32),
        ]
    )
    filt = (filt + bias) * scale
    mixed_spec = transform(ext, jnp.concatenate([prior, mixed], axis=0))
    state = transform(synth_fwd, spectrum_product(mixed_spec, filt, False))
    gated = (queries.astype(f32) * state).astype(bf16)
    gated_all = lax.all_gather(gated, "seq", axis=0, tiled=True)

    if n_seq == n_tp:
        moved = lax.ppermute(
            cot, ("seq", "tp"), [(s * n_tp + t, t * n_tp + s) for s in range(n_seq) for t in range(n_tp)]
        )
        cot_all = lax.all_gather(moved, "tp", axis=0, tiled=True)
    else:
        full = lax.all_gather(cot, "tp", axis=1, tiled=True)
        cot_all = lax.all_to_all(full, "seq", 1, 0, tiled=True)

    grad_gated = own_part + other_part.astype(f32)
    grad_query = (grad_gated * state).astype(bf16)
    signal = (grad_gated * queries.astype(f32)).astype(bf16)
    later = lax.ppermute(signal[:taps], "seq", [(i + 1, i) for i in range(n_seq - 1)])
    signal_spec = transform(ext[:, :length], signal)
    lags = transform(synth_lag, spectrum_product(signal_spec, mixed_spec, True))
    lags = sum_over(sum_over(lags, "dp"), "seq")
    grad_filter = lags.T * (norm_factor * scale)
    signal_spec = signal_spec + transform(ext[:, length:], later)
    back = transform(synth_bwd, spectrum_product(signal_spec, filt, True))
    grad_key = (back * value_rows.astype(f32)).astype(bf16)
    grad_value = (back * key_rows.astype(f32)).astype(bf16)

    rows = cot_all.shape[1] // n_dp

    def weight_part(replica):
        block = lax.dynamic_slice_in_dim(cot_all, replica * rows, rows, axis=1)
        return lax.dot_general(
            block, gated_all, (((0,), (0,)), ((), ())), preferred_element_type=f32
        )

    sent = swap_pairs(weight_part(1 - me_dp).astype(bf16), "dp", 1)
    grad_weight = (weight_part(me_dp) + sent.astype(f32)) * norm_factor
    return (
        grad_query[None],
        grad_key[None],
        grad_value[None],
        grad_filter,
        grad_filter[:, 0],
        grad_weight,
    )


def solution(mesh):
    tokens = P("dp", "seq", "tp")
    return jax.shard_map(
        per_device,
        mesh=mesh,
        in_specs=(tokens, tokens, tokens, P("tp", None), P("tp"), P("tp", "dp"), tokens),
        out_specs=(tokens, tokens, tokens, P("tp", None), P("tp"), P(("seq", "dp"), "tp")),
        check_vma=False,
    )
```

time: 824 us -> 164 us (0.20); the launches traced: 813 us -> 163 us
  waiting for transfers between devices: 426 us -> 73 us
  local copies, waits for them, and re-layouts: 281 us -> 11.6 us
  starting transfers between devices: 6.66 us -> 33.8 us
  matrix products: 48 us -> 25.3 us
  blocking collectives: 19 us -> 0 us
  other arithmetic: 18.1 us -> 4.83 us
    reduce_scatter x1 -> x0, waiting for transfers between devices: 284 us -> none  [per_device(): lax.psum_scatter(lax.dot_general(selected, gated, (((0,), (0,)), ((), ())...]
    reshape x20 -> x0, local copies, waits for them, and re-layouts: 111 us -> none  [the longest x17 90.6 us: windows(): extended[lower:lower + length]]
    concatenate x7 -> x0, local copies, waits for them, and re-layouts: 81.6 us -> none  [the longest x2 71.8 us: windows(): return jnp.concatenate(pieces, axis=1)]
    all_gather x2, waiting for transfers between devices: 99.8 us -> 22.6 us  [the longest x1 22.6 us: per_device(): gated_all = lax.all_gather(gated, 'seq', axis=0, tiled=True)]
    ppermute x2 -> x12, waiting for transfers between devices: 0.01 us -> 50.4 us  [the longest x5 25.4 us: swap_pairs(): return lax.ppermute(value, axis, [(i, i ^ distance) for i in range(count)])]
    psum x1 -> x0, waiting for transfers between devices: 40.7 us -> none  [per_device(): lax.psum((lag_sums(blocks, tap_count), skip_term), ('seq', 'dp'))]
    ppermute x2 -> x12, starting transfers between devices: 6.22 us -> 33.8 us  [the longest x5 17.6 us: swap_pairs(): return lax.ppermute(value, axis, [(i, i ^ distance) for i in range(count)])]
    dot_general x5 -> x17, matrix products: 48 us -> 25.3 us  [the longest x11 12.5 us: transform(): jnp.dot(table, rows.astype(jnp.float32), precision=high, preferred_elemen...]
  transfers between devices with their start and end apart: 6 -> 14, of which waited for: 3 -> 7; matrix products, arithmetic and copies ran while one was open for 22% -> 22% of each run, Pallas kernels for 0% -> 0%
where the time goes in v1:
time: 164 us; the launch traced here: 163 us
  waiting for transfers between devices  73 us (45%)
  starting transfers between devices  33.8 us (21%)
  matrix products  25.3 us (15%)
  between operations  14.4 us (9%)
  local copies, waits for them, and re-layouts  11.6 us (7%)
  other arithmetic  4.83 us (3%)
    ppermute x5, waiting for transfers between devices, swap_pairs(): return lax.ppermute(value, axis, [(i, i ^ distance) for i in range(count)])  25.4 us
    all_gather x1, waiting for transfers between devices, per_device(): gated_all = lax.all_gather(gated, 'seq', axis=0, tiled=True)  22.6 us
    ppermute x5, starting transfers between devices, swap_pairs(): return lax.ppermute(value, axis, [(i, i ^ distance) for i in range(count)])  17.6 us
    ppermute x1, waiting for transfers between devices, per_device(): lax.ppermute(signal[:taps], 'seq', [(i + 1, i) for i in range(n_seq - 1)])  14.2 us
    dot_general x11, matrix products, transform(): jnp.dot(table, rows.astype(jnp.float32), precision=high, preferred_elemen...  12.5 us
    ppermute x2, waiting for transfers between devices, per_device(): rounds.append(lax.ppermute(cot, ('tp', 'dp'), route))  10.7 us
    unnamed x49, local copies, waits for them, and re-layouts  10.2 us
    dot_general x2, matrix products, weight_part(): lax.dot_general(block, gated_all, (((0,), (0,)), ((), ())), preferred_ele...  8.37 us
  transfers between devices with their start and end apart: 14, of which 7 were waited for; matrix products, arithmetic and copies ran while one was open for 22% of the time, Pallas kernels for 0%

profile of v1, /device:TPU:0, one launch (start us, length us, event | category | flops | bytes accessed | tf_op | source)
XLA Modules:
  0.0 163.0 jit_solution(9988232989473953475)
XLA Ops:
  7.2 1.8 %collective-permute-start.10 = (bf16[256,1024]{1,0:T(8,128)(2,1)}, bf16[256,1024]{1,0:T(8,128)(2,1)S(1)}, u32[]{:S(2)}, u32[]{:S(2)}) collective-permute-start(bf16[256,1024]{1,0:T(8,128)(2,1)} %bitcast.55), channel_id=1, source_target_pairs={{0,0},{2,8},{4,16},{6,24},{8,2},{10,10},{12,18},{14,26},{16,4},{18... | collective-permute-start | bytes 1572872 | tf_op jit(solution)/shard_map/ppermute | solution.py:132
  9.1 5.8 %collective-permute-start.1 = (bf16[256,1024]{1,0:T(8,128)(2,1)}, bf16[256,1024]{1,0:T(8,128)(2,1)S(1)}, u32[]{:S(2)}, u32[]{:S(2)}) collective-permute-start(bf16[256,1024]{1,0:T(8,128)(2,1)} %bitcast.56), channel_id=1, source_target_pairs={{0,4},{1,0},{2,6},{3,2},{4,5},{5,1},{6,7},{7,3},{8,12},{9,8},{10,1... | collective-permute-start | bytes 1572872 | tf_op jit(solution)/shard_map/ppermute | solution.py:88
  14.8 1.7 %collective-permute-start = (bf16[256,1024]{1,0:T(8,128)(2,1)}, bf16[256,1024]{1,0:T(8,128)(2,1)S(1)}, u32[]{:S(2)}, u32[]{:S(2)}) collective-permute-start(bf16[256,1024]{1,0:T(8,128)(2,1)} %bitcast.57), channel_id=1, source_target_pairs={{0,0},{1,4},{2,2},{3,6},{4,1},{5,5},{6,3},{7,7},{8,8},{9,12},{10,1... | collective-permute-start | bytes 1572872 | tf_op jit(solution)/shard_map/ppermute | solution.py:88
  16.5 1.2 copy.20
  17.8 1.4 copy.21
  21.0 4.8 %collective-permute-start.5 = (bf16[128,1024]{0,1:T(8,128)(2,1)}, bf16[128,1024]{0,1:T(8,128)(2,1)S(1)}, u32[]{:S(2)}, u32[]{:S(2)}) collective-permute-start(bf16[128,1024]{0,1:T(8,128)(2,1)} %slice.56), channel_id=1, source_target_pairs={{0,8},{8,16},{16,24},{1,9},{9,17},{17,25},{2,10},{10,18},{18,26},{... | collective-permute-start | bytes 786440 | tf_op jit(solution)/shard_map/ppermute | solution.py:75
  27.6 10.7 %collective-permute-done.1 = bf16[256,1024]{1,0:T(8,128)(2,1)S(1)} collective-permute-done((bf16[256,1024]{1,0:T(8,128)(2,1)}, bf16[256,1024]{1,0:T(8,128)(2,1)S(1)}, u32[]{:S(2)}, u32[]{:S(2)}) %collective-permute-start.1) | collective-permute-done | bytes 524320 | tf_op jit(solution)/shard_map/ppermute | solution.py:88
  42.6 3.1 %collective-permute-start.4 = (bf16[256,1024]{1,0:T(8,128)(2,1)S(1)}, bf16[256,1024]{1,0:T(8,128)(2,1)S(1)}, u32[]{:S(2)}, u32[]{:S(2)}) collective-permute-start(bf16[256,1024]{1,0:T(8,128)(2,1)S(1)} %fusion.19), channel_id=1, source_target_pairs={{0,1},{1,0},{2,3},{3,2},{4,5},{5,4},{6,7},{7,6},{8,9},{9,8},{10,11... | collective-permute-start | bytes 1572872 | tf_op jit(solution)/shard_map/ppermute | solution.py:38
  47.2 11.0 %collective-permute-done.4 = bf16[256,1024]{1,0:T(8,128)(2,1)S(1)} collective-permute-done((bf16[256,1024]{1,0:T(8,128)(2,1)S(1)}, bf16[256,1024]{1,0:T(8,128)(2,1)S(1)}, u32[]{:S(2)}, u32[]{:S(2)}) %collective-permute-start.4) | collective-permute-done | bytes 524320 | tf_op jit(solution)/shard_map/ppermute | solution.py:38
  58.2 2.1 %fusion.28 = (bf16[256,1024]{1,0:T(8,128)(2,1)}, bf16[1,256,1024]{2,1,0:T(8,128)(2,1)}, bf16[256,1024]{1,0:T(8,128)(2,1)}) fusion(f32[256,1024]{1,0:T(8,128)S(1)} %fusion.9, bf16[1,256,1024]{2,1,0:T(8,128)(2,1)S(1)} %copy-done.13, bf16[256,1024]{1,0:T(8,128)(2,1)S(1)} %collective-permute-done.4, f32[256,1024]{1,0:T(8,128)S(1)} %fusion.2, ...), kind=kOutput, calls=%fused_computation.33 | convolution fusion | flops 539492352 | bytes 7340036 | tf_op jit(solution)/shard_map/dot_general | solution.py:109
  60.4 1.8 %fusion.94 = f32[384,1024]{1,0:T(8,128)S(1)} fusion(f32[384,256]{1,0:T(8,128)} %constant.79.clone, bf16[256,1024]{1,0:T(8,128)(2,1)} %get-tuple-element.14), kind=kOutput, calls=%fused_computation.101 | convolution fusion | flops 603979776 | bytes 2490368 | tf_op jit(solution)/shard_map/dot_general | solution.py:20
  63.1 1.2 fusion.23
  64.3 1.7 %collective-permute-start.7 = (bf16[128,1024]{1,0:T(8,128)(2,1)}, bf16[128,1024]{1,0:T(8,128)(2,1)S(1)}, u32[]{:S(2)}, u32[]{:S(2)}) collective-permute-start(bf16[128,1024]{1,0:T(8,128)(2,1)} %fusion.23), channel_id=1, source_target_pairs={{0,1},{1,0},{2,3},{3,2},{4,5},{5,4},{6,7},{7,6},{8,9},{9,8},{10,11... | collective-permute-start | bytes 786440 | tf_op jit(solution)/shard_map/ppermute | solution.py:38
  66.0 1.5 collective-permute-start.6
  67.5 5.2 %collective-permute-done.7 = bf16[128,1024]{1,0:T(8,128)(2,1)S(1)} collective-permute-done((bf16[128,1024]{1,0:T(8,128)(2,1)}, bf16[128,1024]{1,0:T(8,128)(2,1)S(1)}, u32[]{:S(2)}, u32[]{:S(2)}) %collective-permute-start.7) | collective-permute-done | bytes 262176 | tf_op jit(solution)/shard_map/ppermute | solution.py:38
  72.7 1.7 %add_convert_fusion.1 = bf16[128,1024]{1,0:T(8,128)(2,1)} fusion(bf16[128,1024]{1,0:T(8,128)(2,1)S(1)} %collective-permute-done.7, bf16[128,1024]{1,0:T(8,128)(2,1)} %fusion.23), kind=kLoop, calls=%fused_computation.91 | loop fusion | flops 524288 | bytes 786432 | tf_op jit(solution)/shard_map/convert_element_type | solution.py:44
  74.4 8.5 %collective-permute-start.8 = (bf16[128,1024]{1,0:T(8,128)(2,1)}, bf16[128,1024]{1,0:T(8,128)(2,1)}, u32[]{:S(2)}, u32[]{:S(2)}) collective-permute-start(bf16[128,1024]{1,0:T(8,128)(2,1)} %add_convert_fusion.1), channel_id=1, source_target_pairs={{0,8},{8,0},{16,24},{24,16},{1,9},{9,1},{17,25},{25,17},{2,10},{10... | collective-permute-start | bytes 786440 | tf_op jit(solution)/shard_map/ppermute | solution.py:38
  82.9 14.2 %collective-permute-done.6 = bf16[128,1024]{1,0:T(8,128)(2,1)S(1)} collective-permute-done((bf16[128,1024]{1,0:T(8,128)(2,1)S(1)}, bf16[128,1024]{1,0:T(8,128)(2,1)S(1)}, u32[]{:S(2)}, u32[]{:S(2)}) %collective-permute-start.6) | collective-permute-done | bytes 262176 | tf_op jit(solution)/shard_map/ppermute | solution.py:143
  97.1 2.6 %convolution_add_fusion = f32[384,1024]{1,0:T(8,128)} fusion(f32[384,1024]{1,0:T(8,128)S(1)} %fusion.94, f32[384,128]{1,0:T(8,128)} %constant.81.clone, bf16[128,1024]{1,0:T(8,128)(2,1)S(1)} %collective-permute-done.6), kind=kOutput, calls=%fused_computation.12 | convolution fusion | flops 302383104 | bytes 3604480 | tf_op jit(solution)/shard_map/dot_general | solution.py:20
  99.7 22.6 %all-gather.5.cloned.1.call-done = bf16[1024,1024]{1,0:T(8,128)(2,1)} async-done(((bf16[256,1024]{1,0:T(8,128)(2,1)}), bf16[1024,1024]{1,0:T(8,128)(2,1)}) %all-gather.5.cloned.1.call-update) | async-done | bytes 2097168 | tf_op jit(solution)/shard_map/all_gather | solution.py:129
  122.3 4.2 %convolution_convert_fusion = bf16[512,1024]{1,0:T(8,128)(2,1)} fusion(bf16[1024,1024]{1,0:T(8,128)(2,1)} %all-gather.5.cloned.1.call-done, bf16[1024,1024]{1,0:T(8,128)(2,1)} %all-gather.3.cloned.1.call-done, s32[]{:T(128)S(6)} %select_n.59), kind=kOutput, calls=%fused_computation.11 | convolution fusion | flops 1074266112 | bytes 4194308 | tf_op jit(solution)/shard_map/dot_general | solution.py:157
  126.9 1.0 fusion.41
  127.9 1.8 %add_convert_fusion = bf16[128,1024]{1,0:T(8,128)(2,1)} fusion(bf16[128,1024]{1,0:T(8,128)(2,1)} %collective-permute-done.8, bf16[128,1024]{1,0:T(8,128)(2,1)} %add_convert_fusion.1), kind=kLoop, calls=%fused_computation.90 | loop fusion | flops 524288 | bytes 786432 | tf_op jit(solution)/shard_map/convert_element_type | solution.py:44
  129.7 4.0 %collective-permute-start.9 = (bf16[128,1024]{1,0:T(8,128)(2,1)}, bf16[128,1024]{1,0:T(8,128)(2,1)}, u32[]{:S(2)}, u32[]{:S(2)}) collective-permute-start(bf16[128,1024]{1,0:T(8,128)(2,1)} %add_convert_fusion), channel_id=1, source_target_pairs={{0,16},{8,24},{16,0},{24,8},{1,17},{9,25},{17,1},{25,9},{2,18},{10... | collective-permute-start | bytes 786440 | tf_op jit(solution)/shard_map/ppermute | solution.py:38
  133.7 2.1 %fusion.81 = (bf16[1,256,1024]{1,2,0:T(8,128)(2,1)}, bf16[1,256,1024]{1,2,0:T(8,128)(2,1)}) fusion(bf16[1,256,1024]{1,2,0:T(8,128)(2,1)S(1)} %copy-done.7, bf16[1,256,1024]{1,2,0:T(8,128)(2,1)S(1)} %copy-done.9, f32[1024,256]{1,0:T(8,128)S(1)} %fusion.41, f32[256,192]{1,0:T(8,128)S(1)} %copy-done.15, f32[384,1024]{1,0:T(8,128)S(1)} %copy-done.5, ...), kind=kOutput, calls=%fused_computation.87 | convolution fusion | flops 304611328 | bytes 6488064 | tf_op jit(solution)/shard_map/dot_general | solution.py:20
  135.8 2.0 %copy.24 = bf16[1,256,1024]{2,1,0:T(8,128)(2,1)} copy(bf16[1,256,1024]{1,2,0:T(8,128)(2,1)} %get-tuple-element.16) | data formatting | bytes 1048576
  137.8 2.2 %copy.25 = bf16[1,256,1024]{2,1,0:T(8,128)(2,1)} copy(bf16[1,256,1024]{1,2,0:T(8,128)(2,1)} %get-tuple-element.15) | data formatting | bytes 1048576
  140.0 5.9 %collective-permute-done.9 = bf16[128,1024]{1,0:T(8,128)(2,1)} collective-permute-done((bf16[128,1024]{1,0:T(8,128)(2,1)}, bf16[128,1024]{1,0:T(8,128)(2,1)}, u32[]{:S(2)}, u32[]{:S(2)}) %collective-permute-start.9) | collective-permute-done | bytes 262176 | tf_op jit(solution)/shard_map/ppermute | solution.py:38
  145.9 1.1 multiply_bitcast_fusion
  147.0 1.0 copy.26
  148.6 3.4 %collective-permute-done.11 = bf16[512,1024]{1,0:T(8,128)(2,1)} collective-permute-done((bf16[512,1024]{1,0:T(8,128)(2,1)}, bf16[512,1024]{1,0:T(8,128)(2,1)}, u32[]{:S(2)}, u32[]{:S(2)}) %collective-permute-start.11) | collective-permute-done | bytes 1048608 | tf_op jit(solution)/shard_map/ppermute | solution.py:38
  152.0 4.1 %add_multiply_fusion = f32[512,1024]{1,0:T(8,128)} fusion(bf16[512,1024]{1,0:T(8,128)(2,1)} %collective-permute-done.11, bf16[1024,1024]{1,0:T(8,128)(2,1)S(1)} %copy-done.4, bf16[1024,1024]{1,0:T(8,128)(2,1)} %all-gather.3.cloned.1.call-done, s32[]{:T(128)S(6)} %select_n.58), kind=kOutput, calls=%fused_computation | convolution fusion | flops 1075314688 | bytes 6291460 | tf_op jit(solution)/shard_map/dot_general | solution.py:157
  (73 shorter events, 11.0 us)
Async XLA Ops:
  7.2 18.8 %copy-start = (bf16[1024,128]{1,0:T(8,128)(2,1)S(1)}, bf16[1024,128]{1,0:T(8,128)(2,1)}, u32[]{:S(2)}) copy-start(bf16[1024,128]{1,0:T(8,128)(2,1)} %param.17) | copy-start | bytes 786436
  7.2 92.6 %all-gather.3.cloned.1.call-start = ((), (), s32[]{:S(2)}) async-start(), calls=%async_computation | async-start | bytes 2621440 | tf_op jit(solution)/shard_map/all_gather | solution.py:135
  7.2 12.0 %collective-permute-start.10 = (bf16[256,1024]{1,0:T(8,128)(2,1)}, bf16[256,1024]{1,0:T(8,128)(2,1)S(1)}, u32[]{:S(2)}, u32[]{:S(2)}) collective-permute-start(bf16[256,1024]{1,0:T(8,128)(2,1)} %bitcast.55), channel_id=1, source_target_pairs={{0,0},{2,8},{4,16},{6,24},{8,2},{10,10},{12,18},{14,26},{16,4},{18... | collective-permute-start | bytes 1572872 | tf_op jit(solution)/shard_map/ppermute | solution.py:132
  9.1 29.3 %collective-permute-start.1 = (bf16[256,1024]{1,0:T(8,128)(2,1)}, bf16[256,1024]{1,0:T(8,128)(2,1)S(1)}, u32[]{:S(2)}, u32[]{:S(2)}) collective-permute-start(bf16[256,1024]{1,0:T(8,128)(2,1)} %bitcast.56), channel_id=1, source_target_pairs={{0,4},{1,0},{2,6},{3,2},{4,5},{5,1},{6,7},{7,3},{8,12},{9,8},{10,1... | collective-permute-start | bytes 1572872 | tf_op jit(solution)/shard_map/ppermute | solution.py:88
  14.8 23.6 %collective-permute-start = (bf16[256,1024]{1,0:T(8,128)(2,1)}, bf16[256,1024]{1,0:T(8,128)(2,1)S(1)}, u32[]{:S(2)}, u32[]{:S(2)}) collective-permute-start(bf16[256,1024]{1,0:T(8,128)(2,1)} %bitcast.57), channel_id=1, source_target_pairs={{0,0},{1,4},{2,2},{3,6},{4,1},{5,5},{6,3},{7,7},{8,8},{9,12},{10,1... | collective-permute-start | bytes 1572872 | tf_op jit(solution)/shard_map/ppermute | solution.py:88
  17.8 2.5 %copy-start.6 = (bf16[1,256,1024]{1,2,0:T(8,128)(2,1)}, bf16[1,256,1024]{1,2,0:T(8,128)(2,1)S(1)}, u32[]{:S(2)}) copy-start(bf16[1,256,1024]{1,2,0:T(8,128)(2,1)S(1)} %copy.20) | copy-start | bytes 1572868
  19.2 6.8 %copy-start.8 = (bf16[1,256,1024]{1,2,0:T(8,128)(2,1)}, bf16[1,256,1024]{1,2,0:T(8,128)(2,1)S(1)}, u32[]{:S(2)}) copy-start(bf16[1,256,1024]{1,2,0:T(8,128)(2,1)S(1)} %copy.21) | copy-start | bytes 1572868
  19.2 6.7 %copy-start.21 = (f32[1024]{0:T(1024)S(1)}, f32[1024]{0:T(1024)}, u32[]{:S(2)}) copy-start(f32[1024]{0:T(1024)} %param.18) | copy-start | bytes 12292
  20.1 5.9 %copy-start.11 = (f32[384,128]{1,0:T(8,128)S(1)}, f32[384,128]{1,0:T(8,128)}, u32[]{:S(2)}) copy-start(f32[384,128]{1,0:T(8,128)} %constant.76.clone) | copy-start | bytes 589828
  20.1 102.2 %all-gather.5.cloned.1.call-start = ((), (), s32[]{:S(2)}) async-start(), calls=%async_computation.1 | async-start | bytes 2621440 | tf_op jit(solution)/shard_map/all_gather | solution.py:129
  21.0 17.7 %collective-permute-start.5 = (bf16[128,1024]{0,1:T(8,128)(2,1)}, bf16[128,1024]{0,1:T(8,128)(2,1)S(1)}, u32[]{:S(2)}, u32[]{:S(2)}) collective-permute-start(bf16[128,1024]{0,1:T(8,128)(2,1)} %slice.56), channel_id=1, source_target_pairs={{0,8},{8,16},{16,24},{1,9},{9,17},{17,25},{2,10},{10,18},{18,26},{... | collective-permute-start | bytes 786440 | tf_op jit(solution)/shard_map/ppermute | solution.py:75
  27.0 18.7 %copy-start.2 = (f32[384,1024]{1,0:T(8,128)}, f32[384,1024]{1,0:T(8,128)S(1)}, u32[]{:S(2)}) copy-start(f32[384,1024]{1,0:T(8,128)S(1)} %add_multiply_fusion.1) | copy-start | bytes 4718596
  38.5 2.0 %collective-permute-start.3 = (bf16[256,1024]{1,0:T(8,128)(2,1)S(1)}, bf16[256,1024]{1,0:T(8,128)(2,1)S(1)}, u32[]{:S(2)}, u32[]{:S(2)}) collective-permute-start(bf16[256,1024]{1,0:T(8,128)(2,1)S(1)} %get-tuple-element.17), channel_id=1, source_target_pairs={{0,2},{1,3},{2,0},{3,1},{4,6},{5,7},{6,4},{7,5},{8,10},{9,11},{10,... | collective-permute-start | bytes 1572872 | tf_op jit(solution)/shard_map/ppermute | solution.py:103
  38.8 2.2 %copy-start.1 = (bf16[1024,2048]{1,0:T(8,128)(2,1)S(1)}, bf16[1024,2048]{1,0:T(8,128)(2,1)}, u32[]{:S(2)}) copy-start(bf16[1024,2048]{1,0:T(8,128)(2,1)} %param.19) | copy-start | bytes 12582916
  40.1 6.3 %collective-permute-start.2 = (bf16[256,1024]{1,0:T(8,128)(2,1)S(1)}, bf16[256,1024]{1,0:T(8,128)(2,1)S(1)}, u32[]{:S(2)}, u32[]{:S(2)}) collective-permute-start(bf16[256,1024]{1,0:T(8,128)(2,1)S(1)} %get-tuple-element.18), channel_id=1, source_target_pairs={{0,2},{1,3},{2,0},{3,1},{4,6},{5,7},{6,4},{7,5},{8,10},{9,11},{10,... | collective-permute-start | bytes 1572872 | tf_op jit(solution)/shard_map/ppermute | solution.py:103
  41.7 3.9 %copy-start.18 = (f32[256,192]{1,0:T(8,128)S(1)}, f32[256,192]{1,0:T(8,128)}, u32[]{:S(2)}) copy-start(f32[256,192]{1,0:T(8,128)} %constant.92) | copy-start | bytes 589828
  42.6 15.6 %collective-permute-start.4 = (bf16[256,1024]{1,0:T(8,128)(2,1)S(1)}, bf16[256,1024]{1,0:T(8,128)(2,1)S(1)}, u32[]{:S(2)}, u32[]{:S(2)}) collective-permute-start(bf16[256,1024]{1,0:T(8,128)(2,1)S(1)} %fusion.19), channel_id=1, source_target_pairs={{0,1},{1,0},{2,3},{3,2},{4,5},{5,4},{6,7},{7,6},{8,9},{9,8},{10,11... | collective-permute-start | bytes 1572872 | tf_op jit(solution)/shard_map/ppermute | solution.py:38
  46.4 11.8 %copy-start.13 = (bf16[1,256,1024]{2,1,0:T(8,128)(2,1)S(1)}, bf16[1,256,1024]{2,1,0:T(8,128)(2,1)}, u32[]{:S(2)}) copy-start(bf16[1,256,1024]{2,1,0:T(8,128)(2,1)} %param.14) | copy-start | bytes 1572868
  60.3 1.8 %copy-start.20 = (f32[128,192]{1,0:T(8,128)S(1)}, f32[128,192]{1,0:T(8,128)}, u32[]{:S(2)}) copy-start(f32[128,192]{1,0:T(8,128)} %constant.95) | copy-start | bytes 294916
  63.1 2.9 %copy-start.10 = (bf16[256,1024]{1,0:T(8,128)(2,1)S(1)}, bf16[256,1024]{1,0:T(8,128)(2,1)}, u32[]{:S(2)}) copy-start(bf16[256,1024]{1,0:T(8,128)(2,1)} %get-tuple-element.14) | copy-start | bytes 1572868
  64.3 8.4 %collective-permute-start.7 = (bf16[128,1024]{1,0:T(8,128)(2,1)}, bf16[128,1024]{1,0:T(8,128)(2,1)S(1)}, u32[]{:S(2)}, u32[]{:S(2)}) collective-permute-start(bf16[128,1024]{1,0:T(8,128)(2,1)} %fusion.23), channel_id=1, source_target_pairs={{0,1},{1,0},{2,3},{3,2},{4,5},{5,4},{6,7},{7,6},{8,9},{9,8},{10,11... | collective-permute-start | bytes 786440 | tf_op jit(solution)/shard_map/ppermute | solution.py:38
  66.0 31.1 %collective-permute-start.6 = (bf16[128,1024]{1,0:T(8,128)(2,1)S(1)}, bf16[128,1024]{1,0:T(8,128)(2,1)S(1)}, u32[]{:S(2)}, u32[]{:S(2)}) collective-permute-start(bf16[128,1024]{1,0:T(8,128)(2,1)S(1)} %slice.61), channel_id=1, source_target_pairs={{8,0},{16,8},{24,16},{9,1},{17,9},{25,17},{10,2},{18,10},{26,18},{... | collective-permute-start | bytes 786440 | tf_op jit(solution)/shard_map/ppermute | solution.py:143
  74.4 53.5 %collective-permute-start.8 = (bf16[128,1024]{1,0:T(8,128)(2,1)}, bf16[128,1024]{1,0:T(8,128)(2,1)}, u32[]{:S(2)}, u32[]{:S(2)}) collective-permute-start(bf16[128,1024]{1,0:T(8,128)(2,1)} %add_convert_fusion.1), channel_id=1, source_target_pairs={{0,8},{8,0},{16,24},{24,16},{1,9},{9,1},{17,25},{25,17},{2,10},{10... | collective-permute-start | bytes 786440 | tf_op jit(solution)/shard_map/ppermute | solution.py:38
  99.7 27.1 %copy-start.3 = (f32[384,1024]{1,0:T(8,128)S(1)}, f32[384,1024]{1,0:T(8,128)}, u32[]{:S(2)}) copy-start(f32[384,1024]{1,0:T(8,128)} %copy-done.2) | copy-start | bytes 4718596
  99.7 27.1 %copy-start.5 = (f32[384,1024]{1,0:T(8,128)S(1)}, f32[384,1024]{1,0:T(8,128)}, u32[]{:S(2)}) copy-start(f32[384,1024]{1,0:T(8,128)} %convolution_add_fusion) | copy-start | bytes 4718596
  122.3 4.5 %copy-start.16 = (f32[256,192]{1,0:T(8,128)S(1)}, f32[256,192]{1,0:T(8,128)}, u32[]{:S(2)}) copy-start(f32[256,192]{1,0:T(8,128)} %constant.93) | copy-start | bytes 589828
  126.6 7.1 %copy-start.7 = (bf16[1,256,1024]{1,2,0:T(8,128)(2,1)S(1)}, bf16[1,256,1024]{1,2,0:T(8,128)(2,1)}, u32[]{:S(2)}) copy-start(bf16[1,256,1024]{1,2,0:T(8,128)(2,1)} %copy-done.6) | copy-start | bytes 1572868
  126.6 7.1 %copy-start.9 = (bf16[1,256,1024]{1,2,0:T(8,128)(2,1)S(1)}, bf16[1,256,1024]{1,2,0:T(8,128)(2,1)}, u32[]{:S(2)}) copy-start(bf16[1,256,1024]{1,2,0:T(8,128)(2,1)} %copy-done.8) | copy-start | bytes 1572868
  126.6 7.1 %copy-start.15 = (f32[256,192]{1,0:T(8,128)S(1)}, f32[256,192]{1,0:T(8,128)}, u32[]{:S(2)}) copy-start(f32[256,192]{1,0:T(8,128)} %constant.94) | copy-start | bytes 589828
  126.6 25.4 %collective-permute-start.11 = (bf16[512,1024]{1,0:T(8,128)(2,1)}, bf16[512,1024]{1,0:T(8,128)(2,1)}, u32[]{:S(2)}, u32[]{:S(2)}) collective-permute-start(bf16[512,1024]{1,0:T(8,128)(2,1)} %convolution_convert_fusion), channel_id=1, source_target_pairs={{0,1},{1,0},{2,3},{3,2},{4,5},{5,4},{6,7},{7,6},{8,9},{9,8},{10,11... | collective-permute-start | bytes 3145736 | tf_op jit(solution)/shard_map/ppermute | solution.py:38
  129.7 16.2 %collective-permute-start.9 = (bf16[128,1024]{1,0:T(8,128)(2,1)}, bf16[128,1024]{1,0:T(8,128)(2,1)}, u32[]{:S(2)}, u32[]{:S(2)}) collective-permute-start(bf16[128,1024]{1,0:T(8,128)(2,1)} %add_convert_fusion), channel_id=1, source_target_pairs={{0,16},{8,24},{16,0},{24,8},{1,17},{9,25},{17,1},{25,9},{2,18},{10... | collective-permute-start | bytes 786440 | tf_op jit(solution)/shard_map/ppermute | solution.py:38
  137.8 14.2 %copy-start.4 = (bf16[1024,1024]{1,0:T(8,128)(2,1)S(1)}, bf16[1024,1024]{1,0:T(8,128)(2,1)}, u32[]{:S(2)}) copy-start(bf16[1024,1024]{1,0:T(8,128)(2,1)} %all-gather.5.cloned.1.call-done) | copy-start | bytes 6291460
  (4 other events, 3.7 us)
Sparse Core Ops, SparseCore 0:
  20.2 40.3 all-gather.2
  62.7 59.5 all-gather.4

commit v2 on v1

v2 whole, which is shorter than its diff:
```python
import functools
import math

import jax
import jax.numpy as jnp
import ml_dtypes
import numpy as np
from jax import lax
from jax.experimental import pallas as pl
from jax.experimental.pallas import tpu as pltpu
from jax.sharding import PartitionSpec as P

f32, bf16 = jnp.float32, jnp.bfloat16
lanes = 256
vmem_bytes = 32 * 1024 * 1024


def analysis_table(size, positions):
    half = size // 2
    omega = 2.0 * np.pi * (np.arange(half) + 0.5) / size
    angle = omega[:, None] * np.asarray(positions)[None, :]
    return np.concatenate([np.cos(angle), -np.sin(angle)], axis=0)


def split_table(table):
    high = table.astype(ml_dtypes.bfloat16)
    low = (table - high.astype(np.float64)).astype(ml_dtypes.bfloat16)
    return np.stack([high, low])


def split_rows(rows):
    high = rows.astype(bf16)
    return high, (rows - high.astype(f32)).astype(bf16)


def dot(left, right):
    return jnp.dot(left, right, preferred_element_type=f32)


def dot_nt(left, right):
    return lax.dot_general(left, right, (((1,), (1,)), ((), ())), preferred_element_type=f32)


def forward_transform(table, rows):
    return dot(table[0], rows) + dot(table[1], rows)


def inverse_transform(table, spectrum):
    high, low = split_rows(spectrum)
    return dot(table[0], high) + dot(table[0], low) + dot(table[1], high)


def spectrum_product(left, right, conjugate_right):
    half = left.shape[0] // 2
    left_re, left_im = left[:half], left[half:]
    right_re, right_im = right[:half], right[half:]
    if conjugate_right:
        right_im = -right_im
    return jnp.concatenate(
        [left_re * right_re - left_im * right_im, left_re * right_im + left_im * right_re], axis=0
    )


def prepare_kernel(scale, own_table, tap_table, key_ref, value_ref, taps_ref, skip_ref, spec_ref, filt_ref):
    mixed = (key_ref[...].astype(f32) * value_ref[...].astype(f32)).astype(bf16)
    spec_ref[...] = forward_transform(own_table, mixed)
    filt = dot_nt(tap_table[0], taps_ref[...]) + dot_nt(tap_table[1], taps_ref[...])
    half = filt.shape[0] // 2
    filt_ref[:half] = (filt[:half] + skip_ref[...]) * scale
    filt_ref[half:] = filt[half:] * scale


def state_kernel(prior_table, synth, prior_ref, own_ref, filt_ref, query_ref, spec_ref, state_ref, gated_ref):
    spec = own_ref[...] + forward_transform(prior_table, prior_ref[...])
    spec_ref[...] = spec
    state = inverse_transform(synth, spectrum_product(spec, filt_ref[...], False))
    state_ref[...] = state
    gated_ref[...] = (query_ref[...].astype(f32) * state).astype(bf16)


def project_kernel(count, which_ref, *refs):
    total = None
    for piece_ref, weight_ref in zip(refs[:count], refs[count : 2 * count]):
        part = dot_nt(piece_ref[...], weight_ref[...])
        total = part if total is None else total + part
    refs[-1][...] = total.astype(refs[-1].dtype)


def lag_kernel(own_table, synth, signal_ref, spec_ref, signal_spec_ref, lag_ref):
    signal_spec = forward_transform(own_table, signal_ref[...])
    signal_spec_ref[...] = signal_spec
    lag_ref[...] = inverse_transform(synth, spectrum_product(signal_spec, spec_ref[...], True))


def back_kernel(late_table, synth, own_ref, later_ref, filt_ref, key_ref, value_ref, grad_key_ref, grad_value_ref):
    spec = own_ref[...] + forward_transform(late_table, later_ref[...])
    back = inverse_transform(synth, spectrum_product(spec, filt_ref[...], True))
    grad_key_ref[...] = (back * value_ref[...].astype(f32)).astype(bf16)
    grad_value_ref[...] = (back * key_ref[...].astype(f32)).astype(bf16)


def by_channel(kernel, tables, args, outs, channels, flops):
    count = len(tables)

    def body(*refs):
        kernel(*refs)

    def column_spec(shape, by_row):
        if by_row:
            return pl.BlockSpec((lanes, shape[1]), lambda i: (i, 0))
        return pl.BlockSpec((shape[0], lanes), lambda i: (0, i))

    specs = [pl.BlockSpec(t.shape, lambda i: (0, 0, 0)) for t in tables]
    specs += [column_spec(a.shape, a.shape[1] != channels) for a in args]
    moved = sum(a.size * a.dtype.itemsize for a in args) + sum(
        o.size * jnp.dtype(o.dtype).itemsize for o in outs
    )
    return pl.pallas_call(
        body,
        grid=(channels // lanes,),
        in_specs=specs,
        out_specs=[column_spec(o.shape, False) for o in outs],
        out_shape=outs,
        compiler_params=pltpu.CompilerParams(vmem_limit_bytes=vmem_bytes),
        cost_estimate=pl.CostEstimate(flops=flops // 64, bytes_accessed=moved // 64, transcendentals=0),
    )(*[jnp.asarray(t) for t in tables], *args)


def project(pieces, places, out_weight, dtype):
    count = len(pieces)
    length, width = pieces[0].shape
    channels = out_weight.shape[0]
    grid_spec = pltpu.PrefetchScalarGridSpec(
        num_scalar_prefetch=1,
        grid=(channels // lanes,),
        in_specs=[pl.BlockSpec((length, width), lambda i, w: (0, 0))] * count
        + [pl.BlockSpec((lanes, width), functools.partial(lambda n, i, w: (i, w[n]), n)) for n in range(count)],
        out_specs=pl.BlockSpec((length, lanes), lambda i, w: (0, i)),
    )
    return pl.pallas_call(
        functools.partial(project_kernel, count),
        grid_spec=grid_spec,
        out_shape=jax.ShapeDtypeStruct((length, channels), dtype),
        compiler_params=pltpu.CompilerParams(vmem_limit_bytes=vmem_bytes),
        cost_estimate=pl.CostEstimate(
            flops=2 * length * channels * out_weight.shape[1],
            bytes_accessed=out_weight.size * 2 + length * channels * 6,
            transcendentals=0,
        ),
    )(jnp.stack(places).astype(jnp.int32), *pieces, *([out_weight] * count))


def swap_pairs(value, axis, distance):
    count = lax.axis_size(axis)
    return lax.ppermute(value, axis, [(i, i ^ distance) for i in range(count)])


def after(value, *earlier):
    return lax.optimization_barrier((value, *earlier))[0]


def per_device(query_gate, key_gate, value_input, filter_taps, skip_gain, out_weight, cotangent):
    queries, key_rows, value_rows, cot = (
        query_gate[0],
        key_gate[0],
        value_input[0],
        cotangent[0],
    )
    length, channels = queries.shape
    taps = filter_taps.shape[1]
    n_seq, n_tp, n_dp = lax.axis_size("seq"), lax.axis_size("tp"), lax.axis_size("dp")
    subs = n_tp // n_dp
    me_tp, me_dp = lax.axis_index("tp"), lax.axis_index("dp")
    me_half, me_sub = me_tp // subs, me_tp % subs
    size = length + taps
    norm_factor = 1.0 / math.sqrt(length * n_seq * n_dp)

    whole = analysis_table(size, np.arange(size))
    scale = 2.0 / size
    own_table = split_table(whole[:, :length])
    tap_table = split_table(whole[:, :taps])
    late_table = split_table(whole[:, length:])
    shifted_table = split_table(whole[:, taps:])
    synth_fwd = np.ascontiguousarray(split_table(whole[:, taps:].T))
    synth_bwd = np.ascontiguousarray(split_table(whole[:, :length].T))
    synth_lag = np.ascontiguousarray(split_table(analysis_table(size, np.arange(taps) - taps).T))
    spectrum = jax.ShapeDtypeStruct((size, channels), f32)
    rows16 = jax.ShapeDtypeStruct((length, channels), bf16)
    rows32 = jax.ShapeDtypeStruct((length, channels), f32)
    unit = 2 * size * channels

    tail = (
        key_rows[length - taps :].astype(f32) * value_rows[length - taps :].astype(f32)
    ).astype(bf16)
    prior = lax.ppermute(tail, "seq", [(i, i + 1) for i in range(n_seq - 1)])

    def tp_dp(half, sub, replica):
        return (half * subs + sub) * n_dp + replica

    places = [(h, c, d) for h in range(n_dp) for c in range(subs) for d in range(n_dp)]
    rounds = []
    for turn in range(2):
        route = [(tp_dp(h, c, d), tp_dp(d ^ turn, c, h)) for h, c, d in places]
        rounds.append(lax.ppermute(cot, ("tp", "dp"), route))

    own_spec, filt = by_channel(
        functools.partial(prepare_kernel, scale),
        [shifted_table, tap_table],
        [key_rows, value_rows, filter_taps, skip_gain[None]],
        [spectrum, spectrum],
        channels,
        2 * unit * (length + taps),
    )
    mixed_spec, state, gated = by_channel(
        state_kernel,
        [tap_table, synth_fwd],
        [prior, own_spec, filt, queries],
        [spectrum, rows32, rows16],
        channels,
        unit * (2 * taps + 3 * length),
    )
    gated_all = lax.all_gather(gated, "seq", axis=0, tiled=True)

    same = me_half == me_dp
    other_cot = jnp.where(same, rounds[1], rounds[0])
    own_cot = jnp.where(same, rounds[0], rounds[1])

    def from_subs(piece):
        pieces = [piece]
        for shift in range(1, subs):
            route = [(tp_dp(h, c, d), tp_dp(h, (c + shift) % subs, d)) for h, c, d in places]
            pieces.append(lax.ppermute(piece, ("tp", "dp"), route))
        return pieces

    weight_places = [(me_sub - shift + subs) % subs for shift in range(subs)]
    other_sent = project(from_subs(other_cot), weight_places, out_weight, bf16)
    other_part = swap_pairs(other_sent, "dp", 1)
    own_part = project(from_subs(own_cot), weight_places, out_weight, f32)

    if n_seq == n_tp:
        moved = lax.ppermute(
            after(cot, other_cot),
            ("seq", "tp"),
            [(s * n_tp + t, t * n_tp + s) for s in range(n_seq) for t in range(n_tp)],
        )
        cot_all = lax.all_gather(moved, "tp", axis=0, tiled=True)
    else:
        full = lax.all_gather(cot, "tp", axis=1, tiled=True)
        cot_all = lax.all_to_all(full, "seq", 1, 0, tiled=True)

    grad_gated = own_part + other_part.astype(f32)
    grad_query = (grad_gated * state).astype(bf16)
    signal = (grad_gated * queries.astype(f32)).astype(bf16)
    later = lax.ppermute(signal[:taps], "seq", [(i + 1, i) for i in range(n_seq - 1)])
    signal_spec, lags = by_channel(
        lag_kernel,
        [own_table, synth_lag],
        [signal, mixed_spec],
        [spectrum, jax.ShapeDtypeStruct((taps, channels), f32)],
        channels,
        unit * (2 * length + 3 * taps),
    )
    grad_key, grad_value = by_channel(
        back_kernel,
        [late_table, synth_bwd],
        [signal_spec, later, filt, key_rows, value_rows],
        [rows16, rows16],
        channels,
        unit * (2 * taps + 3 * length),
    )

    share = taps // n_dp
    lag_sum = lax.dynamic_slice_in_dim(lags, me_dp * share, share, axis=0) + swap_pairs(
        lax.dynamic_slice_in_dim(lags, (1 - me_dp) * share, share, axis=0).astype(bf16), "dp", 1
    ).astype(f32)
    distance = 1
    while distance < n_seq:
        rounded = lag_sum.astype(bf16)
        lag_sum = rounded.astype(f32) + swap_pairs(rounded, "seq", distance).astype(f32)
        distance *= 2
    mine = lag_sum.astype(bf16)
    theirs = swap_pairs(mine, "dp", 1)
    first = me_dp == 0
    lag_sum = jnp.concatenate([jnp.where(first, mine, theirs), jnp.where(first, theirs, mine)], axis=0)
    grad_filter = lag_sum.astype(f32).T * (norm_factor * scale)

    rows = cot_all.shape[1] // n_dp

    def weight_part(replica):
        block = lax.dynamic_slice_in_dim(cot_all, replica * rows, rows, axis=1)
        return lax.dot_general(
            block, gated_all, (((0,), (0,)), ((), ())), preferred_element_type=f32
        )

    sent = swap_pairs(weight_part(1 - me_dp).astype(bf16), "dp", 1)
    grad_weight = (weight_part(me_dp) + sent.astype(f32)) * norm_factor
    return (
        grad_query[None],
        grad_key[None],
        grad_value[None],
        grad_filter,
        grad_filter[:, 0],
        grad_weight,
    )


def solution(mesh):
    tokens = P("dp", "seq", "tp")
    return jax.shard_map(
        per_device,
        mesh=mesh,
        in_specs=(tokens, tokens, tokens, P("tp", None), P("tp"), P("tp", "dp"), tokens),
        out_specs=(tokens, tokens, tokens, P("tp", None), P("tp"), P(("seq", "dp"), "tp")),
        check_vma=False,
    )
```

time: 164 us -> 175 us (1.067)
  the two profiles are of different devices: /device:TPU:0 before, /device:TPU:2 now
where the time goes in v2:
time: 175 us; the launch traced here: 174 us
  waiting for transfers between devices  86.4 us (49%)
  Pallas kernels  22.3 us (13%)
  local copies, waits for them, and re-layouts  18.8 us (11%)
  starting transfers between devices  16.1 us (9%)
  between operations  14.3 us (8%)
  matrix products  8.31 us (5%)
  other arithmetic  8.24 us (5%)
    ppermute x1, waiting for transfers between devices, per_device(): lax.ppermute(after(cot, other_cot), ('seq', 'tp'), [(s * n_tp + t, t * n_...  47.5 us
    ppermute x6, waiting for transfers between devices, swap_pairs(): return lax.ppermute(value, axis, [(i, i ^ distance) for i in range(count)])  24.5 us
    unnamed x51, local copies, waits for them, and re-layouts  17.5 us
    pallas_call x4, Pallas kernels, by_channel(): pl.pallas_call(body, grid=(channels // lanes,), in_specs=specs, out_specs...  13.9 us
    ppermute x2, waiting for transfers between devices, per_device(): rounds.append(lax.ppermute(cot, ('tp', 'dp'), route))  12.8 us
    pallas_call x2, Pallas kernels, project(): pl.pallas_call(functools.partial(project_kernel, count), grid_spec=grid_s...  8.35 us
    dot_general x2, matrix products, weight_part(): lax.dot_general(block, gated_all, (((0,), (0,)), ((), ())), preferred_ele...  8.31 us
    ppermute x6, starting transfers between devices, swap_pairs(): return lax.ppermute(value, axis, [(i, i ^ distance) for i in range(count)])  4.85 us
  transfers between devices with their start and end apart: 15, of which 9 were waited for; matrix products, arithmetic and copies ran while one was open for 8% of the time, Pallas kernels for 10%

profile of v2, /device:TPU:2, one launch (start us, length us, event | category | flops | bytes accessed | tf_op | source)
XLA Modules:
  0.0 174.4 jit_solution(15444066910352679828)
XLA Ops:
  7.2 1.1 fusion.3
  8.4 3.5 %collective-permute-start.5 = (bf16[128,1024]{1,0:T(8,128)(2,1)S(1)}, bf16[128,1024]{1,0:T(8,128)(2,1)S(1)}, u32[]{:S(2)}, u32[]{:S(2)}) collective-permute-start(bf16[128,1024]{1,0:T(8,128)(2,1)S(1)} %fusion.3), channel_id=1, source_target_pairs={{0,8},{8,16},{16,24},{1,9},{9,17},{17,25},{2,10},{10,18},{18,26},{... | collective-permute-start | bytes 786440 | tf_op jit(solution)/shard_map/ppermute | solution.py:195
  17.5 1.9 %shard_map.183 = (f32[384,1024]{1,0:T(8,128)S(1)}, f32[384,1024]{1,0:T(8,128)S(1)}) custom-call(bf16[2,384,256]{2,1,0:T(8,128)(2,1)S(1)} %copy-done.17, bf16[2,384,128]{2,1,0:T(8,128)(2,1)S(1)} %copy-done.13, bf16[256,1024]{1,0:T(8,128)(2,1)S(1)} %bitcast.21, bf16[256,1024]{1,0:T(8,128)(2,1)S(1)} %bitcast.19, bf16[1024,128]{1,0:T(8,128)(2,1)S(1)} %copy-done.18, ...), custom_call_target="tpu_custom_call" | custom-call | flops 9437184 | bytes 69696 | tf_op jit(solution)/shard_map/pallas_call | solution.py:118
  19.5 4.5 %shard_map.184 = (f32[384,1024]{1,0:T(8,128)S(1)}, f32[256,1024]{1,0:T(8,128)S(1)}, bf16[256,1024]{1,0:T(8,128)(2,1)}) custom-call(bf16[2,384,128]{2,1,0:T(8,128)(2,1)S(1)} %copy-done.13, bf16[2,256,384]{2,1,0:T(8,128)(2,1)S(1)} %copy-done.15, bf16[128,1024]{1,0:T(8,128)(2,1)S(1)} %collective-permute-done.5.refs_2_, ...), custom_call_target="tpu_custom_call" | custom-call | flops 12582912 | bytes 110592 | tf_op jit(solution)/shard_map/pallas_call | solution.py:118
  23.9 1.1 copy-done.9
  26.2 1.6 collective-permute-start.1
  27.7 2.4 %collective-permute-start = (bf16[256,1024]{1,0:T(8,128)(2,1)S(1)}, bf16[256,1024]{1,0:T(8,128)(2,1)}, u32[]{:S(2)}, u32[]{:S(2)}) collective-permute-start(bf16[256,1024]{1,0:T(8,128)(2,1)S(1)} %bitcast.28), channel_id=1, source_target_pairs={{0,0},{1,4},{2,2},{3,6},{4,1},{5,5},{6,3},{7,7},{8,8},{9,12},{10,1... | collective-permute-start | bytes 1572872 | tf_op jit(solution)/shard_map/ppermute | solution.py:204
  30.1 9.5 %collective-permute-done.1 = bf16[256,1024]{1,0:T(8,128)(2,1)S(1)} collective-permute-done((bf16[256,1024]{1,0:T(8,128)(2,1)S(1)}, bf16[256,1024]{1,0:T(8,128)(2,1)S(1)}, u32[]{:S(2)}, u32[]{:S(2)}) %collective-permute-start.1) | collective-permute-done | bytes 524320 | tf_op jit(solution)/shard_map/ppermute | solution.py:204
  40.4 3.3 %collective-permute-done = bf16[256,1024]{1,0:T(8,128)(2,1)} collective-permute-done((bf16[256,1024]{1,0:T(8,128)(2,1)S(1)}, bf16[256,1024]{1,0:T(8,128)(2,1)}, u32[]{:S(2)}, u32[]{:S(2)}) %collective-permute-start) | collective-permute-done | bytes 524320 | tf_op jit(solution)/shard_map/ppermute | solution.py:204
  43.7 1.3 broadcast_select_fusion
  45.0 1.9 %collective-permute-start.11 = (bf16[256,1024]{1,0:T(8,128)(2,1)}, bf16[256,1024]{1,0:T(8,128)(2,1)}, u32[]{:S(2)}, u32[]{:S(2)}) collective-permute-start(bf16[256,1024]{1,0:T(8,128)(2,1)} %bitcast.26), channel_id=1, source_target_pairs={{0,0},{2,8},{4,16},{6,24},{8,2},{10,10},{12,18},{14,26},{16,4},{18... | collective-permute-start | bytes 1572872 | tf_op jit(solution)/shard_map/ppermute | solution.py:241
  46.9 47.5 %collective-permute-done.11 = bf16[256,1024]{1,0:T(8,128)(2,1)} collective-permute-done((bf16[256,1024]{1,0:T(8,128)(2,1)}, bf16[256,1024]{1,0:T(8,128)(2,1)}, u32[]{:S(2)}, u32[]{:S(2)}) %collective-permute-start.11) | collective-permute-done | bytes 524320 | tf_op jit(solution)/shard_map/ppermute | solution.py:241
  95.1 1.5 collective-permute-done.3.refs_1_
  96.6 2.2 %copy-done = bf16[1024,2048]{1,0:T(8,128)(2,1)S(1)} copy-done((bf16[1024,2048]{1,0:T(8,128)(2,1)S(1)}, bf16[1024,2048]{1,0:T(8,128)(2,1)}, u32[]{:S(2)}) %copy-start) | copy-done | bytes 4194328
  98.8 4.5 %shard_map.182 = bf16[256,1024]{1,0:T(8,128)(2,1)} custom-call(s32[2]{0:T(128)S(1)} %pad_add_fusion.which_ref, bf16[256,1024]{1,0:T(8,128)(2,1)S(1)} %get-tuple-element.34.refs_0_, bf16[256,1024]{1,0:T(8,128)(2,1)} %collective-permute-done.3.refs_1_, bf16[1024,2048]{1,0:T(8,128)(2,1)S(1)} %copy-done, bf16[1024,2048]{1,0:T(8,128)(2,1)S(1)} %copy-done), custom_call_target="tpu_custom_call" | custom-call | flops 1073741824 | bytes 5767168 | tf_op jit(solution)/shard_map/pallas_call | solution.py:140
  103.3 1.1 collective-permute-start.4
  104.4 2.2 %copy-done.1 = bf16[1024,2048]{1,0:T(8,128)(2,1)S(1)} copy-done((bf16[1024,2048]{1,0:T(8,128)(2,1)S(1)}, bf16[1024,2048]{1,0:T(8,128)(2,1)}, u32[]{:S(2)}) %copy-start.1) | copy-done | bytes 4194328
  106.6 3.8 %shard_map.181 = f32[256,1024]{1,0:T(8,128)S(1)} custom-call(s32[2]{0:T(128)S(1)} %pad_add_fusion.which_ref, bf16[256,1024]{1,0:T(8,128)(2,1)S(1)} %get-tuple-element.35.refs_0_, bf16[256,1024]{1,0:T(8,128)(2,1)} %collective-permute-done.2.refs_1_, bf16[1024,2048]{1,0:T(8,128)(2,1)S(1)} %copy-done.1, bf16[1024,2048]{1,0:T(8,128)(2,1)S(1)} %copy-done.1), custom_call_target="tpu_custom_call" | custom-call | flops 1073741824 | bytes 5767168 | tf_op jit(solution)/shard_map/pallas_call | solution.py:140
  110.5 7.1 %collective-permute-done.4 = bf16[256,1024]{1,0:T(8,128)(2,1)} collective-permute-done((bf16[256,1024]{1,0:T(8,128)(2,1)}, bf16[256,1024]{1,0:T(8,128)(2,1)}, u32[]{:S(2)}, u32[]{:S(2)}) %collective-permute-start.4) | collective-permute-done | bytes 524320 | tf_op jit(solution)/shard_map/ppermute | solution.py:155
  117.6 2.3 %multiply_convert_fusion = (bf16[256,1024]{1,0:T(8,128)(2,1)S(1)}, bf16[1,256,1024]{2,1,0:T(8,128)(2,1)}) fusion(f32[256,1024]{1,0:T(8,128)S(1)} %shard_map.181, bf16[256,1024]{1,0:T(8,128)(2,1)} %collective-permute-done.4, bf16[1,256,1024]{2,1,0:T(8,128)(2,1)S(1)} %copy-done.6, f32[256,1024]{1,0:T(8,128)S(1)} %copy-done.12), kind=kLoop, calls=%fused_computation.4 | loop fusion | flops 1835008 | bytes 4194304 | tf_op jit(solution)/shard_map/convert_element_type | solution.py:253
  120.0 3.1 %shard_map.185 = (f32[384,1024]{1,0:T(8,128)S(1)}, f32[128,1024]{1,0:T(8,128)S(1)}) custom-call(bf16[2,384,256]{2,1,0:T(8,128)(2,1)S(1)} %copy-done.16, bf16[2,128,384]{2,1,0:T(8,128)(2,1)S(1)} %copy-done.20, bf16[256,1024]{1,0:T(8,128)(2,1)S(1)} %get-tuple-element.32.refs_2_, f32[384,1024]{1,0:T(8,128)S(1)} %copy-done.10), custom_call_target="tpu_custom_call" | custom-call | flops 11010048 | bytes 65536 | tf_op jit(solution)/shard_map/pallas_call | solution.py:118
  123.1 1.1 copy-done.7
  124.3 1.2 collective-permute-start.7
  125.5 3.8 %collective-permute-done.7 = bf16[64,1024]{1,0:T(8,128)(2,1)S(1)} collective-permute-done((bf16[64,1024]{1,0:T(8,128)(2,1)S(1)}, bf16[64,1024]{1,0:T(8,128)(2,1)S(1)}, u32[]{:S(2)}, u32[]{:S(2)}) %collective-permute-start.7) | collective-permute-done | bytes 131104 | tf_op jit(solution)/shard_map/ppermute | solution.py:155
  130.5 4.2 %convolution_convert_fusion = bf16[512,1024]{1,0:T(8,128)(2,1)} fusion(bf16[1024,1024]{1,0:T(8,128)(2,1)} %all-gather.5.cloned.1.call-done, bf16[1024,1024]{1,0:T(8,128)(2,1)} %all-gather.3.cloned.1.call-done, s32[]{:T(128)S(6)} %select_n.68), kind=kOutput, calls=%fused_computation.1 | convolution fusion | flops 1074266112 | bytes 4194308 | tf_op jit(solution)/shard_map/dot_general | solution.py:291
  137.3 1.3 collective-permute-start.6
  138.5 6.6 %collective-permute-done.9 = bf16[64,1024]{1,0:T(8,128)(2,1)S(1)} collective-permute-done((bf16[64,1024]{1,0:T(8,128)(2,1)S(1)}, bf16[64,1024]{1,0:T(8,128)(2,1)S(1)}, u32[]{:S(2)}, u32[]{:S(2)}) %collective-permute-start.9) | collective-permute-done | bytes 131104 | tf_op jit(solution)/shard_map/ppermute | solution.py:155
  145.9 1.2 collective-permute-start.10
  147.1 1.4 copy-done.8
  149.5 4.4 %shard_map.186 = (bf16[256,1024]{1,0:T(8,128)(2,1)}, bf16[256,1024]{1,0:T(8,128)(2,1)}) custom-call(bf16[2,384,128]{2,1,0:T(8,128)(2,1)S(1)} %copy-done.19, bf16[2,256,384]{2,1,0:T(8,128)(2,1)S(1)} %copy-done.14, f32[384,1024]{1,0:T(8,128)S(1)} %copy-done.8, bf16[128,1024]{1,0:T(8,128)(2,1)S(1)} %collective-permute-done.6.refs_3_, ...), custom_call_target="tpu_custom_call" | custom-call | flops 12582912 | bytes 86016 | tf_op jit(solution)/shard_map/pallas_call | solution.py:118
  153.9 6.9 %collective-permute-done.10 = bf16[64,1024]{1,0:T(8,128)(2,1)} collective-permute-done((bf16[64,1024]{1,0:T(8,128)(2,1)}, bf16[64,1024]{1,0:T(8,128)(2,1)}, u32[]{:S(2)}, u32[]{:S(2)}) %collective-permute-start.10) | collective-permute-done | bytes 131104 | tf_op jit(solution)/shard_map/ppermute | solution.py:155
  163.5 4.1 %add_multiply_fusion = f32[512,1024]{1,0:T(8,128)} fusion(bf16[512,1024]{1,0:T(8,128)(2,1)} %collective-permute-done.12, bf16[1024,1024]{1,0:T(8,128)(2,1)S(1)} %copy-done.22, bf16[1024,1024]{1,0:T(8,128)(2,1)} %all-gather.3.cloned.1.call-done, s32[]{:T(128)S(6)} %select_n.67), kind=kOutput, calls=%fused_computation | convolution fusion | flops 1075314688 | bytes 6291460 | tf_op jit(solution)/shard_map/dot_general | solution.py:291
  (71 shorter events, 16.3 us)
Async XLA Ops:
  7.2 12.3 %copy-start.6 = (bf16[1,256,1024]{2,1,0:T(8,128)(2,1)S(1)}, bf16[1,256,1024]{2,1,0:T(8,128)(2,1)}, u32[]{:S(2)}) copy-start(bf16[1,256,1024]{2,1,0:T(8,128)(2,1)} %param.14) | copy-start | bytes 1572868
  7.2 123.3 %all-gather.5.cloned.1.call-start = ((), (), s32[]{:S(2)}) async-start(), calls=%async_computation.1 | async-start | bytes 2621440 | tf_op jit(solution)/shard_map/all_gather | solution.py:222
  8.4 11.0 %collective-permute-start.5 = (bf16[128,1024]{1,0:T(8,128)(2,1)S(1)}, bf16[128,1024]{1,0:T(8,128)(2,1)S(1)}, u32[]{:S(2)}, u32[]{:S(2)}) collective-permute-start(bf16[128,1024]{1,0:T(8,128)(2,1)S(1)} %fusion.3), channel_id=1, source_target_pairs={{0,8},{8,16},{16,24},{1,9},{9,17},{17,25},{2,10},{10,18},{18,26},{... | collective-permute-start | bytes 786440 | tf_op jit(solution)/shard_map/ppermute | solution.py:195
  11.9 1.0 copy-start.2
  17.5 1.9 %copy-start.15 = (bf16[2,256,384]{2,1,0:T(8,128)(2,1)S(1)}, bf16[2,256,384]{2,1,0:T(8,128)(2,1)}, u32[]{:S(2)}) copy-start(bf16[2,256,384]{2,1,0:T(8,128)(2,1)} %constant.72.clone.refs_1_) | copy-start | bytes 1179652
  19.4 6.7 %copy-start.24 = (bf16[1,256,1024]{2,1,0:T(8,128)(2,1)S(1)}, bf16[1,256,1024]{2,1,0:T(8,128)(2,1)}, u32[]{:S(2)}) copy-start(bf16[1,256,1024]{2,1,0:T(8,128)(2,1)} %param.20) | copy-start | bytes 1572868
  23.9 1.1 copy-start.9
  26.1 104.4 %all-gather.3.cloned.1.call-start = ((), (), s32[]{:S(2)}) async-start(), calls=%async_computation | async-start | bytes 2621440 | tf_op jit(solution)/shard_map/all_gather | solution.py:246
  26.2 13.4 %collective-permute-start.1 = (bf16[256,1024]{1,0:T(8,128)(2,1)S(1)}, bf16[256,1024]{1,0:T(8,128)(2,1)S(1)}, u32[]{:S(2)}, u32[]{:S(2)}) collective-permute-start(bf16[256,1024]{1,0:T(8,128)(2,1)S(1)} %bitcast.27), channel_id=1, source_target_pairs={{0,4},{1,0},{2,6},{3,2},{4,5},{5,1},{6,7},{7,3},{8,12},{9,8},{10,1... | collective-permute-start | bytes 1572872 | tf_op jit(solution)/shard_map/ppermute | solution.py:204
  27.7 16.0 %collective-permute-start = (bf16[256,1024]{1,0:T(8,128)(2,1)S(1)}, bf16[256,1024]{1,0:T(8,128)(2,1)}, u32[]{:S(2)}, u32[]{:S(2)}) collective-permute-start(bf16[256,1024]{1,0:T(8,128)(2,1)S(1)} %bitcast.28), channel_id=1, source_target_pairs={{0,0},{1,4},{2,2},{3,6},{4,1},{5,5},{6,3},{7,7},{8,8},{9,12},{10,1... | collective-permute-start | bytes 1572872 | tf_op jit(solution)/shard_map/ppermute | solution.py:204
  45.0 49.5 %collective-permute-start.11 = (bf16[256,1024]{1,0:T(8,128)(2,1)}, bf16[256,1024]{1,0:T(8,128)(2,1)}, u32[]{:S(2)}, u32[]{:S(2)}) collective-permute-start(bf16[256,1024]{1,0:T(8,128)(2,1)} %bitcast.26), channel_id=1, source_target_pairs={{0,0},{2,8},{4,16},{6,24},{8,2},{10,10},{12,18},{14,26},{16,4},{18... | collective-permute-start | bytes 1572872 | tf_op jit(solution)/shard_map/ppermute | solution.py:241
  94.5 2.1 %collective-permute-start.3 = (bf16[256,1024]{1,0:T(8,128)(2,1)S(1)}, bf16[256,1024]{1,0:T(8,128)(2,1)}, u32[]{:S(2)}, u32[]{:S(2)}) collective-permute-start(bf16[256,1024]{1,0:T(8,128)(2,1)S(1)} %get-tuple-element.34.refs_0_), channel_id=1, source_target_pairs={{0,2},{1,3},{2,0},{3,1},{4,6},{5,7},{6,4},{7,5},{8,10},{9,11},{10,... | collective-permute-start | bytes 1572872 | tf_op jit(solution)/shard_map/ppermute | solution.py:232
  94.7 9.8 %collective-permute-start.2 = (bf16[256,1024]{1,0:T(8,128)(2,1)S(1)}, bf16[256,1024]{1,0:T(8,128)(2,1)}, u32[]{:S(2)}, u32[]{:S(2)}) collective-permute-start(bf16[256,1024]{1,0:T(8,128)(2,1)S(1)} %get-tuple-element.35.refs_0_), channel_id=1, source_target_pairs={{0,2},{1,3},{2,0},{3,1},{4,6},{5,7},{6,4},{7,5},{8,10},{9,11},{10,... | collective-permute-start | bytes 1572872 | tf_op jit(solution)/shard_map/ppermute | solution.py:232
  96.6 2.2 %copy-start = (bf16[1024,2048]{1,0:T(8,128)(2,1)S(1)}, bf16[1024,2048]{1,0:T(8,128)(2,1)}, u32[]{:S(2)}) copy-start(bf16[1024,2048]{1,0:T(8,128)(2,1)} %refs_3_.3) | copy-start | bytes 12582916
  103.3 14.3 %collective-permute-start.4 = (bf16[256,1024]{1,0:T(8,128)(2,1)}, bf16[256,1024]{1,0:T(8,128)(2,1)}, u32[]{:S(2)}, u32[]{:S(2)}) collective-permute-start(bf16[256,1024]{1,0:T(8,128)(2,1)} %shard_map.182), channel_id=1, source_target_pairs={{0,1},{1,0},{2,3},{3,2},{4,5},{5,4},{6,7},{7,6},{8,9},{9,8},{10,11... | collective-permute-start | bytes 1572872 | tf_op jit(solution)/shard_map/ppermute | solution.py:155
  104.4 2.2 %copy-start.1 = (bf16[1024,2048]{1,0:T(8,128)(2,1)S(1)}, bf16[1024,2048]{1,0:T(8,128)(2,1)}, u32[]{:S(2)}) copy-start(bf16[1024,2048]{1,0:T(8,128)(2,1)} %refs_3_.3) | copy-start | bytes 12582916
  106.6 10.9 %copy-start.12 = (f32[256,1024]{1,0:T(8,128)S(1)}, f32[256,1024]{1,0:T(8,128)}, u32[]{:S(2)}) copy-start(f32[256,1024]{1,0:T(8,128)} %copy-done.11) | copy-start | bytes 3145732
  117.6 2.4 %copy-start.10 = (f32[384,1024]{1,0:T(8,128)S(1)}, f32[384,1024]{1,0:T(8,128)}, u32[]{:S(2)}) copy-start(f32[384,1024]{1,0:T(8,128)} %copy-done.9) | copy-start | bytes 4718596
  117.6 2.4 %copy-start.16 = (bf16[2,384,256]{2,1,0:T(8,128)(2,1)S(1)}, bf16[2,384,256]{2,1,0:T(8,128)(2,1)}, u32[]{:S(2)}) copy-start(bf16[2,384,256]{2,1,0:T(8,128)(2,1)} %constant.73.clone.refs_0_) | copy-start | bytes 1179652
  117.6 2.4 %copy-start.20 = (bf16[2,128,384]{2,1,0:T(8,128)(2,1)S(1)}, bf16[2,128,384]{2,1,0:T(8,128)(2,1)}, u32[]{:S(2)}) copy-start(bf16[2,128,384]{2,1,0:T(8,128)(2,1)} %constant.74.clone.refs_1_) | copy-start | bytes 589828
  123.1 1.1 copy-start.7
  124.3 5.0 %collective-permute-start.7 = (bf16[64,1024]{1,0:T(8,128)(2,1)S(1)}, bf16[64,1024]{1,0:T(8,128)(2,1)S(1)}, u32[]{:S(2)}, u32[]{:S(2)}) collective-permute-start(bf16[64,1024]{1,0:T(8,128)(2,1)S(1)} %dynamic-slice_convert_fusion), channel_id=1, source_target_pairs={{0,1},{1,0},{2,3},{3,2},{4,5},{5,4},{6,7},{7,6},{8,9},{9,8},{10,11... | collective-permute-start | bytes 393224 | tf_op jit(solution)/shard_map/ppermute | solution.py:155
  130.0 17.1 %copy-start.3 = (bf16[1,256,1024]{2,1,0:T(8,128)(2,1)S(1)}, bf16[1,256,1024]{2,1,0:T(8,128)(2,1)}, u32[]{:S(2)}) copy-start(bf16[1,256,1024]{2,1,0:T(8,128)(2,1)} %param.16) | copy-start | bytes 1572868
  130.0 17.1 %copy-start.5 = (bf16[1,256,1024]{2,1,0:T(8,128)(2,1)S(1)}, bf16[1,256,1024]{2,1,0:T(8,128)(2,1)}, u32[]{:S(2)}) copy-start(bf16[1,256,1024]{2,1,0:T(8,128)(2,1)} %param.15) | copy-start | bytes 1572868
  130.0 17.1 %copy-start.14 = (bf16[2,256,384]{2,1,0:T(8,128)(2,1)S(1)}, bf16[2,256,384]{2,1,0:T(8,128)(2,1)}, u32[]{:S(2)}) copy-start(bf16[2,256,384]{2,1,0:T(8,128)(2,1)} %constant.76.clone.refs_1_) | copy-start | bytes 1179652
  130.0 5.5 %collective-permute-start.8 = (bf16[64,1024]{1,0:T(8,128)(2,1)}, bf16[64,1024]{1,0:T(8,128)(2,1)}, u32[]{:S(2)}, u32[]{:S(2)}) collective-permute-start(bf16[64,1024]{1,0:T(8,128)(2,1)} %add_convert_fusion.2), channel_id=1, source_target_pairs={{0,8},{8,0},{16,24},{24,16},{1,9},{9,1},{17,25},{25,17},{2,10},{10... | collective-permute-start | bytes 393224 | tf_op jit(solution)/shard_map/ppermute | solution.py:155
  134.7 28.8 %collective-permute-start.12 = (bf16[512,1024]{1,0:T(8,128)(2,1)}, bf16[512,1024]{1,0:T(8,128)(2,1)}, u32[]{:S(2)}, u32[]{:S(2)}) collective-permute-start(bf16[512,1024]{1,0:T(8,128)(2,1)} %convolution_convert_fusion), channel_id=1, source_target_pairs={{0,1},{1,0},{2,3},{3,2},{4,5},{5,4},{6,7},{7,6},{8,9},{9,8},{10,11... | collective-permute-start | bytes 3145736 | tf_op jit(solution)/shard_map/ppermute | solution.py:155
  136.5 8.7 %collective-permute-start.9 = (bf16[64,1024]{1,0:T(8,128)(2,1)S(1)}, bf16[64,1024]{1,0:T(8,128)(2,1)S(1)}, u32[]{:S(2)}, u32[]{:S(2)}) collective-permute-start(bf16[64,1024]{1,0:T(8,128)(2,1)S(1)} %add_convert_fusion.1), channel_id=1, source_target_pairs={{0,16},{8,24},{16,0},{24,8},{1,17},{9,25},{17,1},{25,9},{2,18},{10... | collective-permute-start | bytes 393224 | tf_op jit(solution)/shard_map/ppermute | solution.py:155
  137.3 9.9 %collective-permute-start.6 = (bf16[128,1024]{1,0:T(8,128)(2,1)}, bf16[128,1024]{1,0:T(8,128)(2,1)S(1)}, u32[]{:S(2)}, u32[]{:S(2)}) collective-permute-start(bf16[128,1024]{1,0:T(8,128)(2,1)} %slice.18), channel_id=1, source_target_pairs={{8,0},{16,8},{24,16},{9,1},{17,9},{25,17},{10,2},{18,10},{26,18},{... | collective-permute-start | bytes 786440 | tf_op jit(solution)/shard_map/ppermute | solution.py:254
  145.9 15.0 %collective-permute-start.10 = (bf16[64,1024]{1,0:T(8,128)(2,1)}, bf16[64,1024]{1,0:T(8,128)(2,1)}, u32[]{:S(2)}, u32[]{:S(2)}) collective-permute-start(bf16[64,1024]{1,0:T(8,128)(2,1)} %add_convert_fusion), channel_id=1, source_target_pairs={{0,1},{1,0},{2,3},{3,2},{4,5},{5,4},{6,7},{7,6},{8,9},{9,8},{10,11... | collective-permute-start | bytes 393224 | tf_op jit(solution)/shard_map/ppermute | solution.py:155
  147.1 1.4 copy-start.8
  153.9 9.6 %copy-start.22 = (bf16[1024,1024]{1,0:T(8,128)(2,1)S(1)}, bf16[1024,1024]{1,0:T(8,128)(2,1)}, u32[]{:S(2)}) copy-start(bf16[1024,1024]{1,0:T(8,128)(2,1)} %all-gather.5.cloned.1.call-done) | copy-start | bytes 6291460
  (8 other events, 7.3 us)
Sparse Core Ops, SparseCore 0:
  26.2 53.8 all-gather.4
  94.6 21.8 all-gather.2

commit v3 on v2

--- a/solution.py
+++ b/solution.py
@@ -75,13 +75,22 @@
     spec_ref[...] = spec
     state = inverse_transform(synth, spectrum_product(spec, filt_ref[...], False))
     state_ref[...] = state
-    gated_ref[...] = (query_ref[...].astype(f32) * state).astype(bf16)
-
-
-def project_kernel(count, which_ref, *refs):
+    gated_ref[0] = (query_ref[...].astype(f32) * state).astype(bf16)
+
+
+def project_kernel(place_ref, first_mine, second_mine, first_theirs, second_theirs, weight_mine, weight_theirs, out_ref):
+    def write(mine, theirs):
+        total = dot_nt(mine[...], weight_mine[...]) + dot_nt(theirs[...], weight_theirs[...])
+        out_ref[...] = total.astype(out_ref.dtype)
+
+    pl.when(place_ref[0] == 0)(lambda: write(first_mine, first_theirs))
+    pl.when(place_ref[0] != 0)(lambda: write(second_mine, second_theirs))
+
+
+def weight_kernel(count, place_ref, *refs):
     total = None
-    for piece_ref, weight_ref in zip(refs[:count], refs[count : 2 * count]):
-        part = dot_nt(piece_ref[...], weight_ref[...])
+    for cot_ref, gated_ref in zip(refs[:count], refs[count : 2 * count]):
+        part = dot(cot_ref[0], gated_ref[0])
         total = part if total is None else total + part
     refs[-1][...] = total.astype(refs[-1].dtype)
 
@@ -99,55 +108,82 @@
     grad_value_ref[...] = (back * key_ref[...].astype(f32)).astype(bf16)
 
 
+def estimate(flops, arrays):
+    moved = sum(a.size * jnp.dtype(a.dtype).itemsize for a in arrays)
+    return pl.CostEstimate(flops=flops // 64, bytes_accessed=moved // 64, transcendentals=0)
+
+
 def by_channel(kernel, tables, args, outs, channels, flops):
-    count = len(tables)
-
-    def body(*refs):
-        kernel(*refs)
-
-    def column_spec(shape, by_row):
-        if by_row:
+    def column_spec(shape):
+        if len(shape) == 3:
+            per = shape[2] // lanes
+            return pl.BlockSpec((1, shape[1], lanes), lambda i: (i // per, 0, i % per))
+        if shape[1] != channels:
             return pl.BlockSpec((lanes, shape[1]), lambda i: (i, 0))
         return pl.BlockSpec((shape[0], lanes), lambda i: (0, i))
 
-    specs = [pl.BlockSpec(t.shape, lambda i: (0, 0, 0)) for t in tables]
-    specs += [column_spec(a.shape, a.shape[1] != channels) for a in args]
-    moved = sum(a.size * a.dtype.itemsize for a in args) + sum(
-        o.size * jnp.dtype(o.dtype).itemsize for o in outs
-    )
     return pl.pallas_call(
-        body,
+        kernel,
         grid=(channels // lanes,),
-        in_specs=specs,
-        out_specs=[column_spec(o.shape, False) for o in outs],
+        in_specs=[pl.BlockSpec(t.shape, lambda i: (0, 0, 0)) for t in tables]
+        + [column_spec(a.shape) for a in args],
+        out_specs=[column_spec(o.shape) for o in outs],
         out_shape=outs,
         compiler_params=pltpu.CompilerParams(vmem_limit_bytes=vmem_bytes),
-        cost_estimate=pl.CostEstimate(flops=flops // 64, bytes_accessed=moved // 64, transcendentals=0),
+        cost_estimate=estimate(flops, [*args, *outs]),
     )(*[jnp.asarray(t) for t in tables], *args)
 
 
-def project(pieces, places, out_weight, dtype):
-    count = len(pieces)
-    length, width = pieces[0].shape
+def project(places, firsts, seconds, out_weight, dtype):
+    length, width = firsts[0].shape
     channels = out_weight.shape[0]
+    out = jax.ShapeDtypeStruct((length, channels), dtype)
+    pieces = [firsts[0], seconds[0], firsts[1], seconds[1]]
     grid_spec = pltpu.PrefetchScalarGridSpec(
         num_scalar_prefetch=1,
         grid=(channels // lanes,),
-        in_specs=[pl.BlockSpec((length, width), lambda i, w: (0, 0))] * count
-        + [pl.BlockSpec((lanes, width), functools.partial(lambda n, i, w: (i, w[n]), n)) for n in range(count)],
+        in_specs=[pl.BlockSpec((length, width), lambda i, w: (0, 0))] * 4
+        + [
+            pl.BlockSpec((lanes, width), lambda i, w: (i, w[1])),
+            pl.BlockSpec((lanes, width), lambda i, w: (i, w[2])),
+        ],
         out_specs=pl.BlockSpec((length, lanes), lambda i, w: (0, i)),
     )
     return pl.pallas_call(
-        functools.partial(project_kernel, count),
+        project_kernel,
         grid_spec=grid_spec,
-        out_shape=jax.ShapeDtypeStruct((length, channels), dtype),
+        out_shape=out,
         compiler_params=pltpu.CompilerParams(vmem_limit_bytes=vmem_bytes),
-        cost_estimate=pl.CostEstimate(
-            flops=2 * length * channels * out_weight.shape[1],
-            bytes_accessed=out_weight.size * 2 + length * channels * 6,
-            transcendentals=0,
-        ),
-    )(jnp.stack(places).astype(jnp.int32), *pieces, *([out_weight] * count))
+        cost_estimate=estimate(2 * length * out_weight.size, [*pieces, out_weight, out]),
+    )(places, *pieces, out_weight, out_weight)
+
+
+def weight_sum(places, cot_pieces, gated_pieces, half, rows, dtype):
+    count = len(gated_pieces)
+    _, length, width = gated_pieces[0].shape
+    out = jax.ShapeDtypeStruct((rows, width), dtype)
+
+    def cot_spec(n):
+        return pl.BlockSpec((1, rows, length), lambda i, w: (w[n], w[count], 0))
+
+    def gated_spec(piece):
+        place = half if piece.shape[0] > 1 else 0
+        return pl.BlockSpec((1, length, lanes), lambda i, w: (place, 0, i))
+
+    grid_spec = pltpu.PrefetchScalarGridSpec(
+        num_scalar_prefetch=1,
+        grid=(width // lanes,),
+        in_specs=[cot_spec(n) for n in range(count)]
+        + [gated_spec(piece) for piece in gated_pieces],
+        out_specs=pl.BlockSpec((rows, lanes), lambda i, w: (0, i)),
+    )
+    return pl.pallas_call(
+        functools.partial(weight_kernel, count),
+        grid_spec=grid_spec,
+        out_shape=out,
+        compiler_params=pltpu.CompilerParams(vmem_limit_bytes=vmem_bytes),
+        cost_estimate=estimate(2 * count * length * rows * width, [cot_pieces, *gated_pieces, out]),
+    )(places, *([cot_pieces] * count), *gated_pieces)
 
 
 def swap_pairs(value, axis, distance):
@@ -202,6 +238,13 @@
     for turn in range(2):
         route = [(tp_dp(h, c, d), tp_dp(d ^ turn, c, h)) for h, c, d in places]
         rounds.append(lax.ppermute(cot, ("tp", "dp"), route))
+    square = n_seq == n_tp
+    if square:
+        holder = [(s % n_dp) * subs + s // n_dp for s in range(n_seq)]
+        route = [(s * n_tp + t, t * n_tp + holder[s]) for s in range(n_seq) for t in range(n_tp)]
+        moved = lax.ppermute(cot.T, ("seq", "tp"), route)
+    else:
+        moved = cot
 
     own_spec, filt = by_channel(
         functools.partial(prepare_kernel, scale),
@@ -211,42 +254,75 @@
         channels,
         2 * unit * (length + taps),
     )
+    prior, moved, own_spec, filt, *rounds = lax.optimization_barrier(
+        (prior, moved, own_spec, filt, *rounds)
+    )
     mixed_spec, state, gated = by_channel(
         state_kernel,
         [tap_table, synth_fwd],
         [prior, own_spec, filt, queries],
-        [spectrum, rows32, rows16],
+        [spectrum, rows32, jax.ShapeDtypeStruct((2, length, channels // 2), bf16)],
         channels,
         unit * (2 * taps + 3 * length),
     )
-    gated_all = lax.all_gather(gated, "seq", axis=0, tiled=True)
-
-    same = me_half == me_dp
-    other_cot = jnp.where(same, rounds[1], rounds[0])
-    own_cot = jnp.where(same, rounds[0], rounds[1])
-
-    def from_subs(piece):
-        pieces = [piece]
-        for shift in range(1, subs):
-            route = [(tp_dp(h, c, d), tp_dp(h, (c + shift) % subs, d)) for h, c, d in places]
-            pieces.append(lax.ppermute(piece, ("tp", "dp"), route))
-        return pieces
-
-    weight_places = [(me_sub - shift + subs) % subs for shift in range(subs)]
-    other_sent = project(from_subs(other_cot), weight_places, out_weight, bf16)
+
+    route = [(tp_dp(h, c, d), tp_dp(h, (c + 1) % subs, d)) for h, c, d in places]
+    theirs = [lax.ppermute(r, ("tp", "dp"), route) for r in rounds]
+    gated, *theirs = lax.optimization_barrier((gated, *theirs))
+    firsts, seconds = zip(rounds, theirs)
+    same = (me_half == me_dp).astype(jnp.int32)
+    subs_of = [me_sub, (me_sub + 1) % subs]
+    other_sent = project(jnp.stack([same, *subs_of]).astype(jnp.int32), firsts, seconds, out_weight, bf16)
     other_part = swap_pairs(other_sent, "dp", 1)
-    own_part = project(from_subs(own_cot), weight_places, out_weight, f32)
-
-    if n_seq == n_tp:
-        moved = lax.ppermute(
-            after(cot, other_cot),
-            ("seq", "tp"),
-            [(s * n_tp + t, t * n_tp + s) for s in range(n_seq) for t in range(n_tp)],
-        )
-        cot_all = lax.all_gather(moved, "tp", axis=0, tiled=True)
+
+    rows = n_tp * channels // (n_seq * n_dp)
+    own_place = jnp.stack([1 - same, *subs_of]).astype(jnp.int32)
+    if square:
+        order = [*range(0, n_seq, 2), *reversed(range(1, n_seq, 2))]
+        ring = [(order[k], order[(k + 1) % n_seq]) for k in range(n_seq)]
+        pieces = [gated, lax.ppermute(gated, "seq", ring)]
+        pieces[1], own_place = lax.optimization_barrier((pieces[1], own_place))
+    own_part = project(own_place, firsts, seconds, out_weight, f32)
+
+    if square:
+        cot_pieces = lax.all_gather(moved, "tp", axis=0)
+        table = np.zeros((n_seq, n_seq), np.int32)
+        for k, s in enumerate(order):
+            table[s] = [holder[order[k - r]] for r in range(n_seq)]
+        sources = jnp.asarray(table)[lax.axis_index("seq")]
+        for _ in range(n_seq - 3):
+            pieces.append(lax.ppermute(pieces[-1], "seq", ring))
+
+        def weight_half(half):
+            held = [*pieces, lax.ppermute(pieces[-1][half : half + 1], "seq", ring)]
+
+            def part(replica, dtype):
+                where = jnp.concatenate([sources, replica[None].astype(jnp.int32)])
+                return weight_sum(where, cot_pieces, held, half, rows, dtype)
+
+            sent = swap_pairs(part(1 - me_dp, bf16), "dp", 1)
+            return (part(me_dp, f32) + sent.astype(f32)) * norm_factor
+
+        def weight_all():
+            return jnp.concatenate([weight_half(0), weight_half(1)], axis=1)
+
     else:
         full = lax.all_gather(cot, "tp", axis=1, tiled=True)
         cot_all = lax.all_to_all(full, "seq", 1, 0, tiled=True)
+        gated_all = lax.all_gather(gated, "seq", axis=1, tiled=True)
+
+        def part(replica, piece):
+            block = lax.dynamic_slice_in_dim(cot_all, replica * rows, rows, axis=1)
+            return lax.dot_general(
+                block, piece, (((0,), (0,)), ((), ())), preferred_element_type=f32
+            )
+
+        def weight_one(piece):
+            sent = swap_pairs(part(1 - me_dp, piece).astype(bf16), "dp", 1)
+            return (part(me_dp, piece) + sent.astype(f32)) * norm_factor
+
+        def weight_all():
+            return jnp.concatenate([weight_one(gated_all[0]), weight_one(gated_all[1])], axis=1)
 
     grad_gated = own_part + other_part.astype(f32)
     grad_query = (grad_gated * state).astype(bf16)
@@ -260,6 +336,8 @@
         channels,
         unit * (2 * length + 3 * taps),
     )
+    if square:
+        later, *pieces = lax.optimization_barrier((later, *pieces))
     grad_key, grad_value = by_channel(
         back_kernel,
         [late_table, synth_bwd],
@@ -273,6 +351,7 @@
     lag_sum = lax.dynamic_slice_in_dim(lags, me_dp * share, share, axis=0) + swap_pairs(
         lax.dynamic_slice_in_dim(lags, (1 - me_dp) * share, share, axis=0).astype(bf16), "dp", 1
     ).astype(f32)
+    lag_sum, grad_key, grad_value = lax.optimization_barrier((lag_sum, grad_key, grad_value))
     distance = 1
     while distance < n_seq:
         rounded = lag_sum.astype(bf16)
@@ -284,16 +363,7 @@
     lag_sum = jnp.concatenate([jnp.where(first, mine, theirs), jnp.where(first, theirs, mine)], axis=0)
     grad_filter = lag_sum.astype(f32).T * (norm_factor * scale)
 
-    rows = cot_all.shape[1] // n_dp
-
-    def weight_part(replica):
-        block = lax.dynamic_slice_in_dim(cot_all, replica * rows, rows, axis=1)
-        return lax.dot_general(
-            block, gated_all, (((0,), (0,)), ((), ())), preferred_element_type=f32
-        )
-
-    sent = swap_pairs(weight_part(1 - me_dp).astype(bf16), "dp", 1)
-    grad_weight = (weight_part(me_dp) + sent.astype(f32)) * norm_factor
+    grad_weight = weight_all()
     return (
         grad_query[None],
         grad_key[None],

time: 175 us -> 159 us (0.909)
  the two profiles are of different devices: /device:TPU:2 before, /device:TPU:10 now
where the time goes in v3:
time: 159 us; the launch traced here: 158 us
  local copies, waits for them, and re-layouts  36.4 us (23%)
  waiting for transfers between devices  36.3 us (23%)
  Pallas kernels  32.3 us (20%)
  starting transfers between devices  26 us (16%)
  between operations  14.4 us (9%)
  other arithmetic  12.1 us (8%)
    unnamed x77, local copies, waits for them, and re-layouts  28.8 us
    pallas_call x4, Pallas kernels, by_channel(): pl.pallas_call(kernel, grid=(channels // lanes,), in_specs=[pl.BlockSpec(...  14.1 us
    ppermute x1, waiting for transfers between devices, per_device(): prior = lax.ppermute(tail, 'seq', [(i, i + 1) for i in range(n_seq - 1)])  13.8 us
    ppermute x7, waiting for transfers between devices, swap_pairs(): return lax.ppermute(value, axis, [(i, i ^ distance) for i in range(count)])  11.1 us
    pallas_call x4, Pallas kernels, weight_sum(): pl.pallas_call(functools.partial(weight_kernel, count), grid_spec=grid_sp...  9.44 us
    pallas_call x2, Pallas kernels, project(): pl.pallas_call(project_kernel, grid_spec=grid_spec, out_shape=out, compil...  8.83 us
    ppermute x7, starting transfers between devices, swap_pairs(): return lax.ppermute(value, axis, [(i, i ^ distance) for i in range(count)])  8.71 us
    ppermute x1, waiting for transfers between devices, per_device(): pieces = [gated, lax.ppermute(gated, 'seq', ring)]  7.51 us
  transfers between devices with their start and end apart: 19, of which 7 were waited for; matrix products, arithmetic and copies ran while one was open for 12% of the time, Pallas kernels for 21%

profile of v3, /device:TPU:10, one launch (start us, length us, event | category | flops | bytes accessed | tf_op | source)
XLA Modules:
  0.0 157.5 jit_solution(16946483369611228142)
XLA Ops:
  7.2 3.6 %collective-permute-start.1 = (bf16[1024,256]{0,1:T(8,128)(2,1)}, bf16[1024,256]{0,1:T(8,128)(2,1)}, u32[]{:S(2)}, u32[]{:S(2)}) collective-permute-start(bf16[1024,256]{0,1:T(8,128)(2,1)} %bitcast.49), channel_id=1, source_target_pairs={{0,0},{2,8},{4,16},{6,24},{8,4},{10,12},{12,20},{14,28},{16,2},{18... | collective-permute-start | bytes 1572872 | tf_op jit(solution)/shard_map/ppermute | solution.py:245
  10.8 3.2 %collective-permute-start.2 = (bf16[256,1024]{1,0:T(8,128)(2,1)}, bf16[256,1024]{1,0:T(8,128)(2,1)S(1)}, u32[]{:S(2)}, u32[]{:S(2)}) collective-permute-start(bf16[256,1024]{1,0:T(8,128)(2,1)} %bitcast.50), channel_id=1, source_target_pairs={{0,0},{1,4},{2,2},{3,6},{4,1},{5,5},{6,3},{7,7},{8,8},{9,12},{10,1... | collective-permute-start | bytes 1572872 | tf_op jit(solution)/shard_map/ppermute | solution.py:240
  15.2 2.1 %collective-permute-start = (bf16[128,1024]{1,0:T(8,128)(2,1)S(1)}, bf16[128,1024]{1,0:T(8,128)(2,1)S(1)}, u32[]{:S(2)}, u32[]{:S(2)}) collective-permute-start(bf16[128,1024]{1,0:T(8,128)(2,1)S(1)} %fusion.1), channel_id=1, source_target_pairs={{0,8},{8,16},{16,24},{1,9},{9,17},{17,25},{2,10},{10,18},{18,26},{... | collective-permute-start | bytes 786440 | tf_op jit(solution)/shard_map/ppermute | solution.py:231
  23.0 1.9 %shard_map.190 = (f32[384,1024]{1,0:T(8,128)S(1)}, f32[384,1024]{1,0:T(8,128)S(1)}) custom-call(bf16[2,384,256]{2,1,0:T(8,128)(2,1)S(1)} %copy-done.30, bf16[2,384,128]{2,1,0:T(8,128)(2,1)S(1)} %copy-done.25, bf16[256,1024]{1,0:T(8,128)(2,1)S(1)} %bitcast.44, bf16[256,1024]{1,0:T(8,128)(2,1)S(1)} %bitcast.42, bf16[1024,128]{1,0:T(8,128)(2,1)S(1)} %copy-done.34, ...), custom_call_target="tpu_custom_call" | custom-call | flops 9437184 | bytes 69696 | tf_op jit(solution)/shard_map/pallas_call | solution.py:125
  26.0 13.8 %collective-permute-done.prior_ref = bf16[128,1024]{1,0:T(8,128)(2,1)S(1)} collective-permute-done((bf16[128,1024]{1,0:T(8,128)(2,1)S(1)}, bf16[128,1024]{1,0:T(8,128)(2,1)S(1)}, u32[]{:S(2)}, u32[]{:S(2)}) %collective-permute-start) | collective-permute-done | bytes 262176 | tf_op jit(solution)/shard_map/ppermute | solution.py:231
  41.8 1.4 copy-done.20
  45.1 4.0 %shard_map.191 = (f32[384,1024]{1,0:T(8,128)S(1)}, f32[256,1024]{1,0:T(8,128)S(1)}, bf16[2,256,512]{2,1,0:T(8,128)(2,1)S(1)}) custom-call(bf16[2,384,128]{2,1,0:T(8,128)(2,1)S(1)} %copy-done.26, bf16[2,256,384]{2,1,0:T(8,128)(2,1)S(1)} %copy-done.28, bf16[128,1024]{1,0:T(8,128)(2,1)S(1)} %copy-done.33, f32[384,1024]{1,0:T(8,128)S(1)} %copy-done.20, ...), custom_call_target="tpu_custom_call" | custom-call | flops 12582912 | bytes 110592 | tf_op jit(solution)/shard_map/pallas_call | solution.py:125
  51.7 4.7 %shard_map.193 = bf16[256,1024]{1,0:T(8,128)(2,1)} custom-call(s32[3]{0:T(128)S(1)} %add_add_fusion.1.place_ref, bf16[256,1024]{1,0:T(8,128)(2,1)S(1)} %collective-permute-done.2.first_mine, bf16[256,1024]{1,0:T(8,128)(2,1)S(1)} %copy-done.13, bf16[256,1024]{1,0:T(8,128)(2,1)} %collective-permute-done.4.first_theirs, ...), custom_call_target="tpu_custom_call" | custom-call | flops 16777216 | bytes 106496 | tf_op jit(solution)/shard_map/pallas_call | solution.py:152
  56.4 1.5 collective-permute-start.7
  58.0 7.5 %collective-permute-done.6.refs_5_ = bf16[2,256,512]{2,1,0:T(8,128)(2,1)S(1)} collective-permute-done((bf16[2,256,512]{2,1,0:T(8,128)(2,1)S(1)}, bf16[2,256,512]{2,1,0:T(8,128)(2,1)S(1)}, u32[]{:S(2)}, u32[]{:S(2)}) %collective-permute-start.6) | collective-permute-done | bytes 524320 | tf_op jit(solution)/shard_map/ppermute | solution.py:283
  65.8 2.2 %copy-done.1 = bf16[1024,2048]{1,0:T(8,128)(2,1)S(1)} copy-done((bf16[1024,2048]{1,0:T(8,128)(2,1)S(1)}, bf16[1024,2048]{1,0:T(8,128)(2,1)}, u32[]{:S(2)}) %copy-start.1) | copy-done | bytes 4194328
  70.1 4.1 %shard_map.192 = f32[256,1024]{1,0:T(8,128)S(1)} custom-call(s32[3]{0:T(128)S(1)} %add_add_fusion.place_ref, bf16[256,1024]{1,0:T(8,128)(2,1)S(1)} %copy-done.11, bf16[256,1024]{1,0:T(8,128)(2,1)S(1)} %copy-done.14, bf16[256,1024]{1,0:T(8,128)(2,1)} %collective-permute-done.4.first_theirs, bf16[256,1024]{1,0:T(8,128)(2,1)} %collective-permute-done.5.second_theirs, ...), custom_call_target="tpu_custom_call" | custom-call | flops 16777216 | bytes 114688 | tf_op jit(solution)/shard_map/pallas_call | solution.py:152
  74.3 2.4 %multiply_convert_fusion = (bf16[256,1024]{1,0:T(8,128)(2,1)S(1)}, bf16[1,256,1024]{2,1,0:T(8,128)(2,1)}) fusion(f32[256,1024]{1,0:T(8,128)S(1)} %shard_map.192, bf16[256,1024]{1,0:T(8,128)(2,1)} %collective-permute-done.7, bf16[1,256,1024]{2,1,0:T(8,128)(2,1)S(1)} %copy-done.16, f32[256,1024]{1,0:T(8,128)S(1)} %copy-done.24), kind=kLoop, calls=%fused_computation.3 | loop fusion | flops 1835008 | bytes 4194304 | tf_op jit(solution)/shard_map/convert_element_type | solution.py:329
  76.7 3.1 %shard_map.194 = (f32[384,1024]{1,0:T(8,128)S(1)}, f32[128,1024]{1,0:T(8,128)S(1)}) custom-call(bf16[2,384,256]{2,1,0:T(8,128)(2,1)S(1)} %copy-done.29, bf16[2,128,384]{2,1,0:T(8,128)(2,1)S(1)} %copy-done.36, bf16[256,1024]{1,0:T(8,128)(2,1)S(1)} %get-tuple-element.66.signal_ref, f32[384,1024]{1,0:T(8,128)S(1)} %copy-done.22), custom_call_target="tpu_custom_call" | custom-call | flops 11010048 | bytes 65536 | tf_op jit(solution)/shard_map/pallas_call | solution.py:125
  81.7 1.5 collective-permute-start.8
  83.9 5.3 %collective-permute-start.9 = (bf16[128,1024]{1,0:T(8,128)(2,1)}, bf16[128,1024]{1,0:T(8,128)(2,1)}, u32[]{:S(2)}, u32[]{:S(2)}) collective-permute-start(bf16[128,1024]{1,0:T(8,128)(2,1)} %slice.26), channel_id=1, source_target_pairs={{8,0},{16,8},{24,16},{9,1},{17,9},{25,17},{10,2},{18,10},{26,18},{... | collective-permute-start | bytes 786440 | tf_op jit(solution)/shard_map/ppermute | solution.py:330
  90.3 3.7 %collective-permute-done.9.later_ref = bf16[128,1024]{1,0:T(8,128)(2,1)} collective-permute-done((bf16[128,1024]{1,0:T(8,128)(2,1)}, bf16[128,1024]{1,0:T(8,128)(2,1)}, u32[]{:S(2)}, u32[]{:S(2)}) %collective-permute-start.9) | collective-permute-done | bytes 262176 | tf_op jit(solution)/shard_map/ppermute | solution.py:330
  96.1 1.4 copy-done.18
  98.5 5.1 %shard_map.195 = (bf16[256,1024]{1,0:T(8,128)(2,1)}, bf16[256,1024]{1,0:T(8,128)(2,1)}) custom-call(bf16[2,384,128]{2,1,0:T(8,128)(2,1)S(1)} %copy-done.35, bf16[2,256,384]{2,1,0:T(8,128)(2,1)S(1)} %copy-done.27, f32[384,1024]{1,0:T(8,128)S(1)} %copy-done.18, bf16[128,1024]{1,0:T(8,128)(2,1)} %collective-permute-done.9.later_ref, ...), custom_call_target="tpu_custom_call" | custom-call | flops 12582912 | bytes 86016 | tf_op jit(solution)/shard_map/pallas_call | solution.py:125
  103.6 2.5 %collective-permute-start.11 = (bf16[64,1024]{1,0:T(8,128)(2,1)S(1)}, bf16[64,1024]{1,0:T(8,128)(2,1)S(1)}, u32[]{:S(2)}, u32[]{:S(2)}) collective-permute-start(bf16[64,1024]{1,0:T(8,128)(2,1)S(1)} %convert_add_fusion.1), channel_id=1, source_target_pairs={{0,8},{8,0},{16,24},{24,16},{1,9},{9,1},{17,25},{25,17},{2,10},{10... | collective-permute-start | bytes 393224 | tf_op jit(solution)/shard_map/ppermute | solution.py:191
  106.9 3.6 %collective-permute-done.11 = bf16[64,1024]{1,0:T(8,128)(2,1)S(1)} collective-permute-done((bf16[64,1024]{1,0:T(8,128)(2,1)S(1)}, bf16[64,1024]{1,0:T(8,128)(2,1)S(1)}, u32[]{:S(2)}, u32[]{:S(2)}) %collective-permute-start.11) | collective-permute-done | bytes 131104 | tf_op jit(solution)/shard_map/ppermute | solution.py:191
  111.9 2.0 %collective-permute-start.14 = (bf16[1,256,512]{2,1,0:T(8,128)(2,1)}, bf16[1,256,512]{2,1,0:T(8,128)(2,1)}, u32[]{:S(2)}, u32[]{:S(2)}) collective-permute-start(bf16[1,256,512]{2,1,0:T(8,128)(2,1)} %get-tuple-element.68), channel_id=1, source_target_pairs={{0,16},{16,24},{24,8},{8,0},{1,17},{17,25},{25,9},{9,1},{2,18},{18... | collective-permute-start | bytes 786440 | tf_op jit(solution)/shard_map/ppermute | solution.py:297
  113.9 3.3 %copy.21 = bf16[4096,256]{1,0:T(8,128)(2,1)S(1)} copy(bf16[4096,256]{0,1:T(8,128)(2,1)} %all-gather.3.cloned.1.call-done) | data formatting | bytes 4194304 | tf_op jit(solution)/shard_map/all_gather | solution.py:288
  118.4 2.3 %shard_map.199 = bf16[512,512]{1,0:T(8,128)(2,1)} custom-call(s32[5]{0:T(128)S(1)} %get-tuple-element.72.place_ref, bf16[4,1024,256]{2,1,0:T(8,128)(2,1)S(1)} %bitcast.26, bf16[4,1024,256]{2,1,0:T(8,128)(2,1)S(1)} %bitcast.27, bf16[4,1024,256]{2,1,0:T(8,128)(2,1)S(1)} %bitcast.28, bf16[4,1024,256]{2,1,0:T(8,128)(2,1)S(1)} %bitcast.29, ...), custom_call_target="tpu_custom_call" | custom-call | flops 8388608 | bytes 69632 | tf_op jit(solution)/shard_map/pallas_call | solution.py:180
  122.5 1.6 %add_convert_fusion = bf16[64,1024]{1,0:T(8,128)(2,1)} fusion(bf16[64,1024]{1,0:T(8,128)(2,1)} %collective-permute-done.12, bf16[64,1024]{1,0:T(8,128)(2,1)S(1)} %add_convert_fusion.1), kind=kLoop, calls=%fused_computation.10 | loop fusion | flops 262144 | bytes 393216 | tf_op jit(solution)/shard_map/convert_element_type | solution.py:360
  125.6 3.1 %shard_map.197 = bf16[512,512]{1,0:T(8,128)(2,1)} custom-call(s32[5]{0:T(128)S(1)} %get-tuple-element.72.place_ref, bf16[4,1024,256]{2,1,0:T(8,128)(2,1)S(1)} %bitcast.30, bf16[4,1024,256]{2,1,0:T(8,128)(2,1)S(1)} %bitcast.31, bf16[4,1024,256]{2,1,0:T(8,128)(2,1)S(1)} %bitcast.32, bf16[4,1024,256]{2,1,0:T(8,128)(2,1)S(1)} %bitcast.33, ...), custom_call_target="tpu_custom_call" | custom-call | flops 8388608 | bytes 69632 | tf_op jit(solution)/shard_map/pallas_call | solution.py:180
  128.7 1.5 collective-permute-start.15
  130.3 6.2 %collective-permute-done.13 = bf16[64,1024]{1,0:T(8,128)(2,1)S(1)} collective-permute-done((bf16[64,1024]{1,0:T(8,128)(2,1)}, bf16[64,1024]{1,0:T(8,128)(2,1)S(1)}, u32[]{:S(2)}, u32[]{:S(2)}) %collective-permute-start.13) | collective-permute-done | bytes 131104 | tf_op jit(solution)/shard_map/ppermute | solution.py:191
  138.2 2.0 %copy.22 = f32[1024,128]{1,0:T(8,128)} copy(f32[1024,128]{0,1:T(8,128)} %multiply_bitcast_fusion) | data formatting | bytes 1048576
  142.6 1.6 %shard_map.198 = f32[512,512]{1,0:T(8,128)S(1)} custom-call(s32[5]{0:T(128)S(1)} %get-tuple-element.73.place_ref, bf16[4,1024,256]{2,1,0:T(8,128)(2,1)S(1)} %bitcast.34, bf16[4,1024,256]{2,1,0:T(8,128)(2,1)S(1)} %bitcast.35, bf16[4,1024,256]{2,1,0:T(8,128)(2,1)S(1)} %bitcast.36, bf16[4,1024,256]{2,1,0:T(8,128)(2,1)S(1)} %bitcast.37, ...), custom_call_target="tpu_custom_call" | custom-call | flops 8388608 | bytes 77824 | tf_op jit(solution)/shard_map/pallas_call | solution.py:180
  144.3 2.4 %shard_map.196 = f32[512,512]{1,0:T(8,128)S(1)} custom-call(s32[5]{0:T(128)S(1)} %get-tuple-element.73.place_ref, bf16[4,1024,256]{2,1,0:T(8,128)(2,1)S(1)} %bitcast.38, bf16[4,1024,256]{2,1,0:T(8,128)(2,1)S(1)} %bitcast.39, bf16[4,1024,256]{2,1,0:T(8,128)(2,1)S(1)} %bitcast.40, bf16[4,1024,256]{2,1,0:T(8,128)(2,1)S(1)} %bitcast.41, ...), custom_call_target="tpu_custom_call" | custom-call | flops 8388608 | bytes 77824 | tf_op jit(solution)/shard_map/pallas_call | solution.py:180
  149.2 1.5 pad_maximum_fusion
  (113 shorter events, 36.9 us)
Async XLA Ops:
  7.2 33.6 %copy-start.26 = (bf16[2,384,128]{2,1,0:T(8,128)(2,1)S(1)}, bf16[2,384,128]{2,1,0:T(8,128)(2,1)}, u32[]{:S(2)}) copy-start(bf16[2,384,128]{2,1,0:T(8,128)(2,1)} %constant.68.clone.tap_table.prior_table) | copy-start | bytes 589828
  7.2 106.7 %all-gather.3.cloned.1.call-start = ((), (), s32[]{:S(2)}) async-start(), calls=%async_computation | async-start | bytes 2621440 | tf_op jit(solution)/shard_map/all_gather | solution.py:288
  7.2 32.6 %collective-permute-start.1 = (bf16[1024,256]{0,1:T(8,128)(2,1)}, bf16[1024,256]{0,1:T(8,128)(2,1)}, u32[]{:S(2)}, u32[]{:S(2)}) collective-permute-start(bf16[1024,256]{0,1:T(8,128)(2,1)} %bitcast.49), channel_id=1, source_target_pairs={{0,0},{2,8},{4,16},{6,24},{8,4},{10,12},{12,20},{14,28},{16,2},{18... | collective-permute-start | bytes 1572872 | tf_op jit(solution)/shard_map/ppermute | solution.py:245
  10.8 29.0 %collective-permute-start.2 = (bf16[256,1024]{1,0:T(8,128)(2,1)}, bf16[256,1024]{1,0:T(8,128)(2,1)S(1)}, u32[]{:S(2)}, u32[]{:S(2)}) collective-permute-start(bf16[256,1024]{1,0:T(8,128)(2,1)} %bitcast.50), channel_id=1, source_target_pairs={{0,0},{1,4},{2,2},{3,6},{4,1},{5,5},{6,3},{7,7},{8,8},{9,12},{10,1... | collective-permute-start | bytes 1572872 | tf_op jit(solution)/shard_map/ppermute | solution.py:240
  14.1 25.8 %collective-permute-start.3 = (bf16[256,1024]{1,0:T(8,128)(2,1)}, bf16[256,1024]{1,0:T(8,128)(2,1)S(1)}, u32[]{:S(2)}, u32[]{:S(2)}) collective-permute-start(bf16[256,1024]{1,0:T(8,128)(2,1)} %bitcast.51), channel_id=1, source_target_pairs={{0,4},{1,0},{2,6},{3,2},{4,5},{5,1},{6,7},{7,3},{8,12},{9,8},{10,1... | collective-permute-start | bytes 1572872 | tf_op jit(solution)/shard_map/ppermute | solution.py:240
  15.2 24.6 %collective-permute-start = (bf16[128,1024]{1,0:T(8,128)(2,1)S(1)}, bf16[128,1024]{1,0:T(8,128)(2,1)S(1)}, u32[]{:S(2)}, u32[]{:S(2)}) collective-permute-start(bf16[128,1024]{1,0:T(8,128)(2,1)S(1)} %fusion.1), channel_id=1, source_target_pairs={{0,8},{8,16},{16,24},{1,9},{9,17},{17,25},{2,10},{10,18},{18,26},{... | collective-permute-start | bytes 786440 | tf_op jit(solution)/shard_map/ppermute | solution.py:231
  39.9 10.6 %copy-start.10 = (bf16[256,1024]{1,0:T(8,128)(2,1)}, bf16[256,1024]{1,0:T(8,128)(2,1)S(1)}, u32[]{:S(2)}) copy-start(bf16[256,1024]{1,0:T(8,128)(2,1)S(1)} %collective-permute-done.2.first_mine) | copy-start | bytes 1572868
  39.9 9.2 %copy-start.12 = (bf16[256,1024]{1,0:T(8,128)(2,1)}, bf16[256,1024]{1,0:T(8,128)(2,1)S(1)}, u32[]{:S(2)}) copy-start(bf16[256,1024]{1,0:T(8,128)(2,1)S(1)} %collective-permute-done.3.second_mine) | copy-start | bytes 1572868
  39.9 10.4 %collective-permute-start.4 = (bf16[256,1024]{1,0:T(8,128)(2,1)S(1)}, bf16[256,1024]{1,0:T(8,128)(2,1)}, u32[]{:S(2)}, u32[]{:S(2)}) collective-permute-start(bf16[256,1024]{1,0:T(8,128)(2,1)S(1)} %collective-permute-done.2.first_mine), channel_id=1, source_target_pairs={{0,2},{1,3},{2,0},{3,1},{4,6},{5,7},{6,4},{7,5},{8,10},{9,11},{10,... | collective-permute-start | bytes 1572872 | tf_op jit(solution)/shard_map/ppermute | solution.py:270
  40.5 9.8 %collective-permute-start.5 = (bf16[256,1024]{1,0:T(8,128)(2,1)S(1)}, bf16[256,1024]{1,0:T(8,128)(2,1)}, u32[]{:S(2)}, u32[]{:S(2)}) collective-permute-start(bf16[256,1024]{1,0:T(8,128)(2,1)S(1)} %collective-permute-done.3.second_mine), channel_id=1, source_target_pairs={{0,2},{1,3},{2,0},{3,1},{4,6},{5,7},{6,4},{7,5},{8,10},{9,11},{10,... | collective-permute-start | bytes 1572872 | tf_op jit(solution)/shard_map/ppermute | solution.py:270
  45.1 5.3 %copy-start = (bf16[1024,2048]{1,0:T(8,128)(2,1)S(1)}, bf16[1024,2048]{1,0:T(8,128)(2,1)}, u32[]{:S(2)}) copy-start(bf16[1024,2048]{1,0:T(8,128)(2,1)} %weight_theirs.3) | copy-start | bytes 12582916
  50.3 6.1 %copy-start.23 = (f32[256,1024]{1,0:T(8,128)}, f32[256,1024]{1,0:T(8,128)S(1)}, u32[]{:S(2)}) copy-start(f32[256,1024]{1,0:T(8,128)S(1)} %get-tuple-element.45) | copy-start | bytes 3145732
  50.3 15.3 %collective-permute-start.6 = (bf16[2,256,512]{2,1,0:T(8,128)(2,1)S(1)}, bf16[2,256,512]{2,1,0:T(8,128)(2,1)S(1)}, u32[]{:S(2)}, u32[]{:S(2)}) collective-permute-start(bf16[2,256,512]{2,1,0:T(8,128)(2,1)S(1)} %get-tuple-element.57.refs_4_), channel_id=1, source_target_pairs={{0,16},{16,24},{24,8},{8,0},{1,17},{17,25},{25,9},{9,1},{2,18},{18... | collective-permute-start | bytes 1572872 | tf_op jit(solution)/shard_map/ppermute | solution.py:283
  56.4 17.8 %collective-permute-start.7 = (bf16[256,1024]{1,0:T(8,128)(2,1)}, bf16[256,1024]{1,0:T(8,128)(2,1)}, u32[]{:S(2)}, u32[]{:S(2)}) collective-permute-start(bf16[256,1024]{1,0:T(8,128)(2,1)} %shard_map.193), channel_id=1, source_target_pairs={{0,1},{1,0},{2,3},{3,2},{4,5},{5,4},{6,7},{7,6},{8,9},{9,8},{10,11... | collective-permute-start | bytes 1572872 | tf_op jit(solution)/shard_map/ppermute | solution.py:191
  65.5 8.7 %copy-start.2 = (bf16[2,256,512]{2,1,0:T(8,128)(2,1)}, bf16[2,256,512]{2,1,0:T(8,128)(2,1)S(1)}, u32[]{:S(2)}) copy-start(bf16[2,256,512]{2,1,0:T(8,128)(2,1)S(1)} %collective-permute-done.6.refs_5_) | copy-start | bytes 1572868
  65.5 28.5 %collective-permute-start.10 = (bf16[2,256,512]{2,1,0:T(8,128)(2,1)S(1)}, bf16[2,256,512]{2,1,0:T(8,128)(2,1)S(1)}, u32[]{:S(2)}, u32[]{:S(2)}) collective-permute-start(bf16[2,256,512]{2,1,0:T(8,128)(2,1)S(1)} %collective-permute-done.6.refs_5_), channel_id=1, source_target_pairs={{0,16},{16,24},{24,8},{8,0},{1,17},{17,25},{25,9},{9,1},{2,18},{18... | collective-permute-start | bytes 1572872 | tf_op jit(solution)/shard_map/ppermute | solution.py:294
  70.1 4.2 %copy-start.16 = (bf16[1,256,1024]{2,1,0:T(8,128)(2,1)S(1)}, bf16[1,256,1024]{2,1,0:T(8,128)(2,1)}, u32[]{:S(2)}) copy-start(bf16[1,256,1024]{2,1,0:T(8,128)(2,1)} %param.15) | copy-start | bytes 1572868
  70.1 4.2 %copy-start.24 = (f32[256,1024]{1,0:T(8,128)S(1)}, f32[256,1024]{1,0:T(8,128)}, u32[]{:S(2)}) copy-start(f32[256,1024]{1,0:T(8,128)} %copy-done.23) | copy-start | bytes 3145732
  74.2 2.4 %copy-start.22 = (f32[384,1024]{1,0:T(8,128)S(1)}, f32[384,1024]{1,0:T(8,128)}, u32[]{:S(2)}) copy-start(f32[384,1024]{1,0:T(8,128)} %copy-done.21) | copy-start | bytes 4718596
  74.3 2.4 %copy-start.29 = (bf16[2,384,256]{2,1,0:T(8,128)(2,1)S(1)}, bf16[2,384,256]{2,1,0:T(8,128)(2,1)}, u32[]{:S(2)}) copy-start(bf16[2,384,256]{2,1,0:T(8,128)(2,1)} %constant.71.clone.own_table) | copy-start | bytes 1179652
  74.3 2.4 %copy-start.36 = (bf16[2,128,384]{2,1,0:T(8,128)(2,1)S(1)}, bf16[2,128,384]{2,1,0:T(8,128)(2,1)}, u32[]{:S(2)}) copy-start(bf16[2,128,384]{2,1,0:T(8,128)(2,1)} %constant.72.clone.synth) | copy-start | bytes 589828
  76.7 17.4 %copy-start.27 = (bf16[2,256,384]{2,1,0:T(8,128)(2,1)S(1)}, bf16[2,256,384]{2,1,0:T(8,128)(2,1)}, u32[]{:S(2)}) copy-start(bf16[2,256,384]{2,1,0:T(8,128)(2,1)} %constant.74.clone.synth) | copy-start | bytes 1179652
  81.0 3.0 %copy-start.31 = (f32[128,1024]{1,0:T(8,128)}, f32[128,1024]{1,0:T(8,128)S(1)}, u32[]{:S(2)}) copy-start(f32[128,1024]{1,0:T(8,128)S(1)} %get-tuple-element.47) | copy-start | bytes 1572868
  81.7 7.5 %collective-permute-start.8 = (bf16[64,1024]{1,0:T(8,128)(2,1)}, bf16[64,1024]{1,0:T(8,128)(2,1)}, u32[]{:S(2)}, u32[]{:S(2)}) collective-permute-start(bf16[64,1024]{1,0:T(8,128)(2,1)} %dynamic-slice_convert_fusion), channel_id=1, source_target_pairs={{0,1},{1,0},{2,3},{3,2},{4,5},{5,4},{6,7},{7,6},{8,9},{9,8},{10,11... | collective-permute-start | bytes 393224 | tf_op jit(solution)/shard_map/ppermute | solution.py:191
  83.9 10.1 %collective-permute-start.9 = (bf16[128,1024]{1,0:T(8,128)(2,1)}, bf16[128,1024]{1,0:T(8,128)(2,1)}, u32[]{:S(2)}, u32[]{:S(2)}) collective-permute-start(bf16[128,1024]{1,0:T(8,128)(2,1)} %slice.26), channel_id=1, source_target_pairs={{8,0},{16,8},{24,16},{9,1},{17,9},{25,17},{10,2},{18,10},{26,18},{... | collective-permute-start | bytes 786440 | tf_op jit(solution)/shard_map/ppermute | solution.py:330
  103.6 6.9 %collective-permute-start.11 = (bf16[64,1024]{1,0:T(8,128)(2,1)S(1)}, bf16[64,1024]{1,0:T(8,128)(2,1)S(1)}, u32[]{:S(2)}, u32[]{:S(2)}) collective-permute-start(bf16[64,1024]{1,0:T(8,128)(2,1)S(1)} %convert_add_fusion.1), channel_id=1, source_target_pairs={{0,8},{8,0},{16,24},{24,16},{1,9},{9,1},{17,25},{25,17},{2,10},{10... | collective-permute-start | bytes 393224 | tf_op jit(solution)/shard_map/ppermute | solution.py:191
  106.9 10.5 %collective-permute-start.16 = (bf16[1,256,512]{2,1,0:T(8,128)(2,1)}, bf16[1,256,512]{2,1,0:T(8,128)(2,1)S(1)}, u32[]{:S(2)}, u32[]{:S(2)}) collective-permute-start(bf16[1,256,512]{2,1,0:T(8,128)(2,1)} %get-tuple-element.69), channel_id=1, source_target_pairs={{0,16},{16,24},{24,8},{8,0},{1,17},{17,25},{25,9},{9,1},{2,18},{18... | collective-permute-start | bytes 786440 | tf_op jit(solution)/shard_map/ppermute | solution.py:297
  110.5 12.0 %collective-permute-start.12 = (bf16[64,1024]{1,0:T(8,128)(2,1)S(1)}, bf16[64,1024]{1,0:T(8,128)(2,1)}, u32[]{:S(2)}, u32[]{:S(2)}) collective-permute-start(bf16[64,1024]{1,0:T(8,128)(2,1)S(1)} %add_convert_fusion.1), channel_id=1, source_target_pairs={{0,16},{8,24},{16,0},{24,8},{1,17},{9,25},{17,1},{25,9},{2,18},{10... | collective-permute-start | bytes 393224 | tf_op jit(solution)/shard_map/ppermute | solution.py:191
  111.9 12.7 %collective-permute-start.14 = (bf16[1,256,512]{2,1,0:T(8,128)(2,1)}, bf16[1,256,512]{2,1,0:T(8,128)(2,1)}, u32[]{:S(2)}, u32[]{:S(2)}) collective-permute-start(bf16[1,256,512]{2,1,0:T(8,128)(2,1)} %get-tuple-element.68), channel_id=1, source_target_pairs={{0,16},{16,24},{24,8},{8,0},{1,17},{17,25},{25,9},{9,1},{2,18},{18... | collective-permute-start | bytes 786440 | tf_op jit(solution)/shard_map/ppermute | solution.py:297
  120.6 26.1 %collective-permute-start.17 = (bf16[512,512]{1,0:T(8,128)(2,1)}, bf16[512,512]{1,0:T(8,128)(2,1)}, u32[]{:S(2)}, u32[]{:S(2)}) collective-permute-start(bf16[512,512]{1,0:T(8,128)(2,1)} %shard_map.199), channel_id=1, source_target_pairs={{0,1},{1,0},{2,3},{3,2},{4,5},{5,4},{6,7},{7,6},{8,9},{9,8},{10,11... | collective-permute-start | bytes 1572872 | tf_op jit(solution)/shard_map/ppermute | solution.py:191
  124.0 12.4 %collective-permute-start.13 = (bf16[64,1024]{1,0:T(8,128)(2,1)}, bf16[64,1024]{1,0:T(8,128)(2,1)S(1)}, u32[]{:S(2)}, u32[]{:S(2)}) collective-permute-start(bf16[64,1024]{1,0:T(8,128)(2,1)} %add_convert_fusion), channel_id=1, source_target_pairs={{0,1},{1,0},{2,3},{3,2},{4,5},{5,4},{6,7},{7,6},{8,9},{9,8},{10,11... | collective-permute-start | bytes 393224 | tf_op jit(solution)/shard_map/ppermute | solution.py:191
  128.7 19.2 %collective-permute-start.15 = (bf16[512,512]{1,0:T(8,128)(2,1)}, bf16[512,512]{1,0:T(8,128)(2,1)}, u32[]{:S(2)}, u32[]{:S(2)}) collective-permute-start(bf16[512,512]{1,0:T(8,128)(2,1)} %shard_map.197), channel_id=1, source_target_pairs={{0,1},{1,0},{2,3},{3,2},{4,5},{5,4},{6,7},{7,6},{8,9},{9,8},{10,11... | collective-permute-start | bytes 1572872 | tf_op jit(solution)/shard_map/ppermute | solution.py:191
  (25 other events, 27.4 us)
Sparse Core Ops, SparseCore 0:
  40.0 22.7 all-gather.2

commit v4 on v3

--- a/solution.py
+++ b/solution.py
@@ -12,7 +12,7 @@
 
 f32, bf16 = jnp.float32, jnp.bfloat16
 lanes = 256
-vmem_bytes = 32 * 1024 * 1024
+vmem_bytes = 58 * 1024 * 1024
 
 
 def analysis_table(size, positions):
@@ -228,6 +228,7 @@
     tail = (
         key_rows[length - taps :].astype(f32) * value_rows[length - taps :].astype(f32)
     ).astype(bf16)
+    tail, cot = lax.optimization_barrier((tail, cot))
     prior = lax.ppermute(tail, "seq", [(i, i + 1) for i in range(n_seq - 1)])
 
     def tp_dp(half, sub, replica):
@@ -242,7 +243,7 @@
     if square:
         holder = [(s % n_dp) * subs + s // n_dp for s in range(n_seq)]
         route = [(s * n_tp + t, t * n_tp + holder[s]) for s in range(n_seq) for t in range(n_tp)]
-        moved = lax.ppermute(cot.T, ("seq", "tp"), route)
+        moved = lax.ppermute(after(cot, prior).T, ("seq", "tp"), route)
     else:
         moved = cot
 
@@ -254,9 +255,7 @@
         channels,
         2 * unit * (length + taps),
     )
-    prior, moved, own_spec, filt, *rounds = lax.optimization_barrier(
-        (prior, moved, own_spec, filt, *rounds)
-    )
+    prior, own_spec, filt, *rounds = lax.optimization_barrier((prior, own_spec, filt, *rounds))
     mixed_spec, state, gated = by_channel(
         state_kernel,
         [tap_table, synth_fwd],
@@ -268,7 +267,7 @@
 
     route = [(tp_dp(h, c, d), tp_dp(h, (c + 1) % subs, d)) for h, c, d in places]
     theirs = [lax.ppermute(r, ("tp", "dp"), route) for r in rounds]
-    gated, *theirs = lax.optimization_barrier((gated, *theirs))
+    gated, moved, *theirs = lax.optimization_barrier((gated, moved, *theirs))
     firsts, seconds = zip(rounds, theirs)
     same = (me_half == me_dp).astype(jnp.int32)
     subs_of = [me_sub, (me_sub + 1) % subs]
@@ -336,8 +335,6 @@
         channels,
         unit * (2 * length + 3 * taps),
     )
-    if square:
-        later, *pieces = lax.optimization_barrier((later, *pieces))
     grad_key, grad_value = by_channel(
         back_kernel,
         [late_table, synth_bwd],
@@ -351,7 +348,6 @@
     lag_sum = lax.dynamic_slice_in_dim(lags, me_dp * share, share, axis=0) + swap_pairs(
         lax.dynamic_slice_in_dim(lags, (1 - me_dp) * share, share, axis=0).astype(bf16), "dp", 1
     ).astype(f32)
-    lag_sum, grad_key, grad_value = lax.optimization_barrier((lag_sum, grad_key, grad_value))
     distance = 1
     while distance < n_seq:
         rounded = lag_sum.astype(bf16)

time: 159 us -> 157 us (0.987)
  the two profiles are of different devices: /device:TPU:10 before, /device:TPU:8 now
where the time goes in v4:
time: 157 us; the launch traced here: 156 us
  Pallas kernels  50.5 us (32%)
  starting transfers between devices  45.6 us (29%)
  waiting for transfers between devices  26.9 us (17%)
  between operations  14.3 us (9%)
  local copies, waits for them, and re-layouts  10.3 us (7%)
  other arithmetic  8.48 us (5%)
    pallas_call x4, Pallas kernels, by_channel(): pl.pallas_call(kernel, grid=(channels // lanes,), in_specs=[pl.BlockSpec(...  22.5 us
    ppermute x1, starting transfers between devices, per_device(): pieces.append(lax.ppermute(pieces[-1], 'seq', ring))  17 us
    pallas_call x4, Pallas kernels, weight_sum(): pl.pallas_call(functools.partial(weight_kernel, count), grid_spec=grid_sp...  15.8 us
    ppermute x7, starting transfers between devices, swap_pairs(): return lax.ppermute(value, axis, [(i, i ^ distance) for i in range(count)])  13.6 us
    pallas_call x2, Pallas kernels, project(): pl.pallas_call(project_kernel, grid_spec=grid_spec, out_shape=out, compil...  12.3 us
    ppermute x7, waiting for transfers between devices, swap_pairs(): return lax.ppermute(value, axis, [(i, i ^ distance) for i in range(count)])  10 us
    ppermute x1, waiting for transfers between devices, per_device(): pieces = [gated, lax.ppermute(gated, 'seq', ring)]  7.58 us
    ppermute x1, waiting for transfers between devices, per_device(): lax.ppermute(signal[:taps], 'seq', [(i + 1, i) for i in range(n_seq - 1)])  5.01 us
  transfers between devices with their start and end apart: 19, of which 8 were waited for; matrix products, arithmetic and copies ran while one was open for 8% of the time, Pallas kernels for 32%

profile of v4, /device:TPU:8, one launch (start us, length us, event | category | flops | bytes accessed | tf_op | source)
XLA Modules:
  0.0 156.2 jit_solution(11588768393141580473)
XLA Ops:
  7.2 1.1 fusion.1
  8.4 1.7 %collective-permute-start.1 = (bf16[256,1024]{1,0:T(8,128)(2,1)}, bf16[256,1024]{1,0:T(8,128)(2,1)S(1)}, u32[]{:S(2)}, u32[]{:S(2)}) collective-permute-start(bf16[256,1024]{1,0:T(8,128)(2,1)} %bitcast.48), channel_id=1, source_target_pairs={{0,0},{1,4},{2,2},{3,6},{4,1},{5,5},{6,3},{7,7},{8,8},{9,12},{10,1... | collective-permute-start | bytes 1572872 | tf_op jit(solution)/shard_map/ppermute | solution.py:241
  10.1 3.3 %collective-permute-start.2 = (bf16[256,1024]{1,0:T(8,128)(2,1)}, bf16[256,1024]{1,0:T(8,128)(2,1)S(1)}, u32[]{:S(2)}, u32[]{:S(2)}) collective-permute-start(bf16[256,1024]{1,0:T(8,128)(2,1)} %bitcast.49), channel_id=1, source_target_pairs={{0,4},{1,0},{2,6},{3,2},{4,5},{5,1},{6,7},{7,3},{8,12},{9,8},{10,1... | collective-permute-start | bytes 1572872 | tf_op jit(solution)/shard_map/ppermute | solution.py:241
  13.3 3.5 %collective-permute-start = (bf16[128,1024]{1,0:T(8,128)(2,1)S(1)}, bf16[128,1024]{1,0:T(8,128)(2,1)S(1)}, u32[]{:S(2)}, u32[]{:S(2)}) collective-permute-start(bf16[128,1024]{1,0:T(8,128)(2,1)S(1)} %fusion.1), channel_id=1, source_target_pairs={{0,8},{8,16},{16,24},{1,9},{9,17},{17,25},{2,10},{10,18},{18,26},{... | collective-permute-start | bytes 786440 | tf_op jit(solution)/shard_map/ppermute | solution.py:232
  16.8 4.9 %shard_map.190 = (f32[384,1024]{1,0:T(8,128)}, f32[384,1024]{1,0:T(8,128)}) custom-call(bf16[2,384,256]{2,1,0:T(8,128)(2,1)} %constant.67.clone.own_table, bf16[2,384,128]{2,1,0:T(8,128)(2,1)} %constant.68.clone.tap_table.prior_table, bf16[256,1024]{1,0:T(8,128)(2,1)} %bitcast.43, bf16[256,1024]{1,0:T(8,128)(2,1)} %bitcast.41, bf16[1024,128]{1,0:T(8,128)(2,1)} %taps_ref.1, ...), custom_call_target="tpu_custom_call" | custom-call | flops 9437184 | bytes 69696 | tf_op jit(solution)/shard_map/pallas_call | solution.py:125
  21.7 1.0 collective-permute-done.prior_ref
  22.7 1.9 %collective-permute-start.3 = (bf16[1024,256]{0,1:T(8,128)(2,1)S(1)}, bf16[1024,256]{0,1:T(8,128)(2,1)S(1)}, u32[]{:S(2)}, u32[]{:S(2)}) collective-permute-start(bf16[1024,256]{0,1:T(8,128)(2,1)S(1)} %bitcast.50), channel_id=1, source_target_pairs={{0,0},{2,8},{4,16},{6,24},{8,4},{10,12},{12,20},{14,28},{16,2},{18... | collective-permute-start | bytes 1572872 | tf_op jit(solution)/shard_map/ppermute | solution.py:246
  25.7 6.2 %shard_map.191 = (f32[384,1024]{1,0:T(8,128)}, f32[256,1024]{1,0:T(8,128)}, bf16[2,256,512]{2,1,0:T(8,128)(2,1)}) custom-call(bf16[2,384,128]{2,1,0:T(8,128)(2,1)} %constant.68.clone.tap_table.prior_table, bf16[2,256,384]{2,1,0:T(8,128)(2,1)} %constant.69.clone.synth, bf16[128,1024]{1,0:T(8,128)(2,1)} %copy-done.15, f32[384,1024]{1,0:T(8,128)} %get-tuple-element.34.own_ref, ...), custom_call_target="tpu_custom_call" | custom-call | flops 12582912 | bytes 110592 | tf_op jit(solution)/shard_map/pallas_call | solution.py:125
  31.9 2.7 %collective-permute-done.3 = bf16[1024,256]{0,1:T(8,128)(2,1)S(1)} collective-permute-done((bf16[1024,256]{0,1:T(8,128)(2,1)S(1)}, bf16[1024,256]{0,1:T(8,128)(2,1)S(1)}, u32[]{:S(2)}, u32[]{:S(2)}) %collective-permute-start.3) | collective-permute-done | bytes 524320 | tf_op jit(solution)/shard_map/ppermute | solution.py:246
  36.2 6.1 %shard_map.193 = bf16[256,1024]{1,0:T(8,128)(2,1)} custom-call(s32[3]{0:T(128)} %add_add_fusion.1.place_ref, bf16[256,1024]{1,0:T(8,128)(2,1)} %copy-done.5, bf16[256,1024]{1,0:T(8,128)(2,1)} %copy-done.6, bf16[256,1024]{1,0:T(8,128)(2,1)} %copy-done.7, bf16[256,1024]{1,0:T(8,128)(2,1)} %copy-done.8, bf16[1024,2048]{1,0:T(8,128)(2,1)} %weight_theirs.3, ...), custom_call_target="tpu_custom_call" | custom-call | flops 16777216 | bytes 106496 | tf_op jit(solution)/shard_map/pallas_call | solution.py:152
  42.3 1.7 %collective-permute-start.7 = (bf16[256,1024]{1,0:T(8,128)(2,1)}, bf16[256,1024]{1,0:T(8,128)(2,1)S(1)}, u32[]{:S(2)}, u32[]{:S(2)}) collective-permute-start(bf16[256,1024]{1,0:T(8,128)(2,1)} %shard_map.193), channel_id=1, source_target_pairs={{0,1},{1,0},{2,3},{3,2},{4,5},{5,4},{6,7},{7,6},{8,9},{9,8},{10,11... | collective-permute-start | bytes 1572872 | tf_op jit(solution)/shard_map/ppermute | solution.py:191
  44.6 7.6 %collective-permute-done.6.refs_5_ = bf16[2,256,512]{2,1,0:T(8,128)(2,1)S(1)} collective-permute-done((bf16[2,256,512]{2,1,0:T(8,128)(2,1)}, bf16[2,256,512]{2,1,0:T(8,128)(2,1)S(1)}, u32[]{:S(2)}, u32[]{:S(2)}) %collective-permute-start.6) | collective-permute-done | bytes 524320 | tf_op jit(solution)/shard_map/ppermute | solution.py:282
  52.2 17.0 %collective-permute-start.13 = (bf16[2,256,512]{2,1,0:T(8,128)(2,1)S(1)}, bf16[2,256,512]{2,1,0:T(8,128)(2,1)S(1)}, u32[]{:S(2)}, u32[]{:S(2)}) collective-permute-start(bf16[2,256,512]{2,1,0:T(8,128)(2,1)S(1)} %collective-permute-done.6.refs_5_), channel_id=1, source_target_pairs={{0,16},{16,24},{24,8},{8,0},{1,17},{17,25},{25,9},{9,1},{2,18},{18... | collective-permute-start | bytes 1572872 | tf_op jit(solution)/shard_map/ppermute | solution.py:293
  69.2 6.2 %shard_map.192 = f32[256,1024]{1,0:T(8,128)} custom-call(s32[3]{0:T(128)} %add_add_fusion.place_ref, bf16[256,1024]{1,0:T(8,128)(2,1)} %copy-done.5, bf16[256,1024]{1,0:T(8,128)(2,1)} %copy-done.6, bf16[256,1024]{1,0:T(8,128)(2,1)} %copy-done.7, bf16[256,1024]{1,0:T(8,128)(2,1)} %copy-done.8, bf16[1024,2048]{1,0:T(8,128)(2,1)} %weight_theirs.3, ...), custom_call_target="tpu_custom_call" | custom-call | flops 16777216 | bytes 114688 | tf_op jit(solution)/shard_map/pallas_call | solution.py:152
  75.4 2.6 %multiply_convert_fusion = (bf16[256,1024]{1,0:T(8,128)(2,1)}, bf16[1,256,1024]{2,1,0:T(8,128)(2,1)}) fusion(f32[256,1024]{1,0:T(8,128)} %shard_map.192, bf16[256,1024]{1,0:T(8,128)(2,1)S(1)} %collective-permute-done.7, bf16[1,256,1024]{2,1,0:T(8,128)(2,1)S(1)} %copy-done.9, f32[256,1024]{1,0:T(8,128)S(1)} %copy-done.12), kind=kLoop, calls=%fused_computation.3 | loop fusion | flops 1835008 | bytes 4194304 | tf_op jit(solution)/shard_map/convert_element_type | solution.py:328
  78.0 5.3 %shard_map.194 = (f32[384,1024]{1,0:T(8,128)}, f32[128,1024]{1,0:T(8,128)}) custom-call(bf16[2,384,256]{2,1,0:T(8,128)(2,1)} %constant.71.clone.own_table, bf16[2,128,384]{2,1,0:T(8,128)(2,1)} %constant.72.clone.synth, bf16[256,1024]{1,0:T(8,128)(2,1)} %get-tuple-element.58.signal_ref, f32[384,1024]{1,0:T(8,128)} %get-tuple-element.45.spec_ref), custom_call_target="tpu_custom_call" | custom-call | flops 11010048 | bytes 65536 | tf_op jit(solution)/shard_map/pallas_call | solution.py:125
  84.2 4.8 %collective-permute-start.9 = (bf16[64,1024]{1,0:T(8,128)(2,1)S(1)}, bf16[64,1024]{1,0:T(8,128)(2,1)S(1)}, u32[]{:S(2)}, u32[]{:S(2)}) collective-permute-start(bf16[64,1024]{1,0:T(8,128)(2,1)S(1)} %dynamic-slice_convert_fusion), channel_id=1, source_target_pairs={{0,1},{1,0},{2,3},{3,2},{4,5},{5,4},{6,7},{7,6},{8,9},{9,8},{10,11... | collective-permute-start | bytes 393224 | tf_op jit(solution)/shard_map/ppermute | solution.py:191
  89.1 3.2 %collective-permute-done.9 = bf16[64,1024]{1,0:T(8,128)(2,1)S(1)} collective-permute-done((bf16[64,1024]{1,0:T(8,128)(2,1)S(1)}, bf16[64,1024]{1,0:T(8,128)(2,1)S(1)}, u32[]{:S(2)}, u32[]{:S(2)}) %collective-permute-start.9) | collective-permute-done | bytes 131104 | tf_op jit(solution)/shard_map/ppermute | solution.py:191
  93.2 3.3 %collective-permute-start.10 = (bf16[64,1024]{1,0:T(8,128)(2,1)S(1)}, bf16[64,1024]{1,0:T(8,128)(2,1)S(1)}, u32[]{:S(2)}, u32[]{:S(2)}) collective-permute-start(bf16[64,1024]{1,0:T(8,128)(2,1)S(1)} %add_convert_fusion.2), channel_id=1, source_target_pairs={{0,8},{8,0},{16,24},{24,16},{1,9},{9,1},{17,25},{25,17},{2,10},{10... | collective-permute-start | bytes 393224 | tf_op jit(solution)/shard_map/ppermute | solution.py:191
  96.7 4.3 %collective-permute-done.10 = bf16[64,1024]{1,0:T(8,128)(2,1)S(1)} collective-permute-done((bf16[64,1024]{1,0:T(8,128)(2,1)S(1)}, bf16[64,1024]{1,0:T(8,128)(2,1)S(1)}, u32[]{:S(2)}, u32[]{:S(2)}) %collective-permute-start.10) | collective-permute-done | bytes 131104 | tf_op jit(solution)/shard_map/ppermute | solution.py:191
  102.5 3.9 %collective-permute-start.8 = (bf16[128,1024]{1,0:T(8,128)(2,1)S(1)}, bf16[128,1024]{1,0:T(8,128)(2,1)S(1)}, u32[]{:S(2)}, u32[]{:S(2)}) collective-permute-start(bf16[128,1024]{1,0:T(8,128)(2,1)S(1)} %slice.26), channel_id=1, source_target_pairs={{8,0},{16,8},{24,16},{9,1},{17,9},{25,17},{10,2},{18,10},{26,18},{... | collective-permute-start | bytes 786440 | tf_op jit(solution)/shard_map/ppermute | solution.py:329
  106.5 4.1 %copy.21 = bf16[4096,256]{1,0:T(8,128)(2,1)} copy(bf16[4096,256]{0,1:T(8,128)(2,1)} %all-gather.3.cloned.1.call-done) | data formatting | bytes 4194304 | tf_op jit(solution)/shard_map/all_gather | solution.py:287
  111.3 3.9 %shard_map.199 = bf16[512,512]{1,0:T(8,128)(2,1)} custom-call(s32[5]{0:T(128)} %get-tuple-element.64.place_ref, bf16[4,1024,256]{2,1,0:T(8,128)(2,1)} %bitcast.25, bf16[4,1024,256]{2,1,0:T(8,128)(2,1)} %bitcast.26, bf16[4,1024,256]{2,1,0:T(8,128)(2,1)} %bitcast.27, bf16[4,1024,256]{2,1,0:T(8,128)(2,1)} %bitcast.28, ...), custom_call_target="tpu_custom_call" | custom-call | flops 8388608 | bytes 69632 | tf_op jit(solution)/shard_map/pallas_call | solution.py:180
  115.1 2.0 %collective-permute-start.17 = (bf16[512,512]{1,0:T(8,128)(2,1)}, bf16[512,512]{1,0:T(8,128)(2,1)S(1)}, u32[]{:S(2)}, u32[]{:S(2)}) collective-permute-start(bf16[512,512]{1,0:T(8,128)(2,1)} %shard_map.199), channel_id=1, source_target_pairs={{0,1},{1,0},{2,3},{3,2},{4,5},{5,4},{6,7},{7,6},{8,9},{9,8},{10,11... | collective-permute-start | bytes 1572872 | tf_op jit(solution)/shard_map/ppermute | solution.py:191
  117.2 5.0 %collective-permute-done.8.later_ref = bf16[128,1024]{1,0:T(8,128)(2,1)S(1)} collective-permute-done((bf16[128,1024]{1,0:T(8,128)(2,1)S(1)}, bf16[128,1024]{1,0:T(8,128)(2,1)S(1)}, u32[]{:S(2)}, u32[]{:S(2)}) %collective-permute-start.8) | collective-permute-done | bytes 262176 | tf_op jit(solution)/shard_map/ppermute | solution.py:329
  123.0 6.1 %shard_map.195 = (bf16[256,1024]{1,0:T(8,128)(2,1)}, bf16[256,1024]{1,0:T(8,128)(2,1)}) custom-call(bf16[2,384,128]{2,1,0:T(8,128)(2,1)} %constant.73.clone.late_table, bf16[2,256,384]{2,1,0:T(8,128)(2,1)} %constant.74.clone.synth, f32[384,1024]{1,0:T(8,128)} %get-tuple-element.46.own_ref, bf16[128,1024]{1,0:T(8,128)(2,1)} %copy-done.14, ...), custom_call_target="tpu_custom_call" | custom-call | flops 12582912 | bytes 86016 | tf_op jit(solution)/shard_map/pallas_call | solution.py:125
  129.8 3.8 %shard_map.197 = bf16[512,512]{1,0:T(8,128)(2,1)} custom-call(s32[5]{0:T(128)} %get-tuple-element.64.place_ref, bf16[4,1024,256]{2,1,0:T(8,128)(2,1)} %bitcast.29, bf16[4,1024,256]{2,1,0:T(8,128)(2,1)} %bitcast.30, bf16[4,1024,256]{2,1,0:T(8,128)(2,1)} %bitcast.31, bf16[4,1024,256]{2,1,0:T(8,128)(2,1)} %bitcast.32, ...), custom_call_target="tpu_custom_call" | custom-call | flops 8388608 | bytes 69632 | tf_op jit(solution)/shard_map/pallas_call | solution.py:180
  133.6 1.5 collective-permute-start.15
  136.9 4.0 %shard_map.198 = f32[512,512]{1,0:T(8,128)} custom-call(s32[5]{0:T(128)} %get-tuple-element.65.place_ref, bf16[4,1024,256]{2,1,0:T(8,128)(2,1)} %bitcast.33, bf16[4,1024,256]{2,1,0:T(8,128)(2,1)} %bitcast.34, bf16[4,1024,256]{2,1,0:T(8,128)(2,1)} %bitcast.35, bf16[4,1024,256]{2,1,0:T(8,128)(2,1)} %bitcast.36, ...), custom_call_target="tpu_custom_call" | custom-call | flops 8388608 | bytes 77824 | tf_op jit(solution)/shard_map/pallas_call | solution.py:180
  140.9 4.1 %shard_map.196 = f32[512,512]{1,0:T(8,128)} custom-call(s32[5]{0:T(128)} %get-tuple-element.65.place_ref, bf16[4,1024,256]{2,1,0:T(8,128)(2,1)} %bitcast.37, bf16[4,1024,256]{2,1,0:T(8,128)(2,1)} %bitcast.38, bf16[4,1024,256]{2,1,0:T(8,128)(2,1)} %bitcast.39, bf16[4,1024,256]{2,1,0:T(8,128)(2,1)} %bitcast.40, ...), custom_call_target="tpu_custom_call" | custom-call | flops 8388608 | bytes 77824 | tf_op jit(solution)/shard_map/pallas_call | solution.py:180
  145.1 2.6 %collective-permute-done.15 = bf16[512,512]{1,0:T(8,128)(2,1)S(1)} collective-permute-done((bf16[512,512]{1,0:T(8,128)(2,1)}, bf16[512,512]{1,0:T(8,128)(2,1)S(1)}, u32[]{:S(2)}, u32[]{:S(2)}) %collective-permute-start.15) | collective-permute-done | bytes 524320 | tf_op jit(solution)/shard_map/ppermute | solution.py:191
  147.9 1.5 pad_maximum_fusion
  (71 shorter events, 11.2 us)
Async XLA Ops:
  7.2 15.5 %copy-start.16 = (bf16[1,256,1024]{2,1,0:T(8,128)(2,1)S(1)}, bf16[1,256,1024]{2,1,0:T(8,128)(2,1)}, u32[]{:S(2)}) copy-start(bf16[1,256,1024]{2,1,0:T(8,128)(2,1)} %param.21) | copy-start | bytes 1572868
  7.2 99.3 %all-gather.3.cloned.1.call-start = ((), (), s32[]{:S(2)}) async-start(), calls=%async_computation | async-start | bytes 2621440 | tf_op jit(solution)/shard_map/all_gather | solution.py:287
  8.4 16.2 %collective-permute-start.1 = (bf16[256,1024]{1,0:T(8,128)(2,1)}, bf16[256,1024]{1,0:T(8,128)(2,1)S(1)}, u32[]{:S(2)}, u32[]{:S(2)}) collective-permute-start(bf16[256,1024]{1,0:T(8,128)(2,1)} %bitcast.48), channel_id=1, source_target_pairs={{0,0},{1,4},{2,2},{3,6},{4,1},{5,5},{6,3},{7,7},{8,8},{9,12},{10,1... | collective-permute-start | bytes 1572872 | tf_op jit(solution)/shard_map/ppermute | solution.py:241
  10.1 15.1 %collective-permute-start.2 = (bf16[256,1024]{1,0:T(8,128)(2,1)}, bf16[256,1024]{1,0:T(8,128)(2,1)S(1)}, u32[]{:S(2)}, u32[]{:S(2)}) collective-permute-start(bf16[256,1024]{1,0:T(8,128)(2,1)} %bitcast.49), channel_id=1, source_target_pairs={{0,4},{1,0},{2,6},{3,2},{4,5},{5,1},{6,7},{7,3},{8,12},{9,8},{10,1... | collective-permute-start | bytes 1572872 | tf_op jit(solution)/shard_map/ppermute | solution.py:241
  13.3 9.4 %collective-permute-start = (bf16[128,1024]{1,0:T(8,128)(2,1)S(1)}, bf16[128,1024]{1,0:T(8,128)(2,1)S(1)}, u32[]{:S(2)}, u32[]{:S(2)}) collective-permute-start(bf16[128,1024]{1,0:T(8,128)(2,1)S(1)} %fusion.1), channel_id=1, source_target_pairs={{0,8},{8,16},{16,24},{1,9},{9,17},{17,25},{2,10},{10,18},{18,26},{... | collective-permute-start | bytes 786440 | tf_op jit(solution)/shard_map/ppermute | solution.py:232
  22.7 3.0 %copy-start.15 = (bf16[128,1024]{1,0:T(8,128)(2,1)}, bf16[128,1024]{1,0:T(8,128)(2,1)S(1)}, u32[]{:S(2)}) copy-start(bf16[128,1024]{1,0:T(8,128)(2,1)S(1)} %collective-permute-done.prior_ref) | copy-start | bytes 786436
  22.7 11.9 %collective-permute-start.3 = (bf16[1024,256]{0,1:T(8,128)(2,1)S(1)}, bf16[1024,256]{0,1:T(8,128)(2,1)S(1)}, u32[]{:S(2)}, u32[]{:S(2)}) collective-permute-start(bf16[1024,256]{0,1:T(8,128)(2,1)S(1)} %bitcast.50), channel_id=1, source_target_pairs={{0,0},{2,8},{4,16},{6,24},{8,4},{10,12},{12,20},{14,28},{16,2},{18... | collective-permute-start | bytes 1572872 | tf_op jit(solution)/shard_map/ppermute | solution.py:246
  24.6 7.3 %copy-start.5 = (bf16[256,1024]{1,0:T(8,128)(2,1)}, bf16[256,1024]{1,0:T(8,128)(2,1)S(1)}, u32[]{:S(2)}) copy-start(bf16[256,1024]{1,0:T(8,128)(2,1)S(1)} %collective-permute-done.1.first_mine) | copy-start | bytes 1572868
  25.2 6.8 %copy-start.6 = (bf16[256,1024]{1,0:T(8,128)(2,1)}, bf16[256,1024]{1,0:T(8,128)(2,1)S(1)}, u32[]{:S(2)}) copy-start(bf16[256,1024]{1,0:T(8,128)(2,1)S(1)} %collective-permute-done.2.second_mine) | copy-start | bytes 1572868
  25.2 9.5 %collective-permute-start.4 = (bf16[256,1024]{1,0:T(8,128)(2,1)S(1)}, bf16[256,1024]{1,0:T(8,128)(2,1)S(1)}, u32[]{:S(2)}, u32[]{:S(2)}) collective-permute-start(bf16[256,1024]{1,0:T(8,128)(2,1)S(1)} %collective-permute-done.1.first_mine), channel_id=1, source_target_pairs={{0,2},{1,3},{2,0},{3,1},{4,6},{5,7},{6,4},{7,5},{8,10},{9,11},{10,... | collective-permute-start | bytes 1572872 | tf_op jit(solution)/shard_map/ppermute | solution.py:269
  25.2 9.5 %collective-permute-start.5 = (bf16[256,1024]{1,0:T(8,128)(2,1)S(1)}, bf16[256,1024]{1,0:T(8,128)(2,1)S(1)}, u32[]{:S(2)}, u32[]{:S(2)}) collective-permute-start(bf16[256,1024]{1,0:T(8,128)(2,1)S(1)} %collective-permute-done.2.second_mine), channel_id=1, source_target_pairs={{0,2},{1,3},{2,0},{3,1},{4,6},{5,7},{6,4},{7,5},{8,10},{9,11},{10,... | collective-permute-start | bytes 1572872 | tf_op jit(solution)/shard_map/ppermute | solution.py:269
  34.6 1.6 %copy-start.7 = (bf16[256,1024]{1,0:T(8,128)(2,1)}, bf16[256,1024]{1,0:T(8,128)(2,1)S(1)}, u32[]{:S(2)}) copy-start(bf16[256,1024]{1,0:T(8,128)(2,1)S(1)} %collective-permute-done.4.first_theirs) | copy-start | bytes 1572868
  34.6 1.6 %copy-start.8 = (bf16[256,1024]{1,0:T(8,128)(2,1)}, bf16[256,1024]{1,0:T(8,128)(2,1)S(1)}, u32[]{:S(2)}) copy-start(bf16[256,1024]{1,0:T(8,128)(2,1)S(1)} %collective-permute-done.5.second_theirs) | copy-start | bytes 1572868
  35.5 16.7 %collective-permute-start.6 = (bf16[2,256,512]{2,1,0:T(8,128)(2,1)}, bf16[2,256,512]{2,1,0:T(8,128)(2,1)S(1)}, u32[]{:S(2)}, u32[]{:S(2)}) collective-permute-start(bf16[2,256,512]{2,1,0:T(8,128)(2,1)} %get-tuple-element.40.refs_4_), channel_id=1, source_target_pairs={{0,16},{16,24},{24,8},{8,0},{1,17},{17,25},{25,9},{9,1},{2,18},{18... | collective-permute-start | bytes 1572872 | tf_op jit(solution)/shard_map/ppermute | solution.py:282
  42.3 33.1 %collective-permute-start.7 = (bf16[256,1024]{1,0:T(8,128)(2,1)}, bf16[256,1024]{1,0:T(8,128)(2,1)S(1)}, u32[]{:S(2)}, u32[]{:S(2)}) collective-permute-start(bf16[256,1024]{1,0:T(8,128)(2,1)} %shard_map.193), channel_id=1, source_target_pairs={{0,1},{1,0},{2,3},{3,2},{4,5},{5,4},{6,7},{7,6},{8,9},{9,8},{10,11... | collective-permute-start | bytes 1572872 | tf_op jit(solution)/shard_map/ppermute | solution.py:191
  44.6 30.8 %copy-start.9 = (bf16[1,256,1024]{2,1,0:T(8,128)(2,1)S(1)}, bf16[1,256,1024]{2,1,0:T(8,128)(2,1)}, u32[]{:S(2)}) copy-start(bf16[1,256,1024]{2,1,0:T(8,128)(2,1)} %param.15) | copy-start | bytes 1572868
  44.6 30.8 %copy-start.12 = (f32[256,1024]{1,0:T(8,128)S(1)}, f32[256,1024]{1,0:T(8,128)}, u32[]{:S(2)}) copy-start(f32[256,1024]{1,0:T(8,128)} %get-tuple-element.44) | copy-start | bytes 3145732
  52.2 23.2 %copy-start.1 = (bf16[2,256,512]{2,1,0:T(8,128)(2,1)}, bf16[2,256,512]{2,1,0:T(8,128)(2,1)S(1)}, u32[]{:S(2)}) copy-start(bf16[2,256,512]{2,1,0:T(8,128)(2,1)S(1)} %collective-permute-done.6.refs_5_) | copy-start | bytes 1572868
  52.2 44.3 %collective-permute-start.13 = (bf16[2,256,512]{2,1,0:T(8,128)(2,1)S(1)}, bf16[2,256,512]{2,1,0:T(8,128)(2,1)S(1)}, u32[]{:S(2)}, u32[]{:S(2)}) collective-permute-start(bf16[2,256,512]{2,1,0:T(8,128)(2,1)S(1)} %collective-permute-done.6.refs_5_), channel_id=1, source_target_pairs={{0,16},{16,24},{24,8},{8,0},{1,17},{17,25},{25,9},{9,1},{2,18},{18... | collective-permute-start | bytes 1572872 | tf_op jit(solution)/shard_map/ppermute | solution.py:293
  78.0 24.5 %copy-start.4 = (bf16[256,1024]{1,0:T(8,128)(2,1)S(1)}, bf16[256,1024]{1,0:T(8,128)(2,1)}, u32[]{:S(2)}) copy-start(bf16[256,1024]{1,0:T(8,128)(2,1)} %get-tuple-element.58.signal_ref) | copy-start | bytes 1572868
  84.2 8.0 %collective-permute-start.9 = (bf16[64,1024]{1,0:T(8,128)(2,1)S(1)}, bf16[64,1024]{1,0:T(8,128)(2,1)S(1)}, u32[]{:S(2)}, u32[]{:S(2)}) collective-permute-start(bf16[64,1024]{1,0:T(8,128)(2,1)S(1)} %dynamic-slice_convert_fusion), channel_id=1, source_target_pairs={{0,1},{1,0},{2,3},{3,2},{4,5},{5,4},{6,7},{7,6},{8,9},{9,8},{10,11... | collective-permute-start | bytes 393224 | tf_op jit(solution)/shard_map/ppermute | solution.py:191
  93.2 7.8 %collective-permute-start.10 = (bf16[64,1024]{1,0:T(8,128)(2,1)S(1)}, bf16[64,1024]{1,0:T(8,128)(2,1)S(1)}, u32[]{:S(2)}, u32[]{:S(2)}) collective-permute-start(bf16[64,1024]{1,0:T(8,128)(2,1)S(1)} %add_convert_fusion.2), channel_id=1, source_target_pairs={{0,8},{8,0},{16,24},{24,16},{1,9},{9,1},{17,25},{25,17},{2,10},{10... | collective-permute-start | bytes 393224 | tf_op jit(solution)/shard_map/ppermute | solution.py:191
  96.6 14.0 %copy-start = (bf16[2,256,512]{2,1,0:T(8,128)(2,1)}, bf16[2,256,512]{2,1,0:T(8,128)(2,1)S(1)}, u32[]{:S(2)}) copy-start(bf16[2,256,512]{2,1,0:T(8,128)(2,1)S(1)} %collective-permute-done.13.refs_6_) | copy-start | bytes 1572868
  96.6 13.9 %collective-permute-start.16 = (bf16[1,256,512]{2,1,0:T(8,128)(2,1)S(1)}, bf16[1,256,512]{2,1,0:T(8,128)(2,1)S(1)}, u32[]{:S(2)}, u32[]{:S(2)}) collective-permute-start(bf16[1,256,512]{2,1,0:T(8,128)(2,1)S(1)} %get-tuple-element.61), channel_id=1, source_target_pairs={{0,16},{16,24},{24,8},{8,0},{1,17},{17,25},{25,9},{9,1},{2,18},{18... | collective-permute-start | bytes 786440 | tf_op jit(solution)/shard_map/ppermute | solution.py:296
  101.0 16.1 %collective-permute-start.11 = (bf16[64,1024]{1,0:T(8,128)(2,1)S(1)}, bf16[64,1024]{1,0:T(8,128)(2,1)S(1)}, u32[]{:S(2)}, u32[]{:S(2)}) collective-permute-start(bf16[64,1024]{1,0:T(8,128)(2,1)S(1)} %add_convert_fusion.1), channel_id=1, source_target_pairs={{0,16},{8,24},{16,0},{24,8},{1,17},{9,25},{17,1},{25,9},{2,18},{10... | collective-permute-start | bytes 393224 | tf_op jit(solution)/shard_map/ppermute | solution.py:191
  102.5 19.8 %collective-permute-start.8 = (bf16[128,1024]{1,0:T(8,128)(2,1)S(1)}, bf16[128,1024]{1,0:T(8,128)(2,1)S(1)}, u32[]{:S(2)}, u32[]{:S(2)}) collective-permute-start(bf16[128,1024]{1,0:T(8,128)(2,1)S(1)} %slice.26), channel_id=1, source_target_pairs={{8,0},{16,8},{24,16},{9,1},{17,9},{25,17},{10,2},{18,10},{26,18},{... | collective-permute-start | bytes 786440 | tf_op jit(solution)/shard_map/ppermute | solution.py:329
  106.4 22.7 %collective-permute-start.14 = (bf16[1,256,512]{2,1,0:T(8,128)(2,1)S(1)}, bf16[1,256,512]{2,1,0:T(8,128)(2,1)S(1)}, u32[]{:S(2)}, u32[]{:S(2)}) collective-permute-start(bf16[1,256,512]{2,1,0:T(8,128)(2,1)S(1)} %get-tuple-element.60), channel_id=1, source_target_pairs={{0,16},{16,24},{24,8},{8,0},{1,17},{17,25},{25,9},{9,1},{2,18},{18... | collective-permute-start | bytes 786440 | tf_op jit(solution)/shard_map/ppermute | solution.py:296
  115.1 29.8 %collective-permute-start.17 = (bf16[512,512]{1,0:T(8,128)(2,1)}, bf16[512,512]{1,0:T(8,128)(2,1)S(1)}, u32[]{:S(2)}, u32[]{:S(2)}) collective-permute-start(bf16[512,512]{1,0:T(8,128)(2,1)} %shard_map.199), channel_id=1, source_target_pairs={{0,1},{1,0},{2,3},{3,2},{4,5},{5,4},{6,7},{7,6},{8,9},{9,8},{10,11... | collective-permute-start | bytes 1572872 | tf_op jit(solution)/shard_map/ppermute | solution.py:191
  117.1 18.0 %collective-permute-start.12 = (bf16[64,1024]{1,0:T(8,128)(2,1)S(1)}, bf16[64,1024]{1,0:T(8,128)(2,1)S(1)}, u32[]{:S(2)}, u32[]{:S(2)}) collective-permute-start(bf16[64,1024]{1,0:T(8,128)(2,1)S(1)} %add_convert_fusion), channel_id=1, source_target_pairs={{0,1},{1,0},{2,3},{3,2},{4,5},{5,4},{6,7},{7,6},{8,9},{9,8},{10,11... | collective-permute-start | bytes 393224 | tf_op jit(solution)/shard_map/ppermute | solution.py:191
  133.6 14.1 %collective-permute-start.15 = (bf16[512,512]{1,0:T(8,128)(2,1)}, bf16[512,512]{1,0:T(8,128)(2,1)S(1)}, u32[]{:S(2)}, u32[]{:S(2)}) collective-permute-start(bf16[512,512]{1,0:T(8,128)(2,1)} %shard_map.197), channel_id=1, source_target_pairs={{0,1},{1,0},{2,3},{3,2},{4,5},{5,4},{6,7},{7,6},{8,9},{9,8},{10,11... | collective-permute-start | bytes 1572872 | tf_op jit(solution)/shard_map/ppermute | solution.py:191
  140.9 4.1 %copy-start.3 = (f32[512,512]{1,0:T(8,128)S(1)}, f32[512,512]{1,0:T(8,128)}, u32[]{:S(2)}) copy-start(f32[512,512]{1,0:T(8,128)} %shard_map.198) | copy-start | bytes 3145732
  144.9 2.8 %copy-start.2 = (f32[512,512]{1,0:T(8,128)S(1)}, f32[512,512]{1,0:T(8,128)}, u32[]{:S(2)}) copy-start(f32[512,512]{1,0:T(8,128)} %shard_map.196) | copy-start | bytes 3145732
  (4 other events, 3.0 us)
Sparse Core Ops, SparseCore 0:
  35.6 44.2 all-gather.2

commit v5 on v4

--- a/solution.py
+++ b/solution.py
@@ -12,7 +12,7 @@
 
 f32, bf16 = jnp.float32, jnp.bfloat16
 lanes = 256
-vmem_bytes = 58 * 1024 * 1024
+vmem_bytes = 32 * 1024 * 1024
 
 
 def analysis_table(size, positions):
@@ -41,13 +41,16 @@
     return lax.dot_general(left, right, (((1,), (1,)), ((), ())), preferred_element_type=f32)
 
 
-def forward_transform(table, rows):
-    return dot(table[0], rows) + dot(table[1], rows)
-
-
-def inverse_transform(table, spectrum):
+def forward_transform(table, rows, start):
+    columns = pl.ds(start, rows.shape[0])
+    return dot(table[0, :, columns], rows) + dot(table[1, :, columns], rows)
+
+
+def inverse_transform(table, spectrum, start, count):
     high, low = split_rows(spectrum)
-    return dot(table[0], high) + dot(table[0], low) + dot(table[1], high)
+    rows = pl.ds(start, count)
+    upper = table[0, rows]
+    return dot(upper, high) + dot(upper, low) + dot(table[1, rows], high)
 
 
 def spectrum_product(left, right, conjugate_right):
@@ -61,21 +64,27 @@
     )
 
 
-def prepare_kernel(scale, own_table, tap_table, key_ref, value_ref, taps_ref, skip_ref, spec_ref, filt_ref):
+def prepare_kernel(scale, table, key_ref, value_ref, taps_ref, skip_ref, spec_ref, filt_ref):
     mixed = (key_ref[...].astype(f32) * value_ref[...].astype(f32)).astype(bf16)
-    spec_ref[...] = forward_transform(own_table, mixed)
-    filt = dot_nt(tap_table[0], taps_ref[...]) + dot_nt(tap_table[1], taps_ref[...])
+    taps = taps_ref.shape[1]
+    spec_ref[...] = forward_transform(table, mixed, taps)
+    filt = dot_nt(table[0, :, :taps], taps_ref[...]) + dot_nt(table[1, :, :taps], taps_ref[...])
     half = filt.shape[0] // 2
     filt_ref[:half] = (filt[:half] + skip_ref[...]) * scale
     filt_ref[half:] = filt[half:] * scale
 
 
-def state_kernel(prior_table, synth, prior_ref, own_ref, filt_ref, query_ref, spec_ref, state_ref, gated_ref):
-    spec = own_ref[...] + forward_transform(prior_table, prior_ref[...])
+def state_kernel(table, synth, prior_ref, own_ref, filt_ref, query_ref, spec_ref, state_ref, gated_ref):
+    spec = own_ref[...] + forward_transform(table, prior_ref[...], 0)
     spec_ref[...] = spec
-    state = inverse_transform(synth, spectrum_product(spec, filt_ref[...], False))
+    product = spectrum_product(spec, filt_ref[...], False)
+    state = inverse_transform(synth, product, prior_ref.shape[0], query_ref.shape[0])
     state_ref[...] = state
     gated_ref[0] = (query_ref[...].astype(f32) * state).astype(bf16)
+
+
+def transpose_kernel(rows_ref, out_ref):
+    out_ref[...] = rows_ref[...].T
 
 
 def project_kernel(place_ref, first_mine, second_mine, first_theirs, second_theirs, weight_mine, weight_theirs, out_ref):
@@ -95,22 +104,25 @@
     refs[-1][...] = total.astype(refs[-1].dtype)
 
 
-def lag_kernel(own_table, synth, signal_ref, spec_ref, signal_spec_ref, lag_ref):
-    signal_spec = forward_transform(own_table, signal_ref[...])
+def lag_kernel(table, synth, signal_ref, spec_ref, signal_spec_ref, lag_ref):
+    length, taps = signal_ref.shape[0], lag_ref.shape[0]
+    signal_spec = forward_transform(table, signal_ref[...], 0)
     signal_spec_ref[...] = signal_spec
-    lag_ref[...] = inverse_transform(synth, spectrum_product(signal_spec, spec_ref[...], True))
-
-
-def back_kernel(late_table, synth, own_ref, later_ref, filt_ref, key_ref, value_ref, grad_key_ref, grad_value_ref):
-    spec = own_ref[...] + forward_transform(late_table, later_ref[...])
-    back = inverse_transform(synth, spectrum_product(spec, filt_ref[...], True))
+    product = spectrum_product(signal_spec, spec_ref[...], True)
+    lag_ref[...] = -inverse_transform(synth, product, length, taps)
+
+
+def back_kernel(table, synth, own_ref, later_ref, filt_ref, key_ref, value_ref, grad_key_ref, grad_value_ref):
+    length = key_ref.shape[0]
+    spec = own_ref[...] + forward_transform(table, later_ref[...], length)
+    back = inverse_transform(synth, spectrum_product(spec, filt_ref[...], True), 0, length)
     grad_key_ref[...] = (back * value_ref[...].astype(f32)).astype(bf16)
     grad_value_ref[...] = (back * key_ref[...].astype(f32)).astype(bf16)
 
 
 def estimate(flops, arrays):
     moved = sum(a.size * jnp.dtype(a.dtype).itemsize for a in arrays)
-    return pl.CostEstimate(flops=flops // 64, bytes_accessed=moved // 64, transcendentals=0)
+    return pl.CostEstimate(flops=flops, bytes_accessed=moved, transcendentals=0)
 
 
 def by_channel(kernel, tables, args, outs, channels, flops):
@@ -213,13 +225,7 @@
 
     whole = analysis_table(size, np.arange(size))
     scale = 2.0 / size
-    own_table = split_table(whole[:, :length])
-    tap_table = split_table(whole[:, :taps])
-    late_table = split_table(whole[:, length:])
-    shifted_table = split_table(whole[:, taps:])
-    synth_fwd = np.ascontiguousarray(split_table(whole[:, taps:].T))
-    synth_bwd = np.ascontiguousarray(split_table(whole[:, :length].T))
-    synth_lag = np.ascontiguousarray(split_table(analysis_table(size, np.arange(taps) - taps).T))
+    tables = [split_table(whole), np.ascontiguousarray(split_table(whole.T))]
     spectrum = jax.ShapeDtypeStruct((size, channels), f32)
     rows16 = jax.ShapeDtypeStruct((length, channels), bf16)
     rows32 = jax.ShapeDtypeStruct((length, channels), f32)
@@ -239,17 +245,46 @@
     for turn in range(2):
         route = [(tp_dp(h, c, d), tp_dp(d ^ turn, c, h)) for h, c, d in places]
         rounds.append(lax.ppermute(cot, ("tp", "dp"), route))
-    square = n_seq == n_tp
+    square = n_seq == n_tp == 4 and subs == 2
     if square:
-        holder = [(s % n_dp) * subs + s // n_dp for s in range(n_seq)]
-        route = [(s * n_tp + t, t * n_tp + holder[s]) for s in range(n_seq) for t in range(n_tp)]
-        moved = lax.ppermute(after(cot, prior).T, ("seq", "tp"), route)
+
+        def holder(s, block):
+            return (s + block) % 2 * subs + s // 2
+
+        crossed = {0: (1, 2), 1: (0, 3)}
+        route = [
+            (s * n_tp + t, s * n_tp + sum(crossed[s % 2]) - t)
+            for s in range(n_seq)
+            for t in crossed[s % 2]
+        ]
+        cot_rows = pl.pallas_call(
+            transpose_kernel,
+            grid=(cot.shape[1] // lanes,),
+            in_specs=[pl.BlockSpec((length, lanes), lambda i: (0, i))],
+            out_specs=pl.BlockSpec((lanes, length), lambda i: (i, 0)),
+            out_shape=jax.ShapeDtypeStruct(cot.shape[::-1], bf16),
+            compiler_params=pltpu.CompilerParams(vmem_limit_bytes=vmem_bytes),
+            cost_estimate=estimate(0, [cot, cot]),
+        )(cot)
+        swapped = lax.ppermute(cot_rows, ("seq", "tp"), route)
+        moves_now = sum(
+            jnp.logical_and(lax.axis_index("seq") % 2 == parity, me_tp == t)
+            for parity in crossed
+            for t in crossed[parity]
+        )
+        held = jnp.where(moves_now > 0, swapped, cot_rows)
+        route = []
+        for s in range(n_seq):
+            for t in range(n_tp):
+                block = sum(crossed[s % 2]) - t if t in crossed[s % 2] else t
+                route.append((s * n_tp + t, block * n_tp + holder(s, block)))
+        moved = lax.ppermute(held, ("seq", "tp"), route)
     else:
         moved = cot
 
     own_spec, filt = by_channel(
         functools.partial(prepare_kernel, scale),
-        [shifted_table, tap_table],
+        tables[:1],
         [key_rows, value_rows, filter_taps, skip_gain[None]],
         [spectrum, spectrum],
         channels,
@@ -258,7 +293,7 @@
     prior, own_spec, filt, *rounds = lax.optimization_barrier((prior, own_spec, filt, *rounds))
     mixed_spec, state, gated = by_channel(
         state_kernel,
-        [tap_table, synth_fwd],
+        tables,
         [prior, own_spec, filt, queries],
         [spectrum, rows32, jax.ShapeDtypeStruct((2, length, channels // 2), bf16)],
         channels,
@@ -287,7 +322,7 @@
         cot_pieces = lax.all_gather(moved, "tp", axis=0)
         table = np.zeros((n_seq, n_seq), np.int32)
         for k, s in enumerate(order):
-            table[s] = [holder[order[k - r]] for r in range(n_seq)]
+            table[s] = [holder(order[k - r], s) for r in range(n_seq)]
         sources = jnp.asarray(table)[lax.axis_index("seq")]
         for _ in range(n_seq - 3):
             pieces.append(lax.ppermute(pieces[-1], "seq", ring))
@@ -329,7 +364,7 @@
     later = lax.ppermute(signal[:taps], "seq", [(i + 1, i) for i in range(n_seq - 1)])
     signal_spec, lags = by_channel(
         lag_kernel,
-        [own_table, synth_lag],
+        tables,
         [signal, mixed_spec],
         [spectrum, jax.ShapeDtypeStruct((taps, channels), f32)],
         channels,
@@ -337,7 +372,7 @@
     )
     grad_key, grad_value = by_channel(
         back_kernel,
-        [late_table, synth_bwd],
+        tables,
         [signal_spec, later, filt, key_rows, value_rows],
         [rows16, rows16],
         channels,
@@ -348,6 +383,8 @@
     lag_sum = lax.dynamic_slice_in_dim(lags, me_dp * share, share, axis=0) + swap_pairs(
         lax.dynamic_slice_in_dim(lags, (1 - me_dp) * share, share, axis=0).astype(bf16), "dp", 1
     ).astype(f32)
+    if square:
+        lag_sum, *pieces = lax.optimization_barrier((lag_sum, *pieces))
     distance = 1
     while distance < n_seq:
         rounded = lag_sum.astype(bf16)

time: 157 us -> 150 us (0.955)
  the two profiles are of different devices: /device:TPU:8 before, /device:TPU:26 now
where the time goes in v5:
time: 150 us; the launch traced here: 148 us
  starting transfers between devices  32.8 us (22%)
  Pallas kernels  32.5 us (22%)
  waiting for transfers between devices  29.4 us (20%)
  local copies, waits for them, and re-layouts  28.7 us (19%)
  between operations  14.4 us (10%)
  other arithmetic  10.5 us (7%)
    unnamed x73, local copies, waits for them, and re-layouts  24.8 us
    ppermute x7, waiting for transfers between devices, swap_pairs(): return lax.ppermute(value, axis, [(i, i ^ distance) for i in range(count)])  21.5 us
    pallas_call x4, Pallas kernels, by_channel(): pl.pallas_call(kernel, grid=(channels // lanes,), in_specs=[pl.BlockSpec(...  14 us
    ppermute x7, starting transfers between devices, swap_pairs(): return lax.ppermute(value, axis, [(i, i ^ distance) for i in range(count)])  9.68 us
    pallas_call x4, Pallas kernels, weight_sum(): pl.pallas_call(functools.partial(weight_kernel, count), grid_spec=grid_sp...  9.48 us
    pallas_call x2, Pallas kernels, project(): pl.pallas_call(project_kernel, grid_spec=grid_spec, out_shape=out, compil...  8.5 us
    ppermute x1, starting transfers between devices, per_device(): moved = lax.ppermute(held, ('seq', 'tp'), route)  3.97 us
    ppermute x1, waiting for transfers between devices, per_device(): pieces = [gated, lax.ppermute(gated, 'seq', ring)]  3.95 us
  transfers between devices with their start and end apart: 20, of which 9 were waited for; matrix products, arithmetic and copies ran while one was open for 8% of the time, Pallas kernels for 22%

profile of v5, /device:TPU:26, one launch (start us, length us, event | category | flops | bytes accessed | tf_op | source)
XLA Modules:
  0.0 148.3 jit_solution(18170392853255960312)
XLA Ops:
  8.3 3.4 %collective-permute-start.1 = (bf16[256,1024]{1,0:T(8,128)(2,1)}, bf16[256,1024]{1,0:T(8,128)(2,1)S(1)}, u32[]{:S(2)}, u32[]{:S(2)}) collective-permute-start(bf16[256,1024]{1,0:T(8,128)(2,1)} %bitcast.45), channel_id=1, source_target_pairs={{0,0},{1,4},{2,2},{3,6},{4,1},{5,5},{6,3},{7,7},{8,8},{9,12},{10,1... | collective-permute-start | bytes 1572872 | tf_op jit(solution)/shard_map/ppermute | solution.py:247
  20.2 1.9 %shard_map.145 = (f32[384,1024]{1,0:T(8,128)S(1)}, f32[384,1024]{1,0:T(8,128)S(1)}) custom-call(bf16[2,384,384]{2,1,0:T(8,128)(2,1)S(1)} %copy-done.9, bf16[256,1024]{1,0:T(8,128)(2,1)S(1)} %bitcast.43, bf16[256,1024]{1,0:T(8,128)(2,1)S(1)} %bitcast.41, bf16[1024,128]{1,0:T(8,128)(2,1)S(1)} %copy-done.34, f32[1,1024]{1,0:T(1,128)S(1)} %bitcast.48), custom_call_target="tpu_custom_call" | custom-call | flops 603979776 | bytes 4460544 | tf_op jit(solution)/shard_map/pallas_call | solution.py:137
  22.1 1.7 %collective-permute-done.prior_ref = bf16[128,1024]{1,0:T(8,128)(2,1)S(1)} collective-permute-done((bf16[128,1024]{1,0:T(8,128)(2,1)S(1)}, bf16[128,1024]{1,0:T(8,128)(2,1)S(1)}, u32[]{:S(2)}, u32[]{:S(2)}) %collective-permute-start) | collective-permute-done | bytes 262176 | tf_op jit(solution)/shard_map/ppermute | solution.py:238
  25.4 4.0 %collective-permute-start.4 = (bf16[1024,256]{1,0:T(8,128)(2,1)S(1)}, bf16[1024,256]{1,0:T(8,128)(2,1)}, u32[]{:S(2)}, u32[]{:S(2)}) collective-permute-start(bf16[1024,256]{1,0:T(8,128)(2,1)S(1)} %broadcast_select_fusion), channel_id=1, source_target_pairs={{0,0},{2,16},{4,12},{6,28},{8,24},{10,8},{12,20},{14,4},{16,2},{18... | collective-permute-start | bytes 1572872 | tf_op jit(solution)/shard_map/ppermute | solution.py:281
  29.4 3.4 %collective-permute-start.5 = (bf16[256,1024]{1,0:T(8,128)(2,1)S(1)}, bf16[256,1024]{1,0:T(8,128)(2,1)S(1)}, u32[]{:S(2)}, u32[]{:S(2)}) collective-permute-start(bf16[256,1024]{1,0:T(8,128)(2,1)S(1)} %collective-permute-done.1.first_mine), channel_id=1, source_target_pairs={{0,2},{1,3},{2,0},{3,1},{4,6},{5,7},{6,4},{7,5},{8,10},{9,11},{10,... | collective-permute-start | bytes 1572872 | tf_op jit(solution)/shard_map/ppermute | solution.py:304
  34.0 4.0 %shard_map.146 = (f32[384,1024]{1,0:T(8,128)S(1)}, f32[256,1024]{1,0:T(8,128)S(1)}, bf16[2,256,512]{2,1,0:T(8,128)(2,1)S(1)}) custom-call(bf16[2,384,384]{2,1,0:T(8,128)(2,1)S(1)} %copy-done.9, bf16[2,384,384]{2,1,0:T(8,128)(2,1)S(1)} %copy-done.12, bf16[128,1024]{1,0:T(8,128)(2,1)S(1)} %collective-permute-done.prior_ref, ...), custom_call_target="tpu_custom_call" | custom-call | flops 805306368 | bytes 7077888 | tf_op jit(solution)/shard_map/pallas_call | solution.py:137
  41.6 3.2 %collective-permute-start.7 = (bf16[2,256,512]{2,1,0:T(8,128)(2,1)S(1)}, bf16[2,256,512]{2,1,0:T(8,128)(2,1)S(1)}, u32[]{:S(2)}, u32[]{:S(2)}) collective-permute-start(bf16[2,256,512]{2,1,0:T(8,128)(2,1)S(1)} %get-tuple-element.55.refs_4_), channel_id=1, source_target_pairs={{0,16},{16,24},{24,8},{8,0},{1,17},{17,25},{25,9},{9,1},{2,18},{18... | collective-permute-start | bytes 1572872 | tf_op jit(solution)/shard_map/ppermute | solution.py:317
  44.9 2.2 %copy-done.2 = bf16[1024,2048]{1,0:T(8,128)(2,1)S(1)} copy-done((bf16[1024,2048]{1,0:T(8,128)(2,1)S(1)}, bf16[1024,2048]{1,0:T(8,128)(2,1)}, u32[]{:S(2)}) %copy-start.2) | copy-done | bytes 4194328
  48.1 4.5 %shard_map.149 = bf16[256,1024]{1,0:T(8,128)(2,1)} custom-call(s32[3]{0:T(128)S(1)} %add_add_fusion.1.place_ref, bf16[256,1024]{1,0:T(8,128)(2,1)S(1)} %collective-permute-done.1.first_mine, bf16[256,1024]{1,0:T(8,128)(2,1)S(1)} %collective-permute-done.2.second_mine, bf16[256,1024]{1,0:T(8,128)(2,1)S(1)} %copy-done.17, ...), custom_call_target="tpu_custom_call" | custom-call | flops 1073741824 | bytes 6815744 | tf_op jit(solution)/shard_map/pallas_call | solution.py:164
  52.7 1.5 %collective-permute-start.8 = (bf16[256,1024]{1,0:T(8,128)(2,1)}, bf16[256,1024]{1,0:T(8,128)(2,1)}, u32[]{:S(2)}, u32[]{:S(2)}) collective-permute-start(bf16[256,1024]{1,0:T(8,128)(2,1)} %shard_map.149), channel_id=1, source_target_pairs={{0,1},{1,0},{2,3},{3,2},{4,5},{5,4},{6,7},{7,6},{8,9},{9,8},{10,11... | collective-permute-start | bytes 1572872 | tf_op jit(solution)/shard_map/ppermute | solution.py:203
  54.2 4.0 %collective-permute-done.7.refs_5_ = bf16[2,256,512]{2,1,0:T(8,128)(2,1)S(1)} collective-permute-done((bf16[2,256,512]{2,1,0:T(8,128)(2,1)S(1)}, bf16[2,256,512]{2,1,0:T(8,128)(2,1)S(1)}, u32[]{:S(2)}, u32[]{:S(2)}) %collective-permute-start.7) | collective-permute-done | bytes 524320 | tf_op jit(solution)/shard_map/ppermute | solution.py:317
  58.2 1.8 %collective-permute-start.11 = (bf16[2,256,512]{2,1,0:T(8,128)(2,1)S(1)}, bf16[2,256,512]{2,1,0:T(8,128)(2,1)S(1)}, u32[]{:S(2)}, u32[]{:S(2)}) collective-permute-start(bf16[2,256,512]{2,1,0:T(8,128)(2,1)S(1)} %collective-permute-done.7.refs_5_), channel_id=1, source_target_pairs={{0,16},{16,24},{24,8},{8,0},{1,17},{17,25},{25,9},{9,1},{2,18},{18... | collective-permute-start | bytes 1572872 | tf_op jit(solution)/shard_map/ppermute | solution.py:328
  60.0 2.2 %copy-done.3 = bf16[1024,2048]{1,0:T(8,128)(2,1)S(1)} copy-done((bf16[1024,2048]{1,0:T(8,128)(2,1)S(1)}, bf16[1024,2048]{1,0:T(8,128)(2,1)}, u32[]{:S(2)}) %copy-start.3) | copy-done | bytes 4194328
  64.3 4.0 %shard_map.148 = f32[256,1024]{1,0:T(8,128)S(1)} custom-call(s32[3]{0:T(128)S(1)} %add_add_fusion.place_ref, bf16[256,1024]{1,0:T(8,128)(2,1)S(1)} %collective-permute-done.1.first_mine, bf16[256,1024]{1,0:T(8,128)(2,1)S(1)} %copy-done.15, bf16[256,1024]{1,0:T(8,128)(2,1)S(1)} %copy-done.18, bf16[256,1024]{1,0:T(8,128)(2,1)} %collective-permute-done.6.second_theirs, ...), custom_call_target="tpu_custom_call" | custom-call | flops 1073741824 | bytes 7340032 | tf_op jit(solution)/shard_map/pallas_call | solution.py:164
  68.3 2.4 %multiply_convert_fusion = (bf16[256,1024]{1,0:T(8,128)(2,1)S(1)}, bf16[1,256,1024]{2,1,0:T(8,128)(2,1)}) fusion(f32[256,1024]{1,0:T(8,128)S(1)} %shard_map.148, bf16[256,1024]{1,0:T(8,128)(2,1)} %collective-permute-done.8, bf16[1,256,1024]{2,1,0:T(8,128)(2,1)S(1)} %copy-done.20, f32[256,1024]{1,0:T(8,128)S(1)} %copy-done.30), kind=kLoop, calls=%fused_computation.3 | loop fusion | flops 1835008 | bytes 4194304 | tf_op jit(solution)/shard_map/convert_element_type | solution.py:363
  70.7 3.8 %shard_map.150 = (f32[384,1024]{1,0:T(8,128)S(1)}, f32[128,1024]{1,0:T(8,128)}) custom-call(bf16[2,384,384]{2,1,0:T(8,128)(2,1)S(1)} %copy-done.10, bf16[2,384,384]{2,1,0:T(8,128)(2,1)S(1)} %copy-done.12, bf16[256,1024]{1,0:T(8,128)(2,1)S(1)} %get-tuple-element.64.signal_ref, f32[384,1024]{1,0:T(8,128)S(1)} %copy-done.22), custom_call_target="tpu_custom_call" | custom-call | flops 704643072 | bytes 4194304 | tf_op jit(solution)/shard_map/pallas_call | solution.py:137
  77.3 4.8 %collective-permute-done.10 = bf16[64,1024]{1,0:T(8,128)(2,1)S(1)} collective-permute-done((bf16[64,1024]{1,0:T(8,128)(2,1)S(1)}, bf16[64,1024]{1,0:T(8,128)(2,1)S(1)}, u32[]{:S(2)}, u32[]{:S(2)}) %collective-permute-start.10) | collective-permute-done | bytes 131104 | tf_op jit(solution)/shard_map/ppermute | solution.py:203
  83.9 4.3 %collective-permute-done.12 = bf16[64,1024]{1,0:T(8,128)(2,1)S(1)} collective-permute-done((bf16[64,1024]{1,0:T(8,128)(2,1)S(1)}, bf16[64,1024]{1,0:T(8,128)(2,1)S(1)}, u32[]{:S(2)}, u32[]{:S(2)}) %collective-permute-start.12) | collective-permute-done | bytes 131104 | tf_op jit(solution)/shard_map/ppermute | solution.py:203
  88.2 2.0 %collective-permute-start.13 = (bf16[64,1024]{1,0:T(8,128)(2,1)S(1)}, bf16[64,1024]{1,0:T(8,128)(2,1)S(1)}, u32[]{:S(2)}, u32[]{:S(2)}) collective-permute-start(bf16[64,1024]{1,0:T(8,128)(2,1)S(1)} %add_convert_fusion.1), channel_id=1, source_target_pairs={{0,16},{8,24},{16,0},{24,8},{1,17},{9,25},{17,1},{25,9},{2,18},{10... | collective-permute-start | bytes 393224 | tf_op jit(solution)/shard_map/ppermute | solution.py:203
  92.1 3.0 %collective-permute-start.9 = (bf16[128,1024]{1,0:T(8,128)(2,1)S(1)}, bf16[128,1024]{1,0:T(8,128)(2,1)S(1)}, u32[]{:S(2)}, u32[]{:S(2)}) collective-permute-start(bf16[128,1024]{1,0:T(8,128)(2,1)S(1)} %slice.26), channel_id=1, source_target_pairs={{8,0},{16,8},{24,16},{9,1},{17,9},{25,17},{10,2},{18,10},{26,18},{... | collective-permute-start | bytes 786440 | tf_op jit(solution)/shard_map/ppermute | solution.py:364
  96.2 10.2 %collective-permute-done.13 = bf16[64,1024]{1,0:T(8,128)(2,1)S(1)} collective-permute-done((bf16[64,1024]{1,0:T(8,128)(2,1)S(1)}, bf16[64,1024]{1,0:T(8,128)(2,1)S(1)}, u32[]{:S(2)}, u32[]{:S(2)}) %collective-permute-start.13) | collective-permute-done | bytes 131104 | tf_op jit(solution)/shard_map/ppermute | solution.py:203
  106.4 3.3 %collective-permute-start.14 = (bf16[64,1024]{1,0:T(8,128)(2,1)S(1)}, bf16[64,1024]{1,0:T(8,128)(2,1)}, u32[]{:S(2)}, u32[]{:S(2)}) collective-permute-start(bf16[64,1024]{1,0:T(8,128)(2,1)S(1)} %add_convert_fusion), channel_id=1, source_target_pairs={{0,1},{1,0},{2,3},{3,2},{4,5},{5,4},{6,7},{7,6},{8,9},{9,8},{10,11... | collective-permute-start | bytes 393224 | tf_op jit(solution)/shard_map/ppermute | solution.py:203
  109.8 1.6 %copy-done = bf16[4096,256]{1,0:T(8,128)(2,1)S(1)} copy-done((bf16[4096,256]{1,0:T(8,128)(2,1)S(1)}, bf16[4096,256]{1,0:T(8,128)(2,1)}, u32[]{:S(2)}) %copy-start) | copy-done | bytes 2097176
  111.4 2.3 %shard_map.155 = bf16[512,512]{1,0:T(8,128)(2,1)} custom-call(s32[5]{0:T(128)S(1)} %get-tuple-element.70.place_ref, bf16[4,1024,256]{2,1,0:T(8,128)(2,1)S(1)} %bitcast.24, bf16[4,1024,256]{2,1,0:T(8,128)(2,1)S(1)} %bitcast.25, bf16[4,1024,256]{2,1,0:T(8,128)(2,1)S(1)} %bitcast.26, bf16[4,1024,256]{2,1,0:T(8,128)(2,1)S(1)} %bitcast.27, ...), custom_call_target="tpu_custom_call" | custom-call | flops 536870912 | bytes 4456448 | tf_op jit(solution)/shard_map/pallas_call | solution.py:192
  115.4 4.4 %shard_map.151 = (bf16[256,1024]{1,0:T(8,128)(2,1)}, bf16[256,1024]{1,0:T(8,128)(2,1)}) custom-call(bf16[2,384,384]{2,1,0:T(8,128)(2,1)S(1)} %copy-done.11, bf16[2,384,384]{2,1,0:T(8,128)(2,1)S(1)} %copy-done.13, f32[384,1024]{1,0:T(8,128)S(1)} %copy-done.24, bf16[128,1024]{1,0:T(8,128)(2,1)S(1)} %copy-done.33, f32[384,1024]{1,0:T(8,128)S(1)} %copy-done.8, ...), custom_call_target="tpu_custom_call" | custom-call | flops 805306368 | bytes 5505024 | tf_op jit(solution)/shard_map/pallas_call | solution.py:137
  119.9 3.2 %shard_map.153 = bf16[512,512]{1,0:T(8,128)(2,1)} custom-call(s32[5]{0:T(128)S(1)} %get-tuple-element.70.place_ref, bf16[4,1024,256]{2,1,0:T(8,128)(2,1)S(1)} %bitcast.28, bf16[4,1024,256]{2,1,0:T(8,128)(2,1)S(1)} %bitcast.29, bf16[4,1024,256]{2,1,0:T(8,128)(2,1)S(1)} %bitcast.30, bf16[4,1024,256]{2,1,0:T(8,128)(2,1)S(1)} %bitcast.31, ...), custom_call_target="tpu_custom_call" | custom-call | flops 536870912 | bytes 4456448 | tf_op jit(solution)/shard_map/pallas_call | solution.py:192
  123.0 2.0 %collective-permute-start.16 = (bf16[512,512]{1,0:T(8,128)(2,1)}, bf16[512,512]{1,0:T(8,128)(2,1)}, u32[]{:S(2)}, u32[]{:S(2)}) collective-permute-start(bf16[512,512]{1,0:T(8,128)(2,1)} %shard_map.153), channel_id=1, source_target_pairs={{0,1},{1,0},{2,3},{3,2},{4,5},{5,4},{6,7},{7,6},{8,9},{9,8},{10,11... | collective-permute-start | bytes 1572872 | tf_op jit(solution)/shard_map/ppermute | solution.py:203
  126.8 2.0 %copy.16 = f32[1024,128]{1,0:T(8,128)} copy(f32[1024,128]{0,1:T(8,128)} %multiply_bitcast_fusion) | data formatting | bytes 1048576
  131.2 1.6 %shard_map.154 = f32[512,512]{1,0:T(8,128)S(1)} custom-call(s32[5]{0:T(128)S(1)} %get-tuple-element.71.place_ref, bf16[4,1024,256]{2,1,0:T(8,128)(2,1)S(1)} %bitcast.32, bf16[4,1024,256]{2,1,0:T(8,128)(2,1)S(1)} %bitcast.33, bf16[4,1024,256]{2,1,0:T(8,128)(2,1)S(1)} %bitcast.34, bf16[4,1024,256]{2,1,0:T(8,128)(2,1)S(1)} %bitcast.35, ...), custom_call_target="tpu_custom_call" | custom-call | flops 536870912 | bytes 4980736 | tf_op jit(solution)/shard_map/pallas_call | solution.py:192
  132.8 2.4 %shard_map.152 = f32[512,512]{1,0:T(8,128)S(1)} custom-call(s32[5]{0:T(128)S(1)} %get-tuple-element.71.place_ref, bf16[4,1024,256]{2,1,0:T(8,128)(2,1)S(1)} %bitcast.36, bf16[4,1024,256]{2,1,0:T(8,128)(2,1)S(1)} %bitcast.37, bf16[4,1024,256]{2,1,0:T(8,128)(2,1)S(1)} %bitcast.38, bf16[4,1024,256]{2,1,0:T(8,128)(2,1)S(1)} %bitcast.39, ...), custom_call_target="tpu_custom_call" | custom-call | flops 536870912 | bytes 4980736 | tf_op jit(solution)/shard_map/pallas_call | solution.py:192
  136.5 2.2 %collective-permute-done.16 = bf16[512,512]{1,0:T(8,128)(2,1)} collective-permute-done((bf16[512,512]{1,0:T(8,128)(2,1)}, bf16[512,512]{1,0:T(8,128)(2,1)}, u32[]{:S(2)}, u32[]{:S(2)}) %collective-permute-start.16) | collective-permute-done | bytes 524320 | tf_op jit(solution)/shard_map/ppermute | solution.py:203
  140.0 1.5 pad_maximum_fusion
  (112 shorter events, 35.2 us)
Async XLA Ops:
  7.2 102.6 %all-gather.3.cloned.1.call-start = ((), (), s32[]{:S(2)}) async-start(), calls=%async_computation | async-start | bytes 2621440 | tf_op jit(solution)/shard_map/all_gather | solution.py:322
  8.3 16.7 %collective-permute-start.1 = (bf16[256,1024]{1,0:T(8,128)(2,1)}, bf16[256,1024]{1,0:T(8,128)(2,1)S(1)}, u32[]{:S(2)}, u32[]{:S(2)}) collective-permute-start(bf16[256,1024]{1,0:T(8,128)(2,1)} %bitcast.45), channel_id=1, source_target_pairs={{0,0},{1,4},{2,2},{3,6},{4,1},{5,5},{6,3},{7,7},{8,8},{9,12},{10,1... | collective-permute-start | bytes 1572872 | tf_op jit(solution)/shard_map/ppermute | solution.py:247
  11.7 13.6 %collective-permute-start.2 = (bf16[256,1024]{1,0:T(8,128)(2,1)}, bf16[256,1024]{1,0:T(8,128)(2,1)S(1)}, u32[]{:S(2)}, u32[]{:S(2)}) collective-permute-start(bf16[256,1024]{1,0:T(8,128)(2,1)} %bitcast.46), channel_id=1, source_target_pairs={{0,4},{1,0},{2,6},{3,2},{4,5},{5,1},{6,7},{7,3},{8,12},{9,8},{10,1... | collective-permute-start | bytes 1572872 | tf_op jit(solution)/shard_map/ppermute | solution.py:247
  12.9 20.1 %copy-start.12 = (bf16[2,384,384]{2,1,0:T(8,128)(2,1)S(1)}, bf16[2,384,384]{2,1,0:T(8,128)(2,1)}, u32[]{:S(2)}) copy-start(bf16[2,384,384]{2,1,0:T(8,128)(2,1)} %constant.70.clone.synth) | copy-start | bytes 1769476
  13.3 12.0 %collective-permute-start.3 = (bf16[1024,256]{1,0:T(8,128)(2,1)S(1)}, bf16[1024,256]{1,0:T(8,128)(2,1)S(1)}, u32[]{:S(2)}, u32[]{:S(2)}) collective-permute-start(bf16[1024,256]{1,0:T(8,128)(2,1)S(1)} %shard_map.147), channel_id=1, source_target_pairs={{2,4},{4,2},{8,14},{14,8},{18,20},{20,18},{24,30},{30,24},{3,5},{5... | collective-permute-start | bytes 1572872 | tf_op jit(solution)/shard_map/ppermute | solution.py:269
  14.0 9.7 %collective-permute-start = (bf16[128,1024]{1,0:T(8,128)(2,1)S(1)}, bf16[128,1024]{1,0:T(8,128)(2,1)S(1)}, u32[]{:S(2)}, u32[]{:S(2)}) collective-permute-start(bf16[128,1024]{1,0:T(8,128)(2,1)S(1)} %fusion.1), channel_id=1, source_target_pairs={{0,8},{8,16},{16,24},{1,9},{9,17},{17,25},{2,10},{10,18},{18,26},{... | collective-permute-start | bytes 786440 | tf_op jit(solution)/shard_map/ppermute | solution.py:238
  22.1 15.9 %copy-start.7 = (f32[384,1024]{1,0:T(8,128)}, f32[384,1024]{1,0:T(8,128)S(1)}, u32[]{:S(2)}) copy-start(f32[384,1024]{1,0:T(8,128)S(1)} %get-tuple-element.38.filt_ref) | copy-start | bytes 4718596
  25.4 19.5 %copy-start.14 = (bf16[256,1024]{1,0:T(8,128)(2,1)}, bf16[256,1024]{1,0:T(8,128)(2,1)S(1)}, u32[]{:S(2)}) copy-start(bf16[256,1024]{1,0:T(8,128)(2,1)S(1)} %collective-permute-done.2.second_mine) | copy-start | bytes 1572868
  25.4 15.4 %collective-permute-start.4 = (bf16[1024,256]{1,0:T(8,128)(2,1)S(1)}, bf16[1024,256]{1,0:T(8,128)(2,1)}, u32[]{:S(2)}, u32[]{:S(2)}) collective-permute-start(bf16[1024,256]{1,0:T(8,128)(2,1)S(1)} %broadcast_select_fusion), channel_id=1, source_target_pairs={{0,0},{2,16},{4,12},{6,28},{8,24},{10,8},{12,20},{14,4},{16,2},{18... | collective-permute-start | bytes 1572872 | tf_op jit(solution)/shard_map/ppermute | solution.py:281
  29.4 11.4 %collective-permute-start.5 = (bf16[256,1024]{1,0:T(8,128)(2,1)S(1)}, bf16[256,1024]{1,0:T(8,128)(2,1)S(1)}, u32[]{:S(2)}, u32[]{:S(2)}) collective-permute-start(bf16[256,1024]{1,0:T(8,128)(2,1)S(1)} %collective-permute-done.1.first_mine), channel_id=1, source_target_pairs={{0,2},{1,3},{2,0},{3,1},{4,6},{5,7},{6,4},{7,5},{8,10},{9,11},{10,... | collective-permute-start | bytes 1572872 | tf_op jit(solution)/shard_map/ppermute | solution.py:304
  32.9 7.9 %collective-permute-start.6 = (bf16[256,1024]{1,0:T(8,128)(2,1)S(1)}, bf16[256,1024]{1,0:T(8,128)(2,1)}, u32[]{:S(2)}, u32[]{:S(2)}) collective-permute-start(bf16[256,1024]{1,0:T(8,128)(2,1)S(1)} %collective-permute-done.2.second_mine), channel_id=1, source_target_pairs={{0,2},{1,3},{2,0},{3,1},{4,6},{5,7},{6,4},{7,5},{8,10},{9,11},{10,... | collective-permute-start | bytes 1572872 | tf_op jit(solution)/shard_map/ppermute | solution.py:304
  41.6 16.6 %collective-permute-start.7 = (bf16[2,256,512]{2,1,0:T(8,128)(2,1)S(1)}, bf16[2,256,512]{2,1,0:T(8,128)(2,1)S(1)}, u32[]{:S(2)}, u32[]{:S(2)}) collective-permute-start(bf16[2,256,512]{2,1,0:T(8,128)(2,1)S(1)} %get-tuple-element.55.refs_4_), channel_id=1, source_target_pairs={{0,16},{16,24},{24,8},{8,0},{1,17},{17,25},{25,9},{9,1},{2,18},{18... | collective-permute-start | bytes 1572872 | tf_op jit(solution)/shard_map/ppermute | solution.py:317
  52.7 15.6 %collective-permute-start.8 = (bf16[256,1024]{1,0:T(8,128)(2,1)}, bf16[256,1024]{1,0:T(8,128)(2,1)}, u32[]{:S(2)}, u32[]{:S(2)}) collective-permute-start(bf16[256,1024]{1,0:T(8,128)(2,1)} %shard_map.149), channel_id=1, source_target_pairs={{0,1},{1,0},{2,3},{3,2},{4,5},{5,4},{6,7},{7,6},{8,9},{9,8},{10,11... | collective-permute-start | bytes 1572872 | tf_op jit(solution)/shard_map/ppermute | solution.py:203
  58.2 51.6 %copy-start.4 = (bf16[2,256,512]{2,1,0:T(8,128)(2,1)}, bf16[2,256,512]{2,1,0:T(8,128)(2,1)S(1)}, u32[]{:S(2)}) copy-start(bf16[2,256,512]{2,1,0:T(8,128)(2,1)S(1)} %collective-permute-done.7.refs_5_) | copy-start | bytes 1572868
  58.2 24.9 %collective-permute-start.11 = (bf16[2,256,512]{2,1,0:T(8,128)(2,1)S(1)}, bf16[2,256,512]{2,1,0:T(8,128)(2,1)S(1)}, u32[]{:S(2)}, u32[]{:S(2)}) collective-permute-start(bf16[2,256,512]{2,1,0:T(8,128)(2,1)S(1)} %collective-permute-done.7.refs_5_), channel_id=1, source_target_pairs={{0,16},{16,24},{24,8},{8,0},{1,17},{17,25},{25,9},{9,1},{2,18},{18... | collective-permute-start | bytes 1572872 | tf_op jit(solution)/shard_map/ppermute | solution.py:328
  64.3 4.0 %copy-start.20 = (bf16[1,256,1024]{2,1,0:T(8,128)(2,1)S(1)}, bf16[1,256,1024]{2,1,0:T(8,128)(2,1)}, u32[]{:S(2)}) copy-start(bf16[1,256,1024]{2,1,0:T(8,128)(2,1)} %param.10) | copy-start | bytes 1572868
  64.3 4.0 %copy-start.30 = (f32[256,1024]{1,0:T(8,128)S(1)}, f32[256,1024]{1,0:T(8,128)}, u32[]{:S(2)}) copy-start(f32[256,1024]{1,0:T(8,128)} %copy-done.29) | copy-start | bytes 3145732
  76.6 5.5 %collective-permute-start.10 = (bf16[64,1024]{1,0:T(8,128)(2,1)S(1)}, bf16[64,1024]{1,0:T(8,128)(2,1)S(1)}, u32[]{:S(2)}, u32[]{:S(2)}) collective-permute-start(bf16[64,1024]{1,0:T(8,128)(2,1)S(1)} %dynamic-slice_convert_fusion), channel_id=1, source_target_pairs={{0,1},{1,0},{2,3},{3,2},{4,5},{5,4},{6,7},{7,6},{8,9},{9,8},{10,11... | collective-permute-start | bytes 393224 | tf_op jit(solution)/shard_map/ppermute | solution.py:203
  83.1 5.0 %collective-permute-start.12 = (bf16[64,1024]{1,0:T(8,128)(2,1)S(1)}, bf16[64,1024]{1,0:T(8,128)(2,1)S(1)}, u32[]{:S(2)}, u32[]{:S(2)}) collective-permute-start(bf16[64,1024]{1,0:T(8,128)(2,1)S(1)} %convert_add_fusion.1), channel_id=1, source_target_pairs={{0,8},{8,0},{16,24},{24,16},{1,9},{9,1},{17,25},{25,17},{2,10},{10... | collective-permute-start | bytes 393224 | tf_op jit(solution)/shard_map/ppermute | solution.py:203
  88.2 18.2 %collective-permute-start.13 = (bf16[64,1024]{1,0:T(8,128)(2,1)S(1)}, bf16[64,1024]{1,0:T(8,128)(2,1)S(1)}, u32[]{:S(2)}, u32[]{:S(2)}) collective-permute-start(bf16[64,1024]{1,0:T(8,128)(2,1)S(1)} %add_convert_fusion.1), channel_id=1, source_target_pairs={{0,16},{8,24},{16,0},{24,8},{1,17},{9,25},{17,1},{25,9},{2,18},{10... | collective-permute-start | bytes 393224 | tf_op jit(solution)/shard_map/ppermute | solution.py:203
  91.0 18.7 %collective-permute-start.17 = (bf16[1,256,512]{2,1,0:T(8,128)(2,1)}, bf16[1,256,512]{2,1,0:T(8,128)(2,1)S(1)}, u32[]{:S(2)}, u32[]{:S(2)}) collective-permute-start(bf16[1,256,512]{2,1,0:T(8,128)(2,1)} %get-tuple-element.67), channel_id=1, source_target_pairs={{0,16},{16,24},{24,8},{8,0},{1,17},{17,25},{25,9},{9,1},{2,18},{18... | collective-permute-start | bytes 786440 | tf_op jit(solution)/shard_map/ppermute | solution.py:331
  92.1 21.6 %collective-permute-start.9 = (bf16[128,1024]{1,0:T(8,128)(2,1)S(1)}, bf16[128,1024]{1,0:T(8,128)(2,1)S(1)}, u32[]{:S(2)}, u32[]{:S(2)}) collective-permute-start(bf16[128,1024]{1,0:T(8,128)(2,1)S(1)} %slice.26), channel_id=1, source_target_pairs={{8,0},{16,8},{24,16},{9,1},{17,9},{25,17},{10,2},{18,10},{26,18},{... | collective-permute-start | bytes 786440 | tf_op jit(solution)/shard_map/ppermute | solution.py:364
  95.1 24.8 %collective-permute-start.15 = (bf16[1,256,512]{2,1,0:T(8,128)(2,1)}, bf16[1,256,512]{2,1,0:T(8,128)(2,1)}, u32[]{:S(2)}, u32[]{:S(2)}) collective-permute-start(bf16[1,256,512]{2,1,0:T(8,128)(2,1)} %get-tuple-element.66), channel_id=1, source_target_pairs={{0,16},{16,24},{24,8},{8,0},{1,17},{17,25},{25,9},{9,1},{2,18},{18... | collective-permute-start | bytes 786440 | tf_op jit(solution)/shard_map/ppermute | solution.py:331
  106.4 18.6 %collective-permute-start.14 = (bf16[64,1024]{1,0:T(8,128)(2,1)S(1)}, bf16[64,1024]{1,0:T(8,128)(2,1)}, u32[]{:S(2)}, u32[]{:S(2)}) collective-permute-start(bf16[64,1024]{1,0:T(8,128)(2,1)S(1)} %add_convert_fusion), channel_id=1, source_target_pairs={{0,1},{1,0},{2,3},{3,2},{4,5},{5,4},{6,7},{7,6},{8,9},{9,8},{10,11... | collective-permute-start | bytes 393224 | tf_op jit(solution)/shard_map/ppermute | solution.py:203
  111.4 3.1 %copy-start.11 = (bf16[2,384,384]{2,1,0:T(8,128)(2,1)S(1)}, bf16[2,384,384]{2,1,0:T(8,128)(2,1)}, u32[]{:S(2)}) copy-start(bf16[2,384,384]{2,1,0:T(8,128)(2,1)} %constant.69.clone.table) | copy-start | bytes 1769476
  111.4 3.1 %copy-start.13 = (bf16[2,384,384]{2,1,0:T(8,128)(2,1)S(1)}, bf16[2,384,384]{2,1,0:T(8,128)(2,1)}, u32[]{:S(2)}) copy-start(bf16[2,384,384]{2,1,0:T(8,128)(2,1)} %constant.70.clone.synth) | copy-start | bytes 1769476
  111.4 3.1 %copy-start.24 = (f32[384,1024]{1,0:T(8,128)S(1)}, f32[384,1024]{1,0:T(8,128)}, u32[]{:S(2)}) copy-start(f32[384,1024]{1,0:T(8,128)} %copy-done.23) | copy-start | bytes 4718596
  111.4 3.1 %copy-start.26 = (bf16[1,256,1024]{2,1,0:T(8,128)(2,1)S(1)}, bf16[1,256,1024]{2,1,0:T(8,128)(2,1)}, u32[]{:S(2)}) copy-start(bf16[1,256,1024]{2,1,0:T(8,128)(2,1)} %param.12) | copy-start | bytes 1572868
  113.7 21.6 %collective-permute-start.18 = (bf16[512,512]{1,0:T(8,128)(2,1)}, bf16[512,512]{1,0:T(8,128)(2,1)}, u32[]{:S(2)}, u32[]{:S(2)}) collective-permute-start(bf16[512,512]{1,0:T(8,128)(2,1)} %shard_map.155), channel_id=1, source_target_pairs={{0,1},{1,0},{2,3},{3,2},{4,5},{5,4},{6,7},{7,6},{8,9},{9,8},{10,11... | collective-permute-start | bytes 1572872 | tf_op jit(solution)/shard_map/ppermute | solution.py:203
  115.4 4.4 %copy-start.1 = (bf16[4096,256]{1,0:T(8,128)(2,1)S(1)}, bf16[4096,256]{1,0:T(8,128)(2,1)}, u32[]{:S(2)}) copy-start(bf16[4096,256]{1,0:T(8,128)(2,1)} %all-gather.3.cloned.1.call-done) | copy-start | bytes 6291460
  115.4 4.4 %copy-start.5 = (bf16[2,256,512]{2,1,0:T(8,128)(2,1)S(1)}, bf16[2,256,512]{2,1,0:T(8,128)(2,1)}, u32[]{:S(2)}) copy-start(bf16[2,256,512]{2,1,0:T(8,128)(2,1)} %copy-done.4) | copy-start | bytes 1572868
  123.0 15.7 %collective-permute-start.16 = (bf16[512,512]{1,0:T(8,128)(2,1)}, bf16[512,512]{1,0:T(8,128)(2,1)}, u32[]{:S(2)}, u32[]{:S(2)}) collective-permute-start(bf16[512,512]{1,0:T(8,128)(2,1)} %shard_map.153), channel_id=1, source_target_pairs={{0,1},{1,0},{2,3},{3,2},{4,5},{5,4},{6,7},{7,6},{8,9},{9,8},{10,11... | collective-permute-start | bytes 1572872 | tf_op jit(solution)/shard_map/ppermute | solution.py:203
  (24 other events, 33.8 us)
Sparse Core Ops, SparseCore 0:
  41.0 26.1 all-gather.2

commit v6 on v5

--- a/solution.py
+++ b/solution.py
@@ -64,23 +64,36 @@
     )
 
 
-def prepare_kernel(scale, table, key_ref, value_ref, taps_ref, skip_ref, spec_ref, filt_ref):
+def mixed_spectrum(table, prior_ref, key_ref, value_ref):
     mixed = (key_ref[...].astype(f32) * value_ref[...].astype(f32)).astype(bf16)
+    prior = prior_ref[...]
+    return forward_transform(table, prior, 0) + forward_transform(table, mixed, prior.shape[0])
+
+
+def filter_spectrum(scale, table, taps_ref, skip_ref):
     taps = taps_ref.shape[1]
-    spec_ref[...] = forward_transform(table, mixed, taps)
     filt = dot_nt(table[0, :, :taps], taps_ref[...]) + dot_nt(table[1, :, :taps], taps_ref[...])
     half = filt.shape[0] // 2
-    filt_ref[:half] = (filt[:half] + skip_ref[...]) * scale
-    filt_ref[half:] = filt[half:] * scale
-
-
-def state_kernel(table, synth, prior_ref, own_ref, filt_ref, query_ref, spec_ref, state_ref, gated_ref):
-    spec = own_ref[...] + forward_transform(table, prior_ref[...], 0)
-    spec_ref[...] = spec
-    product = spectrum_product(spec, filt_ref[...], False)
+    return jnp.concatenate([(filt[:half] + skip_ref[...]) * scale, filt[half:] * scale], axis=0)
+
+
+def state_kernel(
+    scale, table, synth, prior_ref, key_ref, value_ref, taps_ref, skip_ref, query_ref, state_ref, first_ref, second_ref
+):
+    spec = mixed_spectrum(table, prior_ref, key_ref, value_ref)
+    product = spectrum_product(spec, filter_spectrum(scale, table, taps_ref, skip_ref), False)
     state = inverse_transform(synth, product, prior_ref.shape[0], query_ref.shape[0])
     state_ref[...] = state
-    gated_ref[0] = (query_ref[...].astype(f32) * state).astype(bf16)
+    gated = (query_ref[...].astype(f32) * state).astype(bf16)
+    in_first = pl.program_id(0) < pl.num_programs(0) // 2
+
+    @pl.when(in_first)
+    def _():
+        first_ref[...] = gated
+
+    @pl.when(jnp.logical_not(in_first))
+    def _():
+        second_ref[...] = gated
 
 
 def transpose_kernel(rows_ref, out_ref):
@@ -97,25 +110,36 @@
 
 
 def weight_kernel(count, place_ref, *refs):
+    out_ref, held_ref = refs[2 * count :]
+    for n, gated_ref in enumerate(refs[count : 2 * count]):
+        held_ref[n] = gated_ref[...]
     total = None
-    for cot_ref, gated_ref in zip(refs[:count], refs[count : 2 * count]):
-        part = dot(cot_ref[0], gated_ref[0])
+    for n, cot_ref in enumerate(refs[:count]):
+        part = dot(cot_ref[...], held_ref[place_ref[n]])
         total = part if total is None else total + part
-    refs[-1][...] = total.astype(refs[-1].dtype)
-
-
-def lag_kernel(table, synth, signal_ref, spec_ref, signal_spec_ref, lag_ref):
+    out_ref[...] = total.astype(out_ref.dtype)
+
+
+def lag_kernel(
+    table, synth, own_ref, other_ref, state_ref, query_ref, prior_ref, key_ref, value_ref, grad_ref, signal_ref, lag_ref
+):
     length, taps = signal_ref.shape[0], lag_ref.shape[0]
-    signal_spec = forward_transform(table, signal_ref[...], 0)
-    signal_spec_ref[...] = signal_spec
-    product = spectrum_product(signal_spec, spec_ref[...], True)
+    grad_gated = own_ref[...] + other_ref[...].astype(f32)
+    grad_ref[...] = (grad_gated * state_ref[...]).astype(bf16)
+    signal = (grad_gated * query_ref[...].astype(f32)).astype(bf16)
+    signal_ref[...] = signal
+    spec = mixed_spectrum(table, prior_ref, key_ref, value_ref)
+    product = spectrum_product(forward_transform(table, signal, 0), spec, True)
     lag_ref[...] = -inverse_transform(synth, product, length, taps)
 
 
-def back_kernel(table, synth, own_ref, later_ref, filt_ref, key_ref, value_ref, grad_key_ref, grad_value_ref):
+def back_kernel(
+    scale, table, synth, signal_ref, later_ref, taps_ref, skip_ref, key_ref, value_ref, grad_key_ref, grad_value_ref
+):
     length = key_ref.shape[0]
-    spec = own_ref[...] + forward_transform(table, later_ref[...], length)
-    back = inverse_transform(synth, spectrum_product(spec, filt_ref[...], True), 0, length)
+    spec = forward_transform(table, signal_ref[...], 0) + forward_transform(table, later_ref[...], length)
+    product = spectrum_product(spec, filter_spectrum(scale, table, taps_ref, skip_ref), True)
+    back = inverse_transform(synth, product, 0, length)
     grad_key_ref[...] = (back * value_ref[...].astype(f32)).astype(bf16)
     grad_value_ref[...] = (back * key_ref[...].astype(f32)).astype(bf16)
 
@@ -126,20 +150,24 @@
 
 
 def by_channel(kernel, tables, args, outs, channels, flops):
-    def column_spec(shape):
-        if len(shape) == 3:
-            per = shape[2] // lanes
-            return pl.BlockSpec((1, shape[1], lanes), lambda i: (i // per, 0, i % per))
+    steps = channels // lanes
+
+    def column_spec(shape, place=0):
+        if shape[1] == channels // 2:
+            shift = place % 2 * (steps // 2)
+            return pl.BlockSpec(
+                (shape[0], lanes), lambda i: (0, jnp.clip(i - shift, 0, steps // 2 - 1))
+            )
         if shape[1] != channels:
             return pl.BlockSpec((lanes, shape[1]), lambda i: (i, 0))
         return pl.BlockSpec((shape[0], lanes), lambda i: (0, i))
 
     return pl.pallas_call(
         kernel,
-        grid=(channels // lanes,),
+        grid=(steps,),
         in_specs=[pl.BlockSpec(t.shape, lambda i: (0, 0, 0)) for t in tables]
         + [column_spec(a.shape) for a in args],
-        out_specs=[column_spec(o.shape) for o in outs],
+        out_specs=[column_spec(o.shape, n + 1) for n, o in enumerate(outs)],
         out_shape=outs,
         compiler_params=pltpu.CompilerParams(vmem_limit_bytes=vmem_bytes),
         cost_estimate=estimate(flops, [*args, *outs]),
@@ -170,32 +198,26 @@
     )(places, *pieces, out_weight, out_weight)
 
 
-def weight_sum(places, cot_pieces, gated_pieces, half, rows, dtype):
+def weight_sum(places, cot_pieces, gated_pieces, rows, dtype):
     count = len(gated_pieces)
-    _, length, width = gated_pieces[0].shape
+    length, width = gated_pieces[0].shape
     out = jax.ShapeDtypeStruct((rows, width), dtype)
-
-    def cot_spec(n):
-        return pl.BlockSpec((1, rows, length), lambda i, w: (w[n], w[count], 0))
-
-    def gated_spec(piece):
-        place = half if piece.shape[0] > 1 else 0
-        return pl.BlockSpec((1, length, lanes), lambda i, w: (place, 0, i))
 
     grid_spec = pltpu.PrefetchScalarGridSpec(
         num_scalar_prefetch=1,
         grid=(width // lanes,),
-        in_specs=[cot_spec(n) for n in range(count)]
-        + [gated_spec(piece) for piece in gated_pieces],
+        in_specs=[pl.BlockSpec((rows, length), lambda i, w: (w[count], 0))] * count
+        + [pl.BlockSpec((length, lanes), lambda i, w: (0, i))] * count,
         out_specs=pl.BlockSpec((rows, lanes), lambda i, w: (0, i)),
+        scratch_shapes=[pltpu.VMEM((count, length, lanes), bf16)],
     )
     return pl.pallas_call(
         functools.partial(weight_kernel, count),
         grid_spec=grid_spec,
         out_shape=out,
         compiler_params=pltpu.CompilerParams(vmem_limit_bytes=vmem_bytes),
-        cost_estimate=estimate(2 * count * length * rows * width, [cot_pieces, *gated_pieces, out]),
-    )(places, *([cot_pieces] * count), *gated_pieces)
+        cost_estimate=estimate(2 * count * length * rows * width, [*cot_pieces, *gated_pieces, out]),
+    )(places, *cot_pieces, *gated_pieces)
 
 
 def swap_pairs(value, axis, distance):
@@ -226,9 +248,9 @@
     whole = analysis_table(size, np.arange(size))
     scale = 2.0 / size
     tables = [split_table(whole), np.ascontiguousarray(split_table(whole.T))]
-    spectrum = jax.ShapeDtypeStruct((size, channels), f32)
     rows16 = jax.ShapeDtypeStruct((length, channels), bf16)
     rows32 = jax.ShapeDtypeStruct((length, channels), f32)
+    half16 = jax.ShapeDtypeStruct((length, channels // 2), bf16)
     unit = 2 * size * channels
 
     tail = (
@@ -282,68 +304,77 @@
     else:
         moved = cot
 
-    own_spec, filt = by_channel(
-        functools.partial(prepare_kernel, scale),
-        tables[:1],
-        [key_rows, value_rows, filter_taps, skip_gain[None]],
-        [spectrum, spectrum],
+    state, *gated = by_channel(
+        functools.partial(state_kernel, scale),
+        tables,
+        [prior, key_rows, value_rows, filter_taps, skip_gain[None], queries],
+        [rows32, half16, half16],
         channels,
-        2 * unit * (length + taps),
-    )
-    prior, own_spec, filt, *rounds = lax.optimization_barrier((prior, own_spec, filt, *rounds))
-    mixed_spec, state, gated = by_channel(
-        state_kernel,
-        tables,
-        [prior, own_spec, filt, queries],
-        [spectrum, rows32, jax.ShapeDtypeStruct((2, length, channels // 2), bf16)],
-        channels,
-        unit * (2 * taps + 3 * length),
-    )
+        unit * (4 * taps + 5 * length),
+    )
+    gated[0], gated[1], *rounds = lax.optimization_barrier((*gated, *rounds))
 
     route = [(tp_dp(h, c, d), tp_dp(h, (c + 1) % subs, d)) for h, c, d in places]
     theirs = [lax.ppermute(r, ("tp", "dp"), route) for r in rounds]
-    gated, moved, *theirs = lax.optimization_barrier((gated, moved, *theirs))
     firsts, seconds = zip(rounds, theirs)
     same = (me_half == me_dp).astype(jnp.int32)
     subs_of = [me_sub, (me_sub + 1) % subs]
-    other_sent = project(jnp.stack([same, *subs_of]).astype(jnp.int32), firsts, seconds, out_weight, bf16)
-    other_part = swap_pairs(other_sent, "dp", 1)
-
+    other_place = jnp.stack([same, *subs_of]).astype(jnp.int32)
     rows = n_tp * channels // (n_seq * n_dp)
     own_place = jnp.stack([1 - same, *subs_of]).astype(jnp.int32)
     if square:
         order = [*range(0, n_seq, 2), *reversed(range(1, n_seq, 2))]
         ring = [(order[k], order[(k + 1) % n_seq]) for k in range(n_seq)]
-        pieces = [gated, lax.ppermute(gated, "seq", ring)]
-        pieces[1], own_place = lax.optimization_barrier((pieces[1], own_place))
+        halves = [[half] for half in gated]
+
+        def ring_step(pieces):
+            pieces.append(lax.ppermute(pieces[-1], "seq", ring))
+
+        ring_step(halves[0])
+        halves[0][1], other_place = lax.optimization_barrier((halves[0][1], other_place))
+        ring_step(halves[0])
+        halves[0][2], own_place = lax.optimization_barrier((halves[0][2], own_place))
+        ring_step(halves[0])
+        ring_step(halves[1])
+    other_sent = project(other_place, firsts, seconds, out_weight, bf16)
+    other_part = swap_pairs(other_sent, "dp", 1)
     own_part = project(own_place, firsts, seconds, out_weight, f32)
 
     if square:
-        cot_pieces = lax.all_gather(moved, "tp", axis=0)
-        table = np.zeros((n_seq, n_seq), np.int32)
+        sent_by = lambda value, flip: lax.ppermute(value, "tp", [(t, t ^ flip) for t in range(n_tp)])
+        across = sent_by(moved, subs)
+        cot_pieces = [moved, sent_by(moved, 1), across, sent_by(across, 1)]
+        table = np.zeros((n_seq, n_tp, n_tp), np.int32)
         for k, s in enumerate(order):
-            table[s] = [holder(order[k - r], s) for r in range(n_seq)]
-        sources = jnp.asarray(table)[lax.axis_index("seq")]
-        for _ in range(n_seq - 3):
-            pieces.append(lax.ppermute(pieces[-1], "seq", ring))
-
-        def weight_half(half):
-            held = [*pieces, lax.ppermute(pieces[-1][half : half + 1], "seq", ring)]
-
+            for r in range(n_seq):
+                for t in range(n_tp):
+                    table[s, t, t ^ holder(order[k - r], s)] = r
+        sources = jnp.asarray(table)[lax.axis_index("seq"), me_tp]
+        halves[0][3], own_part = lax.optimization_barrier((halves[0][3], own_part))
+        ring_step(halves[1])
+
+        def weight_half(held):
             def part(replica, dtype):
                 where = jnp.concatenate([sources, replica[None].astype(jnp.int32)])
-                return weight_sum(where, cot_pieces, held, half, rows, dtype)
-
-            sent = swap_pairs(part(1 - me_dp, bf16), "dp", 1)
-            return (part(me_dp, f32) + sent.astype(f32)) * norm_factor
+                return weight_sum(where, cot_pieces, held, rows, dtype)
+
+            return part
 
         def weight_all():
-            return jnp.concatenate([weight_half(0), weight_half(1)], axis=1)
+            sent = [first_sent, weight_half(halves[1])(1 - me_dp, bf16)]
+            sent = [swap_pairs(value, "dp", 1) for value in sent]
+            return jnp.concatenate(
+                [
+                    (weight_half(held)(me_dp, f32) + value.astype(f32)) * norm_factor
+                    for held, value in zip(halves, sent)
+                ],
+                axis=1,
+            )
 
     else:
         full = lax.all_gather(cot, "tp", axis=1, tiled=True)
         cot_all = lax.all_to_all(full, "seq", 1, 0, tiled=True)
-        gated_all = lax.all_gather(gated, "seq", axis=1, tiled=True)
+        gated_all = [lax.all_gather(half, "seq", axis=0, tiled=True) for half in gated]
 
         def part(replica, piece):
             block = lax.dynamic_slice_in_dim(cot_all, replica * rows, rows, axis=1)
@@ -358,25 +389,22 @@
         def weight_all():
             return jnp.concatenate([weight_one(gated_all[0]), weight_one(gated_all[1])], axis=1)
 
-    grad_gated = own_part + other_part.astype(f32)
-    grad_query = (grad_gated * state).astype(bf16)
-    signal = (grad_gated * queries.astype(f32)).astype(bf16)
-    later = lax.ppermute(signal[:taps], "seq", [(i + 1, i) for i in range(n_seq - 1)])
-    signal_spec, lags = by_channel(
+    grad_query, signal, lags = by_channel(
         lag_kernel,
         tables,
-        [signal, mixed_spec],
-        [spectrum, jax.ShapeDtypeStruct((taps, channels), f32)],
+        [own_part, other_part, state, queries, prior, key_rows, value_rows],
+        [rows16, rows16, jax.ShapeDtypeStruct((taps, channels), f32)],
         channels,
-        unit * (2 * length + 3 * taps),
-    )
+        unit * (2 * taps + 4 * length + 3 * taps),
+    )
+    later = lax.ppermute(signal[:taps], "seq", [(i + 1, i) for i in range(n_seq - 1)])
     grad_key, grad_value = by_channel(
-        back_kernel,
+        functools.partial(back_kernel, scale),
         tables,
-        [signal_spec, later, filt, key_rows, value_rows],
+        [signal, later, filter_taps, skip_gain[None], key_rows, value_rows],
         [rows16, rows16],
         channels,
-        unit * (2 * taps + 3 * length),
+        unit * (4 * taps + 5 * length),
     )
 
     share = taps // n_dp
@@ -384,11 +412,15 @@
         lax.dynamic_slice_in_dim(lags, (1 - me_dp) * share, share, axis=0).astype(bf16), "dp", 1
     ).astype(f32)
     if square:
-        lag_sum, *pieces = lax.optimization_barrier((lag_sum, *pieces))
+        halves[1][2], lag_sum = lax.optimization_barrier((halves[1][2], lag_sum))
+        ring_step(halves[1])
+        first_sent = weight_half(halves[0])(1 - me_dp, bf16)
     distance = 1
     while distance < n_seq:
         rounded = lag_sum.astype(bf16)
         lag_sum = rounded.astype(f32) + swap_pairs(rounded, "seq", distance).astype(f32)
+        if square and distance == 1:
+            first_sent, lag_sum = lax.optimization_barrier((first_sent, lag_sum))
         distance *= 2
     mine = lag_sum.astype(bf16)
     theirs = swap_pairs(mine, "dp", 1)

time: 150 us -> 134 us (0.89)
  the two profiles are of different devices: /device:TPU:26 before, /device:TPU:0 now
where the time goes in v6:
time: 134 us; the launch traced here: 133 us
  starting transfers between devices  45.3 us (34%)
  Pallas kernels  35.1 us (26%)
  waiting for transfers between devices  24.1 us (18%)
  local copies, waits for them, and re-layouts  20.2 us (15%)
  other arithmetic  7.15 us (5%)
    ppermute x6, starting transfers between devices, ring_step(): pieces.append(lax.ppermute(pieces[-1], 'seq', ring))  18.8 us
    unnamed x71, local copies, waits for them, and re-layouts  17.8 us
    pallas_call x3, Pallas kernels, by_channel(): pl.pallas_call(kernel, grid=(steps,), in_specs=[pl.BlockSpec(t.shape, lam...  16.4 us
    ppermute x7, waiting for transfers between devices, swap_pairs(): return lax.ppermute(value, axis, [(i, i ^ distance) for i in range(count)])  14.4 us
    pallas_call x4, Pallas kernels, weight_sum(): pl.pallas_call(functools.partial(weight_kernel, count), grid_spec=grid_sp...  11.8 us
    ppermute x6, waiting for transfers between devices, ring_step(): pieces.append(lax.ppermute(pieces[-1], 'seq', ring))  7.71 us
    ppermute x3, starting transfers between devices, per_device(): lax.ppermute(value, 'tp', [(t, t ^ flip) for t in range(n_tp)])  6.66 us
    pallas_call x2, Pallas kernels, project(): pl.pallas_call(project_kernel, grid_spec=grid_spec, out_shape=out, compil...  6.53 us
  transfers between devices with their start and end apart: 24, of which 8 were waited for; matrix products, arithmetic and copies ran while one was open for 5% of the time, Pallas kernels for 26%

profile of v6, /device:TPU:0, one launch (start us, length us, event | category | flops | bytes accessed | tf_op | source)
XLA Modules:
  0.0 132.8 jit_solution(17723327030318559116)
XLA Ops:
  1.7 1.7 %collective-permute-start.1 = (bf16[256,1024]{1,0:T(8,128)(2,1)}, bf16[256,1024]{1,0:T(8,128)(2,1)S(1)}, u32[]{:S(2)}, u32[]{:S(2)}) collective-permute-start(bf16[256,1024]{1,0:T(8,128)(2,1)} %bitcast.27), channel_id=1, source_target_pairs={{0,0},{1,4},{2,2},{3,6},{4,1},{5,5},{6,3},{7,7},{8,8},{9,12},{10,1... | collective-permute-start | bytes 1572872 | tf_op jit(solution)/shard_map/ppermute | solution.py:269
  3.4 4.7 %collective-permute-start.2 = (bf16[256,1024]{1,0:T(8,128)(2,1)}, bf16[256,1024]{1,0:T(8,128)(2,1)S(1)}, u32[]{:S(2)}, u32[]{:S(2)}) collective-permute-start(bf16[256,1024]{1,0:T(8,128)(2,1)} %bitcast.28), channel_id=1, source_target_pairs={{0,4},{1,0},{2,6},{3,2},{4,5},{5,1},{6,7},{7,3},{8,12},{9,8},{10,1... | collective-permute-start | bytes 1572872 | tf_op jit(solution)/shard_map/ppermute | solution.py:269
  8.1 3.5 %collective-permute-start = (bf16[128,1024]{1,0:T(8,128)(2,1)S(1)}, bf16[128,1024]{1,0:T(8,128)(2,1)S(1)}, u32[]{:S(2)}, u32[]{:S(2)}) collective-permute-start(bf16[128,1024]{1,0:T(8,128)(2,1)S(1)} %fusion), channel_id=1, source_target_pairs={{0,8},{8,16},{16,24},{1,9},{9,17},{17,25},{2,10},{10,18},{18,26},{... | collective-permute-start | bytes 786440 | tf_op jit(solution)/shard_map/ppermute | solution.py:260
  13.2 1.5 %collective-permute-start.10 = (bf16[1024,256]{1,0:T(8,128)(2,1)S(1)}, bf16[1024,256]{1,0:T(8,128)(2,1)}, u32[]{:S(2)}, u32[]{:S(2)}) collective-permute-start(bf16[1024,256]{1,0:T(8,128)(2,1)S(1)} %shard_map.150), channel_id=1, source_target_pairs={{2,4},{4,2},{8,14},{14,8},{18,20},{20,18},{24,30},{30,24},{3,5},{5... | collective-permute-start | bytes 1572872 | tf_op jit(solution)/shard_map/ppermute | solution.py:291
  14.6 2.0 %collective-permute-done.prior_ref = bf16[128,1024]{1,0:T(8,128)(2,1)S(1)} collective-permute-done((bf16[128,1024]{1,0:T(8,128)(2,1)S(1)}, bf16[128,1024]{1,0:T(8,128)(2,1)S(1)}, u32[]{:S(2)}, u32[]{:S(2)}) %collective-permute-start) | collective-permute-done | bytes 262176 | tf_op jit(solution)/shard_map/ppermute | solution.py:260
  23.6 5.4 %shard_map.145 = (f32[256,1024]{1,0:T(8,128)S(1)}, bf16[256,512]{1,0:T(8,128)(2,1)S(1)}, bf16[256,512]{1,0:T(8,128)(2,1)S(1)}) custom-call(bf16[2,384,384]{2,1,0:T(8,128)(2,1)S(1)} %copy-done.18, bf16[2,384,384]{2,1,0:T(8,128)(2,1)S(1)} %copy-done.21, bf16[128,1024]{1,0:T(8,128)(2,1)S(1)} %collective-permute-done.prior_ref, bf16[256,1024]{1,0:T(8,128)(2,1)S(1)} %bitcast.24, ...), custom_call_target="tpu_custom_call" | custom-call | flops 1409286144 | bytes 3674112 | tf_op jit(solution)/shard_map/pallas_call | solution.py:165
  31.3 3.5 %collective-permute-start.3 = (bf16[256,512]{1,0:T(8,128)(2,1)S(1)}, bf16[256,512]{1,0:T(8,128)(2,1)S(1)}, u32[]{:S(2)}, u32[]{:S(2)}) collective-permute-start(bf16[256,512]{1,0:T(8,128)(2,1)S(1)} %get-tuple-element.34.refs_4_), channel_id=1, source_target_pairs={{0,16},{16,24},{24,8},{8,0},{1,17},{17,25},{25,9},{9,1},{2,18},{18... | collective-permute-start | bytes 786440 | tf_op jit(solution)/shard_map/ppermute | solution.py:331
  35.6 1.7 %collective-permute-start.11 = (bf16[1024,256]{1,0:T(8,128)(2,1)}, bf16[1024,256]{1,0:T(8,128)(2,1)S(1)}, u32[]{:S(2)}, u32[]{:S(2)}) collective-permute-start(bf16[1024,256]{1,0:T(8,128)(2,1)} %broadcast_select_fusion), channel_id=1, source_target_pairs={{0,0},{2,16},{4,12},{6,28},{8,24},{10,8},{12,20},{14,4},{16,2},{18... | collective-permute-start | bytes 1572872 | tf_op jit(solution)/shard_map/ppermute | solution.py:303
  37.4 3.9 %collective-permute-done.3.refs_5_ = bf16[256,512]{1,0:T(8,128)(2,1)S(1)} collective-permute-done((bf16[256,512]{1,0:T(8,128)(2,1)S(1)}, bf16[256,512]{1,0:T(8,128)(2,1)S(1)}, u32[]{:S(2)}, u32[]{:S(2)}) %collective-permute-start.3) | collective-permute-done | bytes 262176 | tf_op jit(solution)/shard_map/ppermute | solution.py:331
  41.3 3.5 %collective-permute-start.4 = (bf16[256,512]{1,0:T(8,128)(2,1)S(1)}, bf16[256,512]{1,0:T(8,128)(2,1)}, u32[]{:S(2)}, u32[]{:S(2)}) collective-permute-start(bf16[256,512]{1,0:T(8,128)(2,1)S(1)} %collective-permute-done.3.refs_5_), channel_id=1, source_target_pairs={{0,16},{16,24},{24,8},{8,0},{1,17},{17,25},{25,9},{9,1},{2,18},{18... | collective-permute-start | bytes 786440 | tf_op jit(solution)/shard_map/ppermute | solution.py:331
  44.8 2.2 %copy-done = bf16[1024,2048]{1,0:T(8,128)(2,1)S(1)} copy-done((bf16[1024,2048]{1,0:T(8,128)(2,1)S(1)}, bf16[1024,2048]{1,0:T(8,128)(2,1)}, u32[]{:S(2)}) %copy-start) | copy-done | bytes 4194328
  46.9 3.6 %shard_map.147 = bf16[256,1024]{1,0:T(8,128)(2,1)} custom-call(s32[3]{0:T(128)S(1)} %add_add_fusion.place_ref, bf16[256,1024]{1,0:T(8,128)(2,1)S(1)} %collective-permute-done.1.first_mine, bf16[256,1024]{1,0:T(8,128)(2,1)S(1)} %collective-permute-done.2.second_mine, bf16[256,1024]{1,0:T(8,128)(2,1)S(1)} %collective-permute-done.6.first_theirs, ...), custom_call_target="tpu_custom_call" | custom-call | flops 1073741824 | bytes 6815744 | tf_op jit(solution)/shard_map/pallas_call | solution.py:192
  51.5 3.5 %collective-permute-start.5 = (bf16[256,512]{1,0:T(8,128)(2,1)}, bf16[256,512]{1,0:T(8,128)(2,1)}, u32[]{:S(2)}, u32[]{:S(2)}) collective-permute-start(bf16[256,512]{1,0:T(8,128)(2,1)} %collective-permute-done.4.refs_6_), channel_id=1, source_target_pairs={{0,16},{16,24},{24,8},{8,0},{1,17},{17,25},{25,9},{9,1},{2,18},{18... | collective-permute-start | bytes 786440 | tf_op jit(solution)/shard_map/ppermute | solution.py:331
  55.1 6.2 %collective-permute-start.13 = (bf16[1024,256]{1,0:T(8,128)(2,1)S(1)}, bf16[1024,256]{1,0:T(8,128)(2,1)S(1)}, u32[]{:S(2)}, u32[]{:S(2)}) collective-permute-start(bf16[1024,256]{1,0:T(8,128)(2,1)S(1)} %collective-permute-done.11.refs_0_), channel_id=1, source_target_pairs={{0,4},{2,6},{4,0},{6,2},{1,5},{3,7},{5,1},{7,3},{8,12},{10,14},{12... | collective-permute-start | bytes 1572872 | tf_op jit(solution)/shard_map/ppermute | solution.py:344
  61.2 6.2 %collective-permute-start.15 = (bf16[256,512]{1,0:T(8,128)(2,1)}, bf16[256,512]{1,0:T(8,128)(2,1)}, u32[]{:S(2)}, u32[]{:S(2)}) collective-permute-start(bf16[256,512]{1,0:T(8,128)(2,1)} %copy-done.12), channel_id=1, source_target_pairs={{0,16},{16,24},{24,8},{8,0},{1,17},{17,25},{25,9},{9,1},{2,18},{18... | collective-permute-start | bytes 786440 | tf_op jit(solution)/shard_map/ppermute | solution.py:331
  67.4 2.2 %copy-done.1 = bf16[1024,2048]{1,0:T(8,128)(2,1)S(1)} copy-done((bf16[1024,2048]{1,0:T(8,128)(2,1)S(1)}, bf16[1024,2048]{1,0:T(8,128)(2,1)}, u32[]{:S(2)}) %copy-start.1) | copy-done | bytes 4194328
  69.6 3.0 %shard_map.146.own_ref = f32[256,1024]{1,0:T(8,128)S(1)} custom-call(s32[3]{0:T(128)S(1)} %add_add_fusion.1.place_ref, bf16[256,1024]{1,0:T(8,128)(2,1)S(1)} %collective-permute-done.1.first_mine, bf16[256,1024]{1,0:T(8,128)(2,1)S(1)} %collective-permute-done.2.second_mine, bf16[256,1024]{1,0:T(8,128)(2,1)S(1)} %collective-permute-done.6.first_theirs, ...), custom_call_target="tpu_custom_call" | custom-call | flops 1073741824 | bytes 7340032 | tf_op jit(solution)/shard_map/pallas_call | solution.py:192
  72.7 5.0 %shard_map.148 = (bf16[256,1024]{1,0:T(8,128)(2,1)}, bf16[256,1024]{1,0:T(8,128)(2,1)S(1)}, f32[128,1024]{1,0:T(8,128)S(1)}) custom-call(bf16[2,384,384]{2,1,0:T(8,128)(2,1)S(1)} %copy-done.19, bf16[2,384,384]{2,1,0:T(8,128)(2,1)S(1)} %copy-done.22, f32[256,1024]{1,0:T(8,128)S(1)} %shard_map.146.own_ref, bf16[256,1024]{1,0:T(8,128)(2,1)} %collective-permute-done.8.other_ref, ...), custom_call_target="tpu_custom_call" | custom-call | flops 1308622848 | bytes 6029312 | tf_op jit(solution)/shard_map/pallas_call | solution.py:165
  80.0 4.2 %collective-permute-done.17 = bf16[64,1024]{1,0:T(8,128)(2,1)S(1)} collective-permute-done((bf16[64,1024]{1,0:T(8,128)(2,1)S(1)}, bf16[64,1024]{1,0:T(8,128)(2,1)S(1)}, u32[]{:S(2)}, u32[]{:S(2)}) %collective-permute-start.17) | collective-permute-done | bytes 131104 | tf_op jit(solution)/shard_map/ppermute | solution.py:225
  84.2 3.2 %collective-permute-done.16.refs_6_ = bf16[256,512]{1,0:T(8,128)(2,1)} collective-permute-done((bf16[256,512]{1,0:T(8,128)(2,1)}, bf16[256,512]{1,0:T(8,128)(2,1)}, u32[]{:S(2)}, u32[]{:S(2)}) %collective-permute-start.16) | collective-permute-done | bytes 262176 | tf_op jit(solution)/shard_map/ppermute | solution.py:331
  89.3 4.5 %collective-permute-done.18 = bf16[64,1024]{1,0:T(8,128)(2,1)S(1)} collective-permute-done((bf16[64,1024]{1,0:T(8,128)(2,1)S(1)}, bf16[64,1024]{1,0:T(8,128)(2,1)S(1)}, u32[]{:S(2)}, u32[]{:S(2)}) %collective-permute-start.18) | collective-permute-done | bytes 131104 | tf_op jit(solution)/shard_map/ppermute | solution.py:225
  94.8 3.2 %shard_map.151 = bf16[512,512]{1,0:T(8,128)(2,1)} custom-call(s32[5]{0:T(128)S(1)} %get-tuple-element.63.place_ref, bf16[1024,256]{1,0:T(8,128)(2,1)S(1)} %collective-permute-done.11.refs_0_, bf16[1024,256]{1,0:T(8,128)(2,1)S(1)} %collective-permute-done.12.refs_1_, bf16[1024,256]{1,0:T(8,128)(2,1)S(1)} %collective-permute-done.13.refs_2_, ...), custom_call_target="tpu_custom_call" | custom-call | flops 536870912 | bytes 3670016 | tf_op jit(solution)/shard_map/pallas_call | solution.py:214
  99.4 1.4 %collective-permute-start.9 = (bf16[128,1024]{1,0:T(8,128)(2,1)S(1)}, bf16[128,1024]{1,0:T(8,128)(2,1)S(1)}, u32[]{:S(2)}, u32[]{:S(2)}) collective-permute-start(bf16[128,1024]{1,0:T(8,128)(2,1)S(1)} %slice.16), channel_id=1, source_target_pairs={{8,0},{16,8},{24,16},{9,1},{17,9},{25,17},{10,2},{18,10},{26,18},{... | collective-permute-start | bytes 786440 | tf_op jit(solution)/shard_map/ppermute | solution.py:400
  101.8 3.3 %shard_map.154 = bf16[512,512]{1,0:T(8,128)(2,1)} custom-call(s32[5]{0:T(128)S(1)} %get-tuple-element.63.place_ref, bf16[1024,256]{1,0:T(8,128)(2,1)S(1)} %collective-permute-done.11.refs_0_, bf16[1024,256]{1,0:T(8,128)(2,1)S(1)} %collective-permute-done.12.refs_1_, bf16[1024,256]{1,0:T(8,128)(2,1)S(1)} %collective-permute-done.13.refs_2_, ...), custom_call_target="tpu_custom_call" | custom-call | flops 536870912 | bytes 3670016 | tf_op jit(solution)/shard_map/pallas_call | solution.py:214
  105.1 2.0 %collective-permute-start.23 = (bf16[512,512]{1,0:T(8,128)(2,1)}, bf16[512,512]{1,0:T(8,128)(2,1)}, u32[]{:S(2)}, u32[]{:S(2)}) collective-permute-start(bf16[512,512]{1,0:T(8,128)(2,1)} %shard_map.154), channel_id=1, source_target_pairs={{0,1},{1,0},{2,3},{3,2},{4,5},{5,4},{6,7},{7,6},{8,9},{9,8},{10,11... | collective-permute-start | bytes 1572872 | tf_op jit(solution)/shard_map/ppermute | solution.py:225
  109.2 5.9 %shard_map.149 = (bf16[256,1024]{1,0:T(8,128)(2,1)}, bf16[256,1024]{1,0:T(8,128)(2,1)}) custom-call(bf16[2,384,384]{2,1,0:T(8,128)(2,1)S(1)} %copy-done.20, bf16[2,384,384]{2,1,0:T(8,128)(2,1)S(1)} %copy-done.23, bf16[256,1024]{1,0:T(8,128)(2,1)S(1)} %copy-done.30, bf16[128,1024]{1,0:T(8,128)(2,1)S(1)} %collective-permute-done.9.later_ref, ...), custom_call_target="tpu_custom_call" | custom-call | flops 1409286144 | bytes 3149824 | tf_op jit(solution)/shard_map/pallas_call | solution.py:165
  116.3 2.6 %shard_map.153 = f32[512,512]{1,0:T(8,128)S(1)} custom-call(s32[5]{0:T(128)S(1)} %get-tuple-element.62.place_ref, bf16[1024,256]{1,0:T(8,128)(2,1)S(1)} %collective-permute-done.11.refs_0_, bf16[1024,256]{1,0:T(8,128)(2,1)S(1)} %collective-permute-done.12.refs_1_, bf16[1024,256]{1,0:T(8,128)(2,1)S(1)} %collective-permute-done.13.refs_2_, ...), custom_call_target="tpu_custom_call" | custom-call | flops 536870912 | bytes 4194304 | tf_op jit(solution)/shard_map/pallas_call | solution.py:214
  119.0 2.6 %shard_map.152 = f32[512,512]{1,0:T(8,128)S(1)} custom-call(s32[5]{0:T(128)S(1)} %get-tuple-element.62.place_ref, bf16[1024,256]{1,0:T(8,128)(2,1)S(1)} %collective-permute-done.11.refs_0_, bf16[1024,256]{1,0:T(8,128)(2,1)S(1)} %collective-permute-done.12.refs_1_, bf16[1024,256]{1,0:T(8,128)(2,1)S(1)} %collective-permute-done.13.refs_2_, ...), custom_call_target="tpu_custom_call" | custom-call | flops 536870912 | bytes 4194304 | tf_op jit(solution)/shard_map/pallas_call | solution.py:214
  121.6 1.4 %collective-permute-done.20 = bf16[64,1024]{1,0:T(8,128)(2,1)S(1)} collective-permute-done((bf16[64,1024]{1,0:T(8,128)(2,1)S(1)}, bf16[64,1024]{1,0:T(8,128)(2,1)S(1)}, u32[]{:S(2)}, u32[]{:S(2)}) %collective-permute-start.20) | collective-permute-done | bytes 131104 | tf_op jit(solution)/shard_map/ppermute | solution.py:225
  125.9 4.2 %collective-permute-done.21 = bf16[512,512]{1,0:T(8,128)(2,1)} collective-permute-done((bf16[512,512]{1,0:T(8,128)(2,1)}, bf16[512,512]{1,0:T(8,128)(2,1)}, u32[]{:S(2)}, u32[]{:S(2)}) %collective-permute-start.21) | collective-permute-done | bytes 524320 | tf_op jit(solution)/shard_map/ppermute | solution.py:225
  130.1 1.2 add_multiply_fusion.1
  131.3 1.5 %pad_maximum_fusion = f32[512,1024]{1,0:T(8,128)} fusion(f32[512,512]{1,0:T(8,128)S(1)} %add_multiply_fusion, f32[512,512]{1,0:T(8,128)S(1)} %add_multiply_fusion.1), kind=kLoop, calls=%fused_computation | loop fusion | flops 524288 | bytes 4194304 | tf_op jit(solution)/shard_map/concatenate | solution.py:366
  (114 shorter events, 27.3 us)
Async XLA Ops:
  1.7 29.0 %collective-permute-start.1 = (bf16[256,1024]{1,0:T(8,128)(2,1)}, bf16[256,1024]{1,0:T(8,128)(2,1)S(1)}, u32[]{:S(2)}, u32[]{:S(2)}) collective-permute-start(bf16[256,1024]{1,0:T(8,128)(2,1)} %bitcast.27), channel_id=1, source_target_pairs={{0,0},{1,4},{2,2},{3,6},{4,1},{5,5},{6,3},{7,7},{8,8},{9,12},{10,1... | collective-permute-start | bytes 1572872 | tf_op jit(solution)/shard_map/ppermute | solution.py:269
  3.4 27.3 %collective-permute-start.2 = (bf16[256,1024]{1,0:T(8,128)(2,1)}, bf16[256,1024]{1,0:T(8,128)(2,1)S(1)}, u32[]{:S(2)}, u32[]{:S(2)}) collective-permute-start(bf16[256,1024]{1,0:T(8,128)(2,1)} %bitcast.28), channel_id=1, source_target_pairs={{0,4},{1,0},{2,6},{3,2},{4,5},{5,1},{6,7},{7,3},{8,12},{9,8},{10,1... | collective-permute-start | bytes 1572872 | tf_op jit(solution)/shard_map/ppermute | solution.py:269
  8.1 8.5 %collective-permute-start = (bf16[128,1024]{1,0:T(8,128)(2,1)S(1)}, bf16[128,1024]{1,0:T(8,128)(2,1)S(1)}, u32[]{:S(2)}, u32[]{:S(2)}) collective-permute-start(bf16[128,1024]{1,0:T(8,128)(2,1)S(1)} %fusion), channel_id=1, source_target_pairs={{0,8},{8,16},{16,24},{1,9},{9,17},{17,25},{2,10},{10,18},{18,26},{... | collective-permute-start | bytes 786440 | tf_op jit(solution)/shard_map/ppermute | solution.py:260
  13.2 21.6 %collective-permute-start.10 = (bf16[1024,256]{1,0:T(8,128)(2,1)S(1)}, bf16[1024,256]{1,0:T(8,128)(2,1)}, u32[]{:S(2)}, u32[]{:S(2)}) collective-permute-start(bf16[1024,256]{1,0:T(8,128)(2,1)S(1)} %shard_map.150), channel_id=1, source_target_pairs={{2,4},{4,2},{8,14},{14,8},{18,20},{20,18},{24,30},{30,24},{3,5},{5... | collective-permute-start | bytes 1572872 | tf_op jit(solution)/shard_map/ppermute | solution.py:291
  16.6 12.4 %copy-start.27 = (bf16[128,1024]{1,0:T(8,128)(2,1)}, bf16[128,1024]{1,0:T(8,128)(2,1)S(1)}, u32[]{:S(2)}) copy-start(bf16[128,1024]{1,0:T(8,128)(2,1)S(1)} %collective-permute-done.prior_ref) | copy-start | bytes 786436
  30.7 14.0 %collective-permute-start.6 = (bf16[256,1024]{1,0:T(8,128)(2,1)S(1)}, bf16[256,1024]{1,0:T(8,128)(2,1)S(1)}, u32[]{:S(2)}, u32[]{:S(2)}) collective-permute-start(bf16[256,1024]{1,0:T(8,128)(2,1)S(1)} %collective-permute-done.1.first_mine), channel_id=1, source_target_pairs={{0,2},{1,3},{2,0},{3,1},{4,6},{5,7},{6,4},{7,5},{8,10},{9,11},{10,... | collective-permute-start | bytes 1572872 | tf_op jit(solution)/shard_map/ppermute | solution.py:318
  30.8 14.0 %collective-permute-start.7 = (bf16[256,1024]{1,0:T(8,128)(2,1)S(1)}, bf16[256,1024]{1,0:T(8,128)(2,1)S(1)}, u32[]{:S(2)}, u32[]{:S(2)}) collective-permute-start(bf16[256,1024]{1,0:T(8,128)(2,1)S(1)} %collective-permute-done.2.second_mine), channel_id=1, source_target_pairs={{0,2},{1,3},{2,0},{3,1},{4,6},{5,7},{6,4},{7,5},{8,10},{9,11},{10,... | collective-permute-start | bytes 1572872 | tf_op jit(solution)/shard_map/ppermute | solution.py:318
  31.3 10.0 %collective-permute-start.3 = (bf16[256,512]{1,0:T(8,128)(2,1)S(1)}, bf16[256,512]{1,0:T(8,128)(2,1)S(1)}, u32[]{:S(2)}, u32[]{:S(2)}) collective-permute-start(bf16[256,512]{1,0:T(8,128)(2,1)S(1)} %get-tuple-element.34.refs_4_), channel_id=1, source_target_pairs={{0,16},{16,24},{24,8},{8,0},{1,17},{17,25},{25,9},{9,1},{2,18},{18... | collective-permute-start | bytes 786440 | tf_op jit(solution)/shard_map/ppermute | solution.py:331
  35.6 19.4 %collective-permute-start.11 = (bf16[1024,256]{1,0:T(8,128)(2,1)}, bf16[1024,256]{1,0:T(8,128)(2,1)S(1)}, u32[]{:S(2)}, u32[]{:S(2)}) collective-permute-start(bf16[1024,256]{1,0:T(8,128)(2,1)} %broadcast_select_fusion), channel_id=1, source_target_pairs={{0,0},{2,16},{4,12},{6,28},{8,24},{10,8},{12,20},{14,4},{16,2},{18... | collective-permute-start | bytes 1572872 | tf_op jit(solution)/shard_map/ppermute | solution.py:303
  41.3 9.3 %copy-start.15 = (bf16[256,512]{1,0:T(8,128)(2,1)}, bf16[256,512]{1,0:T(8,128)(2,1)S(1)}, u32[]{:S(2)}) copy-start(bf16[256,512]{1,0:T(8,128)(2,1)S(1)} %collective-permute-done.3.refs_5_) | copy-start | bytes 786436
  41.3 10.2 %collective-permute-start.4 = (bf16[256,512]{1,0:T(8,128)(2,1)S(1)}, bf16[256,512]{1,0:T(8,128)(2,1)}, u32[]{:S(2)}, u32[]{:S(2)}) collective-permute-start(bf16[256,512]{1,0:T(8,128)(2,1)S(1)} %collective-permute-done.3.refs_5_), channel_id=1, source_target_pairs={{0,16},{16,24},{24,8},{8,0},{1,17},{17,25},{25,9},{9,1},{2,18},{18... | collective-permute-start | bytes 786440 | tf_op jit(solution)/shard_map/ppermute | solution.py:331
  50.5 22.1 %collective-permute-start.8 = (bf16[256,1024]{1,0:T(8,128)(2,1)}, bf16[256,1024]{1,0:T(8,128)(2,1)}, u32[]{:S(2)}, u32[]{:S(2)}) collective-permute-start(bf16[256,1024]{1,0:T(8,128)(2,1)} %shard_map.147), channel_id=1, source_target_pairs={{0,1},{1,0},{2,3},{3,2},{4,5},{5,4},{6,7},{7,6},{8,9},{9,8},{10,11... | collective-permute-start | bytes 1572872 | tf_op jit(solution)/shard_map/ppermute | solution.py:225
  51.5 21.1 %collective-permute-start.5 = (bf16[256,512]{1,0:T(8,128)(2,1)}, bf16[256,512]{1,0:T(8,128)(2,1)}, u32[]{:S(2)}, u32[]{:S(2)}) collective-permute-start(bf16[256,512]{1,0:T(8,128)(2,1)} %collective-permute-done.4.refs_6_), channel_id=1, source_target_pairs={{0,16},{16,24},{24,8},{8,0},{1,17},{17,25},{25,9},{9,1},{2,18},{18... | collective-permute-start | bytes 786440 | tf_op jit(solution)/shard_map/ppermute | solution.py:331
  55.1 24.4 %collective-permute-start.13 = (bf16[1024,256]{1,0:T(8,128)(2,1)S(1)}, bf16[1024,256]{1,0:T(8,128)(2,1)S(1)}, u32[]{:S(2)}, u32[]{:S(2)}) collective-permute-start(bf16[1024,256]{1,0:T(8,128)(2,1)S(1)} %collective-permute-done.11.refs_0_), channel_id=1, source_target_pairs={{0,4},{2,6},{4,0},{6,2},{1,5},{3,7},{5,1},{7,3},{8,12},{10,14},{12... | collective-permute-start | bytes 1572872 | tf_op jit(solution)/shard_map/ppermute | solution.py:344
  61.2 17.4 %collective-permute-start.15 = (bf16[256,512]{1,0:T(8,128)(2,1)}, bf16[256,512]{1,0:T(8,128)(2,1)}, u32[]{:S(2)}, u32[]{:S(2)}) collective-permute-start(bf16[256,512]{1,0:T(8,128)(2,1)} %copy-done.12), channel_id=1, source_target_pairs={{0,16},{16,24},{24,8},{8,0},{1,17},{17,25},{25,9},{9,1},{2,18},{18... | collective-permute-start | bytes 786440 | tf_op jit(solution)/shard_map/ppermute | solution.py:331
  78.5 5.7 %collective-permute-start.17 = (bf16[64,1024]{1,0:T(8,128)(2,1)S(1)}, bf16[64,1024]{1,0:T(8,128)(2,1)S(1)}, u32[]{:S(2)}, u32[]{:S(2)}) collective-permute-start(bf16[64,1024]{1,0:T(8,128)(2,1)S(1)} %dynamic-slice_convert_fusion), channel_id=1, source_target_pairs={{0,1},{1,0},{2,3},{3,2},{4,5},{5,4},{6,7},{7,6},{8,9},{9,8},{10,11... | collective-permute-start | bytes 393224 | tf_op jit(solution)/shard_map/ppermute | solution.py:225
  78.6 8.8 %collective-permute-start.16 = (bf16[256,512]{1,0:T(8,128)(2,1)}, bf16[256,512]{1,0:T(8,128)(2,1)}, u32[]{:S(2)}, u32[]{:S(2)}) collective-permute-start(bf16[256,512]{1,0:T(8,128)(2,1)} %collective-permute-done.15.refs_5_), channel_id=1, source_target_pairs={{0,16},{16,24},{24,8},{8,0},{1,17},{17,25},{25,9},{9,1},{2,18},{18... | collective-permute-start | bytes 786440 | tf_op jit(solution)/shard_map/ppermute | solution.py:331
  79.5 14.4 %collective-permute-start.12 = (bf16[1024,256]{1,0:T(8,128)(2,1)S(1)}, bf16[1024,256]{1,0:T(8,128)(2,1)S(1)}, u32[]{:S(2)}, u32[]{:S(2)}) collective-permute-start(bf16[1024,256]{1,0:T(8,128)(2,1)S(1)} %collective-permute-done.11.refs_0_), channel_id=1, source_target_pairs={{0,2},{2,0},{4,6},{6,4},{1,3},{3,1},{5,7},{7,5},{8,10},{10,8},{12,... | collective-permute-start | bytes 1572872 | tf_op jit(solution)/shard_map/ppermute | solution.py:344
  79.5 14.4 %collective-permute-start.14 = (bf16[1024,256]{1,0:T(8,128)(2,1)S(1)}, bf16[1024,256]{1,0:T(8,128)(2,1)S(1)}, u32[]{:S(2)}, u32[]{:S(2)}) collective-permute-start(bf16[1024,256]{1,0:T(8,128)(2,1)S(1)} %collective-permute-done.13.refs_2_), channel_id=1, source_target_pairs={{0,2},{2,0},{4,6},{6,4},{1,3},{3,1},{5,7},{7,5},{8,10},{10,8},{12,... | collective-permute-start | bytes 1572872 | tf_op jit(solution)/shard_map/ppermute | solution.py:344
  87.4 6.4 %collective-permute-start.18 = (bf16[64,1024]{1,0:T(8,128)(2,1)S(1)}, bf16[64,1024]{1,0:T(8,128)(2,1)S(1)}, u32[]{:S(2)}, u32[]{:S(2)}) collective-permute-start(bf16[64,1024]{1,0:T(8,128)(2,1)S(1)} %convert_add_fusion.1), channel_id=1, source_target_pairs={{0,8},{8,0},{16,24},{24,16},{1,9},{9,1},{17,25},{25,17},{2,10},{10... | collective-permute-start | bytes 393224 | tf_op jit(solution)/shard_map/ppermute | solution.py:225
  88.2 12.6 %collective-permute-start.22 = (bf16[256,512]{1,0:T(8,128)(2,1)}, bf16[256,512]{1,0:T(8,128)(2,1)}, u32[]{:S(2)}, u32[]{:S(2)}) collective-permute-start(bf16[256,512]{1,0:T(8,128)(2,1)} %collective-permute-done.16.refs_6_), channel_id=1, source_target_pairs={{0,16},{16,24},{24,8},{8,0},{1,17},{17,25},{25,9},{9,1},{2,18},{18... | collective-permute-start | bytes 786440 | tf_op jit(solution)/shard_map/ppermute | solution.py:331
  98.1 9.1 %collective-permute-start.19 = (bf16[64,1024]{1,0:T(8,128)(2,1)S(1)}, bf16[64,1024]{1,0:T(8,128)(2,1)}, u32[]{:S(2)}, u32[]{:S(2)}) collective-permute-start(bf16[64,1024]{1,0:T(8,128)(2,1)S(1)} %convert_add_fusion), channel_id=1, source_target_pairs={{0,16},{8,24},{16,0},{24,8},{1,17},{9,25},{17,1},{25,9},{2,18},{10... | collective-permute-start | bytes 393224 | tf_op jit(solution)/shard_map/ppermute | solution.py:225
  98.3 10.9 %copy-start.30 = (bf16[256,1024]{1,0:T(8,128)(2,1)S(1)}, bf16[256,1024]{1,0:T(8,128)(2,1)}, u32[]{:S(2)}) copy-start(bf16[256,1024]{1,0:T(8,128)(2,1)} %copy-done.29) | copy-start | bytes 1572868
  99.4 9.8 %copy-start.6 = (bf16[1,256,1024]{2,1,0:T(8,128)(2,1)S(1)}, bf16[1,256,1024]{2,1,0:T(8,128)(2,1)}, u32[]{:S(2)}) copy-start(bf16[1,256,1024]{2,1,0:T(8,128)(2,1)} %param.12) | copy-start | bytes 1572868
  99.4 9.8 %copy-start.9 = (bf16[1,256,1024]{2,1,0:T(8,128)(2,1)S(1)}, bf16[1,256,1024]{2,1,0:T(8,128)(2,1)}, u32[]{:S(2)}) copy-start(bf16[1,256,1024]{2,1,0:T(8,128)(2,1)} %param.11) | copy-start | bytes 1572868
  99.4 9.8 %collective-permute-start.9 = (bf16[128,1024]{1,0:T(8,128)(2,1)S(1)}, bf16[128,1024]{1,0:T(8,128)(2,1)S(1)}, u32[]{:S(2)}, u32[]{:S(2)}) collective-permute-start(bf16[128,1024]{1,0:T(8,128)(2,1)S(1)} %slice.16), channel_id=1, source_target_pairs={{8,0},{16,8},{24,16},{9,1},{17,9},{25,17},{10,2},{18,10},{26,18},{... | collective-permute-start | bytes 786440 | tf_op jit(solution)/shard_map/ppermute | solution.py:400
  101.8 7.4 %copy-start.32 = (bf16[1024,128]{1,0:T(8,128)(2,1)S(1)}, bf16[1024,128]{1,0:T(8,128)(2,1)}, u32[]{:S(2)}) copy-start(bf16[1024,128]{1,0:T(8,128)(2,1)} %taps_ref.3) | copy-start | bytes 786436
  101.8 7.4 %copy-start.34 = (f32[1024]{0:T(1024)S(1)}, f32[1024]{0:T(1024)}, u32[]{:S(2)}) copy-start(f32[1024]{0:T(1024)} %param.14) | copy-start | bytes 12292
  105.1 19.6 %collective-permute-start.23 = (bf16[512,512]{1,0:T(8,128)(2,1)}, bf16[512,512]{1,0:T(8,128)(2,1)}, u32[]{:S(2)}, u32[]{:S(2)}) collective-permute-start(bf16[512,512]{1,0:T(8,128)(2,1)} %shard_map.154), channel_id=1, source_target_pairs={{0,1},{1,0},{2,3},{3,2},{4,5},{5,4},{6,7},{7,6},{8,9},{9,8},{10,11... | collective-permute-start | bytes 1572872 | tf_op jit(solution)/shard_map/ppermute | solution.py:225
  108.1 8.2 %copy-start.14 = (bf16[256,512]{1,0:T(8,128)(2,1)S(1)}, bf16[256,512]{1,0:T(8,128)(2,1)}, u32[]{:S(2)}) copy-start(bf16[256,512]{1,0:T(8,128)(2,1)} %copy-done.12) | copy-start | bytes 786436
  108.1 14.9 %collective-permute-start.20 = (bf16[64,1024]{1,0:T(8,128)(2,1)S(1)}, bf16[64,1024]{1,0:T(8,128)(2,1)S(1)}, u32[]{:S(2)}, u32[]{:S(2)}) collective-permute-start(bf16[64,1024]{1,0:T(8,128)(2,1)S(1)} %add_convert_fusion), channel_id=1, source_target_pairs={{0,1},{1,0},{2,3},{3,2},{4,5},{5,4},{6,7},{7,6},{8,9},{9,8},{10,11... | collective-permute-start | bytes 393224 | tf_op jit(solution)/shard_map/ppermute | solution.py:225
  115.1 15.0 %collective-permute-start.21 = (bf16[512,512]{1,0:T(8,128)(2,1)}, bf16[512,512]{1,0:T(8,128)(2,1)}, u32[]{:S(2)}, u32[]{:S(2)}) collective-permute-start(bf16[512,512]{1,0:T(8,128)(2,1)} %shard_map.151), channel_id=1, source_target_pairs={{0,1},{1,0},{2,3},{3,2},{4,5},{5,4},{6,7},{7,6},{8,9},{9,8},{10,11... | collective-permute-start | bytes 1572872 | tf_op jit(solution)/shard_map/ppermute | solution.py:225
  (27 other events, 59.9 us)

commit v7 on v6

--- a/solution.py
+++ b/solution.py
@@ -12,7 +12,7 @@
 
 f32, bf16 = jnp.float32, jnp.bfloat16
 lanes = 256
-vmem_bytes = 32 * 1024 * 1024
+vmem_bytes = 58 * 1024 * 1024
 
 
 def analysis_table(size, positions):
@@ -78,35 +78,62 @@
 
 
 def state_kernel(
-    scale, table, synth, prior_ref, key_ref, value_ref, taps_ref, skip_ref, query_ref, state_ref, first_ref, second_ref
+    scale, table, synth, prior_ref, key_ref, value_ref, taps_ref, skip_ref, query_ref, state_ref, gated_ref
 ):
     spec = mixed_spectrum(table, prior_ref, key_ref, value_ref)
     product = spectrum_product(spec, filter_spectrum(scale, table, taps_ref, skip_ref), False)
     state = inverse_transform(synth, product, prior_ref.shape[0], query_ref.shape[0])
     state_ref[...] = state
-    gated = (query_ref[...].astype(f32) * state).astype(bf16)
-    in_first = pl.program_id(0) < pl.num_programs(0) // 2
-
-    @pl.when(in_first)
-    def _():
-        first_ref[...] = gated
-
-    @pl.when(jnp.logical_not(in_first))
-    def _():
-        second_ref[...] = gated
+    gated_ref[...] = (query_ref[...].astype(f32) * state).astype(bf16)
 
 
 def transpose_kernel(rows_ref, out_ref):
     out_ref[...] = rows_ref[...].T
 
 
-def project_kernel(place_ref, first_mine, second_mine, first_theirs, second_theirs, weight_mine, weight_theirs, out_ref):
-    def write(mine, theirs):
-        total = dot_nt(mine[...], weight_mine[...]) + dot_nt(theirs[...], weight_theirs[...])
-        out_ref[...] = total.astype(out_ref.dtype)
-
-    pl.when(place_ref[0] == 0)(lambda: write(first_mine, first_theirs))
-    pl.when(place_ref[0] != 0)(lambda: write(second_mine, second_theirs))
+def project_kernel(
+    place_ref, first_mine, second_mine, first_theirs, second_theirs, weight, out, pieces, blocks, totals, piece_sem, block_sem, out_sem
+):
+    steps, _, _, width = blocks.shape
+
+    def piece_copy(n, source):
+        return pltpu.make_async_copy(source, pieces.at[n], piece_sem.at[n])
+
+    def block_copy(n, i):
+        rows = pl.ds(pl.multiple_of(i * lanes, lanes), lanes)
+        columns = pl.ds(pl.multiple_of(place_ref[1 + n] * width, width), width)
+        return pltpu.make_async_copy(weight.at[rows, columns], blocks.at[i, n], block_sem.at[i, n])
+
+    def out_copy(i):
+        place = out.at[:, pl.ds(pl.multiple_of(i * lanes, lanes), lanes)]
+        return pltpu.make_async_copy(totals.at[i], place, out_sem.at[i])
+
+    @pl.when(place_ref[0] == 0)
+    def _():
+        piece_copy(0, first_mine).start()
+        piece_copy(1, first_theirs).start()
+
+    @pl.when(place_ref[0] != 0)
+    def _():
+        piece_copy(0, second_mine).start()
+        piece_copy(1, second_theirs).start()
+
+    for i in range(steps):
+        for n in range(2):
+            block_copy(n, i).start()
+    for n in range(2):
+        piece_copy(n, first_mine).wait()
+
+    @pl.loop(0, steps)
+    def _(i):
+        for n in range(2):
+            block_copy(n, i).wait()
+        total = dot_nt(pieces[0], blocks[i, 0]) + dot_nt(pieces[1], blocks[i, 1])
+        totals[i] = total.astype(totals.dtype)
+        out_copy(i).start()
+
+    for i in range(steps):
+        out_copy(i).wait()
 
 
 def weight_kernel(count, place_ref, *refs):
@@ -149,53 +176,104 @@
     return pl.CostEstimate(flops=flops, bytes_accessed=moved, transcendentals=0)
 
 
-def by_channel(kernel, tables, args, outs, channels, flops):
+def by_channel(body, tables, args, outs, channels, flops):
     steps = channels // lanes
-
-    def column_spec(shape, place=0):
-        if shape[1] == channels // 2:
-            shift = place % 2 * (steps // 2)
-            return pl.BlockSpec(
-                (shape[0], lanes), lambda i: (0, jnp.clip(i - shift, 0, steps // 2 - 1))
-            )
-        if shape[1] != channels:
-            return pl.BlockSpec((lanes, shape[1]), lambda i: (i, 0))
-        return pl.BlockSpec((shape[0], lanes), lambda i: (0, i))
+    flat_outs = [o for group in outs for o in group]
+    n_tables, n_args, n_outs = len(tables), len(args), len(outs)
+
+    def part(ref, i, count):
+        start = pl.multiple_of(i * lanes, lanes)
+        if ref.shape[1] == count * lanes:
+            return ref.at[:, pl.ds(start, lanes)]
+        return ref.at[pl.ds(start, lanes), :]
+
+    def kernel(*refs):
+        refs = list(refs)
+        take = lambda count: [refs.pop(0) for _ in range(count)]
+        table_in, arg_in, outs_to = take(n_tables), take(n_args), take(len(flat_outs))
+        table_held, arg_held, out_held = take(n_tables), take(n_args), take(n_outs)
+        table_sem, arg_sem, out_sem = refs
+        groups = [[outs_to.pop(0) for _ in group] for group in outs]
+
+        def table_copy(k):
+            return pltpu.make_async_copy(table_in[k], table_held[k], table_sem.at[k])
+
+        def arg_copy(k, i):
+            return pltpu.make_async_copy(part(arg_in[k], i, steps), arg_held[k].at[i], arg_sem.at[k, i])
+
+        def out_copy(k, n, i):
+            per = steps // len(groups[k])
+            place = part(groups[k][n], i - n * per, per)
+            return pltpu.make_async_copy(out_held[k].at[i], place, out_sem.at[k, i])
+
+        for k in range(n_tables):
+            table_copy(k).start()
+        for i in range(steps):
+            for k in range(n_args):
+                arg_copy(k, i).start()
+        for k in range(n_tables):
+            table_copy(k).wait()
+
+        for n in range(max(len(group) for group in groups)):
+            per = steps // max(len(group) for group in groups)
+
+            @pl.loop(n * per, (n + 1) * per)
+            def _(i):
+                for k in range(n_args):
+                    arg_copy(k, i).wait()
+                body(*table_held, *[held.at[i] for held in arg_held], *[held.at[i] for held in out_held])
+                for k in range(n_outs):
+                    out_copy(k, min(n, len(groups[k]) - 1), i).start()
+
+        for i in range(steps):
+            for k in range(n_outs):
+                out_copy(k, i * len(groups[k]) // steps, i).wait()
+
+    def held(value):
+        if value.shape[1] in (channels, channels // 2):
+            return pltpu.VMEM((steps, value.shape[0], lanes), value.dtype)
+        return pltpu.VMEM((steps, lanes, value.shape[1]), value.dtype)
 
     return pl.pallas_call(
         kernel,
-        grid=(steps,),
-        in_specs=[pl.BlockSpec(t.shape, lambda i: (0, 0, 0)) for t in tables]
-        + [column_spec(a.shape) for a in args],
-        out_specs=[column_spec(o.shape, n + 1) for n, o in enumerate(outs)],
-        out_shape=outs,
+        in_specs=[pl.BlockSpec(memory_space=pl.ANY)] * (n_tables + n_args),
+        out_specs=[pl.BlockSpec(memory_space=pl.ANY)] * len(flat_outs),
+        out_shape=flat_outs,
+        scratch_shapes=[
+            *[pltpu.VMEM(t.shape, bf16) for t in tables],
+            *[held(a) for a in args],
+            *[held(group[0]) for group in outs],
+            pltpu.SemaphoreType.DMA((n_tables,)),
+            pltpu.SemaphoreType.DMA((n_args, steps)),
+            pltpu.SemaphoreType.DMA((n_outs, steps)),
+        ],
         compiler_params=pltpu.CompilerParams(vmem_limit_bytes=vmem_bytes),
-        cost_estimate=estimate(flops, [*args, *outs]),
+        cost_estimate=estimate(flops, [*args, *flat_outs]),
     )(*[jnp.asarray(t) for t in tables], *args)
 
 
 def project(places, firsts, seconds, out_weight, dtype):
     length, width = firsts[0].shape
     channels = out_weight.shape[0]
+    steps = channels // lanes
     out = jax.ShapeDtypeStruct((length, channels), dtype)
     pieces = [firsts[0], seconds[0], firsts[1], seconds[1]]
-    grid_spec = pltpu.PrefetchScalarGridSpec(
-        num_scalar_prefetch=1,
-        grid=(channels // lanes,),
-        in_specs=[pl.BlockSpec((length, width), lambda i, w: (0, 0))] * 4
-        + [
-            pl.BlockSpec((lanes, width), lambda i, w: (i, w[1])),
-            pl.BlockSpec((lanes, width), lambda i, w: (i, w[2])),
-        ],
-        out_specs=pl.BlockSpec((length, lanes), lambda i, w: (0, i)),
-    )
     return pl.pallas_call(
         project_kernel,
-        grid_spec=grid_spec,
+        in_specs=[pl.BlockSpec(memory_space=pltpu.SMEM)] + [pl.BlockSpec(memory_space=pl.ANY)] * 5,
+        out_specs=pl.BlockSpec(memory_space=pl.ANY),
         out_shape=out,
+        scratch_shapes=[
+            pltpu.VMEM((2, length, width), bf16),
+            pltpu.VMEM((steps, 2, lanes, width), bf16),
+            pltpu.VMEM((steps, length, lanes), dtype),
+            pltpu.SemaphoreType.DMA((2,)),
+            pltpu.SemaphoreType.DMA((steps, 2)),
+            pltpu.SemaphoreType.DMA((steps,)),
+        ],
         compiler_params=pltpu.CompilerParams(vmem_limit_bytes=vmem_bytes),
         cost_estimate=estimate(2 * length * out_weight.size, [*pieces, out_weight, out]),
-    )(places, *pieces, out_weight, out_weight)
+    )(places, *pieces, out_weight)
 
 
 def weight_sum(places, cot_pieces, gated_pieces, rows, dtype):
@@ -206,7 +284,7 @@
     grid_spec = pltpu.PrefetchScalarGridSpec(
         num_scalar_prefetch=1,
         grid=(width // lanes,),
-        in_specs=[pl.BlockSpec((rows, length), lambda i, w: (w[count], 0))] * count
+        in_specs=[pl.BlockSpec((rows, length), lambda i, w: (w[count], 0), pipeline_mode=pl.Buffered(1))] * count
         + [pl.BlockSpec((length, lanes), lambda i, w: (0, i))] * count,
         out_specs=pl.BlockSpec((rows, lanes), lambda i, w: (0, i)),
         scratch_shapes=[pltpu.VMEM((count, length, lanes), bf16)],
@@ -300,7 +378,7 @@
             for t in range(n_tp):
                 block = sum(crossed[s % 2]) - t if t in crossed[s % 2] else t
                 route.append((s * n_tp + t, block * n_tp + holder(s, block)))
-        moved = lax.ppermute(held, ("seq", "tp"), route)
+        moved = lax.ppermute(after(held, prior), ("seq", "tp"), route)
     else:
         moved = cot
 
@@ -308,11 +386,11 @@
         functools.partial(state_kernel, scale),
         tables,
         [prior, key_rows, value_rows, filter_taps, skip_gain[None], queries],
-        [rows32, half16, half16],
+        [[rows32], [half16, half16]],
         channels,
         unit * (4 * taps + 5 * length),
     )
-    gated[0], gated[1], *rounds = lax.optimization_barrier((*gated, *rounds))
+    gated[0], gated[1], moved, *rounds = lax.optimization_barrier((*gated, moved, *rounds))
 
     route = [(tp_dp(h, c, d), tp_dp(h, (c + 1) % subs, d)) for h, c, d in places]
     theirs = [lax.ppermute(r, ("tp", "dp"), route) for r in rounds]
@@ -361,8 +439,7 @@
             return part
 
         def weight_all():
-            sent = [first_sent, weight_half(halves[1])(1 - me_dp, bf16)]
-            sent = [swap_pairs(value, "dp", 1) for value in sent]
+            sent = [first_received, swap_pairs(weight_half(halves[1])(1 - me_dp, bf16), "dp", 1)]
             return jnp.concatenate(
                 [
                     (weight_half(held)(me_dp, f32) + value.astype(f32)) * norm_factor
@@ -393,19 +470,11 @@
         lag_kernel,
         tables,
         [own_part, other_part, state, queries, prior, key_rows, value_rows],
-        [rows16, rows16, jax.ShapeDtypeStruct((taps, channels), f32)],
+        [[rows16], [rows16], [jax.ShapeDtypeStruct((taps, channels), f32)]],
         channels,
         unit * (2 * taps + 4 * length + 3 * taps),
     )
     later = lax.ppermute(signal[:taps], "seq", [(i + 1, i) for i in range(n_seq - 1)])
-    grad_key, grad_value = by_channel(
-        functools.partial(back_kernel, scale),
-        tables,
-        [signal, later, filter_taps, skip_gain[None], key_rows, value_rows],
-        [rows16, rows16],
-        channels,
-        unit * (4 * taps + 5 * length),
-    )
 
     share = taps // n_dp
     lag_sum = lax.dynamic_slice_in_dim(lags, me_dp * share, share, axis=0) + swap_pairs(
@@ -428,6 +497,17 @@
     lag_sum = jnp.concatenate([jnp.where(first, mine, theirs), jnp.where(first, theirs, mine)], axis=0)
     grad_filter = lag_sum.astype(f32).T * (norm_factor * scale)
 
+    if square:
+        first_received = swap_pairs(first_sent, "dp", 1)
+        first_received, later = lax.optimization_barrier((first_received, later))
+    grad_key, grad_value = by_channel(
+        functools.partial(back_kernel, scale),
+        tables,
+        [signal, later, filter_taps, skip_gain[None], key_rows, value_rows],
+        [[rows16], [rows16]],
+        channels,
+        unit * (4 * taps + 5 * length),
+    )
     grad_weight = weight_all()
     return (
         grad_query[None],

time: 134 us -> 134 us (level)
  Pallas kernels: 35.1 us -> 53.5 us
  local copies, waits for them, and re-layouts: 20.2 us -> 9.06 us
  waiting for transfers between devices: 24.1 us -> 17.5 us
    pallas_call x5, Pallas kernels: 22.9 us -> 34.3 us  [the longest x3 23.3 us: by_channel(): pl.pallas_call(kernel, in_specs=[pl.BlockSpec(memory_space=pl.ANY)] * (n_...]
    unnamed x71 -> x39, local copies, waits for them, and re-layouts: 17.8 us -> 6.79 us
    ppermute x7, waiting for transfers between devices: 14.4 us -> 4.18 us  [swap_pairs(): return lax.ppermute(value, axis, [(i, i ^ distance) for i in range(count)])]
    ppermute x2, starting transfers between devices: 0.51 us -> 8.95 us  [per_device(): theirs = [lax.ppermute(r, ('tp', 'dp'), route) for r in rounds]]
    ppermute x6, starting transfers between devices: 18.8 us -> 11 us  [ring_step(): pieces.append(lax.ppermute(pieces[-1], 'seq', ring))]
    pallas_call x4, Pallas kernels: 11.8 us -> 15.8 us  [weight_sum(): pl.pallas_call(functools.partial(weight_kernel, count), grid_spec=grid_sp...]
    ppermute x7, starting transfers between devices: 4.84 us -> 8.64 us  [swap_pairs(): return lax.ppermute(value, axis, [(i, i ^ distance) for i in range(count)])]
    ppermute x1, waiting for transfers between devices: 1.96 us -> 5.44 us  [per_device(): prior = lax.ppermute(tail, 'seq', [(i, i + 1) for i in range(n_seq - 1)])]
  transfers between devices with their start and end apart: 24 -> 24, of which waited for: 8 -> 8; matrix products, arithmetic and copies ran while one was open for 5% -> 6% of each run, Pallas kernels for 26% -> 38%
where the time goes in v7:
time: 134 us; the launch traced here: 133 us
  Pallas kernels  53.5 us (40%)
  starting transfers between devices  44.9 us (34%)
  waiting for transfers between devices  17.5 us (13%)
  local copies, waits for them, and re-layouts  9.06 us (7%)
  other arithmetic  6.92 us (5%)
    pallas_call x3, Pallas kernels, by_channel(): pl.pallas_call(kernel, in_specs=[pl.BlockSpec(memory_space=pl.ANY)] * (n_...  23.3 us
    pallas_call x4, Pallas kernels, weight_sum(): pl.pallas_call(functools.partial(weight_kernel, count), grid_spec=grid_sp...  15.8 us
    pallas_call x2, Pallas kernels, project(): pl.pallas_call(project_kernel, in_specs=[pl.BlockSpec(memory_space=pltpu....  11.1 us
    ppermute x6, starting transfers between devices, ring_step(): pieces.append(lax.ppermute(pieces[-1], 'seq', ring))  11 us
    ppermute x2, starting transfers between devices, per_device(): theirs = [lax.ppermute(r, ('tp', 'dp'), route) for r in rounds]  8.95 us
    ppermute x7, starting transfers between devices, swap_pairs(): return lax.ppermute(value, axis, [(i, i ^ distance) for i in range(count)])  8.64 us
    ppermute x6, waiting for transfers between devices, ring_step(): pieces.append(lax.ppermute(pieces[-1], 'seq', ring))  7.89 us
    unnamed x39, local copies, waits for them, and re-layouts  6.79 us
  transfers between devices with their start and end apart: 24, of which 8 were waited for; matrix products, arithmetic and copies ran while one was open for 6% of the time, Pallas kernels for 38%

profile of v7, /device:TPU:0, one launch (start us, length us, event | category | flops | bytes accessed | tf_op | source)
XLA Modules:
  0.0 132.9 jit_solution(12533386562357850857)
XLA Ops:
  1.7 3.3 %shard_map.146 = bf16[1024,256]{1,0:T(8,128)(2,1)} custom-call(bf16[256,1024]{1,0:T(8,128)(2,1)} %bitcast.27), custom_call_target="tpu_custom_call" | custom-call | bytes 1048576 | tf_op jit(solution)/shard_map/pallas_call | solution.py:360
  5.7 4.2 %collective-permute-start.4 = (bf16[256,1024]{1,0:T(8,128)(2,1)}, bf16[256,1024]{1,0:T(8,128)(2,1)S(1)}, u32[]{:S(2)}, u32[]{:S(2)}) collective-permute-start(bf16[256,1024]{1,0:T(8,128)(2,1)} %bitcast.28), channel_id=1, source_target_pairs={{0,4},{1,0},{2,6},{3,2},{4,5},{5,1},{6,7},{7,3},{8,12},{9,8},{10,1... | collective-permute-start | bytes 1572872 | tf_op jit(solution)/shard_map/ppermute | solution.py:347
  10.0 1.7 %collective-permute-start.3 = (bf16[256,1024]{1,0:T(8,128)(2,1)}, bf16[256,1024]{1,0:T(8,128)(2,1)S(1)}, u32[]{:S(2)}, u32[]{:S(2)}) collective-permute-start(bf16[256,1024]{1,0:T(8,128)(2,1)} %bitcast.29), channel_id=1, source_target_pairs={{0,0},{1,4},{2,2},{3,6},{4,1},{5,5},{6,3},{7,7},{8,8},{9,12},{10,1... | collective-permute-start | bytes 1572872 | tf_op jit(solution)/shard_map/ppermute | solution.py:347
  11.6 2.9 %collective-permute-start = (bf16[128,1024]{1,0:T(8,128)(2,1)S(1)}, bf16[128,1024]{1,0:T(8,128)(2,1)S(1)}, u32[]{:S(2)}, u32[]{:S(2)}) collective-permute-start(bf16[128,1024]{1,0:T(8,128)(2,1)S(1)} %fusion), channel_id=1, source_target_pairs={{0,8},{8,16},{16,24},{1,9},{9,17},{17,25},{2,10},{10,18},{18,26},{... | collective-permute-start | bytes 786440 | tf_op jit(solution)/shard_map/ppermute | solution.py:338
  15.8 5.4 %collective-permute-done.refs_2_.refs_6_ = bf16[128,1024]{1,0:T(8,128)(2,1)S(1)} collective-permute-done((bf16[128,1024]{1,0:T(8,128)(2,1)S(1)}, bf16[128,1024]{1,0:T(8,128)(2,1)S(1)}, u32[]{:S(2)}, u32[]{:S(2)}) %collective-permute-start) | collective-permute-done | bytes 262176 | tf_op jit(solution)/shard_map/ppermute | solution.py:338
  21.9 8.0 %shard_map.145 = (f32[256,1024]{1,0:T(8,128)}, bf16[256,512]{1,0:T(8,128)(2,1)}, bf16[256,512]{1,0:T(8,128)(2,1)}) custom-call(bf16[2,384,384]{2,1,0:T(8,128)(2,1)} %constant.69.clone.refs_0_, bf16[2,384,384]{2,1,0:T(8,128)(2,1)} %constant.70.clone.refs_1_, bf16[128,1024]{1,0:T(8,128)(2,1)} %copy-done.16, bf16[256,1024]{1,0:T(8,128)(2,1)} %bitcast.24, ...), custom_call_target="tpu_custom_call" | custom-call | flops 1409286144 | bytes 3674112 | tf_op jit(solution)/shard_map/pallas_call | solution.py:237
  30.0 8.9 %collective-permute-start.8 = (bf16[256,1024]{1,0:T(8,128)(2,1)S(1)}, bf16[256,1024]{1,0:T(8,128)(2,1)S(1)}, u32[]{:S(2)}, u32[]{:S(2)}) collective-permute-start(bf16[256,1024]{1,0:T(8,128)(2,1)S(1)} %collective-permute-done.3.first_mine), channel_id=1, source_target_pairs={{0,2},{1,3},{2,0},{3,1},{4,6},{5,7},{6,4},{7,5},{8,10},{9,11},{10,... | collective-permute-start | bytes 1572872 | tf_op jit(solution)/shard_map/ppermute | solution.py:396
  39.8 4.6 %collective-permute-start.12 = (bf16[1024,256]{1,0:T(8,128)(2,1)S(1)}, bf16[1024,256]{1,0:T(8,128)(2,1)S(1)}, u32[]{:S(2)}, u32[]{:S(2)}) collective-permute-start(bf16[1024,256]{1,0:T(8,128)(2,1)S(1)} %collective-permute-done.2.refs_0_), channel_id=1, source_target_pairs={{0,4},{2,6},{4,0},{6,2},{1,5},{3,7},{5,1},{7,3},{8,12},{10,14},{12... | collective-permute-start | bytes 1572872 | tf_op jit(solution)/shard_map/ppermute | solution.py:422
  44.4 3.6 %collective-permute-done.5.refs_5_ = bf16[256,512]{1,0:T(8,128)(2,1)} collective-permute-done((bf16[256,512]{1,0:T(8,128)(2,1)}, bf16[256,512]{1,0:T(8,128)(2,1)}, u32[]{:S(2)}, u32[]{:S(2)}) %collective-permute-start.5) | collective-permute-done | bytes 262176 | tf_op jit(solution)/shard_map/ppermute | solution.py:409
  48.0 1.5 %collective-permute-start.6 = (bf16[256,512]{1,0:T(8,128)(2,1)}, bf16[256,512]{1,0:T(8,128)(2,1)}, u32[]{:S(2)}, u32[]{:S(2)}) collective-permute-start(bf16[256,512]{1,0:T(8,128)(2,1)} %collective-permute-done.5.refs_5_), channel_id=1, source_target_pairs={{0,16},{16,24},{24,8},{8,0},{1,17},{17,25},{25,9},{9,1},{2,18},{18... | collective-permute-start | bytes 786440 | tf_op jit(solution)/shard_map/ppermute | solution.py:409
  51.1 5.7 %shard_map.148 = bf16[256,1024]{1,0:T(8,128)(2,1)} custom-call(s32[3]{0:T(128)} %add_add_fusion.place_ref, bf16[256,1024]{1,0:T(8,128)(2,1)} %copy-done.7, bf16[256,1024]{1,0:T(8,128)(2,1)} %copy-done.6, bf16[256,1024]{1,0:T(8,128)(2,1)} %copy-done.8, bf16[256,1024]{1,0:T(8,128)(2,1)} %copy-done.9, bf16[1024,2048]{1,0:T(8,128)(2,1)} %weight.3), custom_call_target="tpu_custom_call" | custom-call | flops 1073741824 | bytes 6815744 | tf_op jit(solution)/shard_map/pallas_call | solution.py:261
  56.8 1.7 %collective-permute-start.10 = (bf16[256,1024]{1,0:T(8,128)(2,1)}, bf16[256,1024]{1,0:T(8,128)(2,1)S(1)}, u32[]{:S(2)}, u32[]{:S(2)}) collective-permute-start(bf16[256,1024]{1,0:T(8,128)(2,1)} %shard_map.148), channel_id=1, source_target_pairs={{0,1},{1,0},{2,3},{3,2},{4,5},{5,4},{6,7},{7,6},{8,9},{9,8},{10,11... | collective-permute-start | bytes 1572872 | tf_op jit(solution)/shard_map/ppermute | solution.py:303
  59.0 2.5 %collective-permute-start.7 = (bf16[256,512]{1,0:T(8,128)(2,1)}, bf16[256,512]{1,0:T(8,128)(2,1)S(1)}, u32[]{:S(2)}, u32[]{:S(2)}) collective-permute-start(bf16[256,512]{1,0:T(8,128)(2,1)} %collective-permute-done.6.refs_6_), channel_id=1, source_target_pairs={{0,16},{16,24},{24,8},{8,0},{1,17},{17,25},{25,9},{9,1},{2,18},{18... | collective-permute-start | bytes 786440 | tf_op jit(solution)/shard_map/ppermute | solution.py:409
  61.5 1.2 collective-permute-start.14
  63.0 5.4 %shard_map.147.refs_2_ = f32[256,1024]{1,0:T(8,128)} custom-call(s32[3]{0:T(128)} %add_add_fusion.1.place_ref, bf16[256,1024]{1,0:T(8,128)(2,1)} %copy-done.7, bf16[256,1024]{1,0:T(8,128)(2,1)} %copy-done.6, bf16[256,1024]{1,0:T(8,128)(2,1)} %copy-done.8, bf16[256,1024]{1,0:T(8,128)(2,1)} %copy-done.9, bf16[1024,2048]{1,0:T(8,128)(2,1)} %weight.3), custom_call_target="tpu_custom_call" | custom-call | flops 1073741824 | bytes 7340032 | tf_op jit(solution)/shard_map/pallas_call | solution.py:261
  68.6 1.4 %collective-permute-done.10.refs_3_ = bf16[256,1024]{1,0:T(8,128)(2,1)S(1)} collective-permute-done((bf16[256,1024]{1,0:T(8,128)(2,1)}, bf16[256,1024]{1,0:T(8,128)(2,1)S(1)}, u32[]{:S(2)}, u32[]{:S(2)}) %collective-permute-start.10) | collective-permute-done | bytes 524320 | tf_op jit(solution)/shard_map/ppermute | solution.py:303
  70.9 7.3 %shard_map.149 = (bf16[256,1024]{1,0:T(8,128)(2,1)}, bf16[256,1024]{1,0:T(8,128)(2,1)}, f32[128,1024]{1,0:T(8,128)}) custom-call(bf16[2,384,384]{2,1,0:T(8,128)(2,1)} %constant.69.clone.refs_0_, bf16[2,384,384]{2,1,0:T(8,128)(2,1)} %constant.70.clone.refs_1_, f32[256,1024]{1,0:T(8,128)} %shard_map.147.refs_2_, bf16[256,1024]{1,0:T(8,128)(2,1)} %copy-done.15, ...), custom_call_target="tpu_custom_call" | custom-call | flops 1308622848 | bytes 6029312 | tf_op jit(solution)/shard_map/pallas_call | solution.py:237
  79.2 1.7 %collective-permute-start.16 = (bf16[64,1024]{1,0:T(8,128)(2,1)S(1)}, bf16[64,1024]{1,0:T(8,128)(2,1)S(1)}, u32[]{:S(2)}, u32[]{:S(2)}) collective-permute-start(bf16[64,1024]{1,0:T(8,128)(2,1)S(1)} %dynamic-slice_convert_fusion), channel_id=1, source_target_pairs={{0,1},{1,0},{2,3},{3,2},{4,5},{5,4},{6,7},{7,6},{8,9},{9,8},{10,11... | collective-permute-start | bytes 393224 | tf_op jit(solution)/shard_map/ppermute | solution.py:303
  80.9 2.2 %collective-permute-start.15 = (bf16[256,512]{1,0:T(8,128)(2,1)S(1)}, bf16[256,512]{1,0:T(8,128)(2,1)S(1)}, u32[]{:S(2)}, u32[]{:S(2)}) collective-permute-start(bf16[256,512]{1,0:T(8,128)(2,1)S(1)} %collective-permute-done.14.refs_5_), channel_id=1, source_target_pairs={{0,16},{16,24},{24,8},{8,0},{1,17},{17,25},{25,9},{9,1},{2,18},{18... | collective-permute-start | bytes 786440 | tf_op jit(solution)/shard_map/ppermute | solution.py:409
  85.2 2.1 %collective-permute-done.15.refs_6_ = bf16[256,512]{1,0:T(8,128)(2,1)S(1)} collective-permute-done((bf16[256,512]{1,0:T(8,128)(2,1)S(1)}, bf16[256,512]{1,0:T(8,128)(2,1)S(1)}, u32[]{:S(2)}, u32[]{:S(2)}) %collective-permute-start.15) | collective-permute-done | bytes 262176 | tf_op jit(solution)/shard_map/ppermute | solution.py:409
  87.3 2.0 %collective-permute-start.17 = (bf16[64,1024]{1,0:T(8,128)(2,1)S(1)}, bf16[64,1024]{1,0:T(8,128)(2,1)S(1)}, u32[]{:S(2)}, u32[]{:S(2)}) collective-permute-start(bf16[64,1024]{1,0:T(8,128)(2,1)S(1)} %convert_add_fusion.1), channel_id=1, source_target_pairs={{0,8},{8,0},{16,24},{24,16},{1,9},{9,1},{17,25},{25,17},{2,10},{10... | collective-permute-start | bytes 393224 | tf_op jit(solution)/shard_map/ppermute | solution.py:303
  90.9 3.9 %shard_map.150 = bf16[512,512]{1,0:T(8,128)(2,1)} custom-call(s32[5]{0:T(128)} %get-tuple-element.71.place_ref, bf16[1024,256]{1,0:T(8,128)(2,1)} %copy-done, bf16[1024,256]{1,0:T(8,128)(2,1)} %copy-done.2, bf16[1024,256]{1,0:T(8,128)(2,1)} %copy-done.1, bf16[1024,256]{1,0:T(8,128)(2,1)} %copy-done.3, bf16[256,512]{1,0:T(8,128)(2,1)} %get-tuple-element.39.refs_4_, ...), custom_call_target="tpu_custom_call" | custom-call | flops 536870912 | bytes 3670016 | tf_op jit(solution)/shard_map/pallas_call | solution.py:292
  94.8 2.0 %collective-permute-start.20 = (bf16[64,1024]{1,0:T(8,128)(2,1)S(1)}, bf16[64,1024]{1,0:T(8,128)(2,1)S(1)}, u32[]{:S(2)}, u32[]{:S(2)}) collective-permute-start(bf16[64,1024]{1,0:T(8,128)(2,1)S(1)} %convert_add_fusion), channel_id=1, source_target_pairs={{0,16},{8,24},{16,0},{24,8},{1,17},{9,25},{17,1},{25,9},{2,18},{10... | collective-permute-start | bytes 393224 | tf_op jit(solution)/shard_map/ppermute | solution.py:303
  96.8 1.3 collective-permute-start.19
  98.1 3.4 %collective-permute-start.22 = (bf16[256,512]{1,0:T(8,128)(2,1)S(1)}, bf16[256,512]{1,0:T(8,128)(2,1)S(1)}, u32[]{:S(2)}, u32[]{:S(2)}) collective-permute-start(bf16[256,512]{1,0:T(8,128)(2,1)S(1)} %collective-permute-done.15.refs_6_), channel_id=1, source_target_pairs={{0,16},{16,24},{24,8},{8,0},{1,17},{17,25},{25,9},{9,1},{2,18},{18... | collective-permute-start | bytes 786440 | tf_op jit(solution)/shard_map/ppermute | solution.py:409
  101.9 2.3 %collective-permute-done.20 = bf16[64,1024]{1,0:T(8,128)(2,1)S(1)} collective-permute-done((bf16[64,1024]{1,0:T(8,128)(2,1)S(1)}, bf16[64,1024]{1,0:T(8,128)(2,1)S(1)}, u32[]{:S(2)}, u32[]{:S(2)}) %collective-permute-start.20) | collective-permute-done | bytes 131104 | tf_op jit(solution)/shard_map/ppermute | solution.py:303
  104.6 4.1 %shard_map.152 = f32[512,512]{1,0:T(8,128)} custom-call(s32[5]{0:T(128)} %get-tuple-element.70.place_ref, bf16[1024,256]{1,0:T(8,128)(2,1)} %copy-done, bf16[1024,256]{1,0:T(8,128)(2,1)} %copy-done.2, bf16[1024,256]{1,0:T(8,128)(2,1)} %copy-done.1, bf16[1024,256]{1,0:T(8,128)(2,1)} %copy-done.3, bf16[256,512]{1,0:T(8,128)(2,1)} %get-tuple-element.39.refs_4_, ...), custom_call_target="tpu_custom_call" | custom-call | flops 536870912 | bytes 4194304 | tf_op jit(solution)/shard_map/pallas_call | solution.py:292
  108.7 2.0 %collective-permute-done.22.refs_7_ = bf16[256,512]{1,0:T(8,128)(2,1)S(1)} collective-permute-done((bf16[256,512]{1,0:T(8,128)(2,1)S(1)}, bf16[256,512]{1,0:T(8,128)(2,1)S(1)}, u32[]{:S(2)}, u32[]{:S(2)}) %collective-permute-start.22) | collective-permute-done | bytes 262176 | tf_op jit(solution)/shard_map/ppermute | solution.py:409
  111.4 3.9 %shard_map.154 = bf16[512,512]{1,0:T(8,128)(2,1)} custom-call(s32[5]{0:T(128)} %get-tuple-element.71.place_ref, bf16[1024,256]{1,0:T(8,128)(2,1)} %copy-done, bf16[1024,256]{1,0:T(8,128)(2,1)} %copy-done.2, bf16[1024,256]{1,0:T(8,128)(2,1)} %copy-done.1, bf16[1024,256]{1,0:T(8,128)(2,1)} %copy-done.3, bf16[256,512]{1,0:T(8,128)(2,1)} %get-tuple-element.52.refs_4_, ...), custom_call_target="tpu_custom_call" | custom-call | flops 536870912 | bytes 3670016 | tf_op jit(solution)/shard_map/pallas_call | solution.py:292
  115.7 4.0 %shard_map.153 = f32[512,512]{1,0:T(8,128)} custom-call(s32[5]{0:T(128)} %get-tuple-element.70.place_ref, bf16[1024,256]{1,0:T(8,128)(2,1)} %copy-done, bf16[1024,256]{1,0:T(8,128)(2,1)} %copy-done.2, bf16[1024,256]{1,0:T(8,128)(2,1)} %copy-done.1, bf16[1024,256]{1,0:T(8,128)(2,1)} %copy-done.3, bf16[256,512]{1,0:T(8,128)(2,1)} %get-tuple-element.52.refs_4_, ...), custom_call_target="tpu_custom_call" | custom-call | flops 536870912 | bytes 4194304 | tf_op jit(solution)/shard_map/pallas_call | solution.py:292
  122.1 7.9 %shard_map.151 = (bf16[256,1024]{1,0:T(8,128)(2,1)}, bf16[256,1024]{1,0:T(8,128)(2,1)}) custom-call(bf16[2,384,384]{2,1,0:T(8,128)(2,1)} %constant.69.clone.refs_0_, bf16[2,384,384]{2,1,0:T(8,128)(2,1)} %constant.70.clone.refs_1_, bf16[256,1024]{1,0:T(8,128)(2,1)} %get-tuple-element.49.refs_2_, bf16[128,1024]{1,0:T(8,128)(2,1)} %copy-done.18, ...), custom_call_target="tpu_custom_call" | custom-call | flops 1409286144 | bytes 3149824 | tf_op jit(solution)/shard_map/pallas_call | solution.py:237
  131.4 1.5 %pad_maximum_fusion = f32[512,1024]{1,0:T(8,128)} fusion(f32[512,512]{1,0:T(8,128)S(1)} %add_multiply_fusion, f32[512,512]{1,0:T(8,128)S(1)} %add_multiply_fusion.1), kind=kLoop, calls=%fused_computation | loop fusion | flops 524288 | bytes 4194304 | tf_op jit(solution)/shard_map/concatenate | solution.py:443
  (82 shorter events, 18.3 us)
Async XLA Ops:
  5.1 9.6 %collective-permute-start.1 = (bf16[1024,256]{1,0:T(8,128)(2,1)}, bf16[1024,256]{1,0:T(8,128)(2,1)S(1)}, u32[]{:S(2)}, u32[]{:S(2)}) collective-permute-start(bf16[1024,256]{1,0:T(8,128)(2,1)} %shard_map.146), channel_id=1, source_target_pairs={{2,4},{4,2},{8,14},{14,8},{18,20},{20,18},{24,30},{30,24},{3,5},{5... | collective-permute-start | bytes 1572872 | tf_op jit(solution)/shard_map/ppermute | solution.py:369
  5.7 24.2 %collective-permute-start.4 = (bf16[256,1024]{1,0:T(8,128)(2,1)}, bf16[256,1024]{1,0:T(8,128)(2,1)S(1)}, u32[]{:S(2)}, u32[]{:S(2)}) collective-permute-start(bf16[256,1024]{1,0:T(8,128)(2,1)} %bitcast.28), channel_id=1, source_target_pairs={{0,4},{1,0},{2,6},{3,2},{4,5},{5,1},{6,7},{7,3},{8,12},{9,8},{10,1... | collective-permute-start | bytes 1572872 | tf_op jit(solution)/shard_map/ppermute | solution.py:347
  10.0 20.0 %collective-permute-start.3 = (bf16[256,1024]{1,0:T(8,128)(2,1)}, bf16[256,1024]{1,0:T(8,128)(2,1)S(1)}, u32[]{:S(2)}, u32[]{:S(2)}) collective-permute-start(bf16[256,1024]{1,0:T(8,128)(2,1)} %bitcast.29), channel_id=1, source_target_pairs={{0,0},{1,4},{2,2},{3,6},{4,1},{5,5},{6,3},{7,7},{8,8},{9,12},{10,1... | collective-permute-start | bytes 1572872 | tf_op jit(solution)/shard_map/ppermute | solution.py:347
  11.6 9.5 %collective-permute-start = (bf16[128,1024]{1,0:T(8,128)(2,1)S(1)}, bf16[128,1024]{1,0:T(8,128)(2,1)S(1)}, u32[]{:S(2)}, u32[]{:S(2)}) collective-permute-start(bf16[128,1024]{1,0:T(8,128)(2,1)S(1)} %fusion), channel_id=1, source_target_pairs={{0,8},{8,16},{16,24},{1,9},{9,17},{17,25},{2,10},{10,18},{18,26},{... | collective-permute-start | bytes 786440 | tf_op jit(solution)/shard_map/ppermute | solution.py:338
  21.2 8.8 %collective-permute-start.2 = (bf16[1024,256]{1,0:T(8,128)(2,1)S(1)}, bf16[1024,256]{1,0:T(8,128)(2,1)S(1)}, u32[]{:S(2)}, u32[]{:S(2)}) collective-permute-start(bf16[1024,256]{1,0:T(8,128)(2,1)S(1)} %broadcast_select_fusion), channel_id=1, source_target_pairs={{0,0},{2,16},{4,12},{6,28},{8,24},{10,8},{12,20},{14,4},{16,2},{18... | collective-permute-start | bytes 1572872 | tf_op jit(solution)/shard_map/ppermute | solution.py:381
  30.0 19.6 %copy-start.6 = (bf16[256,1024]{1,0:T(8,128)(2,1)}, bf16[256,1024]{1,0:T(8,128)(2,1)S(1)}, u32[]{:S(2)}) copy-start(bf16[256,1024]{1,0:T(8,128)(2,1)S(1)} %collective-permute-done.4.second_mine) | copy-start | bytes 1572868
  30.0 19.5 %copy-start.7 = (bf16[256,1024]{1,0:T(8,128)(2,1)}, bf16[256,1024]{1,0:T(8,128)(2,1)S(1)}, u32[]{:S(2)}) copy-start(bf16[256,1024]{1,0:T(8,128)(2,1)S(1)} %collective-permute-done.3.first_mine) | copy-start | bytes 1572868
  30.0 31.5 %copy-start = (bf16[1024,256]{1,0:T(8,128)(2,1)}, bf16[1024,256]{1,0:T(8,128)(2,1)S(1)}, u32[]{:S(2)}) copy-start(bf16[1024,256]{1,0:T(8,128)(2,1)S(1)} %collective-permute-done.2.refs_0_) | copy-start | bytes 1572868
  30.0 19.5 %collective-permute-start.8 = (bf16[256,1024]{1,0:T(8,128)(2,1)S(1)}, bf16[256,1024]{1,0:T(8,128)(2,1)S(1)}, u32[]{:S(2)}, u32[]{:S(2)}) collective-permute-start(bf16[256,1024]{1,0:T(8,128)(2,1)S(1)} %collective-permute-done.3.first_mine), channel_id=1, source_target_pairs={{0,2},{1,3},{2,0},{3,1},{4,6},{5,7},{6,4},{7,5},{8,10},{9,11},{10,... | collective-permute-start | bytes 1572872 | tf_op jit(solution)/shard_map/ppermute | solution.py:396
  39.0 10.5 %collective-permute-start.9 = (bf16[256,1024]{1,0:T(8,128)(2,1)S(1)}, bf16[256,1024]{1,0:T(8,128)(2,1)S(1)}, u32[]{:S(2)}, u32[]{:S(2)}) collective-permute-start(bf16[256,1024]{1,0:T(8,128)(2,1)S(1)} %collective-permute-done.4.second_mine), channel_id=1, source_target_pairs={{0,2},{1,3},{2,0},{3,1},{4,6},{5,7},{6,4},{7,5},{8,10},{9,11},{10,... | collective-permute-start | bytes 1572872 | tf_op jit(solution)/shard_map/ppermute | solution.py:396
  39.0 9.0 %collective-permute-start.5 = (bf16[256,512]{1,0:T(8,128)(2,1)}, bf16[256,512]{1,0:T(8,128)(2,1)}, u32[]{:S(2)}, u32[]{:S(2)}) collective-permute-start(bf16[256,512]{1,0:T(8,128)(2,1)} %get-tuple-element.39.refs_4_), channel_id=1, source_target_pairs={{0,16},{16,24},{24,8},{8,0},{1,17},{17,25},{25,9},{9,1},{2,18},{18... | collective-permute-start | bytes 786440 | tf_op jit(solution)/shard_map/ppermute | solution.py:409
  39.8 21.7 %copy-start.10 = (bf16[256,512]{1,0:T(8,128)(2,1)S(1)}, bf16[256,512]{1,0:T(8,128)(2,1)}, u32[]{:S(2)}) copy-start(bf16[256,512]{1,0:T(8,128)(2,1)} %get-tuple-element.52.refs_4_) | copy-start | bytes 786436
  39.8 22.9 %collective-permute-start.12 = (bf16[1024,256]{1,0:T(8,128)(2,1)S(1)}, bf16[1024,256]{1,0:T(8,128)(2,1)S(1)}, u32[]{:S(2)}, u32[]{:S(2)}) collective-permute-start(bf16[1024,256]{1,0:T(8,128)(2,1)S(1)} %collective-permute-done.2.refs_0_), channel_id=1, source_target_pairs={{0,4},{2,6},{4,0},{6,2},{1,5},{3,7},{5,1},{7,3},{8,12},{10,14},{12... | collective-permute-start | bytes 1572872 | tf_op jit(solution)/shard_map/ppermute | solution.py:422
  48.0 11.1 %collective-permute-start.6 = (bf16[256,512]{1,0:T(8,128)(2,1)}, bf16[256,512]{1,0:T(8,128)(2,1)}, u32[]{:S(2)}, u32[]{:S(2)}) collective-permute-start(bf16[256,512]{1,0:T(8,128)(2,1)} %collective-permute-done.5.refs_5_), channel_id=1, source_target_pairs={{0,16},{16,24},{24,8},{8,0},{1,17},{17,25},{25,9},{9,1},{2,18},{18... | collective-permute-start | bytes 786440 | tf_op jit(solution)/shard_map/ppermute | solution.py:409
  56.8 13.3 %collective-permute-start.10 = (bf16[256,1024]{1,0:T(8,128)(2,1)}, bf16[256,1024]{1,0:T(8,128)(2,1)S(1)}, u32[]{:S(2)}, u32[]{:S(2)}) collective-permute-start(bf16[256,1024]{1,0:T(8,128)(2,1)} %shard_map.148), channel_id=1, source_target_pairs={{0,1},{1,0},{2,3},{3,2},{4,5},{5,4},{6,7},{7,6},{8,9},{9,8},{10,11... | collective-permute-start | bytes 1572872 | tf_op jit(solution)/shard_map/ppermute | solution.py:303
  59.0 9.6 %collective-permute-start.7 = (bf16[256,512]{1,0:T(8,128)(2,1)}, bf16[256,512]{1,0:T(8,128)(2,1)S(1)}, u32[]{:S(2)}, u32[]{:S(2)}) collective-permute-start(bf16[256,512]{1,0:T(8,128)(2,1)} %collective-permute-done.6.refs_6_), channel_id=1, source_target_pairs={{0,16},{16,24},{24,8},{8,0},{1,17},{17,25},{25,9},{9,1},{2,18},{18... | collective-permute-start | bytes 786440 | tf_op jit(solution)/shard_map/ppermute | solution.py:409
  61.5 28.4 %collective-permute-start.11 = (bf16[1024,256]{1,0:T(8,128)(2,1)S(1)}, bf16[1024,256]{1,0:T(8,128)(2,1)S(1)}, u32[]{:S(2)}, u32[]{:S(2)}) collective-permute-start(bf16[1024,256]{1,0:T(8,128)(2,1)S(1)} %collective-permute-done.2.refs_0_), channel_id=1, source_target_pairs={{0,2},{2,0},{4,6},{6,4},{1,3},{3,1},{5,7},{7,5},{8,10},{10,8},{12,... | collective-permute-start | bytes 1572872 | tf_op jit(solution)/shard_map/ppermute | solution.py:422
  61.5 19.4 %collective-permute-start.14 = (bf16[256,512]{1,0:T(8,128)(2,1)S(1)}, bf16[256,512]{1,0:T(8,128)(2,1)S(1)}, u32[]{:S(2)}, u32[]{:S(2)}) collective-permute-start(bf16[256,512]{1,0:T(8,128)(2,1)S(1)} %copy-done.10), channel_id=1, source_target_pairs={{0,16},{16,24},{24,8},{8,0},{1,17},{17,25},{25,9},{9,1},{2,18},{18... | collective-permute-start | bytes 786440 | tf_op jit(solution)/shard_map/ppermute | solution.py:409
  62.8 27.1 %collective-permute-start.13 = (bf16[1024,256]{1,0:T(8,128)(2,1)S(1)}, bf16[1024,256]{1,0:T(8,128)(2,1)S(1)}, u32[]{:S(2)}, u32[]{:S(2)}) collective-permute-start(bf16[1024,256]{1,0:T(8,128)(2,1)S(1)} %collective-permute-done.12.refs_2_), channel_id=1, source_target_pairs={{0,2},{2,0},{4,6},{6,4},{1,3},{3,1},{5,7},{7,5},{8,10},{10,8},{12,... | collective-permute-start | bytes 1572872 | tf_op jit(solution)/shard_map/ppermute | solution.py:422
  68.6 9.6 %copy-start.11 = (bf16[256,512]{1,0:T(8,128)(2,1)}, bf16[256,512]{1,0:T(8,128)(2,1)S(1)}, u32[]{:S(2)}) copy-start(bf16[256,512]{1,0:T(8,128)(2,1)S(1)} %collective-permute-done.7.refs_7_) | copy-start | bytes 786436
  79.2 5.0 %collective-permute-start.16 = (bf16[64,1024]{1,0:T(8,128)(2,1)S(1)}, bf16[64,1024]{1,0:T(8,128)(2,1)S(1)}, u32[]{:S(2)}, u32[]{:S(2)}) collective-permute-start(bf16[64,1024]{1,0:T(8,128)(2,1)S(1)} %dynamic-slice_convert_fusion), channel_id=1, source_target_pairs={{0,1},{1,0},{2,3},{3,2},{4,5},{5,4},{6,7},{7,6},{8,9},{9,8},{10,11... | collective-permute-start | bytes 393224 | tf_op jit(solution)/shard_map/ppermute | solution.py:303
  80.9 13.9 %copy-start.12 = (bf16[256,512]{1,0:T(8,128)(2,1)}, bf16[256,512]{1,0:T(8,128)(2,1)S(1)}, u32[]{:S(2)}) copy-start(bf16[256,512]{1,0:T(8,128)(2,1)S(1)} %collective-permute-done.14.refs_5_) | copy-start | bytes 786436
  80.9 6.4 %collective-permute-start.15 = (bf16[256,512]{1,0:T(8,128)(2,1)S(1)}, bf16[256,512]{1,0:T(8,128)(2,1)S(1)}, u32[]{:S(2)}, u32[]{:S(2)}) collective-permute-start(bf16[256,512]{1,0:T(8,128)(2,1)S(1)} %collective-permute-done.14.refs_5_), channel_id=1, source_target_pairs={{0,16},{16,24},{24,8},{8,0},{1,17},{17,25},{25,9},{9,1},{2,18},{18... | collective-permute-start | bytes 786440 | tf_op jit(solution)/shard_map/ppermute | solution.py:409
  85.2 11.6 %copy-start.17 = (bf16[256,1024]{1,0:T(8,128)(2,1)S(1)}, bf16[256,1024]{1,0:T(8,128)(2,1)}, u32[]{:S(2)}) copy-start(bf16[256,1024]{1,0:T(8,128)(2,1)} %get-tuple-element.49.refs_2_) | copy-start | bytes 1572868
  87.3 23.4 %copy-start.13 = (bf16[256,512]{1,0:T(8,128)(2,1)}, bf16[256,512]{1,0:T(8,128)(2,1)S(1)}, u32[]{:S(2)}) copy-start(bf16[256,512]{1,0:T(8,128)(2,1)S(1)} %collective-permute-done.15.refs_6_) | copy-start | bytes 786436
  87.3 7.5 %collective-permute-start.17 = (bf16[64,1024]{1,0:T(8,128)(2,1)S(1)}, bf16[64,1024]{1,0:T(8,128)(2,1)S(1)}, u32[]{:S(2)}, u32[]{:S(2)}) collective-permute-start(bf16[64,1024]{1,0:T(8,128)(2,1)S(1)} %convert_add_fusion.1), channel_id=1, source_target_pairs={{0,8},{8,0},{16,24},{24,16},{1,9},{9,1},{17,25},{25,17},{2,10},{10... | collective-permute-start | bytes 393224 | tf_op jit(solution)/shard_map/ppermute | solution.py:303
  94.8 9.3 %collective-permute-start.20 = (bf16[64,1024]{1,0:T(8,128)(2,1)S(1)}, bf16[64,1024]{1,0:T(8,128)(2,1)S(1)}, u32[]{:S(2)}, u32[]{:S(2)}) collective-permute-start(bf16[64,1024]{1,0:T(8,128)(2,1)S(1)} %convert_add_fusion), channel_id=1, source_target_pairs={{0,16},{8,24},{16,0},{24,8},{1,17},{9,25},{17,1},{25,9},{2,18},{10... | collective-permute-start | bytes 393224 | tf_op jit(solution)/shard_map/ppermute | solution.py:303
  96.8 24.5 %collective-permute-start.19 = (bf16[128,1024]{1,0:T(8,128)(2,1)S(1)}, bf16[128,1024]{1,0:T(8,128)(2,1)S(1)}, u32[]{:S(2)}, u32[]{:S(2)}) collective-permute-start(bf16[128,1024]{1,0:T(8,128)(2,1)S(1)} %slice.16), channel_id=1, source_target_pairs={{8,0},{16,8},{24,16},{9,1},{17,9},{25,17},{10,2},{18,10},{26,18},{... | collective-permute-start | bytes 786440 | tf_op jit(solution)/shard_map/ppermute | solution.py:477
  98.1 12.5 %collective-permute-start.22 = (bf16[256,512]{1,0:T(8,128)(2,1)S(1)}, bf16[256,512]{1,0:T(8,128)(2,1)S(1)}, u32[]{:S(2)}, u32[]{:S(2)}) collective-permute-start(bf16[256,512]{1,0:T(8,128)(2,1)S(1)} %collective-permute-done.15.refs_6_), channel_id=1, source_target_pairs={{0,16},{16,24},{24,8},{8,0},{1,17},{17,25},{25,9},{9,1},{2,18},{18... | collective-permute-start | bytes 786440 | tf_op jit(solution)/shard_map/ppermute | solution.py:409
  101.5 19.8 %collective-permute-start.18 = (bf16[512,512]{1,0:T(8,128)(2,1)}, bf16[512,512]{1,0:T(8,128)(2,1)S(1)}, u32[]{:S(2)}, u32[]{:S(2)}) collective-permute-start(bf16[512,512]{1,0:T(8,128)(2,1)} %shard_map.150), channel_id=1, source_target_pairs={{0,1},{1,0},{2,3},{3,2},{4,5},{5,4},{6,7},{7,6},{8,9},{9,8},{10,11... | collective-permute-start | bytes 1572872 | tf_op jit(solution)/shard_map/ppermute | solution.py:303
  104.2 15.5 %collective-permute-start.21 = (bf16[64,1024]{1,0:T(8,128)(2,1)S(1)}, bf16[64,1024]{1,0:T(8,128)(2,1)S(1)}, u32[]{:S(2)}, u32[]{:S(2)}) collective-permute-start(bf16[64,1024]{1,0:T(8,128)(2,1)S(1)} %add_convert_fusion), channel_id=1, source_target_pairs={{0,1},{1,0},{2,3},{3,2},{4,5},{5,4},{6,7},{7,6},{8,9},{9,8},{10,11... | collective-permute-start | bytes 393224 | tf_op jit(solution)/shard_map/ppermute | solution.py:303
  115.3 14.9 %collective-permute-start.23 = (bf16[512,512]{1,0:T(8,128)(2,1)}, bf16[512,512]{1,0:T(8,128)(2,1)S(1)}, u32[]{:S(2)}, u32[]{:S(2)}) collective-permute-start(bf16[512,512]{1,0:T(8,128)(2,1)} %shard_map.154), channel_id=1, source_target_pairs={{0,1},{1,0},{2,3},{3,2},{4,5},{5,4},{6,7},{7,6},{8,9},{9,8},{10,11... | collective-permute-start | bytes 1572872 | tf_op jit(solution)/shard_map/ppermute | solution.py:303
  (11 other events, 21.6 us)

commit v8 on v7

--- a/solution.py
+++ b/solution.py
@@ -87,64 +87,89 @@
     gated_ref[...] = (query_ref[...].astype(f32) * state).astype(bf16)
 
 
-def transpose_kernel(rows_ref, out_ref):
-    out_ref[...] = rows_ref[...].T
-
-
 def project_kernel(
-    place_ref, first_mine, second_mine, first_theirs, second_theirs, weight, out, pieces, blocks, totals, piece_sem, block_sem, out_sem
+    place_ref, first_mine, second_mine, first_theirs, second_theirs, weight, other, own, pieces, blocks, others, owns, piece_sem, block_sem, out_sem
 ):
-    steps, _, _, width = blocks.shape
-
-    def piece_copy(n, source):
-        return pltpu.make_async_copy(source, pieces.at[n], piece_sem.at[n])
-
-    def block_copy(n, i):
-        rows = pl.ds(pl.multiple_of(i * lanes, lanes), lanes)
-        columns = pl.ds(pl.multiple_of(place_ref[1 + n] * width, width), width)
-        return pltpu.make_async_copy(weight.at[rows, columns], blocks.at[i, n], block_sem.at[i, n])
-
-    def out_copy(i):
-        place = out.at[:, pl.ds(pl.multiple_of(i * lanes, lanes), lanes)]
-        return pltpu.make_async_copy(totals.at[i], place, out_sem.at[i])
-
-    @pl.when(place_ref[0] == 0)
-    def _():
-        piece_copy(0, first_mine).start()
-        piece_copy(1, first_theirs).start()
-
-    @pl.when(place_ref[0] != 0)
-    def _():
-        piece_copy(0, second_mine).start()
-        piece_copy(1, second_theirs).start()
+    steps, _, total_width = blocks.shape
+    length, width = first_mine.shape
+
+    def piece_copy(n, sub, source):
+        rows = pl.ds(n * length, length)
+        columns = pl.ds(pl.multiple_of(place_ref[1 + sub] * width, width), width)
+        return pltpu.make_async_copy(source, pieces.at[rows, columns], piece_sem.at[n, sub])
+
+    def block_copy(i):
+        return pltpu.make_async_copy(weight.at[pl.ds(i * lanes, lanes)], blocks.at[i], block_sem.at[i])
+
+    def out_copies(i):
+        columns = pl.ds(pl.multiple_of(i * lanes, lanes), lanes)
+        return [
+            pltpu.make_async_copy(others.at[i], other.at[:, columns], out_sem.at[0, i]),
+            pltpu.make_async_copy(owns.at[i], own.at[:, columns], out_sem.at[1, i]),
+        ]
 
     for i in range(steps):
-        for n in range(2):
-            block_copy(n, i).start()
+        block_copy(i).start()
+
+    def fetch(own_first):
+        for sub, (first, second) in enumerate([(first_mine, second_mine), (first_theirs, second_theirs)]):
+            piece_copy(0, sub, second if own_first else first).start()
+            piece_copy(1, sub, first if own_first else second).start()
+
+    pl.when(place_ref[0] != 0)(lambda: fetch(True))
+    pl.when(place_ref[0] == 0)(lambda: fetch(False))
     for n in range(2):
-        piece_copy(n, first_mine).wait()
+        for sub in range(2):
+            piece_copy(n, sub, first_mine).wait()
 
     @pl.loop(0, steps)
     def _(i):
-        for n in range(2):
-            block_copy(n, i).wait()
-        total = dot_nt(pieces[0], blocks[i, 0]) + dot_nt(pieces[1], blocks[i, 1])
-        totals[i] = total.astype(totals.dtype)
-        out_copy(i).start()
+        block_copy(i).wait()
+        total = dot_nt(pieces[...], blocks[i])
+        others[i] = total[:length].astype(bf16)
+        owns[i] = total[length:]
+        for copy in out_copies(i):
+            copy.start()
 
     for i in range(steps):
-        out_copy(i).wait()
+        for copy in out_copies(i):
+            copy.wait()
 
 
 def weight_kernel(count, place_ref, *refs):
-    out_ref, held_ref = refs[2 * count :]
-    for n, gated_ref in enumerate(refs[count : 2 * count]):
-        held_ref[n] = gated_ref[...]
-    total = None
-    for n, cot_ref in enumerate(refs[:count]):
-        part = dot(cot_ref[...], held_ref[place_ref[n]])
-        total = part if total is None else total + part
-    out_ref[...] = total.astype(out_ref.dtype)
+    cot_in, gated_in = refs[:count], refs[count : 2 * count]
+    other, own, cots, gateds, others, owns, in_sem, out_sem = refs[2 * count :]
+    length = gateds.shape[1]
+    rows = other.shape[0]
+    block = min(rows, lanes)
+    copies = [pltpu.make_async_copy(cot_in[n], cots.at[n], in_sem.at[0, n]) for n in range(count)]
+    copies += [pltpu.make_async_copy(gated_in[n], gateds.at[n], in_sem.at[1, n]) for n in range(count)]
+    for copy in copies:
+        copy.start()
+    for copy in copies:
+        copy.wait()
+    outs = [
+        pltpu.make_async_copy(others, other, out_sem.at[0]),
+        pltpu.make_async_copy(owns, own, out_sem.at[1]),
+    ]
+
+    def fill(replica, target):
+        @pl.loop(0, rows // block)
+        def _(i):
+            start = pl.multiple_of(replica * rows + i * block, block)
+            total = None
+            for n in range(count):
+                part = dot(cots[n, pl.ds(start, block), :], gateds[place_ref[n]])
+                total = part if total is None else total + part
+            target[pl.ds(pl.multiple_of(i * block, block), block), :] = total.astype(target.dtype)
+
+    me = place_ref[count]
+    fill(1 - me, others)
+    outs[0].start()
+    fill(me, owns)
+    outs[1].start()
+    for copy in outs:
+        copy.wait()
 
 
 def lag_kernel(
@@ -198,8 +223,8 @@
         def table_copy(k):
             return pltpu.make_async_copy(table_in[k], table_held[k], table_sem.at[k])
 
-        def arg_copy(k, i):
-            return pltpu.make_async_copy(part(arg_in[k], i, steps), arg_held[k].at[i], arg_sem.at[k, i])
+        def arg_copy(k):
+            return pltpu.make_async_copy(arg_in[k], arg_held[k], arg_sem.at[k])
 
         def out_copy(k, n, i):
             per = steps // len(groups[k])
@@ -208,31 +233,25 @@
 
         for k in range(n_tables):
             table_copy(k).start()
-        for i in range(steps):
-            for k in range(n_args):
-                arg_copy(k, i).start()
+        for k in range(n_args):
+            arg_copy(k).start()
         for k in range(n_tables):
             table_copy(k).wait()
+        for k in range(n_args):
+            arg_copy(k).wait()
 
         for n in range(max(len(group) for group in groups)):
             per = steps // max(len(group) for group in groups)
 
             @pl.loop(n * per, (n + 1) * per)
             def _(i):
-                for k in range(n_args):
-                    arg_copy(k, i).wait()
-                body(*table_held, *[held.at[i] for held in arg_held], *[held.at[i] for held in out_held])
+                body(*table_held, *[part(ref, i, steps) for ref in arg_held], *[held.at[i] for held in out_held])
                 for k in range(n_outs):
                     out_copy(k, min(n, len(groups[k]) - 1), i).start()
 
         for i in range(steps):
             for k in range(n_outs):
                 out_copy(k, i * len(groups[k]) // steps, i).wait()
-
-    def held(value):
-        if value.shape[1] in (channels, channels // 2):
-            return pltpu.VMEM((steps, value.shape[0], lanes), value.dtype)
-        return pltpu.VMEM((steps, lanes, value.shape[1]), value.dtype)
 
     return pl.pallas_call(
         kernel,
@@ -241,10 +260,10 @@
         out_shape=flat_outs,
         scratch_shapes=[
             *[pltpu.VMEM(t.shape, bf16) for t in tables],
-            *[held(a) for a in args],
-            *[held(group[0]) for group in outs],
+            *[pltpu.VMEM(a.shape, a.dtype) for a in args],
+            *[pltpu.VMEM((steps, group[0].shape[0], lanes), group[0].dtype) for group in outs],
             pltpu.SemaphoreType.DMA((n_tables,)),
-            pltpu.SemaphoreType.DMA((n_args, steps)),
+            pltpu.SemaphoreType.DMA((n_args,)),
             pltpu.SemaphoreType.DMA((n_outs, steps)),
         ],
         compiler_params=pltpu.CompilerParams(vmem_limit_bytes=vmem_bytes),
@@ -252,50 +271,85 @@
     )(*[jnp.asarray(t) for t in tables], *args)
 
 
-def project(places, firsts, seconds, out_weight, dtype):
+def local_call(kernel, places, args, outs, scratch, flops):
+    return pl.pallas_call(
+        kernel,
+        in_specs=[pl.BlockSpec(memory_space=pltpu.SMEM)] + [pl.BlockSpec(memory_space=pl.ANY)] * len(args),
+        out_specs=[pl.BlockSpec(memory_space=pl.ANY)] * len(outs),
+        out_shape=outs,
+        scratch_shapes=scratch,
+        compiler_params=pltpu.CompilerParams(vmem_limit_bytes=vmem_bytes),
+        cost_estimate=estimate(flops, [*args, *outs]),
+    )(places, *args)
+
+
+def project(places, firsts, seconds, out_weight):
     length, width = firsts[0].shape
-    channels = out_weight.shape[0]
+    channels, total_width = out_weight.shape
     steps = channels // lanes
-    out = jax.ShapeDtypeStruct((length, channels), dtype)
-    pieces = [firsts[0], seconds[0], firsts[1], seconds[1]]
+    return local_call(
+        project_kernel,
+        places,
+        [firsts[0], seconds[0], firsts[1], seconds[1], out_weight],
+        [jax.ShapeDtypeStruct((length, channels), dtype) for dtype in (bf16, f32)],
+        [
+            pltpu.VMEM((2 * length, total_width), bf16),
+            pltpu.VMEM((steps, lanes, total_width), bf16),
+            pltpu.VMEM((steps, length, lanes), bf16),
+            pltpu.VMEM((steps, length, lanes), f32),
+            pltpu.SemaphoreType.DMA((2, 2)),
+            pltpu.SemaphoreType.DMA((steps,)),
+            pltpu.SemaphoreType.DMA((2, steps)),
+        ],
+        4 * length * out_weight.size,
+    )
+
+
+def weight_sum(places, cot_pieces, gated_pieces, rows):
+    count = len(gated_pieces)
+    length, width = gated_pieces[0].shape
+    outs = [jax.ShapeDtypeStruct((rows, width), dtype) for dtype in (bf16, f32)]
+    return local_call(
+        functools.partial(weight_kernel, count),
+        places,
+        [*cot_pieces, *gated_pieces],
+        outs,
+        [
+            pltpu.VMEM((count, *cot_pieces[0].shape), bf16),
+            pltpu.VMEM((count, length, width), bf16),
+            *[pltpu.VMEM(o.shape, o.dtype) for o in outs],
+            pltpu.SemaphoreType.DMA((2, count)),
+            pltpu.SemaphoreType.DMA((2,)),
+        ],
+        4 * count * length * rows * width,
+    )
+
+
+def transpose_kernel(rows_in, out, rows, turned, sems):
+    copy = pltpu.make_async_copy(rows_in, rows, sems.at[0])
+    copy.start()
+    copy.wait()
+    for i in range(rows.shape[1] // lanes):
+        turned[pl.ds(i * lanes, lanes), :] = rows[:, pl.ds(i * lanes, lanes)].T
+    copy = pltpu.make_async_copy(turned, out, sems.at[1])
+    copy.start()
+    copy.wait()
+
+
+def transposed(rows):
     return pl.pallas_call(
-        project_kernel,
-        in_specs=[pl.BlockSpec(memory_space=pltpu.SMEM)] + [pl.BlockSpec(memory_space=pl.ANY)] * 5,
+        transpose_kernel,
+        in_specs=[pl.BlockSpec(memory_space=pl.ANY)],
         out_specs=pl.BlockSpec(memory_space=pl.ANY),
-        out_shape=out,
+        out_shape=jax.ShapeDtypeStruct(rows.shape[::-1], rows.dtype),
         scratch_shapes=[
-            pltpu.VMEM((2, length, width), bf16),
-            pltpu.VMEM((steps, 2, lanes, width), bf16),
-            pltpu.VMEM((steps, length, lanes), dtype),
+            pltpu.VMEM(rows.shape, rows.dtype),
+            pltpu.VMEM(rows.shape[::-1], rows.dtype),
             pltpu.SemaphoreType.DMA((2,)),
-            pltpu.SemaphoreType.DMA((steps, 2)),
-            pltpu.SemaphoreType.DMA((steps,)),
         ],
         compiler_params=pltpu.CompilerParams(vmem_limit_bytes=vmem_bytes),
-        cost_estimate=estimate(2 * length * out_weight.size, [*pieces, out_weight, out]),
-    )(places, *pieces, out_weight)
-
-
-def weight_sum(places, cot_pieces, gated_pieces, rows, dtype):
-    count = len(gated_pieces)
-    length, width = gated_pieces[0].shape
-    out = jax.ShapeDtypeStruct((rows, width), dtype)
-
-    grid_spec = pltpu.PrefetchScalarGridSpec(
-        num_scalar_prefetch=1,
-        grid=(width // lanes,),
-        in_specs=[pl.BlockSpec((rows, length), lambda i, w: (w[count], 0), pipeline_mode=pl.Buffered(1))] * count
-        + [pl.BlockSpec((length, lanes), lambda i, w: (0, i))] * count,
-        out_specs=pl.BlockSpec((rows, lanes), lambda i, w: (0, i)),
-        scratch_shapes=[pltpu.VMEM((count, length, lanes), bf16)],
-    )
-    return pl.pallas_call(
-        functools.partial(weight_kernel, count),
-        grid_spec=grid_spec,
-        out_shape=out,
-        compiler_params=pltpu.CompilerParams(vmem_limit_bytes=vmem_bytes),
-        cost_estimate=estimate(2 * count * length * rows * width, [*cot_pieces, *gated_pieces, out]),
-    )(places, *cot_pieces, *gated_pieces)
+        cost_estimate=estimate(0, [rows, rows]),
+    )(rows)
 
 
 def swap_pairs(value, axis, distance):
@@ -348,37 +402,11 @@
     square = n_seq == n_tp == 4 and subs == 2
     if square:
 
-        def holder(s, block):
-            return (s + block) % 2 * subs + s // 2
-
-        crossed = {0: (1, 2), 1: (0, 3)}
-        route = [
-            (s * n_tp + t, s * n_tp + sum(crossed[s % 2]) - t)
-            for s in range(n_seq)
-            for t in crossed[s % 2]
-        ]
-        cot_rows = pl.pallas_call(
-            transpose_kernel,
-            grid=(cot.shape[1] // lanes,),
-            in_specs=[pl.BlockSpec((length, lanes), lambda i: (0, i))],
-            out_specs=pl.BlockSpec((lanes, length), lambda i: (i, 0)),
-            out_shape=jax.ShapeDtypeStruct(cot.shape[::-1], bf16),
-            compiler_params=pltpu.CompilerParams(vmem_limit_bytes=vmem_bytes),
-            cost_estimate=estimate(0, [cot, cot]),
-        )(cot)
-        swapped = lax.ppermute(cot_rows, ("seq", "tp"), route)
-        moves_now = sum(
-            jnp.logical_and(lax.axis_index("seq") % 2 == parity, me_tp == t)
-            for parity in crossed
-            for t in crossed[parity]
-        )
-        held = jnp.where(moves_now > 0, swapped, cot_rows)
-        route = []
-        for s in range(n_seq):
-            for t in range(n_tp):
-                block = sum(crossed[s % 2]) - t if t in crossed[s % 2] else t
-                route.append((s * n_tp + t, block * n_tp + holder(s, block)))
-        moved = lax.ppermute(after(held, prior), ("seq", "tp"), route)
+        def holder(s):
+            return s % 2 * subs + s // 2
+
+        route = [(s * n_tp + t, t * n_tp + holder(s)) for s in range(n_seq) for t in range(n_tp)]
+        moved = lax.ppermute(cot, ("seq", "tp"), route)
     else:
         moved = cot
 
@@ -390,16 +418,15 @@
         channels,
         unit * (4 * taps + 5 * length),
     )
-    gated[0], gated[1], moved, *rounds = lax.optimization_barrier((*gated, moved, *rounds))
+    gated[0], gated[1], *rounds = lax.optimization_barrier((*gated, *rounds))
 
     route = [(tp_dp(h, c, d), tp_dp(h, (c + 1) % subs, d)) for h, c, d in places]
     theirs = [lax.ppermute(r, ("tp", "dp"), route) for r in rounds]
     firsts, seconds = zip(rounds, theirs)
     same = (me_half == me_dp).astype(jnp.int32)
     subs_of = [me_sub, (me_sub + 1) % subs]
-    other_place = jnp.stack([same, *subs_of]).astype(jnp.int32)
+    place = jnp.stack([same, *subs_of]).astype(jnp.int32)
     rows = n_tp * channels // (n_seq * n_dp)
-    own_place = jnp.stack([1 - same, *subs_of]).astype(jnp.int32)
     if square:
         order = [*range(0, n_seq, 2), *reversed(range(1, n_seq, 2))]
         ring = [(order[k], order[(k + 1) % n_seq]) for k in range(n_seq)]
@@ -409,43 +436,36 @@
             pieces.append(lax.ppermute(pieces[-1], "seq", ring))
 
         ring_step(halves[0])
-        halves[0][1], other_place = lax.optimization_barrier((halves[0][1], other_place))
-        ring_step(halves[0])
-        halves[0][2], own_place = lax.optimization_barrier((halves[0][2], own_place))
+        halves[0][1], place = lax.optimization_barrier((halves[0][1], place))
         ring_step(halves[0])
         ring_step(halves[1])
-    other_sent = project(other_place, firsts, seconds, out_weight, bf16)
+    other_sent, own_part = project(place, firsts, seconds, out_weight)
     other_part = swap_pairs(other_sent, "dp", 1)
-    own_part = project(own_place, firsts, seconds, out_weight, f32)
 
     if square:
         sent_by = lambda value, flip: lax.ppermute(value, "tp", [(t, t ^ flip) for t in range(n_tp)])
+        moved = transposed(moved)
         across = sent_by(moved, subs)
         cot_pieces = [moved, sent_by(moved, 1), across, sent_by(across, 1)]
         table = np.zeros((n_seq, n_tp, n_tp), np.int32)
         for k, s in enumerate(order):
             for r in range(n_seq):
                 for t in range(n_tp):
-                    table[s, t, t ^ holder(order[k - r], s)] = r
+                    table[s, t, t ^ holder(order[k - r])] = r
         sources = jnp.asarray(table)[lax.axis_index("seq"), me_tp]
-        halves[0][3], own_part = lax.optimization_barrier((halves[0][3], own_part))
+        halves[0][2], halves[1][1], own_part = lax.optimization_barrier(
+            (halves[0][2], halves[1][1], own_part)
+        )
+        ring_step(halves[0])
         ring_step(halves[1])
 
-        def weight_half(held):
-            def part(replica, dtype):
-                where = jnp.concatenate([sources, replica[None].astype(jnp.int32)])
-                return weight_sum(where, cot_pieces, held, rows, dtype)
-
-            return part
+        weight_place = jnp.concatenate([sources, me_dp[None].astype(jnp.int32)])
 
         def weight_all():
-            sent = [first_received, swap_pairs(weight_half(halves[1])(1 - me_dp, bf16), "dp", 1)]
+            second_sent, second_own = weight_sum(weight_place, cot_pieces, halves[1], rows)
+            parts = [(first_own, first_received), (second_own, swap_pairs(second_sent, "dp", 1))]
             return jnp.concatenate(
-                [
-                    (weight_half(held)(me_dp, f32) + value.astype(f32)) * norm_factor
-                    for held, value in zip(halves, sent)
-                ],
-                axis=1,
+                [(mine + theirs.astype(f32)) * norm_factor for mine, theirs in parts], axis=1
             )
 
     else:
@@ -483,7 +503,7 @@
     if square:
         halves[1][2], lag_sum = lax.optimization_barrier((halves[1][2], lag_sum))
         ring_step(halves[1])
-        first_sent = weight_half(halves[0])(1 - me_dp, bf16)
+        first_sent, first_own = weight_sum(weight_place, cot_pieces, halves[0], rows)
     distance = 1
     while distance < n_seq:
         rounded = lag_sum.astype(bf16)

time: 134 us -> 140 us (1.045)
  waiting for transfers between devices: 17.5 us -> 44.2 us
  Pallas kernels: 53.5 us -> 41.5 us
  starting transfers between devices: 44.9 us -> 37.3 us
  other arithmetic: 6.92 us -> 5.21 us
    ppermute x6, waiting for transfers between devices: 7.89 us -> 20.4 us  [ring_step(): pieces.append(lax.ppermute(pieces[-1], 'seq', ring))]
    pallas_call x7 -> x4, Pallas kernels: 30.2 us -> 19 us  [the longest x3 16.9 us: local_call(): pl.pallas_call(kernel, in_specs=[pl.BlockSpec(memory_space=pltpu.SMEM)] +...]
    ppermute x7, waiting for transfers between devices: 4.18 us -> 15 us  [swap_pairs(): return lax.ppermute(value, axis, [(i, i ^ distance) for i in range(count)])]
    ppermute x2, starting transfers between devices: 8.95 us -> 0.51 us  [per_device(): theirs = [lax.ppermute(r, ('tp', 'dp'), route) for r in rounds]]
    ppermute x6, starting transfers between devices: 11 us -> 3.04 us  [ring_step(): pieces.append(lax.ppermute(pieces[-1], 'seq', ring))]
    ppermute x3, starting transfers between devices: 4.78 us -> 11.1 us  [per_device(): lax.ppermute(value, 'tp', [(t, t ^ flip) for t in range(n_tp)])]
    ppermute x2, waiting for transfers between devices: 0.01 us -> 4.82 us  [per_device(): rounds.append(lax.ppermute(cot, ('tp', 'dp'), route))]
    ppermute x1, waiting for transfers between devices: 5.44 us -> 3.99 us  [per_device(): prior = lax.ppermute(tail, 'seq', [(i, i + 1) for i in range(n_seq - 1)])]
  transfers between devices with their start and end apart: 24 -> 23, of which waited for: 8 -> 9; matrix products, arithmetic and copies ran while one was open for 6% -> 4% of each run, Pallas kernels for 38% -> 30%
where the time goes in v8:
time: 140 us; the launch traced here: 138 us
  waiting for transfers between devices  44.2 us (32%)
  Pallas kernels  41.5 us (30%)
  starting transfers between devices  37.3 us (27%)
  local copies, waits for them, and re-layouts  8.5 us (6%)
  other arithmetic  5.21 us (4%)
    pallas_call x3, Pallas kernels, by_channel(): pl.pallas_call(kernel, in_specs=[pl.BlockSpec(memory_space=pl.ANY)] * (n_...  22.5 us
    ppermute x6, waiting for transfers between devices, ring_step(): pieces.append(lax.ppermute(pieces[-1], 'seq', ring))  20.4 us
    pallas_call x3, Pallas kernels, local_call(): pl.pallas_call(kernel, in_specs=[pl.BlockSpec(memory_space=pltpu.SMEM)] +...  16.9 us
    ppermute x7, waiting for transfers between devices, swap_pairs(): return lax.ppermute(value, axis, [(i, i ^ distance) for i in range(count)])  15 us
    ppermute x3, starting transfers between devices, per_device(): lax.ppermute(value, 'tp', [(t, t ^ flip) for t in range(n_tp)])  11.1 us
    ppermute x7, starting transfers between devices, swap_pairs(): return lax.ppermute(value, axis, [(i, i ^ distance) for i in range(count)])  9.79 us
    ppermute x2, starting transfers between devices, per_device(): rounds.append(lax.ppermute(cot, ('tp', 'dp'), route))  6.4 us
    unnamed x35, local copies, waits for them, and re-layouts  6.23 us
  transfers between devices with their start and end apart: 23, of which 9 were waited for; matrix products, arithmetic and copies ran while one was open for 4% of the time, Pallas kernels for 30%

profile of v8, /device:TPU:0, one launch (start us, length us, event | category | flops | bytes accessed | tf_op | source)
XLA Modules:
  0.0 137.7 jit_solution(5804004153337923817)
XLA Ops:
  0.6 1.1 fusion
  1.7 1.7 %collective-permute-start.1 = (bf16[256,1024]{1,0:T(8,128)(2,1)}, bf16[256,1024]{1,0:T(8,128)(2,1)S(1)}, u32[]{:S(2)}, u32[]{:S(2)}) collective-permute-start(bf16[256,1024]{1,0:T(8,128)(2,1)} %bitcast.28), channel_id=1, source_target_pairs={{0,0},{1,4},{2,2},{3,6},{4,1},{5,5},{6,3},{7,7},{8,8},{9,12},{10,1... | collective-permute-start | bytes 1572872 | tf_op jit(solution)/shard_map/ppermute | solution.py:401
  3.4 4.7 %collective-permute-start.2 = (bf16[256,1024]{1,0:T(8,128)(2,1)}, bf16[256,1024]{1,0:T(8,128)(2,1)S(1)}, u32[]{:S(2)}, u32[]{:S(2)}) collective-permute-start(bf16[256,1024]{1,0:T(8,128)(2,1)} %bitcast.29), channel_id=1, source_target_pairs={{0,4},{1,0},{2,6},{3,2},{4,5},{5,1},{6,7},{7,3},{8,12},{9,8},{10,1... | collective-permute-start | bytes 1572872 | tf_op jit(solution)/shard_map/ppermute | solution.py:401
  8.1 3.5 %collective-permute-start = (bf16[128,1024]{1,0:T(8,128)(2,1)S(1)}, bf16[128,1024]{1,0:T(8,128)(2,1)S(1)}, u32[]{:S(2)}, u32[]{:S(2)}) collective-permute-start(bf16[128,1024]{1,0:T(8,128)(2,1)S(1)} %fusion), channel_id=1, source_target_pairs={{0,8},{8,16},{16,24},{1,9},{9,17},{17,25},{2,10},{10,18},{18,26},{... | collective-permute-start | bytes 786440 | tf_op jit(solution)/shard_map/ppermute | solution.py:392
  11.6 1.7 %collective-permute-start.9 = (bf16[256,1024]{1,0:T(8,128)(2,1)}, bf16[256,1024]{1,0:T(8,128)(2,1)S(1)}, u32[]{:S(2)}, u32[]{:S(2)}) collective-permute-start(bf16[256,1024]{1,0:T(8,128)(2,1)} %bitcast.30), channel_id=1, source_target_pairs={{0,0},{2,8},{4,16},{6,24},{8,4},{10,12},{12,20},{14,28},{16,2},{18... | collective-permute-start | bytes 1572872 | tf_op jit(solution)/shard_map/ppermute | solution.py:409
  13.3 4.0 %collective-permute-done.refs_2_.refs_6_ = bf16[128,1024]{1,0:T(8,128)(2,1)S(1)} collective-permute-done((bf16[128,1024]{1,0:T(8,128)(2,1)S(1)}, bf16[128,1024]{1,0:T(8,128)(2,1)S(1)}, u32[]{:S(2)}, u32[]{:S(2)}) %collective-permute-start) | collective-permute-done | bytes 262176 | tf_op jit(solution)/shard_map/ppermute | solution.py:392
  18.0 7.7 %shard_map.145 = (f32[256,1024]{1,0:T(8,128)}, bf16[256,512]{1,0:T(8,128)(2,1)}, bf16[256,512]{1,0:T(8,128)(2,1)}) custom-call(bf16[2,384,384]{2,1,0:T(8,128)(2,1)} %constant.57.clone.refs_0_, bf16[2,384,384]{2,1,0:T(8,128)(2,1)} %constant.58.clone.refs_1_, bf16[128,1024]{1,0:T(8,128)(2,1)} %copy-done.5, bf16[256,1024]{1,0:T(8,128)(2,1)} %bitcast.22, ...), custom_call_target="tpu_custom_call" | custom-call | flops 1409286144 | bytes 3674112 | tf_op jit(solution)/shard_map/pallas_call | solution.py:256
  25.8 4.8 %collective-permute-done.2.second_mine = bf16[256,1024]{1,0:T(8,128)(2,1)S(1)} collective-permute-done((bf16[256,1024]{1,0:T(8,128)(2,1)}, bf16[256,1024]{1,0:T(8,128)(2,1)S(1)}, u32[]{:S(2)}, u32[]{:S(2)}) %collective-permute-start.2) | collective-permute-done | bytes 524320 | tf_op jit(solution)/shard_map/ppermute | solution.py:401
  32.5 2.1 %shard_map.148.refs_0_ = bf16[1024,256]{1,0:T(8,128)(2,1)} custom-call(bf16[256,1024]{1,0:T(8,128)(2,1)} %copy-done.3), custom_call_target="tpu_custom_call" | custom-call | bytes 1048576 | tf_op jit(solution)/shard_map/pallas_call | solution.py:340
  34.6 11.1 %collective-permute-start.11 = (bf16[1024,256]{1,0:T(8,128)(2,1)}, bf16[1024,256]{1,0:T(8,128)(2,1)S(1)}, u32[]{:S(2)}, u32[]{:S(2)}) collective-permute-start(bf16[1024,256]{1,0:T(8,128)(2,1)} %shard_map.148.refs_0_), channel_id=1, source_target_pairs={{0,4},{2,6},{4,0},{6,2},{1,5},{3,7},{5,1},{7,3},{8,12},{10,14},{12... | collective-permute-start | bytes 1572872 | tf_op jit(solution)/shard_map/ppermute | solution.py:446
  46.5 6.3 %shard_map.146 = (bf16[256,1024]{1,0:T(8,128)(2,1)}, f32[256,1024]{1,0:T(8,128)}) custom-call(s32[3]{0:T(128)} %pad_add_fusion.place_ref, bf16[256,1024]{1,0:T(8,128)(2,1)} %copy-done.9, bf16[256,1024]{1,0:T(8,128)(2,1)} %copy-done.10, bf16[256,1024]{1,0:T(8,128)(2,1)} %copy-done.11, bf16[256,1024]{1,0:T(8,128)(2,1)} %collective-permute-done.7.second_theirs, ...), custom_call_target="tpu_custom_call" | custom-call | flops 2147483648 | bytes 7864320 | tf_op jit(solution)/shard_map/pallas_call | solution.py:275
  52.9 3.0 %collective-permute-start.8 = (bf16[256,1024]{1,0:T(8,128)(2,1)}, bf16[256,1024]{1,0:T(8,128)(2,1)S(1)}, u32[]{:S(2)}, u32[]{:S(2)}) collective-permute-start(bf16[256,1024]{1,0:T(8,128)(2,1)} %get-tuple-element.49), channel_id=1, source_target_pairs={{0,1},{1,0},{2,3},{3,2},{4,5},{5,4},{6,7},{7,6},{8,9},{9,8},{10,11... | collective-permute-start | bytes 1572872 | tf_op jit(solution)/shard_map/ppermute | solution.py:357
  55.8 1.0 collective-permute-start.4
  56.8 8.4 %collective-permute-done.5.refs_5_ = bf16[256,512]{1,0:T(8,128)(2,1)S(1)} collective-permute-done((bf16[256,512]{1,0:T(8,128)(2,1)}, bf16[256,512]{1,0:T(8,128)(2,1)S(1)}, u32[]{:S(2)}, u32[]{:S(2)}) %collective-permute-start.5) | collective-permute-done | bytes 262176 | tf_op jit(solution)/shard_map/ppermute | solution.py:436
  65.3 4.2 %collective-permute-done.4.refs_6_ = bf16[256,512]{1,0:T(8,128)(2,1)} collective-permute-done((bf16[256,512]{1,0:T(8,128)(2,1)}, bf16[256,512]{1,0:T(8,128)(2,1)}, u32[]{:S(2)}, u32[]{:S(2)}) %collective-permute-start.4) | collective-permute-done | bytes 262176 | tf_op jit(solution)/shard_map/ppermute | solution.py:436
  70.3 7.2 %shard_map.147 = (bf16[256,1024]{1,0:T(8,128)(2,1)}, bf16[256,1024]{1,0:T(8,128)(2,1)}, f32[128,1024]{1,0:T(8,128)}) custom-call(bf16[2,384,384]{2,1,0:T(8,128)(2,1)} %constant.57.clone.refs_0_, bf16[2,384,384]{2,1,0:T(8,128)(2,1)} %constant.58.clone.refs_1_, f32[256,1024]{1,0:T(8,128)} %get-tuple-element.48.refs_2_, bf16[256,1024]{1,0:T(8,128)(2,1)} %copy-done.4, ...), custom_call_target="tpu_custom_call" | custom-call | flops 1308622848 | bytes 6029312 | tf_op jit(solution)/shard_map/pallas_call | solution.py:256
  79.4 1.2 collective-permute-start.14
  81.3 3.2 %collective-permute-done.15 = bf16[64,1024]{1,0:T(8,128)(2,1)S(1)} collective-permute-done((bf16[64,1024]{1,0:T(8,128)(2,1)S(1)}, bf16[64,1024]{1,0:T(8,128)(2,1)S(1)}, u32[]{:S(2)}, u32[]{:S(2)}) %collective-permute-start.15) | collective-permute-done | bytes 131104 | tf_op jit(solution)/shard_map/ppermute | solution.py:357
  84.5 1.0 convert_add_fusion.1
  85.4 3.1 %collective-permute-done.14.refs_6_ = bf16[256,512]{1,0:T(8,128)(2,1)S(1)} collective-permute-done((bf16[256,512]{1,0:T(8,128)(2,1)S(1)}, bf16[256,512]{1,0:T(8,128)(2,1)S(1)}, u32[]{:S(2)}, u32[]{:S(2)}) %collective-permute-start.14) | collective-permute-done | bytes 262176 | tf_op jit(solution)/shard_map/ppermute | solution.py:436
  89.6 4.6 %collective-permute-done.13.refs_7_ = bf16[256,512]{1,0:T(8,128)(2,1)S(1)} collective-permute-done((bf16[256,512]{1,0:T(8,128)(2,1)}, bf16[256,512]{1,0:T(8,128)(2,1)S(1)}, u32[]{:S(2)}, u32[]{:S(2)}) %collective-permute-start.13) | collective-permute-done | bytes 262176 | tf_op jit(solution)/shard_map/ppermute | solution.py:436
  94.9 5.3 %shard_map.149 = (bf16[512,512]{1,0:T(8,128)(2,1)}, f32[512,512]{1,0:T(8,128)}) custom-call(s32[5]{0:T(128)} %pad_add_fusion.1.place_ref, bf16[1024,256]{1,0:T(8,128)(2,1)} %shard_map.148.refs_0_, bf16[1024,256]{1,0:T(8,128)(2,1)} %copy-done.8, bf16[1024,256]{1,0:T(8,128)(2,1)} %copy-done.7, bf16[1024,256]{1,0:T(8,128)(2,1)} %collective-permute-done.12.refs_3_, ...), custom_call_target="tpu_custom_call" | custom-call | flops 1073741824 | bytes 4718592 | tf_op jit(solution)/shard_map/pallas_call | solution.py:275
  100.2 2.2 %collective-permute-start.19 = (bf16[64,1024]{1,0:T(8,128)(2,1)S(1)}, bf16[64,1024]{1,0:T(8,128)(2,1)S(1)}, u32[]{:S(2)}, u32[]{:S(2)}) collective-permute-start(bf16[64,1024]{1,0:T(8,128)(2,1)S(1)} %convert_add_fusion), channel_id=1, source_target_pairs={{0,16},{8,24},{16,0},{24,8},{1,17},{9,25},{17,1},{25,9},{2,18},{10... | collective-permute-start | bytes 393224 | tf_op jit(solution)/shard_map/ppermute | solution.py:357
  103.2 1.2 collective-permute-start.17
  104.4 9.1 %collective-permute-done.19 = bf16[64,1024]{1,0:T(8,128)(2,1)S(1)} collective-permute-done((bf16[64,1024]{1,0:T(8,128)(2,1)S(1)}, bf16[64,1024]{1,0:T(8,128)(2,1)S(1)}, u32[]{:S(2)}, u32[]{:S(2)}) %collective-permute-start.19) | collective-permute-done | bytes 131104 | tf_op jit(solution)/shard_map/ppermute | solution.py:357
  113.6 1.4 collective-permute-start.20
  115.0 1.3 collective-permute-start.18
  117.0 5.3 %shard_map.151 = (bf16[512,512]{1,0:T(8,128)(2,1)}, f32[512,512]{1,0:T(8,128)}) custom-call(s32[5]{0:T(128)} %pad_add_fusion.1.place_ref, bf16[1024,256]{1,0:T(8,128)(2,1)} %shard_map.148.refs_0_, bf16[1024,256]{1,0:T(8,128)(2,1)} %copy-done.8, bf16[1024,256]{1,0:T(8,128)(2,1)} %copy-done.7, bf16[1024,256]{1,0:T(8,128)(2,1)} %collective-permute-done.12.refs_3_, ...), custom_call_target="tpu_custom_call" | custom-call | flops 1073741824 | bytes 4718592 | tf_op jit(solution)/shard_map/pallas_call | solution.py:275
  123.2 1.0 copy.16
  125.5 7.6 %shard_map.150 = (bf16[256,1024]{1,0:T(8,128)(2,1)}, bf16[256,1024]{1,0:T(8,128)(2,1)}) custom-call(bf16[2,384,384]{2,1,0:T(8,128)(2,1)} %constant.57.clone.refs_0_, bf16[2,384,384]{2,1,0:T(8,128)(2,1)} %constant.58.clone.refs_1_, bf16[256,1024]{1,0:T(8,128)(2,1)} %get-tuple-element.52.refs_2_, bf16[128,1024]{1,0:T(8,128)(2,1)} %copy-done.14, ...), custom_call_target="tpu_custom_call" | custom-call | flops 1409286144 | bytes 3149824 | tf_op jit(solution)/shard_map/pallas_call | solution.py:256
  133.3 2.7 %collective-permute-done.22 = bf16[512,512]{1,0:T(8,128)(2,1)S(1)} collective-permute-done((bf16[512,512]{1,0:T(8,128)(2,1)}, bf16[512,512]{1,0:T(8,128)(2,1)S(1)}, u32[]{:S(2)}, u32[]{:S(2)}) %collective-permute-start.22) | collective-permute-done | bytes 524320 | tf_op jit(solution)/shard_map/ppermute | solution.py:357
  136.2 1.5 %pad_maximum_fusion = f32[512,1024]{1,0:T(8,128)} fusion(f32[512,512]{1,0:T(8,128)S(1)} %add_multiply_fusion, f32[512,512]{1,0:T(8,128)S(1)} %add_multiply_fusion.1), kind=kLoop, calls=%fused_computation | loop fusion | flops 524288 | bytes 4194304 | tf_op jit(solution)/shard_map/concatenate | solution.py:467
  (71 shorter events, 12.7 us)
Async XLA Ops:
  1.7 24.0 %collective-permute-start.1 = (bf16[256,1024]{1,0:T(8,128)(2,1)}, bf16[256,1024]{1,0:T(8,128)(2,1)S(1)}, u32[]{:S(2)}, u32[]{:S(2)}) collective-permute-start(bf16[256,1024]{1,0:T(8,128)(2,1)} %bitcast.28), channel_id=1, source_target_pairs={{0,0},{1,4},{2,2},{3,6},{4,1},{5,5},{6,3},{7,7},{8,8},{9,12},{10,1... | collective-permute-start | bytes 1572872 | tf_op jit(solution)/shard_map/ppermute | solution.py:401
  3.4 27.2 %collective-permute-start.2 = (bf16[256,1024]{1,0:T(8,128)(2,1)}, bf16[256,1024]{1,0:T(8,128)(2,1)S(1)}, u32[]{:S(2)}, u32[]{:S(2)}) collective-permute-start(bf16[256,1024]{1,0:T(8,128)(2,1)} %bitcast.29), channel_id=1, source_target_pairs={{0,4},{1,0},{2,6},{3,2},{4,5},{5,1},{6,7},{7,3},{8,12},{9,8},{10,1... | collective-permute-start | bytes 1572872 | tf_op jit(solution)/shard_map/ppermute | solution.py:401
  8.1 9.2 %collective-permute-start = (bf16[128,1024]{1,0:T(8,128)(2,1)S(1)}, bf16[128,1024]{1,0:T(8,128)(2,1)S(1)}, u32[]{:S(2)}, u32[]{:S(2)}) collective-permute-start(bf16[128,1024]{1,0:T(8,128)(2,1)S(1)} %fusion), channel_id=1, source_target_pairs={{0,8},{8,16},{16,24},{1,9},{9,17},{17,25},{2,10},{10,18},{18,26},{... | collective-permute-start | bytes 786440 | tf_op jit(solution)/shard_map/ppermute | solution.py:392
  11.6 20.1 %collective-permute-start.9 = (bf16[256,1024]{1,0:T(8,128)(2,1)}, bf16[256,1024]{1,0:T(8,128)(2,1)S(1)}, u32[]{:S(2)}, u32[]{:S(2)}) collective-permute-start(bf16[256,1024]{1,0:T(8,128)(2,1)} %bitcast.30), channel_id=1, source_target_pairs={{0,0},{2,8},{4,16},{6,24},{8,4},{10,12},{12,20},{14,28},{16,2},{18... | collective-permute-start | bytes 1572872 | tf_op jit(solution)/shard_map/ppermute | solution.py:409
  25.8 20.0 %copy-start.9 = (bf16[256,1024]{1,0:T(8,128)(2,1)}, bf16[256,1024]{1,0:T(8,128)(2,1)S(1)}, u32[]{:S(2)}) copy-start(bf16[256,1024]{1,0:T(8,128)(2,1)S(1)} %collective-permute-done.1.first_mine) | copy-start | bytes 1572868
  30.6 15.1 %copy-start.10 = (bf16[256,1024]{1,0:T(8,128)(2,1)}, bf16[256,1024]{1,0:T(8,128)(2,1)S(1)}, u32[]{:S(2)}) copy-start(bf16[256,1024]{1,0:T(8,128)(2,1)S(1)} %collective-permute-done.2.second_mine) | copy-start | bytes 1572868
  30.6 15.1 %collective-permute-start.6 = (bf16[256,1024]{1,0:T(8,128)(2,1)S(1)}, bf16[256,1024]{1,0:T(8,128)(2,1)S(1)}, u32[]{:S(2)}, u32[]{:S(2)}) collective-permute-start(bf16[256,1024]{1,0:T(8,128)(2,1)S(1)} %collective-permute-done.1.first_mine), channel_id=1, source_target_pairs={{0,2},{1,3},{2,0},{3,1},{4,6},{5,7},{6,4},{7,5},{8,10},{9,11},{10,... | collective-permute-start | bytes 1572872 | tf_op jit(solution)/shard_map/ppermute | solution.py:424
  30.6 15.1 %collective-permute-start.7 = (bf16[256,1024]{1,0:T(8,128)(2,1)S(1)}, bf16[256,1024]{1,0:T(8,128)(2,1)}, u32[]{:S(2)}, u32[]{:S(2)}) collective-permute-start(bf16[256,1024]{1,0:T(8,128)(2,1)S(1)} %collective-permute-done.2.second_mine), channel_id=1, source_target_pairs={{0,2},{1,3},{2,0},{3,1},{4,6},{5,7},{6,4},{7,5},{8,10},{9,11},{10,... | collective-permute-start | bytes 1572872 | tf_op jit(solution)/shard_map/ppermute | solution.py:424
  31.1 14.6 %collective-permute-start.3 = (bf16[256,512]{1,0:T(8,128)(2,1)}, bf16[256,512]{1,0:T(8,128)(2,1)}, u32[]{:S(2)}, u32[]{:S(2)}) collective-permute-start(bf16[256,512]{1,0:T(8,128)(2,1)} %get-tuple-element.41.refs_4_), channel_id=1, source_target_pairs={{0,16},{16,24},{24,8},{8,0},{1,17},{17,25},{25,9},{9,1},{2,18},{18... | collective-permute-start | bytes 786440 | tf_op jit(solution)/shard_map/ppermute | solution.py:436
  34.6 22.3 %copy-start.2 = (bf16[1024,256]{1,0:T(8,128)(2,1)S(1)}, bf16[1024,256]{1,0:T(8,128)(2,1)}, u32[]{:S(2)}) copy-start(bf16[1024,256]{1,0:T(8,128)(2,1)} %shard_map.148.refs_0_) | copy-start | bytes 1572868
  34.6 34.9 %collective-permute-start.11 = (bf16[1024,256]{1,0:T(8,128)(2,1)}, bf16[1024,256]{1,0:T(8,128)(2,1)S(1)}, u32[]{:S(2)}, u32[]{:S(2)}) collective-permute-start(bf16[1024,256]{1,0:T(8,128)(2,1)} %shard_map.148.refs_0_), channel_id=1, source_target_pairs={{0,4},{2,6},{4,0},{6,2},{1,5},{3,7},{5,1},{7,3},{8,12},{10,14},{12... | collective-permute-start | bytes 1572872 | tf_op jit(solution)/shard_map/ppermute | solution.py:446
  52.9 16.6 %collective-permute-start.8 = (bf16[256,1024]{1,0:T(8,128)(2,1)}, bf16[256,1024]{1,0:T(8,128)(2,1)S(1)}, u32[]{:S(2)}, u32[]{:S(2)}) collective-permute-start(bf16[256,1024]{1,0:T(8,128)(2,1)} %get-tuple-element.49), channel_id=1, source_target_pairs={{0,1},{1,0},{2,3},{3,2},{4,5},{5,4},{6,7},{7,6},{8,9},{9,8},{10,11... | collective-permute-start | bytes 1572872 | tf_op jit(solution)/shard_map/ppermute | solution.py:357
  55.8 9.4 %collective-permute-start.5 = (bf16[256,512]{1,0:T(8,128)(2,1)}, bf16[256,512]{1,0:T(8,128)(2,1)S(1)}, u32[]{:S(2)}, u32[]{:S(2)}) collective-permute-start(bf16[256,512]{1,0:T(8,128)(2,1)} %get-tuple-element.43.refs_4_), channel_id=1, source_target_pairs={{0,16},{16,24},{24,8},{8,0},{1,17},{17,25},{25,9},{9,1},{2,18},{18... | collective-permute-start | bytes 786440 | tf_op jit(solution)/shard_map/ppermute | solution.py:436
  55.8 13.7 %collective-permute-start.4 = (bf16[256,512]{1,0:T(8,128)(2,1)}, bf16[256,512]{1,0:T(8,128)(2,1)}, u32[]{:S(2)}, u32[]{:S(2)}) collective-permute-start(bf16[256,512]{1,0:T(8,128)(2,1)} %collective-permute-done.3.refs_5_), channel_id=1, source_target_pairs={{0,16},{16,24},{24,8},{8,0},{1,17},{17,25},{25,9},{9,1},{2,18},{18... | collective-permute-start | bytes 786440 | tf_op jit(solution)/shard_map/ppermute | solution.py:436
  56.8 32.8 %collective-permute-start.10 = (bf16[1024,256]{1,0:T(8,128)(2,1)S(1)}, bf16[1024,256]{1,0:T(8,128)(2,1)S(1)}, u32[]{:S(2)}, u32[]{:S(2)}) collective-permute-start(bf16[1024,256]{1,0:T(8,128)(2,1)S(1)} %copy-done.2), channel_id=1, source_target_pairs={{0,2},{2,0},{4,6},{6,4},{1,3},{3,1},{5,7},{7,5},{8,10},{10,8},{12,... | collective-permute-start | bytes 1572872 | tf_op jit(solution)/shard_map/ppermute | solution.py:446
  65.3 51.0 %copy-start.12 = (bf16[256,512]{1,0:T(8,128)(2,1)}, bf16[256,512]{1,0:T(8,128)(2,1)S(1)}, u32[]{:S(2)}) copy-start(bf16[256,512]{1,0:T(8,128)(2,1)S(1)} %collective-permute-done.5.refs_5_) | copy-start | bytes 786436
  69.5 24.7 %copy-start.7 = (bf16[1024,256]{1,0:T(8,128)(2,1)}, bf16[1024,256]{1,0:T(8,128)(2,1)S(1)}, u32[]{:S(2)}) copy-start(bf16[1024,256]{1,0:T(8,128)(2,1)S(1)} %collective-permute-done.11.refs_2_) | copy-start | bytes 1572868
  69.5 24.7 %collective-permute-start.12 = (bf16[1024,256]{1,0:T(8,128)(2,1)S(1)}, bf16[1024,256]{1,0:T(8,128)(2,1)}, u32[]{:S(2)}, u32[]{:S(2)}) collective-permute-start(bf16[1024,256]{1,0:T(8,128)(2,1)S(1)} %collective-permute-done.11.refs_2_), channel_id=1, source_target_pairs={{0,2},{2,0},{4,6},{6,4},{1,3},{3,1},{5,7},{7,5},{8,10},{10,8},{12,... | collective-permute-start | bytes 1572872 | tf_op jit(solution)/shard_map/ppermute | solution.py:446
  78.5 5.9 %collective-permute-start.15 = (bf16[64,1024]{1,0:T(8,128)(2,1)S(1)}, bf16[64,1024]{1,0:T(8,128)(2,1)S(1)}, u32[]{:S(2)}, u32[]{:S(2)}) collective-permute-start(bf16[64,1024]{1,0:T(8,128)(2,1)S(1)} %dynamic-slice_convert_fusion), channel_id=1, source_target_pairs={{0,1},{1,0},{2,3},{3,2},{4,5},{5,4},{6,7},{7,6},{8,9},{9,8},{10,11... | collective-permute-start | bytes 393224 | tf_op jit(solution)/shard_map/ppermute | solution.py:357
  79.4 9.1 %collective-permute-start.14 = (bf16[256,512]{1,0:T(8,128)(2,1)S(1)}, bf16[256,512]{1,0:T(8,128)(2,1)S(1)}, u32[]{:S(2)}, u32[]{:S(2)}) collective-permute-start(bf16[256,512]{1,0:T(8,128)(2,1)S(1)} %collective-permute-done.5.refs_5_), channel_id=1, source_target_pairs={{0,16},{16,24},{24,8},{8,0},{1,17},{17,25},{25,9},{9,1},{2,18},{18... | collective-permute-start | bytes 786440 | tf_op jit(solution)/shard_map/ppermute | solution.py:436
  81.3 12.9 %collective-permute-start.13 = (bf16[256,512]{1,0:T(8,128)(2,1)}, bf16[256,512]{1,0:T(8,128)(2,1)S(1)}, u32[]{:S(2)}, u32[]{:S(2)}) collective-permute-start(bf16[256,512]{1,0:T(8,128)(2,1)} %collective-permute-done.4.refs_6_), channel_id=1, source_target_pairs={{0,16},{16,24},{24,8},{8,0},{1,17},{17,25},{25,9},{9,1},{2,18},{18... | collective-permute-start | bytes 786440 | tf_op jit(solution)/shard_map/ppermute | solution.py:436
  88.6 27.7 %copy-start.13 = (bf16[256,512]{1,0:T(8,128)(2,1)}, bf16[256,512]{1,0:T(8,128)(2,1)S(1)}, u32[]{:S(2)}) copy-start(bf16[256,512]{1,0:T(8,128)(2,1)S(1)} %collective-permute-done.14.refs_6_) | copy-start | bytes 786436
  88.6 11.6 %collective-permute-start.16 = (bf16[64,1024]{1,0:T(8,128)(2,1)S(1)}, bf16[64,1024]{1,0:T(8,128)(2,1)S(1)}, u32[]{:S(2)}, u32[]{:S(2)}) collective-permute-start(bf16[64,1024]{1,0:T(8,128)(2,1)S(1)} %convert_add_fusion.1), channel_id=1, source_target_pairs={{0,8},{8,0},{16,24},{24,16},{1,9},{9,1},{17,25},{25,17},{2,10},{10... | collective-permute-start | bytes 393224 | tf_op jit(solution)/shard_map/ppermute | solution.py:357
  89.6 25.3 %copy-start.6 = (bf16[256,1024]{1,0:T(8,128)(2,1)S(1)}, bf16[256,1024]{1,0:T(8,128)(2,1)}, u32[]{:S(2)}) copy-start(bf16[256,1024]{1,0:T(8,128)(2,1)} %get-tuple-element.52.refs_2_) | copy-start | bytes 1572868
  89.6 4.6 %copy-start.8 = (bf16[1024,256]{1,0:T(8,128)(2,1)}, bf16[1024,256]{1,0:T(8,128)(2,1)S(1)}, u32[]{:S(2)}) copy-start(bf16[1024,256]{1,0:T(8,128)(2,1)S(1)} %collective-permute-done.10.refs_1_) | copy-start | bytes 1572868
  100.2 13.3 %collective-permute-start.19 = (bf16[64,1024]{1,0:T(8,128)(2,1)S(1)}, bf16[64,1024]{1,0:T(8,128)(2,1)S(1)}, u32[]{:S(2)}, u32[]{:S(2)}) collective-permute-start(bf16[64,1024]{1,0:T(8,128)(2,1)S(1)} %convert_add_fusion), channel_id=1, source_target_pairs={{0,16},{8,24},{16,0},{24,8},{1,17},{9,25},{17,1},{25,9},{2,18},{10... | collective-permute-start | bytes 393224 | tf_op jit(solution)/shard_map/ppermute | solution.py:357
  102.4 13.9 %collective-permute-start.21 = (bf16[256,512]{1,0:T(8,128)(2,1)S(1)}, bf16[256,512]{1,0:T(8,128)(2,1)S(1)}, u32[]{:S(2)}, u32[]{:S(2)}) collective-permute-start(bf16[256,512]{1,0:T(8,128)(2,1)S(1)} %collective-permute-done.14.refs_6_), channel_id=1, source_target_pairs={{0,16},{16,24},{24,8},{8,0},{1,17},{17,25},{25,9},{9,1},{2,18},{18... | collective-permute-start | bytes 786440 | tf_op jit(solution)/shard_map/ppermute | solution.py:436
  103.2 21.6 %collective-permute-start.17 = (bf16[512,512]{1,0:T(8,128)(2,1)}, bf16[512,512]{1,0:T(8,128)(2,1)S(1)}, u32[]{:S(2)}, u32[]{:S(2)}) collective-permute-start(bf16[512,512]{1,0:T(8,128)(2,1)} %get-tuple-element.58), channel_id=1, source_target_pairs={{0,1},{1,0},{2,3},{3,2},{4,5},{5,4},{6,7},{7,6},{8,9},{9,8},{10,11... | collective-permute-start | bytes 1572872 | tf_op jit(solution)/shard_map/ppermute | solution.py:357
  113.6 9.5 %collective-permute-start.20 = (bf16[64,1024]{1,0:T(8,128)(2,1)S(1)}, bf16[64,1024]{1,0:T(8,128)(2,1)S(1)}, u32[]{:S(2)}, u32[]{:S(2)}) collective-permute-start(bf16[64,1024]{1,0:T(8,128)(2,1)S(1)} %add_convert_fusion), channel_id=1, source_target_pairs={{0,1},{1,0},{2,3},{3,2},{4,5},{5,4},{6,7},{7,6},{8,9},{9,8},{10,11... | collective-permute-start | bytes 393224 | tf_op jit(solution)/shard_map/ppermute | solution.py:357
  115.0 9.8 %collective-permute-start.18 = (bf16[128,1024]{1,0:T(8,128)(2,1)S(1)}, bf16[128,1024]{1,0:T(8,128)(2,1)S(1)}, u32[]{:S(2)}, u32[]{:S(2)}) collective-permute-start(bf16[128,1024]{1,0:T(8,128)(2,1)S(1)} %slice.16), channel_id=1, source_target_pairs={{8,0},{16,8},{24,16},{9,1},{17,9},{25,17},{10,2},{18,10},{26,18},{... | collective-permute-start | bytes 786440 | tf_op jit(solution)/shard_map/ppermute | solution.py:497
  122.3 13.7 %collective-permute-start.22 = (bf16[512,512]{1,0:T(8,128)(2,1)}, bf16[512,512]{1,0:T(8,128)(2,1)S(1)}, u32[]{:S(2)}, u32[]{:S(2)}) collective-permute-start(bf16[512,512]{1,0:T(8,128)(2,1)} %get-tuple-element.67), channel_id=1, source_target_pairs={{0,1},{1,0},{2,3},{3,2},{4,5},{5,4},{6,7},{7,6},{8,9},{9,8},{10,11... | collective-permute-start | bytes 1572872 | tf_op jit(solution)/shard_map/ppermute | solution.py:357
  124.8 8.4 %copy-start = (f32[512,512]{1,0:T(8,128)S(1)}, f32[512,512]{1,0:T(8,128)}, u32[]{:S(2)}) copy-start(f32[512,512]{1,0:T(8,128)} %get-tuple-element.63) | copy-start | bytes 3145732
  (8 other events, 8.2 us)

commit v9 on v8

--- a/solution.py
+++ b/solution.py
@@ -11,7 +11,8 @@
 from jax.sharding import PartitionSpec as P
 
 f32, bf16 = jnp.float32, jnp.bfloat16
-lanes = 256
+lanes = 512
+turn = 256
 vmem_bytes = 58 * 1024 * 1024
 
 
@@ -25,7 +26,7 @@
 def split_table(table):
     high = table.astype(ml_dtypes.bfloat16)
     low = (table - high.astype(np.float64)).astype(ml_dtypes.bfloat16)
-    return np.stack([high, low])
+    return np.concatenate([high, low])
 
 
 def split_rows(rows):
@@ -41,16 +42,20 @@
     return lax.dot_general(left, right, (((1,), (1,)), ((), ())), preferred_element_type=f32)
 
 
+def add_halves(both):
+    half = both.shape[0] // 2
+    return both[:half] + both[half:]
+
+
 def forward_transform(table, rows, start):
-    columns = pl.ds(start, rows.shape[0])
-    return dot(table[0, :, columns], rows) + dot(table[1, :, columns], rows)
+    return add_halves(dot(table[:, pl.ds(start, rows.shape[0])], rows))
 
 
 def inverse_transform(table, spectrum, start, count):
     high, low = split_rows(spectrum)
-    rows = pl.ds(start, count)
-    upper = table[0, rows]
-    return dot(upper, high) + dot(upper, low) + dot(table[1, rows], high)
+    upper = table[pl.ds(start, count)]
+    lower = table[pl.ds(table.shape[0] // 2 + start, count)]
+    return dot(upper, high) + dot(upper, low) + dot(lower, high)
 
 
 def spectrum_product(left, right, conjugate_right):
@@ -72,7 +77,7 @@
 
 def filter_spectrum(scale, table, taps_ref, skip_ref):
     taps = taps_ref.shape[1]
-    filt = dot_nt(table[0, :, :taps], taps_ref[...]) + dot_nt(table[1, :, :taps], taps_ref[...])
+    filt = add_halves(dot_nt(table[:, :taps], taps_ref[...]))
     half = filt.shape[0] // 2
     return jnp.concatenate([(filt[:half] + skip_ref[...]) * scale, filt[half:] * scale], axis=0)
 
@@ -198,7 +203,7 @@
 
 def estimate(flops, arrays):
     moved = sum(a.size * jnp.dtype(a.dtype).itemsize for a in arrays)
-    return pl.CostEstimate(flops=flops, bytes_accessed=moved, transcendentals=0)
+    return pl.CostEstimate(flops=flops // 64, bytes_accessed=moved // 64, transcendentals=0)
 
 
 def by_channel(body, tables, args, outs, channels, flops):
@@ -207,7 +212,7 @@
     n_tables, n_args, n_outs = len(tables), len(args), len(outs)
 
     def part(ref, i, count):
-        start = pl.multiple_of(i * lanes, lanes)
+        start = i * lanes
         if ref.shape[1] == count * lanes:
             return ref.at[:, pl.ds(start, lanes)]
         return ref.at[pl.ds(start, lanes), :]
@@ -240,14 +245,10 @@
         for k in range(n_args):
             arg_copy(k).wait()
 
-        for n in range(max(len(group) for group in groups)):
-            per = steps // max(len(group) for group in groups)
-
-            @pl.loop(n * per, (n + 1) * per)
-            def _(i):
-                body(*table_held, *[part(ref, i, steps) for ref in arg_held], *[held.at[i] for held in out_held])
-                for k in range(n_outs):
-                    out_copy(k, min(n, len(groups[k]) - 1), i).start()
+        for i in range(steps):
+            body(*table_held, *[part(ref, i, steps) for ref in arg_held], *[held.at[i] for held in out_held])
+            for k in range(n_outs):
+                out_copy(k, i * len(groups[k]) // steps, i).start()
 
         for i in range(steps):
             for k in range(n_outs):
@@ -329,8 +330,8 @@
     copy = pltpu.make_async_copy(rows_in, rows, sems.at[0])
     copy.start()
     copy.wait()
-    for i in range(rows.shape[1] // lanes):
-        turned[pl.ds(i * lanes, lanes), :] = rows[:, pl.ds(i * lanes, lanes)].T
+    for i in range(rows.shape[1] // turn):
+        turned[pl.ds(i * turn, turn), :] = rows[:, pl.ds(i * turn, turn)].T
     copy = pltpu.make_async_copy(turned, out, sems.at[1])
     copy.start()
     copy.wait()
@@ -402,11 +403,28 @@
     square = n_seq == n_tp == 4 and subs == 2
     if square:
 
-        def holder(s):
-            return s % 2 * subs + s // 2
-
-        route = [(s * n_tp + t, t * n_tp + holder(s)) for s in range(n_seq) for t in range(n_tp)]
-        moved = lax.ppermute(cot, ("seq", "tp"), route)
+        def holder(s, block):
+            return (s + block) % 2 * subs + s // 2
+
+        crossed = {0: (1, 2), 1: (0, 3)}
+        route = [
+            (s * n_tp + t, s * n_tp + sum(crossed[s % 2]) - t)
+            for s in range(n_seq)
+            for t in crossed[s % 2]
+        ]
+        swapped = lax.ppermute(cot, ("seq", "tp"), route)
+        moves_now = sum(
+            jnp.logical_and(lax.axis_index("seq") % 2 == parity, me_tp == t)
+            for parity in crossed
+            for t in crossed[parity]
+        )
+        held = jnp.where(moves_now > 0, swapped, cot)
+        route = []
+        for s in range(n_seq):
+            for t in range(n_tp):
+                block = sum(crossed[s % 2]) - t if t in crossed[s % 2] else t
+                route.append((s * n_tp + t, block * n_tp + holder(s, block)))
+        moved = lax.ppermute(after(held, prior), ("seq", "tp"), route)
     else:
         moved = cot
 
@@ -418,7 +436,7 @@
         channels,
         unit * (4 * taps + 5 * length),
     )
-    gated[0], gated[1], *rounds = lax.optimization_barrier((*gated, *rounds))
+    gated[0], gated[1], moved, *rounds = lax.optimization_barrier((*gated, moved, *rounds))
 
     route = [(tp_dp(h, c, d), tp_dp(h, (c + 1) % subs, d)) for h, c, d in places]
     theirs = [lax.ppermute(r, ("tp", "dp"), route) for r in rounds]
@@ -436,7 +454,8 @@
             pieces.append(lax.ppermute(pieces[-1], "seq", ring))
 
         ring_step(halves[0])
-        halves[0][1], place = lax.optimization_barrier((halves[0][1], place))
+        moved = transposed(moved)
+        halves[0][1], moved, place = lax.optimization_barrier((halves[0][1], moved, place))
         ring_step(halves[0])
         ring_step(halves[1])
     other_sent, own_part = project(place, firsts, seconds, out_weight)
@@ -444,14 +463,13 @@
 
     if square:
         sent_by = lambda value, flip: lax.ppermute(value, "tp", [(t, t ^ flip) for t in range(n_tp)])
-        moved = transposed(moved)
         across = sent_by(moved, subs)
         cot_pieces = [moved, sent_by(moved, 1), across, sent_by(across, 1)]
         table = np.zeros((n_seq, n_tp, n_tp), np.int32)
         for k, s in enumerate(order):
             for r in range(n_seq):
                 for t in range(n_tp):
-                    table[s, t, t ^ holder(order[k - r])] = r
+                    table[s, t, t ^ holder(order[k - r], s)] = r
         sources = jnp.asarray(table)[lax.axis_index("seq"), me_tp]
         halves[0][2], halves[1][1], own_part = lax.optimization_barrier(
             (halves[0][2], halves[1][1], own_part)
@@ -461,13 +479,6 @@
 
         weight_place = jnp.concatenate([sources, me_dp[None].astype(jnp.int32)])
 
-        def weight_all():
-            second_sent, second_own = weight_sum(weight_place, cot_pieces, halves[1], rows)
-            parts = [(first_own, first_received), (second_own, swap_pairs(second_sent, "dp", 1))]
-            return jnp.concatenate(
-                [(mine + theirs.astype(f32)) * norm_factor for mine, theirs in parts], axis=1
-            )
-
     else:
         full = lax.all_gather(cot, "tp", axis=1, tiled=True)
         cot_all = lax.all_to_all(full, "seq", 1, 0, tiled=True)
@@ -480,11 +491,7 @@
             )
 
         def weight_one(piece):
-            sent = swap_pairs(part(1 - me_dp, piece).astype(bf16), "dp", 1)
-            return (part(me_dp, piece) + sent.astype(f32)) * norm_factor
-
-        def weight_all():
-            return jnp.concatenate([weight_one(gated_all[0]), weight_one(gated_all[1])], axis=1)
+            return part(me_dp, piece), swap_pairs(part(1 - me_dp, piece).astype(bf16), "dp", 1)
 
     grad_query, signal, lags = by_channel(
         lag_kernel,
@@ -496,39 +503,56 @@
     )
     later = lax.ppermute(signal[:taps], "seq", [(i + 1, i) for i in range(n_seq - 1)])
 
+    def run_back(later):
+        return by_channel(
+            functools.partial(back_kernel, scale),
+            tables,
+            [signal, later, filter_taps, skip_gain[None], key_rows, value_rows],
+            [[rows16], [rows16]],
+            channels,
+            256 * unit * (4 * taps + 5 * length),
+        )
+
     share = taps // n_dp
-    lag_sum = lax.dynamic_slice_in_dim(lags, me_dp * share, share, axis=0) + swap_pairs(
+    received = swap_pairs(
         lax.dynamic_slice_in_dim(lags, (1 - me_dp) * share, share, axis=0).astype(bf16), "dp", 1
-    ).astype(f32)
-    if square:
-        halves[1][2], lag_sum = lax.optimization_barrier((halves[1][2], lag_sum))
+    )
+    if square:
+        halves[1][2], weight_place = lax.optimization_barrier((halves[1][2], weight_place))
         ring_step(halves[1])
         first_sent, first_own = weight_sum(weight_place, cot_pieces, halves[0], rows)
+        first_received = swap_pairs(first_sent, "dp", 1)
+        received, first_own = lax.optimization_barrier((received, first_own))
+    lag_sum = lax.dynamic_slice_in_dim(lags, me_dp * share, share, axis=0) + received.astype(f32)
     distance = 1
     while distance < n_seq:
         rounded = lag_sum.astype(bf16)
-        lag_sum = rounded.astype(f32) + swap_pairs(rounded, "seq", distance).astype(f32)
+        received = swap_pairs(rounded, "seq", distance)
         if square and distance == 1:
-            first_sent, lag_sum = lax.optimization_barrier((first_sent, lag_sum))
+            weight_place = after(weight_place, first_own)
+            second_sent, second_own = weight_sum(weight_place, cot_pieces, halves[1], rows)
+            second_received = swap_pairs(second_sent, "dp", 1)
+            received, second_own = lax.optimization_barrier((received, second_own))
+        lag_sum = rounded.astype(f32) + received.astype(f32)
         distance *= 2
+    if square:
+        first_received, lag_sum = lax.optimization_barrier((first_received, lag_sum))
     mine = lag_sum.astype(bf16)
     theirs = swap_pairs(mine, "dp", 1)
+    if square:
+        later = after(later, second_own)
+    grad_key, grad_value = run_back(later)
     first = me_dp == 0
     lag_sum = jnp.concatenate([jnp.where(first, mine, theirs), jnp.where(first, theirs, mine)], axis=0)
     grad_filter = lag_sum.astype(f32).T * (norm_factor * scale)
 
     if square:
-        first_received = swap_pairs(first_sent, "dp", 1)
-        first_received, later = lax.optimization_barrier((first_received, later))
-    grad_key, grad_value = by_channel(
-        functools.partial(back_kernel, scale),
-        tables,
-        [signal, later, filter_taps, skip_gain[None], key_rows, value_rows],
-        [[rows16], [rows16]],
-        channels,
-        unit * (4 * taps + 5 * length),
-    )
-    grad_weight = weight_all()
+        parts = [(first_own, first_received), (second_own, second_received)]
+    else:
+        parts = [weight_one(half) for half in gated_all]
+    grad_weight = jnp.concatenate(
+        [(mine + theirs.astype(f32)) * norm_factor for mine, theirs in parts], axis=1
+    )
     return (
         grad_query[None],
         grad_key[None],

time: 140 us -> 123 us (0.88); the launches traced: 138 us -> 123 us
  waiting for transfers between devices: 44.2 us -> 26 us
  starting transfers between devices: 37.3 us -> 46.7 us
  Pallas kernels: 41.5 us -> 34.7 us
    ppermute x2, starting transfers between devices: 0.51 us -> 12.2 us  [per_device(): theirs = [lax.ppermute(r, ('tp', 'dp'), route) for r in rounds]]
    ppermute x3, starting transfers between devices: 11.1 us -> 0.73 us  [per_device(): lax.ppermute(value, 'tp', [(t, t ^ flip) for t in range(n_tp)])]
    ppermute x6, starting transfers between devices: 3.04 us -> 10 us  [ring_step(): pieces.append(lax.ppermute(pieces[-1], 'seq', ring))]
    ppermute x7, waiting for transfers between devices: 15 us -> 8.32 us  [swap_pairs(): return lax.ppermute(value, axis, [(i, i ^ distance) for i in range(count)])]
    pallas_call x3, Pallas kernels: 22.5 us -> 16.7 us  [by_channel(): pl.pallas_call(kernel, in_specs=[pl.BlockSpec(memory_space=pl.ANY)] * (n_...]
    ppermute x6, waiting for transfers between devices: 20.4 us -> 14.9 us  [ring_step(): pieces.append(lax.ppermute(pieces[-1], 'seq', ring))]
    ppermute x2, waiting for transfers between devices: 4.82 us -> 0.01 us  [per_device(): rounds.append(lax.ppermute(cot, ('tp', 'dp'), route))]
    ppermute x1, starting transfers between devices: 3.48 us -> 5.63 us  [per_device(): prior = lax.ppermute(tail, 'seq', [(i, i + 1) for i in range(n_seq - 1)])]
  transfers between devices with their start and end apart: 23 -> 24, of which waited for: 9 -> 7; matrix products, arithmetic and copies ran while one was open for 4% -> 6% of each run, Pallas kernels for 30% -> 28%
where the time goes in v9:
time: 123 us
  starting transfers between devices  46.7 us (38%)
  Pallas kernels  34.7 us (28%)
  waiting for transfers between devices  26 us (21%)
  local copies, waits for them, and re-layouts  8.63 us (7%)
  other arithmetic  5.35 us (4%)
    pallas_call x3, Pallas kernels, by_channel(): pl.pallas_call(kernel, in_specs=[pl.BlockSpec(memory_space=pl.ANY)] * (n_...  16.7 us
    pallas_call x3, Pallas kernels, local_call(): pl.pallas_call(kernel, in_specs=[pl.BlockSpec(memory_space=pltpu.SMEM)] +...  16 us
    ppermute x6, waiting for transfers between devices, ring_step(): pieces.append(lax.ppermute(pieces[-1], 'seq', ring))  14.9 us
    ppermute x2, starting transfers between devices, per_device(): theirs = [lax.ppermute(r, ('tp', 'dp'), route) for r in rounds]  12.2 us
    ppermute x6, starting transfers between devices, ring_step(): pieces.append(lax.ppermute(pieces[-1], 'seq', ring))  10 us
    ppermute x7, starting transfers between devices, swap_pairs(): return lax.ppermute(value, axis, [(i, i ^ distance) for i in range(count)])  9.1 us
    ppermute x7, waiting for transfers between devices, swap_pairs(): return lax.ppermute(value, axis, [(i, i ^ distance) for i in range(count)])  8.32 us
    ppermute x2, starting transfers between devices, per_device(): rounds.append(lax.ppermute(cot, ('tp', 'dp'), route))  6.4 us
  transfers between devices with their start and end apart: 24, of which 7 were waited for; matrix products, arithmetic and copies ran while one was open for 6% of the time, Pallas kernels for 28%

profile of v9, /device:TPU:0, one launch (start us, length us, event | category | flops | bytes accessed | tf_op | source)
XLA Modules:
  0.0 122.5 jit_solution(6961757315333331808)
XLA Ops:
  0.6 1.1 fusion
  2.4 1.7 %collective-permute-start.3 = (bf16[256,1024]{1,0:T(8,128)(2,1)}, bf16[256,1024]{1,0:T(8,128)(2,1)S(1)}, u32[]{:S(2)}, u32[]{:S(2)}) collective-permute-start(bf16[256,1024]{1,0:T(8,128)(2,1)} %bitcast.28), channel_id=1, source_target_pairs={{0,0},{1,4},{2,2},{3,6},{4,1},{5,5},{6,3},{7,7},{8,8},{9,12},{10,1... | collective-permute-start | bytes 1572872 | tf_op jit(solution)/shard_map/ppermute | solution.py:402
  4.1 4.7 %collective-permute-start.4 = (bf16[256,1024]{1,0:T(8,128)(2,1)}, bf16[256,1024]{1,0:T(8,128)(2,1)S(1)}, u32[]{:S(2)}, u32[]{:S(2)}) collective-permute-start(bf16[256,1024]{1,0:T(8,128)(2,1)} %bitcast.29), channel_id=1, source_target_pairs={{0,4},{1,0},{2,6},{3,2},{4,5},{5,1},{6,7},{7,3},{8,12},{9,8},{10,1... | collective-permute-start | bytes 1572872 | tf_op jit(solution)/shard_map/ppermute | solution.py:402
  8.8 5.6 %collective-permute-start = (bf16[128,1024]{1,0:T(8,128)(2,1)S(1)}, bf16[128,1024]{1,0:T(8,128)(2,1)S(1)}, u32[]{:S(2)}, u32[]{:S(2)}) collective-permute-start(bf16[128,1024]{1,0:T(8,128)(2,1)S(1)} %fusion), channel_id=1, source_target_pairs={{0,8},{8,16},{16,24},{1,9},{9,17},{17,25},{2,10},{10,18},{18,26},{... | collective-permute-start | bytes 786440 | tf_op jit(solution)/shard_map/ppermute | solution.py:393
  14.5 1.1 broadcast_select_fusion
  15.6 2.7 %collective-permute-done.refs_2_.refs_6_ = bf16[128,1024]{1,0:T(8,128)(2,1)S(1)} collective-permute-done((bf16[128,1024]{1,0:T(8,128)(2,1)S(1)}, bf16[128,1024]{1,0:T(8,128)(2,1)S(1)}, u32[]{:S(2)}, u32[]{:S(2)}) %collective-permute-start) | collective-permute-done | bytes 262176 | tf_op jit(solution)/shard_map/ppermute | solution.py:393
  19.1 5.5 %shard_map.145 = (f32[256,1024]{1,0:T(8,128)}, bf16[256,512]{1,0:T(8,128)(2,1)}, bf16[256,512]{1,0:T(8,128)(2,1)}) custom-call(bf16[768,384]{1,0:T(8,128)(2,1)} %constant.69.clone.refs_0_, bf16[768,384]{1,0:T(8,128)(2,1)} %constant.70.clone.refs_1_, bf16[128,1024]{1,0:T(8,128)(2,1)} %copy-done.4, bf16[256,1024]{1,0:T(8,128)(2,1)} %bitcast.22, ...), custom_call_target="tpu_custom_call" | custom-call | flops 22020096 | bytes 57408 | tf_op jit(solution)/shard_map/pallas_call | solution.py:257
  24.7 12.2 %collective-permute-start.8 = (bf16[256,1024]{1,0:T(8,128)(2,1)S(1)}, bf16[256,1024]{1,0:T(8,128)(2,1)S(1)}, u32[]{:S(2)}, u32[]{:S(2)}) collective-permute-start(bf16[256,1024]{1,0:T(8,128)(2,1)S(1)} %collective-permute-done.3.first_mine), channel_id=1, source_target_pairs={{0,2},{1,3},{2,0},{3,1},{4,6},{5,7},{6,4},{7,5},{8,10},{9,11},{10,... | collective-permute-start | bytes 1572872 | tf_op jit(solution)/shard_map/ppermute | solution.py:442
  37.7 2.1 %shard_map.146.refs_0_ = bf16[1024,256]{1,0:T(8,128)(2,1)} custom-call(bf16[256,1024]{1,0:T(8,128)(2,1)} %copy-done.11), custom_call_target="tpu_custom_call" | custom-call | bytes 16384 | tf_op jit(solution)/shard_map/pallas_call | solution.py:341
  39.8 6.1 %collective-permute-done.5.refs_5_ = bf16[256,512]{1,0:T(8,128)(2,1)} collective-permute-done((bf16[256,512]{1,0:T(8,128)(2,1)}, bf16[256,512]{1,0:T(8,128)(2,1)}, u32[]{:S(2)}, u32[]{:S(2)}) %collective-permute-start.5) | collective-permute-done | bytes 262176 | tf_op jit(solution)/shard_map/ppermute | solution.py:454
  47.8 6.4 %shard_map.147 = (bf16[256,1024]{1,0:T(8,128)(2,1)}, f32[256,1024]{1,0:T(8,128)}) custom-call(s32[3]{0:T(128)} %pad_add_fusion.place_ref, bf16[256,1024]{1,0:T(8,128)(2,1)} %copy-done.7, bf16[256,1024]{1,0:T(8,128)(2,1)} %copy-done.8, bf16[256,1024]{1,0:T(8,128)(2,1)} %copy-done.9, bf16[256,1024]{1,0:T(8,128)(2,1)} %copy-done.10, bf16[1024,2048]{1,0:T(8,128)(2,1)} %weight.1), custom_call_target="tpu_custom_call" | custom-call | flops 33554432 | bytes 122880 | tf_op jit(solution)/shard_map/pallas_call | solution.py:276
  54.1 2.1 %collective-permute-start.10 = (bf16[256,1024]{1,0:T(8,128)(2,1)}, bf16[256,1024]{1,0:T(8,128)(2,1)S(1)}, u32[]{:S(2)}, u32[]{:S(2)}) collective-permute-start(bf16[256,1024]{1,0:T(8,128)(2,1)} %get-tuple-element.58), channel_id=1, source_target_pairs={{0,1},{1,0},{2,3},{3,2},{4,5},{5,4},{6,7},{7,6},{8,9},{9,8},{10,11... | collective-permute-start | bytes 1572872 | tf_op jit(solution)/shard_map/ppermute | solution.py:358
  56.2 2.3 %collective-permute-start.7 = (bf16[256,512]{1,0:T(8,128)(2,1)S(1)}, bf16[256,512]{1,0:T(8,128)(2,1)S(1)}, u32[]{:S(2)}, u32[]{:S(2)}) collective-permute-start(bf16[256,512]{1,0:T(8,128)(2,1)S(1)} %copy-done.14), channel_id=1, source_target_pairs={{0,16},{16,24},{24,8},{8,0},{1,17},{17,25},{25,9},{9,1},{2,18},{18... | collective-permute-start | bytes 786440 | tf_op jit(solution)/shard_map/ppermute | solution.py:454
  58.5 2.0 %collective-permute-start.6 = (bf16[256,512]{1,0:T(8,128)(2,1)}, bf16[256,512]{1,0:T(8,128)(2,1)}, u32[]{:S(2)}, u32[]{:S(2)}) collective-permute-start(bf16[256,512]{1,0:T(8,128)(2,1)} %collective-permute-done.5.refs_5_), channel_id=1, source_target_pairs={{0,16},{16,24},{24,8},{8,0},{1,17},{17,25},{25,9},{9,1},{2,18},{18... | collective-permute-start | bytes 786440 | tf_op jit(solution)/shard_map/ppermute | solution.py:454
  61.0 5.0 %collective-permute-done.7.refs_5_ = bf16[256,512]{1,0:T(8,128)(2,1)S(1)} collective-permute-done((bf16[256,512]{1,0:T(8,128)(2,1)S(1)}, bf16[256,512]{1,0:T(8,128)(2,1)S(1)}, u32[]{:S(2)}, u32[]{:S(2)}) %collective-permute-start.7) | collective-permute-done | bytes 262176 | tf_op jit(solution)/shard_map/ppermute | solution.py:454
  65.9 3.9 %collective-permute-done.6.refs_6_ = bf16[256,512]{1,0:T(8,128)(2,1)} collective-permute-done((bf16[256,512]{1,0:T(8,128)(2,1)}, bf16[256,512]{1,0:T(8,128)(2,1)}, u32[]{:S(2)}, u32[]{:S(2)}) %collective-permute-start.6) | collective-permute-done | bytes 262176 | tf_op jit(solution)/shard_map/ppermute | solution.py:454
  69.8 2.4 %collective-permute-start.13 = (bf16[256,512]{1,0:T(8,128)(2,1)S(1)}, bf16[256,512]{1,0:T(8,128)(2,1)S(1)}, u32[]{:S(2)}, u32[]{:S(2)}) collective-permute-start(bf16[256,512]{1,0:T(8,128)(2,1)S(1)} %collective-permute-done.7.refs_5_), channel_id=1, source_target_pairs={{0,16},{16,24},{24,8},{8,0},{1,17},{17,25},{25,9},{9,1},{2,18},{18... | collective-permute-start | bytes 786440 | tf_op jit(solution)/shard_map/ppermute | solution.py:454
  73.8 5.7 %shard_map.148 = (bf16[256,1024]{1,0:T(8,128)(2,1)}, bf16[256,1024]{1,0:T(8,128)(2,1)}, f32[128,1024]{1,0:T(8,128)}) custom-call(bf16[768,384]{1,0:T(8,128)(2,1)} %constant.69.clone.refs_0_, bf16[768,384]{1,0:T(8,128)(2,1)} %constant.70.clone.refs_1_, f32[256,1024]{1,0:T(8,128)} %get-tuple-element.57.refs_2_, bf16[256,1024]{1,0:T(8,128)(2,1)} %copy-done.12, ...), custom_call_target="tpu_custom_call" | custom-call | flops 20447232 | bytes 94208 | tf_op jit(solution)/shard_map/pallas_call | solution.py:257
  79.5 1.7 %dynamic-slice_convert_fusion = bf16[64,1024]{1,0:T(8,128)(2,1)} fusion(f32[128,1024]{1,0:T(8,128)} %get-tuple-element.62, s32[]{:T(128)S(6)} %select_n.64), kind=kLoop, calls=%fused_computation.10 | loop fusion | bytes 262148 | tf_op jit(solution)/shard_map/convert_element_type | solution.py:518
  82.8 2.4 %collective-permute-start.19 = (bf16[256,512]{1,0:T(8,128)(2,1)S(1)}, bf16[256,512]{1,0:T(8,128)(2,1)}, u32[]{:S(2)}, u32[]{:S(2)}) collective-permute-start(bf16[256,512]{1,0:T(8,128)(2,1)S(1)} %collective-permute-done.13.refs_6_), channel_id=1, source_target_pairs={{0,16},{16,24},{24,8},{8,0},{1,17},{17,25},{25,9},{9,1},{2,18},{18... | collective-permute-start | bytes 786440 | tf_op jit(solution)/shard_map/ppermute | solution.py:454
  85.2 1.0 slice.16
  86.2 1.3 %collective-permute-start.11 = (bf16[128,1024]{1,0:T(8,128)(2,1)S(1)}, bf16[128,1024]{1,0:T(8,128)(2,1)S(1)}, u32[]{:S(2)}, u32[]{:S(2)}) collective-permute-start(bf16[128,1024]{1,0:T(8,128)(2,1)S(1)} %slice.16), channel_id=1, source_target_pairs={{8,0},{16,8},{24,16},{9,1},{17,9},{25,17},{10,2},{18,10},{26,18},{... | collective-permute-start | bytes 786440 | tf_op jit(solution)/shard_map/ppermute | solution.py:504
  88.3 4.8 %shard_map.149 = (bf16[512,512]{1,0:T(8,128)(2,1)}, f32[512,512]{1,0:T(8,128)}) custom-call(s32[5]{0:T(128)} %pad_add_fusion.1.place_ref, bf16[1024,256]{1,0:T(8,128)(2,1)} %shard_map.146.refs_0_, bf16[1024,256]{1,0:T(8,128)(2,1)} %copy-done.2, bf16[1024,256]{1,0:T(8,128)(2,1)} %copy-done.1, bf16[1024,256]{1,0:T(8,128)(2,1)} %copy-done.3, ...), custom_call_target="tpu_custom_call" | custom-call | flops 16777216 | bytes 73728 | tf_op jit(solution)/shard_map/pallas_call | solution.py:276
  93.2 2.7 %collective-permute-start.18 = (bf16[64,1024]{1,0:T(8,128)(2,1)S(1)}, bf16[64,1024]{1,0:T(8,128)(2,1)S(1)}, u32[]{:S(2)}, u32[]{:S(2)}) collective-permute-start(bf16[64,1024]{1,0:T(8,128)(2,1)S(1)} %add_convert_fusion.1), channel_id=1, source_target_pairs={{0,8},{8,0},{16,24},{24,16},{1,9},{9,1},{17,25},{25,17},{2,10},{10... | collective-permute-start | bytes 393224 | tf_op jit(solution)/shard_map/ppermute | solution.py:358
  95.9 1.7 %collective-permute-start.20 = (bf16[512,512]{1,0:T(8,128)(2,1)}, bf16[512,512]{1,0:T(8,128)(2,1)S(1)}, u32[]{:S(2)}, u32[]{:S(2)}) collective-permute-start(bf16[512,512]{1,0:T(8,128)(2,1)} %get-tuple-element.77), channel_id=1, source_target_pairs={{0,1},{1,0},{2,3},{3,2},{4,5},{5,4},{6,7},{7,6},{8,9},{9,8},{10,11... | collective-permute-start | bytes 1572872 | tf_op jit(solution)/shard_map/ppermute | solution.py:358
  97.6 4.8 %shard_map.150 = (bf16[512,512]{1,0:T(8,128)(2,1)}, f32[512,512]{1,0:T(8,128)}) custom-call(s32[5]{0:T(128)} %pad_add_fusion.1.place_ref, bf16[1024,256]{1,0:T(8,128)(2,1)} %shard_map.146.refs_0_, bf16[1024,256]{1,0:T(8,128)(2,1)} %copy-done.2, bf16[1024,256]{1,0:T(8,128)(2,1)} %copy-done.1, bf16[1024,256]{1,0:T(8,128)(2,1)} %copy-done.3, ...), custom_call_target="tpu_custom_call" | custom-call | flops 16777216 | bytes 73728 | tf_op jit(solution)/shard_map/pallas_call | solution.py:276
  103.5 5.5 %shard_map.151 = (bf16[256,1024]{1,0:T(8,128)(2,1)}, bf16[256,1024]{1,0:T(8,128)(2,1)}) custom-call(bf16[768,384]{1,0:T(8,128)(2,1)} %constant.69.clone.refs_0_, bf16[768,384]{1,0:T(8,128)(2,1)} %constant.70.clone.refs_1_, bf16[256,1024]{1,0:T(8,128)(2,1)} %get-tuple-element.61.refs_2_, bf16[128,1024]{1,0:T(8,128)(2,1)} %copy-done.17, ...), custom_call_target="tpu_custom_call" | custom-call | flops 5637144576 | bytes 49216 | tf_op jit(solution)/shard_map/pallas_call | solution.py:257
  109.8 1.2 collective-permute-done.20
  111.0 1.7 %collective-permute-start.22 = (bf16[64,1024]{1,0:T(8,128)(2,1)S(1)}, bf16[64,1024]{1,0:T(8,128)(2,1)S(1)}, u32[]{:S(2)}, u32[]{:S(2)}) collective-permute-start(bf16[64,1024]{1,0:T(8,128)(2,1)S(1)} %convert_add_fusion), channel_id=1, source_target_pairs={{0,1},{1,0},{2,3},{3,2},{4,5},{5,4},{6,7},{7,6},{8,9},{9,8},{10,11... | collective-permute-start | bytes 393224 | tf_op jit(solution)/shard_map/ppermute | solution.py:358
  112.9 6.3 %collective-permute-done.23 = bf16[512,512]{1,0:T(8,128)(2,1)S(1)} collective-permute-done((bf16[512,512]{1,0:T(8,128)(2,1)}, bf16[512,512]{1,0:T(8,128)(2,1)S(1)}, u32[]{:S(2)}, u32[]{:S(2)}) %collective-permute-start.23) | collective-permute-done | bytes 524320 | tf_op jit(solution)/shard_map/ppermute | solution.py:358
  119.4 1.5 %pad_maximum_fusion = f32[512,1024]{1,0:T(8,128)} fusion(f32[512,512]{1,0:T(8,128)S(1)} %add_multiply_fusion, f32[512,512]{1,0:T(8,128)S(1)} %add_multiply_fusion.1), kind=kLoop, calls=%fused_computation | loop fusion | flops 524288 | bytes 4194304 | tf_op jit(solution)/shard_map/concatenate | solution.py:553
  120.9 1.0 copy.16
  (76 shorter events, 11.5 us)
Async XLA Ops:
  1.7 12.8 %collective-permute-start.1 = (bf16[256,1024]{1,0:T(8,128)(2,1)}, bf16[256,1024]{1,0:T(8,128)(2,1)S(1)}, u32[]{:S(2)}, u32[]{:S(2)}) collective-permute-start(bf16[256,1024]{1,0:T(8,128)(2,1)} %bitcast.27), channel_id=1, source_target_pairs={{2,4},{4,2},{8,14},{14,8},{18,20},{20,18},{24,30},{30,24},{3,5},{5... | collective-permute-start | bytes 1572872 | tf_op jit(solution)/shard_map/ppermute | solution.py:415
  2.4 22.2 %collective-permute-start.3 = (bf16[256,1024]{1,0:T(8,128)(2,1)}, bf16[256,1024]{1,0:T(8,128)(2,1)S(1)}, u32[]{:S(2)}, u32[]{:S(2)}) collective-permute-start(bf16[256,1024]{1,0:T(8,128)(2,1)} %bitcast.28), channel_id=1, source_target_pairs={{0,0},{1,4},{2,2},{3,6},{4,1},{5,5},{6,3},{7,7},{8,8},{9,12},{10,1... | collective-permute-start | bytes 1572872 | tf_op jit(solution)/shard_map/ppermute | solution.py:402
  4.1 20.5 %collective-permute-start.4 = (bf16[256,1024]{1,0:T(8,128)(2,1)}, bf16[256,1024]{1,0:T(8,128)(2,1)S(1)}, u32[]{:S(2)}, u32[]{:S(2)}) collective-permute-start(bf16[256,1024]{1,0:T(8,128)(2,1)} %bitcast.29), channel_id=1, source_target_pairs={{0,4},{1,0},{2,6},{3,2},{4,5},{5,1},{6,7},{7,3},{8,12},{9,8},{10,1... | collective-permute-start | bytes 1572872 | tf_op jit(solution)/shard_map/ppermute | solution.py:402
  8.8 9.5 %collective-permute-start = (bf16[128,1024]{1,0:T(8,128)(2,1)S(1)}, bf16[128,1024]{1,0:T(8,128)(2,1)S(1)}, u32[]{:S(2)}, u32[]{:S(2)}) collective-permute-start(bf16[128,1024]{1,0:T(8,128)(2,1)S(1)} %fusion), channel_id=1, source_target_pairs={{0,8},{8,16},{16,24},{1,9},{9,17},{17,25},{2,10},{10,18},{18,26},{... | collective-permute-start | bytes 786440 | tf_op jit(solution)/shard_map/ppermute | solution.py:393
  18.4 6.3 %collective-permute-start.2 = (bf16[256,1024]{1,0:T(8,128)(2,1)S(1)}, bf16[256,1024]{1,0:T(8,128)(2,1)S(1)}, u32[]{:S(2)}, u32[]{:S(2)}) collective-permute-start(bf16[256,1024]{1,0:T(8,128)(2,1)S(1)} %broadcast_select_fusion), channel_id=1, source_target_pairs={{0,0},{2,16},{4,12},{6,28},{8,24},{10,8},{12,20},{14,4},{16,2},{18... | collective-permute-start | bytes 1572872 | tf_op jit(solution)/shard_map/ppermute | solution.py:427
  24.7 21.5 %copy-start.7 = (bf16[256,1024]{1,0:T(8,128)(2,1)}, bf16[256,1024]{1,0:T(8,128)(2,1)S(1)}, u32[]{:S(2)}) copy-start(bf16[256,1024]{1,0:T(8,128)(2,1)S(1)} %collective-permute-done.3.first_mine) | copy-start | bytes 1572868
  24.7 21.5 %copy-start.8 = (bf16[256,1024]{1,0:T(8,128)(2,1)}, bf16[256,1024]{1,0:T(8,128)(2,1)S(1)}, u32[]{:S(2)}) copy-start(bf16[256,1024]{1,0:T(8,128)(2,1)S(1)} %collective-permute-done.4.second_mine) | copy-start | bytes 1572868
  24.7 13.0 %copy-start.11 = (bf16[256,1024]{1,0:T(8,128)(2,1)}, bf16[256,1024]{1,0:T(8,128)(2,1)S(1)}, u32[]{:S(2)}) copy-start(bf16[256,1024]{1,0:T(8,128)(2,1)S(1)} %collective-permute-done.2.rows_in) | copy-start | bytes 1572868
  24.7 21.4 %collective-permute-start.8 = (bf16[256,1024]{1,0:T(8,128)(2,1)S(1)}, bf16[256,1024]{1,0:T(8,128)(2,1)S(1)}, u32[]{:S(2)}, u32[]{:S(2)}) collective-permute-start(bf16[256,1024]{1,0:T(8,128)(2,1)S(1)} %collective-permute-done.3.first_mine), channel_id=1, source_target_pairs={{0,2},{1,3},{2,0},{3,1},{4,6},{5,7},{6,4},{7,5},{8,10},{9,11},{10,... | collective-permute-start | bytes 1572872 | tf_op jit(solution)/shard_map/ppermute | solution.py:442
  36.9 9.3 %collective-permute-start.9 = (bf16[256,1024]{1,0:T(8,128)(2,1)S(1)}, bf16[256,1024]{1,0:T(8,128)(2,1)S(1)}, u32[]{:S(2)}, u32[]{:S(2)}) collective-permute-start(bf16[256,1024]{1,0:T(8,128)(2,1)S(1)} %collective-permute-done.4.second_mine), channel_id=1, source_target_pairs={{0,2},{1,3},{2,0},{3,1},{4,6},{5,7},{6,4},{7,5},{8,10},{9,11},{10,... | collective-permute-start | bytes 1572872 | tf_op jit(solution)/shard_map/ppermute | solution.py:442
  36.9 9.0 %collective-permute-start.5 = (bf16[256,512]{1,0:T(8,128)(2,1)}, bf16[256,512]{1,0:T(8,128)(2,1)}, u32[]{:S(2)}, u32[]{:S(2)}) collective-permute-start(bf16[256,512]{1,0:T(8,128)(2,1)} %get-tuple-element.49.refs_4_), channel_id=1, source_target_pairs={{0,16},{16,24},{24,8},{8,0},{1,17},{17,25},{25,9},{9,1},{2,18},{18... | collective-permute-start | bytes 786440 | tf_op jit(solution)/shard_map/ppermute | solution.py:454
  39.8 16.4 %copy-start.14 = (bf16[256,512]{1,0:T(8,128)(2,1)S(1)}, bf16[256,512]{1,0:T(8,128)(2,1)}, u32[]{:S(2)}) copy-start(bf16[256,512]{1,0:T(8,128)(2,1)} %get-tuple-element.52.refs_4_) | copy-start | bytes 786436
  39.8 20.6 %copy-start = (bf16[1024,256]{1,0:T(8,128)(2,1)S(1)}, bf16[1024,256]{1,0:T(8,128)(2,1)}, u32[]{:S(2)}) copy-start(bf16[1024,256]{1,0:T(8,128)(2,1)} %shard_map.146.refs_0_) | copy-start | bytes 1572868
  45.9 14.5 %collective-permute-start.15 = (bf16[1024,256]{1,0:T(8,128)(2,1)}, bf16[1024,256]{1,0:T(8,128)(2,1)S(1)}, u32[]{:S(2)}, u32[]{:S(2)}) collective-permute-start(bf16[1024,256]{1,0:T(8,128)(2,1)} %shard_map.146.refs_0_), channel_id=1, source_target_pairs={{0,4},{2,6},{4,0},{6,2},{1,5},{3,7},{5,1},{7,3},{8,12},{10,14},{12... | collective-permute-start | bytes 1572872 | tf_op jit(solution)/shard_map/ppermute | solution.py:465
  54.1 18.8 %collective-permute-start.10 = (bf16[256,1024]{1,0:T(8,128)(2,1)}, bf16[256,1024]{1,0:T(8,128)(2,1)S(1)}, u32[]{:S(2)}, u32[]{:S(2)}) collective-permute-start(bf16[256,1024]{1,0:T(8,128)(2,1)} %get-tuple-element.58), channel_id=1, source_target_pairs={{0,1},{1,0},{2,3},{3,2},{4,5},{5,4},{6,7},{7,6},{8,9},{9,8},{10,11... | collective-permute-start | bytes 1572872 | tf_op jit(solution)/shard_map/ppermute | solution.py:358
  56.2 9.7 %collective-permute-start.7 = (bf16[256,512]{1,0:T(8,128)(2,1)S(1)}, bf16[256,512]{1,0:T(8,128)(2,1)S(1)}, u32[]{:S(2)}, u32[]{:S(2)}) collective-permute-start(bf16[256,512]{1,0:T(8,128)(2,1)S(1)} %copy-done.14), channel_id=1, source_target_pairs={{0,16},{16,24},{24,8},{8,0},{1,17},{17,25},{25,9},{9,1},{2,18},{18... | collective-permute-start | bytes 786440 | tf_op jit(solution)/shard_map/ppermute | solution.py:454
  58.5 11.3 %collective-permute-start.6 = (bf16[256,512]{1,0:T(8,128)(2,1)}, bf16[256,512]{1,0:T(8,128)(2,1)}, u32[]{:S(2)}, u32[]{:S(2)}) collective-permute-start(bf16[256,512]{1,0:T(8,128)(2,1)} %collective-permute-done.5.refs_5_), channel_id=1, source_target_pairs={{0,16},{16,24},{24,8},{8,0},{1,17},{17,25},{25,9},{9,1},{2,18},{18... | collective-permute-start | bytes 786440 | tf_op jit(solution)/shard_map/ppermute | solution.py:454
  60.5 25.7 %collective-permute-start.14 = (bf16[1024,256]{1,0:T(8,128)(2,1)S(1)}, bf16[1024,256]{1,0:T(8,128)(2,1)S(1)}, u32[]{:S(2)}, u32[]{:S(2)}) collective-permute-start(bf16[1024,256]{1,0:T(8,128)(2,1)S(1)} %copy-done), channel_id=1, source_target_pairs={{0,2},{2,0},{4,6},{6,4},{1,3},{3,1},{5,7},{7,5},{8,10},{10,8},{12,... | collective-permute-start | bytes 1572872 | tf_op jit(solution)/shard_map/ppermute | solution.py:465
  60.5 19.0 %copy-start.1 = (bf16[1024,256]{1,0:T(8,128)(2,1)}, bf16[1024,256]{1,0:T(8,128)(2,1)S(1)}, u32[]{:S(2)}) copy-start(bf16[1024,256]{1,0:T(8,128)(2,1)S(1)} %collective-permute-done.15.refs_2_) | copy-start | bytes 1572868
  60.5 27.0 %collective-permute-start.16 = (bf16[1024,256]{1,0:T(8,128)(2,1)S(1)}, bf16[1024,256]{1,0:T(8,128)(2,1)S(1)}, u32[]{:S(2)}, u32[]{:S(2)}) collective-permute-start(bf16[1024,256]{1,0:T(8,128)(2,1)S(1)} %collective-permute-done.15.refs_2_), channel_id=1, source_target_pairs={{0,2},{2,0},{4,6},{6,4},{1,3},{3,1},{5,7},{7,5},{8,10},{10,8},{12,... | collective-permute-start | bytes 1572872 | tf_op jit(solution)/shard_map/ppermute | solution.py:465
  65.9 31.7 %copy-start.15 = (bf16[256,512]{1,0:T(8,128)(2,1)}, bf16[256,512]{1,0:T(8,128)(2,1)S(1)}, u32[]{:S(2)}) copy-start(bf16[256,512]{1,0:T(8,128)(2,1)S(1)} %collective-permute-done.7.refs_5_) | copy-start | bytes 786436
  69.8 13.0 %collective-permute-start.13 = (bf16[256,512]{1,0:T(8,128)(2,1)S(1)}, bf16[256,512]{1,0:T(8,128)(2,1)S(1)}, u32[]{:S(2)}, u32[]{:S(2)}) collective-permute-start(bf16[256,512]{1,0:T(8,128)(2,1)S(1)} %collective-permute-done.7.refs_5_), channel_id=1, source_target_pairs={{0,16},{16,24},{24,8},{8,0},{1,17},{17,25},{25,9},{9,1},{2,18},{18... | collective-permute-start | bytes 786440 | tf_op jit(solution)/shard_map/ppermute | solution.py:454
  72.3 15.3 %collective-permute-start.17 = (bf16[256,512]{1,0:T(8,128)(2,1)}, bf16[256,512]{1,0:T(8,128)(2,1)}, u32[]{:S(2)}, u32[]{:S(2)}) collective-permute-start(bf16[256,512]{1,0:T(8,128)(2,1)} %collective-permute-done.6.refs_6_), channel_id=1, source_target_pairs={{0,16},{16,24},{24,8},{8,0},{1,17},{17,25},{25,9},{9,1},{2,18},{18... | collective-permute-start | bytes 786440 | tf_op jit(solution)/shard_map/ppermute | solution.py:454
  79.5 13.7 %copy-start.13 = (f32[128,1024]{1,0:T(8,128)S(1)}, f32[128,1024]{1,0:T(8,128)}, u32[]{:S(2)}) copy-start(f32[128,1024]{1,0:T(8,128)} %get-tuple-element.62) | copy-start | bytes 1572868
  81.2 12.0 %collective-permute-start.12 = (bf16[64,1024]{1,0:T(8,128)(2,1)}, bf16[64,1024]{1,0:T(8,128)(2,1)S(1)}, u32[]{:S(2)}, u32[]{:S(2)}) collective-permute-start(bf16[64,1024]{1,0:T(8,128)(2,1)} %dynamic-slice_convert_fusion), channel_id=1, source_target_pairs={{0,1},{1,0},{2,3},{3,2},{4,5},{5,4},{6,7},{7,6},{8,9},{9,8},{10,11... | collective-permute-start | bytes 393224 | tf_op jit(solution)/shard_map/ppermute | solution.py:358
  82.8 14.8 %collective-permute-start.19 = (bf16[256,512]{1,0:T(8,128)(2,1)S(1)}, bf16[256,512]{1,0:T(8,128)(2,1)}, u32[]{:S(2)}, u32[]{:S(2)}) collective-permute-start(bf16[256,512]{1,0:T(8,128)(2,1)S(1)} %collective-permute-done.13.refs_6_), channel_id=1, source_target_pairs={{0,16},{16,24},{24,8},{8,0},{1,17},{17,25},{25,9},{9,1},{2,18},{18... | collective-permute-start | bytes 786440 | tf_op jit(solution)/shard_map/ppermute | solution.py:454
  86.2 16.6 %collective-permute-start.11 = (bf16[128,1024]{1,0:T(8,128)(2,1)S(1)}, bf16[128,1024]{1,0:T(8,128)(2,1)S(1)}, u32[]{:S(2)}, u32[]{:S(2)}) collective-permute-start(bf16[128,1024]{1,0:T(8,128)(2,1)S(1)} %slice.16), channel_id=1, source_target_pairs={{8,0},{16,8},{24,16},{9,1},{17,9},{25,17},{10,2},{18,10},{26,18},{... | collective-permute-start | bytes 786440 | tf_op jit(solution)/shard_map/ppermute | solution.py:504
  93.2 9.6 %collective-permute-start.18 = (bf16[64,1024]{1,0:T(8,128)(2,1)S(1)}, bf16[64,1024]{1,0:T(8,128)(2,1)S(1)}, u32[]{:S(2)}, u32[]{:S(2)}) collective-permute-start(bf16[64,1024]{1,0:T(8,128)(2,1)S(1)} %add_convert_fusion.1), channel_id=1, source_target_pairs={{0,8},{8,0},{16,24},{24,16},{1,9},{9,1},{17,25},{25,17},{2,10},{10... | collective-permute-start | bytes 393224 | tf_op jit(solution)/shard_map/ppermute | solution.py:358
  95.9 15.1 %collective-permute-start.20 = (bf16[512,512]{1,0:T(8,128)(2,1)}, bf16[512,512]{1,0:T(8,128)(2,1)S(1)}, u32[]{:S(2)}, u32[]{:S(2)}) collective-permute-start(bf16[512,512]{1,0:T(8,128)(2,1)} %get-tuple-element.77), channel_id=1, source_target_pairs={{0,1},{1,0},{2,3},{3,2},{4,5},{5,4},{6,7},{7,6},{8,9},{9,8},{10,11... | collective-permute-start | bytes 1572872 | tf_op jit(solution)/shard_map/ppermute | solution.py:358
  102.4 16.8 %collective-permute-start.23 = (bf16[512,512]{1,0:T(8,128)(2,1)}, bf16[512,512]{1,0:T(8,128)(2,1)S(1)}, u32[]{:S(2)}, u32[]{:S(2)}) collective-permute-start(bf16[512,512]{1,0:T(8,128)(2,1)} %get-tuple-element.81), channel_id=1, source_target_pairs={{0,1},{1,0},{2,3},{3,2},{4,5},{5,4},{6,7},{7,6},{8,9},{9,8},{10,11... | collective-permute-start | bytes 1572872 | tf_op jit(solution)/shard_map/ppermute | solution.py:358
  102.9 6.9 %collective-permute-start.21 = (bf16[64,1024]{1,0:T(8,128)(2,1)S(1)}, bf16[64,1024]{1,0:T(8,128)(2,1)S(1)}, u32[]{:S(2)}, u32[]{:S(2)}) collective-permute-start(bf16[64,1024]{1,0:T(8,128)(2,1)S(1)} %add_convert_fusion), channel_id=1, source_target_pairs={{0,16},{8,24},{16,0},{24,8},{1,17},{9,25},{17,1},{25,9},{2,18},{10... | collective-permute-start | bytes 393224 | tf_op jit(solution)/shard_map/ppermute | solution.py:358
  111.0 9.8 %collective-permute-start.22 = (bf16[64,1024]{1,0:T(8,128)(2,1)S(1)}, bf16[64,1024]{1,0:T(8,128)(2,1)S(1)}, u32[]{:S(2)}, u32[]{:S(2)}) collective-permute-start(bf16[64,1024]{1,0:T(8,128)(2,1)S(1)} %convert_add_fusion), channel_id=1, source_target_pairs={{0,1},{1,0},{2,3},{3,2},{4,5},{5,4},{6,7},{7,6},{8,9},{9,8},{10,11... | collective-permute-start | bytes 393224 | tf_op jit(solution)/shard_map/ppermute | solution.py:358
  (10 other events, 36.3 us)

commit v10 on v9

--- a/solution.py
+++ b/solution.py
@@ -302,7 +302,7 @@
             pltpu.SemaphoreType.DMA((steps,)),
             pltpu.SemaphoreType.DMA((2, steps)),
         ],
-        4 * length * out_weight.size,
+        256 * length * out_weight.size,
     )
 
 
@@ -399,7 +399,7 @@
     rounds = []
     for turn in range(2):
         route = [(tp_dp(h, c, d), tp_dp(d ^ turn, c, h)) for h, c, d in places]
-        rounds.append(lax.ppermute(cot, ("tp", "dp"), route))
+        rounds.append(lax.ppermute(after(cot, prior) if turn else cot, ("tp", "dp"), route))
     square = n_seq == n_tp == 4 and subs == 2
     if square:
 
@@ -424,7 +424,7 @@
             for t in range(n_tp):
                 block = sum(crossed[s % 2]) - t if t in crossed[s % 2] else t
                 route.append((s * n_tp + t, block * n_tp + holder(s, block)))
-        moved = lax.ppermute(after(held, prior), ("seq", "tp"), route)
+        moved = lax.ppermute(held, ("seq", "tp"), route)
     else:
         moved = cot
 
@@ -454,31 +454,35 @@
             pieces.append(lax.ppermute(pieces[-1], "seq", ring))
 
         ring_step(halves[0])
-        moved = transposed(moved)
-        halves[0][1], moved, place = lax.optimization_barrier((halves[0][1], moved, place))
-        ring_step(halves[0])
-        ring_step(halves[1])
-    other_sent, own_part = project(place, firsts, seconds, out_weight)
-    other_part = swap_pairs(other_sent, "dp", 1)
-
-    if square:
-        sent_by = lambda value, flip: lax.ppermute(value, "tp", [(t, t ^ flip) for t in range(n_tp)])
-        across = sent_by(moved, subs)
-        cot_pieces = [moved, sent_by(moved, 1), across, sent_by(across, 1)]
         table = np.zeros((n_seq, n_tp, n_tp), np.int32)
         for k, s in enumerate(order):
             for r in range(n_seq):
                 for t in range(n_tp):
                     table[s, t, t ^ holder(order[k - r], s)] = r
         sources = jnp.asarray(table)[lax.axis_index("seq"), me_tp]
-        halves[0][2], halves[1][1], own_part = lax.optimization_barrier(
-            (halves[0][2], halves[1][1], own_part)
+        weight_place = jnp.concatenate([sources, me_dp[None].astype(jnp.int32)])
+        moved = transposed(moved)
+        halves[0][1], moved, place, weight_place = lax.optimization_barrier(
+            (halves[0][1], moved, place, weight_place)
         )
         ring_step(halves[0])
+    other_sent, own_part = project(place, firsts, seconds, out_weight)
+    if square:
+        halves[0][2], halves[1][0], other_sent = lax.optimization_barrier(
+            (halves[0][2], halves[1][0], other_sent)
+        )
+    other_part = swap_pairs(other_sent, "dp", 1)
+
+    if square:
+        sent_by = lambda value, flip: lax.ppermute(value, "tp", [(t, t ^ flip) for t in range(n_tp)])
+        across = sent_by(moved, subs)
+        cot_pieces = [moved, sent_by(moved, 1), across, sent_by(after(across, halves[0][2]), 1)]
+        ring_step(halves[0])
         ring_step(halves[1])
-
-        weight_place = jnp.concatenate([sources, me_dp[None].astype(jnp.int32)])
-
+        halves[0][3], halves[1][1], own_part = lax.optimization_barrier(
+            (halves[0][3], halves[1][1], own_part)
+        )
+        ring_step(halves[1])
     else:
         full = lax.all_gather(cot, "tp", axis=1, tiled=True)
         cot_all = lax.all_to_all(full, "seq", 1, 0, tiled=True)
@@ -518,7 +522,7 @@
         lax.dynamic_slice_in_dim(lags, (1 - me_dp) * share, share, axis=0).astype(bf16), "dp", 1
     )
     if square:
-        halves[1][2], weight_place = lax.optimization_barrier((halves[1][2], weight_place))
+        weight_place, halves[1][2], signal = lax.optimization_barrier((weight_place, halves[1][2], signal))
         ring_step(halves[1])
         first_sent, first_own = weight_sum(weight_place, cot_pieces, halves[0], rows)
         first_received = swap_pairs(first_sent, "dp", 1)
@@ -529,7 +533,6 @@
         rounded = lag_sum.astype(bf16)
         received = swap_pairs(rounded, "seq", distance)
         if square and distance == 1:
-            weight_place = after(weight_place, first_own)
             second_sent, second_own = weight_sum(weight_place, cot_pieces, halves[1], rows)
             second_received = swap_pairs(second_sent, "dp", 1)
             received, second_own = lax.optimization_barrier((received, second_own))
@@ -539,9 +542,7 @@
         first_received, lag_sum = lax.optimization_barrier((first_received, lag_sum))
     mine = lag_sum.astype(bf16)
     theirs = swap_pairs(mine, "dp", 1)
-    if square:
-        later = after(later, second_own)
-    grad_key, grad_value = run_back(later)
+    grad_key, grad_value = run_back(after(later, second_own) if square else later)
     first = me_dp == 0
     lag_sum = jnp.concatenate([jnp.where(first, mine, theirs), jnp.where(first, theirs, mine)], axis=0)
     grad_filter = lag_sum.astype(f32).T * (norm_factor * scale)

time: 123 us -> 117 us (0.951)
  starting transfers between devices: 46.7 us -> 37.3 us
  waiting for transfers between devices: 26 us -> 29.9 us
    ppermute x3, waiting for transfers between devices: 0.01 us -> 5.19 us  [the longest x2 5.19 us: per_device(): lax.ppermute(after(cot, prior) if turn else cot, ('tp', 'dp'), route)]
    ppermute x2, starting transfers between devices: 12.2 us -> 7.02 us  [per_device(): theirs = [lax.ppermute(r, ('tp', 'dp'), route) for r in rounds]]
    ppermute x3, starting transfers between devices: 7.08 us -> 3.06 us  [the longest x2 2.37 us: per_device(): lax.ppermute(after(cot, prior) if turn else cot, ('tp', 'dp'), route)]
    ppermute x7, starting transfers between devices: 9.1 us -> 7 us  [swap_pairs(): return lax.ppermute(value, axis, [(i, i ^ distance) for i in range(count)])]
    ppermute x7, waiting for transfers between devices: 8.32 us -> 6.54 us  [swap_pairs(): return lax.ppermute(value, axis, [(i, i ^ distance) for i in range(count)])]
    ppermute x1, starting transfers between devices: 5.63 us -> 7.09 us  [per_device(): prior = lax.ppermute(tail, 'seq', [(i, i + 1) for i in range(n_seq - 1)])]
    unnamed x37 -> x39, local copies, waits for them, and re-layouts: 4.7 us -> 4.21 us
  transfers between devices with their start and end apart: 24 -> 24, of which waited for: 7 -> 8; matrix products, arithmetic and copies ran while one was open for 6% -> 7% of each run, Pallas kernels for 28% -> 30%
where the time goes in v10:
time: 117 us; the launch traced here: 116 us
  starting transfers between devices  37.3 us (32%)
  Pallas kernels  34.7 us (30%)
  waiting for transfers between devices  29.9 us (26%)
  local copies, waits for them, and re-layouts  8.14 us (7%)
  other arithmetic  5.46 us (5%)
    pallas_call x3, Pallas kernels, by_channel(): pl.pallas_call(kernel, in_specs=[pl.BlockSpec(memory_space=pl.ANY)] * (n_...  16.8 us
    pallas_call x3, Pallas kernels, local_call(): pl.pallas_call(kernel, in_specs=[pl.BlockSpec(memory_space=pltpu.SMEM)] +...  15.9 us
    ppermute x6, waiting for transfers between devices, ring_step(): pieces.append(lax.ppermute(pieces[-1], 'seq', ring))  15.4 us
    ppermute x6, starting transfers between devices, ring_step(): pieces.append(lax.ppermute(pieces[-1], 'seq', ring))  10.5 us
    ppermute x1, starting transfers between devices, per_device(): prior = lax.ppermute(tail, 'seq', [(i, i + 1) for i in range(n_seq - 1)])  7.09 us
    ppermute x2, starting transfers between devices, per_device(): theirs = [lax.ppermute(r, ('tp', 'dp'), route) for r in rounds]  7.02 us
    ppermute x7, starting transfers between devices, swap_pairs(): return lax.ppermute(value, axis, [(i, i ^ distance) for i in range(count)])  7 us
    ppermute x7, waiting for transfers between devices, swap_pairs(): return lax.ppermute(value, axis, [(i, i ^ distance) for i in range(count)])  6.54 us
  transfers between devices with their start and end apart: 24, of which 8 were waited for; matrix products, arithmetic and copies ran while one was open for 7% of the time, Pallas kernels for 30%

profile of v10, /device:TPU:0, one launch (start us, length us, event | category | flops | bytes accessed | tf_op | source)
XLA Modules:
  0.0 116.5 jit_solution(1859320157911790975)
XLA Ops:
  0.6 1.1 fusion
  2.4 7.1 %collective-permute-start = (bf16[128,1024]{1,0:T(8,128)(2,1)S(1)}, bf16[128,1024]{1,0:T(8,128)(2,1)S(1)}, u32[]{:S(2)}, u32[]{:S(2)}) collective-permute-start(bf16[128,1024]{1,0:T(8,128)(2,1)S(1)} %fusion), channel_id=1, source_target_pairs={{0,8},{8,16},{16,24},{1,9},{9,17},{17,25},{2,10},{10,18},{18,26},{... | collective-permute-start | bytes 786440 | tf_op jit(solution)/shard_map/ppermute | solution.py:393
  9.5 1.7 %collective-permute-start.3 = (bf16[256,1024]{1,0:T(8,128)(2,1)}, bf16[256,1024]{1,0:T(8,128)(2,1)S(1)}, u32[]{:S(2)}, u32[]{:S(2)}) collective-permute-start(bf16[256,1024]{1,0:T(8,128)(2,1)} %bitcast.28), channel_id=1, source_target_pairs={{0,0},{1,4},{2,2},{3,6},{4,1},{5,5},{6,3},{7,7},{8,8},{9,12},{10,1... | collective-permute-start | bytes 1572872 | tf_op jit(solution)/shard_map/ppermute | solution.py:402
  11.2 2.8 %collective-permute-done.refs_2_.refs_6_ = bf16[128,1024]{1,0:T(8,128)(2,1)S(1)} collective-permute-done((bf16[128,1024]{1,0:T(8,128)(2,1)S(1)}, bf16[128,1024]{1,0:T(8,128)(2,1)S(1)}, u32[]{:S(2)}, u32[]{:S(2)}) %collective-permute-start) | collective-permute-done | bytes 262176 | tf_op jit(solution)/shard_map/ppermute | solution.py:393
  14.7 1.1 broadcast_select_fusion
  16.5 5.5 %shard_map.145 = (f32[256,1024]{1,0:T(8,128)}, bf16[256,512]{1,0:T(8,128)(2,1)}, bf16[256,512]{1,0:T(8,128)(2,1)}) custom-call(bf16[768,384]{1,0:T(8,128)(2,1)} %constant.69.clone.refs_0_, bf16[768,384]{1,0:T(8,128)(2,1)} %constant.70.clone.refs_1_, bf16[128,1024]{1,0:T(8,128)(2,1)} %copy-done.4, bf16[256,1024]{1,0:T(8,128)(2,1)} %bitcast.22, ...), custom_call_target="tpu_custom_call" | custom-call | flops 22020096 | bytes 57408 | tf_op jit(solution)/shard_map/pallas_call | solution.py:257
  22.1 5.2 %collective-permute-done.4.second_mine = bf16[256,1024]{1,0:T(8,128)(2,1)S(1)} collective-permute-done((bf16[256,1024]{1,0:T(8,128)(2,1)}, bf16[256,1024]{1,0:T(8,128)(2,1)S(1)}, u32[]{:S(2)}, u32[]{:S(2)}) %collective-permute-start.4) | collective-permute-done | bytes 524320 | tf_op jit(solution)/shard_map/ppermute | solution.py:402
  27.3 7.0 %collective-permute-start.7 = (bf16[256,1024]{1,0:T(8,128)(2,1)S(1)}, bf16[256,1024]{1,0:T(8,128)(2,1)S(1)}, u32[]{:S(2)}, u32[]{:S(2)}) collective-permute-start(bf16[256,1024]{1,0:T(8,128)(2,1)S(1)} %collective-permute-done.3.first_mine), channel_id=1, source_target_pairs={{0,2},{1,3},{2,0},{3,1},{4,6},{5,7},{6,4},{7,5},{8,10},{9,11},{10,... | collective-permute-start | bytes 1572872 | tf_op jit(solution)/shard_map/ppermute | solution.py:442
  36.5 2.0 %shard_map.146.refs_0_ = bf16[1024,256]{1,0:T(8,128)(2,1)} custom-call(bf16[256,1024]{1,0:T(8,128)(2,1)} %copy-done.7), custom_call_target="tpu_custom_call" | custom-call | bytes 16384 | tf_op jit(solution)/shard_map/pallas_call | solution.py:341
  38.6 4.7 %collective-permute-done.5.refs_5_ = bf16[256,512]{1,0:T(8,128)(2,1)S(1)} collective-permute-done((bf16[256,512]{1,0:T(8,128)(2,1)}, bf16[256,512]{1,0:T(8,128)(2,1)S(1)}, u32[]{:S(2)}, u32[]{:S(2)}) %collective-permute-start.5) | collective-permute-done | bytes 262176 | tf_op jit(solution)/shard_map/ppermute | solution.py:454
  43.4 2.4 %collective-permute-start.6 = (bf16[256,512]{1,0:T(8,128)(2,1)S(1)}, bf16[256,512]{1,0:T(8,128)(2,1)S(1)}, u32[]{:S(2)}, u32[]{:S(2)}) collective-permute-start(bf16[256,512]{1,0:T(8,128)(2,1)S(1)} %collective-permute-done.5.refs_5_), channel_id=1, source_target_pairs={{0,16},{16,24},{24,8},{8,0},{1,17},{17,25},{25,9},{9,1},{2,18},{18... | collective-permute-start | bytes 786440 | tf_op jit(solution)/shard_map/ppermute | solution.py:454
  46.6 6.4 %shard_map.147 = (bf16[256,1024]{1,0:T(8,128)(2,1)}, f32[256,1024]{1,0:T(8,128)}) custom-call(s32[3]{0:T(128)} %pad_add_fusion.place_ref, bf16[256,1024]{1,0:T(8,128)(2,1)} %copy-done.16, bf16[256,1024]{1,0:T(8,128)(2,1)} %copy-done.17, bf16[256,1024]{1,0:T(8,128)(2,1)} %copy-done.18, bf16[256,1024]{1,0:T(8,128)(2,1)} %collective-permute-done.8.second_theirs, ...), custom_call_target="tpu_custom_call" | custom-call | flops 2147483648 | bytes 122880 | tf_op jit(solution)/shard_map/pallas_call | solution.py:276
  53.0 1.6 %collective-permute-start.11 = (bf16[256,1024]{1,0:T(8,128)(2,1)}, bf16[256,1024]{1,0:T(8,128)(2,1)S(1)}, u32[]{:S(2)}, u32[]{:S(2)}) collective-permute-start(bf16[256,1024]{1,0:T(8,128)(2,1)} %get-tuple-element.66), channel_id=1, source_target_pairs={{0,1},{1,0},{2,3},{3,2},{4,5},{5,4},{6,7},{7,6},{8,9},{9,8},{10,11... | collective-permute-start | bytes 1572872 | tf_op jit(solution)/shard_map/ppermute | solution.py:358
  54.6 2.3 %collective-permute-start.9 = (bf16[256,512]{1,0:T(8,128)(2,1)S(1)}, bf16[256,512]{1,0:T(8,128)(2,1)S(1)}, u32[]{:S(2)}, u32[]{:S(2)}) collective-permute-start(bf16[256,512]{1,0:T(8,128)(2,1)S(1)} %collective-permute-done.6.refs_6_), channel_id=1, source_target_pairs={{0,16},{16,24},{24,8},{8,0},{1,17},{17,25},{25,9},{9,1},{2,18},{18... | collective-permute-start | bytes 786440 | tf_op jit(solution)/shard_map/ppermute | solution.py:454
  57.0 1.2 %collective-permute-start.10 = (bf16[256,512]{1,0:T(8,128)(2,1)S(1)}, bf16[256,512]{1,0:T(8,128)(2,1)S(1)}, u32[]{:S(2)}, u32[]{:S(2)}) collective-permute-start(bf16[256,512]{1,0:T(8,128)(2,1)S(1)} %copy-done.10), channel_id=1, source_target_pairs={{0,16},{16,24},{24,8},{8,0},{1,17},{17,25},{25,9},{9,1},{2,18},{18... | collective-permute-start | bytes 786440 | tf_op jit(solution)/shard_map/ppermute | solution.py:454
  58.7 5.2 %collective-permute-done.9.refs_7_ = bf16[256,512]{1,0:T(8,128)(2,1)S(1)} collective-permute-done((bf16[256,512]{1,0:T(8,128)(2,1)S(1)}, bf16[256,512]{1,0:T(8,128)(2,1)S(1)}, u32[]{:S(2)}, u32[]{:S(2)}) %collective-permute-start.9) | collective-permute-done | bytes 262176 | tf_op jit(solution)/shard_map/ppermute | solution.py:454
  63.9 3.4 %collective-permute-done.10.refs_5_ = bf16[256,512]{1,0:T(8,128)(2,1)S(1)} collective-permute-done((bf16[256,512]{1,0:T(8,128)(2,1)S(1)}, bf16[256,512]{1,0:T(8,128)(2,1)S(1)}, u32[]{:S(2)}, u32[]{:S(2)}) %collective-permute-start.10) | collective-permute-done | bytes 262176 | tf_op jit(solution)/shard_map/ppermute | solution.py:454
  67.3 2.7 %collective-permute-start.12 = (bf16[256,512]{1,0:T(8,128)(2,1)S(1)}, bf16[256,512]{1,0:T(8,128)(2,1)S(1)}, u32[]{:S(2)}, u32[]{:S(2)}) collective-permute-start(bf16[256,512]{1,0:T(8,128)(2,1)S(1)} %collective-permute-done.10.refs_5_), channel_id=1, source_target_pairs={{0,16},{16,24},{24,8},{8,0},{1,17},{17,25},{25,9},{9,1},{2,18},{18... | collective-permute-start | bytes 786440 | tf_op jit(solution)/shard_map/ppermute | solution.py:454
  70.8 5.7 %shard_map.148 = (bf16[256,1024]{1,0:T(8,128)(2,1)}, bf16[256,1024]{1,0:T(8,128)(2,1)}, f32[128,1024]{1,0:T(8,128)}) custom-call(bf16[768,384]{1,0:T(8,128)(2,1)} %constant.69.clone.refs_0_, bf16[768,384]{1,0:T(8,128)(2,1)} %constant.70.clone.refs_1_, f32[256,1024]{1,0:T(8,128)} %get-tuple-element.65.refs_2_, bf16[256,1024]{1,0:T(8,128)(2,1)} %copy-done.8, ...), custom_call_target="tpu_custom_call" | custom-call | flops 20447232 | bytes 94208 | tf_op jit(solution)/shard_map/pallas_call | solution.py:257
  76.5 1.7 %dynamic-slice_convert_fusion = bf16[64,1024]{1,0:T(8,128)(2,1)} fusion(f32[128,1024]{1,0:T(8,128)} %get-tuple-element.73, s32[]{:T(128)S(6)} %select_n.66), kind=kLoop, calls=%fused_computation.10 | loop fusion | bytes 262148 | tf_op jit(solution)/shard_map/convert_element_type | solution.py:522
  79.5 1.3 %collective-permute-start.13 = (bf16[128,1024]{1,0:T(8,128)(2,1)S(1)}, bf16[128,1024]{1,0:T(8,128)(2,1)}, u32[]{:S(2)}, u32[]{:S(2)}) collective-permute-start(bf16[128,1024]{1,0:T(8,128)(2,1)S(1)} %slice.16), channel_id=1, source_target_pairs={{8,0},{16,8},{24,16},{9,1},{17,9},{25,17},{10,2},{18,10},{26,18},{... | collective-permute-start | bytes 786440 | tf_op jit(solution)/shard_map/ppermute | solution.py:508
  80.8 1.6 %collective-permute-start.19 = (bf16[256,512]{1,0:T(8,128)(2,1)S(1)}, bf16[256,512]{1,0:T(8,128)(2,1)}, u32[]{:S(2)}, u32[]{:S(2)}) collective-permute-start(bf16[256,512]{1,0:T(8,128)(2,1)S(1)} %collective-permute-done.12.refs_6_), channel_id=1, source_target_pairs={{0,16},{16,24},{24,8},{8,0},{1,17},{17,25},{25,9},{9,1},{2,18},{18... | collective-permute-start | bytes 786440 | tf_op jit(solution)/shard_map/ppermute | solution.py:454
  84.1 4.8 %shard_map.149 = (bf16[512,512]{1,0:T(8,128)(2,1)}, f32[512,512]{1,0:T(8,128)}) custom-call(s32[5]{0:T(128)} %pad_add_fusion.1.place_ref, bf16[1024,256]{1,0:T(8,128)(2,1)} %shard_map.146.refs_0_, bf16[1024,256]{1,0:T(8,128)(2,1)} %copy-done.2, bf16[1024,256]{1,0:T(8,128)(2,1)} %copy-done.1, bf16[1024,256]{1,0:T(8,128)(2,1)} %copy-done.3, ...), custom_call_target="tpu_custom_call" | custom-call | flops 16777216 | bytes 73728 | tf_op jit(solution)/shard_map/pallas_call | solution.py:276
  88.9 1.1 collective-permute-start.18
  90.0 1.7 %collective-permute-start.20 = (bf16[512,512]{1,0:T(8,128)(2,1)}, bf16[512,512]{1,0:T(8,128)(2,1)S(1)}, u32[]{:S(2)}, u32[]{:S(2)}) collective-permute-start(bf16[512,512]{1,0:T(8,128)(2,1)} %get-tuple-element.86), channel_id=1, source_target_pairs={{0,1},{1,0},{2,3},{3,2},{4,5},{5,4},{6,7},{7,6},{8,9},{9,8},{10,11... | collective-permute-start | bytes 1572872 | tf_op jit(solution)/shard_map/ppermute | solution.py:358
  91.7 2.1 %collective-permute-done.19.refs_7_ = bf16[256,512]{1,0:T(8,128)(2,1)} collective-permute-done((bf16[256,512]{1,0:T(8,128)(2,1)S(1)}, bf16[256,512]{1,0:T(8,128)(2,1)}, u32[]{:S(2)}, u32[]{:S(2)}) %collective-permute-start.19) | collective-permute-done | bytes 262176 | tf_op jit(solution)/shard_map/ppermute | solution.py:454
  93.8 4.8 %shard_map.150 = (bf16[512,512]{1,0:T(8,128)(2,1)}, f32[512,512]{1,0:T(8,128)}) custom-call(s32[5]{0:T(128)} %pad_add_fusion.1.place_ref, bf16[1024,256]{1,0:T(8,128)(2,1)} %shard_map.146.refs_0_, bf16[1024,256]{1,0:T(8,128)(2,1)} %copy-done.2, bf16[1024,256]{1,0:T(8,128)(2,1)} %copy-done.1, bf16[1024,256]{1,0:T(8,128)(2,1)} %copy-done.3, ...), custom_call_target="tpu_custom_call" | custom-call | flops 16777216 | bytes 73728 | tf_op jit(solution)/shard_map/pallas_call | solution.py:276
  98.6 1.5 %collective-permute-start.23 = (bf16[512,512]{1,0:T(8,128)(2,1)}, bf16[512,512]{1,0:T(8,128)(2,1)S(1)}, u32[]{:S(2)}, u32[]{:S(2)}) collective-permute-start(bf16[512,512]{1,0:T(8,128)(2,1)} %get-tuple-element.91), channel_id=1, source_target_pairs={{0,1},{1,0},{2,3},{3,2},{4,5},{5,4},{6,7},{7,6},{8,9},{9,8},{10,11... | collective-permute-start | bytes 1572872 | tf_op jit(solution)/shard_map/ppermute | solution.py:358
  100.3 5.5 %shard_map.151 = (bf16[256,1024]{1,0:T(8,128)(2,1)}, bf16[256,1024]{1,0:T(8,128)(2,1)}) custom-call(bf16[768,384]{1,0:T(8,128)(2,1)} %constant.69.clone.refs_0_, bf16[768,384]{1,0:T(8,128)(2,1)} %constant.70.clone.refs_1_, bf16[256,1024]{1,0:T(8,128)(2,1)} %get-tuple-element.72.refs_2_, bf16[128,1024]{1,0:T(8,128)(2,1)} %collective-permute-done.13.refs_3_, ...), custom_call_target="tpu_custom_call" | custom-call | flops 5637144576 | bytes 49216 | tf_op jit(solution)/shard_map/pallas_call | solution.py:257
  105.8 1.7 %collective-permute-done.21 = bf16[64,1024]{1,0:T(8,128)(2,1)S(1)} collective-permute-done((bf16[64,1024]{1,0:T(8,128)(2,1)S(1)}, bf16[64,1024]{1,0:T(8,128)(2,1)S(1)}, u32[]{:S(2)}, u32[]{:S(2)}) %collective-permute-start.21) | collective-permute-done | bytes 131104 | tf_op jit(solution)/shard_map/ppermute | solution.py:358
  108.3 4.8 %collective-permute-done.23 = bf16[512,512]{1,0:T(8,128)(2,1)S(1)} collective-permute-done((bf16[512,512]{1,0:T(8,128)(2,1)}, bf16[512,512]{1,0:T(8,128)(2,1)S(1)}, u32[]{:S(2)}, u32[]{:S(2)}) %collective-permute-start.23) | collective-permute-done | bytes 524320 | tf_op jit(solution)/shard_map/ppermute | solution.py:358
  113.4 1.5 %pad_maximum_fusion = f32[512,1024]{1,0:T(8,128)} fusion(f32[512,512]{1,0:T(8,128)S(1)} %add_multiply_fusion, f32[512,512]{1,0:T(8,128)S(1)} %add_multiply_fusion.1), kind=kLoop, calls=%fused_computation | loop fusion | flops 524288 | bytes 4194304 | tf_op jit(solution)/shard_map/concatenate | solution.py:554
  (78 shorter events, 12.3 us)
Async XLA Ops:
  1.7 12.9 %collective-permute-start.1 = (bf16[256,1024]{1,0:T(8,128)(2,1)}, bf16[256,1024]{1,0:T(8,128)(2,1)S(1)}, u32[]{:S(2)}, u32[]{:S(2)}) collective-permute-start(bf16[256,1024]{1,0:T(8,128)(2,1)} %bitcast.27), channel_id=1, source_target_pairs={{2,4},{4,2},{8,14},{14,8},{18,20},{20,18},{24,30},{30,24},{3,5},{5... | collective-permute-start | bytes 1572872 | tf_op jit(solution)/shard_map/ppermute | solution.py:415
  2.4 11.6 %collective-permute-start = (bf16[128,1024]{1,0:T(8,128)(2,1)S(1)}, bf16[128,1024]{1,0:T(8,128)(2,1)S(1)}, u32[]{:S(2)}, u32[]{:S(2)}) collective-permute-start(bf16[128,1024]{1,0:T(8,128)(2,1)S(1)} %fusion), channel_id=1, source_target_pairs={{0,8},{8,16},{16,24},{1,9},{9,17},{17,25},{2,10},{10,18},{18,26},{... | collective-permute-start | bytes 786440 | tf_op jit(solution)/shard_map/ppermute | solution.py:393
  9.5 12.5 %collective-permute-start.3 = (bf16[256,1024]{1,0:T(8,128)(2,1)}, bf16[256,1024]{1,0:T(8,128)(2,1)S(1)}, u32[]{:S(2)}, u32[]{:S(2)}) collective-permute-start(bf16[256,1024]{1,0:T(8,128)(2,1)} %bitcast.28), channel_id=1, source_target_pairs={{0,0},{1,4},{2,2},{3,6},{4,1},{5,5},{6,3},{7,7},{8,8},{9,12},{10,1... | collective-permute-start | bytes 1572872 | tf_op jit(solution)/shard_map/ppermute | solution.py:402
  14.0 13.3 %collective-permute-start.4 = (bf16[256,1024]{1,0:T(8,128)(2,1)}, bf16[256,1024]{1,0:T(8,128)(2,1)S(1)}, u32[]{:S(2)}, u32[]{:S(2)}) collective-permute-start(bf16[256,1024]{1,0:T(8,128)(2,1)} %bitcast.29), channel_id=1, source_target_pairs={{0,4},{1,0},{2,6},{3,2},{4,5},{5,1},{6,7},{7,3},{8,12},{9,8},{10,1... | collective-permute-start | bytes 1572872 | tf_op jit(solution)/shard_map/ppermute | solution.py:402
  15.8 11.5 %collective-permute-start.2 = (bf16[256,1024]{1,0:T(8,128)(2,1)S(1)}, bf16[256,1024]{1,0:T(8,128)(2,1)S(1)}, u32[]{:S(2)}, u32[]{:S(2)}) collective-permute-start(bf16[256,1024]{1,0:T(8,128)(2,1)S(1)} %broadcast_select_fusion), channel_id=1, source_target_pairs={{0,0},{2,16},{4,12},{6,28},{8,24},{10,8},{12,20},{14,4},{16,2},{18... | collective-permute-start | bytes 1572872 | tf_op jit(solution)/shard_map/ppermute | solution.py:427
  22.1 23.7 %copy-start.16 = (bf16[256,1024]{1,0:T(8,128)(2,1)}, bf16[256,1024]{1,0:T(8,128)(2,1)S(1)}, u32[]{:S(2)}) copy-start(bf16[256,1024]{1,0:T(8,128)(2,1)S(1)} %collective-permute-done.3.first_mine) | copy-start | bytes 1572868
  27.3 18.6 %copy-start.17 = (bf16[256,1024]{1,0:T(8,128)(2,1)}, bf16[256,1024]{1,0:T(8,128)(2,1)S(1)}, u32[]{:S(2)}) copy-start(bf16[256,1024]{1,0:T(8,128)(2,1)S(1)} %collective-permute-done.4.second_mine) | copy-start | bytes 1572868
  27.3 18.5 %collective-permute-start.7 = (bf16[256,1024]{1,0:T(8,128)(2,1)S(1)}, bf16[256,1024]{1,0:T(8,128)(2,1)S(1)}, u32[]{:S(2)}, u32[]{:S(2)}) collective-permute-start(bf16[256,1024]{1,0:T(8,128)(2,1)S(1)} %collective-permute-done.3.first_mine), channel_id=1, source_target_pairs={{0,2},{1,3},{2,0},{3,1},{4,6},{5,7},{6,4},{7,5},{8,10},{9,11},{10,... | collective-permute-start | bytes 1572872 | tf_op jit(solution)/shard_map/ppermute | solution.py:442
  34.3 11.5 %collective-permute-start.8 = (bf16[256,1024]{1,0:T(8,128)(2,1)S(1)}, bf16[256,1024]{1,0:T(8,128)(2,1)}, u32[]{:S(2)}, u32[]{:S(2)}) collective-permute-start(bf16[256,1024]{1,0:T(8,128)(2,1)S(1)} %collective-permute-done.4.second_mine), channel_id=1, source_target_pairs={{0,2},{1,3},{2,0},{3,1},{4,6},{5,7},{6,4},{7,5},{8,10},{9,11},{10,... | collective-permute-start | bytes 1572872 | tf_op jit(solution)/shard_map/ppermute | solution.py:442
  34.3 8.9 %collective-permute-start.5 = (bf16[256,512]{1,0:T(8,128)(2,1)}, bf16[256,512]{1,0:T(8,128)(2,1)S(1)}, u32[]{:S(2)}, u32[]{:S(2)}) collective-permute-start(bf16[256,512]{1,0:T(8,128)(2,1)} %get-tuple-element.54.refs_4_), channel_id=1, source_target_pairs={{0,16},{16,24},{24,8},{8,0},{1,17},{17,25},{25,9},{9,1},{2,18},{18... | collective-permute-start | bytes 786440 | tf_op jit(solution)/shard_map/ppermute | solution.py:454
  38.5 18.4 %copy-start.10 = (bf16[256,512]{1,0:T(8,128)(2,1)S(1)}, bf16[256,512]{1,0:T(8,128)(2,1)}, u32[]{:S(2)}) copy-start(bf16[256,512]{1,0:T(8,128)(2,1)} %get-tuple-element.63.refs_4_) | copy-start | bytes 786436
  38.6 19.6 %copy-start = (bf16[1024,256]{1,0:T(8,128)(2,1)S(1)}, bf16[1024,256]{1,0:T(8,128)(2,1)}, u32[]{:S(2)}) copy-start(bf16[1024,256]{1,0:T(8,128)(2,1)} %shard_map.146.refs_0_) | copy-start | bytes 1572868
  43.2 14.9 %collective-permute-start.16 = (bf16[1024,256]{1,0:T(8,128)(2,1)}, bf16[1024,256]{1,0:T(8,128)(2,1)S(1)}, u32[]{:S(2)}, u32[]{:S(2)}) collective-permute-start(bf16[1024,256]{1,0:T(8,128)(2,1)} %shard_map.146.refs_0_), channel_id=1, source_target_pairs={{0,4},{2,6},{4,0},{6,2},{1,5},{3,7},{5,1},{7,3},{8,12},{10,14},{12... | collective-permute-start | bytes 1572872 | tf_op jit(solution)/shard_map/ppermute | solution.py:477
  43.4 9.6 %collective-permute-start.6 = (bf16[256,512]{1,0:T(8,128)(2,1)S(1)}, bf16[256,512]{1,0:T(8,128)(2,1)S(1)}, u32[]{:S(2)}, u32[]{:S(2)}) collective-permute-start(bf16[256,512]{1,0:T(8,128)(2,1)S(1)} %collective-permute-done.5.refs_5_), channel_id=1, source_target_pairs={{0,16},{16,24},{24,8},{8,0},{1,17},{17,25},{25,9},{9,1},{2,18},{18... | collective-permute-start | bytes 786440 | tf_op jit(solution)/shard_map/ppermute | solution.py:454
  53.0 25.5 %copy-start.13 = (bf16[256,512]{1,0:T(8,128)(2,1)}, bf16[256,512]{1,0:T(8,128)(2,1)S(1)}, u32[]{:S(2)}) copy-start(bf16[256,512]{1,0:T(8,128)(2,1)S(1)} %collective-permute-done.6.refs_6_) | copy-start | bytes 786436
  53.0 17.0 %collective-permute-start.11 = (bf16[256,1024]{1,0:T(8,128)(2,1)}, bf16[256,1024]{1,0:T(8,128)(2,1)S(1)}, u32[]{:S(2)}, u32[]{:S(2)}) collective-permute-start(bf16[256,1024]{1,0:T(8,128)(2,1)} %get-tuple-element.66), channel_id=1, source_target_pairs={{0,1},{1,0},{2,3},{3,2},{4,5},{5,4},{6,7},{7,6},{8,9},{9,8},{10,11... | collective-permute-start | bytes 1572872 | tf_op jit(solution)/shard_map/ppermute | solution.py:358
  54.6 9.3 %collective-permute-start.9 = (bf16[256,512]{1,0:T(8,128)(2,1)S(1)}, bf16[256,512]{1,0:T(8,128)(2,1)S(1)}, u32[]{:S(2)}, u32[]{:S(2)}) collective-permute-start(bf16[256,512]{1,0:T(8,128)(2,1)S(1)} %collective-permute-done.6.refs_6_), channel_id=1, source_target_pairs={{0,16},{16,24},{24,8},{8,0},{1,17},{17,25},{25,9},{9,1},{2,18},{18... | collective-permute-start | bytes 786440 | tf_op jit(solution)/shard_map/ppermute | solution.py:454
  57.0 10.4 %collective-permute-start.10 = (bf16[256,512]{1,0:T(8,128)(2,1)S(1)}, bf16[256,512]{1,0:T(8,128)(2,1)S(1)}, u32[]{:S(2)}, u32[]{:S(2)}) collective-permute-start(bf16[256,512]{1,0:T(8,128)(2,1)S(1)} %copy-done.10), channel_id=1, source_target_pairs={{0,16},{16,24},{24,8},{8,0},{1,17},{17,25},{25,9},{9,1},{2,18},{18... | collective-permute-start | bytes 786440 | tf_op jit(solution)/shard_map/ppermute | solution.py:454
  58.1 24.3 %collective-permute-start.15 = (bf16[1024,256]{1,0:T(8,128)(2,1)S(1)}, bf16[1024,256]{1,0:T(8,128)(2,1)S(1)}, u32[]{:S(2)}, u32[]{:S(2)}) collective-permute-start(bf16[1024,256]{1,0:T(8,128)(2,1)S(1)} %copy-done), channel_id=1, source_target_pairs={{0,2},{2,0},{4,6},{6,4},{1,3},{3,1},{5,7},{7,5},{8,10},{10,8},{12,... | collective-permute-start | bytes 1572872 | tf_op jit(solution)/shard_map/ppermute | solution.py:477
  58.1 18.3 %copy-start.1 = (bf16[1024,256]{1,0:T(8,128)(2,1)}, bf16[1024,256]{1,0:T(8,128)(2,1)S(1)}, u32[]{:S(2)}) copy-start(bf16[1024,256]{1,0:T(8,128)(2,1)S(1)} %collective-permute-done.16.refs_2_) | copy-start | bytes 1572868
  58.2 24.3 %collective-permute-start.17 = (bf16[1024,256]{1,0:T(8,128)(2,1)S(1)}, bf16[1024,256]{1,0:T(8,128)(2,1)S(1)}, u32[]{:S(2)}, u32[]{:S(2)}) collective-permute-start(bf16[1024,256]{1,0:T(8,128)(2,1)S(1)} %collective-permute-done.16.refs_2_), channel_id=1, source_target_pairs={{0,2},{2,0},{4,6},{6,4},{1,3},{3,1},{5,7},{7,5},{8,10},{10,8},{12,... | collective-permute-start | bytes 1572872 | tf_op jit(solution)/shard_map/ppermute | solution.py:477
  67.3 26.5 %copy-start.12 = (bf16[256,512]{1,0:T(8,128)(2,1)}, bf16[256,512]{1,0:T(8,128)(2,1)S(1)}, u32[]{:S(2)}) copy-start(bf16[256,512]{1,0:T(8,128)(2,1)S(1)} %collective-permute-done.10.refs_5_) | copy-start | bytes 786436
  67.3 12.2 %collective-permute-start.12 = (bf16[256,512]{1,0:T(8,128)(2,1)S(1)}, bf16[256,512]{1,0:T(8,128)(2,1)S(1)}, u32[]{:S(2)}, u32[]{:S(2)}) collective-permute-start(bf16[256,512]{1,0:T(8,128)(2,1)S(1)} %collective-permute-done.10.refs_5_), channel_id=1, source_target_pairs={{0,16},{16,24},{24,8},{8,0},{1,17},{17,25},{25,9},{9,1},{2,18},{18... | collective-permute-start | bytes 786440 | tf_op jit(solution)/shard_map/ppermute | solution.py:454
  78.2 10.7 %collective-permute-start.14 = (bf16[64,1024]{1,0:T(8,128)(2,1)}, bf16[64,1024]{1,0:T(8,128)(2,1)S(1)}, u32[]{:S(2)}, u32[]{:S(2)}) collective-permute-start(bf16[64,1024]{1,0:T(8,128)(2,1)} %dynamic-slice_convert_fusion), channel_id=1, source_target_pairs={{0,1},{1,0},{2,3},{3,2},{4,5},{5,4},{6,7},{7,6},{8,9},{9,8},{10,11... | collective-permute-start | bytes 393224 | tf_op jit(solution)/shard_map/ppermute | solution.py:358
  79.5 14.3 %copy-start.14 = (bf16[256,512]{1,0:T(8,128)(2,1)}, bf16[256,512]{1,0:T(8,128)(2,1)S(1)}, u32[]{:S(2)}) copy-start(bf16[256,512]{1,0:T(8,128)(2,1)S(1)} %collective-permute-done.12.refs_6_) | copy-start | bytes 786436
  79.5 20.6 %collective-permute-start.13 = (bf16[128,1024]{1,0:T(8,128)(2,1)S(1)}, bf16[128,1024]{1,0:T(8,128)(2,1)}, u32[]{:S(2)}, u32[]{:S(2)}) collective-permute-start(bf16[128,1024]{1,0:T(8,128)(2,1)S(1)} %slice.16), channel_id=1, source_target_pairs={{8,0},{16,8},{24,16},{9,1},{17,9},{25,17},{10,2},{18,10},{26,18},{... | collective-permute-start | bytes 786440 | tf_op jit(solution)/shard_map/ppermute | solution.py:508
  80.8 13.0 %collective-permute-start.19 = (bf16[256,512]{1,0:T(8,128)(2,1)S(1)}, bf16[256,512]{1,0:T(8,128)(2,1)}, u32[]{:S(2)}, u32[]{:S(2)}) collective-permute-start(bf16[256,512]{1,0:T(8,128)(2,1)S(1)} %collective-permute-done.12.refs_6_), channel_id=1, source_target_pairs={{0,16},{16,24},{24,8},{8,0},{1,17},{17,25},{25,9},{9,1},{2,18},{18... | collective-permute-start | bytes 786440 | tf_op jit(solution)/shard_map/ppermute | solution.py:454
  88.9 11.2 %collective-permute-start.18 = (bf16[64,1024]{1,0:T(8,128)(2,1)S(1)}, bf16[64,1024]{1,0:T(8,128)(2,1)S(1)}, u32[]{:S(2)}, u32[]{:S(2)}) collective-permute-start(bf16[64,1024]{1,0:T(8,128)(2,1)S(1)} %add_convert_fusion.1), channel_id=1, source_target_pairs={{0,8},{8,0},{16,24},{24,16},{1,9},{9,1},{17,25},{25,17},{2,10},{10... | collective-permute-start | bytes 393224 | tf_op jit(solution)/shard_map/ppermute | solution.py:358
  90.0 17.5 %collective-permute-start.20 = (bf16[512,512]{1,0:T(8,128)(2,1)}, bf16[512,512]{1,0:T(8,128)(2,1)S(1)}, u32[]{:S(2)}, u32[]{:S(2)}) collective-permute-start(bf16[512,512]{1,0:T(8,128)(2,1)} %get-tuple-element.86), channel_id=1, source_target_pairs={{0,1},{1,0},{2,3},{3,2},{4,5},{5,4},{6,7},{7,6},{8,9},{9,8},{10,11... | collective-permute-start | bytes 1572872 | tf_op jit(solution)/shard_map/ppermute | solution.py:358
  98.6 14.6 %collective-permute-start.23 = (bf16[512,512]{1,0:T(8,128)(2,1)}, bf16[512,512]{1,0:T(8,128)(2,1)S(1)}, u32[]{:S(2)}, u32[]{:S(2)}) collective-permute-start(bf16[512,512]{1,0:T(8,128)(2,1)} %get-tuple-element.91), channel_id=1, source_target_pairs={{0,1},{1,0},{2,3},{3,2},{4,5},{5,4},{6,7},{7,6},{8,9},{9,8},{10,11... | collective-permute-start | bytes 1572872 | tf_op jit(solution)/shard_map/ppermute | solution.py:358
  100.2 7.3 %collective-permute-start.21 = (bf16[64,1024]{1,0:T(8,128)(2,1)S(1)}, bf16[64,1024]{1,0:T(8,128)(2,1)S(1)}, u32[]{:S(2)}, u32[]{:S(2)}) collective-permute-start(bf16[64,1024]{1,0:T(8,128)(2,1)S(1)} %add_convert_fusion), channel_id=1, source_target_pairs={{0,16},{8,24},{16,0},{24,8},{1,17},{9,25},{17,1},{25,9},{2,18},{10... | collective-permute-start | bytes 393224 | tf_op jit(solution)/shard_map/ppermute | solution.py:358
  107.6 7.3 %collective-permute-start.22 = (bf16[64,1024]{1,0:T(8,128)(2,1)S(1)}, bf16[64,1024]{1,0:T(8,128)(2,1)S(1)}, u32[]{:S(2)}, u32[]{:S(2)}) collective-permute-start(bf16[64,1024]{1,0:T(8,128)(2,1)S(1)} %convert_add_fusion), channel_id=1, source_target_pairs={{0,1},{1,0},{2,3},{3,2},{4,5},{5,4},{6,7},{7,6},{8,9},{9,8},{10,11... | collective-permute-start | bytes 393224 | tf_op jit(solution)/shard_map/ppermute | solution.py:358
  (11 other events, 55.9 us)

commit v11 on v10

--- a/solution.py
+++ b/solution.py
@@ -178,16 +178,34 @@
 
 
 def lag_kernel(
-    table, synth, own_ref, other_ref, state_ref, query_ref, prior_ref, key_ref, value_ref, grad_ref, signal_ref, lag_ref
+    table,
+    synth,
+    own_ref,
+    other_ref,
+    state_ref,
+    query_ref,
+    prior_ref,
+    key_ref,
+    value_ref,
+    place_ref,
+    grad_ref,
+    signal_ref,
+    head_ref,
+    sent_lag_ref,
+    own_lag_ref,
 ):
-    length, taps = signal_ref.shape[0], lag_ref.shape[0]
+    length, taps, share = signal_ref.shape[0], prior_ref.shape[0], own_lag_ref.shape[0]
     grad_gated = own_ref[...] + other_ref[...].astype(f32)
     grad_ref[...] = (grad_gated * state_ref[...]).astype(bf16)
     signal = (grad_gated * query_ref[...].astype(f32)).astype(bf16)
     signal_ref[...] = signal
+    head_ref[...] = signal[:taps]
     spec = mixed_spectrum(table, prior_ref, key_ref, value_ref)
     product = spectrum_product(forward_transform(table, signal, 0), spec, True)
-    lag_ref[...] = -inverse_transform(synth, product, length, taps)
+    lags = -inverse_transform(synth, product, length, taps)
+    first = place_ref[...] == 0.0
+    own_lag_ref[...] = jnp.where(first, lags[:share], lags[share:])
+    sent_lag_ref[...] = jnp.where(first, lags[share:], lags[:share]).astype(bf16)
 
 
 def back_kernel(
@@ -436,15 +454,7 @@
         channels,
         unit * (4 * taps + 5 * length),
     )
-    gated[0], gated[1], moved, *rounds = lax.optimization_barrier((*gated, moved, *rounds))
-
-    route = [(tp_dp(h, c, d), tp_dp(h, (c + 1) % subs, d)) for h, c, d in places]
-    theirs = [lax.ppermute(r, ("tp", "dp"), route) for r in rounds]
-    firsts, seconds = zip(rounds, theirs)
-    same = (me_half == me_dp).astype(jnp.int32)
-    subs_of = [me_sub, (me_sub + 1) % subs]
-    place = jnp.stack([same, *subs_of]).astype(jnp.int32)
-    rows = n_tp * channels // (n_seq * n_dp)
+    dp_row = jnp.broadcast_to(me_dp.astype(f32), (1, channels))
     if square:
         order = [*range(0, n_seq, 2), *reversed(range(1, n_seq, 2))]
         ring = [(order[k], order[(k + 1) % n_seq]) for k in range(n_seq)]
@@ -461,16 +471,25 @@
                     table[s, t, t ^ holder(order[k - r], s)] = r
         sources = jnp.asarray(table)[lax.axis_index("seq"), me_tp]
         weight_place = jnp.concatenate([sources, me_dp[None].astype(jnp.int32)])
-        moved = transposed(moved)
-        halves[0][1], moved, place, weight_place = lax.optimization_barrier(
-            (halves[0][1], moved, place, weight_place)
+        halves[0][1], halves[1][0], weight_place, dp_row, moved, *rounds = lax.optimization_barrier(
+            (halves[0][1], halves[1][0], weight_place, dp_row, moved, *rounds)
         )
         ring_step(halves[0])
+        ring_step(halves[1])
+        moved = transposed(moved)
+    else:
+        gated[0], *rounds = lax.optimization_barrier((gated[0], *rounds))
+
+    route = [(tp_dp(h, c, d), tp_dp(h, (c + 1) % subs, d)) for h, c, d in places]
+    theirs = [lax.ppermute(r, ("tp", "dp"), route) for r in rounds]
+    firsts, seconds = zip(rounds, theirs)
+    same = (me_half == me_dp).astype(jnp.int32)
+    subs_of = [me_sub, (me_sub + 1) % subs]
+    place = jnp.stack([same, *subs_of]).astype(jnp.int32)
+    rows = n_tp * channels // (n_seq * n_dp)
+    if square:
+        moved, place = lax.optimization_barrier((moved, place))
     other_sent, own_part = project(place, firsts, seconds, out_weight)
-    if square:
-        halves[0][2], halves[1][0], other_sent = lax.optimization_barrier(
-            (halves[0][2], halves[1][0], other_sent)
-        )
     other_part = swap_pairs(other_sent, "dp", 1)
 
     if square:
@@ -479,10 +498,9 @@
         cot_pieces = [moved, sent_by(moved, 1), across, sent_by(after(across, halves[0][2]), 1)]
         ring_step(halves[0])
         ring_step(halves[1])
-        halves[0][3], halves[1][1], own_part = lax.optimization_barrier(
-            (halves[0][3], halves[1][1], own_part)
+        halves[0][3], halves[1][2], own_part = lax.optimization_barrier(
+            (halves[0][3], halves[1][2], own_part)
         )
-        ring_step(halves[1])
     else:
         full = lax.all_gather(cot, "tp", axis=1, tiled=True)
         cot_all = lax.all_to_all(full, "seq", 1, 0, tiled=True)
@@ -497,15 +515,22 @@
         def weight_one(piece):
             return part(me_dp, piece), swap_pairs(part(1 - me_dp, piece).astype(bf16), "dp", 1)
 
-    grad_query, signal, lags = by_channel(
+    share = taps // n_dp
+    grad_query, signal, head, sent_lag, own_lag = by_channel(
         lag_kernel,
         tables,
-        [own_part, other_part, state, queries, prior, key_rows, value_rows],
-        [[rows16], [rows16], [jax.ShapeDtypeStruct((taps, channels), f32)]],
+        [own_part, other_part, state, queries, prior, key_rows, value_rows, dp_row],
+        [
+            [rows16],
+            [rows16],
+            [jax.ShapeDtypeStruct((taps, channels), bf16)],
+            [jax.ShapeDtypeStruct((share, channels), bf16)],
+            [jax.ShapeDtypeStruct((share, channels), f32)],
+        ],
         channels,
         unit * (2 * taps + 4 * length + 3 * taps),
     )
-    later = lax.ppermute(signal[:taps], "seq", [(i + 1, i) for i in range(n_seq - 1)])
+    later = lax.ppermute(head, "seq", [(i + 1, i) for i in range(n_seq - 1)])
 
     def run_back(later):
         return by_channel(
@@ -517,17 +542,14 @@
             256 * unit * (4 * taps + 5 * length),
         )
 
-    share = taps // n_dp
-    received = swap_pairs(
-        lax.dynamic_slice_in_dim(lags, (1 - me_dp) * share, share, axis=0).astype(bf16), "dp", 1
-    )
-    if square:
-        weight_place, halves[1][2], signal = lax.optimization_barrier((weight_place, halves[1][2], signal))
+    received = swap_pairs(sent_lag, "dp", 1)
+    if square:
         ring_step(halves[1])
+        weight_place, signal = lax.optimization_barrier((weight_place, signal))
         first_sent, first_own = weight_sum(weight_place, cot_pieces, halves[0], rows)
         first_received = swap_pairs(first_sent, "dp", 1)
         received, first_own = lax.optimization_barrier((received, first_own))
-    lag_sum = lax.dynamic_slice_in_dim(lags, me_dp * share, share, axis=0) + received.astype(f32)
+    lag_sum = own_lag + received.astype(f32)
     distance = 1
     while distance < n_seq:
         rounded = lag_sum.astype(bf16)

time: 117 us -> 122 us (1.043)
  starting transfers between devices: 37.3 us -> 42.9 us
  local copies, waits for them, and re-layouts: 8.14 us -> 6.12 us
  waiting for transfers between devices: 29.9 us -> 31.4 us
    ppermute x2, waiting for transfers between devices: 5.19 us -> 0.01 us  [per_device(): lax.ppermute(after(cot, prior) if turn else cot, ('tp', 'dp'), route)]
    ppermute x6, starting transfers between devices: 10.5 us -> 14.1 us  [ring_step(): pieces.append(lax.ppermute(pieces[-1], 'seq', ring))]
    ppermute x7, waiting for transfers between devices: 6.54 us -> 10.1 us  [swap_pairs(): return lax.ppermute(value, axis, [(i, i ^ distance) for i in range(count)])]
    ppermute x7, starting transfers between devices: 7 us -> 10.5 us  [swap_pairs(): return lax.ppermute(value, axis, [(i, i ^ distance) for i in range(count)])]
    ppermute x3, waiting for transfers between devices: 0.01 us -> 2.36 us  [per_device(): lax.ppermute(value, 'tp', [(t, t ^ flip) for t in range(n_tp)])]
    convert_element_type x1 -> x0, local copies, waits for them, and re-layouts: 1.68 us -> none  [per_device(): lax.dynamic_slice_in_dim(lags, (1 - me_dp) * share, share, axis=0)]
  transfers between devices with their start and end apart: 24 -> 24, of which waited for: 8 -> 8; matrix products, arithmetic and copies ran while one was open for 7% -> 4% of each run, Pallas kernels for 30% -> 29%
where the time goes in v11:
time: 122 us
  starting transfers between devices  42.9 us (35%)
  Pallas kernels  34.9 us (29%)
  waiting for transfers between devices  31.4 us (26%)
  local copies, waits for them, and re-layouts  6.12 us (5%)
  other arithmetic  5.4 us (4%)
    pallas_call x3, Pallas kernels, by_channel(): pl.pallas_call(kernel, in_specs=[pl.BlockSpec(memory_space=pl.ANY)] * (n_...  16.8 us
    ppermute x6, waiting for transfers between devices, ring_step(): pieces.append(lax.ppermute(pieces[-1], 'seq', ring))  16.1 us
    pallas_call x3, Pallas kernels, local_call(): pl.pallas_call(kernel, in_specs=[pl.BlockSpec(memory_space=pltpu.SMEM)] +...  16 us
    ppermute x6, starting transfers between devices, ring_step(): pieces.append(lax.ppermute(pieces[-1], 'seq', ring))  14.1 us
    ppermute x7, starting transfers between devices, swap_pairs(): return lax.ppermute(value, axis, [(i, i ^ distance) for i in range(count)])  10.5 us
    ppermute x7, waiting for transfers between devices, swap_pairs(): return lax.ppermute(value, axis, [(i, i ^ distance) for i in range(count)])  10.1 us
    ppermute x1, starting transfers between devices, per_device(): prior = lax.ppermute(tail, 'seq', [(i, i + 1) for i in range(n_seq - 1)])  7.09 us
    ppermute x2, starting transfers between devices, per_device(): theirs = [lax.ppermute(r, ('tp', 'dp'), route) for r in rounds]  6.02 us
  transfers between devices with their start and end apart: 24, of which 8 were waited for; matrix products, arithmetic and copies ran while one was open for 4% of the time, Pallas kernels for 29%

profile of v11, /device:TPU:0, one launch (start us, length us, event | category | flops | bytes accessed | tf_op | source)
XLA Modules:
  0.0 121.6 jit_solution(10312141791123779329)
XLA Ops:
  0.6 1.1 fusion
  2.4 7.1 %collective-permute-start = (bf16[128,1024]{1,0:T(8,128)(2,1)S(1)}, bf16[128,1024]{1,0:T(8,128)(2,1)S(1)}, u32[]{:S(2)}, u32[]{:S(2)}) collective-permute-start(bf16[128,1024]{1,0:T(8,128)(2,1)S(1)} %fusion), channel_id=1, source_target_pairs={{0,8},{8,16},{16,24},{1,9},{9,17},{17,25},{2,10},{10,18},{18,26},{... | collective-permute-start | bytes 786440 | tf_op jit(solution)/shard_map/ppermute | solution.py:411
  9.5 1.7 %collective-permute-start.4 = (bf16[256,1024]{1,0:T(8,128)(2,1)}, bf16[256,1024]{1,0:T(8,128)(2,1)S(1)}, u32[]{:S(2)}, u32[]{:S(2)}) collective-permute-start(bf16[256,1024]{1,0:T(8,128)(2,1)} %bitcast.28), channel_id=1, source_target_pairs={{0,0},{1,4},{2,2},{3,6},{4,1},{5,5},{6,3},{7,7},{8,8},{9,12},{10,1... | collective-permute-start | bytes 1572872 | tf_op jit(solution)/shard_map/ppermute | solution.py:420
  11.2 2.8 %collective-permute-done.refs_2_.refs_6_ = bf16[128,1024]{1,0:T(8,128)(2,1)S(1)} collective-permute-done((bf16[128,1024]{1,0:T(8,128)(2,1)S(1)}, bf16[128,1024]{1,0:T(8,128)(2,1)S(1)}, u32[]{:S(2)}, u32[]{:S(2)}) %collective-permute-start) | collective-permute-done | bytes 262176 | tf_op jit(solution)/shard_map/ppermute | solution.py:411
  14.7 1.1 broadcast_select_fusion
  16.5 5.5 %shard_map.145 = (f32[256,1024]{1,0:T(8,128)}, bf16[256,512]{1,0:T(8,128)(2,1)}, bf16[256,512]{1,0:T(8,128)(2,1)}) custom-call(bf16[768,384]{1,0:T(8,128)(2,1)} %constant.65.clone.refs_0_, bf16[768,384]{1,0:T(8,128)(2,1)} %constant.66.clone.refs_1_, bf16[128,1024]{1,0:T(8,128)(2,1)} %copy-done.4, bf16[256,1024]{1,0:T(8,128)(2,1)} %bitcast.22, ...), custom_call_target="tpu_custom_call" | custom-call | flops 22020096 | bytes 57408 | tf_op jit(solution)/shard_map/pallas_call | solution.py:275
  22.1 5.3 %collective-permute-start.1 = (bf16[256,512]{1,0:T(8,128)(2,1)}, bf16[256,512]{1,0:T(8,128)(2,1)S(1)}, u32[]{:S(2)}, u32[]{:S(2)}) collective-permute-start(bf16[256,512]{1,0:T(8,128)(2,1)} %get-tuple-element.48.refs_4_), channel_id=1, source_target_pairs={{0,16},{16,24},{24,8},{8,0},{1,17},{17,25},{25,9},{9,1},{2,18},{18... | collective-permute-start | bytes 786440 | tf_op jit(solution)/shard_map/ppermute | solution.py:464
  28.6 5.2 %collective-permute-done.1.refs_5_ = bf16[256,512]{1,0:T(8,128)(2,1)S(1)} collective-permute-done((bf16[256,512]{1,0:T(8,128)(2,1)}, bf16[256,512]{1,0:T(8,128)(2,1)S(1)}, u32[]{:S(2)}, u32[]{:S(2)}) %collective-permute-start.1) | collective-permute-done | bytes 262176 | tf_op jit(solution)/shard_map/ppermute | solution.py:464
  34.5 6.0 %collective-permute-start.10 = (bf16[256,1024]{1,0:T(8,128)(2,1)S(1)}, bf16[256,1024]{1,0:T(8,128)(2,1)}, u32[]{:S(2)}, u32[]{:S(2)}) collective-permute-start(bf16[256,1024]{1,0:T(8,128)(2,1)S(1)} %collective-permute-done.4.first_mine), channel_id=1, source_target_pairs={{0,2},{1,3},{2,0},{3,1},{4,6},{5,7},{6,4},{7,5},{8,10},{9,11},{10,... | collective-permute-start | bytes 1572872 | tf_op jit(solution)/shard_map/ppermute | solution.py:484
  41.2 2.1 %shard_map.146.refs_0_ = bf16[1024,256]{1,0:T(8,128)(2,1)} custom-call(bf16[256,1024]{1,0:T(8,128)(2,1)} %copy-done.8), custom_call_target="tpu_custom_call" | custom-call | bytes 16384 | tf_op jit(solution)/shard_map/pallas_call | solution.py:359
  43.4 3.0 %collective-permute-start.6 = (bf16[256,512]{1,0:T(8,128)(2,1)S(1)}, bf16[256,512]{1,0:T(8,128)(2,1)S(1)}, u32[]{:S(2)}, u32[]{:S(2)}) collective-permute-start(bf16[256,512]{1,0:T(8,128)(2,1)S(1)} %collective-permute-done.1.refs_5_), channel_id=1, source_target_pairs={{0,16},{16,24},{24,8},{8,0},{1,17},{17,25},{25,9},{9,1},{2,18},{18... | collective-permute-start | bytes 786440 | tf_op jit(solution)/shard_map/ppermute | solution.py:464
  47.1 6.4 %shard_map.147 = (bf16[256,1024]{1,0:T(8,128)(2,1)}, f32[256,1024]{1,0:T(8,128)}) custom-call(s32[3]{0:T(128)} %pad_add_fusion.1.place_ref, bf16[256,1024]{1,0:T(8,128)(2,1)} %copy-done.16, bf16[256,1024]{1,0:T(8,128)(2,1)} %copy-done.17, bf16[256,1024]{1,0:T(8,128)(2,1)} %collective-permute-done.10.first_theirs, ...), custom_call_target="tpu_custom_call" | custom-call | flops 2147483648 | bytes 122880 | tf_op jit(solution)/shard_map/pallas_call | solution.py:294
  53.4 2.1 %collective-permute-start.12 = (bf16[256,1024]{1,0:T(8,128)(2,1)}, bf16[256,1024]{1,0:T(8,128)(2,1)S(1)}, u32[]{:S(2)}, u32[]{:S(2)}) collective-permute-start(bf16[256,1024]{1,0:T(8,128)(2,1)} %get-tuple-element.60), channel_id=1, source_target_pairs={{0,1},{1,0},{2,3},{3,2},{4,5},{5,4},{6,7},{7,6},{8,9},{9,8},{10,11... | collective-permute-start | bytes 1572872 | tf_op jit(solution)/shard_map/ppermute | solution.py:376
  55.5 2.4 %collective-permute-done.16.refs_2_ = bf16[1024,256]{1,0:T(8,128)(2,1)S(1)} collective-permute-done((bf16[1024,256]{1,0:T(8,128)(2,1)}, bf16[1024,256]{1,0:T(8,128)(2,1)S(1)}, u32[]{:S(2)}, u32[]{:S(2)}) %collective-permute-start.16) | collective-permute-done | bytes 524320 | tf_op jit(solution)/shard_map/ppermute | solution.py:496
  57.9 1.3 %collective-permute-start.7 = (bf16[256,512]{1,0:T(8,128)(2,1)S(1)}, bf16[256,512]{1,0:T(8,128)(2,1)S(1)}, u32[]{:S(2)}, u32[]{:S(2)}) collective-permute-start(bf16[256,512]{1,0:T(8,128)(2,1)S(1)} %collective-permute-done.6.refs_6_), channel_id=1, source_target_pairs={{0,16},{16,24},{24,8},{8,0},{1,17},{17,25},{25,9},{9,1},{2,18},{18... | collective-permute-start | bytes 786440 | tf_op jit(solution)/shard_map/ppermute | solution.py:464
  59.2 2.1 %collective-permute-start.9 = (bf16[256,512]{1,0:T(8,128)(2,1)S(1)}, bf16[256,512]{1,0:T(8,128)(2,1)S(1)}, u32[]{:S(2)}, u32[]{:S(2)}) collective-permute-start(bf16[256,512]{1,0:T(8,128)(2,1)S(1)} %collective-permute-done.8.refs_5_), channel_id=1, source_target_pairs={{0,16},{16,24},{24,8},{8,0},{1,17},{17,25},{25,9},{9,1},{2,18},{18... | collective-permute-start | bytes 786440 | tf_op jit(solution)/shard_map/ppermute | solution.py:464
  61.4 5.7 %collective-permute-done.7.refs_7_ = bf16[256,512]{1,0:T(8,128)(2,1)S(1)} collective-permute-done((bf16[256,512]{1,0:T(8,128)(2,1)S(1)}, bf16[256,512]{1,0:T(8,128)(2,1)S(1)}, u32[]{:S(2)}, u32[]{:S(2)}) %collective-permute-start.7) | collective-permute-done | bytes 262176 | tf_op jit(solution)/shard_map/ppermute | solution.py:464
  67.0 5.2 %collective-permute-done.9.refs_6_ = bf16[256,512]{1,0:T(8,128)(2,1)S(1)} collective-permute-done((bf16[256,512]{1,0:T(8,128)(2,1)S(1)}, bf16[256,512]{1,0:T(8,128)(2,1)S(1)}, u32[]{:S(2)}, u32[]{:S(2)}) %collective-permute-start.9) | collective-permute-done | bytes 262176 | tf_op jit(solution)/shard_map/ppermute | solution.py:464
  72.3 0.8 copy-done.7
  73.1 5.8 %shard_map.148 = (bf16[256,1024]{1,0:T(8,128)(2,1)}, bf16[256,1024]{1,0:T(8,128)(2,1)}, bf16[128,1024]{1,0:T(8,128)(2,1)}, bf16[64,1024]{1,0:T(8,128)(2,1)}, f32[64,1024]{1,0:T(8,128)}) custom-call(bf16[768,384]{1,0:T(8,128)(2,1)} %constant.65.clone.refs_0_, bf16[768,384]{1,0:T(8,128)(2,1)} %constant.66.clone.refs_1_, ...), custom_call_target="tpu_custom_call" | custom-call | flops 20447232 | bytes 96320 | tf_op jit(solution)/shard_map/pallas_call | solution.py:275
  79.0 1.9 %collective-permute-start.14 = (bf16[64,1024]{1,0:T(8,128)(2,1)}, bf16[64,1024]{1,0:T(8,128)(2,1)S(1)}, u32[]{:S(2)}, u32[]{:S(2)}) collective-permute-start(bf16[64,1024]{1,0:T(8,128)(2,1)} %get-tuple-element.69), channel_id=1, source_target_pairs={{0,1},{1,0},{2,3},{3,2},{4,5},{5,4},{6,7},{7,6},{8,9},{9,8},{10,11... | collective-permute-start | bytes 393224 | tf_op jit(solution)/shard_map/ppermute | solution.py:376
  80.8 1.8 %collective-permute-start.19 = (bf16[256,512]{1,0:T(8,128)(2,1)S(1)}, bf16[256,512]{1,0:T(8,128)(2,1)S(1)}, u32[]{:S(2)}, u32[]{:S(2)}) collective-permute-start(bf16[256,512]{1,0:T(8,128)(2,1)S(1)} %collective-permute-done.9.refs_6_), channel_id=1, source_target_pairs={{0,16},{16,24},{24,8},{8,0},{1,17},{17,25},{25,9},{9,1},{2,18},{18... | collective-permute-start | bytes 786440 | tf_op jit(solution)/shard_map/ppermute | solution.py:464
  82.6 1.3 %collective-permute-start.13 = (bf16[128,1024]{1,0:T(8,128)(2,1)}, bf16[128,1024]{1,0:T(8,128)(2,1)S(1)}, u32[]{:S(2)}, u32[]{:S(2)}) collective-permute-start(bf16[128,1024]{1,0:T(8,128)(2,1)} %get-tuple-element.67), channel_id=1, source_target_pairs={{8,0},{16,8},{24,16},{9,1},{17,9},{25,17},{10,2},{18,10},{26,18},{... | collective-permute-start | bytes 786440 | tf_op jit(solution)/shard_map/ppermute | solution.py:533
  85.5 4.8 %shard_map.149 = (bf16[512,512]{1,0:T(8,128)(2,1)}, f32[512,512]{1,0:T(8,128)}) custom-call(s32[5]{0:T(128)} %pad_add_fusion.place_ref, bf16[1024,256]{1,0:T(8,128)(2,1)} %shard_map.146.refs_0_, bf16[1024,256]{1,0:T(8,128)(2,1)} %copy-done.2, bf16[1024,256]{1,0:T(8,128)(2,1)} %copy-done.1, bf16[1024,256]{1,0:T(8,128)(2,1)} %copy-done.3, ...), custom_call_target="tpu_custom_call" | custom-call | flops 16777216 | bytes 73728 | tf_op jit(solution)/shard_map/pallas_call | solution.py:294
  90.3 2.7 %collective-permute-start.18 = (bf16[64,1024]{1,0:T(8,128)(2,1)S(1)}, bf16[64,1024]{1,0:T(8,128)(2,1)S(1)}, u32[]{:S(2)}, u32[]{:S(2)}) collective-permute-start(bf16[64,1024]{1,0:T(8,128)(2,1)S(1)} %add_convert_fusion.1), channel_id=1, source_target_pairs={{0,8},{8,0},{16,24},{24,16},{1,9},{9,1},{17,25},{25,17},{2,10},{10... | collective-permute-start | bytes 393224 | tf_op jit(solution)/shard_map/ppermute | solution.py:376
  94.4 4.8 %shard_map.150 = (bf16[512,512]{1,0:T(8,128)(2,1)}, f32[512,512]{1,0:T(8,128)}) custom-call(s32[5]{0:T(128)} %pad_add_fusion.place_ref, bf16[1024,256]{1,0:T(8,128)(2,1)} %shard_map.146.refs_0_, bf16[1024,256]{1,0:T(8,128)(2,1)} %copy-done.2, bf16[1024,256]{1,0:T(8,128)(2,1)} %copy-done.1, bf16[1024,256]{1,0:T(8,128)(2,1)} %copy-done.3, ...), custom_call_target="tpu_custom_call" | custom-call | flops 16777216 | bytes 73728 | tf_op jit(solution)/shard_map/pallas_call | solution.py:294
  99.2 1.4 %collective-permute-start.23 = (bf16[512,512]{1,0:T(8,128)(2,1)}, bf16[512,512]{1,0:T(8,128)(2,1)S(1)}, u32[]{:S(2)}, u32[]{:S(2)}) collective-permute-start(bf16[512,512]{1,0:T(8,128)(2,1)} %get-tuple-element.87), channel_id=1, source_target_pairs={{0,1},{1,0},{2,3},{3,2},{4,5},{5,4},{6,7},{7,6},{8,9},{9,8},{10,11... | collective-permute-start | bytes 1572872 | tf_op jit(solution)/shard_map/ppermute | solution.py:376
  100.7 1.1 collective-permute-start.21
  101.8 5.5 %shard_map.151 = (bf16[256,1024]{1,0:T(8,128)(2,1)}, bf16[256,1024]{1,0:T(8,128)(2,1)}) custom-call(bf16[768,384]{1,0:T(8,128)(2,1)} %constant.65.clone.refs_0_, bf16[768,384]{1,0:T(8,128)(2,1)} %constant.66.clone.refs_1_, bf16[256,1024]{1,0:T(8,128)(2,1)} %get-tuple-element.66.refs_2_, bf16[128,1024]{1,0:T(8,128)(2,1)} %copy-done.18, ...), custom_call_target="tpu_custom_call" | custom-call | flops 5637144576 | bytes 49216 | tf_op jit(solution)/shard_map/pallas_call | solution.py:275
  109.0 9.4 %collective-permute-done.23 = bf16[512,512]{1,0:T(8,128)(2,1)S(1)} collective-permute-done((bf16[512,512]{1,0:T(8,128)(2,1)}, bf16[512,512]{1,0:T(8,128)(2,1)S(1)}, u32[]{:S(2)}, u32[]{:S(2)}) %collective-permute-start.23) | collective-permute-done | bytes 524320 | tf_op jit(solution)/shard_map/ppermute | solution.py:376
  118.5 1.5 %pad_maximum_fusion = f32[512,1024]{1,0:T(8,128)} fusion(f32[512,512]{1,0:T(8,128)S(1)} %add_multiply_fusion, f32[512,512]{1,0:T(8,128)S(1)} %add_multiply_fusion.1), kind=kLoop, calls=%fused_computation | loop fusion | flops 524288 | bytes 4194304 | tf_op jit(solution)/shard_map/concatenate | solution.py:576
  120.0 1.0 copy.16
  (77 shorter events, 11.0 us)
Async XLA Ops:
  1.7 12.9 %collective-permute-start.2 = (bf16[256,1024]{1,0:T(8,128)(2,1)}, bf16[256,1024]{1,0:T(8,128)(2,1)S(1)}, u32[]{:S(2)}, u32[]{:S(2)}) collective-permute-start(bf16[256,1024]{1,0:T(8,128)(2,1)} %bitcast.27), channel_id=1, source_target_pairs={{2,4},{4,2},{8,14},{14,8},{18,20},{20,18},{24,30},{30,24},{3,5},{5... | collective-permute-start | bytes 1572872 | tf_op jit(solution)/shard_map/ppermute | solution.py:433
  2.4 11.6 %collective-permute-start = (bf16[128,1024]{1,0:T(8,128)(2,1)S(1)}, bf16[128,1024]{1,0:T(8,128)(2,1)S(1)}, u32[]{:S(2)}, u32[]{:S(2)}) collective-permute-start(bf16[128,1024]{1,0:T(8,128)(2,1)S(1)} %fusion), channel_id=1, source_target_pairs={{0,8},{8,16},{16,24},{1,9},{9,17},{17,25},{2,10},{10,18},{18,26},{... | collective-permute-start | bytes 786440 | tf_op jit(solution)/shard_map/ppermute | solution.py:411
  9.5 24.2 %collective-permute-start.4 = (bf16[256,1024]{1,0:T(8,128)(2,1)}, bf16[256,1024]{1,0:T(8,128)(2,1)S(1)}, u32[]{:S(2)}, u32[]{:S(2)}) collective-permute-start(bf16[256,1024]{1,0:T(8,128)(2,1)} %bitcast.28), channel_id=1, source_target_pairs={{0,0},{1,4},{2,2},{3,6},{4,1},{5,5},{6,3},{7,7},{8,8},{9,12},{10,1... | collective-permute-start | bytes 1572872 | tf_op jit(solution)/shard_map/ppermute | solution.py:420
  14.0 19.8 %collective-permute-start.5 = (bf16[256,1024]{1,0:T(8,128)(2,1)}, bf16[256,1024]{1,0:T(8,128)(2,1)S(1)}, u32[]{:S(2)}, u32[]{:S(2)}) collective-permute-start(bf16[256,1024]{1,0:T(8,128)(2,1)} %bitcast.29), channel_id=1, source_target_pairs={{0,4},{1,0},{2,6},{3,2},{4,5},{5,1},{6,7},{7,3},{8,12},{9,8},{10,1... | collective-permute-start | bytes 1572872 | tf_op jit(solution)/shard_map/ppermute | solution.py:420
  15.8 18.0 %collective-permute-start.3 = (bf16[256,1024]{1,0:T(8,128)(2,1)S(1)}, bf16[256,1024]{1,0:T(8,128)(2,1)S(1)}, u32[]{:S(2)}, u32[]{:S(2)}) collective-permute-start(bf16[256,1024]{1,0:T(8,128)(2,1)S(1)} %broadcast_select_fusion), channel_id=1, source_target_pairs={{0,0},{2,16},{4,12},{6,28},{8,24},{10,8},{12,20},{14,4},{16,2},{18... | collective-permute-start | bytes 1572872 | tf_op jit(solution)/shard_map/ppermute | solution.py:445
  22.1 11.7 %collective-permute-start.1 = (bf16[256,512]{1,0:T(8,128)(2,1)}, bf16[256,512]{1,0:T(8,128)(2,1)S(1)}, u32[]{:S(2)}, u32[]{:S(2)}) collective-permute-start(bf16[256,512]{1,0:T(8,128)(2,1)} %get-tuple-element.48.refs_4_), channel_id=1, source_target_pairs={{0,16},{16,24},{24,8},{8,0},{1,17},{17,25},{25,9},{9,1},{2,18},{18... | collective-permute-start | bytes 786440 | tf_op jit(solution)/shard_map/ppermute | solution.py:464
  33.8 45.1 %copy-start.10 = (bf16[256,512]{1,0:T(8,128)(2,1)}, bf16[256,512]{1,0:T(8,128)(2,1)S(1)}, u32[]{:S(2)}) copy-start(bf16[256,512]{1,0:T(8,128)(2,1)S(1)} %collective-permute-done.1.refs_5_) | copy-start | bytes 786436
  33.8 13.3 %copy-start.16 = (bf16[256,1024]{1,0:T(8,128)(2,1)}, bf16[256,1024]{1,0:T(8,128)(2,1)S(1)}, u32[]{:S(2)}) copy-start(bf16[256,1024]{1,0:T(8,128)(2,1)S(1)} %collective-permute-done.4.first_mine) | copy-start | bytes 1572868
  33.8 13.3 %copy-start.17 = (bf16[256,1024]{1,0:T(8,128)(2,1)}, bf16[256,1024]{1,0:T(8,128)(2,1)S(1)}, u32[]{:S(2)}) copy-start(bf16[256,1024]{1,0:T(8,128)(2,1)S(1)} %collective-permute-done.5.second_mine) | copy-start | bytes 1572868
  34.5 12.5 %collective-permute-start.10 = (bf16[256,1024]{1,0:T(8,128)(2,1)S(1)}, bf16[256,1024]{1,0:T(8,128)(2,1)}, u32[]{:S(2)}, u32[]{:S(2)}) collective-permute-start(bf16[256,1024]{1,0:T(8,128)(2,1)S(1)} %collective-permute-done.4.first_mine), channel_id=1, source_target_pairs={{0,2},{1,3},{2,0},{3,1},{4,6},{5,7},{6,4},{7,5},{8,10},{9,11},{10,... | collective-permute-start | bytes 1572872 | tf_op jit(solution)/shard_map/ppermute | solution.py:484
  40.5 6.5 %collective-permute-start.11 = (bf16[256,1024]{1,0:T(8,128)(2,1)S(1)}, bf16[256,1024]{1,0:T(8,128)(2,1)}, u32[]{:S(2)}, u32[]{:S(2)}) collective-permute-start(bf16[256,1024]{1,0:T(8,128)(2,1)S(1)} %collective-permute-done.5.second_mine), channel_id=1, source_target_pairs={{0,2},{1,3},{2,0},{3,1},{4,6},{5,7},{6,4},{7,5},{8,10},{9,11},{10,... | collective-permute-start | bytes 1572872 | tf_op jit(solution)/shard_map/ppermute | solution.py:484
  43.3 14.6 %collective-permute-start.16 = (bf16[1024,256]{1,0:T(8,128)(2,1)}, bf16[1024,256]{1,0:T(8,128)(2,1)S(1)}, u32[]{:S(2)}, u32[]{:S(2)}) collective-permute-start(bf16[1024,256]{1,0:T(8,128)(2,1)} %shard_map.146.refs_0_), channel_id=1, source_target_pairs={{0,4},{2,6},{4,0},{6,2},{1,5},{3,7},{5,1},{7,3},{8,12},{10,14},{12... | collective-permute-start | bytes 1572872 | tf_op jit(solution)/shard_map/ppermute | solution.py:496
  43.4 12.1 %collective-permute-start.6 = (bf16[256,512]{1,0:T(8,128)(2,1)S(1)}, bf16[256,512]{1,0:T(8,128)(2,1)S(1)}, u32[]{:S(2)}, u32[]{:S(2)}) collective-permute-start(bf16[256,512]{1,0:T(8,128)(2,1)S(1)} %collective-permute-done.1.refs_5_), channel_id=1, source_target_pairs={{0,16},{16,24},{24,8},{8,0},{1,17},{17,25},{25,9},{9,1},{2,18},{18... | collective-permute-start | bytes 786440 | tf_op jit(solution)/shard_map/ppermute | solution.py:464
  46.4 12.8 %collective-permute-start.8 = (bf16[256,512]{1,0:T(8,128)(2,1)}, bf16[256,512]{1,0:T(8,128)(2,1)S(1)}, u32[]{:S(2)}, u32[]{:S(2)}) collective-permute-start(bf16[256,512]{1,0:T(8,128)(2,1)} %get-tuple-element.53.refs_4_), channel_id=1, source_target_pairs={{0,16},{16,24},{24,8},{8,0},{1,17},{17,25},{25,9},{9,1},{2,18},{18... | collective-permute-start | bytes 786440 | tf_op jit(solution)/shard_map/ppermute | solution.py:464
  53.4 18.8 %collective-permute-start.12 = (bf16[256,1024]{1,0:T(8,128)(2,1)}, bf16[256,1024]{1,0:T(8,128)(2,1)S(1)}, u32[]{:S(2)}, u32[]{:S(2)}) collective-permute-start(bf16[256,1024]{1,0:T(8,128)(2,1)} %get-tuple-element.60), channel_id=1, source_target_pairs={{0,1},{1,0},{2,3},{3,2},{4,5},{5,4},{6,7},{7,6},{8,9},{9,8},{10,11... | collective-permute-start | bytes 1572872 | tf_op jit(solution)/shard_map/ppermute | solution.py:376
  55.5 28.3 %collective-permute-start.15 = (bf16[1024,256]{1,0:T(8,128)(2,1)S(1)}, bf16[1024,256]{1,0:T(8,128)(2,1)S(1)}, u32[]{:S(2)}, u32[]{:S(2)}) collective-permute-start(bf16[1024,256]{1,0:T(8,128)(2,1)S(1)} %copy-done), channel_id=1, source_target_pairs={{0,2},{2,0},{4,6},{6,4},{1,3},{3,1},{5,7},{7,5},{8,10},{10,8},{12,... | collective-permute-start | bytes 1572872 | tf_op jit(solution)/shard_map/ppermute | solution.py:496
  55.5 28.4 %copy-start.12 = (bf16[256,512]{1,0:T(8,128)(2,1)}, bf16[256,512]{1,0:T(8,128)(2,1)S(1)}, u32[]{:S(2)}) copy-start(bf16[256,512]{1,0:T(8,128)(2,1)S(1)} %collective-permute-done.6.refs_6_) | copy-start | bytes 786436
  57.9 21.0 %copy-start.1 = (bf16[1024,256]{1,0:T(8,128)(2,1)}, bf16[1024,256]{1,0:T(8,128)(2,1)S(1)}, u32[]{:S(2)}) copy-start(bf16[1024,256]{1,0:T(8,128)(2,1)S(1)} %collective-permute-done.16.refs_2_) | copy-start | bytes 1572868
  57.9 26.0 %collective-permute-start.17 = (bf16[1024,256]{1,0:T(8,128)(2,1)S(1)}, bf16[1024,256]{1,0:T(8,128)(2,1)S(1)}, u32[]{:S(2)}, u32[]{:S(2)}) collective-permute-start(bf16[1024,256]{1,0:T(8,128)(2,1)S(1)} %collective-permute-done.16.refs_2_), channel_id=1, source_target_pairs={{0,2},{2,0},{4,6},{6,4},{1,3},{3,1},{5,7},{7,5},{8,10},{10,8},{12,... | collective-permute-start | bytes 1572872 | tf_op jit(solution)/shard_map/ppermute | solution.py:496
  57.9 9.1 %collective-permute-start.7 = (bf16[256,512]{1,0:T(8,128)(2,1)S(1)}, bf16[256,512]{1,0:T(8,128)(2,1)S(1)}, u32[]{:S(2)}, u32[]{:S(2)}) collective-permute-start(bf16[256,512]{1,0:T(8,128)(2,1)S(1)} %collective-permute-done.6.refs_6_), channel_id=1, source_target_pairs={{0,16},{16,24},{24,8},{8,0},{1,17},{17,25},{25,9},{9,1},{2,18},{18... | collective-permute-start | bytes 786440 | tf_op jit(solution)/shard_map/ppermute | solution.py:464
  59.2 34.5 %copy-start.11 = (bf16[256,512]{1,0:T(8,128)(2,1)}, bf16[256,512]{1,0:T(8,128)(2,1)S(1)}, u32[]{:S(2)}) copy-start(bf16[256,512]{1,0:T(8,128)(2,1)S(1)} %collective-permute-done.8.refs_5_) | copy-start | bytes 786436
  59.2 13.0 %collective-permute-start.9 = (bf16[256,512]{1,0:T(8,128)(2,1)S(1)}, bf16[256,512]{1,0:T(8,128)(2,1)S(1)}, u32[]{:S(2)}, u32[]{:S(2)}) collective-permute-start(bf16[256,512]{1,0:T(8,128)(2,1)S(1)} %collective-permute-done.8.refs_5_), channel_id=1, source_target_pairs={{0,16},{16,24},{24,8},{8,0},{1,17},{17,25},{25,9},{9,1},{2,18},{18... | collective-permute-start | bytes 786440 | tf_op jit(solution)/shard_map/ppermute | solution.py:464
  67.0 16.9 %copy-start.14 = (bf16[256,512]{1,0:T(8,128)(2,1)}, bf16[256,512]{1,0:T(8,128)(2,1)S(1)}, u32[]{:S(2)}) copy-start(bf16[256,512]{1,0:T(8,128)(2,1)S(1)} %collective-permute-done.7.refs_7_) | copy-start | bytes 786436
  72.2 21.5 %copy-start.13 = (bf16[256,512]{1,0:T(8,128)(2,1)}, bf16[256,512]{1,0:T(8,128)(2,1)S(1)}, u32[]{:S(2)}) copy-start(bf16[256,512]{1,0:T(8,128)(2,1)S(1)} %collective-permute-done.9.refs_6_) | copy-start | bytes 786436
  79.0 11.3 %collective-permute-start.14 = (bf16[64,1024]{1,0:T(8,128)(2,1)}, bf16[64,1024]{1,0:T(8,128)(2,1)S(1)}, u32[]{:S(2)}, u32[]{:S(2)}) collective-permute-start(bf16[64,1024]{1,0:T(8,128)(2,1)} %get-tuple-element.69), channel_id=1, source_target_pairs={{0,1},{1,0},{2,3},{3,2},{4,5},{5,4},{6,7},{7,6},{8,9},{9,8},{10,11... | collective-permute-start | bytes 393224 | tf_op jit(solution)/shard_map/ppermute | solution.py:376
  80.8 12.9 %collective-permute-start.19 = (bf16[256,512]{1,0:T(8,128)(2,1)S(1)}, bf16[256,512]{1,0:T(8,128)(2,1)S(1)}, u32[]{:S(2)}, u32[]{:S(2)}) collective-permute-start(bf16[256,512]{1,0:T(8,128)(2,1)S(1)} %collective-permute-done.9.refs_6_), channel_id=1, source_target_pairs={{0,16},{16,24},{24,8},{8,0},{1,17},{17,25},{25,9},{9,1},{2,18},{18... | collective-permute-start | bytes 786440 | tf_op jit(solution)/shard_map/ppermute | solution.py:464
  82.6 18.1 %collective-permute-start.13 = (bf16[128,1024]{1,0:T(8,128)(2,1)}, bf16[128,1024]{1,0:T(8,128)(2,1)S(1)}, u32[]{:S(2)}, u32[]{:S(2)}) collective-permute-start(bf16[128,1024]{1,0:T(8,128)(2,1)} %get-tuple-element.67), channel_id=1, source_target_pairs={{8,0},{16,8},{24,16},{9,1},{17,9},{25,17},{10,2},{18,10},{26,18},{... | collective-permute-start | bytes 786440 | tf_op jit(solution)/shard_map/ppermute | solution.py:533
  90.3 10.3 %collective-permute-start.18 = (bf16[64,1024]{1,0:T(8,128)(2,1)S(1)}, bf16[64,1024]{1,0:T(8,128)(2,1)S(1)}, u32[]{:S(2)}, u32[]{:S(2)}) collective-permute-start(bf16[64,1024]{1,0:T(8,128)(2,1)S(1)} %add_convert_fusion.1), channel_id=1, source_target_pairs={{0,8},{8,0},{16,24},{24,16},{1,9},{9,1},{17,25},{25,17},{2,10},{10... | collective-permute-start | bytes 393224 | tf_op jit(solution)/shard_map/ppermute | solution.py:376
  93.0 15.1 %collective-permute-start.20 = (bf16[512,512]{1,0:T(8,128)(2,1)}, bf16[512,512]{1,0:T(8,128)(2,1)S(1)}, u32[]{:S(2)}, u32[]{:S(2)}) collective-permute-start(bf16[512,512]{1,0:T(8,128)(2,1)} %get-tuple-element.82), channel_id=1, source_target_pairs={{0,1},{1,0},{2,3},{3,2},{4,5},{5,4},{6,7},{7,6},{8,9},{9,8},{10,11... | collective-permute-start | bytes 1572872 | tf_op jit(solution)/shard_map/ppermute | solution.py:376
  99.2 19.1 %collective-permute-start.23 = (bf16[512,512]{1,0:T(8,128)(2,1)}, bf16[512,512]{1,0:T(8,128)(2,1)S(1)}, u32[]{:S(2)}, u32[]{:S(2)}) collective-permute-start(bf16[512,512]{1,0:T(8,128)(2,1)} %get-tuple-element.87), channel_id=1, source_target_pairs={{0,1},{1,0},{2,3},{3,2},{4,5},{5,4},{6,7},{7,6},{8,9},{9,8},{10,11... | collective-permute-start | bytes 1572872 | tf_op jit(solution)/shard_map/ppermute | solution.py:376
  100.7 7.0 %collective-permute-start.21 = (bf16[64,1024]{1,0:T(8,128)(2,1)S(1)}, bf16[64,1024]{1,0:T(8,128)(2,1)S(1)}, u32[]{:S(2)}, u32[]{:S(2)}) collective-permute-start(bf16[64,1024]{1,0:T(8,128)(2,1)S(1)} %add_convert_fusion), channel_id=1, source_target_pairs={{0,16},{8,24},{16,0},{24,8},{1,17},{9,25},{17,1},{25,9},{2,18},{10... | collective-permute-start | bytes 393224 | tf_op jit(solution)/shard_map/ppermute | solution.py:376
  108.1 11.8 %collective-permute-start.22 = (bf16[64,1024]{1,0:T(8,128)(2,1)S(1)}, bf16[64,1024]{1,0:T(8,128)(2,1)S(1)}, u32[]{:S(2)}, u32[]{:S(2)}) collective-permute-start(bf16[64,1024]{1,0:T(8,128)(2,1)S(1)} %convert_add_fusion), channel_id=1, source_target_pairs={{0,1},{1,0},{2,3},{3,2},{4,5},{5,4},{6,7},{7,6},{8,9},{9,8},{10,11... | collective-permute-start | bytes 393224 | tf_op jit(solution)/shard_map/ppermute | solution.py:376
  (11 other events, 56.9 us)

commit v12 on v11

--- a/solution.py
+++ b/solution.py
@@ -320,7 +320,7 @@
             pltpu.SemaphoreType.DMA((steps,)),
             pltpu.SemaphoreType.DMA((2, steps)),
         ],
-        256 * length * out_weight.size,
+        4 * length * out_weight.size,
     )
 
 
@@ -446,6 +446,23 @@
     else:
         moved = cot
 
+    same = (me_half == me_dp).astype(jnp.int32)
+    subs_of = [me_sub, (me_sub + 1) % subs]
+    place = jnp.stack([same, *subs_of]).astype(jnp.int32)
+    dp_row = jnp.broadcast_to(me_dp.astype(f32), (1, channels))
+    if square:
+        order = [*range(0, n_seq, 2), *reversed(range(1, n_seq, 2))]
+        ring = [(order[k], order[(k + 1) % n_seq]) for k in range(n_seq)]
+        table = np.zeros((n_seq, n_tp, n_tp), np.int32)
+        for k, s in enumerate(order):
+            for r in range(n_seq):
+                for t in range(n_tp):
+                    table[s, t, t ^ holder(order[k - r], s)] = r
+        sources = jnp.asarray(table)[lax.axis_index("seq"), me_tp]
+        weight_place = jnp.concatenate([sources, me_dp[None].astype(jnp.int32)])
+        prior, place, weight_place, dp_row = lax.optimization_barrier(
+            (prior, place, weight_place, dp_row)
+        )
     state, *gated = by_channel(
         functools.partial(state_kernel, scale),
         tables,
@@ -454,53 +471,43 @@
         channels,
         unit * (4 * taps + 5 * length),
     )
-    dp_row = jnp.broadcast_to(me_dp.astype(f32), (1, channels))
-    if square:
-        order = [*range(0, n_seq, 2), *reversed(range(1, n_seq, 2))]
-        ring = [(order[k], order[(k + 1) % n_seq]) for k in range(n_seq)]
+    if square:
         halves = [[half] for half in gated]
 
         def ring_step(pieces):
             pieces.append(lax.ppermute(pieces[-1], "seq", ring))
 
+        halves[0][0], moved = lax.optimization_barrier((halves[0][0], moved))
         ring_step(halves[0])
-        table = np.zeros((n_seq, n_tp, n_tp), np.int32)
-        for k, s in enumerate(order):
-            for r in range(n_seq):
-                for t in range(n_tp):
-                    table[s, t, t ^ holder(order[k - r], s)] = r
-        sources = jnp.asarray(table)[lax.axis_index("seq"), me_tp]
-        weight_place = jnp.concatenate([sources, me_dp[None].astype(jnp.int32)])
-        halves[0][1], halves[1][0], weight_place, dp_row, moved, *rounds = lax.optimization_barrier(
-            (halves[0][1], halves[1][0], weight_place, dp_row, moved, *rounds)
+        halves[1][0], *rounds = lax.optimization_barrier((halves[1][0], *rounds))
+    else:
+        gated[0], *rounds = lax.optimization_barrier((gated[0], *rounds))
+
+    route = [(tp_dp(h, c, d), tp_dp(h, (c + 1) % subs, d)) for h, c, d in places]
+    theirs = [lax.ppermute(r, ("tp", "dp"), route) for r in rounds]
+    firsts, seconds = zip(rounds, theirs)
+    rows = n_tp * channels // (n_seq * n_dp)
+    if square:
+        moved = transposed(after(moved, *rounds))
+        moved, place = lax.optimization_barrier((moved, place))
+    other_sent, own_part = project(place, firsts, seconds, out_weight)
+    other_part = swap_pairs(other_sent, "dp", 1)
+    if square:
+        halves[0][1], halves[1][0], _ = lax.optimization_barrier(
+            (halves[0][1], halves[1][0], other_sent)
         )
         ring_step(halves[0])
         ring_step(halves[1])
-        moved = transposed(moved)
-    else:
-        gated[0], *rounds = lax.optimization_barrier((gated[0], *rounds))
-
-    route = [(tp_dp(h, c, d), tp_dp(h, (c + 1) % subs, d)) for h, c, d in places]
-    theirs = [lax.ppermute(r, ("tp", "dp"), route) for r in rounds]
-    firsts, seconds = zip(rounds, theirs)
-    same = (me_half == me_dp).astype(jnp.int32)
-    subs_of = [me_sub, (me_sub + 1) % subs]
-    place = jnp.stack([same, *subs_of]).astype(jnp.int32)
-    rows = n_tp * channels // (n_seq * n_dp)
-    if square:
-        moved, place = lax.optimization_barrier((moved, place))
-    other_sent, own_part = project(place, firsts, seconds, out_weight)
-    other_part = swap_pairs(other_sent, "dp", 1)
 
     if square:
         sent_by = lambda value, flip: lax.ppermute(value, "tp", [(t, t ^ flip) for t in range(n_tp)])
         across = sent_by(moved, subs)
         cot_pieces = [moved, sent_by(moved, 1), across, sent_by(after(across, halves[0][2]), 1)]
+        halves[0][2], halves[1][1], own_part = lax.optimization_barrier(
+            (halves[0][2], halves[1][1], own_part)
+        )
         ring_step(halves[0])
         ring_step(halves[1])
-        halves[0][3], halves[1][2], own_part = lax.optimization_barrier(
-            (halves[0][3], halves[1][2], own_part)
-        )
     else:
         full = lax.all_gather(cot, "tp", axis=1, tiled=True)
         cot_all = lax.all_to_all(full, "seq", 1, 0, tiled=True)
@@ -544,8 +551,8 @@
 
     received = swap_pairs(sent_lag, "dp", 1)
     if square:
+        weight_place, halves[1][2], signal = lax.optimization_barrier((weight_place, halves[1][2], signal))
         ring_step(halves[1])
-        weight_place, signal = lax.optimization_barrier((weight_place, signal))
         first_sent, first_own = weight_sum(weight_place, cot_pieces, halves[0], rows)
         first_received = swap_pairs(first_sent, "dp", 1)
         received, first_own = lax.optimization_barrier((received, first_own))

time: 122 us -> 113 us (0.926)
  starting transfers between devices: 42.9 us -> 35.6 us
  waiting for transfers between devices: 31.4 us -> 27.9 us
  local copies, waits for them, and re-layouts: 6.12 us -> 8.05 us
    ppermute x7, starting transfers between devices: 10.5 us -> 5.69 us  [swap_pairs(): return lax.ppermute(value, axis, [(i, i ^ distance) for i in range(count)])]
    ppermute x6, waiting for transfers between devices: 16.1 us -> 12.6 us  [ring_step(): pieces.append(lax.ppermute(pieces[-1], 'seq', ring))]
    ppermute x2, starting transfers between devices: 6.02 us -> 2.88 us  [per_device(): theirs = [lax.ppermute(r, ('tp', 'dp'), route) for r in rounds]]
    ppermute x2, waiting for transfers between devices: 0.01 us -> 2.6 us  [per_device(): lax.ppermute(after(cot, prior) if turn else cot, ('tp', 'dp'), route)]
    ppermute x7, waiting for transfers between devices: 10.1 us -> 7.8 us  [swap_pairs(): return lax.ppermute(value, axis, [(i, i ^ distance) for i in range(count)])]
    unnamed x39 -> x45, local copies, waits for them, and re-layouts: 4.15 us -> 6.17 us
  transfers between devices with their start and end apart: 24 -> 24, of which waited for: 8 -> 10; matrix products, arithmetic and copies ran while one was open for 4% -> 5% of each run, Pallas kernels for 29% -> 31%
where the time goes in v12:
time: 113 us
  starting transfers between devices  35.6 us (32%)
  Pallas kernels  34.9 us (31%)
  waiting for transfers between devices  27.9 us (25%)
  local copies, waits for them, and re-layouts  8.05 us (7%)
  other arithmetic  5.48 us (5%)
    pallas_call x3, Pallas kernels, by_channel(): pl.pallas_call(kernel, in_specs=[pl.BlockSpec(memory_space=pl.ANY)] * (n_...  16.8 us
    pallas_call x3, Pallas kernels, local_call(): pl.pallas_call(kernel, in_specs=[pl.BlockSpec(memory_space=pltpu.SMEM)] +...  16 us
    ppermute x6, starting transfers between devices, ring_step(): pieces.append(lax.ppermute(pieces[-1], 'seq', ring))  14.4 us
    ppermute x6, waiting for transfers between devices, ring_step(): pieces.append(lax.ppermute(pieces[-1], 'seq', ring))  12.6 us
    ppermute x7, waiting for transfers between devices, swap_pairs(): return lax.ppermute(value, axis, [(i, i ^ distance) for i in range(count)])  7.8 us
    ppermute x1, starting transfers between devices, per_device(): prior = lax.ppermute(tail, 'seq', [(i, i + 1) for i in range(n_seq - 1)])  7.09 us
    unnamed x45, local copies, waits for them, and re-layouts  6.17 us
    ppermute x7, starting transfers between devices, swap_pairs(): return lax.ppermute(value, axis, [(i, i ^ distance) for i in range(count)])  5.69 us
  transfers between devices with their start and end apart: 24, of which 10 were waited for; matrix products, arithmetic and copies ran while one was open for 5% of the time, Pallas kernels for 31%

profile of v12, /device:TPU:0, one launch (start us, length us, event | category | flops | bytes accessed | tf_op | source)
XLA Modules:
  0.0 112.9 jit_solution(15650411532109763397)
XLA Ops:
  0.6 1.1 fusion
  2.4 7.1 %collective-permute-start = (bf16[128,1024]{1,0:T(8,128)(2,1)S(1)}, bf16[128,1024]{1,0:T(8,128)(2,1)S(1)}, u32[]{:S(2)}, u32[]{:S(2)}) collective-permute-start(bf16[128,1024]{1,0:T(8,128)(2,1)S(1)} %fusion), channel_id=1, source_target_pairs={{0,8},{8,16},{16,24},{1,9},{9,17},{17,25},{2,10},{10,18},{18,26},{... | collective-permute-start | bytes 786440 | tf_op jit(solution)/shard_map/ppermute | solution.py:411
  9.5 1.7 %collective-permute-start.4 = (bf16[256,1024]{1,0:T(8,128)(2,1)}, bf16[256,1024]{1,0:T(8,128)(2,1)S(1)}, u32[]{:S(2)}, u32[]{:S(2)}) collective-permute-start(bf16[256,1024]{1,0:T(8,128)(2,1)} %bitcast.28), channel_id=1, source_target_pairs={{0,0},{1,4},{2,2},{3,6},{4,1},{5,5},{6,3},{7,7},{8,8},{9,12},{10,1... | collective-permute-start | bytes 1572872 | tf_op jit(solution)/shard_map/ppermute | solution.py:420
  11.2 2.8 %collective-permute-done.refs_2_.refs_6_ = bf16[128,1024]{1,0:T(8,128)(2,1)S(1)} collective-permute-done((bf16[128,1024]{1,0:T(8,128)(2,1)S(1)}, bf16[128,1024]{1,0:T(8,128)(2,1)S(1)}, u32[]{:S(2)}, u32[]{:S(2)}) %collective-permute-start) | collective-permute-done | bytes 262176 | tf_op jit(solution)/shard_map/ppermute | solution.py:411
  14.7 1.1 broadcast_select_fusion
  19.1 5.5 %shard_map.145 = (f32[256,1024]{1,0:T(8,128)}, bf16[256,512]{1,0:T(8,128)(2,1)}, bf16[256,512]{1,0:T(8,128)(2,1)}) custom-call(bf16[768,384]{1,0:T(8,128)(2,1)} %constant.66.clone.refs_0_, bf16[768,384]{1,0:T(8,128)(2,1)} %constant.67.clone.refs_1_, bf16[128,1024]{1,0:T(8,128)(2,1)} %copy-done.4, bf16[256,1024]{1,0:T(8,128)(2,1)} %bitcast.22, ...), custom_call_target="tpu_custom_call" | custom-call | flops 22020096 | bytes 57408 | tf_op jit(solution)/shard_map/pallas_call | solution.py:275
  24.7 2.6 %collective-permute-done.5.second_mine = bf16[256,1024]{1,0:T(8,128)(2,1)S(1)} collective-permute-done((bf16[256,1024]{1,0:T(8,128)(2,1)}, bf16[256,1024]{1,0:T(8,128)(2,1)S(1)}, u32[]{:S(2)}, u32[]{:S(2)}) %collective-permute-start.5) | collective-permute-done | bytes 524320 | tf_op jit(solution)/shard_map/ppermute | solution.py:420
  27.3 2.8 %collective-permute-start.6 = (bf16[256,1024]{1,0:T(8,128)(2,1)S(1)}, bf16[256,1024]{1,0:T(8,128)(2,1)S(1)}, u32[]{:S(2)}, u32[]{:S(2)}) collective-permute-start(bf16[256,1024]{1,0:T(8,128)(2,1)S(1)} %collective-permute-done.4.first_mine), channel_id=1, source_target_pairs={{0,2},{1,3},{2,0},{3,1},{4,6},{5,7},{6,4},{7,5},{8,10},{9,11},{10,... | collective-permute-start | bytes 1572872 | tf_op jit(solution)/shard_map/ppermute | solution.py:487
  30.2 6.7 %collective-permute-start.3 = (bf16[256,512]{1,0:T(8,128)(2,1)}, bf16[256,512]{1,0:T(8,128)(2,1)S(1)}, u32[]{:S(2)}, u32[]{:S(2)}) collective-permute-start(bf16[256,512]{1,0:T(8,128)(2,1)} %get-tuple-element.57.refs_4_), channel_id=1, source_target_pairs={{0,16},{16,24},{24,8},{8,0},{1,17},{17,25},{25,9},{9,1},{2,18},{18... | collective-permute-start | bytes 786440 | tf_op jit(solution)/shard_map/ppermute | solution.py:478
  36.9 2.1 %shard_map.146.refs_0_ = bf16[1024,256]{1,0:T(8,128)(2,1)} custom-call(bf16[256,1024]{1,0:T(8,128)(2,1)} %copy-done.12), custom_call_target="tpu_custom_call" | custom-call | bytes 16384 | tf_op jit(solution)/shard_map/pallas_call | solution.py:359
  40.6 6.4 %shard_map.147 = (bf16[256,1024]{1,0:T(8,128)(2,1)}, f32[256,1024]{1,0:T(8,128)}) custom-call(s32[3]{0:T(128)} %pad_add_fusion.place_ref, bf16[256,1024]{1,0:T(8,128)(2,1)} %copy-done.7, bf16[256,1024]{1,0:T(8,128)(2,1)} %copy-done.8, bf16[256,1024]{1,0:T(8,128)(2,1)} %copy-done.10, bf16[256,1024]{1,0:T(8,128)(2,1)} %copy-done.11, bf16[1024,2048]{1,0:T(8,128)(2,1)} %weight.1), custom_call_target="tpu_custom_call" | custom-call | flops 33554432 | bytes 122880 | tf_op jit(solution)/shard_map/pallas_call | solution.py:294
  47.0 2.0 %collective-permute-start.8 = (bf16[256,512]{1,0:T(8,128)(2,1)S(1)}, bf16[256,512]{1,0:T(8,128)(2,1)S(1)}, u32[]{:S(2)}, u32[]{:S(2)}) collective-permute-start(bf16[256,512]{1,0:T(8,128)(2,1)S(1)} %collective-permute-done.3.refs_5_), channel_id=1, source_target_pairs={{0,16},{16,24},{24,8},{8,0},{1,17},{17,25},{25,9},{9,1},{2,18},{18... | collective-permute-start | bytes 786440 | tf_op jit(solution)/shard_map/ppermute | solution.py:478
  49.1 1.9 %collective-permute-start.10 = (bf16[256,1024]{1,0:T(8,128)(2,1)}, bf16[256,1024]{1,0:T(8,128)(2,1)S(1)}, u32[]{:S(2)}, u32[]{:S(2)}) collective-permute-start(bf16[256,1024]{1,0:T(8,128)(2,1)} %get-tuple-element.67), channel_id=1, source_target_pairs={{0,1},{1,0},{2,3},{3,2},{4,5},{5,4},{6,7},{7,6},{8,9},{9,8},{10,11... | collective-permute-start | bytes 1572872 | tf_op jit(solution)/shard_map/ppermute | solution.py:376
  51.0 0.8 collective-permute-start.9
  51.8 2.1 %collective-permute-done.15.refs_2_ = bf16[1024,256]{1,0:T(8,128)(2,1)S(1)} collective-permute-done((bf16[1024,256]{1,0:T(8,128)(2,1)}, bf16[1024,256]{1,0:T(8,128)(2,1)S(1)}, u32[]{:S(2)}, u32[]{:S(2)}) %collective-permute-start.15) | collective-permute-done | bytes 524320 | tf_op jit(solution)/shard_map/ppermute | solution.py:503
  53.9 2.2 %collective-permute-done.8.refs_6_ = bf16[256,512]{1,0:T(8,128)(2,1)S(1)} collective-permute-done((bf16[256,512]{1,0:T(8,128)(2,1)S(1)}, bf16[256,512]{1,0:T(8,128)(2,1)S(1)}, u32[]{:S(2)}, u32[]{:S(2)}) %collective-permute-start.8) | collective-permute-done | bytes 262176 | tf_op jit(solution)/shard_map/ppermute | solution.py:478
  56.6 5.2 %collective-permute-done.9.refs_5_ = bf16[256,512]{1,0:T(8,128)(2,1)S(1)} collective-permute-done((bf16[256,512]{1,0:T(8,128)(2,1)S(1)}, bf16[256,512]{1,0:T(8,128)(2,1)S(1)}, u32[]{:S(2)}, u32[]{:S(2)}) %collective-permute-start.9) | collective-permute-done | bytes 262176 | tf_op jit(solution)/shard_map/ppermute | solution.py:478
  61.7 1.5 %collective-permute-start.11 = (bf16[256,512]{1,0:T(8,128)(2,1)S(1)}, bf16[256,512]{1,0:T(8,128)(2,1)S(1)}, u32[]{:S(2)}, u32[]{:S(2)}) collective-permute-start(bf16[256,512]{1,0:T(8,128)(2,1)S(1)} %collective-permute-done.9.refs_5_), channel_id=1, source_target_pairs={{0,16},{16,24},{24,8},{8,0},{1,17},{17,25},{25,9},{9,1},{2,18},{18... | collective-permute-start | bytes 786440 | tf_op jit(solution)/shard_map/ppermute | solution.py:478
  63.3 0.8 copy-done.9
  64.1 5.8 %shard_map.148 = (bf16[256,1024]{1,0:T(8,128)(2,1)}, bf16[256,1024]{1,0:T(8,128)(2,1)}, bf16[128,1024]{1,0:T(8,128)(2,1)}, bf16[64,1024]{1,0:T(8,128)(2,1)}, f32[64,1024]{1,0:T(8,128)}) custom-call(bf16[768,384]{1,0:T(8,128)(2,1)} %constant.66.clone.refs_0_, bf16[768,384]{1,0:T(8,128)(2,1)} %constant.67.clone.refs_1_, ...), custom_call_target="tpu_custom_call" | custom-call | flops 20447232 | bytes 96320 | tf_op jit(solution)/shard_map/pallas_call | solution.py:275
  70.8 1.3 %collective-permute-start.12 = (bf16[128,1024]{1,0:T(8,128)(2,1)}, bf16[128,1024]{1,0:T(8,128)(2,1)S(1)}, u32[]{:S(2)}, u32[]{:S(2)}) collective-permute-start(bf16[128,1024]{1,0:T(8,128)(2,1)} %get-tuple-element.79), channel_id=1, source_target_pairs={{8,0},{16,8},{24,16},{9,1},{17,9},{25,17},{10,2},{18,10},{26,18},{... | collective-permute-start | bytes 786440 | tf_op jit(solution)/shard_map/ppermute | solution.py:540
  72.2 3.3 %collective-permute-start.19 = (bf16[256,512]{1,0:T(8,128)(2,1)S(1)}, bf16[256,512]{1,0:T(8,128)(2,1)S(1)}, u32[]{:S(2)}, u32[]{:S(2)}) collective-permute-start(bf16[256,512]{1,0:T(8,128)(2,1)S(1)} %collective-permute-done.11.refs_6_), channel_id=1, source_target_pairs={{0,16},{16,24},{24,8},{8,0},{1,17},{17,25},{25,9},{9,1},{2,18},{18... | collective-permute-start | bytes 786440 | tf_op jit(solution)/shard_map/ppermute | solution.py:478
  75.5 1.0 collective-permute-done.17.refs_7_
  78.0 4.8 %shard_map.149 = (bf16[512,512]{1,0:T(8,128)(2,1)}, f32[512,512]{1,0:T(8,128)}) custom-call(s32[5]{0:T(128)} %pad_add_fusion.1.place_ref, bf16[1024,256]{1,0:T(8,128)(2,1)} %shard_map.146.refs_0_, bf16[1024,256]{1,0:T(8,128)(2,1)} %copy-done.2, bf16[1024,256]{1,0:T(8,128)(2,1)} %copy-done.1, bf16[1024,256]{1,0:T(8,128)(2,1)} %copy-done.3, ...), custom_call_target="tpu_custom_call" | custom-call | flops 16777216 | bytes 73728 | tf_op jit(solution)/shard_map/pallas_call | solution.py:294
  84.0 3.8 %collective-permute-done.19.refs_7_ = bf16[256,512]{1,0:T(8,128)(2,1)S(1)} collective-permute-done((bf16[256,512]{1,0:T(8,128)(2,1)S(1)}, bf16[256,512]{1,0:T(8,128)(2,1)S(1)}, u32[]{:S(2)}, u32[]{:S(2)}) %collective-permute-start.19) | collective-permute-done | bytes 262176 | tf_op jit(solution)/shard_map/ppermute | solution.py:478
  88.5 4.8 %shard_map.150 = (bf16[512,512]{1,0:T(8,128)(2,1)}, f32[512,512]{1,0:T(8,128)}) custom-call(s32[5]{0:T(128)} %pad_add_fusion.1.place_ref, bf16[1024,256]{1,0:T(8,128)(2,1)} %shard_map.146.refs_0_, bf16[1024,256]{1,0:T(8,128)(2,1)} %copy-done.2, bf16[1024,256]{1,0:T(8,128)(2,1)} %copy-done.1, bf16[1024,256]{1,0:T(8,128)(2,1)} %copy-done.3, ...), custom_call_target="tpu_custom_call" | custom-call | flops 16777216 | bytes 73728 | tf_op jit(solution)/shard_map/pallas_call | solution.py:294
  94.4 5.5 %shard_map.151 = (bf16[256,1024]{1,0:T(8,128)(2,1)}, bf16[256,1024]{1,0:T(8,128)(2,1)}) custom-call(bf16[768,384]{1,0:T(8,128)(2,1)} %constant.66.clone.refs_0_, bf16[768,384]{1,0:T(8,128)(2,1)} %constant.67.clone.refs_1_, bf16[256,1024]{1,0:T(8,128)(2,1)} %get-tuple-element.78.refs_2_, bf16[128,1024]{1,0:T(8,128)(2,1)} %copy-done.21, ...), custom_call_target="tpu_custom_call" | custom-call | flops 5637144576 | bytes 49216 | tf_op jit(solution)/shard_map/pallas_call | solution.py:275
  99.9 1.5 %collective-permute-done.21 = bf16[64,1024]{1,0:T(8,128)(2,1)S(1)} collective-permute-done((bf16[64,1024]{1,0:T(8,128)(2,1)S(1)}, bf16[64,1024]{1,0:T(8,128)(2,1)S(1)}, u32[]{:S(2)}, u32[]{:S(2)}) %collective-permute-start.21) | collective-permute-done | bytes 131104 | tf_op jit(solution)/shard_map/ppermute | solution.py:376
  101.4 1.7 %collective-permute-start.22 = (bf16[64,1024]{1,0:T(8,128)(2,1)S(1)}, bf16[64,1024]{1,0:T(8,128)(2,1)S(1)}, u32[]{:S(2)}, u32[]{:S(2)}) collective-permute-start(bf16[64,1024]{1,0:T(8,128)(2,1)S(1)} %convert_add_fusion), channel_id=1, source_target_pairs={{0,1},{1,0},{2,3},{3,2},{4,5},{5,4},{6,7},{7,6},{8,9},{9,8},{10,11... | collective-permute-start | bytes 393224 | tf_op jit(solution)/shard_map/ppermute | solution.py:376
  103.3 6.3 %collective-permute-done.23 = bf16[512,512]{1,0:T(8,128)(2,1)S(1)} collective-permute-done((bf16[512,512]{1,0:T(8,128)(2,1)}, bf16[512,512]{1,0:T(8,128)(2,1)S(1)}, u32[]{:S(2)}, u32[]{:S(2)}) %collective-permute-start.23) | collective-permute-done | bytes 524320 | tf_op jit(solution)/shard_map/ppermute | solution.py:376
  109.8 1.5 %pad_maximum_fusion = f32[512,1024]{1,0:T(8,128)} fusion(f32[512,512]{1,0:T(8,128)S(1)} %add_multiply_fusion, f32[512,512]{1,0:T(8,128)S(1)} %add_multiply_fusion.1), kind=kLoop, calls=%fused_computation | loop fusion | flops 524288 | bytes 4194304 | tf_op jit(solution)/shard_map/concatenate | solution.py:583
  111.3 1.0 copy.16
  (83 shorter events, 13.3 us)
Async XLA Ops:
  1.7 12.9 %collective-permute-start.1 = (bf16[256,1024]{1,0:T(8,128)(2,1)}, bf16[256,1024]{1,0:T(8,128)(2,1)S(1)}, u32[]{:S(2)}, u32[]{:S(2)}) collective-permute-start(bf16[256,1024]{1,0:T(8,128)(2,1)} %bitcast.27), channel_id=1, source_target_pairs={{2,4},{4,2},{8,14},{14,8},{18,20},{20,18},{24,30},{30,24},{3,5},{5... | collective-permute-start | bytes 1572872 | tf_op jit(solution)/shard_map/ppermute | solution.py:433
  2.4 11.6 %collective-permute-start = (bf16[128,1024]{1,0:T(8,128)(2,1)S(1)}, bf16[128,1024]{1,0:T(8,128)(2,1)S(1)}, u32[]{:S(2)}, u32[]{:S(2)}) collective-permute-start(bf16[128,1024]{1,0:T(8,128)(2,1)S(1)} %fusion), channel_id=1, source_target_pairs={{0,8},{8,16},{16,24},{1,9},{9,17},{17,25},{2,10},{10,18},{18,26},{... | collective-permute-start | bytes 786440 | tf_op jit(solution)/shard_map/ppermute | solution.py:411
  9.5 15.1 %collective-permute-start.4 = (bf16[256,1024]{1,0:T(8,128)(2,1)}, bf16[256,1024]{1,0:T(8,128)(2,1)S(1)}, u32[]{:S(2)}, u32[]{:S(2)}) collective-permute-start(bf16[256,1024]{1,0:T(8,128)(2,1)} %bitcast.28), channel_id=1, source_target_pairs={{0,0},{1,4},{2,2},{3,6},{4,1},{5,5},{6,3},{7,7},{8,8},{9,12},{10,1... | collective-permute-start | bytes 1572872 | tf_op jit(solution)/shard_map/ppermute | solution.py:420
  14.0 13.3 %collective-permute-start.5 = (bf16[256,1024]{1,0:T(8,128)(2,1)}, bf16[256,1024]{1,0:T(8,128)(2,1)S(1)}, u32[]{:S(2)}, u32[]{:S(2)}) collective-permute-start(bf16[256,1024]{1,0:T(8,128)(2,1)} %bitcast.29), channel_id=1, source_target_pairs={{0,4},{1,0},{2,6},{3,2},{4,5},{5,1},{6,7},{7,3},{8,12},{9,8},{10,1... | collective-permute-start | bytes 1572872 | tf_op jit(solution)/shard_map/ppermute | solution.py:420
  15.8 14.4 %collective-permute-start.2 = (bf16[256,1024]{1,0:T(8,128)(2,1)S(1)}, bf16[256,1024]{1,0:T(8,128)(2,1)S(1)}, u32[]{:S(2)}, u32[]{:S(2)}) collective-permute-start(bf16[256,1024]{1,0:T(8,128)(2,1)S(1)} %broadcast_select_fusion), channel_id=1, source_target_pairs={{0,0},{2,16},{4,12},{6,28},{8,24},{10,8},{12,20},{14,4},{16,2},{18... | collective-permute-start | bytes 1572872 | tf_op jit(solution)/shard_map/ppermute | solution.py:445
  24.7 14.4 %copy-start.7 = (bf16[256,1024]{1,0:T(8,128)(2,1)}, bf16[256,1024]{1,0:T(8,128)(2,1)S(1)}, u32[]{:S(2)}) copy-start(bf16[256,1024]{1,0:T(8,128)(2,1)S(1)} %collective-permute-done.4.first_mine) | copy-start | bytes 1572868
  27.3 11.8 %collective-permute-start.6 = (bf16[256,1024]{1,0:T(8,128)(2,1)S(1)}, bf16[256,1024]{1,0:T(8,128)(2,1)S(1)}, u32[]{:S(2)}, u32[]{:S(2)}) collective-permute-start(bf16[256,1024]{1,0:T(8,128)(2,1)S(1)} %collective-permute-done.4.first_mine), channel_id=1, source_target_pairs={{0,2},{1,3},{2,0},{3,1},{4,6},{5,7},{6,4},{7,5},{8,10},{9,11},{10,... | collective-permute-start | bytes 1572872 | tf_op jit(solution)/shard_map/ppermute | solution.py:487
  30.1 9.0 %collective-permute-start.7 = (bf16[256,1024]{1,0:T(8,128)(2,1)S(1)}, bf16[256,1024]{1,0:T(8,128)(2,1)S(1)}, u32[]{:S(2)}, u32[]{:S(2)}) collective-permute-start(bf16[256,1024]{1,0:T(8,128)(2,1)S(1)} %collective-permute-done.5.second_mine), channel_id=1, source_target_pairs={{0,2},{1,3},{2,0},{3,1},{4,6},{5,7},{6,4},{7,5},{8,10},{9,11},{10,... | collective-permute-start | bytes 1572872 | tf_op jit(solution)/shard_map/ppermute | solution.py:487
  30.2 16.9 %collective-permute-start.3 = (bf16[256,512]{1,0:T(8,128)(2,1)}, bf16[256,512]{1,0:T(8,128)(2,1)S(1)}, u32[]{:S(2)}, u32[]{:S(2)}) collective-permute-start(bf16[256,512]{1,0:T(8,128)(2,1)} %get-tuple-element.57.refs_4_), channel_id=1, source_target_pairs={{0,16},{16,24},{24,8},{8,0},{1,17},{17,25},{25,9},{9,1},{2,18},{18... | collective-permute-start | bytes 786440 | tf_op jit(solution)/shard_map/ppermute | solution.py:478
  38.9 12.8 %copy-start = (bf16[1024,256]{1,0:T(8,128)(2,1)S(1)}, bf16[1024,256]{1,0:T(8,128)(2,1)}, u32[]{:S(2)}) copy-start(bf16[1024,256]{1,0:T(8,128)(2,1)} %shard_map.146.refs_0_) | copy-start | bytes 1572868
  39.0 14.9 %collective-permute-start.15 = (bf16[1024,256]{1,0:T(8,128)(2,1)}, bf16[1024,256]{1,0:T(8,128)(2,1)S(1)}, u32[]{:S(2)}, u32[]{:S(2)}) collective-permute-start(bf16[1024,256]{1,0:T(8,128)(2,1)} %shard_map.146.refs_0_), channel_id=1, source_target_pairs={{0,4},{2,6},{4,0},{6,2},{1,5},{3,7},{5,1},{7,3},{8,12},{10,14},{12... | collective-permute-start | bytes 1572872 | tf_op jit(solution)/shard_map/ppermute | solution.py:503
  47.0 29.4 %copy-start.15 = (bf16[256,512]{1,0:T(8,128)(2,1)}, bf16[256,512]{1,0:T(8,128)(2,1)S(1)}, u32[]{:S(2)}) copy-start(bf16[256,512]{1,0:T(8,128)(2,1)S(1)} %collective-permute-done.3.refs_5_) | copy-start | bytes 786436
  47.0 9.1 %collective-permute-start.8 = (bf16[256,512]{1,0:T(8,128)(2,1)S(1)}, bf16[256,512]{1,0:T(8,128)(2,1)S(1)}, u32[]{:S(2)}, u32[]{:S(2)}) collective-permute-start(bf16[256,512]{1,0:T(8,128)(2,1)S(1)} %collective-permute-done.3.refs_5_), channel_id=1, source_target_pairs={{0,16},{16,24},{24,8},{8,0},{1,17},{17,25},{25,9},{9,1},{2,18},{18... | collective-permute-start | bytes 786440 | tf_op jit(solution)/shard_map/ppermute | solution.py:478
  49.1 14.2 %collective-permute-start.10 = (bf16[256,1024]{1,0:T(8,128)(2,1)}, bf16[256,1024]{1,0:T(8,128)(2,1)S(1)}, u32[]{:S(2)}, u32[]{:S(2)}) collective-permute-start(bf16[256,1024]{1,0:T(8,128)(2,1)} %get-tuple-element.67), channel_id=1, source_target_pairs={{0,1},{1,0},{2,3},{3,2},{4,5},{5,4},{6,7},{7,6},{8,9},{9,8},{10,11... | collective-permute-start | bytes 1572872 | tf_op jit(solution)/shard_map/ppermute | solution.py:376
  51.0 10.7 %collective-permute-start.9 = (bf16[256,512]{1,0:T(8,128)(2,1)S(1)}, bf16[256,512]{1,0:T(8,128)(2,1)S(1)}, u32[]{:S(2)}, u32[]{:S(2)}) collective-permute-start(bf16[256,512]{1,0:T(8,128)(2,1)S(1)} %copy-done.14), channel_id=1, source_target_pairs={{0,16},{16,24},{24,8},{8,0},{1,17},{17,25},{25,9},{9,1},{2,18},{18... | collective-permute-start | bytes 786440 | tf_op jit(solution)/shard_map/ppermute | solution.py:478
  51.8 20.4 %collective-permute-start.14 = (bf16[1024,256]{1,0:T(8,128)(2,1)S(1)}, bf16[1024,256]{1,0:T(8,128)(2,1)S(1)}, u32[]{:S(2)}, u32[]{:S(2)}) collective-permute-start(bf16[1024,256]{1,0:T(8,128)(2,1)S(1)} %copy-done), channel_id=1, source_target_pairs={{0,2},{2,0},{4,6},{6,4},{1,3},{3,1},{5,7},{7,5},{8,10},{10,8},{12,... | collective-permute-start | bytes 1572872 | tf_op jit(solution)/shard_map/ppermute | solution.py:503
  53.9 16.0 %copy-start.1 = (bf16[1024,256]{1,0:T(8,128)(2,1)}, bf16[1024,256]{1,0:T(8,128)(2,1)S(1)}, u32[]{:S(2)}) copy-start(bf16[1024,256]{1,0:T(8,128)(2,1)S(1)} %collective-permute-done.15.refs_2_) | copy-start | bytes 1572868
  56.1 20.4 %copy-start.18 = (bf16[256,512]{1,0:T(8,128)(2,1)}, bf16[256,512]{1,0:T(8,128)(2,1)S(1)}, u32[]{:S(2)}) copy-start(bf16[256,512]{1,0:T(8,128)(2,1)S(1)} %collective-permute-done.8.refs_6_) | copy-start | bytes 786436
  56.1 20.4 %collective-permute-start.16 = (bf16[1024,256]{1,0:T(8,128)(2,1)S(1)}, bf16[1024,256]{1,0:T(8,128)(2,1)S(1)}, u32[]{:S(2)}, u32[]{:S(2)}) collective-permute-start(bf16[1024,256]{1,0:T(8,128)(2,1)S(1)} %collective-permute-done.15.refs_2_), channel_id=1, source_target_pairs={{0,2},{2,0},{4,6},{6,4},{1,3},{3,1},{5,7},{7,5},{8,10},{10,8},{12,... | collective-permute-start | bytes 1572872 | tf_op jit(solution)/shard_map/ppermute | solution.py:503
  61.7 26.1 %copy-start.16 = (bf16[256,512]{1,0:T(8,128)(2,1)}, bf16[256,512]{1,0:T(8,128)(2,1)S(1)}, u32[]{:S(2)}) copy-start(bf16[256,512]{1,0:T(8,128)(2,1)S(1)} %collective-permute-done.9.refs_5_) | copy-start | bytes 786436
  61.7 9.1 %collective-permute-start.11 = (bf16[256,512]{1,0:T(8,128)(2,1)S(1)}, bf16[256,512]{1,0:T(8,128)(2,1)S(1)}, u32[]{:S(2)}, u32[]{:S(2)}) collective-permute-start(bf16[256,512]{1,0:T(8,128)(2,1)S(1)} %collective-permute-done.9.refs_5_), channel_id=1, source_target_pairs={{0,16},{16,24},{24,8},{8,0},{1,17},{17,25},{25,9},{9,1},{2,18},{18... | collective-permute-start | bytes 786440 | tf_op jit(solution)/shard_map/ppermute | solution.py:478
  63.2 13.2 %collective-permute-start.17 = (bf16[256,512]{1,0:T(8,128)(2,1)S(1)}, bf16[256,512]{1,0:T(8,128)(2,1)S(1)}, u32[]{:S(2)}, u32[]{:S(2)}) collective-permute-start(bf16[256,512]{1,0:T(8,128)(2,1)S(1)} %collective-permute-done.8.refs_6_), channel_id=1, source_target_pairs={{0,16},{16,24},{24,8},{8,0},{1,17},{17,25},{25,9},{9,1},{2,18},{18... | collective-permute-start | bytes 786440 | tf_op jit(solution)/shard_map/ppermute | solution.py:478
  69.9 12.9 %copy-start.13 = (f32[64,1024]{1,0:T(8,128)S(1)}, f32[64,1024]{1,0:T(8,128)}, u32[]{:S(2)}) copy-start(f32[64,1024]{1,0:T(8,128)} %get-tuple-element.80) | copy-start | bytes 786436
  69.9 12.9 %collective-permute-start.13 = (bf16[64,1024]{1,0:T(8,128)(2,1)}, bf16[64,1024]{1,0:T(8,128)(2,1)S(1)}, u32[]{:S(2)}, u32[]{:S(2)}) collective-permute-start(bf16[64,1024]{1,0:T(8,128)(2,1)} %get-tuple-element.81), channel_id=1, source_target_pairs={{0,1},{1,0},{2,3},{3,2},{4,5},{5,4},{6,7},{7,6},{8,9},{9,8},{10,11... | collective-permute-start | bytes 393224 | tf_op jit(solution)/shard_map/ppermute | solution.py:376
  70.8 17.0 %copy-start.17 = (bf16[256,512]{1,0:T(8,128)(2,1)}, bf16[256,512]{1,0:T(8,128)(2,1)S(1)}, u32[]{:S(2)}) copy-start(bf16[256,512]{1,0:T(8,128)(2,1)S(1)} %collective-permute-done.11.refs_6_) | copy-start | bytes 786436
  70.8 22.8 %collective-permute-start.12 = (bf16[128,1024]{1,0:T(8,128)(2,1)}, bf16[128,1024]{1,0:T(8,128)(2,1)S(1)}, u32[]{:S(2)}, u32[]{:S(2)}) collective-permute-start(bf16[128,1024]{1,0:T(8,128)(2,1)} %get-tuple-element.79), channel_id=1, source_target_pairs={{8,0},{16,8},{24,16},{9,1},{17,9},{25,17},{10,2},{18,10},{26,18},{... | collective-permute-start | bytes 786440 | tf_op jit(solution)/shard_map/ppermute | solution.py:540
  72.2 15.6 %collective-permute-start.19 = (bf16[256,512]{1,0:T(8,128)(2,1)S(1)}, bf16[256,512]{1,0:T(8,128)(2,1)S(1)}, u32[]{:S(2)}, u32[]{:S(2)}) collective-permute-start(bf16[256,512]{1,0:T(8,128)(2,1)S(1)} %collective-permute-done.11.refs_6_), channel_id=1, source_target_pairs={{0,16},{16,24},{24,8},{8,0},{1,17},{17,25},{25,9},{9,1},{2,18},{18... | collective-permute-start | bytes 786440 | tf_op jit(solution)/shard_map/ppermute | solution.py:478
  82.8 10.8 %collective-permute-start.18 = (bf16[64,1024]{1,0:T(8,128)(2,1)S(1)}, bf16[64,1024]{1,0:T(8,128)(2,1)S(1)}, u32[]{:S(2)}, u32[]{:S(2)}) collective-permute-start(bf16[64,1024]{1,0:T(8,128)(2,1)S(1)} %add_convert_fusion.1), channel_id=1, source_target_pairs={{0,8},{8,0},{16,24},{24,16},{1,9},{9,1},{17,25},{25,17},{2,10},{10... | collective-permute-start | bytes 393224 | tf_op jit(solution)/shard_map/ppermute | solution.py:376
  83.3 18.0 %collective-permute-start.20 = (bf16[512,512]{1,0:T(8,128)(2,1)}, bf16[512,512]{1,0:T(8,128)(2,1)S(1)}, u32[]{:S(2)}, u32[]{:S(2)}) collective-permute-start(bf16[512,512]{1,0:T(8,128)(2,1)} %get-tuple-element.94), channel_id=1, source_target_pairs={{0,1},{1,0},{2,3},{3,2},{4,5},{5,4},{6,7},{7,6},{8,9},{9,8},{10,11... | collective-permute-start | bytes 1572872 | tf_op jit(solution)/shard_map/ppermute | solution.py:376
  93.3 16.3 %collective-permute-start.23 = (bf16[512,512]{1,0:T(8,128)(2,1)}, bf16[512,512]{1,0:T(8,128)(2,1)S(1)}, u32[]{:S(2)}, u32[]{:S(2)}) collective-permute-start(bf16[512,512]{1,0:T(8,128)(2,1)} %get-tuple-element.99), channel_id=1, source_target_pairs={{0,1},{1,0},{2,3},{3,2},{4,5},{5,4},{6,7},{7,6},{8,9},{9,8},{10,11... | collective-permute-start | bytes 1572872 | tf_op jit(solution)/shard_map/ppermute | solution.py:376
  93.7 7.6 %collective-permute-start.21 = (bf16[64,1024]{1,0:T(8,128)(2,1)S(1)}, bf16[64,1024]{1,0:T(8,128)(2,1)S(1)}, u32[]{:S(2)}, u32[]{:S(2)}) collective-permute-start(bf16[64,1024]{1,0:T(8,128)(2,1)S(1)} %add_convert_fusion), channel_id=1, source_target_pairs={{0,16},{8,24},{16,0},{24,8},{1,17},{9,25},{17,1},{25,9},{2,18},{10... | collective-permute-start | bytes 393224 | tf_op jit(solution)/shard_map/ppermute | solution.py:376
  101.4 9.9 %collective-permute-start.22 = (bf16[64,1024]{1,0:T(8,128)(2,1)S(1)}, bf16[64,1024]{1,0:T(8,128)(2,1)S(1)}, u32[]{:S(2)}, u32[]{:S(2)}) collective-permute-start(bf16[64,1024]{1,0:T(8,128)(2,1)S(1)} %convert_add_fusion), channel_id=1, source_target_pairs={{0,1},{1,0},{2,3},{3,2},{4,5},{5,4},{6,7},{7,6},{8,9},{9,8},{10,11... | collective-permute-start | bytes 393224 | tf_op jit(solution)/shard_map/ppermute | solution.py:376
  (14 other events, 64.4 us)

commit v13 on v12

--- a/solution.py
+++ b/solution.py
@@ -477,7 +477,6 @@
         def ring_step(pieces):
             pieces.append(lax.ppermute(pieces[-1], "seq", ring))
 
-        halves[0][0], moved = lax.optimization_barrier((halves[0][0], moved))
         ring_step(halves[0])
         halves[1][0], *rounds = lax.optimization_barrier((halves[1][0], *rounds))
     else:
@@ -493,18 +492,15 @@
     other_sent, own_part = project(place, firsts, seconds, out_weight)
     other_part = swap_pairs(other_sent, "dp", 1)
     if square:
-        halves[0][1], halves[1][0], _ = lax.optimization_barrier(
-            (halves[0][1], halves[1][0], other_sent)
-        )
+        halves[0][1] = after(halves[0][1], other_sent)
         ring_step(halves[0])
-        ring_step(halves[1])
 
     if square:
         sent_by = lambda value, flip: lax.ppermute(value, "tp", [(t, t ^ flip) for t in range(n_tp)])
         across = sent_by(moved, subs)
         cot_pieces = [moved, sent_by(moved, 1), across, sent_by(after(across, halves[0][2]), 1)]
-        halves[0][2], halves[1][1], own_part = lax.optimization_barrier(
-            (halves[0][2], halves[1][1], own_part)
+        halves[0][2], halves[1][0], own_part = lax.optimization_barrier(
+            (halves[0][2], halves[1][0], own_part)
         )
         ring_step(halves[0])
         ring_step(halves[1])
@@ -551,11 +547,12 @@
 
     received = swap_pairs(sent_lag, "dp", 1)
     if square:
-        weight_place, halves[1][2], signal = lax.optimization_barrier((weight_place, halves[1][2], signal))
+        weight_place, halves[1][1], signal = lax.optimization_barrier((weight_place, halves[1][1], signal))
         ring_step(halves[1])
         first_sent, first_own = weight_sum(weight_place, cot_pieces, halves[0], rows)
         first_received = swap_pairs(first_sent, "dp", 1)
-        received, first_own = lax.optimization_barrier((received, first_own))
+        received, first_own, halves[1][2] = lax.optimization_barrier((received, first_own, halves[1][2]))
+        ring_step(halves[1])
     lag_sum = own_lag + received.astype(f32)
     distance = 1
     while distance < n_seq:

time: 113 us -> 115 us (1.018)
  starting transfers between devices: 35.6 us -> 42.8 us
  waiting for transfers between devices: 27.9 us -> 22.3 us
    ppermute x7, starting transfers between devices: 5.69 us -> 10.3 us  [swap_pairs(): return lax.ppermute(value, axis, [(i, i ^ distance) for i in range(count)])]
    ppermute x6, starting transfers between devices: 14.4 us -> 16.8 us  [ring_step(): pieces.append(lax.ppermute(pieces[-1], 'seq', ring))]
    ppermute x7, waiting for transfers between devices: 7.8 us -> 5.65 us  [swap_pairs(): return lax.ppermute(value, axis, [(i, i ^ distance) for i in range(count)])]
    ppermute x3, waiting for transfers between devices: 2.1 us -> 0.01 us  [per_device(): lax.ppermute(value, 'tp', [(t, t ^ flip) for t in range(n_tp)])]
    ppermute x6, waiting for transfers between devices: 12.6 us -> 11.2 us  [ring_step(): pieces.append(lax.ppermute(pieces[-1], 'seq', ring))]
  transfers between devices with their start and end apart: 24 -> 24, of which waited for: 10 -> 5; matrix products, arithmetic and copies ran while one was open for 5% -> 5% of each run, Pallas kernels for 31% -> 30%
where the time goes in v13:
time: 115 us
  starting transfers between devices  42.8 us (37%)
  Pallas kernels  34.9 us (30%)
  waiting for transfers between devices  22.3 us (19%)
  local copies, waits for them, and re-layouts  8.27 us (7%)
  other arithmetic  5.47 us (5%)
    pallas_call x3, Pallas kernels, by_channel(): pl.pallas_call(kernel, in_specs=[pl.BlockSpec(memory_space=pl.ANY)] * (n_...  16.8 us
    ppermute x6, starting transfers between devices, ring_step(): pieces.append(lax.ppermute(pieces[-1], 'seq', ring))  16.8 us
    pallas_call x3, Pallas kernels, local_call(): pl.pallas_call(kernel, in_specs=[pl.BlockSpec(memory_space=pltpu.SMEM)] +...  16 us
    ppermute x6, waiting for transfers between devices, ring_step(): pieces.append(lax.ppermute(pieces[-1], 'seq', ring))  11.2 us
    ppermute x7, starting transfers between devices, swap_pairs(): return lax.ppermute(value, axis, [(i, i ^ distance) for i in range(count)])  10.3 us
    ppermute x1, starting transfers between devices, per_device(): prior = lax.ppermute(tail, 'seq', [(i, i + 1) for i in range(n_seq - 1)])  7.09 us
    unnamed x45, local copies, waits for them, and re-layouts  6.38 us
    ppermute x7, waiting for transfers between devices, swap_pairs(): return lax.ppermute(value, axis, [(i, i ^ distance) for i in range(count)])  5.65 us
  transfers between devices with their start and end apart: 24, of which 5 were waited for; matrix products, arithmetic and copies ran while one was open for 5% of the time, Pallas kernels for 30%

profile of v13, /device:TPU:0, one launch (start us, length us, event | category | flops | bytes accessed | tf_op | source)
XLA Modules:
  0.0 114.7 jit_solution(2758674741423320492)
XLA Ops:
  0.6 1.1 fusion
  2.4 7.1 %collective-permute-start = (bf16[128,1024]{1,0:T(8,128)(2,1)S(1)}, bf16[128,1024]{1,0:T(8,128)(2,1)S(1)}, u32[]{:S(2)}, u32[]{:S(2)}) collective-permute-start(bf16[128,1024]{1,0:T(8,128)(2,1)S(1)} %fusion), channel_id=1, source_target_pairs={{0,8},{8,16},{16,24},{1,9},{9,17},{17,25},{2,10},{10,18},{18,26},{... | collective-permute-start | bytes 786440 | tf_op jit(solution)/shard_map/ppermute | solution.py:411
  9.5 1.7 %collective-permute-start.4 = (bf16[256,1024]{1,0:T(8,128)(2,1)}, bf16[256,1024]{1,0:T(8,128)(2,1)S(1)}, u32[]{:S(2)}, u32[]{:S(2)}) collective-permute-start(bf16[256,1024]{1,0:T(8,128)(2,1)} %bitcast.28), channel_id=1, source_target_pairs={{0,0},{1,4},{2,2},{3,6},{4,1},{5,5},{6,3},{7,7},{8,8},{9,12},{10,1... | collective-permute-start | bytes 1572872 | tf_op jit(solution)/shard_map/ppermute | solution.py:420
  11.2 2.8 %collective-permute-done.refs_2_.refs_6_ = bf16[128,1024]{1,0:T(8,128)(2,1)S(1)} collective-permute-done((bf16[128,1024]{1,0:T(8,128)(2,1)S(1)}, bf16[128,1024]{1,0:T(8,128)(2,1)S(1)}, u32[]{:S(2)}, u32[]{:S(2)}) %collective-permute-start) | collective-permute-done | bytes 262176 | tf_op jit(solution)/shard_map/ppermute | solution.py:411
  14.7 1.1 broadcast_select_fusion
  19.1 5.5 %shard_map.145 = (f32[256,1024]{1,0:T(8,128)}, bf16[256,512]{1,0:T(8,128)(2,1)}, bf16[256,512]{1,0:T(8,128)(2,1)}) custom-call(bf16[768,384]{1,0:T(8,128)(2,1)} %constant.66.clone.refs_0_, bf16[768,384]{1,0:T(8,128)(2,1)} %constant.67.clone.refs_1_, bf16[128,1024]{1,0:T(8,128)(2,1)} %copy-done.4, bf16[256,1024]{1,0:T(8,128)(2,1)} %bitcast.22, ...), custom_call_target="tpu_custom_call" | custom-call | flops 22020096 | bytes 57408 | tf_op jit(solution)/shard_map/pallas_call | solution.py:275
  24.6 2.6 %collective-permute-done.5.second_mine = bf16[256,1024]{1,0:T(8,128)(2,1)S(1)} collective-permute-done((bf16[256,1024]{1,0:T(8,128)(2,1)}, bf16[256,1024]{1,0:T(8,128)(2,1)S(1)}, u32[]{:S(2)}, u32[]{:S(2)}) %collective-permute-start.5) | collective-permute-done | bytes 524320 | tf_op jit(solution)/shard_map/ppermute | solution.py:420
  27.3 2.8 %collective-permute-start.6 = (bf16[256,1024]{1,0:T(8,128)(2,1)S(1)}, bf16[256,1024]{1,0:T(8,128)(2,1)S(1)}, u32[]{:S(2)}, u32[]{:S(2)}) collective-permute-start(bf16[256,1024]{1,0:T(8,128)(2,1)S(1)} %collective-permute-done.4.first_mine), channel_id=1, source_target_pairs={{0,2},{1,3},{2,0},{3,1},{4,6},{5,7},{6,4},{7,5},{8,10},{9,11},{10,... | collective-permute-start | bytes 1572872 | tf_op jit(solution)/shard_map/ppermute | solution.py:486
  30.1 2.4 %collective-permute-start.1 = (bf16[256,512]{1,0:T(8,128)(2,1)}, bf16[256,512]{1,0:T(8,128)(2,1)S(1)}, u32[]{:S(2)}, u32[]{:S(2)}) collective-permute-start(bf16[256,512]{1,0:T(8,128)(2,1)} %get-tuple-element.53.refs_4_), channel_id=1, source_target_pairs={{0,16},{16,24},{24,8},{8,0},{1,17},{17,25},{25,9},{9,1},{2,18},{18... | collective-permute-start | bytes 786440 | tf_op jit(solution)/shard_map/ppermute | solution.py:478
  32.5 0.8 copy-done.12
  33.3 2.1 %shard_map.146.refs_0_ = bf16[1024,256]{1,0:T(8,128)(2,1)} custom-call(bf16[256,1024]{1,0:T(8,128)(2,1)} %copy-done.12), custom_call_target="tpu_custom_call" | custom-call | bytes 16384 | tf_op jit(solution)/shard_map/pallas_call | solution.py:359
  37.4 6.4 %shard_map.147 = (bf16[256,1024]{1,0:T(8,128)(2,1)}, f32[256,1024]{1,0:T(8,128)}) custom-call(s32[3]{0:T(128)} %pad_add_fusion.place_ref, bf16[256,1024]{1,0:T(8,128)(2,1)} %copy-done.7, bf16[256,1024]{1,0:T(8,128)(2,1)} %copy-done.8, bf16[256,1024]{1,0:T(8,128)(2,1)} %copy-done.10, bf16[256,1024]{1,0:T(8,128)(2,1)} %copy-done.11, bf16[1024,2048]{1,0:T(8,128)(2,1)} %weight.1), custom_call_target="tpu_custom_call" | custom-call | flops 33554432 | bytes 122880 | tf_op jit(solution)/shard_map/pallas_call | solution.py:294
  43.7 2.1 %collective-permute-start.9 = (bf16[256,1024]{1,0:T(8,128)(2,1)}, bf16[256,1024]{1,0:T(8,128)(2,1)S(1)}, u32[]{:S(2)}, u32[]{:S(2)}) collective-permute-start(bf16[256,1024]{1,0:T(8,128)(2,1)} %get-tuple-element.62), channel_id=1, source_target_pairs={{0,1},{1,0},{2,3},{3,2},{4,5},{5,4},{6,7},{7,6},{8,9},{9,8},{10,11... | collective-permute-start | bytes 1572872 | tf_op jit(solution)/shard_map/ppermute | solution.py:376
  45.9 4.9 %collective-permute-start.8 = (bf16[256,512]{1,0:T(8,128)(2,1)S(1)}, bf16[256,512]{1,0:T(8,128)(2,1)S(1)}, u32[]{:S(2)}, u32[]{:S(2)}) collective-permute-start(bf16[256,512]{1,0:T(8,128)(2,1)S(1)} %collective-permute-done.1.refs_5_), channel_id=1, source_target_pairs={{0,16},{16,24},{24,8},{8,0},{1,17},{17,25},{25,9},{9,1},{2,18},{18... | collective-permute-start | bytes 786440 | tf_op jit(solution)/shard_map/ppermute | solution.py:478
  51.1 5.9 %collective-permute-done.8.refs_6_ = bf16[256,512]{1,0:T(8,128)(2,1)S(1)} collective-permute-done((bf16[256,512]{1,0:T(8,128)(2,1)S(1)}, bf16[256,512]{1,0:T(8,128)(2,1)S(1)}, u32[]{:S(2)}, u32[]{:S(2)}) %collective-permute-start.8) | collective-permute-done | bytes 262176 | tf_op jit(solution)/shard_map/ppermute | solution.py:478
  57.0 3.4 %collective-permute-start.10 = (bf16[256,512]{1,0:T(8,128)(2,1)S(1)}, bf16[256,512]{1,0:T(8,128)(2,1)S(1)}, u32[]{:S(2)}, u32[]{:S(2)}) collective-permute-start(bf16[256,512]{1,0:T(8,128)(2,1)S(1)} %copy-done.14), channel_id=1, source_target_pairs={{0,16},{16,24},{24,8},{8,0},{1,17},{17,25},{25,9},{9,1},{2,18},{18... | collective-permute-start | bytes 786440 | tf_op jit(solution)/shard_map/ppermute | solution.py:478
  60.6 0.8 copy-done.9
  61.4 5.8 %shard_map.148 = (bf16[256,1024]{1,0:T(8,128)(2,1)}, bf16[256,1024]{1,0:T(8,128)(2,1)}, bf16[128,1024]{1,0:T(8,128)(2,1)}, bf16[64,1024]{1,0:T(8,128)(2,1)}, f32[64,1024]{1,0:T(8,128)}) custom-call(bf16[768,384]{1,0:T(8,128)(2,1)} %constant.66.clone.refs_0_, bf16[768,384]{1,0:T(8,128)(2,1)} %constant.67.clone.refs_1_, ...), custom_call_target="tpu_custom_call" | custom-call | flops 20447232 | bytes 96320 | tf_op jit(solution)/shard_map/pallas_call | solution.py:275
  67.3 3.2 %collective-permute-start.17 = (bf16[256,512]{1,0:T(8,128)(2,1)S(1)}, bf16[256,512]{1,0:T(8,128)(2,1)S(1)}, u32[]{:S(2)}, u32[]{:S(2)}) collective-permute-start(bf16[256,512]{1,0:T(8,128)(2,1)S(1)} %collective-permute-done.10.refs_5_), channel_id=1, source_target_pairs={{0,16},{16,24},{24,8},{8,0},{1,17},{17,25},{25,9},{9,1},{2,18},{18... | collective-permute-start | bytes 786440 | tf_op jit(solution)/shard_map/ppermute | solution.py:478
  70.5 1.7 %collective-permute-start.12 = (bf16[64,1024]{1,0:T(8,128)(2,1)}, bf16[64,1024]{1,0:T(8,128)(2,1)S(1)}, u32[]{:S(2)}, u32[]{:S(2)}) collective-permute-start(bf16[64,1024]{1,0:T(8,128)(2,1)} %get-tuple-element.76), channel_id=1, source_target_pairs={{0,1},{1,0},{2,3},{3,2},{4,5},{5,4},{6,7},{7,6},{8,9},{9,8},{10,11... | collective-permute-start | bytes 393224 | tf_op jit(solution)/shard_map/ppermute | solution.py:376
  72.1 1.3 %collective-permute-start.11 = (bf16[128,1024]{1,0:T(8,128)(2,1)}, bf16[128,1024]{1,0:T(8,128)(2,1)S(1)}, u32[]{:S(2)}, u32[]{:S(2)}) collective-permute-start(bf16[128,1024]{1,0:T(8,128)(2,1)} %get-tuple-element.74), channel_id=1, source_target_pairs={{8,0},{16,8},{24,16},{9,1},{17,9},{25,17},{10,2},{18,10},{26,18},{... | collective-permute-start | bytes 786440 | tf_op jit(solution)/shard_map/ppermute | solution.py:536
  74.9 4.8 %shard_map.149 = (bf16[512,512]{1,0:T(8,128)(2,1)}, f32[512,512]{1,0:T(8,128)}) custom-call(s32[5]{0:T(128)} %pad_add_fusion.1.place_ref, bf16[1024,256]{1,0:T(8,128)(2,1)} %shard_map.146.refs_0_, bf16[1024,256]{1,0:T(8,128)(2,1)} %copy-done.2, bf16[1024,256]{1,0:T(8,128)(2,1)} %copy-done.1, bf16[1024,256]{1,0:T(8,128)(2,1)} %copy-done.3, ...), custom_call_target="tpu_custom_call" | custom-call | flops 16777216 | bytes 73728 | tf_op jit(solution)/shard_map/pallas_call | solution.py:294
  79.8 2.7 %collective-permute-start.19 = (bf16[256,512]{1,0:T(8,128)(2,1)S(1)}, bf16[256,512]{1,0:T(8,128)(2,1)S(1)}, u32[]{:S(2)}, u32[]{:S(2)}) collective-permute-start(bf16[256,512]{1,0:T(8,128)(2,1)S(1)} %collective-permute-done.17.refs_6_), channel_id=1, source_target_pairs={{0,16},{16,24},{24,8},{8,0},{1,17},{17,25},{25,9},{9,1},{2,18},{18... | collective-permute-start | bytes 786440 | tf_op jit(solution)/shard_map/ppermute | solution.py:478
  82.6 1.7 %collective-permute-start.20 = (bf16[512,512]{1,0:T(8,128)(2,1)}, bf16[512,512]{1,0:T(8,128)(2,1)S(1)}, u32[]{:S(2)}, u32[]{:S(2)}) collective-permute-start(bf16[512,512]{1,0:T(8,128)(2,1)} %get-tuple-element.90), channel_id=1, source_target_pairs={{0,1},{1,0},{2,3},{3,2},{4,5},{5,4},{6,7},{7,6},{8,9},{9,8},{10,11... | collective-permute-start | bytes 1572872 | tf_op jit(solution)/shard_map/ppermute | solution.py:376
  84.3 5.3 %collective-permute-done.19.refs_7_ = bf16[256,512]{1,0:T(8,128)(2,1)S(1)} collective-permute-done((bf16[256,512]{1,0:T(8,128)(2,1)S(1)}, bf16[256,512]{1,0:T(8,128)(2,1)S(1)}, u32[]{:S(2)}, u32[]{:S(2)}) %collective-permute-start.19) | collective-permute-done | bytes 262176 | tf_op jit(solution)/shard_map/ppermute | solution.py:478
  90.4 4.8 %shard_map.150 = (bf16[512,512]{1,0:T(8,128)(2,1)}, f32[512,512]{1,0:T(8,128)}) custom-call(s32[5]{0:T(128)} %pad_add_fusion.1.place_ref, bf16[1024,256]{1,0:T(8,128)(2,1)} %shard_map.146.refs_0_, bf16[1024,256]{1,0:T(8,128)(2,1)} %copy-done.2, bf16[1024,256]{1,0:T(8,128)(2,1)} %copy-done.1, bf16[1024,256]{1,0:T(8,128)(2,1)} %copy-done.3, ...), custom_call_target="tpu_custom_call" | custom-call | flops 16777216 | bytes 73728 | tf_op jit(solution)/shard_map/pallas_call | solution.py:294
  95.2 2.7 %collective-permute-start.21 = (bf16[64,1024]{1,0:T(8,128)(2,1)S(1)}, bf16[64,1024]{1,0:T(8,128)(2,1)S(1)}, u32[]{:S(2)}, u32[]{:S(2)}) collective-permute-start(bf16[64,1024]{1,0:T(8,128)(2,1)S(1)} %add_convert_fusion), channel_id=1, source_target_pairs={{0,16},{8,24},{16,0},{24,8},{1,17},{9,25},{17,1},{25,9},{2,18},{10... | collective-permute-start | bytes 393224 | tf_op jit(solution)/shard_map/ppermute | solution.py:376
  97.9 1.7 %collective-permute-start.23 = (bf16[512,512]{1,0:T(8,128)(2,1)}, bf16[512,512]{1,0:T(8,128)(2,1)S(1)}, u32[]{:S(2)}, u32[]{:S(2)}) collective-permute-start(bf16[512,512]{1,0:T(8,128)(2,1)} %get-tuple-element.95), channel_id=1, source_target_pairs={{0,1},{1,0},{2,3},{3,2},{4,5},{5,4},{6,7},{7,6},{8,9},{9,8},{10,11... | collective-permute-start | bytes 1572872 | tf_op jit(solution)/shard_map/ppermute | solution.py:376
  99.6 5.5 %shard_map.151 = (bf16[256,1024]{1,0:T(8,128)(2,1)}, bf16[256,1024]{1,0:T(8,128)(2,1)}) custom-call(bf16[768,384]{1,0:T(8,128)(2,1)} %constant.66.clone.refs_0_, bf16[768,384]{1,0:T(8,128)(2,1)} %constant.67.clone.refs_1_, bf16[256,1024]{1,0:T(8,128)(2,1)} %get-tuple-element.73.refs_2_, bf16[128,1024]{1,0:T(8,128)(2,1)} %copy-done.21, ...), custom_call_target="tpu_custom_call" | custom-call | flops 5637144576 | bytes 49216 | tf_op jit(solution)/shard_map/pallas_call | solution.py:275
  105.7 5.6 %collective-permute-done.22 = bf16[64,1024]{1,0:T(8,128)(2,1)S(1)} collective-permute-done((bf16[64,1024]{1,0:T(8,128)(2,1)S(1)}, bf16[64,1024]{1,0:T(8,128)(2,1)S(1)}, u32[]{:S(2)}, u32[]{:S(2)}) %collective-permute-start.22) | collective-permute-done | bytes 131104 | tf_op jit(solution)/shard_map/ppermute | solution.py:376
  111.4 1.0 copy.16
  113.2 1.5 %pad_maximum_fusion = f32[512,1024]{1,0:T(8,128)} fusion(f32[512,512]{1,0:T(8,128)S(1)} %add_multiply_fusion, f32[512,512]{1,0:T(8,128)S(1)} %add_multiply_fusion.1), kind=kLoop, calls=%fused_computation | loop fusion | flops 524288 | bytes 4194304 | tf_op jit(solution)/shard_map/concatenate | solution.py:580
  (83 shorter events, 11.0 us)
Async XLA Ops:
  1.7 12.9 %collective-permute-start.2 = (bf16[256,1024]{1,0:T(8,128)(2,1)}, bf16[256,1024]{1,0:T(8,128)(2,1)S(1)}, u32[]{:S(2)}, u32[]{:S(2)}) collective-permute-start(bf16[256,1024]{1,0:T(8,128)(2,1)} %bitcast.27), channel_id=1, source_target_pairs={{2,4},{4,2},{8,14},{14,8},{18,20},{20,18},{24,30},{30,24},{3,5},{5... | collective-permute-start | bytes 1572872 | tf_op jit(solution)/shard_map/ppermute | solution.py:433
  2.4 11.6 %collective-permute-start = (bf16[128,1024]{1,0:T(8,128)(2,1)S(1)}, bf16[128,1024]{1,0:T(8,128)(2,1)S(1)}, u32[]{:S(2)}, u32[]{:S(2)}) collective-permute-start(bf16[128,1024]{1,0:T(8,128)(2,1)S(1)} %fusion), channel_id=1, source_target_pairs={{0,8},{8,16},{16,24},{1,9},{9,17},{17,25},{2,10},{10,18},{18,26},{... | collective-permute-start | bytes 786440 | tf_op jit(solution)/shard_map/ppermute | solution.py:411
  9.5 15.1 %collective-permute-start.4 = (bf16[256,1024]{1,0:T(8,128)(2,1)}, bf16[256,1024]{1,0:T(8,128)(2,1)S(1)}, u32[]{:S(2)}, u32[]{:S(2)}) collective-permute-start(bf16[256,1024]{1,0:T(8,128)(2,1)} %bitcast.28), channel_id=1, source_target_pairs={{0,0},{1,4},{2,2},{3,6},{4,1},{5,5},{6,3},{7,7},{8,8},{9,12},{10,1... | collective-permute-start | bytes 1572872 | tf_op jit(solution)/shard_map/ppermute | solution.py:420
  14.0 13.3 %collective-permute-start.5 = (bf16[256,1024]{1,0:T(8,128)(2,1)}, bf16[256,1024]{1,0:T(8,128)(2,1)S(1)}, u32[]{:S(2)}, u32[]{:S(2)}) collective-permute-start(bf16[256,1024]{1,0:T(8,128)(2,1)} %bitcast.29), channel_id=1, source_target_pairs={{0,4},{1,0},{2,6},{3,2},{4,5},{5,1},{6,7},{7,3},{8,12},{9,8},{10,1... | collective-permute-start | bytes 1572872 | tf_op jit(solution)/shard_map/ppermute | solution.py:420
  15.8 16.7 %collective-permute-start.3 = (bf16[256,1024]{1,0:T(8,128)(2,1)S(1)}, bf16[256,1024]{1,0:T(8,128)(2,1)S(1)}, u32[]{:S(2)}, u32[]{:S(2)}) collective-permute-start(bf16[256,1024]{1,0:T(8,128)(2,1)S(1)} %broadcast_select_fusion), channel_id=1, source_target_pairs={{0,0},{2,16},{4,12},{6,28},{8,24},{10,8},{12,20},{14,4},{16,2},{18... | collective-permute-start | bytes 1572872 | tf_op jit(solution)/shard_map/ppermute | solution.py:445
  24.6 11.2 %copy-start.7 = (bf16[256,1024]{1,0:T(8,128)(2,1)}, bf16[256,1024]{1,0:T(8,128)(2,1)S(1)}, u32[]{:S(2)}) copy-start(bf16[256,1024]{1,0:T(8,128)(2,1)S(1)} %collective-permute-done.4.first_mine) | copy-start | bytes 1572868
  27.3 8.5 %collective-permute-start.6 = (bf16[256,1024]{1,0:T(8,128)(2,1)S(1)}, bf16[256,1024]{1,0:T(8,128)(2,1)S(1)}, u32[]{:S(2)}, u32[]{:S(2)}) collective-permute-start(bf16[256,1024]{1,0:T(8,128)(2,1)S(1)} %collective-permute-done.4.first_mine), channel_id=1, source_target_pairs={{0,2},{1,3},{2,0},{3,1},{4,6},{5,7},{6,4},{7,5},{8,10},{9,11},{10,... | collective-permute-start | bytes 1572872 | tf_op jit(solution)/shard_map/ppermute | solution.py:486
  30.0 5.7 %collective-permute-start.7 = (bf16[256,1024]{1,0:T(8,128)(2,1)S(1)}, bf16[256,1024]{1,0:T(8,128)(2,1)S(1)}, u32[]{:S(2)}, u32[]{:S(2)}) collective-permute-start(bf16[256,1024]{1,0:T(8,128)(2,1)S(1)} %collective-permute-done.5.second_mine), channel_id=1, source_target_pairs={{0,2},{1,3},{2,0},{3,1},{4,6},{5,7},{6,4},{7,5},{8,10},{9,11},{10,... | collective-permute-start | bytes 1572872 | tf_op jit(solution)/shard_map/ppermute | solution.py:486
  30.1 15.7 %collective-permute-start.1 = (bf16[256,512]{1,0:T(8,128)(2,1)}, bf16[256,512]{1,0:T(8,128)(2,1)S(1)}, u32[]{:S(2)}, u32[]{:S(2)}) collective-permute-start(bf16[256,512]{1,0:T(8,128)(2,1)} %get-tuple-element.53.refs_4_), channel_id=1, source_target_pairs={{0,16},{16,24},{24,8},{8,0},{1,17},{17,25},{25,9},{9,1},{2,18},{18... | collective-permute-start | bytes 786440 | tf_op jit(solution)/shard_map/ppermute | solution.py:478
  35.4 15.4 %copy-start = (bf16[1024,256]{1,0:T(8,128)(2,1)S(1)}, bf16[1024,256]{1,0:T(8,128)(2,1)}, u32[]{:S(2)}) copy-start(bf16[1024,256]{1,0:T(8,128)(2,1)} %shard_map.146.refs_0_) | copy-start | bytes 1572868
  35.4 21.6 %copy-start.14 = (bf16[256,512]{1,0:T(8,128)(2,1)S(1)}, bf16[256,512]{1,0:T(8,128)(2,1)}, u32[]{:S(2)}) copy-start(bf16[256,512]{1,0:T(8,128)(2,1)} %get-tuple-element.71.refs_4_) | copy-start | bytes 786436
  35.4 15.7 %collective-permute-start.14 = (bf16[1024,256]{1,0:T(8,128)(2,1)}, bf16[1024,256]{1,0:T(8,128)(2,1)S(1)}, u32[]{:S(2)}, u32[]{:S(2)}) collective-permute-start(bf16[1024,256]{1,0:T(8,128)(2,1)} %shard_map.146.refs_0_), channel_id=1, source_target_pairs={{0,4},{2,6},{4,0},{6,2},{1,5},{3,7},{5,1},{7,3},{8,12},{10,14},{12... | collective-permute-start | bytes 1572872 | tf_op jit(solution)/shard_map/ppermute | solution.py:499
  43.7 16.8 %collective-permute-start.9 = (bf16[256,1024]{1,0:T(8,128)(2,1)}, bf16[256,1024]{1,0:T(8,128)(2,1)S(1)}, u32[]{:S(2)}, u32[]{:S(2)}) collective-permute-start(bf16[256,1024]{1,0:T(8,128)(2,1)} %get-tuple-element.62), channel_id=1, source_target_pairs={{0,1},{1,0},{2,3},{3,2},{4,5},{5,4},{6,7},{7,6},{8,9},{9,8},{10,11... | collective-permute-start | bytes 1572872 | tf_op jit(solution)/shard_map/ppermute | solution.py:376
  45.9 27.6 %copy-start.15 = (bf16[256,512]{1,0:T(8,128)(2,1)}, bf16[256,512]{1,0:T(8,128)(2,1)S(1)}, u32[]{:S(2)}) copy-start(bf16[256,512]{1,0:T(8,128)(2,1)S(1)} %collective-permute-done.1.refs_5_) | copy-start | bytes 786436
  45.9 11.2 %collective-permute-start.8 = (bf16[256,512]{1,0:T(8,128)(2,1)S(1)}, bf16[256,512]{1,0:T(8,128)(2,1)S(1)}, u32[]{:S(2)}, u32[]{:S(2)}) collective-permute-start(bf16[256,512]{1,0:T(8,128)(2,1)S(1)} %collective-permute-done.1.refs_5_), channel_id=1, source_target_pairs={{0,16},{16,24},{24,8},{8,0},{1,17},{17,25},{25,9},{9,1},{2,18},{18... | collective-permute-start | bytes 786440 | tf_op jit(solution)/shard_map/ppermute | solution.py:478
  50.8 21.4 %collective-permute-start.13 = (bf16[1024,256]{1,0:T(8,128)(2,1)S(1)}, bf16[1024,256]{1,0:T(8,128)(2,1)S(1)}, u32[]{:S(2)}, u32[]{:S(2)}) collective-permute-start(bf16[1024,256]{1,0:T(8,128)(2,1)S(1)} %copy-done), channel_id=1, source_target_pairs={{0,2},{2,0},{4,6},{6,4},{1,3},{3,1},{5,7},{7,5},{8,10},{10,8},{12,... | collective-permute-start | bytes 1572872 | tf_op jit(solution)/shard_map/ppermute | solution.py:499
  51.1 16.1 %copy-start.1 = (bf16[1024,256]{1,0:T(8,128)(2,1)}, bf16[1024,256]{1,0:T(8,128)(2,1)S(1)}, u32[]{:S(2)}) copy-start(bf16[1024,256]{1,0:T(8,128)(2,1)S(1)} %collective-permute-done.14.refs_2_) | copy-start | bytes 1572868
  57.0 16.5 %copy-start.17 = (bf16[256,512]{1,0:T(8,128)(2,1)}, bf16[256,512]{1,0:T(8,128)(2,1)S(1)}, u32[]{:S(2)}) copy-start(bf16[256,512]{1,0:T(8,128)(2,1)S(1)} %collective-permute-done.8.refs_6_) | copy-start | bytes 786436
  57.0 16.4 %collective-permute-start.15 = (bf16[1024,256]{1,0:T(8,128)(2,1)S(1)}, bf16[1024,256]{1,0:T(8,128)(2,1)S(1)}, u32[]{:S(2)}, u32[]{:S(2)}) collective-permute-start(bf16[1024,256]{1,0:T(8,128)(2,1)S(1)} %collective-permute-done.14.refs_2_), channel_id=1, source_target_pairs={{0,2},{2,0},{4,6},{6,4},{1,3},{3,1},{5,7},{7,5},{8,10},{10,8},{12,... | collective-permute-start | bytes 1572872 | tf_op jit(solution)/shard_map/ppermute | solution.py:499
  57.0 10.2 %collective-permute-start.10 = (bf16[256,512]{1,0:T(8,128)(2,1)S(1)}, bf16[256,512]{1,0:T(8,128)(2,1)S(1)}, u32[]{:S(2)}, u32[]{:S(2)}) collective-permute-start(bf16[256,512]{1,0:T(8,128)(2,1)S(1)} %copy-done.14), channel_id=1, source_target_pairs={{0,16},{16,24},{24,8},{8,0},{1,17},{17,25},{25,9},{9,1},{2,18},{18... | collective-permute-start | bytes 786440 | tf_op jit(solution)/shard_map/ppermute | solution.py:478
  60.5 13.0 %collective-permute-start.16 = (bf16[256,512]{1,0:T(8,128)(2,1)S(1)}, bf16[256,512]{1,0:T(8,128)(2,1)S(1)}, u32[]{:S(2)}, u32[]{:S(2)}) collective-permute-start(bf16[256,512]{1,0:T(8,128)(2,1)S(1)} %collective-permute-done.8.refs_6_), channel_id=1, source_target_pairs={{0,16},{16,24},{24,8},{8,0},{1,17},{17,25},{25,9},{9,1},{2,18},{18... | collective-permute-start | bytes 786440 | tf_op jit(solution)/shard_map/ppermute | solution.py:478
  67.2 15.3 %copy-start.13 = (f32[64,1024]{1,0:T(8,128)S(1)}, f32[64,1024]{1,0:T(8,128)}, u32[]{:S(2)}) copy-start(f32[64,1024]{1,0:T(8,128)} %get-tuple-element.75) | copy-start | bytes 786436
  67.2 22.4 %copy-start.16 = (bf16[256,512]{1,0:T(8,128)(2,1)}, bf16[256,512]{1,0:T(8,128)(2,1)S(1)}, u32[]{:S(2)}) copy-start(bf16[256,512]{1,0:T(8,128)(2,1)S(1)} %collective-permute-done.10.refs_5_) | copy-start | bytes 786436
  67.3 12.5 %collective-permute-start.17 = (bf16[256,512]{1,0:T(8,128)(2,1)S(1)}, bf16[256,512]{1,0:T(8,128)(2,1)S(1)}, u32[]{:S(2)}, u32[]{:S(2)}) collective-permute-start(bf16[256,512]{1,0:T(8,128)(2,1)S(1)} %collective-permute-done.10.refs_5_), channel_id=1, source_target_pairs={{0,16},{16,24},{24,8},{8,0},{1,17},{17,25},{25,9},{9,1},{2,18},{18... | collective-permute-start | bytes 786440 | tf_op jit(solution)/shard_map/ppermute | solution.py:478
  70.5 9.3 %collective-permute-start.12 = (bf16[64,1024]{1,0:T(8,128)(2,1)}, bf16[64,1024]{1,0:T(8,128)(2,1)S(1)}, u32[]{:S(2)}, u32[]{:S(2)}) collective-permute-start(bf16[64,1024]{1,0:T(8,128)(2,1)} %get-tuple-element.76), channel_id=1, source_target_pairs={{0,1},{1,0},{2,3},{3,2},{4,5},{5,4},{6,7},{7,6},{8,9},{9,8},{10,11... | collective-permute-start | bytes 393224 | tf_op jit(solution)/shard_map/ppermute | solution.py:376
  72.1 23.0 %collective-permute-start.11 = (bf16[128,1024]{1,0:T(8,128)(2,1)}, bf16[128,1024]{1,0:T(8,128)(2,1)S(1)}, u32[]{:S(2)}, u32[]{:S(2)}) collective-permute-start(bf16[128,1024]{1,0:T(8,128)(2,1)} %get-tuple-element.74), channel_id=1, source_target_pairs={{8,0},{16,8},{24,16},{9,1},{17,9},{25,17},{10,2},{18,10},{26,18},{... | collective-permute-start | bytes 786440 | tf_op jit(solution)/shard_map/ppermute | solution.py:536
  79.8 9.8 %collective-permute-start.19 = (bf16[256,512]{1,0:T(8,128)(2,1)S(1)}, bf16[256,512]{1,0:T(8,128)(2,1)S(1)}, u32[]{:S(2)}, u32[]{:S(2)}) collective-permute-start(bf16[256,512]{1,0:T(8,128)(2,1)S(1)} %collective-permute-done.17.refs_6_), channel_id=1, source_target_pairs={{0,16},{16,24},{24,8},{8,0},{1,17},{17,25},{25,9},{9,1},{2,18},{18... | collective-permute-start | bytes 786440 | tf_op jit(solution)/shard_map/ppermute | solution.py:478
  82.5 12.6 %collective-permute-start.18 = (bf16[64,1024]{1,0:T(8,128)(2,1)S(1)}, bf16[64,1024]{1,0:T(8,128)(2,1)S(1)}, u32[]{:S(2)}, u32[]{:S(2)}) collective-permute-start(bf16[64,1024]{1,0:T(8,128)(2,1)S(1)} %add_convert_fusion.1), channel_id=1, source_target_pairs={{0,8},{8,0},{16,24},{24,16},{1,9},{9,1},{17,25},{25,17},{2,10},{10... | collective-permute-start | bytes 393224 | tf_op jit(solution)/shard_map/ppermute | solution.py:376
  82.6 22.5 %collective-permute-start.20 = (bf16[512,512]{1,0:T(8,128)(2,1)}, bf16[512,512]{1,0:T(8,128)(2,1)S(1)}, u32[]{:S(2)}, u32[]{:S(2)}) collective-permute-start(bf16[512,512]{1,0:T(8,128)(2,1)} %get-tuple-element.90), channel_id=1, source_target_pairs={{0,1},{1,0},{2,3},{3,2},{4,5},{5,4},{6,7},{7,6},{8,9},{9,8},{10,11... | collective-permute-start | bytes 1572872 | tf_op jit(solution)/shard_map/ppermute | solution.py:376
  95.2 9.8 %collective-permute-start.21 = (bf16[64,1024]{1,0:T(8,128)(2,1)S(1)}, bf16[64,1024]{1,0:T(8,128)(2,1)S(1)}, u32[]{:S(2)}, u32[]{:S(2)}) collective-permute-start(bf16[64,1024]{1,0:T(8,128)(2,1)S(1)} %add_convert_fusion), channel_id=1, source_target_pairs={{0,16},{8,24},{16,0},{24,8},{1,17},{9,25},{17,1},{25,9},{2,18},{10... | collective-permute-start | bytes 393224 | tf_op jit(solution)/shard_map/ppermute | solution.py:376
  97.9 15.1 %collective-permute-start.23 = (bf16[512,512]{1,0:T(8,128)(2,1)}, bf16[512,512]{1,0:T(8,128)(2,1)S(1)}, u32[]{:S(2)}, u32[]{:S(2)}) collective-permute-start(bf16[512,512]{1,0:T(8,128)(2,1)} %get-tuple-element.95), channel_id=1, source_target_pairs={{0,1},{1,0},{2,3},{3,2},{4,5},{5,4},{6,7},{7,6},{8,9},{9,8},{10,11... | collective-permute-start | bytes 1572872 | tf_op jit(solution)/shard_map/ppermute | solution.py:376
  105.1 6.2 %collective-permute-start.22 = (bf16[64,1024]{1,0:T(8,128)(2,1)S(1)}, bf16[64,1024]{1,0:T(8,128)(2,1)S(1)}, u32[]{:S(2)}, u32[]{:S(2)}) collective-permute-start(bf16[64,1024]{1,0:T(8,128)(2,1)S(1)} %convert_add_fusion), channel_id=1, source_target_pairs={{0,1},{1,0},{2,3},{3,2},{4,5},{5,4},{6,7},{7,6},{8,9},{9,8},{10,11... | collective-permute-start | bytes 393224 | tf_op jit(solution)/shard_map/ppermute | solution.py:376
  (14 other events, 50.2 us)

commit v14 on v13

--- a/solution.py
+++ b/solution.py
@@ -142,13 +142,12 @@
 
 
 def weight_kernel(count, place_ref, *refs):
-    cot_in, gated_in = refs[:count], refs[count : 2 * count]
-    other, own, cots, gateds, others, owns, in_sem, out_sem = refs[2 * count :]
-    length = gateds.shape[1]
+    cot_in, gated_in = refs[: 2 * count], refs[2 * count : 3 * count]
+    other, own, cots, gateds, others, owns, cot_sem, gated_sem, out_sem = refs[3 * count :]
     rows = other.shape[0]
-    block = min(rows, lanes)
-    copies = [pltpu.make_async_copy(cot_in[n], cots.at[n], in_sem.at[0, n]) for n in range(count)]
-    copies += [pltpu.make_async_copy(gated_in[n], gateds.at[n], in_sem.at[1, n]) for n in range(count)]
+    block = min(rows, turn)
+    copies = [pltpu.make_async_copy(gated_in[n], gateds.at[n], gated_sem.at[n]) for n in range(count)]
+    copies += [pltpu.make_async_copy(cot_in[n], cots.at[n], cot_sem.at[n]) for n in range(2 * count)]
     for copy in copies:
         copy.start()
     for copy in copies:
@@ -163,8 +162,9 @@
         def _(i):
             start = pl.multiple_of(replica * rows + i * block, block)
             total = None
-            for n in range(count):
-                part = dot(cots[n, pl.ds(start, block), :], gateds[place_ref[n]])
+            for n in range(2 * count):
+                gated = gateds[place_ref[n % count], n // count]
+                part = dot(cots[n, pl.ds(start, block), :], gated)
                 total = part if total is None else total + part
             target[pl.ds(pl.multiple_of(i * block, block), block), :] = total.astype(target.dtype)
 
@@ -224,7 +224,7 @@
     return pl.CostEstimate(flops=flops // 64, bytes_accessed=moved // 64, transcendentals=0)
 
 
-def by_channel(body, tables, args, outs, channels, flops):
+def by_channel(body, tables, args, outs, channels, flops, swap=None):
     steps = channels // lanes
     flat_outs = [o for group in outs for o in group]
     n_tables, n_args, n_outs = len(tables), len(args), len(outs)
@@ -238,6 +238,7 @@
     def kernel(*refs):
         refs = list(refs)
         take = lambda count: [refs.pop(0) for _ in range(count)]
+        swap_ref = None if swap is None else refs.pop(0)
         table_in, arg_in, outs_to = take(n_tables), take(n_args), take(len(flat_outs))
         table_held, arg_held, out_held = take(n_tables), take(n_args), take(n_outs)
         table_sem, arg_sem, out_sem = refs
@@ -250,8 +251,7 @@
             return pltpu.make_async_copy(arg_in[k], arg_held[k], arg_sem.at[k])
 
         def out_copy(k, n, i):
-            per = steps // len(groups[k])
-            place = part(groups[k][n], i - n * per, per)
+            place = groups[k][n] if len(groups[k]) > 1 else part(groups[k][n], i, steps)
             return pltpu.make_async_copy(out_held[k].at[i], place, out_sem.at[k, i])
 
         for k in range(n_tables):
@@ -266,15 +266,21 @@
         for i in range(steps):
             body(*table_held, *[part(ref, i, steps) for ref in arg_held], *[held.at[i] for held in out_held])
             for k in range(n_outs):
-                out_copy(k, i * len(groups[k]) // steps, i).start()
+                count = len(groups[k])
+                if count == 1:
+                    out_copy(k, 0, i).start()
+                else:
+                    pl.when(swap_ref[0] == 0)(out_copy(k, i, i).start)
+                    pl.when(swap_ref[0] != 0)(out_copy(k, count - 1 - i, i).start)
 
         for i in range(steps):
             for k in range(n_outs):
-                out_copy(k, i * len(groups[k]) // steps, i).wait()
+                out_copy(k, 0 if len(groups[k]) == 1 else i, i).wait()
 
     return pl.pallas_call(
         kernel,
-        in_specs=[pl.BlockSpec(memory_space=pl.ANY)] * (n_tables + n_args),
+        in_specs=[pl.BlockSpec(memory_space=pltpu.SMEM)] * (swap is not None)
+        + [pl.BlockSpec(memory_space=pl.ANY)] * (n_tables + n_args),
         out_specs=[pl.BlockSpec(memory_space=pl.ANY)] * len(flat_outs),
         out_shape=flat_outs,
         scratch_shapes=[
@@ -287,7 +293,7 @@
         ],
         compiler_params=pltpu.CompilerParams(vmem_limit_bytes=vmem_bytes),
         cost_estimate=estimate(flops, [*args, *flat_outs]),
-    )(*[jnp.asarray(t) for t in tables], *args)
+    )(*([] if swap is None else [swap]), *[jnp.asarray(t) for t in tables], *args)
 
 
 def local_call(kernel, places, args, outs, scratch, flops):
@@ -326,7 +332,7 @@
 
 def weight_sum(places, cot_pieces, gated_pieces, rows):
     count = len(gated_pieces)
-    length, width = gated_pieces[0].shape
+    _, length, width = gated_pieces[0].shape
     outs = [jax.ShapeDtypeStruct((rows, width), dtype) for dtype in (bf16, f32)]
     return local_call(
         functools.partial(weight_kernel, count),
@@ -334,13 +340,14 @@
         [*cot_pieces, *gated_pieces],
         outs,
         [
-            pltpu.VMEM((count, *cot_pieces[0].shape), bf16),
-            pltpu.VMEM((count, length, width), bf16),
+            pltpu.VMEM((2 * count, *cot_pieces[0].shape), bf16),
+            pltpu.VMEM((count, *gated_pieces[0].shape), bf16),
             *[pltpu.VMEM(o.shape, o.dtype) for o in outs],
-            pltpu.SemaphoreType.DMA((2, count)),
+            pltpu.SemaphoreType.DMA((2 * count,)),
+            pltpu.SemaphoreType.DMA((count,)),
             pltpu.SemaphoreType.DMA((2,)),
         ],
-        4 * count * length * rows * width,
+        8 * count * length * rows * width,
     )
 
 
@@ -470,40 +477,46 @@
         [[rows32], [half16, half16]],
         channels,
         unit * (4 * taps + 5 * length),
+        jnp.reshape(me_dp if square else 0 * me_dp, (1,)).astype(jnp.int32),
     )
     if square:
-        halves = [[half] for half in gated]
-
-        def ring_step(pieces):
-            pieces.append(lax.ppermute(pieces[-1], "seq", ring))
-
-        ring_step(halves[0])
-        halves[1][0], *rounds = lax.optimization_barrier((halves[1][0], *rounds))
-    else:
-        gated[0], *rounds = lax.optimization_barrier((gated[0], *rounds))
+        ring_pieces = [jnp.stack([gated[0], swap_pairs(gated[1], "dp", 1)])]
+
+        def ring_step():
+            ring_pieces.append(lax.ppermute(ring_pieces[-1], "seq", ring))
+
+        ring_step()
+    gated[0], *rounds = lax.optimization_barrier((gated[0], *rounds))
 
     route = [(tp_dp(h, c, d), tp_dp(h, (c + 1) % subs, d)) for h, c, d in places]
     theirs = [lax.ppermute(r, ("tp", "dp"), route) for r in rounds]
     firsts, seconds = zip(rounds, theirs)
     rows = n_tp * channels // (n_seq * n_dp)
     if square:
-        moved = transposed(after(moved, *rounds))
+        moved = after(moved, *rounds)
+        moved_other = swap_pairs(moved, "dp", 1)
+        moved = transposed(moved)
         moved, place = lax.optimization_barrier((moved, place))
     other_sent, own_part = project(place, firsts, seconds, out_weight)
     other_part = swap_pairs(other_sent, "dp", 1)
     if square:
-        halves[0][1] = after(halves[0][1], other_sent)
-        ring_step(halves[0])
-
-    if square:
-        sent_by = lambda value, flip: lax.ppermute(value, "tp", [(t, t ^ flip) for t in range(n_tp)])
-        across = sent_by(moved, subs)
-        cot_pieces = [moved, sent_by(moved, 1), across, sent_by(after(across, halves[0][2]), 1)]
-        halves[0][2], halves[1][0], own_part = lax.optimization_barrier(
-            (halves[0][2], halves[1][0], own_part)
-        )
-        ring_step(halves[0])
-        ring_step(halves[1])
+
+        def spread(piece, gate):
+            across = lax.ppermute(piece, "tp", [(t, t ^ subs) for t in range(n_tp)])
+            near = [(t, t ^ 1) for t in range(n_tp)]
+            return [
+                piece,
+                lax.ppermute(piece, "tp", near),
+                across,
+                lax.ppermute(after(across, gate), "tp", near),
+            ]
+
+        moved_other = transposed(after(moved_other, other_sent))
+        ring_pieces[1] = after(ring_pieces[1], other_sent)
+        ring_step()
+        ring_pieces[2], own_part = lax.optimization_barrier((ring_pieces[2], own_part))
+        ring_step()
+        cot_pieces = spread(moved, ring_pieces[2]) + spread(moved_other, own_part)
     else:
         full = lax.all_gather(cot, "tp", axis=1, tiled=True)
         cot_all = lax.all_to_all(full, "seq", 1, 0, tiled=True)
@@ -547,39 +560,40 @@
 
     received = swap_pairs(sent_lag, "dp", 1)
     if square:
-        weight_place, halves[1][1], signal = lax.optimization_barrier((weight_place, halves[1][1], signal))
-        ring_step(halves[1])
-        first_sent, first_own = weight_sum(weight_place, cot_pieces, halves[0], rows)
-        first_received = swap_pairs(first_sent, "dp", 1)
-        received, first_own, halves[1][2] = lax.optimization_barrier((received, first_own, halves[1][2]))
-        ring_step(halves[1])
+        ring_pieces[3], received = lax.optimization_barrier((ring_pieces[3], received))
     lag_sum = own_lag + received.astype(f32)
     distance = 1
     while distance < n_seq:
         rounded = lag_sum.astype(bf16)
         received = swap_pairs(rounded, "seq", distance)
         if square and distance == 1:
-            second_sent, second_own = weight_sum(weight_place, cot_pieces, halves[1], rows)
-            second_received = swap_pairs(second_sent, "dp", 1)
-            received, second_own = lax.optimization_barrier((received, second_own))
+            weight_place, rounded = lax.optimization_barrier((weight_place, rounded))
+            weight_sent, weight_own = weight_sum(weight_place, cot_pieces, ring_pieces, rows)
+            weight_received = swap_pairs(weight_sent, "dp", 1)
+            received, weight_own = lax.optimization_barrier((received, weight_own))
         lag_sum = rounded.astype(f32) + received.astype(f32)
         distance *= 2
-    if square:
-        first_received, lag_sum = lax.optimization_barrier((first_received, lag_sum))
     mine = lag_sum.astype(bf16)
     theirs = swap_pairs(mine, "dp", 1)
-    grad_key, grad_value = run_back(after(later, second_own) if square else later)
+    grad_key, grad_value = run_back(after(later, weight_own) if square else later)
     first = me_dp == 0
     lag_sum = jnp.concatenate([jnp.where(first, mine, theirs), jnp.where(first, theirs, mine)], axis=0)
     grad_filter = lag_sum.astype(f32).T * (norm_factor * scale)
 
     if square:
-        parts = [(first_own, first_received), (second_own, second_received)]
+        weight_own, weight_received = weight_own * norm_factor, weight_received.astype(f32) * norm_factor
+        grad_weight = jnp.concatenate(
+            [
+                jnp.where(first, weight_own, weight_received),
+                jnp.where(first, weight_received, weight_own),
+            ],
+            axis=1,
+        )
     else:
         parts = [weight_one(half) for half in gated_all]
-    grad_weight = jnp.concatenate(
-        [(mine + theirs.astype(f32)) * norm_factor for mine, theirs in parts], axis=1
-    )
+        grad_weight = jnp.concatenate(
+            [(mine + theirs.astype(f32)) * norm_factor for mine, theirs in parts], axis=1
+        )
     return (
         grad_query[None],
         grad_key[None],

time: 115 us -> 128 us (1.11)
  starting transfers between devices: 42.8 us -> 49.3 us
  waiting for transfers between devices: 22.3 us -> 26.6 us
    ppermute x9, starting transfers between devices: 17.5 us -> 24.4 us  [the longest x3 20.4 us: ring_step(): ring_pieces.append(lax.ppermute(ring_pieces[-1], 'seq', ring))]
    ppermute x7 -> x8, waiting for transfers between devices: 5.65 us -> 11.3 us  [swap_pairs(): return lax.ppermute(value, axis, [(i, i ^ distance) for i in range(count)])]
    pallas_call x3 -> x2, Pallas kernels: 16 us -> 13.7 us  [local_call(): pl.pallas_call(kernel, in_specs=[pl.BlockSpec(memory_space=pltpu.SMEM)] +...]
    pallas_call x1 -> x2, Pallas kernels: 2.07 us -> 4.07 us  [transposed(): pl.pallas_call(transpose_kernel, in_specs=[pl.BlockSpec(memory_space=pl.A...]
    ppermute x2, starting transfers between devices: 2.84 us -> 1.19 us  [per_device(): theirs = [lax.ppermute(r, ('tp', 'dp'), route) for r in rounds]]
    ppermute x9, waiting for transfers between devices: 11.2 us -> 9.73 us  [the longest x3 7.21 us: ring_step(): ring_pieces.append(lax.ppermute(ring_pieces[-1], 'seq', ring))]
    ppermute x7 -> x8, starting transfers between devices: 10.3 us -> 11 us  [swap_pairs(): return lax.ppermute(value, axis, [(i, i ^ distance) for i in range(count)])]
    unnamed x45 -> x47, local copies, waits for them, and re-layouts: 6.38 us -> 6.67 us
  transfers between devices with their start and end apart: 24 -> 25, of which waited for: 5 -> 10; matrix products, arithmetic and copies ran while one was open for 5% -> 5% of each run, Pallas kernels for 30% -> 27%
where the time goes in v14:
time: 128 us; the launch traced here: 127 us
  starting transfers between devices  49.3 us (39%)
  Pallas kernels  34.6 us (27%)
  waiting for transfers between devices  26.6 us (21%)
  local copies, waits for them, and re-layouts  8.55 us (7%)
  other arithmetic  6.45 us (5%)
    ppermute x3, starting transfers between devices, ring_step(): ring_pieces.append(lax.ppermute(ring_pieces[-1], 'seq', ring))  20.4 us
    pallas_call x3, Pallas kernels, by_channel(): pl.pallas_call(kernel, in_specs=[pl.BlockSpec(memory_space=pltpu.SMEM)] *...  16.8 us
    pallas_call x2, Pallas kernels, local_call(): pl.pallas_call(kernel, in_specs=[pl.BlockSpec(memory_space=pltpu.SMEM)] +...  13.7 us
    ppermute x8, waiting for transfers between devices, swap_pairs(): return lax.ppermute(value, axis, [(i, i ^ distance) for i in range(count)])  11.3 us
    ppermute x8, starting transfers between devices, swap_pairs(): return lax.ppermute(value, axis, [(i, i ^ distance) for i in range(count)])  11 us
    ppermute x3, waiting for transfers between devices, ring_step(): ring_pieces.append(lax.ppermute(ring_pieces[-1], 'seq', ring))  7.21 us
    ppermute x1, starting transfers between devices, per_device(): prior = lax.ppermute(tail, 'seq', [(i, i + 1) for i in range(n_seq - 1)])  7.09 us
    unnamed x47, local copies, waits for them, and re-layouts  6.67 us
  transfers between devices with their start and end apart: 25, of which 10 were waited for; matrix products, arithmetic and copies ran while one was open for 5% of the time, Pallas kernels for 27%

profile of v14, /device:TPU:0, one launch (start us, length us, event | category | flops | bytes accessed | tf_op | source)
XLA Modules:
  0.0 126.6 jit_solution(5499334654040338771)
XLA Ops:
  0.6 1.2 fusion.2
  2.5 7.1 %collective-permute-start = (bf16[128,1024]{1,0:T(8,128)(2,1)S(1)}, bf16[128,1024]{1,0:T(8,128)(2,1)S(1)}, u32[]{:S(2)}, u32[]{:S(2)}) collective-permute-start(bf16[128,1024]{1,0:T(8,128)(2,1)S(1)} %fusion.2), channel_id=1, source_target_pairs={{0,8},{8,16},{16,24},{1,9},{9,17},{17,25},{2,10},{10,18},{18,26},{... | collective-permute-start | bytes 786440 | tf_op jit(solution)/shard_map/ppermute | solution.py:418
  9.6 1.7 %collective-permute-start.5 = (bf16[256,1024]{1,0:T(8,128)(2,1)}, bf16[256,1024]{1,0:T(8,128)(2,1)S(1)}, u32[]{:S(2)}, u32[]{:S(2)}) collective-permute-start(bf16[256,1024]{1,0:T(8,128)(2,1)} %bitcast.30), channel_id=1, source_target_pairs={{0,0},{1,4},{2,2},{3,6},{4,1},{5,5},{6,3},{7,7},{8,8},{9,12},{10,1... | collective-permute-start | bytes 1572872 | tf_op jit(solution)/shard_map/ppermute | solution.py:427
  12.0 2.1 %collective-permute-done.refs_3_.refs_6_ = bf16[128,1024]{1,0:T(8,128)(2,1)S(1)} collective-permute-done((bf16[128,1024]{1,0:T(8,128)(2,1)S(1)}, bf16[128,1024]{1,0:T(8,128)(2,1)S(1)}, u32[]{:S(2)}, u32[]{:S(2)}) %collective-permute-start) | collective-permute-done | bytes 262176 | tf_op jit(solution)/shard_map/ppermute | solution.py:418
  14.1 1.2 collective-permute-start.6
  17.1 5.5 %shard_map.145 = (f32[256,1024]{1,0:T(8,128)}, bf16[256,512]{1,0:T(8,128)(2,1)}, bf16[256,512]{1,0:T(8,128)(2,1)}) custom-call(s32[1]{0:T(128)} %bitcast.refs_0_, bf16[768,384]{1,0:T(8,128)(2,1)} %constant.66.clone.refs_1_.refs_0_, bf16[768,384]{1,0:T(8,128)(2,1)} %constant.67.clone.refs_2_.refs_1_, bf16[128,1024]{1,0:T(8,128)(2,1)} %copy-done.4, ...), custom_call_target="tpu_custom_call" | custom-call | flops 22020096 | bytes 57408 | tf_op jit(solution)/shard_map/pallas_call | solution.py:280
  24.3 3.5 %collective-permute-done.6.second_mine = bf16[256,1024]{1,0:T(8,128)(2,1)S(1)} collective-permute-done((bf16[256,1024]{1,0:T(8,128)(2,1)}, bf16[256,1024]{1,0:T(8,128)(2,1)S(1)}, u32[]{:S(2)}, u32[]{:S(2)}) %collective-permute-start.6) | collective-permute-done | bytes 524320 | tf_op jit(solution)/shard_map/ppermute | solution.py:427
  27.8 1.1 collective-permute-start.7
  29.0 3.4 %collective-permute-done.1 = bf16[256,512]{1,0:T(8,128)(2,1)S(1)} collective-permute-done((bf16[256,512]{1,0:T(8,128)(2,1)}, bf16[256,512]{1,0:T(8,128)(2,1)S(1)}, u32[]{:S(2)}, u32[]{:S(2)}) %collective-permute-start.1) | collective-permute-done | bytes 262176 | tf_op jit(solution)/shard_map/ppermute | solution.py:383
  33.4 5.4 %collective-permute-start.2 = (bf16[2,256,512]{2,1,0:T(8,128)(2,1)S(1)}, bf16[2,256,512]{2,1,0:T(8,128)(2,1)S(1)}, u32[]{:S(2)}, u32[]{:S(2)}) collective-permute-start(bf16[2,256,512]{2,1,0:T(8,128)(2,1)S(1)} %pad_maximum_fusion.1.refs_8_), channel_id=1, source_target_pairs={{0,16},{16,24},{24,8},{8,0},{1,17},{17,25},{25,9},{9,1},{2,18},{18... | collective-permute-start | bytes 1572872 | tf_op jit(solution)/shard_map/ppermute | solution.py:486
  39.5 2.0 %shard_map.146.refs_0_ = bf16[1024,256]{1,0:T(8,128)(2,1)} custom-call(bf16[256,1024]{1,0:T(8,128)(2,1)} %copy-done.20), custom_call_target="tpu_custom_call" | custom-call | bytes 16384 | tf_op jit(solution)/shard_map/pallas_call | solution.py:366
  43.2 6.4 %shard_map.147 = (bf16[256,1024]{1,0:T(8,128)(2,1)}, f32[256,1024]{1,0:T(8,128)}) custom-call(s32[3]{0:T(128)} %pad_add_fusion.place_ref, bf16[256,1024]{1,0:T(8,128)(2,1)} %copy-done.5, bf16[256,1024]{1,0:T(8,128)(2,1)} %copy-done.11, bf16[256,1024]{1,0:T(8,128)(2,1)} %copy-done.17, bf16[256,1024]{1,0:T(8,128)(2,1)} %copy-done.18, bf16[1024,2048]{1,0:T(8,128)(2,1)} %weight.1), custom_call_target="tpu_custom_call" | custom-call | flops 33554432 | bytes 122880 | tf_op jit(solution)/shard_map/pallas_call | solution.py:300
  50.3 13.5 %collective-permute-start.9 = (bf16[2,256,512]{2,1,0:T(8,128)(2,1)S(1)}, bf16[2,256,512]{2,1,0:T(8,128)(2,1)S(1)}, u32[]{:S(2)}, u32[]{:S(2)}) collective-permute-start(bf16[2,256,512]{2,1,0:T(8,128)(2,1)S(1)} %collective-permute-done.2.refs_9_), channel_id=1, source_target_pairs={{0,16},{16,24},{24,8},{8,0},{1,17},{17,25},{25,9},{9,1},{2,18},{18... | collective-permute-start | bytes 1572872 | tf_op jit(solution)/shard_map/ppermute | solution.py:486
  63.8 1.3 %collective-permute-start.10 = (bf16[256,1024]{1,0:T(8,128)(2,1)}, bf16[256,1024]{1,0:T(8,128)(2,1)S(1)}, u32[]{:S(2)}, u32[]{:S(2)}) collective-permute-start(bf16[256,1024]{1,0:T(8,128)(2,1)} %get-tuple-element.56), channel_id=1, source_target_pairs={{0,1},{1,0},{2,3},{3,2},{4,5},{5,4},{6,7},{7,6},{8,9},{9,8},{10,11... | collective-permute-start | bytes 1572872 | tf_op jit(solution)/shard_map/ppermute | solution.py:383
  65.1 3.4 %collective-permute-start.16 = (bf16[1024,256]{1,0:T(8,128)(2,1)S(1)}, bf16[1024,256]{1,0:T(8,128)(2,1)S(1)}, u32[]{:S(2)}, u32[]{:S(2)}) collective-permute-start(bf16[1024,256]{1,0:T(8,128)(2,1)S(1)} %copy-done.1), channel_id=1, source_target_pairs={{0,4},{2,6},{4,0},{6,2},{1,5},{3,7},{5,1},{7,3},{8,12},{10,14},{12... | collective-permute-start | bytes 1572872 | tf_op jit(solution)/shard_map/ppermute | solution.py:505
  69.3 2.0 %shard_map.149.refs_4_ = bf16[1024,256]{1,0:T(8,128)(2,1)} custom-call(bf16[256,1024]{1,0:T(8,128)(2,1)} %copy-done.21), custom_call_target="tpu_custom_call" | custom-call | bytes 16384 | tf_op jit(solution)/shard_map/pallas_call | solution.py:366
  71.5 5.8 %collective-permute-done.9.refs_10_ = bf16[2,256,512]{2,1,0:T(8,128)(2,1)S(1)} collective-permute-done((bf16[2,256,512]{2,1,0:T(8,128)(2,1)S(1)}, bf16[2,256,512]{2,1,0:T(8,128)(2,1)S(1)}, u32[]{:S(2)}, u32[]{:S(2)}) %collective-permute-start.9) | collective-permute-done | bytes 524320 | tf_op jit(solution)/shard_map/ppermute | solution.py:486
  77.3 1.5 %collective-permute-start.12 = (bf16[2,256,512]{2,1,0:T(8,128)(2,1)S(1)}, bf16[2,256,512]{2,1,0:T(8,128)(2,1)S(1)}, u32[]{:S(2)}, u32[]{:S(2)}) collective-permute-start(bf16[2,256,512]{2,1,0:T(8,128)(2,1)S(1)} %collective-permute-done.9.refs_10_), channel_id=1, source_target_pairs={{0,16},{16,24},{24,8},{8,0},{1,17},{17,25},{25,9},{9,1},{2,18},{18... | collective-permute-start | bytes 1572872 | tf_op jit(solution)/shard_map/ppermute | solution.py:486
  79.6 5.9 %shard_map.148 = (bf16[256,1024]{1,0:T(8,128)(2,1)}, bf16[256,1024]{1,0:T(8,128)(2,1)}, bf16[128,1024]{1,0:T(8,128)(2,1)}, bf16[64,1024]{1,0:T(8,128)(2,1)}, f32[64,1024]{1,0:T(8,128)}) custom-call(bf16[768,384]{1,0:T(8,128)(2,1)} %constant.66.clone.refs_1_.refs_0_, bf16[768,384]{1,0:T(8,128)(2,1)} %constant.67.clone.refs_2_.refs_1_, ...), custom_call_target="tpu_custom_call" | custom-call | flops 20447232 | bytes 96320 | tf_op jit(solution)/shard_map/pallas_call | solution.py:280
  85.5 1.7 %collective-permute-start.13 = (bf16[64,1024]{1,0:T(8,128)(2,1)}, bf16[64,1024]{1,0:T(8,128)(2,1)S(1)}, u32[]{:S(2)}, u32[]{:S(2)}) collective-permute-start(bf16[64,1024]{1,0:T(8,128)(2,1)} %get-tuple-element.67), channel_id=1, source_target_pairs={{0,1},{1,0},{2,3},{3,2},{4,5},{5,4},{6,7},{7,6},{8,9},{9,8},{10,11... | collective-permute-start | bytes 393224 | tf_op jit(solution)/shard_map/ppermute | solution.py:383
  87.8 2.5 %collective-permute-done.20.refs_6_ = bf16[1024,256]{1,0:T(8,128)(2,1)S(1)} collective-permute-done((bf16[1024,256]{1,0:T(8,128)(2,1)}, bf16[1024,256]{1,0:T(8,128)(2,1)S(1)}, u32[]{:S(2)}, u32[]{:S(2)}) %collective-permute-start.20) | collective-permute-done | bytes 524320 | tf_op jit(solution)/shard_map/ppermute | solution.py:505
  91.4 1.1 add_convert_fusion.2
  92.6 1.1 collective-permute-start.14
  93.7 1.3 %collective-permute-start.11 = (bf16[128,1024]{1,0:T(8,128)(2,1)}, bf16[128,1024]{1,0:T(8,128)(2,1)S(1)}, u32[]{:S(2)}, u32[]{:S(2)}) collective-permute-start(bf16[128,1024]{1,0:T(8,128)(2,1)} %get-tuple-element.64), channel_id=1, source_target_pairs={{8,0},{16,8},{24,16},{9,1},{17,9},{25,17},{10,2},{18,10},{26,18},{... | collective-permute-start | bytes 786440 | tf_op jit(solution)/shard_map/ppermute | solution.py:549
  96.7 7.4 %shard_map.150 = (bf16[512,512]{1,0:T(8,128)(2,1)}, f32[512,512]{1,0:T(8,128)}) custom-call(s32[5]{0:T(128)} %pad_add_fusion.1.place_ref, bf16[1024,256]{1,0:T(8,128)(2,1)} %shard_map.146.refs_0_, bf16[1024,256]{1,0:T(8,128)(2,1)} %copy-done.12, bf16[1024,256]{1,0:T(8,128)(2,1)} %copy-done.8, bf16[1024,256]{1,0:T(8,128)(2,1)} %copy-done.14, ...), custom_call_target="tpu_custom_call" | custom-call | flops 33554432 | bytes 122880 | tf_op jit(solution)/shard_map/pallas_call | solution.py:300
  104.2 3.1 %collective-permute-start.22 = (bf16[64,1024]{1,0:T(8,128)(2,1)S(1)}, bf16[64,1024]{1,0:T(8,128)(2,1)S(1)}, u32[]{:S(2)}, u32[]{:S(2)}) collective-permute-start(bf16[64,1024]{1,0:T(8,128)(2,1)S(1)} %add_convert_fusion.1), channel_id=1, source_target_pairs={{0,16},{8,24},{16,0},{24,8},{1,17},{9,25},{17,1},{25,9},{2,18},{10... | collective-permute-start | bytes 393224 | tf_op jit(solution)/shard_map/ppermute | solution.py:383
  107.3 1.3 %collective-permute-start.24 = (bf16[512,512]{1,0:T(8,128)(2,1)}, bf16[512,512]{1,0:T(8,128)(2,1)S(1)}, u32[]{:S(2)}, u32[]{:S(2)}) collective-permute-start(bf16[512,512]{1,0:T(8,128)(2,1)} %get-tuple-element.83), channel_id=1, source_target_pairs={{0,1},{1,0},{2,3},{3,2},{4,5},{5,4},{6,7},{7,6},{8,9},{9,8},{10,11... | collective-permute-start | bytes 1572872 | tf_op jit(solution)/shard_map/ppermute | solution.py:383
  108.6 4.5 %collective-permute-done.22 = bf16[64,1024]{1,0:T(8,128)(2,1)S(1)} collective-permute-done((bf16[64,1024]{1,0:T(8,128)(2,1)S(1)}, bf16[64,1024]{1,0:T(8,128)(2,1)S(1)}, u32[]{:S(2)}, u32[]{:S(2)}) %collective-permute-start.22) | collective-permute-done | bytes 131104 | tf_op jit(solution)/shard_map/ppermute | solution.py:383
  113.2 1.6 %collective-permute-start.23 = (bf16[64,1024]{1,0:T(8,128)(2,1)S(1)}, bf16[64,1024]{1,0:T(8,128)(2,1)S(1)}, u32[]{:S(2)}, u32[]{:S(2)}) collective-permute-start(bf16[64,1024]{1,0:T(8,128)(2,1)S(1)} %add_convert_fusion), channel_id=1, source_target_pairs={{0,1},{1,0},{2,3},{3,2},{4,5},{5,4},{6,7},{7,6},{8,9},{9,8},{10,11... | collective-permute-start | bytes 393224 | tf_op jit(solution)/shard_map/ppermute | solution.py:383
  114.8 5.5 %shard_map.151 = (bf16[256,1024]{1,0:T(8,128)(2,1)}, bf16[256,1024]{1,0:T(8,128)(2,1)}) custom-call(bf16[768,384]{1,0:T(8,128)(2,1)} %constant.66.clone.refs_1_.refs_0_, bf16[768,384]{1,0:T(8,128)(2,1)} %constant.67.clone.refs_2_.refs_1_, bf16[256,1024]{1,0:T(8,128)(2,1)} %get-tuple-element.63.refs_2_, bf16[128,1024]{1,0:T(8,128)(2,1)} %copy-done.22, ...), custom_call_target="tpu_custom_call" | custom-call | flops 5637144576 | bytes 49216 | tf_op jit(solution)/shard_map/pallas_call | solution.py:280
  120.3 2.9 %collective-permute-done.23 = bf16[64,1024]{1,0:T(8,128)(2,1)S(1)} collective-permute-done((bf16[64,1024]{1,0:T(8,128)(2,1)S(1)}, bf16[64,1024]{1,0:T(8,128)(2,1)S(1)}, u32[]{:S(2)}, u32[]{:S(2)}) %collective-permute-start.23) | collective-permute-done | bytes 131104 | tf_op jit(solution)/shard_map/ppermute | solution.py:383
  125.1 1.5 %pad_maximum_fusion = f32[512,1024]{1,0:T(8,128)} fusion(f32[512,512]{1,0:T(8,128)S(1)} %get-tuple-element.91, f32[512,512]{1,0:T(8,128)S(1)} %get-tuple-element.90), kind=kLoop, calls=%fused_computation | loop fusion | flops 524288 | bytes 4194304 | tf_op jit(solution)/shard_map/concatenate | solution.py:585
  (87 shorter events, 16.1 us)
Async XLA Ops:
  0.6 22.8 %copy-start.19 = (bf16[1,256,1024]{2,1,0:T(8,128)(2,1)S(1)}, bf16[1,256,1024]{2,1,0:T(8,128)(2,1)}, u32[]{:S(2)}) copy-start(bf16[1,256,1024]{2,1,0:T(8,128)(2,1)} %param.16) | copy-start | bytes 1572868
  1.8 21.7 %collective-permute-start.3 = (bf16[256,1024]{1,0:T(8,128)(2,1)}, bf16[256,1024]{1,0:T(8,128)(2,1)S(1)}, u32[]{:S(2)}, u32[]{:S(2)}) collective-permute-start(bf16[256,1024]{1,0:T(8,128)(2,1)} %bitcast.29), channel_id=1, source_target_pairs={{2,4},{4,2},{8,14},{14,8},{18,20},{20,18},{24,30},{30,24},{3,5},{5... | collective-permute-start | bytes 1572872 | tf_op jit(solution)/shard_map/ppermute | solution.py:440
  2.5 11.6 %collective-permute-start = (bf16[128,1024]{1,0:T(8,128)(2,1)S(1)}, bf16[128,1024]{1,0:T(8,128)(2,1)S(1)}, u32[]{:S(2)}, u32[]{:S(2)}) collective-permute-start(bf16[128,1024]{1,0:T(8,128)(2,1)S(1)} %fusion.2), channel_id=1, source_target_pairs={{0,8},{8,16},{16,24},{1,9},{9,17},{17,25},{2,10},{10,18},{18,26},{... | collective-permute-start | bytes 786440 | tf_op jit(solution)/shard_map/ppermute | solution.py:418
  9.6 14.6 %collective-permute-start.5 = (bf16[256,1024]{1,0:T(8,128)(2,1)}, bf16[256,1024]{1,0:T(8,128)(2,1)S(1)}, u32[]{:S(2)}, u32[]{:S(2)}) collective-permute-start(bf16[256,1024]{1,0:T(8,128)(2,1)} %bitcast.30), channel_id=1, source_target_pairs={{0,0},{1,4},{2,2},{3,6},{4,1},{5,5},{6,3},{7,7},{8,8},{9,12},{10,1... | collective-permute-start | bytes 1572872 | tf_op jit(solution)/shard_map/ppermute | solution.py:427
  14.1 13.7 %collective-permute-start.6 = (bf16[256,1024]{1,0:T(8,128)(2,1)}, bf16[256,1024]{1,0:T(8,128)(2,1)S(1)}, u32[]{:S(2)}, u32[]{:S(2)}) collective-permute-start(bf16[256,1024]{1,0:T(8,128)(2,1)} %bitcast.31), channel_id=1, source_target_pairs={{0,4},{1,0},{2,6},{3,2},{4,5},{5,1},{6,7},{7,3},{8,12},{9,8},{10,1... | collective-permute-start | bytes 1572872 | tf_op jit(solution)/shard_map/ppermute | solution.py:427
  22.6 9.8 %collective-permute-start.1 = (bf16[256,512]{1,0:T(8,128)(2,1)}, bf16[256,512]{1,0:T(8,128)(2,1)S(1)}, u32[]{:S(2)}, u32[]{:S(2)}) collective-permute-start(bf16[256,512]{1,0:T(8,128)(2,1)} %get-tuple-element.48), channel_id=1, source_target_pairs={{0,1},{1,0},{2,3},{3,2},{4,5},{5,4},{6,7},{7,6},{8,9},{9,8},{10,11... | collective-permute-start | bytes 786440 | tf_op jit(solution)/shard_map/ppermute | solution.py:383
  23.5 15.2 %collective-permute-start.4 = (bf16[256,1024]{1,0:T(8,128)(2,1)S(1)}, bf16[256,1024]{1,0:T(8,128)(2,1)S(1)}, u32[]{:S(2)}, u32[]{:S(2)}) collective-permute-start(bf16[256,1024]{1,0:T(8,128)(2,1)S(1)} %broadcast_select_fusion), channel_id=1, source_target_pairs={{0,0},{2,16},{4,12},{6,28},{8,24},{10,8},{12,20},{14,4},{16,2},{18... | collective-permute-start | bytes 1572872 | tf_op jit(solution)/shard_map/ppermute | solution.py:452
  24.2 17.4 %copy-start.5 = (bf16[256,1024]{1,0:T(8,128)(2,1)}, bf16[256,1024]{1,0:T(8,128)(2,1)S(1)}, u32[]{:S(2)}) copy-start(bf16[256,1024]{1,0:T(8,128)(2,1)S(1)} %collective-permute-done.5.first_mine) | copy-start | bytes 1572868
  27.8 13.9 %copy-start.11 = (bf16[256,1024]{1,0:T(8,128)(2,1)}, bf16[256,1024]{1,0:T(8,128)(2,1)S(1)}, u32[]{:S(2)}) copy-start(bf16[256,1024]{1,0:T(8,128)(2,1)S(1)} %collective-permute-done.6.second_mine) | copy-start | bytes 1572868
  27.8 13.8 %collective-permute-start.7 = (bf16[256,1024]{1,0:T(8,128)(2,1)S(1)}, bf16[256,1024]{1,0:T(8,128)(2,1)S(1)}, u32[]{:S(2)}, u32[]{:S(2)}) collective-permute-start(bf16[256,1024]{1,0:T(8,128)(2,1)S(1)} %collective-permute-done.5.first_mine), channel_id=1, source_target_pairs={{0,2},{1,3},{2,0},{3,1},{4,6},{5,7},{6,4},{7,5},{8,10},{9,11},{10,... | collective-permute-start | bytes 1572872 | tf_op jit(solution)/shard_map/ppermute | solution.py:492
  28.9 12.7 %collective-permute-start.8 = (bf16[256,1024]{1,0:T(8,128)(2,1)S(1)}, bf16[256,1024]{1,0:T(8,128)(2,1)S(1)}, u32[]{:S(2)}, u32[]{:S(2)}) collective-permute-start(bf16[256,1024]{1,0:T(8,128)(2,1)S(1)} %collective-permute-done.6.second_mine), channel_id=1, source_target_pairs={{0,2},{1,3},{2,0},{3,1},{4,6},{5,7},{6,4},{7,5},{8,10},{9,11},{10,... | collective-permute-start | bytes 1572872 | tf_op jit(solution)/shard_map/ppermute | solution.py:492
  33.4 16.2 %copy-start = (bf16[2,256,512]{2,1,0:T(8,128)(2,1)}, bf16[2,256,512]{2,1,0:T(8,128)(2,1)S(1)}, u32[]{:S(2)}) copy-start(bf16[2,256,512]{2,1,0:T(8,128)(2,1)S(1)} %pad_maximum_fusion.1.refs_8_) | copy-start | bytes 1572868
  33.4 17.0 %collective-permute-start.2 = (bf16[2,256,512]{2,1,0:T(8,128)(2,1)S(1)}, bf16[2,256,512]{2,1,0:T(8,128)(2,1)S(1)}, u32[]{:S(2)}, u32[]{:S(2)}) collective-permute-start(bf16[2,256,512]{2,1,0:T(8,128)(2,1)S(1)} %pad_maximum_fusion.1.refs_8_), channel_id=1, source_target_pairs={{0,16},{16,24},{24,8},{8,0},{1,17},{17,25},{25,9},{9,1},{2,18},{18... | collective-permute-start | bytes 1572872 | tf_op jit(solution)/shard_map/ppermute | solution.py:486
  38.7 29.8 %collective-permute-start.18 = (bf16[256,1024]{1,0:T(8,128)(2,1)S(1)}, bf16[256,1024]{1,0:T(8,128)(2,1)S(1)}, u32[]{:S(2)}, u32[]{:S(2)}) collective-permute-start(bf16[256,1024]{1,0:T(8,128)(2,1)S(1)} %collective-permute-done.4.rows_in), channel_id=1, source_target_pairs={{0,1},{1,0},{2,3},{3,2},{4,5},{5,4},{6,7},{7,6},{8,9},{9,8},{10,11... | collective-permute-start | bytes 1572872 | tf_op jit(solution)/shard_map/ppermute | solution.py:383
  41.6 23.6 %copy-start.1 = (bf16[1024,256]{1,0:T(8,128)(2,1)S(1)}, bf16[1024,256]{1,0:T(8,128)(2,1)}, u32[]{:S(2)}) copy-start(bf16[1024,256]{1,0:T(8,128)(2,1)} %shard_map.146.refs_0_) | copy-start | bytes 1572868
  50.3 35.2 %copy-start.6 = (bf16[2,256,512]{2,1,0:T(8,128)(2,1)}, bf16[2,256,512]{2,1,0:T(8,128)(2,1)S(1)}, u32[]{:S(2)}) copy-start(bf16[2,256,512]{2,1,0:T(8,128)(2,1)S(1)} %collective-permute-done.2.refs_9_) | copy-start | bytes 1572868
  50.3 27.0 %collective-permute-start.9 = (bf16[2,256,512]{2,1,0:T(8,128)(2,1)S(1)}, bf16[2,256,512]{2,1,0:T(8,128)(2,1)S(1)}, u32[]{:S(2)}, u32[]{:S(2)}) collective-permute-start(bf16[2,256,512]{2,1,0:T(8,128)(2,1)S(1)} %collective-permute-done.2.refs_9_), channel_id=1, source_target_pairs={{0,16},{16,24},{24,8},{8,0},{1,17},{17,25},{25,9},{9,1},{2,18},{18... | collective-permute-start | bytes 1572872 | tf_op jit(solution)/shard_map/ppermute | solution.py:486
  63.8 15.0 %collective-permute-start.10 = (bf16[256,1024]{1,0:T(8,128)(2,1)}, bf16[256,1024]{1,0:T(8,128)(2,1)S(1)}, u32[]{:S(2)}, u32[]{:S(2)}) collective-permute-start(bf16[256,1024]{1,0:T(8,128)(2,1)} %get-tuple-element.56), channel_id=1, source_target_pairs={{0,1},{1,0},{2,3},{3,2},{4,5},{5,4},{6,7},{7,6},{8,9},{9,8},{10,11... | collective-permute-start | bytes 1572872 | tf_op jit(solution)/shard_map/ppermute | solution.py:383
  65.1 22.1 %collective-permute-start.16 = (bf16[1024,256]{1,0:T(8,128)(2,1)S(1)}, bf16[1024,256]{1,0:T(8,128)(2,1)S(1)}, u32[]{:S(2)}, u32[]{:S(2)}) collective-permute-start(bf16[1024,256]{1,0:T(8,128)(2,1)S(1)} %copy-done.1), channel_id=1, source_target_pairs={{0,4},{2,6},{4,0},{6,2},{1,5},{3,7},{5,1},{7,3},{8,12},{10,14},{12... | collective-permute-start | bytes 1572872 | tf_op jit(solution)/shard_map/ppermute | solution.py:505
  71.4 18.9 %collective-permute-start.20 = (bf16[1024,256]{1,0:T(8,128)(2,1)}, bf16[1024,256]{1,0:T(8,128)(2,1)S(1)}, u32[]{:S(2)}, u32[]{:S(2)}) collective-permute-start(bf16[1024,256]{1,0:T(8,128)(2,1)} %shard_map.149.refs_4_), channel_id=1, source_target_pairs={{0,4},{2,6},{4,0},{6,2},{1,5},{3,7},{5,1},{7,3},{8,12},{10,14},{12... | collective-permute-start | bytes 1572872 | tf_op jit(solution)/shard_map/ppermute | solution.py:505
  77.3 8.2 %copy-start.7 = (bf16[2,256,512]{2,1,0:T(8,128)(2,1)}, bf16[2,256,512]{2,1,0:T(8,128)(2,1)S(1)}, u32[]{:S(2)}) copy-start(bf16[2,256,512]{2,1,0:T(8,128)(2,1)S(1)} %collective-permute-done.9.refs_10_) | copy-start | bytes 1572868
  77.3 14.1 %collective-permute-start.12 = (bf16[2,256,512]{2,1,0:T(8,128)(2,1)S(1)}, bf16[2,256,512]{2,1,0:T(8,128)(2,1)S(1)}, u32[]{:S(2)}, u32[]{:S(2)}) collective-permute-start(bf16[2,256,512]{2,1,0:T(8,128)(2,1)S(1)} %collective-permute-done.9.refs_10_), channel_id=1, source_target_pairs={{0,16},{16,24},{24,8},{8,0},{1,17},{17,25},{25,9},{9,1},{2,18},{18... | collective-permute-start | bytes 1572872 | tf_op jit(solution)/shard_map/ppermute | solution.py:486
  85.5 5.2 %collective-permute-start.13 = (bf16[64,1024]{1,0:T(8,128)(2,1)}, bf16[64,1024]{1,0:T(8,128)(2,1)S(1)}, u32[]{:S(2)}, u32[]{:S(2)}) collective-permute-start(bf16[64,1024]{1,0:T(8,128)(2,1)} %get-tuple-element.67), channel_id=1, source_target_pairs={{0,1},{1,0},{2,3},{3,2},{4,5},{5,4},{6,7},{7,6},{8,9},{9,8},{10,11... | collective-permute-start | bytes 393224 | tf_op jit(solution)/shard_map/ppermute | solution.py:383
  87.2 6.5 %collective-permute-start.15 = (bf16[1024,256]{1,0:T(8,128)(2,1)S(1)}, bf16[1024,256]{1,0:T(8,128)(2,1)S(1)}, u32[]{:S(2)}, u32[]{:S(2)}) collective-permute-start(bf16[1024,256]{1,0:T(8,128)(2,1)S(1)} %copy-done.1), channel_id=1, source_target_pairs={{0,2},{2,0},{4,6},{6,4},{1,3},{3,1},{5,7},{7,5},{8,10},{10,8},{12,... | collective-permute-start | bytes 1572872 | tf_op jit(solution)/shard_map/ppermute | solution.py:509
  87.2 7.8 %collective-permute-start.19 = (bf16[1024,256]{1,0:T(8,128)(2,1)S(1)}, bf16[1024,256]{1,0:T(8,128)(2,1)S(1)}, u32[]{:S(2)}, u32[]{:S(2)}) collective-permute-start(bf16[1024,256]{1,0:T(8,128)(2,1)S(1)} %copy-done.2), channel_id=1, source_target_pairs={{0,2},{2,0},{4,6},{6,4},{1,3},{3,1},{5,7},{7,5},{8,10},{10,8},{12,... | collective-permute-start | bytes 1572872 | tf_op jit(solution)/shard_map/ppermute | solution.py:509
  90.3 4.7 %collective-permute-start.17 = (bf16[1024,256]{1,0:T(8,128)(2,1)S(1)}, bf16[1024,256]{1,0:T(8,128)(2,1)S(1)}, u32[]{:S(2)}, u32[]{:S(2)}) collective-permute-start(bf16[1024,256]{1,0:T(8,128)(2,1)S(1)} %collective-permute-done.16.refs_2_), channel_id=1, source_target_pairs={{0,2},{2,0},{4,6},{6,4},{1,3},{3,1},{5,7},{7,5},{8,10},{10,8},{12,... | collective-permute-start | bytes 1572872 | tf_op jit(solution)/shard_map/ppermute | solution.py:511
  90.8 4.2 %collective-permute-start.21 = (bf16[1024,256]{1,0:T(8,128)(2,1)S(1)}, bf16[1024,256]{1,0:T(8,128)(2,1)S(1)}, u32[]{:S(2)}, u32[]{:S(2)}) collective-permute-start(bf16[1024,256]{1,0:T(8,128)(2,1)S(1)} %collective-permute-done.20.refs_6_), channel_id=1, source_target_pairs={{0,2},{2,0},{4,6},{6,4},{1,3},{3,1},{5,7},{7,5},{8,10},{10,8},{12,... | collective-permute-start | bytes 1572872 | tf_op jit(solution)/shard_map/ppermute | solution.py:511
  92.6 11.5 %collective-permute-start.14 = (bf16[64,1024]{1,0:T(8,128)(2,1)S(1)}, bf16[64,1024]{1,0:T(8,128)(2,1)S(1)}, u32[]{:S(2)}, u32[]{:S(2)}) collective-permute-start(bf16[64,1024]{1,0:T(8,128)(2,1)S(1)} %add_convert_fusion.2), channel_id=1, source_target_pairs={{0,8},{8,0},{16,24},{24,16},{1,9},{9,1},{17,25},{25,17},{2,10},{10... | collective-permute-start | bytes 393224 | tf_op jit(solution)/shard_map/ppermute | solution.py:383
  93.7 13.6 %collective-permute-start.11 = (bf16[128,1024]{1,0:T(8,128)(2,1)}, bf16[128,1024]{1,0:T(8,128)(2,1)S(1)}, u32[]{:S(2)}, u32[]{:S(2)}) collective-permute-start(bf16[128,1024]{1,0:T(8,128)(2,1)} %get-tuple-element.64), channel_id=1, source_target_pairs={{8,0},{16,8},{24,16},{9,1},{17,9},{25,17},{10,2},{18,10},{26,18},{... | collective-permute-start | bytes 786440 | tf_op jit(solution)/shard_map/ppermute | solution.py:549
  104.2 9.0 %collective-permute-start.22 = (bf16[64,1024]{1,0:T(8,128)(2,1)S(1)}, bf16[64,1024]{1,0:T(8,128)(2,1)S(1)}, u32[]{:S(2)}, u32[]{:S(2)}) collective-permute-start(bf16[64,1024]{1,0:T(8,128)(2,1)S(1)} %add_convert_fusion.1), channel_id=1, source_target_pairs={{0,16},{8,24},{16,0},{24,8},{1,17},{9,25},{17,1},{25,9},{2,18},{10... | collective-permute-start | bytes 393224 | tf_op jit(solution)/shard_map/ppermute | solution.py:383
  107.3 17.6 %collective-permute-start.24 = (bf16[512,512]{1,0:T(8,128)(2,1)}, bf16[512,512]{1,0:T(8,128)(2,1)S(1)}, u32[]{:S(2)}, u32[]{:S(2)}) collective-permute-start(bf16[512,512]{1,0:T(8,128)(2,1)} %get-tuple-element.83), channel_id=1, source_target_pairs={{0,1},{1,0},{2,3},{3,2},{4,5},{5,4},{6,7},{7,6},{8,9},{9,8},{10,11... | collective-permute-start | bytes 1572872 | tf_op jit(solution)/shard_map/ppermute | solution.py:383
  113.2 10.0 %collective-permute-start.23 = (bf16[64,1024]{1,0:T(8,128)(2,1)S(1)}, bf16[64,1024]{1,0:T(8,128)(2,1)S(1)}, u32[]{:S(2)}, u32[]{:S(2)}) collective-permute-start(bf16[64,1024]{1,0:T(8,128)(2,1)S(1)} %add_convert_fusion), channel_id=1, source_target_pairs={{0,1},{1,0},{2,3},{3,2},{4,5},{5,4},{6,7},{7,6},{8,9},{9,8},{10,11... | collective-permute-start | bytes 393224 | tf_op jit(solution)/shard_map/ppermute | solution.py:383
  (16 other events, 46.8 us)

commit v15 on v14

--- a/solution.py
+++ b/solution.py
@@ -142,11 +142,12 @@
 
 
 def weight_kernel(count, place_ref, *refs):
-    cot_in, gated_in = refs[: 2 * count], refs[2 * count : 3 * count]
-    other, own, cots, gateds, others, owns, cot_sem, gated_sem, out_sem = refs[3 * count :]
+    cot_in, gated_in = refs[: 2 * count], list(refs[2 * count : 4 * count - 1])
+    other, own, cots, gateds, others, owns, cot_sem, gated_sem, out_sem = refs[4 * count - 1 :]
+    gated_in[-1:] = [gated_in[-1].at[0], gated_in[-1].at[1]]
     rows = other.shape[0]
     block = min(rows, turn)
-    copies = [pltpu.make_async_copy(gated_in[n], gateds.at[n], gated_sem.at[n]) for n in range(count)]
+    copies = [pltpu.make_async_copy(gated_in[n], gateds.at[n], gated_sem.at[n]) for n in range(2 * count)]
     copies += [pltpu.make_async_copy(cot_in[n], cots.at[n], cot_sem.at[n]) for n in range(2 * count)]
     for copy in copies:
         copy.start()
@@ -163,7 +164,7 @@
             start = pl.multiple_of(replica * rows + i * block, block)
             total = None
             for n in range(2 * count):
-                gated = gateds[place_ref[n % count], n // count]
+                gated = gateds[2 * place_ref[n % count] + n // count]
                 part = dot(cots[n, pl.ds(start, block), :], gated)
                 total = part if total is None else total + part
             target[pl.ds(pl.multiple_of(i * block, block), block), :] = total.astype(target.dtype)
@@ -331,8 +332,8 @@
 
 
 def weight_sum(places, cot_pieces, gated_pieces, rows):
-    count = len(gated_pieces)
-    _, length, width = gated_pieces[0].shape
+    count = (len(gated_pieces) + 1) // 2
+    length, width = gated_pieces[0].shape
     outs = [jax.ShapeDtypeStruct((rows, width), dtype) for dtype in (bf16, f32)]
     return local_call(
         functools.partial(weight_kernel, count),
@@ -341,10 +342,10 @@
         outs,
         [
             pltpu.VMEM((2 * count, *cot_pieces[0].shape), bf16),
-            pltpu.VMEM((count, *gated_pieces[0].shape), bf16),
+            pltpu.VMEM((2 * count, *gated_pieces[0].shape), bf16),
             *[pltpu.VMEM(o.shape, o.dtype) for o in outs],
             pltpu.SemaphoreType.DMA((2 * count,)),
-            pltpu.SemaphoreType.DMA((count,)),
+            pltpu.SemaphoreType.DMA((2 * count,)),
             pltpu.SemaphoreType.DMA((2,)),
         ],
         8 * count * length * rows * width,
@@ -480,10 +481,12 @@
         jnp.reshape(me_dp if square else 0 * me_dp, (1,)).astype(jnp.int32),
     )
     if square:
-        ring_pieces = [jnp.stack([gated[0], swap_pairs(gated[1], "dp", 1)])]
+        ring_pieces = [gated[0], swap_pairs(gated[1], "dp", 1)]
+        ring_pieces[0], ring_pieces[1], moved = lax.optimization_barrier((*ring_pieces, moved))
 
         def ring_step():
-            ring_pieces.append(lax.ppermute(ring_pieces[-1], "seq", ring))
+            for _ in range(2):
+                ring_pieces.append(lax.ppermute(ring_pieces[-2], "seq", ring))
 
         ring_step()
     gated[0], *rounds = lax.optimization_barrier((gated[0], *rounds))
@@ -498,6 +501,8 @@
         moved = transposed(moved)
         moved, place = lax.optimization_barrier((moved, place))
     other_sent, own_part = project(place, firsts, seconds, out_weight)
+    if square:
+        other_sent, moved_other = lax.optimization_barrier((other_sent, moved_other))
     other_part = swap_pairs(other_sent, "dp", 1)
     if square:
 
@@ -511,12 +516,12 @@
                 lax.ppermute(after(across, gate), "tp", near),
             ]
 
-        moved_other = transposed(after(moved_other, other_sent))
-        ring_pieces[1] = after(ring_pieces[1], other_sent)
+        ring_pieces[2], ring_pieces[3], _ = lax.optimization_barrier((*ring_pieces[2:4], other_sent))
         ring_step()
-        ring_pieces[2], own_part = lax.optimization_barrier((ring_pieces[2], own_part))
-        ring_step()
-        cot_pieces = spread(moved, ring_pieces[2]) + spread(moved_other, own_part)
+        *last, own_part, other_part = lax.optimization_barrier((*ring_pieces[4:6], own_part, other_part))
+        last = lax.ppermute(jnp.stack(last), "seq", ring)
+        moved_other = transposed(after(moved_other, ring_pieces[2]))
+        cot_pieces = spread(moved, ring_pieces[4]) + spread(moved_other, own_part)
     else:
         full = lax.all_gather(cot, "tp", axis=1, tiled=True)
         cot_all = lax.all_to_all(full, "seq", 1, 0, tiled=True)
@@ -560,7 +565,8 @@
 
     received = swap_pairs(sent_lag, "dp", 1)
     if square:
-        ring_pieces[3], received = lax.optimization_barrier((ring_pieces[3], received))
+        last, received = lax.optimization_barrier((last, received))
+        ring_pieces.append(last)
     lag_sum = own_lag + received.astype(f32)
     distance = 1
     while distance < n_seq:

time: 128 us -> 117 us (0.914)
  starting transfers between devices: 49.3 us -> 42.9 us
  local copies, waits for them, and re-layouts: 8.55 us -> 6.19 us
  waiting for transfers between devices: 26.6 us -> 24.9 us
    ppermute x3 -> x5, starting transfers between devices: 20.4 us -> 11.9 us  [the longest x4 10.7 us: ring_step(): ring_pieces.append(lax.ppermute(ring_pieces[-2], 'seq', ring))]
    unnamed x47 -> x49, local copies, waits for them, and re-layouts: 6.67 us -> 4.3 us
    ppermute x2, waiting for transfers between devices: 3.52 us -> 1.28 us  [per_device(): lax.ppermute(after(cot, prior) if turn else cot, ('tp', 'dp'), route)]
    ppermute x8, waiting for transfers between devices: 11.3 us -> 9.24 us  [swap_pairs(): return lax.ppermute(value, axis, [(i, i ^ distance) for i in range(count)])]
    ppermute x2, starting transfers between devices: 1.19 us -> 3.15 us  [per_device(): theirs = [lax.ppermute(r, ('tp', 'dp'), route) for r in rounds]]
    ppermute x2, waiting for transfers between devices: 2.51 us -> 4.32 us  [spread(): across = lax.ppermute(piece, 'tp', [(t, t ^ subs) for t in range(n_tp)])]
    ppermute x8, starting transfers between devices: 11 us -> 12.5 us  [swap_pairs(): return lax.ppermute(value, axis, [(i, i ^ distance) for i in range(count)])]
    ppermute x2, starting transfers between devices: 3.47 us -> 2.09 us  [spread(): across = lax.ppermute(piece, 'tp', [(t, t ^ subs) for t in range(n_tp)])]
  transfers between devices with their start and end apart: 25 -> 27, of which waited for: 10 -> 9; matrix products, arithmetic and copies ran while one was open for 5% -> 6% of each run, Pallas kernels for 27% -> 30%
where the time goes in v15:
time: 117 us; the launch traced here: 116 us
  starting transfers between devices  42.9 us (37%)
  Pallas kernels  34.7 us (30%)
  waiting for transfers between devices  24.9 us (21%)
  other arithmetic  6.55 us (6%)
  local copies, waits for them, and re-layouts  6.19 us (5%)
    pallas_call x3, Pallas kernels, by_channel(): pl.pallas_call(kernel, in_specs=[pl.BlockSpec(memory_space=pltpu.SMEM)] *...  16.8 us
    pallas_call x2, Pallas kernels, local_call(): pl.pallas_call(kernel, in_specs=[pl.BlockSpec(memory_space=pltpu.SMEM)] +...  13.8 us
    ppermute x8, starting transfers between devices, swap_pairs(): return lax.ppermute(value, axis, [(i, i ^ distance) for i in range(count)])  12.5 us
    ppermute x4, starting transfers between devices, ring_step(): ring_pieces.append(lax.ppermute(ring_pieces[-2], 'seq', ring))  10.7 us
    ppermute x8, waiting for transfers between devices, swap_pairs(): return lax.ppermute(value, axis, [(i, i ^ distance) for i in range(count)])  9.24 us
    ppermute x4, waiting for transfers between devices, ring_step(): ring_pieces.append(lax.ppermute(ring_pieces[-2], 'seq', ring))  7.28 us
    ppermute x1, starting transfers between devices, per_device(): prior = lax.ppermute(tail, 'seq', [(i, i + 1) for i in range(n_seq - 1)])  7.09 us
    ppermute x2, waiting for transfers between devices, spread(): across = lax.ppermute(piece, 'tp', [(t, t ^ subs) for t in range(n_tp)])  4.32 us
  transfers between devices with their start and end apart: 27, of which 9 were waited for; matrix products, arithmetic and copies ran while one was open for 6% of the time, Pallas kernels for 30%

profile of v15, /device:TPU:0, one launch (start us, length us, event | category | flops | bytes accessed | tf_op | source)
XLA Modules:
  0.0 116.2 jit_solution(11280314804003515040)
XLA Ops:
  2.4 7.1 %collective-permute-start = (bf16[128,1024]{1,0:T(8,128)(2,1)S(1)}, bf16[128,1024]{1,0:T(8,128)(2,1)S(1)}, u32[]{:S(2)}, u32[]{:S(2)}) collective-permute-start(bf16[128,1024]{1,0:T(8,128)(2,1)S(1)} %fusion.2), channel_id=1, source_target_pairs={{0,8},{8,16},{16,24},{1,9},{9,17},{17,25},{2,10},{10,18},{18,26},{... | collective-permute-start | bytes 786440 | tf_op jit(solution)/shard_map/ppermute | solution.py:419
  9.5 1.7 %collective-permute-start.6 = (bf16[256,1024]{1,0:T(8,128)(2,1)}, bf16[256,1024]{1,0:T(8,128)(2,1)S(1)}, u32[]{:S(2)}, u32[]{:S(2)}) collective-permute-start(bf16[256,1024]{1,0:T(8,128)(2,1)} %bitcast.32), channel_id=1, source_target_pairs={{0,0},{1,4},{2,2},{3,6},{4,1},{5,5},{6,3},{7,7},{8,8},{9,12},{10,1... | collective-permute-start | bytes 1572872 | tf_op jit(solution)/shard_map/ppermute | solution.py:428
  11.2 2.8 %collective-permute-done.refs_3_.refs_6_ = bf16[128,1024]{1,0:T(8,128)(2,1)S(1)} collective-permute-done((bf16[128,1024]{1,0:T(8,128)(2,1)S(1)}, bf16[128,1024]{1,0:T(8,128)(2,1)S(1)}, u32[]{:S(2)}, u32[]{:S(2)}) %collective-permute-start) | collective-permute-done | bytes 262176 | tf_op jit(solution)/shard_map/ppermute | solution.py:419
  19.0 5.5 %shard_map.145 = (f32[256,1024]{1,0:T(8,128)}, bf16[256,512]{1,0:T(8,128)(2,1)}, bf16[256,512]{1,0:T(8,128)(2,1)}) custom-call(s32[1]{0:T(128)} %bitcast.refs_0_, bf16[768,384]{1,0:T(8,128)(2,1)} %constant.66.clone.refs_1_.refs_0_, bf16[768,384]{1,0:T(8,128)(2,1)} %constant.67.clone.refs_2_.refs_1_, bf16[128,1024]{1,0:T(8,128)(2,1)} %copy-done.5, ...), custom_call_target="tpu_custom_call" | custom-call | flops 22020096 | bytes 57408 | tf_op jit(solution)/shard_map/pallas_call | solution.py:281
  24.5 1.5 %collective-permute-start.1 = (bf16[256,512]{1,0:T(8,128)(2,1)}, bf16[256,512]{1,0:T(8,128)(2,1)S(1)}, u32[]{:S(2)}, u32[]{:S(2)}) collective-permute-start(bf16[256,512]{1,0:T(8,128)(2,1)} %get-tuple-element.56), channel_id=1, source_target_pairs={{0,1},{1,0},{2,3},{3,2},{4,5},{5,4},{6,7},{7,6},{8,9},{9,8},{10,11... | collective-permute-start | bytes 786440 | tf_op jit(solution)/shard_map/ppermute | solution.py:384
  26.0 1.3 %collective-permute-done.7.second_mine = bf16[256,1024]{1,0:T(8,128)(2,1)S(1)} collective-permute-done((bf16[256,1024]{1,0:T(8,128)(2,1)}, bf16[256,1024]{1,0:T(8,128)(2,1)S(1)}, u32[]{:S(2)}, u32[]{:S(2)}) %collective-permute-start.7) | collective-permute-done | bytes 524320 | tf_op jit(solution)/shard_map/ppermute | solution.py:428
  27.3 3.1 %collective-permute-start.8 = (bf16[256,1024]{1,0:T(8,128)(2,1)S(1)}, bf16[256,1024]{1,0:T(8,128)(2,1)S(1)}, u32[]{:S(2)}, u32[]{:S(2)}) collective-permute-start(bf16[256,1024]{1,0:T(8,128)(2,1)S(1)} %collective-permute-done.6.first_mine), channel_id=1, source_target_pairs={{0,2},{1,3},{2,0},{3,1},{4,6},{5,7},{6,4},{7,5},{8,10},{9,11},{10,... | collective-permute-start | bytes 1572872 | tf_op jit(solution)/shard_map/ppermute | solution.py:495
  31.2 1.4 %collective-permute-start.10 = (bf16[256,1024]{1,0:T(8,128)(2,1)S(1)}, bf16[256,1024]{1,0:T(8,128)(2,1)S(1)}, u32[]{:S(2)}, u32[]{:S(2)}) collective-permute-start(bf16[256,1024]{1,0:T(8,128)(2,1)S(1)} %collective-permute-done.3.rows_in), channel_id=1, source_target_pairs={{0,1},{1,0},{2,3},{3,2},{4,5},{5,4},{6,7},{7,6},{8,9},{9,8},{10,11... | collective-permute-start | bytes 1572872 | tf_op jit(solution)/shard_map/ppermute | solution.py:384
  32.6 2.0 %shard_map.146.refs_0_ = bf16[1024,256]{1,0:T(8,128)(2,1)} custom-call(bf16[256,1024]{1,0:T(8,128)(2,1)} %copy-done.18), custom_call_target="tpu_custom_call" | custom-call | bytes 16384 | tf_op jit(solution)/shard_map/pallas_call | solution.py:367
  34.7 5.8 %collective-permute-start.4 = (bf16[256,512]{1,0:T(8,128)(2,1)}, bf16[256,512]{1,0:T(8,128)(2,1)S(1)}, u32[]{:S(2)}, u32[]{:S(2)}) collective-permute-start(bf16[256,512]{1,0:T(8,128)(2,1)} %get-tuple-element.58.refs_8_), channel_id=1, source_target_pairs={{0,16},{16,24},{24,8},{8,0},{1,17},{17,25},{25,9},{9,1},{2,18},{18... | collective-permute-start | bytes 786440 | tf_op jit(solution)/shard_map/ppermute | solution.py:489
  40.5 2.2 %collective-permute-start.5 = (bf16[256,512]{1,0:T(8,128)(2,1)S(1)}, bf16[256,512]{1,0:T(8,128)(2,1)S(1)}, u32[]{:S(2)}, u32[]{:S(2)}) collective-permute-start(bf16[256,512]{1,0:T(8,128)(2,1)S(1)} %collective-permute-done.1.refs_9_), channel_id=1, source_target_pairs={{0,16},{16,24},{24,8},{8,0},{1,17},{17,25},{25,9},{9,1},{2,18},{18... | collective-permute-start | bytes 786440 | tf_op jit(solution)/shard_map/ppermute | solution.py:489
  44.3 6.4 %shard_map.147 = (bf16[256,1024]{1,0:T(8,128)(2,1)}, f32[256,1024]{1,0:T(8,128)}) custom-call(s32[3]{0:T(128)} %pad_add_fusion.place_ref, bf16[256,1024]{1,0:T(8,128)(2,1)} %copy-done.6, bf16[256,1024]{1,0:T(8,128)(2,1)} %copy-done.7, bf16[256,1024]{1,0:T(8,128)(2,1)} %copy-done.16, bf16[256,1024]{1,0:T(8,128)(2,1)} %copy-done.17, bf16[1024,2048]{1,0:T(8,128)(2,1)} %weight.1), custom_call_target="tpu_custom_call" | custom-call | flops 33554432 | bytes 122880 | tf_op jit(solution)/shard_map/pallas_call | solution.py:301
  50.7 1.9 %collective-permute-start.13 = (bf16[256,1024]{1,0:T(8,128)(2,1)}, bf16[256,1024]{1,0:T(8,128)(2,1)S(1)}, u32[]{:S(2)}, u32[]{:S(2)}) collective-permute-start(bf16[256,1024]{1,0:T(8,128)(2,1)} %get-tuple-element.68), channel_id=1, source_target_pairs={{0,1},{1,0},{2,3},{3,2},{4,5},{5,4},{6,7},{7,6},{8,9},{9,8},{10,11... | collective-permute-start | bytes 1572872 | tf_op jit(solution)/shard_map/ppermute | solution.py:384
  53.3 1.2 %collective-permute-start.11 = (bf16[256,512]{1,0:T(8,128)(2,1)S(1)}, bf16[256,512]{1,0:T(8,128)(2,1)S(1)}, u32[]{:S(2)}, u32[]{:S(2)}) collective-permute-start(bf16[256,512]{1,0:T(8,128)(2,1)S(1)} %collective-permute-done.4.refs_10_), channel_id=1, source_target_pairs={{0,16},{16,24},{24,8},{8,0},{1,17},{17,25},{25,9},{9,1},{2,18},{18... | collective-permute-start | bytes 786440 | tf_op jit(solution)/shard_map/ppermute | solution.py:489
  54.5 1.5 %collective-permute-start.12 = (bf16[256,512]{1,0:T(8,128)(2,1)S(1)}, bf16[256,512]{1,0:T(8,128)(2,1)S(1)}, u32[]{:S(2)}, u32[]{:S(2)}) collective-permute-start(bf16[256,512]{1,0:T(8,128)(2,1)S(1)} %collective-permute-done.5.refs_11_), channel_id=1, source_target_pairs={{0,16},{16,24},{24,8},{8,0},{1,17},{17,25},{25,9},{9,1},{2,18},{18... | collective-permute-start | bytes 786440 | tf_op jit(solution)/shard_map/ppermute | solution.py:489
  56.0 1.6 %collective-permute-start.19 = (bf16[1024,256]{1,0:T(8,128)(2,1)S(1)}, bf16[1024,256]{1,0:T(8,128)(2,1)S(1)}, u32[]{:S(2)}, u32[]{:S(2)}) collective-permute-start(bf16[1024,256]{1,0:T(8,128)(2,1)S(1)} %copy-done), channel_id=1, source_target_pairs={{0,4},{2,6},{4,0},{6,2},{1,5},{3,7},{5,1},{7,3},{8,12},{10,14},{12... | collective-permute-start | bytes 1572872 | tf_op jit(solution)/shard_map/ppermute | solution.py:510
  57.6 2.0 %shard_map.149.refs_4_ = bf16[1024,256]{1,0:T(8,128)(2,1)} custom-call(bf16[256,1024]{1,0:T(8,128)(2,1)} %copy-done.19), custom_call_target="tpu_custom_call" | custom-call | bytes 16384 | tf_op jit(solution)/shard_map/pallas_call | solution.py:367
  60.1 2.4 %collective-permute-done.11.refs_12_ = bf16[256,512]{1,0:T(8,128)(2,1)S(1)} collective-permute-done((bf16[256,512]{1,0:T(8,128)(2,1)S(1)}, bf16[256,512]{1,0:T(8,128)(2,1)S(1)}, u32[]{:S(2)}, u32[]{:S(2)}) %collective-permute-start.11) | collective-permute-done | bytes 262176 | tf_op jit(solution)/shard_map/ppermute | solution.py:489
  62.5 4.2 %collective-permute-done.12.refs_13_ = bf16[256,512]{1,0:T(8,128)(2,1)S(1)} collective-permute-done((bf16[256,512]{1,0:T(8,128)(2,1)S(1)}, bf16[256,512]{1,0:T(8,128)(2,1)S(1)}, u32[]{:S(2)}, u32[]{:S(2)}) %collective-permute-start.12) | collective-permute-done | bytes 262176 | tf_op jit(solution)/shard_map/ppermute | solution.py:489
  66.8 1.2 %collective-permute-start.15 = (bf16[2,256,512]{2,1,0:T(8,128)(2,1)S(1)}, bf16[2,256,512]{2,1,0:T(8,128)(2,1)S(1)}, u32[]{:S(2)}, u32[]{:S(2)}) collective-permute-start(bf16[2,256,512]{2,1,0:T(8,128)(2,1)S(1)} %pad_maximum_fusion.1), channel_id=1, source_target_pairs={{0,16},{16,24},{24,8},{8,0},{1,17},{17,25},{25,9},{9,1},{2,18},{18... | collective-permute-start | bytes 1572872 | tf_op jit(solution)/shard_map/ppermute | solution.py:522
  68.0 5.9 %shard_map.148 = (bf16[256,1024]{1,0:T(8,128)(2,1)}, bf16[256,1024]{1,0:T(8,128)(2,1)}, bf16[128,1024]{1,0:T(8,128)(2,1)}, bf16[64,1024]{1,0:T(8,128)(2,1)}, f32[64,1024]{1,0:T(8,128)}) custom-call(bf16[768,384]{1,0:T(8,128)(2,1)} %constant.66.clone.refs_1_.refs_0_, bf16[768,384]{1,0:T(8,128)(2,1)} %constant.67.clone.refs_2_.refs_1_, ...), custom_call_target="tpu_custom_call" | custom-call | flops 20447232 | bytes 96320 | tf_op jit(solution)/shard_map/pallas_call | solution.py:281
  73.9 1.2 %collective-permute-start.16 = (bf16[64,1024]{1,0:T(8,128)(2,1)}, bf16[64,1024]{1,0:T(8,128)(2,1)S(1)}, u32[]{:S(2)}, u32[]{:S(2)}) collective-permute-start(bf16[64,1024]{1,0:T(8,128)(2,1)} %get-tuple-element.82), channel_id=1, source_target_pairs={{0,1},{1,0},{2,3},{3,2},{4,5},{5,4},{6,7},{7,6},{8,9},{9,8},{10,11... | collective-permute-start | bytes 393224 | tf_op jit(solution)/shard_map/ppermute | solution.py:384
  75.7 4.3 %collective-permute-done.22.refs_6_ = bf16[1024,256]{1,0:T(8,128)(2,1)S(1)} collective-permute-done((bf16[1024,256]{1,0:T(8,128)(2,1)}, bf16[1024,256]{1,0:T(8,128)(2,1)S(1)}, u32[]{:S(2)}, u32[]{:S(2)}) %collective-permute-start.22) | collective-permute-done | bytes 524320 | tf_op jit(solution)/shard_map/ppermute | solution.py:510
  81.7 1.8 %collective-permute-start.17 = (bf16[64,1024]{1,0:T(8,128)(2,1)S(1)}, bf16[64,1024]{1,0:T(8,128)(2,1)S(1)}, u32[]{:S(2)}, u32[]{:S(2)}) collective-permute-start(bf16[64,1024]{1,0:T(8,128)(2,1)S(1)} %add_convert_fusion.2), channel_id=1, source_target_pairs={{0,8},{8,0},{16,24},{24,16},{1,9},{9,1},{17,25},{25,17},{2,10},{10... | collective-permute-start | bytes 393224 | tf_op jit(solution)/shard_map/ppermute | solution.py:384
  83.5 1.3 %collective-permute-start.14 = (bf16[128,1024]{1,0:T(8,128)(2,1)}, bf16[128,1024]{1,0:T(8,128)(2,1)S(1)}, u32[]{:S(2)}, u32[]{:S(2)}) collective-permute-start(bf16[128,1024]{1,0:T(8,128)(2,1)} %get-tuple-element.78), channel_id=1, source_target_pairs={{8,0},{16,8},{24,16},{9,1},{17,9},{25,17},{10,2},{18,10},{26,18},{... | collective-permute-start | bytes 786440 | tf_op jit(solution)/shard_map/ppermute | solution.py:554
  86.6 7.4 %shard_map.150 = (bf16[512,512]{1,0:T(8,128)(2,1)}, f32[512,512]{1,0:T(8,128)}) custom-call(s32[5]{0:T(128)} %pad_add_fusion.1.place_ref, bf16[1024,256]{1,0:T(8,128)(2,1)} %shard_map.146.refs_0_, bf16[1024,256]{1,0:T(8,128)(2,1)} %copy-done.11, bf16[1024,256]{1,0:T(8,128)(2,1)} %copy-done.8, bf16[1024,256]{1,0:T(8,128)(2,1)} %copy-done.13, ...), custom_call_target="tpu_custom_call" | custom-call | flops 33554432 | bytes 122880 | tf_op jit(solution)/shard_map/pallas_call | solution.py:301
  94.0 2.5 %collective-permute-start.24 = (bf16[64,1024]{1,0:T(8,128)(2,1)S(1)}, bf16[64,1024]{1,0:T(8,128)(2,1)S(1)}, u32[]{:S(2)}, u32[]{:S(2)}) collective-permute-start(bf16[64,1024]{1,0:T(8,128)(2,1)S(1)} %add_convert_fusion.1), channel_id=1, source_target_pairs={{0,16},{8,24},{16,0},{24,8},{1,17},{9,25},{17,1},{25,9},{2,18},{10... | collective-permute-start | bytes 393224 | tf_op jit(solution)/shard_map/ppermute | solution.py:384
  96.5 1.2 %collective-permute-start.26 = (bf16[512,512]{1,0:T(8,128)(2,1)}, bf16[512,512]{1,0:T(8,128)(2,1)S(1)}, u32[]{:S(2)}, u32[]{:S(2)}) collective-permute-start(bf16[512,512]{1,0:T(8,128)(2,1)} %get-tuple-element.99), channel_id=1, source_target_pairs={{0,1},{1,0},{2,3},{3,2},{4,5},{5,4},{6,7},{7,6},{8,9},{9,8},{10,11... | collective-permute-start | bytes 1572872 | tf_op jit(solution)/shard_map/ppermute | solution.py:384
  97.7 5.3 %collective-permute-done.24 = bf16[64,1024]{1,0:T(8,128)(2,1)S(1)} collective-permute-done((bf16[64,1024]{1,0:T(8,128)(2,1)S(1)}, bf16[64,1024]{1,0:T(8,128)(2,1)S(1)}, u32[]{:S(2)}, u32[]{:S(2)}) %collective-permute-start.24) | collective-permute-done | bytes 131104 | tf_op jit(solution)/shard_map/ppermute | solution.py:384
  104.1 5.5 %shard_map.151 = (bf16[256,1024]{1,0:T(8,128)(2,1)}, bf16[256,1024]{1,0:T(8,128)(2,1)}) custom-call(bf16[768,384]{1,0:T(8,128)(2,1)} %constant.66.clone.refs_1_.refs_0_, bf16[768,384]{1,0:T(8,128)(2,1)} %constant.67.clone.refs_2_.refs_1_, bf16[256,1024]{1,0:T(8,128)(2,1)} %get-tuple-element.77.refs_2_, bf16[128,1024]{1,0:T(8,128)(2,1)} %copy-done.23, ...), custom_call_target="tpu_custom_call" | custom-call | flops 5637144576 | bytes 49216 | tf_op jit(solution)/shard_map/pallas_call | solution.py:281
  109.6 3.2 %collective-permute-done.25 = bf16[64,1024]{1,0:T(8,128)(2,1)S(1)} collective-permute-done((bf16[64,1024]{1,0:T(8,128)(2,1)S(1)}, bf16[64,1024]{1,0:T(8,128)(2,1)S(1)}, u32[]{:S(2)}, u32[]{:S(2)}) %collective-permute-start.25) | collective-permute-done | bytes 131104 | tf_op jit(solution)/shard_map/ppermute | solution.py:384
  114.7 1.5 %pad_maximum_fusion = f32[512,1024]{1,0:T(8,128)} fusion(f32[512,512]{1,0:T(8,128)S(1)} %get-tuple-element.107, f32[512,512]{1,0:T(8,128)S(1)} %get-tuple-element.106), kind=kLoop, calls=%fused_computation | loop fusion | flops 524288 | bytes 4194304 | tf_op jit(solution)/shard_map/concatenate | solution.py:591
  (93 shorter events, 17.5 us)
Async XLA Ops:
  1.7 12.9 %collective-permute-start.2 = (bf16[256,1024]{1,0:T(8,128)(2,1)}, bf16[256,1024]{1,0:T(8,128)(2,1)S(1)}, u32[]{:S(2)}, u32[]{:S(2)}) collective-permute-start(bf16[256,1024]{1,0:T(8,128)(2,1)} %bitcast.31), channel_id=1, source_target_pairs={{2,4},{4,2},{8,14},{14,8},{18,20},{20,18},{24,30},{30,24},{3,5},{5... | collective-permute-start | bytes 1572872 | tf_op jit(solution)/shard_map/ppermute | solution.py:441
  2.4 11.6 %collective-permute-start = (bf16[128,1024]{1,0:T(8,128)(2,1)S(1)}, bf16[128,1024]{1,0:T(8,128)(2,1)S(1)}, u32[]{:S(2)}, u32[]{:S(2)}) collective-permute-start(bf16[128,1024]{1,0:T(8,128)(2,1)S(1)} %fusion.2), channel_id=1, source_target_pairs={{0,8},{8,16},{16,24},{1,9},{9,17},{17,25},{2,10},{10,18},{18,26},{... | collective-permute-start | bytes 786440 | tf_op jit(solution)/shard_map/ppermute | solution.py:419
  9.5 16.5 %collective-permute-start.6 = (bf16[256,1024]{1,0:T(8,128)(2,1)}, bf16[256,1024]{1,0:T(8,128)(2,1)S(1)}, u32[]{:S(2)}, u32[]{:S(2)}) collective-permute-start(bf16[256,1024]{1,0:T(8,128)(2,1)} %bitcast.32), channel_id=1, source_target_pairs={{0,0},{1,4},{2,2},{3,6},{4,1},{5,5},{6,3},{7,7},{8,8},{9,12},{10,1... | collective-permute-start | bytes 1572872 | tf_op jit(solution)/shard_map/ppermute | solution.py:428
  14.0 13.3 %collective-permute-start.7 = (bf16[256,1024]{1,0:T(8,128)(2,1)}, bf16[256,1024]{1,0:T(8,128)(2,1)S(1)}, u32[]{:S(2)}, u32[]{:S(2)}) collective-permute-start(bf16[256,1024]{1,0:T(8,128)(2,1)} %bitcast.33), channel_id=1, source_target_pairs={{0,4},{1,0},{2,6},{3,2},{4,5},{5,1},{6,7},{7,3},{8,12},{9,8},{10,1... | collective-permute-start | bytes 1572872 | tf_op jit(solution)/shard_map/ppermute | solution.py:428
  15.8 15.4 %collective-permute-start.3 = (bf16[256,1024]{1,0:T(8,128)(2,1)S(1)}, bf16[256,1024]{1,0:T(8,128)(2,1)S(1)}, u32[]{:S(2)}, u32[]{:S(2)}) collective-permute-start(bf16[256,1024]{1,0:T(8,128)(2,1)S(1)} %broadcast_select_fusion), channel_id=1, source_target_pairs={{0,0},{2,16},{4,12},{6,28},{8,24},{10,8},{12,20},{14,4},{16,2},{18... | collective-permute-start | bytes 1572872 | tf_op jit(solution)/shard_map/ppermute | solution.py:453
  24.5 6.6 %collective-permute-start.1 = (bf16[256,512]{1,0:T(8,128)(2,1)}, bf16[256,512]{1,0:T(8,128)(2,1)S(1)}, u32[]{:S(2)}, u32[]{:S(2)}) collective-permute-start(bf16[256,512]{1,0:T(8,128)(2,1)} %get-tuple-element.56), channel_id=1, source_target_pairs={{0,1},{1,0},{2,3},{3,2},{4,5},{5,4},{6,7},{7,6},{8,9},{9,8},{10,11... | collective-permute-start | bytes 786440 | tf_op jit(solution)/shard_map/ppermute | solution.py:384
  26.0 16.7 %copy-start.6 = (bf16[256,1024]{1,0:T(8,128)(2,1)}, bf16[256,1024]{1,0:T(8,128)(2,1)S(1)}, u32[]{:S(2)}) copy-start(bf16[256,1024]{1,0:T(8,128)(2,1)S(1)} %collective-permute-done.6.first_mine) | copy-start | bytes 1572868
  27.3 15.4 %collective-permute-start.8 = (bf16[256,1024]{1,0:T(8,128)(2,1)S(1)}, bf16[256,1024]{1,0:T(8,128)(2,1)S(1)}, u32[]{:S(2)}, u32[]{:S(2)}) collective-permute-start(bf16[256,1024]{1,0:T(8,128)(2,1)S(1)} %collective-permute-done.6.first_mine), channel_id=1, source_target_pairs={{0,2},{1,3},{2,0},{3,1},{4,6},{5,7},{6,4},{7,5},{8,10},{9,11},{10,... | collective-permute-start | bytes 1572872 | tf_op jit(solution)/shard_map/ppermute | solution.py:495
  30.3 12.4 %collective-permute-start.9 = (bf16[256,1024]{1,0:T(8,128)(2,1)S(1)}, bf16[256,1024]{1,0:T(8,128)(2,1)S(1)}, u32[]{:S(2)}, u32[]{:S(2)}) collective-permute-start(bf16[256,1024]{1,0:T(8,128)(2,1)S(1)} %collective-permute-done.7.second_mine), channel_id=1, source_target_pairs={{0,2},{1,3},{2,0},{3,1},{4,6},{5,7},{6,4},{7,5},{8,10},{9,11},{10,... | collective-permute-start | bytes 1572872 | tf_op jit(solution)/shard_map/ppermute | solution.py:495
  31.2 42.7 %copy-start.20 = (bf16[256,512]{1,0:T(8,128)(2,1)}, bf16[256,512]{1,0:T(8,128)(2,1)S(1)}, u32[]{:S(2)}) copy-start(bf16[256,512]{1,0:T(8,128)(2,1)S(1)} %collective-permute-done.1.refs_9_) | copy-start | bytes 786436
  31.2 19.5 %collective-permute-start.10 = (bf16[256,1024]{1,0:T(8,128)(2,1)S(1)}, bf16[256,1024]{1,0:T(8,128)(2,1)S(1)}, u32[]{:S(2)}, u32[]{:S(2)}) collective-permute-start(bf16[256,1024]{1,0:T(8,128)(2,1)S(1)} %collective-permute-done.3.rows_in), channel_id=1, source_target_pairs={{0,1},{1,0},{2,3},{3,2},{4,5},{5,4},{6,7},{7,6},{8,9},{9,8},{10,11... | collective-permute-start | bytes 1572872 | tf_op jit(solution)/shard_map/ppermute | solution.py:384
  34.7 21.3 %copy-start = (bf16[1024,256]{1,0:T(8,128)(2,1)S(1)}, bf16[1024,256]{1,0:T(8,128)(2,1)}, u32[]{:S(2)}) copy-start(bf16[1024,256]{1,0:T(8,128)(2,1)} %shard_map.146.refs_0_) | copy-start | bytes 1572868
  34.7 17.9 %collective-permute-start.4 = (bf16[256,512]{1,0:T(8,128)(2,1)}, bf16[256,512]{1,0:T(8,128)(2,1)S(1)}, u32[]{:S(2)}, u32[]{:S(2)}) collective-permute-start(bf16[256,512]{1,0:T(8,128)(2,1)} %get-tuple-element.58.refs_8_), channel_id=1, source_target_pairs={{0,16},{16,24},{24,8},{8,0},{1,17},{17,25},{25,9},{9,1},{2,18},{18... | collective-permute-start | bytes 786440 | tf_op jit(solution)/shard_map/ppermute | solution.py:489
  40.5 12.7 %collective-permute-start.5 = (bf16[256,512]{1,0:T(8,128)(2,1)S(1)}, bf16[256,512]{1,0:T(8,128)(2,1)S(1)}, u32[]{:S(2)}, u32[]{:S(2)}) collective-permute-start(bf16[256,512]{1,0:T(8,128)(2,1)S(1)} %collective-permute-done.1.refs_9_), channel_id=1, source_target_pairs={{0,16},{16,24},{24,8},{8,0},{1,17},{17,25},{25,9},{9,1},{2,18},{18... | collective-permute-start | bytes 786440 | tf_op jit(solution)/shard_map/ppermute | solution.py:489
  50.7 16.0 %collective-permute-start.13 = (bf16[256,1024]{1,0:T(8,128)(2,1)}, bf16[256,1024]{1,0:T(8,128)(2,1)S(1)}, u32[]{:S(2)}, u32[]{:S(2)}) collective-permute-start(bf16[256,1024]{1,0:T(8,128)(2,1)} %get-tuple-element.68), channel_id=1, source_target_pairs={{0,1},{1,0},{2,3},{3,2},{4,5},{5,4},{6,7},{7,6},{8,9},{9,8},{10,11... | collective-permute-start | bytes 1572872 | tf_op jit(solution)/shard_map/ppermute | solution.py:384
  52.6 21.3 %copy-start.21 = (bf16[256,512]{1,0:T(8,128)(2,1)}, bf16[256,512]{1,0:T(8,128)(2,1)S(1)}, u32[]{:S(2)}) copy-start(bf16[256,512]{1,0:T(8,128)(2,1)S(1)} %collective-permute-done.4.refs_10_) | copy-start | bytes 786436
  53.3 20.6 %copy-start.22 = (bf16[256,512]{1,0:T(8,128)(2,1)}, bf16[256,512]{1,0:T(8,128)(2,1)S(1)}, u32[]{:S(2)}) copy-start(bf16[256,512]{1,0:T(8,128)(2,1)S(1)} %collective-permute-done.5.refs_11_) | copy-start | bytes 786436
  53.3 9.2 %collective-permute-start.11 = (bf16[256,512]{1,0:T(8,128)(2,1)S(1)}, bf16[256,512]{1,0:T(8,128)(2,1)S(1)}, u32[]{:S(2)}, u32[]{:S(2)}) collective-permute-start(bf16[256,512]{1,0:T(8,128)(2,1)S(1)} %collective-permute-done.4.refs_10_), channel_id=1, source_target_pairs={{0,16},{16,24},{24,8},{8,0},{1,17},{17,25},{25,9},{9,1},{2,18},{18... | collective-permute-start | bytes 786440 | tf_op jit(solution)/shard_map/ppermute | solution.py:489
  54.5 12.2 %collective-permute-start.12 = (bf16[256,512]{1,0:T(8,128)(2,1)S(1)}, bf16[256,512]{1,0:T(8,128)(2,1)S(1)}, u32[]{:S(2)}, u32[]{:S(2)}) collective-permute-start(bf16[256,512]{1,0:T(8,128)(2,1)S(1)} %collective-permute-done.5.refs_11_), channel_id=1, source_target_pairs={{0,16},{16,24},{24,8},{8,0},{1,17},{17,25},{25,9},{9,1},{2,18},{18... | collective-permute-start | bytes 786440 | tf_op jit(solution)/shard_map/ppermute | solution.py:489
  56.0 19.2 %collective-permute-start.19 = (bf16[1024,256]{1,0:T(8,128)(2,1)S(1)}, bf16[1024,256]{1,0:T(8,128)(2,1)S(1)}, u32[]{:S(2)}, u32[]{:S(2)}) collective-permute-start(bf16[1024,256]{1,0:T(8,128)(2,1)S(1)} %copy-done), channel_id=1, source_target_pairs={{0,4},{2,6},{4,0},{6,2},{1,5},{3,7},{5,1},{7,3},{8,12},{10,14},{12... | collective-permute-start | bytes 1572872 | tf_op jit(solution)/shard_map/ppermute | solution.py:510
  59.6 20.4 %collective-permute-start.22 = (bf16[1024,256]{1,0:T(8,128)(2,1)}, bf16[1024,256]{1,0:T(8,128)(2,1)S(1)}, u32[]{:S(2)}, u32[]{:S(2)}) collective-permute-start(bf16[1024,256]{1,0:T(8,128)(2,1)} %shard_map.149.refs_4_), channel_id=1, source_target_pairs={{0,4},{2,6},{4,0},{6,2},{1,5},{3,7},{5,1},{7,3},{8,12},{10,14},{12... | collective-permute-start | bytes 1572872 | tf_op jit(solution)/shard_map/ppermute | solution.py:510
  66.8 13.8 %collective-permute-start.15 = (bf16[2,256,512]{2,1,0:T(8,128)(2,1)S(1)}, bf16[2,256,512]{2,1,0:T(8,128)(2,1)S(1)}, u32[]{:S(2)}, u32[]{:S(2)}) collective-permute-start(bf16[2,256,512]{2,1,0:T(8,128)(2,1)S(1)} %pad_maximum_fusion.1), channel_id=1, source_target_pairs={{0,16},{16,24},{24,8},{8,0},{1,17},{17,25},{25,9},{9,1},{2,18},{18... | collective-permute-start | bytes 1572872 | tf_op jit(solution)/shard_map/ppermute | solution.py:522
  73.9 6.1 %collective-permute-start.16 = (bf16[64,1024]{1,0:T(8,128)(2,1)}, bf16[64,1024]{1,0:T(8,128)(2,1)S(1)}, u32[]{:S(2)}, u32[]{:S(2)}) collective-permute-start(bf16[64,1024]{1,0:T(8,128)(2,1)} %get-tuple-element.82), channel_id=1, source_target_pairs={{0,1},{1,0},{2,3},{3,2},{4,5},{5,4},{6,7},{7,6},{8,9},{9,8},{10,11... | collective-permute-start | bytes 393224 | tf_op jit(solution)/shard_map/ppermute | solution.py:384
  75.2 8.3 %collective-permute-start.18 = (bf16[1024,256]{1,0:T(8,128)(2,1)S(1)}, bf16[1024,256]{1,0:T(8,128)(2,1)S(1)}, u32[]{:S(2)}, u32[]{:S(2)}) collective-permute-start(bf16[1024,256]{1,0:T(8,128)(2,1)S(1)} %copy-done), channel_id=1, source_target_pairs={{0,2},{2,0},{4,6},{6,4},{1,3},{3,1},{5,7},{7,5},{8,10},{10,8},{12,... | collective-permute-start | bytes 1572872 | tf_op jit(solution)/shard_map/ppermute | solution.py:514
  75.2 9.6 %collective-permute-start.21 = (bf16[1024,256]{1,0:T(8,128)(2,1)S(1)}, bf16[1024,256]{1,0:T(8,128)(2,1)S(1)}, u32[]{:S(2)}, u32[]{:S(2)}) collective-permute-start(bf16[1024,256]{1,0:T(8,128)(2,1)S(1)} %copy-done.1), channel_id=1, source_target_pairs={{0,2},{2,0},{4,6},{6,4},{1,3},{3,1},{5,7},{7,5},{8,10},{10,8},{12,... | collective-permute-start | bytes 1572872 | tf_op jit(solution)/shard_map/ppermute | solution.py:514
  80.1 4.8 %collective-permute-start.20 = (bf16[1024,256]{1,0:T(8,128)(2,1)S(1)}, bf16[1024,256]{1,0:T(8,128)(2,1)S(1)}, u32[]{:S(2)}, u32[]{:S(2)}) collective-permute-start(bf16[1024,256]{1,0:T(8,128)(2,1)S(1)} %collective-permute-done.19.refs_2_), channel_id=1, source_target_pairs={{0,2},{2,0},{4,6},{6,4},{1,3},{3,1},{5,7},{7,5},{8,10},{10,8},{12,... | collective-permute-start | bytes 1572872 | tf_op jit(solution)/shard_map/ppermute | solution.py:516
  80.1 4.8 %collective-permute-start.23 = (bf16[1024,256]{1,0:T(8,128)(2,1)S(1)}, bf16[1024,256]{1,0:T(8,128)(2,1)S(1)}, u32[]{:S(2)}, u32[]{:S(2)}) collective-permute-start(bf16[1024,256]{1,0:T(8,128)(2,1)S(1)} %collective-permute-done.22.refs_6_), channel_id=1, source_target_pairs={{0,2},{2,0},{4,6},{6,4},{1,3},{3,1},{5,7},{7,5},{8,10},{10,8},{12,... | collective-permute-start | bytes 1572872 | tf_op jit(solution)/shard_map/ppermute | solution.py:516
  81.7 12.2 %collective-permute-start.17 = (bf16[64,1024]{1,0:T(8,128)(2,1)S(1)}, bf16[64,1024]{1,0:T(8,128)(2,1)S(1)}, u32[]{:S(2)}, u32[]{:S(2)}) collective-permute-start(bf16[64,1024]{1,0:T(8,128)(2,1)S(1)} %add_convert_fusion.2), channel_id=1, source_target_pairs={{0,8},{8,0},{16,24},{24,16},{1,9},{9,1},{17,25},{25,17},{2,10},{10... | collective-permute-start | bytes 393224 | tf_op jit(solution)/shard_map/ppermute | solution.py:384
  83.5 14.2 %collective-permute-start.14 = (bf16[128,1024]{1,0:T(8,128)(2,1)}, bf16[128,1024]{1,0:T(8,128)(2,1)S(1)}, u32[]{:S(2)}, u32[]{:S(2)}) collective-permute-start(bf16[128,1024]{1,0:T(8,128)(2,1)} %get-tuple-element.78), channel_id=1, source_target_pairs={{8,0},{16,8},{24,16},{9,1},{17,9},{25,17},{10,2},{18,10},{26,18},{... | collective-permute-start | bytes 786440 | tf_op jit(solution)/shard_map/ppermute | solution.py:554
  94.0 9.0 %collective-permute-start.24 = (bf16[64,1024]{1,0:T(8,128)(2,1)S(1)}, bf16[64,1024]{1,0:T(8,128)(2,1)S(1)}, u32[]{:S(2)}, u32[]{:S(2)}) collective-permute-start(bf16[64,1024]{1,0:T(8,128)(2,1)S(1)} %add_convert_fusion.1), channel_id=1, source_target_pairs={{0,16},{8,24},{16,0},{24,8},{1,17},{9,25},{17,1},{25,9},{2,18},{10... | collective-permute-start | bytes 393224 | tf_op jit(solution)/shard_map/ppermute | solution.py:384
  96.5 18.0 %collective-permute-start.26 = (bf16[512,512]{1,0:T(8,128)(2,1)}, bf16[512,512]{1,0:T(8,128)(2,1)S(1)}, u32[]{:S(2)}, u32[]{:S(2)}) collective-permute-start(bf16[512,512]{1,0:T(8,128)(2,1)} %get-tuple-element.99), channel_id=1, source_target_pairs={{0,1},{1,0},{2,3},{3,2},{4,5},{5,4},{6,7},{7,6},{8,9},{9,8},{10,11... | collective-permute-start | bytes 1572872 | tf_op jit(solution)/shard_map/ppermute | solution.py:384
  103.0 9.7 %collective-permute-start.25 = (bf16[64,1024]{1,0:T(8,128)(2,1)S(1)}, bf16[64,1024]{1,0:T(8,128)(2,1)S(1)}, u32[]{:S(2)}, u32[]{:S(2)}) collective-permute-start(bf16[64,1024]{1,0:T(8,128)(2,1)S(1)} %add_convert_fusion), channel_id=1, source_target_pairs={{0,1},{1,0},{2,3},{3,2},{4,5},{5,4},{6,7},{7,6},{8,9},{9,8},{10,11... | collective-permute-start | bytes 393224 | tf_op jit(solution)/shard_map/ppermute | solution.py:384
  (19 other events, 91.5 us)

commit v16 on v15

--- a/solution.py
+++ b/solution.py
@@ -506,8 +506,7 @@
     other_part = swap_pairs(other_sent, "dp", 1)
     if square:
 
-        def spread(piece, gate):
-            across = lax.ppermute(piece, "tp", [(t, t ^ subs) for t in range(n_tp)])
+        def spread(piece, across, gate):
             near = [(t, t ^ 1) for t in range(n_tp)]
             return [
                 piece,
@@ -516,12 +515,15 @@
                 lax.ppermute(after(across, gate), "tp", near),
             ]
 
+        opposite = [(t, t ^ subs) for t in range(n_tp)]
+        across = lax.ppermute(moved, "tp", opposite)
         ring_pieces[2], ring_pieces[3], _ = lax.optimization_barrier((*ring_pieces[2:4], other_sent))
         ring_step()
         *last, own_part, other_part = lax.optimization_barrier((*ring_pieces[4:6], own_part, other_part))
         last = lax.ppermute(jnp.stack(last), "seq", ring)
-        moved_other = transposed(after(moved_other, ring_pieces[2]))
-        cot_pieces = spread(moved, ring_pieces[4]) + spread(moved_other, own_part)
+        moved_other = transposed(after(moved_other, across))
+        across_other = lax.ppermute(moved_other, "tp", opposite)
+        cot_pieces = spread(moved, across, other_part) + spread(moved_other, across_other, own_part)
     else:
         full = lax.all_gather(cot, "tp", axis=1, tiled=True)
         cot_all = lax.all_to_all(full, "seq", 1, 0, tiled=True)
@@ -572,7 +574,7 @@
     while distance < n_seq:
         rounded = lag_sum.astype(bf16)
         received = swap_pairs(rounded, "seq", distance)
-        if square and distance == 1:
+        if square and distance == 2:
             weight_place, rounded = lax.optimization_barrier((weight_place, rounded))
             weight_sent, weight_own = weight_sum(weight_place, cot_pieces, ring_pieces, rows)
             weight_received = swap_pairs(weight_sent, "dp", 1)
@@ -580,8 +582,10 @@
         lag_sum = rounded.astype(f32) + received.astype(f32)
         distance *= 2
     mine = lag_sum.astype(bf16)
+    grad_key, grad_value = run_back(after(later, weight_own) if square else later)
+    if square:
+        mine, grad_key = lax.optimization_barrier((mine, grad_key))
     theirs = swap_pairs(mine, "dp", 1)
-    grad_key, grad_value = run_back(after(later, weight_own) if square else later)
     first = me_dp == 0
     lag_sum = jnp.concatenate([jnp.where(first, mine, theirs), jnp.where(first, theirs, mine)], axis=0)
     grad_filter = lag_sum.astype(f32).T * (norm_factor * scale)

time: 117 us -> 120 us (1.026)
  waiting for transfers between devices: 24.9 us -> 27.9 us
    ppermute x8, waiting for transfers between devices: 9.24 us -> 16.3 us  [swap_pairs(): return lax.ppermute(value, axis, [(i, i ^ distance) for i in range(count)])]
    ppermute x2, waiting for transfers between devices: 4.32 us -> 0.01 us  [the longest x1 0.01 us: per_device(): across = lax.ppermute(moved, 'tp', opposite)]
  transfers between devices with their start and end apart: 27 -> 27, of which waited for: 9 -> 11; matrix products, arithmetic and copies ran while one was open for 6% -> 6% of each run, Pallas kernels for 30% -> 29%
where the time goes in v16:
time: 120 us; the launch traced here: 119 us
  starting transfers between devices  42.9 us (36%)
  Pallas kernels  34.9 us (29%)
  waiting for transfers between devices  27.9 us (23%)
  other arithmetic  6.56 us (5%)
  local copies, waits for them, and re-layouts  6.14 us (5%)
    pallas_call x3, Pallas kernels, by_channel(): pl.pallas_call(kernel, in_specs=[pl.BlockSpec(memory_space=pltpu.SMEM)] *...  16.9 us
    ppermute x8, waiting for transfers between devices, swap_pairs(): return lax.ppermute(value, axis, [(i, i ^ distance) for i in range(count)])  16.3 us
    pallas_call x2, Pallas kernels, local_call(): pl.pallas_call(kernel, in_specs=[pl.BlockSpec(memory_space=pltpu.SMEM)] +...  13.8 us
    ppermute x8, starting transfers between devices, swap_pairs(): return lax.ppermute(value, axis, [(i, i ^ distance) for i in range(count)])  12.3 us
    ppermute x4, starting transfers between devices, ring_step(): ring_pieces.append(lax.ppermute(ring_pieces[-2], 'seq', ring))  10.7 us
    ppermute x4, waiting for transfers between devices, ring_step(): ring_pieces.append(lax.ppermute(ring_pieces[-2], 'seq', ring))  7.44 us
    ppermute x1, starting transfers between devices, per_device(): prior = lax.ppermute(tail, 'seq', [(i, i + 1) for i in range(n_seq - 1)])  7.09 us
    pallas_call x2, Pallas kernels, transposed(): pl.pallas_call(transpose_kernel, in_specs=[pl.BlockSpec(memory_space=pl.A...  4.27 us
  transfers between devices with their start and end apart: 27, of which 11 were waited for; matrix products, arithmetic and copies ran while one was open for 6% of the time, Pallas kernels for 29%

profile of v16, /device:TPU:0, one launch (start us, length us, event | category | flops | bytes accessed | tf_op | source)
XLA Modules:
  0.0 119.3 jit_solution(4705062406052969262)
XLA Ops:
  2.4 7.1 %collective-permute-start = (bf16[128,1024]{1,0:T(8,128)(2,1)S(1)}, bf16[128,1024]{1,0:T(8,128)(2,1)S(1)}, u32[]{:S(2)}, u32[]{:S(2)}) collective-permute-start(bf16[128,1024]{1,0:T(8,128)(2,1)S(1)} %fusion.2), channel_id=1, source_target_pairs={{0,8},{8,16},{16,24},{1,9},{9,17},{17,25},{2,10},{10,18},{18,26},{... | collective-permute-start | bytes 786440 | tf_op jit(solution)/shard_map/ppermute | solution.py:419
  9.5 1.7 %collective-permute-start.6 = (bf16[256,1024]{1,0:T(8,128)(2,1)}, bf16[256,1024]{1,0:T(8,128)(2,1)S(1)}, u32[]{:S(2)}, u32[]{:S(2)}) collective-permute-start(bf16[256,1024]{1,0:T(8,128)(2,1)} %bitcast.32), channel_id=1, source_target_pairs={{0,0},{1,4},{2,2},{3,6},{4,1},{5,5},{6,3},{7,7},{8,8},{9,12},{10,1... | collective-permute-start | bytes 1572872 | tf_op jit(solution)/shard_map/ppermute | solution.py:428
  11.2 2.8 %collective-permute-done.refs_3_.refs_6_ = bf16[128,1024]{1,0:T(8,128)(2,1)S(1)} collective-permute-done((bf16[128,1024]{1,0:T(8,128)(2,1)S(1)}, bf16[128,1024]{1,0:T(8,128)(2,1)S(1)}, u32[]{:S(2)}, u32[]{:S(2)}) %collective-permute-start) | collective-permute-done | bytes 262176 | tf_op jit(solution)/shard_map/ppermute | solution.py:419
  19.0 5.5 %shard_map.145 = (f32[256,1024]{1,0:T(8,128)}, bf16[256,512]{1,0:T(8,128)(2,1)}, bf16[256,512]{1,0:T(8,128)(2,1)}) custom-call(s32[1]{0:T(128)} %bitcast.refs_0_, bf16[768,384]{1,0:T(8,128)(2,1)} %constant.66.clone.refs_1_.refs_0_, bf16[768,384]{1,0:T(8,128)(2,1)} %constant.67.clone.refs_2_.refs_1_, bf16[128,1024]{1,0:T(8,128)(2,1)} %copy-done.5, ...), custom_call_target="tpu_custom_call" | custom-call | flops 22020096 | bytes 57408 | tf_op jit(solution)/shard_map/pallas_call | solution.py:281
  24.5 1.5 %collective-permute-start.1 = (bf16[256,512]{1,0:T(8,128)(2,1)}, bf16[256,512]{1,0:T(8,128)(2,1)S(1)}, u32[]{:S(2)}, u32[]{:S(2)}) collective-permute-start(bf16[256,512]{1,0:T(8,128)(2,1)} %get-tuple-element.58), channel_id=1, source_target_pairs={{0,1},{1,0},{2,3},{3,2},{4,5},{5,4},{6,7},{7,6},{8,9},{9,8},{10,11... | collective-permute-start | bytes 786440 | tf_op jit(solution)/shard_map/ppermute | solution.py:384
  26.0 1.3 %collective-permute-done.7.second_mine = bf16[256,1024]{1,0:T(8,128)(2,1)S(1)} collective-permute-done((bf16[256,1024]{1,0:T(8,128)(2,1)}, bf16[256,1024]{1,0:T(8,128)(2,1)S(1)}, u32[]{:S(2)}, u32[]{:S(2)}) %collective-permute-start.7) | collective-permute-done | bytes 524320 | tf_op jit(solution)/shard_map/ppermute | solution.py:428
  27.3 3.1 %collective-permute-start.8 = (bf16[256,1024]{1,0:T(8,128)(2,1)S(1)}, bf16[256,1024]{1,0:T(8,128)(2,1)S(1)}, u32[]{:S(2)}, u32[]{:S(2)}) collective-permute-start(bf16[256,1024]{1,0:T(8,128)(2,1)S(1)} %collective-permute-done.6.first_mine), channel_id=1, source_target_pairs={{0,2},{1,3},{2,0},{3,1},{4,6},{5,7},{6,4},{7,5},{8,10},{9,11},{10,... | collective-permute-start | bytes 1572872 | tf_op jit(solution)/shard_map/ppermute | solution.py:495
  31.2 1.4 %collective-permute-start.10 = (bf16[256,1024]{1,0:T(8,128)(2,1)S(1)}, bf16[256,1024]{1,0:T(8,128)(2,1)S(1)}, u32[]{:S(2)}, u32[]{:S(2)}) collective-permute-start(bf16[256,1024]{1,0:T(8,128)(2,1)S(1)} %collective-permute-done.3.rows_in), channel_id=1, source_target_pairs={{0,1},{1,0},{2,3},{3,2},{4,5},{5,4},{6,7},{7,6},{8,9},{9,8},{10,11... | collective-permute-start | bytes 1572872 | tf_op jit(solution)/shard_map/ppermute | solution.py:384
  32.7 2.0 %shard_map.146.refs_0_ = bf16[1024,256]{1,0:T(8,128)(2,1)} custom-call(bf16[256,1024]{1,0:T(8,128)(2,1)} %copy-done.18), custom_call_target="tpu_custom_call" | custom-call | bytes 16384 | tf_op jit(solution)/shard_map/pallas_call | solution.py:367
  34.7 5.8 %collective-permute-start.4 = (bf16[256,512]{1,0:T(8,128)(2,1)}, bf16[256,512]{1,0:T(8,128)(2,1)S(1)}, u32[]{:S(2)}, u32[]{:S(2)}) collective-permute-start(bf16[256,512]{1,0:T(8,128)(2,1)} %get-tuple-element.60.refs_8_), channel_id=1, source_target_pairs={{0,16},{16,24},{24,8},{8,0},{1,17},{17,25},{25,9},{9,1},{2,18},{18... | collective-permute-start | bytes 786440 | tf_op jit(solution)/shard_map/ppermute | solution.py:489
  40.5 2.2 %collective-permute-start.5 = (bf16[256,512]{1,0:T(8,128)(2,1)S(1)}, bf16[256,512]{1,0:T(8,128)(2,1)S(1)}, u32[]{:S(2)}, u32[]{:S(2)}) collective-permute-start(bf16[256,512]{1,0:T(8,128)(2,1)S(1)} %collective-permute-done.1.refs_9_), channel_id=1, source_target_pairs={{0,16},{16,24},{24,8},{8,0},{1,17},{17,25},{25,9},{9,1},{2,18},{18... | collective-permute-start | bytes 786440 | tf_op jit(solution)/shard_map/ppermute | solution.py:489
  44.6 6.4 %shard_map.147 = (bf16[256,1024]{1,0:T(8,128)(2,1)}, f32[256,1024]{1,0:T(8,128)}) custom-call(s32[3]{0:T(128)} %pad_add_fusion.place_ref, bf16[256,1024]{1,0:T(8,128)(2,1)} %copy-done.6, bf16[256,1024]{1,0:T(8,128)(2,1)} %copy-done.7, bf16[256,1024]{1,0:T(8,128)(2,1)} %copy-done.16, bf16[256,1024]{1,0:T(8,128)(2,1)} %copy-done.17, bf16[1024,2048]{1,0:T(8,128)(2,1)} %weight.1), custom_call_target="tpu_custom_call" | custom-call | flops 33554432 | bytes 122880 | tf_op jit(solution)/shard_map/pallas_call | solution.py:301
  51.0 1.6 %collective-permute-start.13 = (bf16[256,1024]{1,0:T(8,128)(2,1)}, bf16[256,1024]{1,0:T(8,128)(2,1)S(1)}, u32[]{:S(2)}, u32[]{:S(2)}) collective-permute-start(bf16[256,1024]{1,0:T(8,128)(2,1)} %get-tuple-element.70), channel_id=1, source_target_pairs={{0,1},{1,0},{2,3},{3,2},{4,5},{5,4},{6,7},{7,6},{8,9},{9,8},{10,11... | collective-permute-start | bytes 1572872 | tf_op jit(solution)/shard_map/ppermute | solution.py:384
  53.3 1.2 collective-permute-start.11
  54.5 1.5 %collective-permute-start.12 = (bf16[256,512]{1,0:T(8,128)(2,1)S(1)}, bf16[256,512]{1,0:T(8,128)(2,1)S(1)}, u32[]{:S(2)}, u32[]{:S(2)}) collective-permute-start(bf16[256,512]{1,0:T(8,128)(2,1)S(1)} %collective-permute-done.5.refs_11_), channel_id=1, source_target_pairs={{0,16},{16,24},{24,8},{8,0},{1,17},{17,25},{25,9},{9,1},{2,18},{18... | collective-permute-start | bytes 786440 | tf_op jit(solution)/shard_map/ppermute | solution.py:489
  56.0 2.2 %shard_map.149.refs_4_ = bf16[1024,256]{1,0:T(8,128)(2,1)} custom-call(bf16[256,1024]{1,0:T(8,128)(2,1)} %copy-done.19), custom_call_target="tpu_custom_call" | custom-call | bytes 16384 | tf_op jit(solution)/shard_map/pallas_call | solution.py:367
  58.2 1.7 %collective-permute-start.22 = (bf16[1024,256]{1,0:T(8,128)(2,1)}, bf16[1024,256]{1,0:T(8,128)(2,1)S(1)}, u32[]{:S(2)}, u32[]{:S(2)}) collective-permute-start(bf16[1024,256]{1,0:T(8,128)(2,1)} %shard_map.149.refs_4_), channel_id=1, source_target_pairs={{0,4},{2,6},{4,0},{6,2},{1,5},{3,7},{5,1},{7,3},{8,12},{10,14},{12... | collective-permute-start | bytes 1572872 | tf_op jit(solution)/shard_map/ppermute | solution.py:525
  59.9 2.6 %collective-permute-done.11.refs_12_ = bf16[256,512]{1,0:T(8,128)(2,1)S(1)} collective-permute-done((bf16[256,512]{1,0:T(8,128)(2,1)S(1)}, bf16[256,512]{1,0:T(8,128)(2,1)S(1)}, u32[]{:S(2)}, u32[]{:S(2)}) %collective-permute-start.11) | collective-permute-done | bytes 262176 | tf_op jit(solution)/shard_map/ppermute | solution.py:489
  62.5 4.2 %collective-permute-done.12.refs_13_ = bf16[256,512]{1,0:T(8,128)(2,1)S(1)} collective-permute-done((bf16[256,512]{1,0:T(8,128)(2,1)S(1)}, bf16[256,512]{1,0:T(8,128)(2,1)S(1)}, u32[]{:S(2)}, u32[]{:S(2)}) %collective-permute-start.12) | collective-permute-done | bytes 262176 | tf_op jit(solution)/shard_map/ppermute | solution.py:489
  66.7 1.2 %collective-permute-start.14 = (bf16[2,256,512]{2,1,0:T(8,128)(2,1)S(1)}, bf16[2,256,512]{2,1,0:T(8,128)(2,1)S(1)}, u32[]{:S(2)}, u32[]{:S(2)}) collective-permute-start(bf16[2,256,512]{2,1,0:T(8,128)(2,1)S(1)} %pad_maximum_fusion.1), channel_id=1, source_target_pairs={{0,16},{16,24},{24,8},{8,0},{1,17},{17,25},{25,9},{9,1},{2,18},{18... | collective-permute-start | bytes 1572872 | tf_op jit(solution)/shard_map/ppermute | solution.py:523
  68.0 5.9 %shard_map.148 = (bf16[256,1024]{1,0:T(8,128)(2,1)}, bf16[256,1024]{1,0:T(8,128)(2,1)}, bf16[128,1024]{1,0:T(8,128)(2,1)}, bf16[64,1024]{1,0:T(8,128)(2,1)}, f32[64,1024]{1,0:T(8,128)}) custom-call(bf16[768,384]{1,0:T(8,128)(2,1)} %constant.66.clone.refs_1_.refs_0_, bf16[768,384]{1,0:T(8,128)(2,1)} %constant.67.clone.refs_2_.refs_1_, ...), custom_call_target="tpu_custom_call" | custom-call | flops 20447232 | bytes 96320 | tf_op jit(solution)/shard_map/pallas_call | solution.py:281
  73.9 1.3 %collective-permute-start.15 = (bf16[64,1024]{1,0:T(8,128)(2,1)}, bf16[64,1024]{1,0:T(8,128)(2,1)S(1)}, u32[]{:S(2)}, u32[]{:S(2)}) collective-permute-start(bf16[64,1024]{1,0:T(8,128)(2,1)} %get-tuple-element.83), channel_id=1, source_target_pairs={{0,1},{1,0},{2,3},{3,2},{4,5},{5,4},{6,7},{7,6},{8,9},{9,8},{10,11... | collective-permute-start | bytes 393224 | tf_op jit(solution)/shard_map/ppermute | solution.py:384
  75.9 3.3 %collective-permute-done.15 = bf16[64,1024]{1,0:T(8,128)(2,1)S(1)} collective-permute-done((bf16[64,1024]{1,0:T(8,128)(2,1)}, bf16[64,1024]{1,0:T(8,128)(2,1)S(1)}, u32[]{:S(2)}, u32[]{:S(2)}) %collective-permute-start.15) | collective-permute-done | bytes 131104 | tf_op jit(solution)/shard_map/ppermute | solution.py:384
  81.3 5.1 %collective-permute-done.16 = bf16[64,1024]{1,0:T(8,128)(2,1)S(1)} collective-permute-done((bf16[64,1024]{1,0:T(8,128)(2,1)S(1)}, bf16[64,1024]{1,0:T(8,128)(2,1)S(1)}, u32[]{:S(2)}, u32[]{:S(2)}) %collective-permute-start.16) | collective-permute-done | bytes 131104 | tf_op jit(solution)/shard_map/ppermute | solution.py:384
  86.3 1.3 %collective-permute-start.24 = (bf16[128,1024]{1,0:T(8,128)(2,1)}, bf16[128,1024]{1,0:T(8,128)(2,1)S(1)}, u32[]{:S(2)}, u32[]{:S(2)}) collective-permute-start(bf16[128,1024]{1,0:T(8,128)(2,1)} %get-tuple-element.96), channel_id=1, source_target_pairs={{8,0},{16,8},{24,16},{9,1},{17,9},{25,17},{10,2},{18,10},{26,18},{... | collective-permute-start | bytes 786440 | tf_op jit(solution)/shard_map/ppermute | solution.py:556
  87.7 3.0 %collective-permute-start.17 = (bf16[64,1024]{1,0:T(8,128)(2,1)S(1)}, bf16[64,1024]{1,0:T(8,128)(2,1)S(1)}, u32[]{:S(2)}, u32[]{:S(2)}) collective-permute-start(bf16[64,1024]{1,0:T(8,128)(2,1)S(1)} %add_convert_fusion.1), channel_id=1, source_target_pairs={{0,16},{8,24},{16,0},{24,8},{1,17},{9,25},{17,1},{25,9},{2,18},{10... | collective-permute-start | bytes 393224 | tf_op jit(solution)/shard_map/ppermute | solution.py:384
  92.4 7.4 %shard_map.150 = (bf16[512,512]{1,0:T(8,128)(2,1)}, f32[512,512]{1,0:T(8,128)}) custom-call(s32[5]{0:T(128)} %pad_add_fusion.1.place_ref, bf16[1024,256]{1,0:T(8,128)(2,1)} %shard_map.146.refs_0_, bf16[1024,256]{1,0:T(8,128)(2,1)} %copy-done.11, bf16[1024,256]{1,0:T(8,128)(2,1)} %copy-done.8, bf16[1024,256]{1,0:T(8,128)(2,1)} %copy-done.13, ...), custom_call_target="tpu_custom_call" | custom-call | flops 33554432 | bytes 122880 | tf_op jit(solution)/shard_map/pallas_call | solution.py:301
  99.8 1.3 %collective-permute-start.26 = (bf16[512,512]{1,0:T(8,128)(2,1)}, bf16[512,512]{1,0:T(8,128)(2,1)S(1)}, u32[]{:S(2)}, u32[]{:S(2)}) collective-permute-start(bf16[512,512]{1,0:T(8,128)(2,1)} %get-tuple-element.103), channel_id=1, source_target_pairs={{0,1},{1,0},{2,3},{3,2},{4,5},{5,4},{6,7},{7,6},{8,9},{9,8},{10,11... | collective-permute-start | bytes 1572872 | tf_op jit(solution)/shard_map/ppermute | solution.py:384
  102.9 5.5 %shard_map.151 = (bf16[256,1024]{1,0:T(8,128)(2,1)}, bf16[256,1024]{1,0:T(8,128)(2,1)}) custom-call(bf16[768,384]{1,0:T(8,128)(2,1)} %constant.66.clone.refs_1_.refs_0_, bf16[768,384]{1,0:T(8,128)(2,1)} %constant.67.clone.refs_2_.refs_1_, bf16[256,1024]{1,0:T(8,128)(2,1)} %get-tuple-element.95.refs_2_, bf16[128,1024]{1,0:T(8,128)(2,1)} %copy-done.23, ...), custom_call_target="tpu_custom_call" | custom-call | flops 5637144576 | bytes 49216 | tf_op jit(solution)/shard_map/pallas_call | solution.py:281
  108.5 1.3 %collective-permute-start.25 = (bf16[64,1024]{1,0:T(8,128)(2,1)S(1)}, bf16[64,1024]{1,0:T(8,128)(2,1)S(1)}, u32[]{:S(2)}, u32[]{:S(2)}) collective-permute-start(bf16[64,1024]{1,0:T(8,128)(2,1)S(1)} %add_convert_fusion), channel_id=1, source_target_pairs={{0,1},{1,0},{2,3},{3,2},{4,5},{5,4},{6,7},{7,6},{8,9},{9,8},{10,11... | collective-permute-start | bytes 393224 | tf_op jit(solution)/shard_map/ppermute | solution.py:384
  109.8 6.1 %collective-permute-done.25 = bf16[64,1024]{1,0:T(8,128)(2,1)S(1)} collective-permute-done((bf16[64,1024]{1,0:T(8,128)(2,1)S(1)}, bf16[64,1024]{1,0:T(8,128)(2,1)S(1)}, u32[]{:S(2)}, u32[]{:S(2)}) %collective-permute-start.25) | collective-permute-done | bytes 131104 | tf_op jit(solution)/shard_map/ppermute | solution.py:384
  117.9 1.5 %pad_maximum_fusion = f32[512,1024]{1,0:T(8,128)} fusion(f32[512,512]{1,0:T(8,128)S(1)} %get-tuple-element.111, f32[512,512]{1,0:T(8,128)S(1)} %get-tuple-element.110), kind=kLoop, calls=%fused_computation | loop fusion | flops 524288 | bytes 4194304 | tf_op jit(solution)/shard_map/concatenate | solution.py:595
  (93 shorter events, 18.6 us)
Async XLA Ops:
  1.7 12.9 %collective-permute-start.2 = (bf16[256,1024]{1,0:T(8,128)(2,1)}, bf16[256,1024]{1,0:T(8,128)(2,1)S(1)}, u32[]{:S(2)}, u32[]{:S(2)}) collective-permute-start(bf16[256,1024]{1,0:T(8,128)(2,1)} %bitcast.31), channel_id=1, source_target_pairs={{2,4},{4,2},{8,14},{14,8},{18,20},{20,18},{24,30},{30,24},{3,5},{5... | collective-permute-start | bytes 1572872 | tf_op jit(solution)/shard_map/ppermute | solution.py:441
  2.4 11.6 %collective-permute-start = (bf16[128,1024]{1,0:T(8,128)(2,1)S(1)}, bf16[128,1024]{1,0:T(8,128)(2,1)S(1)}, u32[]{:S(2)}, u32[]{:S(2)}) collective-permute-start(bf16[128,1024]{1,0:T(8,128)(2,1)S(1)} %fusion.2), channel_id=1, source_target_pairs={{0,8},{8,16},{16,24},{1,9},{9,17},{17,25},{2,10},{10,18},{18,26},{... | collective-permute-start | bytes 786440 | tf_op jit(solution)/shard_map/ppermute | solution.py:419
  9.5 16.5 %collective-permute-start.6 = (bf16[256,1024]{1,0:T(8,128)(2,1)}, bf16[256,1024]{1,0:T(8,128)(2,1)S(1)}, u32[]{:S(2)}, u32[]{:S(2)}) collective-permute-start(bf16[256,1024]{1,0:T(8,128)(2,1)} %bitcast.32), channel_id=1, source_target_pairs={{0,0},{1,4},{2,2},{3,6},{4,1},{5,5},{6,3},{7,7},{8,8},{9,12},{10,1... | collective-permute-start | bytes 1572872 | tf_op jit(solution)/shard_map/ppermute | solution.py:428
  14.0 13.3 %collective-permute-start.7 = (bf16[256,1024]{1,0:T(8,128)(2,1)}, bf16[256,1024]{1,0:T(8,128)(2,1)S(1)}, u32[]{:S(2)}, u32[]{:S(2)}) collective-permute-start(bf16[256,1024]{1,0:T(8,128)(2,1)} %bitcast.33), channel_id=1, source_target_pairs={{0,4},{1,0},{2,6},{3,2},{4,5},{5,1},{6,7},{7,3},{8,12},{9,8},{10,1... | collective-permute-start | bytes 1572872 | tf_op jit(solution)/shard_map/ppermute | solution.py:428
  15.8 15.4 %collective-permute-start.3 = (bf16[256,1024]{1,0:T(8,128)(2,1)S(1)}, bf16[256,1024]{1,0:T(8,128)(2,1)S(1)}, u32[]{:S(2)}, u32[]{:S(2)}) collective-permute-start(bf16[256,1024]{1,0:T(8,128)(2,1)S(1)} %broadcast_select_fusion), channel_id=1, source_target_pairs={{0,0},{2,16},{4,12},{6,28},{8,24},{10,8},{12,20},{14,4},{16,2},{18... | collective-permute-start | bytes 1572872 | tf_op jit(solution)/shard_map/ppermute | solution.py:453
  24.5 6.6 %collective-permute-start.1 = (bf16[256,512]{1,0:T(8,128)(2,1)}, bf16[256,512]{1,0:T(8,128)(2,1)S(1)}, u32[]{:S(2)}, u32[]{:S(2)}) collective-permute-start(bf16[256,512]{1,0:T(8,128)(2,1)} %get-tuple-element.58), channel_id=1, source_target_pairs={{0,1},{1,0},{2,3},{3,2},{4,5},{5,4},{6,7},{7,6},{8,9},{9,8},{10,11... | collective-permute-start | bytes 786440 | tf_op jit(solution)/shard_map/ppermute | solution.py:384
  26.0 17.8 %copy-start.6 = (bf16[256,1024]{1,0:T(8,128)(2,1)}, bf16[256,1024]{1,0:T(8,128)(2,1)S(1)}, u32[]{:S(2)}) copy-start(bf16[256,1024]{1,0:T(8,128)(2,1)S(1)} %collective-permute-done.6.first_mine) | copy-start | bytes 1572868
  27.3 15.5 %collective-permute-start.8 = (bf16[256,1024]{1,0:T(8,128)(2,1)S(1)}, bf16[256,1024]{1,0:T(8,128)(2,1)S(1)}, u32[]{:S(2)}, u32[]{:S(2)}) collective-permute-start(bf16[256,1024]{1,0:T(8,128)(2,1)S(1)} %collective-permute-done.6.first_mine), channel_id=1, source_target_pairs={{0,2},{1,3},{2,0},{3,1},{4,6},{5,7},{6,4},{7,5},{8,10},{9,11},{10,... | collective-permute-start | bytes 1572872 | tf_op jit(solution)/shard_map/ppermute | solution.py:495
  30.4 13.4 %collective-permute-start.9 = (bf16[256,1024]{1,0:T(8,128)(2,1)S(1)}, bf16[256,1024]{1,0:T(8,128)(2,1)S(1)}, u32[]{:S(2)}, u32[]{:S(2)}) collective-permute-start(bf16[256,1024]{1,0:T(8,128)(2,1)S(1)} %collective-permute-done.7.second_mine), channel_id=1, source_target_pairs={{0,2},{1,3},{2,0},{3,1},{4,6},{5,7},{6,4},{7,5},{8,10},{9,11},{10,... | collective-permute-start | bytes 1572872 | tf_op jit(solution)/shard_map/ppermute | solution.py:495
  31.2 42.7 %copy-start.20 = (bf16[256,512]{1,0:T(8,128)(2,1)}, bf16[256,512]{1,0:T(8,128)(2,1)S(1)}, u32[]{:S(2)}) copy-start(bf16[256,512]{1,0:T(8,128)(2,1)S(1)} %collective-permute-done.1.refs_9_) | copy-start | bytes 786436
  31.2 19.8 %collective-permute-start.10 = (bf16[256,1024]{1,0:T(8,128)(2,1)S(1)}, bf16[256,1024]{1,0:T(8,128)(2,1)S(1)}, u32[]{:S(2)}, u32[]{:S(2)}) collective-permute-start(bf16[256,1024]{1,0:T(8,128)(2,1)S(1)} %collective-permute-done.3.rows_in), channel_id=1, source_target_pairs={{0,1},{1,0},{2,3},{3,2},{4,5},{5,4},{6,7},{7,6},{8,9},{9,8},{10,11... | collective-permute-start | bytes 1572872 | tf_op jit(solution)/shard_map/ppermute | solution.py:384
  34.7 17.9 %collective-permute-start.4 = (bf16[256,512]{1,0:T(8,128)(2,1)}, bf16[256,512]{1,0:T(8,128)(2,1)S(1)}, u32[]{:S(2)}, u32[]{:S(2)}) collective-permute-start(bf16[256,512]{1,0:T(8,128)(2,1)} %get-tuple-element.60.refs_8_), channel_id=1, source_target_pairs={{0,16},{16,24},{24,8},{8,0},{1,17},{17,25},{25,9},{9,1},{2,18},{18... | collective-permute-start | bytes 786440 | tf_op jit(solution)/shard_map/ppermute | solution.py:489
  40.5 12.7 %collective-permute-start.5 = (bf16[256,512]{1,0:T(8,128)(2,1)S(1)}, bf16[256,512]{1,0:T(8,128)(2,1)S(1)}, u32[]{:S(2)}, u32[]{:S(2)}) collective-permute-start(bf16[256,512]{1,0:T(8,128)(2,1)S(1)} %collective-permute-done.1.refs_9_), channel_id=1, source_target_pairs={{0,16},{16,24},{24,8},{8,0},{1,17},{17,25},{25,9},{9,1},{2,18},{18... | collective-permute-start | bytes 786440 | tf_op jit(solution)/shard_map/ppermute | solution.py:489
  42.7 13.3 %collective-permute-start.19 = (bf16[1024,256]{1,0:T(8,128)(2,1)}, bf16[1024,256]{1,0:T(8,128)(2,1)S(1)}, u32[]{:S(2)}, u32[]{:S(2)}) collective-permute-start(bf16[1024,256]{1,0:T(8,128)(2,1)} %shard_map.146.refs_0_), channel_id=1, source_target_pairs={{0,4},{2,6},{4,0},{6,2},{1,5},{3,7},{5,1},{7,3},{8,12},{10,14},{12... | collective-permute-start | bytes 1572872 | tf_op jit(solution)/shard_map/ppermute | solution.py:519
  51.0 15.7 %collective-permute-start.13 = (bf16[256,1024]{1,0:T(8,128)(2,1)}, bf16[256,1024]{1,0:T(8,128)(2,1)S(1)}, u32[]{:S(2)}, u32[]{:S(2)}) collective-permute-start(bf16[256,1024]{1,0:T(8,128)(2,1)} %get-tuple-element.70), channel_id=1, source_target_pairs={{0,1},{1,0},{2,3},{3,2},{4,5},{5,4},{6,7},{7,6},{8,9},{9,8},{10,11... | collective-permute-start | bytes 1572872 | tf_op jit(solution)/shard_map/ppermute | solution.py:384
  52.6 21.3 %copy-start.21 = (bf16[256,512]{1,0:T(8,128)(2,1)}, bf16[256,512]{1,0:T(8,128)(2,1)S(1)}, u32[]{:S(2)}) copy-start(bf16[256,512]{1,0:T(8,128)(2,1)S(1)} %collective-permute-done.4.refs_10_) | copy-start | bytes 786436
  53.3 20.6 %copy-start.22 = (bf16[256,512]{1,0:T(8,128)(2,1)}, bf16[256,512]{1,0:T(8,128)(2,1)S(1)}, u32[]{:S(2)}) copy-start(bf16[256,512]{1,0:T(8,128)(2,1)S(1)} %collective-permute-done.5.refs_11_) | copy-start | bytes 786436
  53.3 9.2 %collective-permute-start.11 = (bf16[256,512]{1,0:T(8,128)(2,1)S(1)}, bf16[256,512]{1,0:T(8,128)(2,1)S(1)}, u32[]{:S(2)}, u32[]{:S(2)}) collective-permute-start(bf16[256,512]{1,0:T(8,128)(2,1)S(1)} %collective-permute-done.4.refs_10_), channel_id=1, source_target_pairs={{0,16},{16,24},{24,8},{8,0},{1,17},{17,25},{25,9},{9,1},{2,18},{18... | collective-permute-start | bytes 786440 | tf_op jit(solution)/shard_map/ppermute | solution.py:489
  54.5 12.2 %collective-permute-start.12 = (bf16[256,512]{1,0:T(8,128)(2,1)S(1)}, bf16[256,512]{1,0:T(8,128)(2,1)S(1)}, u32[]{:S(2)}, u32[]{:S(2)}) collective-permute-start(bf16[256,512]{1,0:T(8,128)(2,1)S(1)} %collective-permute-done.5.refs_11_), channel_id=1, source_target_pairs={{0,16},{16,24},{24,8},{8,0},{1,17},{17,25},{25,9},{9,1},{2,18},{18... | collective-permute-start | bytes 786440 | tf_op jit(solution)/shard_map/ppermute | solution.py:489
  56.0 19.8 %copy-start.8 = (bf16[1024,256]{1,0:T(8,128)(2,1)}, bf16[1024,256]{1,0:T(8,128)(2,1)S(1)}, u32[]{:S(2)}) copy-start(bf16[1024,256]{1,0:T(8,128)(2,1)S(1)} %collective-permute-done.19.refs_2_) | copy-start | bytes 1572868
  58.2 17.6 %collective-permute-start.22 = (bf16[1024,256]{1,0:T(8,128)(2,1)}, bf16[1024,256]{1,0:T(8,128)(2,1)S(1)}, u32[]{:S(2)}, u32[]{:S(2)}) collective-permute-start(bf16[1024,256]{1,0:T(8,128)(2,1)} %shard_map.149.refs_4_), channel_id=1, source_target_pairs={{0,4},{2,6},{4,0},{6,2},{1,5},{3,7},{5,1},{7,3},{8,12},{10,14},{12... | collective-permute-start | bytes 1572872 | tf_op jit(solution)/shard_map/ppermute | solution.py:525
  66.7 12.5 %collective-permute-start.14 = (bf16[2,256,512]{2,1,0:T(8,128)(2,1)S(1)}, bf16[2,256,512]{2,1,0:T(8,128)(2,1)S(1)}, u32[]{:S(2)}, u32[]{:S(2)}) collective-permute-start(bf16[2,256,512]{2,1,0:T(8,128)(2,1)S(1)} %pad_maximum_fusion.1), channel_id=1, source_target_pairs={{0,16},{16,24},{24,8},{8,0},{1,17},{17,25},{25,9},{9,1},{2,18},{18... | collective-permute-start | bytes 1572872 | tf_op jit(solution)/shard_map/ppermute | solution.py:523
  73.9 5.2 %collective-permute-start.15 = (bf16[64,1024]{1,0:T(8,128)(2,1)}, bf16[64,1024]{1,0:T(8,128)(2,1)S(1)}, u32[]{:S(2)}, u32[]{:S(2)}) collective-permute-start(bf16[64,1024]{1,0:T(8,128)(2,1)} %get-tuple-element.83), channel_id=1, source_target_pairs={{0,1},{1,0},{2,3},{3,2},{4,5},{5,4},{6,7},{7,6},{8,9},{9,8},{10,11... | collective-permute-start | bytes 393224 | tf_op jit(solution)/shard_map/ppermute | solution.py:384
  75.3 12.4 %collective-permute-start.18 = (bf16[1024,256]{1,0:T(8,128)(2,1)S(1)}, bf16[1024,256]{1,0:T(8,128)(2,1)S(1)}, u32[]{:S(2)}, u32[]{:S(2)}) collective-permute-start(bf16[1024,256]{1,0:T(8,128)(2,1)S(1)} %copy-done), channel_id=1, source_target_pairs={{0,2},{2,0},{4,6},{6,4},{1,3},{3,1},{5,7},{7,5},{8,10},{10,8},{12,... | collective-permute-start | bytes 1572872 | tf_op jit(solution)/shard_map/ppermute | solution.py:513
  75.3 15.4 %collective-permute-start.21 = (bf16[1024,256]{1,0:T(8,128)(2,1)S(1)}, bf16[1024,256]{1,0:T(8,128)(2,1)S(1)}, u32[]{:S(2)}, u32[]{:S(2)}) collective-permute-start(bf16[1024,256]{1,0:T(8,128)(2,1)S(1)} %copy-done.1), channel_id=1, source_target_pairs={{0,2},{2,0},{4,6},{6,4},{1,3},{3,1},{5,7},{7,5},{8,10},{10,8},{12,... | collective-permute-start | bytes 1572872 | tf_op jit(solution)/shard_map/ppermute | solution.py:513
  75.8 14.9 %collective-permute-start.20 = (bf16[1024,256]{1,0:T(8,128)(2,1)S(1)}, bf16[1024,256]{1,0:T(8,128)(2,1)S(1)}, u32[]{:S(2)}, u32[]{:S(2)}) collective-permute-start(bf16[1024,256]{1,0:T(8,128)(2,1)S(1)} %collective-permute-done.19.refs_2_), channel_id=1, source_target_pairs={{0,2},{2,0},{4,6},{6,4},{1,3},{3,1},{5,7},{7,5},{8,10},{10,8},{12,... | collective-permute-start | bytes 1572872 | tf_op jit(solution)/shard_map/ppermute | solution.py:515
  79.2 11.5 %collective-permute-start.23 = (bf16[1024,256]{1,0:T(8,128)(2,1)S(1)}, bf16[1024,256]{1,0:T(8,128)(2,1)S(1)}, u32[]{:S(2)}, u32[]{:S(2)}) collective-permute-start(bf16[1024,256]{1,0:T(8,128)(2,1)S(1)} %collective-permute-done.22.refs_6_), channel_id=1, source_target_pairs={{0,2},{2,0},{4,6},{6,4},{1,3},{3,1},{5,7},{7,5},{8,10},{10,8},{12,... | collective-permute-start | bytes 1572872 | tf_op jit(solution)/shard_map/ppermute | solution.py:515
  80.4 5.9 %collective-permute-start.16 = (bf16[64,1024]{1,0:T(8,128)(2,1)S(1)}, bf16[64,1024]{1,0:T(8,128)(2,1)S(1)}, u32[]{:S(2)}, u32[]{:S(2)}) collective-permute-start(bf16[64,1024]{1,0:T(8,128)(2,1)S(1)} %add_convert_fusion.2), channel_id=1, source_target_pairs={{0,8},{8,0},{16,24},{24,16},{1,9},{9,1},{17,25},{25,17},{2,10},{10... | collective-permute-start | bytes 393224 | tf_op jit(solution)/shard_map/ppermute | solution.py:384
  86.3 15.9 %collective-permute-start.24 = (bf16[128,1024]{1,0:T(8,128)(2,1)}, bf16[128,1024]{1,0:T(8,128)(2,1)S(1)}, u32[]{:S(2)}, u32[]{:S(2)}) collective-permute-start(bf16[128,1024]{1,0:T(8,128)(2,1)} %get-tuple-element.96), channel_id=1, source_target_pairs={{8,0},{16,8},{24,16},{9,1},{17,9},{25,17},{10,2},{18,10},{26,18},{... | collective-permute-start | bytes 786440 | tf_op jit(solution)/shard_map/ppermute | solution.py:556
  87.7 14.5 %collective-permute-start.17 = (bf16[64,1024]{1,0:T(8,128)(2,1)S(1)}, bf16[64,1024]{1,0:T(8,128)(2,1)S(1)}, u32[]{:S(2)}, u32[]{:S(2)}) collective-permute-start(bf16[64,1024]{1,0:T(8,128)(2,1)S(1)} %add_convert_fusion.1), channel_id=1, source_target_pairs={{0,16},{8,24},{16,0},{24,8},{1,17},{9,25},{17,1},{25,9},{2,18},{10... | collective-permute-start | bytes 393224 | tf_op jit(solution)/shard_map/ppermute | solution.py:384
  99.8 17.8 %collective-permute-start.26 = (bf16[512,512]{1,0:T(8,128)(2,1)}, bf16[512,512]{1,0:T(8,128)(2,1)S(1)}, u32[]{:S(2)}, u32[]{:S(2)}) collective-permute-start(bf16[512,512]{1,0:T(8,128)(2,1)} %get-tuple-element.103), channel_id=1, source_target_pairs={{0,1},{1,0},{2,3},{3,2},{4,5},{5,4},{6,7},{7,6},{8,9},{9,8},{10,11... | collective-permute-start | bytes 1572872 | tf_op jit(solution)/shard_map/ppermute | solution.py:384
  108.5 7.4 %collective-permute-start.25 = (bf16[64,1024]{1,0:T(8,128)(2,1)S(1)}, bf16[64,1024]{1,0:T(8,128)(2,1)S(1)}, u32[]{:S(2)}, u32[]{:S(2)}) collective-permute-start(bf16[64,1024]{1,0:T(8,128)(2,1)S(1)} %add_convert_fusion), channel_id=1, source_target_pairs={{0,1},{1,0},{2,3},{3,2},{4,5},{5,4},{6,7},{7,6},{8,9},{9,8},{10,11... | collective-permute-start | bytes 393224 | tf_op jit(solution)/shard_map/ppermute | solution.py:384
  (19 other events, 106.2 us)

commit v17 on v16

--- a/solution.py
+++ b/solution.py
@@ -574,17 +574,19 @@
     while distance < n_seq:
         rounded = lag_sum.astype(bf16)
         received = swap_pairs(rounded, "seq", distance)
-        if square and distance == 2:
+        if square and distance == 1:
             weight_place, rounded = lax.optimization_barrier((weight_place, rounded))
             weight_sent, weight_own = weight_sum(weight_place, cot_pieces, ring_pieces, rows)
             weight_received = swap_pairs(weight_sent, "dp", 1)
             received, weight_own = lax.optimization_barrier((received, weight_own))
+        if square and distance == 2:
+            grad_key, grad_value = run_back(after(later, weight_own))
+            received, grad_key = lax.optimization_barrier((received, grad_key))
         lag_sum = rounded.astype(f32) + received.astype(f32)
         distance *= 2
     mine = lag_sum.astype(bf16)
-    grad_key, grad_value = run_back(after(later, weight_own) if square else later)
-    if square:
-        mine, grad_key = lax.optimization_barrier((mine, grad_key))
+    if not square:
+        grad_key, grad_value = run_back(later)
     theirs = swap_pairs(mine, "dp", 1)
     first = me_dp == 0
     lag_sum = jnp.concatenate([jnp.where(first, mine, theirs), jnp.where(first, theirs, mine)], axis=0)

time: 120 us -> 117 us (0.975)
  starting transfers between devices: 42.9 us -> 40 us
  waiting for transfers between devices: 27.9 us -> 29.2 us
    ppermute x4, starting transfers between devices: 10.7 us -> 4.4 us  [ring_step(): ring_pieces.append(lax.ppermute(ring_pieces[-2], 'seq', ring))]
    ppermute x4, waiting for transfers between devices: 7.44 us -> 13 us  [ring_step(): ring_pieces.append(lax.ppermute(ring_pieces[-2], 'seq', ring))]
    ppermute x1, starting transfers between devices: 1.07 us -> 6.23 us  [per_device(): across = lax.ppermute(moved, 'tp', opposite)]
    ppermute x8, waiting for transfers between devices: 16.3 us -> 11.3 us  [swap_pairs(): return lax.ppermute(value, axis, [(i, i ^ distance) for i in range(count)])]
  transfers between devices with their start and end apart: 27 -> 27, of which waited for: 11 -> 10; matrix products, arithmetic and copies ran while one was open for 6% -> 5% of each run, Pallas kernels for 29% -> 30%
where the time goes in v17:
time: 117 us
  starting transfers between devices  40 us (34%)
  Pallas kernels  34.9 us (30%)
  waiting for transfers between devices  29.2 us (25%)
  other arithmetic  6.39 us (5%)
  local copies, waits for them, and re-layouts  5.44 us (5%)
    pallas_call x3, Pallas kernels, by_channel(): pl.pallas_call(kernel, in_specs=[pl.BlockSpec(memory_space=pltpu.SMEM)] *...  16.9 us
    pallas_call x2, Pallas kernels, local_call(): pl.pallas_call(kernel, in_specs=[pl.BlockSpec(memory_space=pltpu.SMEM)] +...  13.8 us
    ppermute x4, waiting for transfers between devices, ring_step(): ring_pieces.append(lax.ppermute(ring_pieces[-2], 'seq', ring))  13 us
    ppermute x8, starting transfers between devices, swap_pairs(): return lax.ppermute(value, axis, [(i, i ^ distance) for i in range(count)])  11.7 us
    ppermute x8, waiting for transfers between devices, swap_pairs(): return lax.ppermute(value, axis, [(i, i ^ distance) for i in range(count)])  11.3 us
    ppermute x1, starting transfers between devices, per_device(): prior = lax.ppermute(tail, 'seq', [(i, i + 1) for i in range(n_seq - 1)])  7.09 us
    ppermute x1, starting transfers between devices, per_device(): across = lax.ppermute(moved, 'tp', opposite)  6.23 us
    ppermute x4, starting transfers between devices, ring_step(): ring_pieces.append(lax.ppermute(ring_pieces[-2], 'seq', ring))  4.4 us
  transfers between devices with their start and end apart: 27, of which 10 were waited for; matrix products, arithmetic and copies ran while one was open for 5% of the time, Pallas kernels for 30%

profile of v17, /device:TPU:0, one launch (start us, length us, event | category | flops | bytes accessed | tf_op | source)
XLA Modules:
  0.0 116.9 jit_solution(6514966582901591315)
XLA Ops:
  0.6 1.1 fusion.2
  2.4 7.1 %collective-permute-start = (bf16[128,1024]{1,0:T(8,128)(2,1)S(1)}, bf16[128,1024]{1,0:T(8,128)(2,1)S(1)}, u32[]{:S(2)}, u32[]{:S(2)}) collective-permute-start(bf16[128,1024]{1,0:T(8,128)(2,1)S(1)} %fusion.2), channel_id=1, source_target_pairs={{0,8},{8,16},{16,24},{1,9},{9,17},{17,25},{2,10},{10,18},{18,26},{... | collective-permute-start | bytes 786440 | tf_op jit(solution)/shard_map/ppermute | solution.py:419
  9.5 1.7 %collective-permute-start.6 = (bf16[256,1024]{1,0:T(8,128)(2,1)}, bf16[256,1024]{1,0:T(8,128)(2,1)S(1)}, u32[]{:S(2)}, u32[]{:S(2)}) collective-permute-start(bf16[256,1024]{1,0:T(8,128)(2,1)} %bitcast.32), channel_id=1, source_target_pairs={{0,0},{1,4},{2,2},{3,6},{4,1},{5,5},{6,3},{7,7},{8,8},{9,12},{10,1... | collective-permute-start | bytes 1572872 | tf_op jit(solution)/shard_map/ppermute | solution.py:428
  11.2 2.8 %collective-permute-done.refs_3_.refs_6_ = bf16[128,1024]{1,0:T(8,128)(2,1)S(1)} collective-permute-done((bf16[128,1024]{1,0:T(8,128)(2,1)S(1)}, bf16[128,1024]{1,0:T(8,128)(2,1)S(1)}, u32[]{:S(2)}, u32[]{:S(2)}) %collective-permute-start) | collective-permute-done | bytes 262176 | tf_op jit(solution)/shard_map/ppermute | solution.py:419
  14.7 1.1 broadcast_select_fusion
  19.0 5.5 %shard_map.145 = (f32[256,1024]{1,0:T(8,128)}, bf16[256,512]{1,0:T(8,128)(2,1)}, bf16[256,512]{1,0:T(8,128)(2,1)}) custom-call(s32[1]{0:T(128)} %bitcast.refs_0_, bf16[768,384]{1,0:T(8,128)(2,1)} %constant.66.clone.refs_1_.refs_0_, bf16[768,384]{1,0:T(8,128)(2,1)} %constant.67.clone.refs_2_.refs_1_, bf16[128,1024]{1,0:T(8,128)(2,1)} %copy-done.5, ...), custom_call_target="tpu_custom_call" | custom-call | flops 22020096 | bytes 57408 | tf_op jit(solution)/shard_map/pallas_call | solution.py:281
  24.5 1.5 %collective-permute-start.1 = (bf16[256,512]{1,0:T(8,128)(2,1)}, bf16[256,512]{1,0:T(8,128)(2,1)S(1)}, u32[]{:S(2)}, u32[]{:S(2)}) collective-permute-start(bf16[256,512]{1,0:T(8,128)(2,1)} %get-tuple-element.58), channel_id=1, source_target_pairs={{0,1},{1,0},{2,3},{3,2},{4,5},{5,4},{6,7},{7,6},{8,9},{9,8},{10,11... | collective-permute-start | bytes 786440 | tf_op jit(solution)/shard_map/ppermute | solution.py:384
  26.0 1.3 %collective-permute-done.7.second_mine = bf16[256,1024]{1,0:T(8,128)(2,1)S(1)} collective-permute-done((bf16[256,1024]{1,0:T(8,128)(2,1)}, bf16[256,1024]{1,0:T(8,128)(2,1)S(1)}, u32[]{:S(2)}, u32[]{:S(2)}) %collective-permute-start.7) | collective-permute-done | bytes 524320 | tf_op jit(solution)/shard_map/ppermute | solution.py:428
  27.3 3.1 %collective-permute-start.8 = (bf16[256,1024]{1,0:T(8,128)(2,1)S(1)}, bf16[256,1024]{1,0:T(8,128)(2,1)S(1)}, u32[]{:S(2)}, u32[]{:S(2)}) collective-permute-start(bf16[256,1024]{1,0:T(8,128)(2,1)S(1)} %collective-permute-done.6.first_mine), channel_id=1, source_target_pairs={{0,2},{1,3},{2,0},{3,1},{4,6},{5,7},{6,4},{7,5},{8,10},{9,11},{10,... | collective-permute-start | bytes 1572872 | tf_op jit(solution)/shard_map/ppermute | solution.py:495
  31.2 1.4 %collective-permute-start.10 = (bf16[256,1024]{1,0:T(8,128)(2,1)S(1)}, bf16[256,1024]{1,0:T(8,128)(2,1)S(1)}, u32[]{:S(2)}, u32[]{:S(2)}) collective-permute-start(bf16[256,1024]{1,0:T(8,128)(2,1)S(1)} %collective-permute-done.3.rows_in), channel_id=1, source_target_pairs={{0,1},{1,0},{2,3},{3,2},{4,5},{5,4},{6,7},{7,6},{8,9},{9,8},{10,11... | collective-permute-start | bytes 1572872 | tf_op jit(solution)/shard_map/ppermute | solution.py:384
  32.7 2.0 %shard_map.146.refs_0_ = bf16[1024,256]{1,0:T(8,128)(2,1)} custom-call(bf16[256,1024]{1,0:T(8,128)(2,1)} %copy-done.18), custom_call_target="tpu_custom_call" | custom-call | bytes 16384 | tf_op jit(solution)/shard_map/pallas_call | solution.py:367
  34.7 6.2 %collective-permute-start.18 = (bf16[1024,256]{1,0:T(8,128)(2,1)}, bf16[1024,256]{1,0:T(8,128)(2,1)S(1)}, u32[]{:S(2)}, u32[]{:S(2)}) collective-permute-start(bf16[1024,256]{1,0:T(8,128)(2,1)} %shard_map.146.refs_0_), channel_id=1, source_target_pairs={{0,4},{2,6},{4,0},{6,2},{1,5},{3,7},{5,1},{7,3},{8,12},{10,14},{12... | collective-permute-start | bytes 1572872 | tf_op jit(solution)/shard_map/ppermute | solution.py:519
  40.9 1.4 %collective-permute-start.4 = (bf16[256,512]{1,0:T(8,128)(2,1)}, bf16[256,512]{1,0:T(8,128)(2,1)S(1)}, u32[]{:S(2)}, u32[]{:S(2)}) collective-permute-start(bf16[256,512]{1,0:T(8,128)(2,1)} %get-tuple-element.60.refs_8_), channel_id=1, source_target_pairs={{0,16},{16,24},{24,8},{8,0},{1,17},{17,25},{25,9},{9,1},{2,18},{18... | collective-permute-start | bytes 786440 | tf_op jit(solution)/shard_map/ppermute | solution.py:489
  42.4 1.4 %collective-permute-start.5 = (bf16[256,512]{1,0:T(8,128)(2,1)S(1)}, bf16[256,512]{1,0:T(8,128)(2,1)S(1)}, u32[]{:S(2)}, u32[]{:S(2)}) collective-permute-start(bf16[256,512]{1,0:T(8,128)(2,1)S(1)} %collective-permute-done.1.refs_9_), channel_id=1, source_target_pairs={{0,16},{16,24},{24,8},{8,0},{1,17},{17,25},{25,9},{9,1},{2,18},{18... | collective-permute-start | bytes 786440 | tf_op jit(solution)/shard_map/ppermute | solution.py:489
  44.6 6.4 %shard_map.147 = (bf16[256,1024]{1,0:T(8,128)(2,1)}, f32[256,1024]{1,0:T(8,128)}) custom-call(s32[3]{0:T(128)} %pad_add_fusion.place_ref, bf16[256,1024]{1,0:T(8,128)(2,1)} %copy-done.6, bf16[256,1024]{1,0:T(8,128)(2,1)} %copy-done.7, bf16[256,1024]{1,0:T(8,128)(2,1)} %copy-done.16, bf16[256,1024]{1,0:T(8,128)(2,1)} %copy-done.17, bf16[1024,2048]{1,0:T(8,128)(2,1)} %weight.1), custom_call_target="tpu_custom_call" | custom-call | flops 33554432 | bytes 122880 | tf_op jit(solution)/shard_map/pallas_call | solution.py:301
  51.0 1.6 %collective-permute-start.13 = (bf16[256,1024]{1,0:T(8,128)(2,1)}, bf16[256,1024]{1,0:T(8,128)(2,1)S(1)}, u32[]{:S(2)}, u32[]{:S(2)}) collective-permute-start(bf16[256,1024]{1,0:T(8,128)(2,1)} %get-tuple-element.70), channel_id=1, source_target_pairs={{0,1},{1,0},{2,3},{3,2},{4,5},{5,4},{6,7},{7,6},{8,9},{9,8},{10,11... | collective-permute-start | bytes 1572872 | tf_op jit(solution)/shard_map/ppermute | solution.py:384
  52.6 3.2 %collective-permute-done.5.refs_11_ = bf16[256,512]{1,0:T(8,128)(2,1)S(1)} collective-permute-done((bf16[256,512]{1,0:T(8,128)(2,1)S(1)}, bf16[256,512]{1,0:T(8,128)(2,1)S(1)}, u32[]{:S(2)}, u32[]{:S(2)}) %collective-permute-start.5) | collective-permute-done | bytes 262176 | tf_op jit(solution)/shard_map/ppermute | solution.py:489
  55.8 1.5 %collective-permute-start.11 = (bf16[256,512]{1,0:T(8,128)(2,1)S(1)}, bf16[256,512]{1,0:T(8,128)(2,1)S(1)}, u32[]{:S(2)}, u32[]{:S(2)}) collective-permute-start(bf16[256,512]{1,0:T(8,128)(2,1)S(1)} %collective-permute-done.4.refs_10_), channel_id=1, source_target_pairs={{0,16},{16,24},{24,8},{8,0},{1,17},{17,25},{25,9},{9,1},{2,18},{18... | collective-permute-start | bytes 786440 | tf_op jit(solution)/shard_map/ppermute | solution.py:489
  57.3 2.2 %shard_map.149.refs_4_ = bf16[1024,256]{1,0:T(8,128)(2,1)} custom-call(bf16[256,1024]{1,0:T(8,128)(2,1)} %copy-done.19), custom_call_target="tpu_custom_call" | custom-call | bytes 16384 | tf_op jit(solution)/shard_map/pallas_call | solution.py:367
  60.0 4.9 %collective-permute-done.11.refs_12_ = bf16[256,512]{1,0:T(8,128)(2,1)S(1)} collective-permute-done((bf16[256,512]{1,0:T(8,128)(2,1)S(1)}, bf16[256,512]{1,0:T(8,128)(2,1)S(1)}, u32[]{:S(2)}, u32[]{:S(2)}) %collective-permute-start.11) | collective-permute-done | bytes 262176 | tf_op jit(solution)/shard_map/ppermute | solution.py:489
  64.9 5.0 %collective-permute-done.12.refs_13_ = bf16[256,512]{1,0:T(8,128)(2,1)S(1)} collective-permute-done((bf16[256,512]{1,0:T(8,128)(2,1)S(1)}, bf16[256,512]{1,0:T(8,128)(2,1)S(1)}, u32[]{:S(2)}, u32[]{:S(2)}) %collective-permute-start.12) | collective-permute-done | bytes 262176 | tf_op jit(solution)/shard_map/ppermute | solution.py:489
  70.0 1.3 %collective-permute-start.14 = (bf16[2,256,512]{2,1,0:T(8,128)(2,1)S(1)}, bf16[2,256,512]{2,1,0:T(8,128)(2,1)S(1)}, u32[]{:S(2)}, u32[]{:S(2)}) collective-permute-start(bf16[2,256,512]{2,1,0:T(8,128)(2,1)S(1)} %pad_maximum_fusion.1), channel_id=1, source_target_pairs={{0,16},{16,24},{24,8},{8,0},{1,17},{17,25},{25,9},{9,1},{2,18},{18... | collective-permute-start | bytes 1572872 | tf_op jit(solution)/shard_map/ppermute | solution.py:523
  71.3 5.9 %shard_map.148 = (bf16[256,1024]{1,0:T(8,128)(2,1)}, bf16[256,1024]{1,0:T(8,128)(2,1)}, bf16[128,1024]{1,0:T(8,128)(2,1)}, bf16[64,1024]{1,0:T(8,128)(2,1)}, f32[64,1024]{1,0:T(8,128)}) custom-call(bf16[768,384]{1,0:T(8,128)(2,1)} %constant.66.clone.refs_1_.refs_0_, bf16[768,384]{1,0:T(8,128)(2,1)} %constant.67.clone.refs_2_.refs_1_, ...), custom_call_target="tpu_custom_call" | custom-call | flops 20447232 | bytes 96320 | tf_op jit(solution)/shard_map/pallas_call | solution.py:281
  78.8 3.6 %collective-permute-done.15 = bf16[64,1024]{1,0:T(8,128)(2,1)S(1)} collective-permute-done((bf16[64,1024]{1,0:T(8,128)(2,1)}, bf16[64,1024]{1,0:T(8,128)(2,1)S(1)}, u32[]{:S(2)}, u32[]{:S(2)}) %collective-permute-start.15) | collective-permute-done | bytes 131104 | tf_op jit(solution)/shard_map/ppermute | solution.py:384
  83.3 1.3 %collective-permute-start.24 = (bf16[128,1024]{1,0:T(8,128)(2,1)}, bf16[128,1024]{1,0:T(8,128)(2,1)S(1)}, u32[]{:S(2)}, u32[]{:S(2)}) collective-permute-start(bf16[128,1024]{1,0:T(8,128)(2,1)} %get-tuple-element.96), channel_id=1, source_target_pairs={{8,0},{16,8},{24,16},{9,1},{17,9},{25,17},{10,2},{18,10},{26,18},{... | collective-permute-start | bytes 786440 | tf_op jit(solution)/shard_map/ppermute | solution.py:556
  85.6 2.7 %collective-permute-start.16 = (bf16[64,1024]{1,0:T(8,128)(2,1)S(1)}, bf16[64,1024]{1,0:T(8,128)(2,1)S(1)}, u32[]{:S(2)}, u32[]{:S(2)}) collective-permute-start(bf16[64,1024]{1,0:T(8,128)(2,1)S(1)} %add_convert_fusion.2), channel_id=1, source_target_pairs={{0,8},{8,0},{16,24},{24,16},{1,9},{9,1},{17,25},{25,17},{2,10},{10... | collective-permute-start | bytes 393224 | tf_op jit(solution)/shard_map/ppermute | solution.py:384
  90.1 7.4 %shard_map.150 = (bf16[512,512]{1,0:T(8,128)(2,1)}, f32[512,512]{1,0:T(8,128)}) custom-call(s32[5]{0:T(128)} %pad_add_fusion.1.place_ref, bf16[1024,256]{1,0:T(8,128)(2,1)} %shard_map.146.refs_0_, bf16[1024,256]{1,0:T(8,128)(2,1)} %copy-done.11, bf16[1024,256]{1,0:T(8,128)(2,1)} %copy-done.8, bf16[1024,256]{1,0:T(8,128)(2,1)} %copy-done.13, ...), custom_call_target="tpu_custom_call" | custom-call | flops 33554432 | bytes 122880 | tf_op jit(solution)/shard_map/pallas_call | solution.py:301
  98.6 1.3 %collective-permute-start.23 = (bf16[64,1024]{1,0:T(8,128)(2,1)S(1)}, bf16[64,1024]{1,0:T(8,128)(2,1)S(1)}, u32[]{:S(2)}, u32[]{:S(2)}) collective-permute-start(bf16[64,1024]{1,0:T(8,128)(2,1)S(1)} %add_convert_fusion.1), channel_id=1, source_target_pairs={{0,16},{8,24},{16,0},{24,8},{1,17},{9,25},{17,1},{25,9},{2,18},{10... | collective-permute-start | bytes 393224 | tf_op jit(solution)/shard_map/ppermute | solution.py:384
  99.9 5.5 %shard_map.151 = (bf16[256,1024]{1,0:T(8,128)(2,1)}, bf16[256,1024]{1,0:T(8,128)(2,1)}) custom-call(bf16[768,384]{1,0:T(8,128)(2,1)} %constant.66.clone.refs_1_.refs_0_, bf16[768,384]{1,0:T(8,128)(2,1)} %constant.67.clone.refs_2_.refs_1_, bf16[256,1024]{1,0:T(8,128)(2,1)} %get-tuple-element.95.refs_2_, bf16[128,1024]{1,0:T(8,128)(2,1)} %copy-done.23, ...), custom_call_target="tpu_custom_call" | custom-call | flops 5637144576 | bytes 49216 | tf_op jit(solution)/shard_map/pallas_call | solution.py:281
  106.3 1.2 %collective-permute-start.25 = (bf16[64,1024]{1,0:T(8,128)(2,1)S(1)}, bf16[64,1024]{1,0:T(8,128)(2,1)S(1)}, u32[]{:S(2)}, u32[]{:S(2)}) collective-permute-start(bf16[64,1024]{1,0:T(8,128)(2,1)S(1)} %add_convert_fusion), channel_id=1, source_target_pairs={{0,1},{1,0},{2,3},{3,2},{4,5},{5,4},{6,7},{7,6},{8,9},{9,8},{10,11... | collective-permute-start | bytes 393224 | tf_op jit(solution)/shard_map/ppermute | solution.py:384
  107.5 6.0 %collective-permute-done.25 = bf16[64,1024]{1,0:T(8,128)(2,1)S(1)} collective-permute-done((bf16[64,1024]{1,0:T(8,128)(2,1)S(1)}, bf16[64,1024]{1,0:T(8,128)(2,1)S(1)}, u32[]{:S(2)}, u32[]{:S(2)}) %collective-permute-start.25) | collective-permute-done | bytes 131104 | tf_op jit(solution)/shard_map/ppermute | solution.py:384
  115.5 1.5 %pad_maximum_fusion = f32[512,1024]{1,0:T(8,128)} fusion(f32[512,512]{1,0:T(8,128)S(1)} %get-tuple-element.111, f32[512,512]{1,0:T(8,128)S(1)} %get-tuple-element.110), kind=kLoop, calls=%fused_computation | loop fusion | flops 524288 | bytes 4194304 | tf_op jit(solution)/shard_map/concatenate | solution.py:597
  (93 shorter events, 16.0 us)
Async XLA Ops:
  1.7 12.9 %collective-permute-start.2 = (bf16[256,1024]{1,0:T(8,128)(2,1)}, bf16[256,1024]{1,0:T(8,128)(2,1)S(1)}, u32[]{:S(2)}, u32[]{:S(2)}) collective-permute-start(bf16[256,1024]{1,0:T(8,128)(2,1)} %bitcast.31), channel_id=1, source_target_pairs={{2,4},{4,2},{8,14},{14,8},{18,20},{20,18},{24,30},{30,24},{3,5},{5... | collective-permute-start | bytes 1572872 | tf_op jit(solution)/shard_map/ppermute | solution.py:441
  2.4 11.6 %collective-permute-start = (bf16[128,1024]{1,0:T(8,128)(2,1)S(1)}, bf16[128,1024]{1,0:T(8,128)(2,1)S(1)}, u32[]{:S(2)}, u32[]{:S(2)}) collective-permute-start(bf16[128,1024]{1,0:T(8,128)(2,1)S(1)} %fusion.2), channel_id=1, source_target_pairs={{0,8},{8,16},{16,24},{1,9},{9,17},{17,25},{2,10},{10,18},{18,26},{... | collective-permute-start | bytes 786440 | tf_op jit(solution)/shard_map/ppermute | solution.py:419
  9.5 16.5 %collective-permute-start.6 = (bf16[256,1024]{1,0:T(8,128)(2,1)}, bf16[256,1024]{1,0:T(8,128)(2,1)S(1)}, u32[]{:S(2)}, u32[]{:S(2)}) collective-permute-start(bf16[256,1024]{1,0:T(8,128)(2,1)} %bitcast.32), channel_id=1, source_target_pairs={{0,0},{1,4},{2,2},{3,6},{4,1},{5,5},{6,3},{7,7},{8,8},{9,12},{10,1... | collective-permute-start | bytes 1572872 | tf_op jit(solution)/shard_map/ppermute | solution.py:428
  14.0 13.3 %collective-permute-start.7 = (bf16[256,1024]{1,0:T(8,128)(2,1)}, bf16[256,1024]{1,0:T(8,128)(2,1)S(1)}, u32[]{:S(2)}, u32[]{:S(2)}) collective-permute-start(bf16[256,1024]{1,0:T(8,128)(2,1)} %bitcast.33), channel_id=1, source_target_pairs={{0,4},{1,0},{2,6},{3,2},{4,5},{5,1},{6,7},{7,3},{8,12},{9,8},{10,1... | collective-permute-start | bytes 1572872 | tf_op jit(solution)/shard_map/ppermute | solution.py:428
  15.8 15.4 %collective-permute-start.3 = (bf16[256,1024]{1,0:T(8,128)(2,1)S(1)}, bf16[256,1024]{1,0:T(8,128)(2,1)S(1)}, u32[]{:S(2)}, u32[]{:S(2)}) collective-permute-start(bf16[256,1024]{1,0:T(8,128)(2,1)S(1)} %broadcast_select_fusion), channel_id=1, source_target_pairs={{0,0},{2,16},{4,12},{6,28},{8,24},{10,8},{12,20},{14,4},{16,2},{18... | collective-permute-start | bytes 1572872 | tf_op jit(solution)/shard_map/ppermute | solution.py:453
  24.5 6.6 %collective-permute-start.1 = (bf16[256,512]{1,0:T(8,128)(2,1)}, bf16[256,512]{1,0:T(8,128)(2,1)S(1)}, u32[]{:S(2)}, u32[]{:S(2)}) collective-permute-start(bf16[256,512]{1,0:T(8,128)(2,1)} %get-tuple-element.58), channel_id=1, source_target_pairs={{0,1},{1,0},{2,3},{3,2},{4,5},{5,4},{6,7},{7,6},{8,9},{9,8},{10,11... | collective-permute-start | bytes 786440 | tf_op jit(solution)/shard_map/ppermute | solution.py:384
  26.0 17.8 %copy-start.6 = (bf16[256,1024]{1,0:T(8,128)(2,1)}, bf16[256,1024]{1,0:T(8,128)(2,1)S(1)}, u32[]{:S(2)}) copy-start(bf16[256,1024]{1,0:T(8,128)(2,1)S(1)} %collective-permute-done.6.first_mine) | copy-start | bytes 1572868
  27.3 15.1 %collective-permute-start.8 = (bf16[256,1024]{1,0:T(8,128)(2,1)S(1)}, bf16[256,1024]{1,0:T(8,128)(2,1)S(1)}, u32[]{:S(2)}, u32[]{:S(2)}) collective-permute-start(bf16[256,1024]{1,0:T(8,128)(2,1)S(1)} %collective-permute-done.6.first_mine), channel_id=1, source_target_pairs={{0,2},{1,3},{2,0},{3,1},{4,6},{5,7},{6,4},{7,5},{8,10},{9,11},{10,... | collective-permute-start | bytes 1572872 | tf_op jit(solution)/shard_map/ppermute | solution.py:495
  30.4 13.5 %collective-permute-start.9 = (bf16[256,1024]{1,0:T(8,128)(2,1)S(1)}, bf16[256,1024]{1,0:T(8,128)(2,1)S(1)}, u32[]{:S(2)}, u32[]{:S(2)}) collective-permute-start(bf16[256,1024]{1,0:T(8,128)(2,1)S(1)} %collective-permute-done.7.second_mine), channel_id=1, source_target_pairs={{0,2},{1,3},{2,0},{3,1},{4,6},{5,7},{6,4},{7,5},{8,10},{9,11},{10,... | collective-permute-start | bytes 1572872 | tf_op jit(solution)/shard_map/ppermute | solution.py:495
  31.2 46.0 %copy-start.20 = (bf16[256,512]{1,0:T(8,128)(2,1)}, bf16[256,512]{1,0:T(8,128)(2,1)S(1)}, u32[]{:S(2)}) copy-start(bf16[256,512]{1,0:T(8,128)(2,1)S(1)} %collective-permute-done.1.refs_9_) | copy-start | bytes 786436
  31.2 19.8 %collective-permute-start.10 = (bf16[256,1024]{1,0:T(8,128)(2,1)S(1)}, bf16[256,1024]{1,0:T(8,128)(2,1)S(1)}, u32[]{:S(2)}, u32[]{:S(2)}) collective-permute-start(bf16[256,1024]{1,0:T(8,128)(2,1)S(1)} %collective-permute-done.3.rows_in), channel_id=1, source_target_pairs={{0,1},{1,0},{2,3},{3,2},{4,5},{5,4},{6,7},{7,6},{8,9},{9,8},{10,11... | collective-permute-start | bytes 1572872 | tf_op jit(solution)/shard_map/ppermute | solution.py:384
  34.7 22.6 %collective-permute-start.18 = (bf16[1024,256]{1,0:T(8,128)(2,1)}, bf16[1024,256]{1,0:T(8,128)(2,1)S(1)}, u32[]{:S(2)}, u32[]{:S(2)}) collective-permute-start(bf16[1024,256]{1,0:T(8,128)(2,1)} %shard_map.146.refs_0_), channel_id=1, source_target_pairs={{0,4},{2,6},{4,0},{6,2},{1,5},{3,7},{5,1},{7,3},{8,12},{10,14},{12... | collective-permute-start | bytes 1572872 | tf_op jit(solution)/shard_map/ppermute | solution.py:519
  40.9 11.7 %collective-permute-start.4 = (bf16[256,512]{1,0:T(8,128)(2,1)}, bf16[256,512]{1,0:T(8,128)(2,1)S(1)}, u32[]{:S(2)}, u32[]{:S(2)}) collective-permute-start(bf16[256,512]{1,0:T(8,128)(2,1)} %get-tuple-element.60.refs_8_), channel_id=1, source_target_pairs={{0,16},{16,24},{24,8},{8,0},{1,17},{17,25},{25,9},{9,1},{2,18},{18... | collective-permute-start | bytes 786440 | tf_op jit(solution)/shard_map/ppermute | solution.py:489
  42.4 13.4 %collective-permute-start.5 = (bf16[256,512]{1,0:T(8,128)(2,1)S(1)}, bf16[256,512]{1,0:T(8,128)(2,1)S(1)}, u32[]{:S(2)}, u32[]{:S(2)}) collective-permute-start(bf16[256,512]{1,0:T(8,128)(2,1)S(1)} %collective-permute-done.1.refs_9_), channel_id=1, source_target_pairs={{0,16},{16,24},{24,8},{8,0},{1,17},{17,25},{25,9},{9,1},{2,18},{18... | collective-permute-start | bytes 786440 | tf_op jit(solution)/shard_map/ppermute | solution.py:489
  51.0 18.9 %collective-permute-start.13 = (bf16[256,1024]{1,0:T(8,128)(2,1)}, bf16[256,1024]{1,0:T(8,128)(2,1)S(1)}, u32[]{:S(2)}, u32[]{:S(2)}) collective-permute-start(bf16[256,1024]{1,0:T(8,128)(2,1)} %get-tuple-element.70), channel_id=1, source_target_pairs={{0,1},{1,0},{2,3},{3,2},{4,5},{5,4},{6,7},{7,6},{8,9},{9,8},{10,11... | collective-permute-start | bytes 1572872 | tf_op jit(solution)/shard_map/ppermute | solution.py:384
  52.6 24.6 %copy-start.21 = (bf16[256,512]{1,0:T(8,128)(2,1)}, bf16[256,512]{1,0:T(8,128)(2,1)S(1)}, u32[]{:S(2)}) copy-start(bf16[256,512]{1,0:T(8,128)(2,1)S(1)} %collective-permute-done.4.refs_10_) | copy-start | bytes 786436
  55.8 21.4 %copy-start.22 = (bf16[256,512]{1,0:T(8,128)(2,1)}, bf16[256,512]{1,0:T(8,128)(2,1)S(1)}, u32[]{:S(2)}) copy-start(bf16[256,512]{1,0:T(8,128)(2,1)S(1)} %collective-permute-done.5.refs_11_) | copy-start | bytes 786436
  55.8 9.1 %collective-permute-start.11 = (bf16[256,512]{1,0:T(8,128)(2,1)S(1)}, bf16[256,512]{1,0:T(8,128)(2,1)S(1)}, u32[]{:S(2)}, u32[]{:S(2)}) collective-permute-start(bf16[256,512]{1,0:T(8,128)(2,1)S(1)} %collective-permute-done.4.refs_10_), channel_id=1, source_target_pairs={{0,16},{16,24},{24,8},{8,0},{1,17},{17,25},{25,9},{9,1},{2,18},{18... | collective-permute-start | bytes 786440 | tf_op jit(solution)/shard_map/ppermute | solution.py:489
  57.3 12.6 %collective-permute-start.12 = (bf16[256,512]{1,0:T(8,128)(2,1)S(1)}, bf16[256,512]{1,0:T(8,128)(2,1)S(1)}, u32[]{:S(2)}, u32[]{:S(2)}) collective-permute-start(bf16[256,512]{1,0:T(8,128)(2,1)S(1)} %collective-permute-done.5.refs_11_), channel_id=1, source_target_pairs={{0,16},{16,24},{24,8},{8,0},{1,17},{17,25},{25,9},{9,1},{2,18},{18... | collective-permute-start | bytes 786440 | tf_op jit(solution)/shard_map/ppermute | solution.py:489
  57.3 21.4 %copy-start.8 = (bf16[1024,256]{1,0:T(8,128)(2,1)}, bf16[1024,256]{1,0:T(8,128)(2,1)S(1)}, u32[]{:S(2)}) copy-start(bf16[1024,256]{1,0:T(8,128)(2,1)S(1)} %collective-permute-done.18.refs_2_) | copy-start | bytes 1572868
  59.6 19.1 %collective-permute-start.21 = (bf16[1024,256]{1,0:T(8,128)(2,1)}, bf16[1024,256]{1,0:T(8,128)(2,1)S(1)}, u32[]{:S(2)}, u32[]{:S(2)}) collective-permute-start(bf16[1024,256]{1,0:T(8,128)(2,1)} %shard_map.149.refs_4_), channel_id=1, source_target_pairs={{0,4},{2,6},{4,0},{6,2},{1,5},{3,7},{5,1},{7,3},{8,12},{10,14},{12... | collective-permute-start | bytes 1572872 | tf_op jit(solution)/shard_map/ppermute | solution.py:525
  70.0 13.3 %collective-permute-start.14 = (bf16[2,256,512]{2,1,0:T(8,128)(2,1)S(1)}, bf16[2,256,512]{2,1,0:T(8,128)(2,1)S(1)}, u32[]{:S(2)}, u32[]{:S(2)}) collective-permute-start(bf16[2,256,512]{2,1,0:T(8,128)(2,1)S(1)} %pad_maximum_fusion.1), channel_id=1, source_target_pairs={{0,16},{16,24},{24,8},{8,0},{1,17},{17,25},{25,9},{9,1},{2,18},{18... | collective-permute-start | bytes 1572872 | tf_op jit(solution)/shard_map/ppermute | solution.py:523
  77.2 5.2 %collective-permute-start.15 = (bf16[64,1024]{1,0:T(8,128)(2,1)}, bf16[64,1024]{1,0:T(8,128)(2,1)S(1)}, u32[]{:S(2)}, u32[]{:S(2)}) collective-permute-start(bf16[64,1024]{1,0:T(8,128)(2,1)} %get-tuple-element.83), channel_id=1, source_target_pairs={{0,1},{1,0},{2,3},{3,2},{4,5},{5,4},{6,7},{7,6},{8,9},{9,8},{10,11... | collective-permute-start | bytes 393224 | tf_op jit(solution)/shard_map/ppermute | solution.py:384
  78.2 7.4 %collective-permute-start.17 = (bf16[1024,256]{1,0:T(8,128)(2,1)S(1)}, bf16[1024,256]{1,0:T(8,128)(2,1)S(1)}, u32[]{:S(2)}, u32[]{:S(2)}) collective-permute-start(bf16[1024,256]{1,0:T(8,128)(2,1)S(1)} %copy-done), channel_id=1, source_target_pairs={{0,2},{2,0},{4,6},{6,4},{1,3},{3,1},{5,7},{7,5},{8,10},{10,8},{12,... | collective-permute-start | bytes 1572872 | tf_op jit(solution)/shard_map/ppermute | solution.py:513
  78.2 10.1 %collective-permute-start.20 = (bf16[1024,256]{1,0:T(8,128)(2,1)S(1)}, bf16[1024,256]{1,0:T(8,128)(2,1)S(1)}, u32[]{:S(2)}, u32[]{:S(2)}) collective-permute-start(bf16[1024,256]{1,0:T(8,128)(2,1)S(1)} %copy-done.1), channel_id=1, source_target_pairs={{0,2},{2,0},{4,6},{6,4},{1,3},{3,1},{5,7},{7,5},{8,10},{10,8},{12,... | collective-permute-start | bytes 1572872 | tf_op jit(solution)/shard_map/ppermute | solution.py:513
  78.7 9.6 %collective-permute-start.19 = (bf16[1024,256]{1,0:T(8,128)(2,1)S(1)}, bf16[1024,256]{1,0:T(8,128)(2,1)S(1)}, u32[]{:S(2)}, u32[]{:S(2)}) collective-permute-start(bf16[1024,256]{1,0:T(8,128)(2,1)S(1)} %collective-permute-done.18.refs_2_), channel_id=1, source_target_pairs={{0,2},{2,0},{4,6},{6,4},{1,3},{3,1},{5,7},{7,5},{8,10},{10,8},{12,... | collective-permute-start | bytes 1572872 | tf_op jit(solution)/shard_map/ppermute | solution.py:515
  82.5 5.9 %collective-permute-start.22 = (bf16[1024,256]{1,0:T(8,128)(2,1)S(1)}, bf16[1024,256]{1,0:T(8,128)(2,1)S(1)}, u32[]{:S(2)}, u32[]{:S(2)}) collective-permute-start(bf16[1024,256]{1,0:T(8,128)(2,1)S(1)} %collective-permute-done.21.refs_6_), channel_id=1, source_target_pairs={{0,2},{2,0},{4,6},{6,4},{1,3},{3,1},{5,7},{7,5},{8,10},{10,8},{12,... | collective-permute-start | bytes 1572872 | tf_op jit(solution)/shard_map/ppermute | solution.py:515
  83.3 15.2 %collective-permute-start.24 = (bf16[128,1024]{1,0:T(8,128)(2,1)}, bf16[128,1024]{1,0:T(8,128)(2,1)S(1)}, u32[]{:S(2)}, u32[]{:S(2)}) collective-permute-start(bf16[128,1024]{1,0:T(8,128)(2,1)} %get-tuple-element.96), channel_id=1, source_target_pairs={{8,0},{16,8},{24,16},{9,1},{17,9},{25,17},{10,2},{18,10},{26,18},{... | collective-permute-start | bytes 786440 | tf_op jit(solution)/shard_map/ppermute | solution.py:556
  85.6 13.0 %collective-permute-start.16 = (bf16[64,1024]{1,0:T(8,128)(2,1)S(1)}, bf16[64,1024]{1,0:T(8,128)(2,1)S(1)}, u32[]{:S(2)}, u32[]{:S(2)}) collective-permute-start(bf16[64,1024]{1,0:T(8,128)(2,1)S(1)} %add_convert_fusion.2), channel_id=1, source_target_pairs={{0,8},{8,0},{16,24},{24,16},{1,9},{9,1},{17,25},{25,17},{2,10},{10... | collective-permute-start | bytes 393224 | tf_op jit(solution)/shard_map/ppermute | solution.py:384
  97.5 17.7 %collective-permute-start.26 = (bf16[512,512]{1,0:T(8,128)(2,1)}, bf16[512,512]{1,0:T(8,128)(2,1)S(1)}, u32[]{:S(2)}, u32[]{:S(2)}) collective-permute-start(bf16[512,512]{1,0:T(8,128)(2,1)} %get-tuple-element.103), channel_id=1, source_target_pairs={{0,1},{1,0},{2,3},{3,2},{4,5},{5,4},{6,7},{7,6},{8,9},{9,8},{10,11... | collective-permute-start | bytes 1572872 | tf_op jit(solution)/shard_map/ppermute | solution.py:384
  98.6 7.7 %collective-permute-start.23 = (bf16[64,1024]{1,0:T(8,128)(2,1)S(1)}, bf16[64,1024]{1,0:T(8,128)(2,1)S(1)}, u32[]{:S(2)}, u32[]{:S(2)}) collective-permute-start(bf16[64,1024]{1,0:T(8,128)(2,1)S(1)} %add_convert_fusion.1), channel_id=1, source_target_pairs={{0,16},{8,24},{16,0},{24,8},{1,17},{9,25},{17,1},{25,9},{2,18},{10... | collective-permute-start | bytes 393224 | tf_op jit(solution)/shard_map/ppermute | solution.py:384
  106.3 7.2 %collective-permute-start.25 = (bf16[64,1024]{1,0:T(8,128)(2,1)S(1)}, bf16[64,1024]{1,0:T(8,128)(2,1)S(1)}, u32[]{:S(2)}, u32[]{:S(2)}) collective-permute-start(bf16[64,1024]{1,0:T(8,128)(2,1)S(1)} %add_convert_fusion), channel_id=1, source_target_pairs={{0,1},{1,0},{2,3},{3,2},{4,5},{5,4},{6,7},{7,6},{8,9},{9,8},{10,11... | collective-permute-start | bytes 393224 | tf_op jit(solution)/shard_map/ppermute | solution.py:384
  (19 other events, 97.6 us)

commit v18 on v17

--- a/solution.py
+++ b/solution.py
@@ -482,7 +482,6 @@
     )
     if square:
         ring_pieces = [gated[0], swap_pairs(gated[1], "dp", 1)]
-        ring_pieces[0], ring_pieces[1], moved = lax.optimization_barrier((*ring_pieces, moved))
 
         def ring_step():
             for _ in range(2):
@@ -492,14 +491,14 @@
     gated[0], *rounds = lax.optimization_barrier((gated[0], *rounds))
 
     route = [(tp_dp(h, c, d), tp_dp(h, (c + 1) % subs, d)) for h, c, d in places]
+    if square:
+        rounds[1], moved, _ = lax.optimization_barrier((rounds[1], moved, ring_pieces[1]))
     theirs = [lax.ppermute(r, ("tp", "dp"), route) for r in rounds]
     firsts, seconds = zip(rounds, theirs)
     rows = n_tp * channels // (n_seq * n_dp)
     if square:
         moved = after(moved, *rounds)
         moved_other = swap_pairs(moved, "dp", 1)
-        moved = transposed(moved)
-        moved, place = lax.optimization_barrier((moved, place))
     other_sent, own_part = project(place, firsts, seconds, out_weight)
     if square:
         other_sent, moved_other = lax.optimization_barrier((other_sent, moved_other))
@@ -516,11 +515,12 @@
             ]
 
         opposite = [(t, t ^ subs) for t in range(n_tp)]
+        ring_pieces[2], ring_pieces[3], _ = lax.optimization_barrier((*ring_pieces[2:4], other_sent))
+        moved = transposed(after(moved, ring_pieces[2]))
         across = lax.ppermute(moved, "tp", opposite)
-        ring_pieces[2], ring_pieces[3], _ = lax.optimization_barrier((*ring_pieces[2:4], other_sent))
         ring_step()
-        *last, own_part, other_part = lax.optimization_barrier((*ring_pieces[4:6], own_part, other_part))
-        last = lax.ppermute(jnp.stack(last), "seq", ring)
+        last = jnp.stack([after(piece, other_part) for piece in ring_pieces[4:6]])
+        last = lax.ppermute(last, "seq", ring)
         moved_other = transposed(after(moved_other, across))
         across_other = lax.ppermute(moved_other, "tp", opposite)
         cot_pieces = spread(moved, across, other_part) + spread(moved_other, across_other, own_part)

time: 117 us -> 121 us (1.034)
  starting transfers between devices: 40 us -> 43.6 us
    ppermute x4, waiting for transfers between devices: 13 us -> 1.71 us  [ring_step(): ring_pieces.append(lax.ppermute(ring_pieces[-2], 'seq', ring))]
    ppermute x1, waiting for transfers between devices: 0.01 us -> 8.59 us  [per_device(): across = lax.ppermute(moved, 'tp', opposite)]
    ppermute x2, starting transfers between devices: 3.16 us -> 7.39 us  [per_device(): theirs = [lax.ppermute(r, ('tp', 'dp'), route) for r in rounds]]
    ppermute x1, starting transfers between devices: 6.23 us -> 3.37 us  [per_device(): across = lax.ppermute(moved, 'tp', opposite)]
    ppermute x4, starting transfers between devices: 4.4 us -> 6.44 us  [ring_step(): ring_pieces.append(lax.ppermute(ring_pieces[-2], 'seq', ring))]
    ppermute x8, waiting for transfers between devices: 11.3 us -> 12.8 us  [swap_pairs(): return lax.ppermute(value, axis, [(i, i ^ distance) for i in range(count)])]
    ppermute x8, starting transfers between devices: 11.7 us -> 10.4 us  [swap_pairs(): return lax.ppermute(value, axis, [(i, i ^ distance) for i in range(count)])]
    ppermute x1, starting transfers between devices: 0.49 us -> 1.81 us  [per_device(): across_other = lax.ppermute(moved_other, 'tp', opposite)]
  transfers between devices with their start and end apart: 27 -> 27, of which waited for: 10 -> 9; matrix products, arithmetic and copies ran while one was open for 5% -> 6% of each run, Pallas kernels for 30% -> 27%
where the time goes in v18:
time: 121 us
  starting transfers between devices  43.6 us (36%)
  Pallas kernels  35 us (29%)
  waiting for transfers between devices  28.3 us (23%)
  other arithmetic  6.63 us (5%)
  local copies, waits for them, and re-layouts  6.21 us (5%)
    pallas_call x3, Pallas kernels, by_channel(): pl.pallas_call(kernel, in_specs=[pl.BlockSpec(memory_space=pltpu.SMEM)] *...  16.9 us
    pallas_call x2, Pallas kernels, local_call(): pl.pallas_call(kernel, in_specs=[pl.BlockSpec(memory_space=pltpu.SMEM)] +...  13.8 us
    ppermute x8, waiting for transfers between devices, swap_pairs(): return lax.ppermute(value, axis, [(i, i ^ distance) for i in range(count)])  12.8 us
    ppermute x8, starting transfers between devices, swap_pairs(): return lax.ppermute(value, axis, [(i, i ^ distance) for i in range(count)])  10.4 us
    ppermute x1, waiting for transfers between devices, per_device(): across = lax.ppermute(moved, 'tp', opposite)  8.59 us
    ppermute x2, starting transfers between devices, per_device(): theirs = [lax.ppermute(r, ('tp', 'dp'), route) for r in rounds]  7.39 us
    ppermute x1, starting transfers between devices, per_device(): prior = lax.ppermute(tail, 'seq', [(i, i + 1) for i in range(n_seq - 1)])  7.09 us
    ppermute x4, starting transfers between devices, ring_step(): ring_pieces.append(lax.ppermute(ring_pieces[-2], 'seq', ring))  6.44 us
  transfers between devices with their start and end apart: 27, of which 9 were waited for; matrix products, arithmetic and copies ran while one was open for 6% of the time, Pallas kernels for 27%

profile of v18, /device:TPU:0, one launch (start us, length us, event | category | flops | bytes accessed | tf_op | source)
XLA Modules:
  0.0 120.6 jit_solution(4607196103879008026)
XLA Ops:
  2.4 7.1 %collective-permute-start = (bf16[128,1024]{1,0:T(8,128)(2,1)S(1)}, bf16[128,1024]{1,0:T(8,128)(2,1)S(1)}, u32[]{:S(2)}, u32[]{:S(2)}) collective-permute-start(bf16[128,1024]{1,0:T(8,128)(2,1)S(1)} %fusion.2), channel_id=1, source_target_pairs={{0,8},{8,16},{16,24},{1,9},{9,17},{17,25},{2,10},{10,18},{18,26},{... | collective-permute-start | bytes 786440 | tf_op jit(solution)/shard_map/ppermute | solution.py:419
  9.5 1.7 %collective-permute-start.1 = (bf16[256,1024]{1,0:T(8,128)(2,1)}, bf16[256,1024]{1,0:T(8,128)(2,1)S(1)}, u32[]{:S(2)}, u32[]{:S(2)}) collective-permute-start(bf16[256,1024]{1,0:T(8,128)(2,1)} %bitcast.32), channel_id=1, source_target_pairs={{0,0},{1,4},{2,2},{3,6},{4,1},{5,5},{6,3},{7,7},{8,8},{9,12},{10,1... | collective-permute-start | bytes 1572872 | tf_op jit(solution)/shard_map/ppermute | solution.py:428
  11.2 2.8 %collective-permute-done.refs_3_.refs_6_ = bf16[128,1024]{1,0:T(8,128)(2,1)S(1)} collective-permute-done((bf16[128,1024]{1,0:T(8,128)(2,1)S(1)}, bf16[128,1024]{1,0:T(8,128)(2,1)S(1)}, u32[]{:S(2)}, u32[]{:S(2)}) %collective-permute-start) | collective-permute-done | bytes 262176 | tf_op jit(solution)/shard_map/ppermute | solution.py:419
  14.7 1.1 broadcast_select_fusion
  19.1 5.5 %shard_map.145 = (f32[256,1024]{1,0:T(8,128)}, bf16[256,512]{1,0:T(8,128)(2,1)}, bf16[256,512]{1,0:T(8,128)(2,1)}) custom-call(s32[1]{0:T(128)} %bitcast.6.refs_0_, bf16[768,384]{1,0:T(8,128)(2,1)} %constant.66.clone.refs_1_.refs_0_, bf16[768,384]{1,0:T(8,128)(2,1)} %constant.67.clone.refs_2_.refs_1_, bf16[128,1024]{1,0:T(8,128)(2,1)} %copy-done.5, ...), custom_call_target="tpu_custom_call" | custom-call | flops 22020096 | bytes 57408 | tf_op jit(solution)/shard_map/pallas_call | solution.py:281
  24.6 1.5 %collective-permute-start.5 = (bf16[256,512]{1,0:T(8,128)(2,1)}, bf16[256,512]{1,0:T(8,128)(2,1)S(1)}, u32[]{:S(2)}, u32[]{:S(2)}) collective-permute-start(bf16[256,512]{1,0:T(8,128)(2,1)} %get-tuple-element.59), channel_id=1, source_target_pairs={{0,1},{1,0},{2,3},{3,2},{4,5},{5,4},{6,7},{7,6},{8,9},{9,8},{10,11... | collective-permute-start | bytes 786440 | tf_op jit(solution)/shard_map/ppermute | solution.py:384
  26.1 1.2 collective-permute-done.2.second_mine
  27.3 3.2 %collective-permute-start.6 = (bf16[256,1024]{1,0:T(8,128)(2,1)S(1)}, bf16[256,1024]{1,0:T(8,128)(2,1)S(1)}, u32[]{:S(2)}, u32[]{:S(2)}) collective-permute-start(bf16[256,1024]{1,0:T(8,128)(2,1)S(1)} %collective-permute-done.1.first_mine), channel_id=1, source_target_pairs={{0,2},{1,3},{2,0},{3,1},{4,6},{5,7},{6,4},{7,5},{8,10},{9,11},{10,... | collective-permute-start | bytes 1572872 | tf_op jit(solution)/shard_map/ppermute | solution.py:496
  31.3 4.2 %collective-permute-start.7 = (bf16[256,1024]{1,0:T(8,128)(2,1)S(1)}, bf16[256,1024]{1,0:T(8,128)(2,1)S(1)}, u32[]{:S(2)}, u32[]{:S(2)}) collective-permute-start(bf16[256,1024]{1,0:T(8,128)(2,1)S(1)} %collective-permute-done.2.second_mine), channel_id=1, source_target_pairs={{0,2},{1,3},{2,0},{3,1},{4,6},{5,7},{6,4},{7,5},{8,10},{9,11},{10,... | collective-permute-start | bytes 1572872 | tf_op jit(solution)/shard_map/ppermute | solution.py:496
  36.1 1.7 %collective-permute-start.10 = (bf16[256,512]{1,0:T(8,128)(2,1)}, bf16[256,512]{1,0:T(8,128)(2,1)S(1)}, u32[]{:S(2)}, u32[]{:S(2)}) collective-permute-start(bf16[256,512]{1,0:T(8,128)(2,1)} %get-tuple-element.54.refs_8_), channel_id=1, source_target_pairs={{0,16},{16,24},{24,8},{8,0},{1,17},{17,25},{25,9},{9,1},{2,18},{18... | collective-permute-start | bytes 786440 | tf_op jit(solution)/shard_map/ppermute | solution.py:488
  37.8 2.7 %collective-permute-start.11 = (bf16[256,512]{1,0:T(8,128)(2,1)S(1)}, bf16[256,512]{1,0:T(8,128)(2,1)S(1)}, u32[]{:S(2)}, u32[]{:S(2)}) collective-permute-start(bf16[256,512]{1,0:T(8,128)(2,1)S(1)} %collective-permute-done.5.refs_9_), channel_id=1, source_target_pairs={{0,16},{16,24},{24,8},{8,0},{1,17},{17,25},{25,9},{9,1},{2,18},{18... | collective-permute-start | bytes 786440 | tf_op jit(solution)/shard_map/ppermute | solution.py:488
  42.2 6.4 %shard_map.146 = (bf16[256,1024]{1,0:T(8,128)(2,1)}, f32[256,1024]{1,0:T(8,128)}) custom-call(s32[3]{0:T(128)} %pad_add_fusion.place_ref, bf16[256,1024]{1,0:T(8,128)(2,1)} %copy-done.6, bf16[256,1024]{1,0:T(8,128)(2,1)} %copy-done.7, bf16[256,1024]{1,0:T(8,128)(2,1)} %copy-done.16, bf16[256,1024]{1,0:T(8,128)(2,1)} %copy-done.17, bf16[1024,2048]{1,0:T(8,128)(2,1)} %weight.1), custom_call_target="tpu_custom_call" | custom-call | flops 33554432 | bytes 122880 | tf_op jit(solution)/shard_map/pallas_call | solution.py:301
  49.4 1.7 %collective-permute-done.11.refs_11_ = bf16[256,512]{1,0:T(8,128)(2,1)S(1)} collective-permute-done((bf16[256,512]{1,0:T(8,128)(2,1)S(1)}, bf16[256,512]{1,0:T(8,128)(2,1)S(1)}, u32[]{:S(2)}, u32[]{:S(2)}) %collective-permute-start.11) | collective-permute-done | bytes 262176 | tf_op jit(solution)/shard_map/ppermute | solution.py:488
  51.1 2.1 %shard_map.148.refs_0_ = bf16[1024,256]{1,0:T(8,128)(2,1)} custom-call(bf16[256,1024]{1,0:T(8,128)(2,1)} %copy-done.18), custom_call_target="tpu_custom_call" | custom-call | bytes 16384 | tf_op jit(solution)/shard_map/pallas_call | solution.py:367
  53.3 3.4 %collective-permute-start.18 = (bf16[1024,256]{1,0:T(8,128)(2,1)}, bf16[1024,256]{1,0:T(8,128)(2,1)S(1)}, u32[]{:S(2)}, u32[]{:S(2)}) collective-permute-start(bf16[1024,256]{1,0:T(8,128)(2,1)} %shard_map.148.refs_0_), channel_id=1, source_target_pairs={{0,4},{2,6},{4,0},{6,2},{1,5},{3,7},{5,1},{7,3},{8,12},{10,14},{12... | collective-permute-start | bytes 1572872 | tf_op jit(solution)/shard_map/ppermute | solution.py:520
  57.3 1.7 %collective-permute-start.13 = (bf16[256,512]{1,0:T(8,128)(2,1)S(1)}, bf16[256,512]{1,0:T(8,128)(2,1)S(1)}, u32[]{:S(2)}, u32[]{:S(2)}) collective-permute-start(bf16[256,512]{1,0:T(8,128)(2,1)S(1)} %collective-permute-done.11.refs_11_), channel_id=1, source_target_pairs={{0,16},{16,24},{24,8},{8,0},{1,17},{17,25},{25,9},{9,1},{2,18},{18... | collective-permute-start | bytes 786440 | tf_op jit(solution)/shard_map/ppermute | solution.py:488
  59.3 8.6 %collective-permute-done.18.refs_2_ = bf16[1024,256]{1,0:T(8,128)(2,1)S(1)} collective-permute-done((bf16[1024,256]{1,0:T(8,128)(2,1)}, bf16[1024,256]{1,0:T(8,128)(2,1)S(1)}, u32[]{:S(2)}, u32[]{:S(2)}) %collective-permute-start.18) | collective-permute-done | bytes 524320 | tf_op jit(solution)/shard_map/ppermute | solution.py:520
  67.8 2.2 %shard_map.149.refs_4_ = bf16[1024,256]{1,0:T(8,128)(2,1)} custom-call(bf16[256,1024]{1,0:T(8,128)(2,1)} %copy-done.19), custom_call_target="tpu_custom_call" | custom-call | bytes 16384 | tf_op jit(solution)/shard_map/pallas_call | solution.py:367
  70.1 1.8 %collective-permute-start.21 = (bf16[1024,256]{1,0:T(8,128)(2,1)}, bf16[1024,256]{1,0:T(8,128)(2,1)S(1)}, u32[]{:S(2)}, u32[]{:S(2)}) collective-permute-start(bf16[1024,256]{1,0:T(8,128)(2,1)} %shard_map.149.refs_4_), channel_id=1, source_target_pairs={{0,4},{2,6},{4,0},{6,2},{1,5},{3,7},{5,1},{7,3},{8,12},{10,14},{12... | collective-permute-start | bytes 1572872 | tf_op jit(solution)/shard_map/ppermute | solution.py:525
  72.0 1.6 %collective-permute-start.14 = (bf16[2,256,512]{2,1,0:T(8,128)(2,1)S(1)}, bf16[2,256,512]{2,1,0:T(8,128)(2,1)S(1)}, u32[]{:S(2)}, u32[]{:S(2)}) collective-permute-start(bf16[2,256,512]{2,1,0:T(8,128)(2,1)S(1)} %pad_maximum_fusion.1), channel_id=1, source_target_pairs={{0,16},{16,24},{24,8},{8,0},{1,17},{17,25},{25,9},{9,1},{2,18},{18... | collective-permute-start | bytes 1572872 | tf_op jit(solution)/shard_map/ppermute | solution.py:523
  73.6 5.9 %shard_map.147 = (bf16[256,1024]{1,0:T(8,128)(2,1)}, bf16[256,1024]{1,0:T(8,128)(2,1)}, bf16[128,1024]{1,0:T(8,128)(2,1)}, bf16[64,1024]{1,0:T(8,128)(2,1)}, f32[64,1024]{1,0:T(8,128)}) custom-call(bf16[768,384]{1,0:T(8,128)(2,1)} %constant.66.clone.refs_1_.refs_0_, bf16[768,384]{1,0:T(8,128)(2,1)} %constant.67.clone.refs_2_.refs_1_, ...), custom_call_target="tpu_custom_call" | custom-call | flops 20447232 | bytes 96320 | tf_op jit(solution)/shard_map/pallas_call | solution.py:281
  79.5 1.2 %collective-permute-start.15 = (bf16[64,1024]{1,0:T(8,128)(2,1)}, bf16[64,1024]{1,0:T(8,128)(2,1)S(1)}, u32[]{:S(2)}, u32[]{:S(2)}) collective-permute-start(bf16[64,1024]{1,0:T(8,128)(2,1)} %get-tuple-element.75), channel_id=1, source_target_pairs={{0,1},{1,0},{2,3},{3,2},{4,5},{5,4},{6,7},{7,6},{8,9},{9,8},{10,11... | collective-permute-start | bytes 393224 | tf_op jit(solution)/shard_map/ppermute | solution.py:384
  81.3 1.2 collective-permute-done.21.refs_6_
  82.5 2.3 %collective-permute-done.15 = bf16[64,1024]{1,0:T(8,128)(2,1)S(1)} collective-permute-done((bf16[64,1024]{1,0:T(8,128)(2,1)}, bf16[64,1024]{1,0:T(8,128)(2,1)S(1)}, u32[]{:S(2)}, u32[]{:S(2)}) %collective-permute-start.15) | collective-permute-done | bytes 131104 | tf_op jit(solution)/shard_map/ppermute | solution.py:384
  84.8 1.1 add_convert_fusion.2
  86.5 1.3 %collective-permute-start.24 = (bf16[128,1024]{1,0:T(8,128)(2,1)}, bf16[128,1024]{1,0:T(8,128)(2,1)S(1)}, u32[]{:S(2)}, u32[]{:S(2)}) collective-permute-start(bf16[128,1024]{1,0:T(8,128)(2,1)} %get-tuple-element.88), channel_id=1, source_target_pairs={{8,0},{16,8},{24,16},{9,1},{17,9},{25,17},{10,2},{18,10},{26,18},{... | collective-permute-start | bytes 786440 | tf_op jit(solution)/shard_map/ppermute | solution.py:556
  89.6 7.4 %shard_map.150 = (bf16[512,512]{1,0:T(8,128)(2,1)}, f32[512,512]{1,0:T(8,128)}) custom-call(s32[5]{0:T(128)} %pad_add_fusion.1.place_ref, bf16[1024,256]{1,0:T(8,128)(2,1)} %shard_map.148.refs_0_, bf16[1024,256]{1,0:T(8,128)(2,1)} %copy-done.11, bf16[1024,256]{1,0:T(8,128)(2,1)} %copy-done.8, bf16[1024,256]{1,0:T(8,128)(2,1)} %copy-done.13, ...), custom_call_target="tpu_custom_call" | custom-call | flops 33554432 | bytes 122880 | tf_op jit(solution)/shard_map/pallas_call | solution.py:301
  97.0 3.6 %collective-permute-start.23 = (bf16[64,1024]{1,0:T(8,128)(2,1)S(1)}, bf16[64,1024]{1,0:T(8,128)(2,1)S(1)}, u32[]{:S(2)}, u32[]{:S(2)}) collective-permute-start(bf16[64,1024]{1,0:T(8,128)(2,1)S(1)} %add_convert_fusion.1), channel_id=1, source_target_pairs={{0,16},{8,24},{16,0},{24,8},{1,17},{9,25},{17,1},{25,9},{2,18},{10... | collective-permute-start | bytes 393224 | tf_op jit(solution)/shard_map/ppermute | solution.py:384
  100.7 1.2 collective-permute-start.26
  101.9 5.5 %shard_map.151 = (bf16[256,1024]{1,0:T(8,128)(2,1)}, bf16[256,1024]{1,0:T(8,128)(2,1)}) custom-call(bf16[768,384]{1,0:T(8,128)(2,1)} %constant.66.clone.refs_1_.refs_0_, bf16[768,384]{1,0:T(8,128)(2,1)} %constant.67.clone.refs_2_.refs_1_, bf16[256,1024]{1,0:T(8,128)(2,1)} %get-tuple-element.87.refs_2_, bf16[128,1024]{1,0:T(8,128)(2,1)} %copy-done.23, ...), custom_call_target="tpu_custom_call" | custom-call | flops 5637144576 | bytes 49216 | tf_op jit(solution)/shard_map/pallas_call | solution.py:281
  108.4 8.8 %collective-permute-done.25 = bf16[64,1024]{1,0:T(8,128)(2,1)S(1)} collective-permute-done((bf16[64,1024]{1,0:T(8,128)(2,1)S(1)}, bf16[64,1024]{1,0:T(8,128)(2,1)S(1)}, u32[]{:S(2)}, u32[]{:S(2)}) %collective-permute-start.25) | collective-permute-done | bytes 131104 | tf_op jit(solution)/shard_map/ppermute | solution.py:384
  119.2 1.5 %pad_maximum_fusion = f32[512,1024]{1,0:T(8,128)} fusion(f32[512,512]{1,0:T(8,128)S(1)} %get-tuple-element.103, f32[512,512]{1,0:T(8,128)S(1)} %get-tuple-element.102), kind=kLoop, calls=%fused_computation | loop fusion | flops 524288 | bytes 4194304 | tf_op jit(solution)/shard_map/concatenate | solution.py:597
  (93 shorter events, 16.5 us)
Async XLA Ops:
  1.7 12.9 %collective-permute-start.3 = (bf16[256,1024]{1,0:T(8,128)(2,1)}, bf16[256,1024]{1,0:T(8,128)(2,1)S(1)}, u32[]{:S(2)}, u32[]{:S(2)}) collective-permute-start(bf16[256,1024]{1,0:T(8,128)(2,1)} %bitcast.31), channel_id=1, source_target_pairs={{2,4},{4,2},{8,14},{14,8},{18,20},{20,18},{24,30},{30,24},{3,5},{5... | collective-permute-start | bytes 1572872 | tf_op jit(solution)/shard_map/ppermute | solution.py:441
  2.4 11.6 %collective-permute-start = (bf16[128,1024]{1,0:T(8,128)(2,1)S(1)}, bf16[128,1024]{1,0:T(8,128)(2,1)S(1)}, u32[]{:S(2)}, u32[]{:S(2)}) collective-permute-start(bf16[128,1024]{1,0:T(8,128)(2,1)S(1)} %fusion.2), channel_id=1, source_target_pairs={{0,8},{8,16},{16,24},{1,9},{9,17},{17,25},{2,10},{10,18},{18,26},{... | collective-permute-start | bytes 786440 | tf_op jit(solution)/shard_map/ppermute | solution.py:419
  9.5 16.5 %collective-permute-start.1 = (bf16[256,1024]{1,0:T(8,128)(2,1)}, bf16[256,1024]{1,0:T(8,128)(2,1)S(1)}, u32[]{:S(2)}, u32[]{:S(2)}) collective-permute-start(bf16[256,1024]{1,0:T(8,128)(2,1)} %bitcast.32), channel_id=1, source_target_pairs={{0,0},{1,4},{2,2},{3,6},{4,1},{5,5},{6,3},{7,7},{8,8},{9,12},{10,1... | collective-permute-start | bytes 1572872 | tf_op jit(solution)/shard_map/ppermute | solution.py:428
  14.0 13.3 %collective-permute-start.2 = (bf16[256,1024]{1,0:T(8,128)(2,1)}, bf16[256,1024]{1,0:T(8,128)(2,1)S(1)}, u32[]{:S(2)}, u32[]{:S(2)}) collective-permute-start(bf16[256,1024]{1,0:T(8,128)(2,1)} %bitcast.33), channel_id=1, source_target_pairs={{0,4},{1,0},{2,6},{3,2},{4,5},{5,1},{6,7},{7,3},{8,12},{9,8},{10,1... | collective-permute-start | bytes 1572872 | tf_op jit(solution)/shard_map/ppermute | solution.py:428
  15.8 15.5 %collective-permute-start.4 = (bf16[256,1024]{1,0:T(8,128)(2,1)S(1)}, bf16[256,1024]{1,0:T(8,128)(2,1)S(1)}, u32[]{:S(2)}, u32[]{:S(2)}) collective-permute-start(bf16[256,1024]{1,0:T(8,128)(2,1)S(1)} %broadcast_select_fusion), channel_id=1, source_target_pairs={{0,0},{2,16},{4,12},{6,28},{8,24},{10,8},{12,20},{14,4},{16,2},{18... | collective-permute-start | bytes 1572872 | tf_op jit(solution)/shard_map/ppermute | solution.py:453
  24.6 6.6 %collective-permute-start.5 = (bf16[256,512]{1,0:T(8,128)(2,1)}, bf16[256,512]{1,0:T(8,128)(2,1)S(1)}, u32[]{:S(2)}, u32[]{:S(2)}) collective-permute-start(bf16[256,512]{1,0:T(8,128)(2,1)} %get-tuple-element.59), channel_id=1, source_target_pairs={{0,1},{1,0},{2,3},{3,2},{4,5},{5,4},{6,7},{7,6},{8,9},{9,8},{10,11... | collective-permute-start | bytes 786440 | tf_op jit(solution)/shard_map/ppermute | solution.py:384
  27.3 13.3 %collective-permute-start.6 = (bf16[256,1024]{1,0:T(8,128)(2,1)S(1)}, bf16[256,1024]{1,0:T(8,128)(2,1)S(1)}, u32[]{:S(2)}, u32[]{:S(2)}) collective-permute-start(bf16[256,1024]{1,0:T(8,128)(2,1)S(1)} %collective-permute-done.1.first_mine), channel_id=1, source_target_pairs={{0,2},{1,3},{2,0},{3,1},{4,6},{5,7},{6,4},{7,5},{8,10},{9,11},{10,... | collective-permute-start | bytes 1572872 | tf_op jit(solution)/shard_map/ppermute | solution.py:496
  31.3 48.2 %copy-start.20 = (bf16[256,512]{1,0:T(8,128)(2,1)}, bf16[256,512]{1,0:T(8,128)(2,1)S(1)}, u32[]{:S(2)}) copy-start(bf16[256,512]{1,0:T(8,128)(2,1)S(1)} %collective-permute-done.5.refs_9_) | copy-start | bytes 786436
  31.3 19.8 %copy-start.18 = (bf16[256,1024]{1,0:T(8,128)(2,1)}, bf16[256,1024]{1,0:T(8,128)(2,1)S(1)}, u32[]{:S(2)}) copy-start(bf16[256,1024]{1,0:T(8,128)(2,1)S(1)} %collective-permute-done.4.rows_in) | copy-start | bytes 1572868
  31.3 9.3 %collective-permute-start.7 = (bf16[256,1024]{1,0:T(8,128)(2,1)S(1)}, bf16[256,1024]{1,0:T(8,128)(2,1)S(1)}, u32[]{:S(2)}, u32[]{:S(2)}) collective-permute-start(bf16[256,1024]{1,0:T(8,128)(2,1)S(1)} %collective-permute-done.2.second_mine), channel_id=1, source_target_pairs={{0,2},{1,3},{2,0},{3,1},{4,6},{5,7},{6,4},{7,5},{8,10},{9,11},{10,... | collective-permute-start | bytes 1572872 | tf_op jit(solution)/shard_map/ppermute | solution.py:496
  35.5 13.9 %collective-permute-start.8 = (bf16[256,1024]{1,0:T(8,128)(2,1)S(1)}, bf16[256,1024]{1,0:T(8,128)(2,1)S(1)}, u32[]{:S(2)}, u32[]{:S(2)}) collective-permute-start(bf16[256,1024]{1,0:T(8,128)(2,1)S(1)} %collective-permute-done.4.rows_in), channel_id=1, source_target_pairs={{0,1},{1,0},{2,3},{3,2},{4,5},{5,4},{6,7},{7,6},{8,9},{9,8},{10,11... | collective-permute-start | bytes 1572872 | tf_op jit(solution)/shard_map/ppermute | solution.py:384
  36.1 13.3 %collective-permute-start.10 = (bf16[256,512]{1,0:T(8,128)(2,1)}, bf16[256,512]{1,0:T(8,128)(2,1)S(1)}, u32[]{:S(2)}, u32[]{:S(2)}) collective-permute-start(bf16[256,512]{1,0:T(8,128)(2,1)} %get-tuple-element.54.refs_8_), channel_id=1, source_target_pairs={{0,16},{16,24},{24,8},{8,0},{1,17},{17,25},{25,9},{9,1},{2,18},{18... | collective-permute-start | bytes 786440 | tf_op jit(solution)/shard_map/ppermute | solution.py:488
  37.8 13.3 %collective-permute-start.11 = (bf16[256,512]{1,0:T(8,128)(2,1)S(1)}, bf16[256,512]{1,0:T(8,128)(2,1)S(1)}, u32[]{:S(2)}, u32[]{:S(2)}) collective-permute-start(bf16[256,512]{1,0:T(8,128)(2,1)S(1)} %collective-permute-done.5.refs_9_), channel_id=1, source_target_pairs={{0,16},{16,24},{24,8},{8,0},{1,17},{17,25},{25,9},{9,1},{2,18},{18... | collective-permute-start | bytes 786440 | tf_op jit(solution)/shard_map/ppermute | solution.py:488
  49.4 18.4 %copy-start.19 = (bf16[256,1024]{1,0:T(8,128)(2,1)}, bf16[256,1024]{1,0:T(8,128)(2,1)S(1)}, u32[]{:S(2)}) copy-start(bf16[256,1024]{1,0:T(8,128)(2,1)S(1)} %collective-permute-done.8.rows_in) | copy-start | bytes 1572868
  49.4 30.1 %copy-start.21 = (bf16[256,512]{1,0:T(8,128)(2,1)}, bf16[256,512]{1,0:T(8,128)(2,1)S(1)}, u32[]{:S(2)}) copy-start(bf16[256,512]{1,0:T(8,128)(2,1)S(1)} %collective-permute-done.10.refs_10_) | copy-start | bytes 786436
  51.1 28.4 %copy-start.22 = (bf16[256,512]{1,0:T(8,128)(2,1)}, bf16[256,512]{1,0:T(8,128)(2,1)S(1)}, u32[]{:S(2)}) copy-start(bf16[256,512]{1,0:T(8,128)(2,1)S(1)} %collective-permute-done.11.refs_11_) | copy-start | bytes 786436
  53.3 14.6 %collective-permute-start.18 = (bf16[1024,256]{1,0:T(8,128)(2,1)}, bf16[1024,256]{1,0:T(8,128)(2,1)S(1)}, u32[]{:S(2)}, u32[]{:S(2)}) collective-permute-start(bf16[1024,256]{1,0:T(8,128)(2,1)} %shard_map.148.refs_0_), channel_id=1, source_target_pairs={{0,4},{2,6},{4,0},{6,2},{1,5},{3,7},{5,1},{7,3},{8,12},{10,14},{12... | collective-permute-start | bytes 1572872 | tf_op jit(solution)/shard_map/ppermute | solution.py:520
  56.6 15.3 %collective-permute-start.9 = (bf16[256,1024]{1,0:T(8,128)(2,1)}, bf16[256,1024]{1,0:T(8,128)(2,1)S(1)}, u32[]{:S(2)}, u32[]{:S(2)}) collective-permute-start(bf16[256,1024]{1,0:T(8,128)(2,1)} %get-tuple-element.65), channel_id=1, source_target_pairs={{0,1},{1,0},{2,3},{3,2},{4,5},{5,4},{6,7},{7,6},{8,9},{9,8},{10,11... | collective-permute-start | bytes 1572872 | tf_op jit(solution)/shard_map/ppermute | solution.py:384
  57.3 14.6 %collective-permute-start.13 = (bf16[256,512]{1,0:T(8,128)(2,1)S(1)}, bf16[256,512]{1,0:T(8,128)(2,1)S(1)}, u32[]{:S(2)}, u32[]{:S(2)}) collective-permute-start(bf16[256,512]{1,0:T(8,128)(2,1)S(1)} %collective-permute-done.11.refs_11_), channel_id=1, source_target_pairs={{0,16},{16,24},{24,8},{8,0},{1,17},{17,25},{25,9},{9,1},{2,18},{18... | collective-permute-start | bytes 786440 | tf_op jit(solution)/shard_map/ppermute | solution.py:488
  59.0 12.9 %collective-permute-start.12 = (bf16[256,512]{1,0:T(8,128)(2,1)S(1)}, bf16[256,512]{1,0:T(8,128)(2,1)S(1)}, u32[]{:S(2)}, u32[]{:S(2)}) collective-permute-start(bf16[256,512]{1,0:T(8,128)(2,1)S(1)} %collective-permute-done.10.refs_10_), channel_id=1, source_target_pairs={{0,16},{16,24},{24,8},{8,0},{1,17},{17,25},{25,9},{9,1},{2,18},{18... | collective-permute-start | bytes 786440 | tf_op jit(solution)/shard_map/ppermute | solution.py:488
  70.1 12.4 %collective-permute-start.21 = (bf16[1024,256]{1,0:T(8,128)(2,1)}, bf16[1024,256]{1,0:T(8,128)(2,1)S(1)}, u32[]{:S(2)}, u32[]{:S(2)}) collective-permute-start(bf16[1024,256]{1,0:T(8,128)(2,1)} %shard_map.149.refs_4_), channel_id=1, source_target_pairs={{0,4},{2,6},{4,0},{6,2},{1,5},{3,7},{5,1},{7,3},{8,12},{10,14},{12... | collective-permute-start | bytes 1572872 | tf_op jit(solution)/shard_map/ppermute | solution.py:525
  72.0 12.8 %collective-permute-start.14 = (bf16[2,256,512]{2,1,0:T(8,128)(2,1)S(1)}, bf16[2,256,512]{2,1,0:T(8,128)(2,1)S(1)}, u32[]{:S(2)}, u32[]{:S(2)}) collective-permute-start(bf16[2,256,512]{2,1,0:T(8,128)(2,1)S(1)} %pad_maximum_fusion.1), channel_id=1, source_target_pairs={{0,16},{16,24},{24,8},{8,0},{1,17},{17,25},{25,9},{9,1},{2,18},{18... | collective-permute-start | bytes 1572872 | tf_op jit(solution)/shard_map/ppermute | solution.py:523
  79.5 5.2 %collective-permute-start.15 = (bf16[64,1024]{1,0:T(8,128)(2,1)}, bf16[64,1024]{1,0:T(8,128)(2,1)S(1)}, u32[]{:S(2)}, u32[]{:S(2)}) collective-permute-start(bf16[64,1024]{1,0:T(8,128)(2,1)} %get-tuple-element.75), channel_id=1, source_target_pairs={{0,1},{1,0},{2,3},{3,2},{4,5},{5,4},{6,7},{7,6},{8,9},{9,8},{10,11... | collective-permute-start | bytes 393224 | tf_op jit(solution)/shard_map/ppermute | solution.py:384
  80.8 5.7 %collective-permute-start.17 = (bf16[1024,256]{1,0:T(8,128)(2,1)S(1)}, bf16[1024,256]{1,0:T(8,128)(2,1)S(1)}, u32[]{:S(2)}, u32[]{:S(2)}) collective-permute-start(bf16[1024,256]{1,0:T(8,128)(2,1)S(1)} %copy-done), channel_id=1, source_target_pairs={{0,2},{2,0},{4,6},{6,4},{1,3},{3,1},{5,7},{7,5},{8,10},{10,8},{12,... | collective-permute-start | bytes 1572872 | tf_op jit(solution)/shard_map/ppermute | solution.py:512
  80.8 7.1 %collective-permute-start.20 = (bf16[1024,256]{1,0:T(8,128)(2,1)S(1)}, bf16[1024,256]{1,0:T(8,128)(2,1)S(1)}, u32[]{:S(2)}, u32[]{:S(2)}) collective-permute-start(bf16[1024,256]{1,0:T(8,128)(2,1)S(1)} %copy-done.1), channel_id=1, source_target_pairs={{0,2},{2,0},{4,6},{6,4},{1,3},{3,1},{5,7},{7,5},{8,10},{10,8},{12,... | collective-permute-start | bytes 1572872 | tf_op jit(solution)/shard_map/ppermute | solution.py:512
  82.5 5.3 %collective-permute-start.19 = (bf16[1024,256]{1,0:T(8,128)(2,1)S(1)}, bf16[1024,256]{1,0:T(8,128)(2,1)S(1)}, u32[]{:S(2)}, u32[]{:S(2)}) collective-permute-start(bf16[1024,256]{1,0:T(8,128)(2,1)S(1)} %collective-permute-done.18.refs_2_), channel_id=1, source_target_pairs={{0,2},{2,0},{4,6},{6,4},{1,3},{3,1},{5,7},{7,5},{8,10},{10,8},{12,... | collective-permute-start | bytes 1572872 | tf_op jit(solution)/shard_map/ppermute | solution.py:514
  84.8 3.1 %collective-permute-start.22 = (bf16[1024,256]{1,0:T(8,128)(2,1)S(1)}, bf16[1024,256]{1,0:T(8,128)(2,1)S(1)}, u32[]{:S(2)}, u32[]{:S(2)}) collective-permute-start(bf16[1024,256]{1,0:T(8,128)(2,1)S(1)} %collective-permute-done.21.refs_6_), channel_id=1, source_target_pairs={{0,2},{2,0},{4,6},{6,4},{1,3},{3,1},{5,7},{7,5},{8,10},{10,8},{12,... | collective-permute-start | bytes 1572872 | tf_op jit(solution)/shard_map/ppermute | solution.py:514
  85.9 11.1 %collective-permute-start.16 = (bf16[64,1024]{1,0:T(8,128)(2,1)S(1)}, bf16[64,1024]{1,0:T(8,128)(2,1)S(1)}, u32[]{:S(2)}, u32[]{:S(2)}) collective-permute-start(bf16[64,1024]{1,0:T(8,128)(2,1)S(1)} %add_convert_fusion.2), channel_id=1, source_target_pairs={{0,8},{8,0},{16,24},{24,16},{1,9},{9,1},{17,25},{25,17},{2,10},{10... | collective-permute-start | bytes 393224 | tf_op jit(solution)/shard_map/ppermute | solution.py:384
  86.5 14.2 %collective-permute-start.24 = (bf16[128,1024]{1,0:T(8,128)(2,1)}, bf16[128,1024]{1,0:T(8,128)(2,1)S(1)}, u32[]{:S(2)}, u32[]{:S(2)}) collective-permute-start(bf16[128,1024]{1,0:T(8,128)(2,1)} %get-tuple-element.88), channel_id=1, source_target_pairs={{8,0},{16,8},{24,16},{9,1},{17,9},{25,17},{10,2},{18,10},{26,18},{... | collective-permute-start | bytes 786440 | tf_op jit(solution)/shard_map/ppermute | solution.py:556
  97.0 10.3 %collective-permute-start.23 = (bf16[64,1024]{1,0:T(8,128)(2,1)S(1)}, bf16[64,1024]{1,0:T(8,128)(2,1)S(1)}, u32[]{:S(2)}, u32[]{:S(2)}) collective-permute-start(bf16[64,1024]{1,0:T(8,128)(2,1)S(1)} %add_convert_fusion.1), channel_id=1, source_target_pairs={{0,16},{8,24},{16,0},{24,8},{1,17},{9,25},{17,1},{25,9},{2,18},{10... | collective-permute-start | bytes 393224 | tf_op jit(solution)/shard_map/ppermute | solution.py:384
  100.7 18.2 %collective-permute-start.26 = (bf16[512,512]{1,0:T(8,128)(2,1)}, bf16[512,512]{1,0:T(8,128)(2,1)S(1)}, u32[]{:S(2)}, u32[]{:S(2)}) collective-permute-start(bf16[512,512]{1,0:T(8,128)(2,1)} %get-tuple-element.95), channel_id=1, source_target_pairs={{0,1},{1,0},{2,3},{3,2},{4,5},{5,4},{6,7},{7,6},{8,9},{9,8},{10,11... | collective-permute-start | bytes 1572872 | tf_op jit(solution)/shard_map/ppermute | solution.py:384
  107.4 9.8 %collective-permute-start.25 = (bf16[64,1024]{1,0:T(8,128)(2,1)S(1)}, bf16[64,1024]{1,0:T(8,128)(2,1)S(1)}, u32[]{:S(2)}, u32[]{:S(2)}) collective-permute-start(bf16[64,1024]{1,0:T(8,128)(2,1)S(1)} %add_convert_fusion), channel_id=1, source_target_pairs={{0,1},{1,0},{2,3},{3,2},{4,5},{5,4},{6,7},{7,6},{8,9},{9,8},{10,11... | collective-permute-start | bytes 393224 | tf_op jit(solution)/shard_map/ppermute | solution.py:384
  (19 other events, 105.5 us)

commit v19 on v12

--- a/solution.py
+++ b/solution.py
@@ -477,7 +477,6 @@
         def ring_step(pieces):
             pieces.append(lax.ppermute(pieces[-1], "seq", ring))
 
-        halves[0][0], moved = lax.optimization_barrier((halves[0][0], moved))
         ring_step(halves[0])
         halves[1][0], *rounds = lax.optimization_barrier((halves[1][0], *rounds))
     else:
@@ -503,11 +502,8 @@
         sent_by = lambda value, flip: lax.ppermute(value, "tp", [(t, t ^ flip) for t in range(n_tp)])
         across = sent_by(moved, subs)
         cot_pieces = [moved, sent_by(moved, 1), across, sent_by(after(across, halves[0][2]), 1)]
-        halves[0][2], halves[1][1], own_part = lax.optimization_barrier(
-            (halves[0][2], halves[1][1], own_part)
-        )
+        halves[0][2], own_part = lax.optimization_barrier((halves[0][2], own_part))
         ring_step(halves[0])
-        ring_step(halves[1])
     else:
         full = lax.all_gather(cot, "tp", axis=1, tiled=True)
         cot_all = lax.all_to_all(full, "seq", 1, 0, tiled=True)
@@ -537,8 +533,6 @@
         channels,
         unit * (2 * taps + 4 * length + 3 * taps),
     )
-    later = lax.ppermute(head, "seq", [(i + 1, i) for i in range(n_seq - 1)])
-
     def run_back(later):
         return by_channel(
             functools.partial(back_kernel, scale),
@@ -550,25 +544,30 @@
         )
 
     received = swap_pairs(sent_lag, "dp", 1)
-    if square:
-        weight_place, halves[1][2], signal = lax.optimization_barrier((weight_place, halves[1][2], signal))
+    back_route = [(i + 1, i) for i in range(n_seq - 1)]
+    if square:
+        weight_place, halves[1][1], signal = lax.optimization_barrier((weight_place, halves[1][1], signal))
         ring_step(halves[1])
         first_sent, first_own = weight_sum(weight_place, cot_pieces, halves[0], rows)
         first_received = swap_pairs(first_sent, "dp", 1)
-        received, first_own = lax.optimization_barrier((received, first_own))
+        received, first_own, halves[1][2], head = lax.optimization_barrier(
+            (received, first_own, halves[1][2], head)
+        )
+        ring_step(halves[1])
+    later = lax.ppermute(head, "seq", back_route)
     lag_sum = own_lag + received.astype(f32)
     distance = 1
     while distance < n_seq:
         rounded = lag_sum.astype(bf16)
         received = swap_pairs(rounded, "seq", distance)
         if square and distance == 1:
+            weight_place, first_received = lax.optimization_barrier((weight_place, first_received))
             second_sent, second_own = weight_sum(weight_place, cot_pieces, halves[1], rows)
             second_received = swap_pairs(second_sent, "dp", 1)
+        if square and distance == 2:
             received, second_own = lax.optimization_barrier((received, second_own))
         lag_sum = rounded.astype(f32) + received.astype(f32)
         distance *= 2
-    if square:
-        first_received, lag_sum = lax.optimization_barrier((first_received, lag_sum))
     mine = lag_sum.astype(bf16)
     theirs = swap_pairs(mine, "dp", 1)
     grad_key, grad_value = run_back(after(later, second_own) if square else later)

time: 113 us -> 117 us (1.035)
  starting transfers between devices: 35.6 us -> 44.3 us
  waiting for transfers between devices: 27.9 us -> 21.9 us
    ppermute x6, waiting for transfers between devices: 12.6 us -> 6.5 us  [ring_step(): pieces.append(lax.ppermute(pieces[-1], 'seq', ring))]
    ppermute x7, starting transfers between devices: 5.69 us -> 11.2 us  [swap_pairs(): return lax.ppermute(value, axis, [(i, i ^ distance) for i in range(count)])]
    ppermute x6, starting transfers between devices: 14.4 us -> 17.6 us  [ring_step(): pieces.append(lax.ppermute(pieces[-1], 'seq', ring))]
    ppermute x3, waiting for transfers between devices: 2.1 us -> 0.01 us  [per_device(): lax.ppermute(value, 'tp', [(t, t ^ flip) for t in range(n_tp)])]
    ppermute x7, waiting for transfers between devices: 7.8 us -> 9.89 us  [swap_pairs(): return lax.ppermute(value, axis, [(i, i ^ distance) for i in range(count)])]
    unnamed x45 -> x47, local copies, waits for them, and re-layouts: 6.17 us -> 7.08 us
  transfers between devices with their start and end apart: 24 -> 24, of which waited for: 10 -> 7; matrix products, arithmetic and copies ran while one was open for 5% -> 5% of each run, Pallas kernels for 31% -> 30%
where the time goes in v19:
time: 117 us; the launch traced here: 116 us
  starting transfers between devices  44.3 us (38%)
  Pallas kernels  34.8 us (30%)
  waiting for transfers between devices  21.9 us (19%)
  local copies, waits for them, and re-layouts  8.97 us (8%)
  other arithmetic  5.4 us (5%)
    ppermute x6, starting transfers between devices, ring_step(): pieces.append(lax.ppermute(pieces[-1], 'seq', ring))  17.6 us
    pallas_call x3, Pallas kernels, by_channel(): pl.pallas_call(kernel, in_specs=[pl.BlockSpec(memory_space=pl.ANY)] * (n_...  16.8 us
    pallas_call x3, Pallas kernels, local_call(): pl.pallas_call(kernel, in_specs=[pl.BlockSpec(memory_space=pltpu.SMEM)] +...  16 us
    ppermute x7, starting transfers between devices, swap_pairs(): return lax.ppermute(value, axis, [(i, i ^ distance) for i in range(count)])  11.2 us
    ppermute x7, waiting for transfers between devices, swap_pairs(): return lax.ppermute(value, axis, [(i, i ^ distance) for i in range(count)])  9.89 us
    ppermute x1, starting transfers between devices, per_device(): prior = lax.ppermute(tail, 'seq', [(i, i + 1) for i in range(n_seq - 1)])  7.09 us
    unnamed x47, local copies, waits for them, and re-layouts  7.08 us
    ppermute x6, waiting for transfers between devices, ring_step(): pieces.append(lax.ppermute(pieces[-1], 'seq', ring))  6.5 us
  transfers between devices with their start and end apart: 24, of which 7 were waited for; matrix products, arithmetic and copies ran while one was open for 5% of the time, Pallas kernels for 30%

profile of v19, /device:TPU:0, one launch (start us, length us, event | category | flops | bytes accessed | tf_op | source)
XLA Modules:
  0.0 116.4 jit_solution(1179628171864030742)
XLA Ops:
  0.6 1.1 fusion
  2.4 7.1 %collective-permute-start = (bf16[128,1024]{1,0:T(8,128)(2,1)S(1)}, bf16[128,1024]{1,0:T(8,128)(2,1)S(1)}, u32[]{:S(2)}, u32[]{:S(2)}) collective-permute-start(bf16[128,1024]{1,0:T(8,128)(2,1)S(1)} %fusion), channel_id=1, source_target_pairs={{0,8},{8,16},{16,24},{1,9},{9,17},{17,25},{2,10},{10,18},{18,26},{... | collective-permute-start | bytes 786440 | tf_op jit(solution)/shard_map/ppermute | solution.py:411
  9.5 1.7 %collective-permute-start.2 = (bf16[256,1024]{1,0:T(8,128)(2,1)}, bf16[256,1024]{1,0:T(8,128)(2,1)S(1)}, u32[]{:S(2)}, u32[]{:S(2)}) collective-permute-start(bf16[256,1024]{1,0:T(8,128)(2,1)} %bitcast.28), channel_id=1, source_target_pairs={{0,0},{1,4},{2,2},{3,6},{4,1},{5,5},{6,3},{7,7},{8,8},{9,12},{10,1... | collective-permute-start | bytes 1572872 | tf_op jit(solution)/shard_map/ppermute | solution.py:420
  11.2 2.8 %collective-permute-done.refs_2_.refs_6_ = bf16[128,1024]{1,0:T(8,128)(2,1)S(1)} collective-permute-done((bf16[128,1024]{1,0:T(8,128)(2,1)S(1)}, bf16[128,1024]{1,0:T(8,128)(2,1)S(1)}, u32[]{:S(2)}, u32[]{:S(2)}) %collective-permute-start) | collective-permute-done | bytes 262176 | tf_op jit(solution)/shard_map/ppermute | solution.py:411
  14.7 1.1 broadcast_select_fusion
  19.0 5.5 %shard_map.145 = (f32[256,1024]{1,0:T(8,128)}, bf16[256,512]{1,0:T(8,128)(2,1)}, bf16[256,512]{1,0:T(8,128)(2,1)}) custom-call(bf16[768,384]{1,0:T(8,128)(2,1)} %constant.66.clone.refs_0_, bf16[768,384]{1,0:T(8,128)(2,1)} %constant.67.clone.refs_1_, bf16[128,1024]{1,0:T(8,128)(2,1)} %copy-done.4, bf16[256,1024]{1,0:T(8,128)(2,1)} %bitcast.22, ...), custom_call_target="tpu_custom_call" | custom-call | flops 22020096 | bytes 57408 | tf_op jit(solution)/shard_map/pallas_call | solution.py:275
  24.5 2.7 %collective-permute-done.3.second_mine = bf16[256,1024]{1,0:T(8,128)(2,1)S(1)} collective-permute-done((bf16[256,1024]{1,0:T(8,128)(2,1)}, bf16[256,1024]{1,0:T(8,128)(2,1)S(1)}, u32[]{:S(2)}, u32[]{:S(2)}) %collective-permute-start.3) | collective-permute-done | bytes 524320 | tf_op jit(solution)/shard_map/ppermute | solution.py:420
  27.3 2.7 %collective-permute-start.6 = (bf16[256,1024]{1,0:T(8,128)(2,1)S(1)}, bf16[256,1024]{1,0:T(8,128)(2,1)S(1)}, u32[]{:S(2)}, u32[]{:S(2)}) collective-permute-start(bf16[256,1024]{1,0:T(8,128)(2,1)S(1)} %collective-permute-done.2.first_mine), channel_id=1, source_target_pairs={{0,2},{1,3},{2,0},{3,1},{4,6},{5,7},{6,4},{7,5},{8,10},{9,11},{10,... | collective-permute-start | bytes 1572872 | tf_op jit(solution)/shard_map/ppermute | solution.py:486
  30.0 2.5 %collective-permute-start.1 = (bf16[256,512]{1,0:T(8,128)(2,1)}, bf16[256,512]{1,0:T(8,128)(2,1)S(1)}, u32[]{:S(2)}, u32[]{:S(2)}) collective-permute-start(bf16[256,512]{1,0:T(8,128)(2,1)} %get-tuple-element.54.refs_4_), channel_id=1, source_target_pairs={{0,16},{16,24},{24,8},{8,0},{1,17},{17,25},{25,9},{9,1},{2,18},{18... | collective-permute-start | bytes 786440 | tf_op jit(solution)/shard_map/ppermute | solution.py:478
  32.5 0.8 copy-done.12
  33.3 2.1 %shard_map.146.refs_0_ = bf16[1024,256]{1,0:T(8,128)(2,1)} custom-call(bf16[256,1024]{1,0:T(8,128)(2,1)} %copy-done.12), custom_call_target="tpu_custom_call" | custom-call | bytes 16384 | tf_op jit(solution)/shard_map/pallas_call | solution.py:359
  37.4 6.4 %shard_map.147 = (bf16[256,1024]{1,0:T(8,128)(2,1)}, f32[256,1024]{1,0:T(8,128)}) custom-call(s32[3]{0:T(128)} %pad_add_fusion.place_ref, bf16[256,1024]{1,0:T(8,128)(2,1)} %copy-done.7, bf16[256,1024]{1,0:T(8,128)(2,1)} %copy-done.8, bf16[256,1024]{1,0:T(8,128)(2,1)} %copy-done.10, bf16[256,1024]{1,0:T(8,128)(2,1)} %copy-done.11, bf16[1024,2048]{1,0:T(8,128)(2,1)} %weight.1), custom_call_target="tpu_custom_call" | custom-call | flops 33554432 | bytes 122880 | tf_op jit(solution)/shard_map/pallas_call | solution.py:294
  43.7 2.1 %collective-permute-start.9 = (bf16[256,1024]{1,0:T(8,128)(2,1)}, bf16[256,1024]{1,0:T(8,128)(2,1)S(1)}, u32[]{:S(2)}, u32[]{:S(2)}) collective-permute-start(bf16[256,1024]{1,0:T(8,128)(2,1)} %get-tuple-element.64), channel_id=1, source_target_pairs={{0,1},{1,0},{2,3},{3,2},{4,5},{5,4},{6,7},{7,6},{8,9},{9,8},{10,11... | collective-permute-start | bytes 1572872 | tf_op jit(solution)/shard_map/ppermute | solution.py:376
  45.8 4.9 %collective-permute-start.8 = (bf16[256,512]{1,0:T(8,128)(2,1)S(1)}, bf16[256,512]{1,0:T(8,128)(2,1)S(1)}, u32[]{:S(2)}, u32[]{:S(2)}) collective-permute-start(bf16[256,512]{1,0:T(8,128)(2,1)S(1)} %collective-permute-done.1.refs_5_), channel_id=1, source_target_pairs={{0,16},{16,24},{24,8},{8,0},{1,17},{17,25},{25,9},{9,1},{2,18},{18... | collective-permute-start | bytes 786440 | tf_op jit(solution)/shard_map/ppermute | solution.py:478
  51.1 5.9 %collective-permute-done.8.refs_6_ = bf16[256,512]{1,0:T(8,128)(2,1)S(1)} collective-permute-done((bf16[256,512]{1,0:T(8,128)(2,1)S(1)}, bf16[256,512]{1,0:T(8,128)(2,1)S(1)}, u32[]{:S(2)}, u32[]{:S(2)}) %collective-permute-start.8) | collective-permute-done | bytes 262176 | tf_op jit(solution)/shard_map/ppermute | solution.py:478
  57.0 3.4 %collective-permute-start.10 = (bf16[256,512]{1,0:T(8,128)(2,1)S(1)}, bf16[256,512]{1,0:T(8,128)(2,1)S(1)}, u32[]{:S(2)}, u32[]{:S(2)}) collective-permute-start(bf16[256,512]{1,0:T(8,128)(2,1)S(1)} %copy-done.14), channel_id=1, source_target_pairs={{0,16},{16,24},{24,8},{8,0},{1,17},{17,25},{25,9},{9,1},{2,18},{18... | collective-permute-start | bytes 786440 | tf_op jit(solution)/shard_map/ppermute | solution.py:478
  60.6 0.8 copy-done.9
  61.4 5.8 %shard_map.148 = (bf16[256,1024]{1,0:T(8,128)(2,1)}, bf16[256,1024]{1,0:T(8,128)(2,1)}, bf16[128,1024]{1,0:T(8,128)(2,1)}, bf16[64,1024]{1,0:T(8,128)(2,1)}, f32[64,1024]{1,0:T(8,128)}) custom-call(bf16[768,384]{1,0:T(8,128)(2,1)} %constant.66.clone.refs_0_, bf16[768,384]{1,0:T(8,128)(2,1)} %constant.67.clone.refs_1_, ...), custom_call_target="tpu_custom_call" | custom-call | flops 20447232 | bytes 96320 | tf_op jit(solution)/shard_map/pallas_call | solution.py:275
  67.3 3.2 %collective-permute-start.16 = (bf16[256,512]{1,0:T(8,128)(2,1)S(1)}, bf16[256,512]{1,0:T(8,128)(2,1)S(1)}, u32[]{:S(2)}, u32[]{:S(2)}) collective-permute-start(bf16[256,512]{1,0:T(8,128)(2,1)S(1)} %collective-permute-done.10.refs_5_), channel_id=1, source_target_pairs={{0,16},{16,24},{24,8},{8,0},{1,17},{17,25},{25,9},{9,1},{2,18},{18... | collective-permute-start | bytes 786440 | tf_op jit(solution)/shard_map/ppermute | solution.py:478
  70.5 1.7 %collective-permute-start.11 = (bf16[64,1024]{1,0:T(8,128)(2,1)}, bf16[64,1024]{1,0:T(8,128)(2,1)S(1)}, u32[]{:S(2)}, u32[]{:S(2)}) collective-permute-start(bf16[64,1024]{1,0:T(8,128)(2,1)} %get-tuple-element.75), channel_id=1, source_target_pairs={{0,1},{1,0},{2,3},{3,2},{4,5},{5,4},{6,7},{7,6},{8,9},{9,8},{10,11... | collective-permute-start | bytes 393224 | tf_op jit(solution)/shard_map/ppermute | solution.py:376
  74.2 4.8 %shard_map.149 = (bf16[512,512]{1,0:T(8,128)(2,1)}, f32[512,512]{1,0:T(8,128)}) custom-call(s32[5]{0:T(128)} %pad_add_fusion.1.place_ref, bf16[1024,256]{1,0:T(8,128)(2,1)} %shard_map.146.refs_0_, bf16[1024,256]{1,0:T(8,128)(2,1)} %copy-done.2, bf16[1024,256]{1,0:T(8,128)(2,1)} %copy-done.1, bf16[1024,256]{1,0:T(8,128)(2,1)} %copy-done.3, ...), custom_call_target="tpu_custom_call" | custom-call | flops 16777216 | bytes 73728 | tf_op jit(solution)/shard_map/pallas_call | solution.py:294
  79.0 1.7 %collective-permute-start.20 = (bf16[512,512]{1,0:T(8,128)(2,1)}, bf16[512,512]{1,0:T(8,128)(2,1)S(1)}, u32[]{:S(2)}, u32[]{:S(2)}) collective-permute-start(bf16[512,512]{1,0:T(8,128)(2,1)} %get-tuple-element.86), channel_id=1, source_target_pairs={{0,1},{1,0},{2,3},{3,2},{4,5},{5,4},{6,7},{7,6},{8,9},{9,8},{10,11... | collective-permute-start | bytes 1572872 | tf_op jit(solution)/shard_map/ppermute | solution.py:376
  80.9 3.4 %collective-permute-start.21 = (bf16[256,512]{1,0:T(8,128)(2,1)S(1)}, bf16[256,512]{1,0:T(8,128)(2,1)S(1)}, u32[]{:S(2)}, u32[]{:S(2)}) collective-permute-start(bf16[256,512]{1,0:T(8,128)(2,1)S(1)} %collective-permute-done.16.refs_6_), channel_id=1, source_target_pairs={{0,16},{16,24},{24,8},{8,0},{1,17},{17,25},{25,9},{9,1},{2,18},{18... | collective-permute-start | bytes 786440 | tf_op jit(solution)/shard_map/ppermute | solution.py:478
  84.3 3.0 %collective-permute-done.18 = bf16[64,1024]{1,0:T(8,128)(2,1)S(1)} collective-permute-done((bf16[64,1024]{1,0:T(8,128)(2,1)S(1)}, bf16[64,1024]{1,0:T(8,128)(2,1)S(1)}, u32[]{:S(2)}, u32[]{:S(2)}) %collective-permute-start.18) | collective-permute-done | bytes 131104 | tf_op jit(solution)/shard_map/ppermute | solution.py:376
  87.3 3.4 %collective-permute-start.19 = (bf16[64,1024]{1,0:T(8,128)(2,1)S(1)}, bf16[64,1024]{1,0:T(8,128)(2,1)S(1)}, u32[]{:S(2)}, u32[]{:S(2)}) collective-permute-start(bf16[64,1024]{1,0:T(8,128)(2,1)S(1)} %add_convert_fusion.1), channel_id=1, source_target_pairs={{0,16},{8,24},{16,0},{24,8},{1,17},{9,25},{17,1},{25,9},{2,18},{10... | collective-permute-start | bytes 393224 | tf_op jit(solution)/shard_map/ppermute | solution.py:376
  90.8 1.3 %collective-permute-start.17 = (bf16[128,1024]{1,0:T(8,128)(2,1)S(1)}, bf16[128,1024]{1,0:T(8,128)(2,1)S(1)}, u32[]{:S(2)}, u32[]{:S(2)}) collective-permute-start(bf16[128,1024]{1,0:T(8,128)(2,1)S(1)} %copy-done.21), channel_id=1, source_target_pairs={{8,0},{16,8},{24,16},{9,1},{17,9},{25,17},{10,2},{18,10},{26,18},{... | collective-permute-start | bytes 786440 | tf_op jit(solution)/shard_map/ppermute | solution.py:557
  93.1 4.8 %shard_map.150 = (bf16[512,512]{1,0:T(8,128)(2,1)}, f32[512,512]{1,0:T(8,128)}) custom-call(s32[5]{0:T(128)} %pad_add_fusion.1.place_ref, bf16[1024,256]{1,0:T(8,128)(2,1)} %shard_map.146.refs_0_, bf16[1024,256]{1,0:T(8,128)(2,1)} %copy-done.2, bf16[1024,256]{1,0:T(8,128)(2,1)} %copy-done.1, bf16[1024,256]{1,0:T(8,128)(2,1)} %copy-done.3, ...), custom_call_target="tpu_custom_call" | custom-call | flops 16777216 | bytes 73728 | tf_op jit(solution)/shard_map/pallas_call | solution.py:294
  97.8 1.7 %collective-permute-start.23 = (bf16[512,512]{1,0:T(8,128)(2,1)}, bf16[512,512]{1,0:T(8,128)(2,1)S(1)}, u32[]{:S(2)}, u32[]{:S(2)}) collective-permute-start(bf16[512,512]{1,0:T(8,128)(2,1)} %get-tuple-element.97), channel_id=1, source_target_pairs={{0,1},{1,0},{2,3},{3,2},{4,5},{5,4},{6,7},{7,6},{8,9},{9,8},{10,11... | collective-permute-start | bytes 1572872 | tf_op jit(solution)/shard_map/ppermute | solution.py:376
  100.8 5.5 %shard_map.151 = (bf16[256,1024]{1,0:T(8,128)(2,1)}, bf16[256,1024]{1,0:T(8,128)(2,1)}) custom-call(bf16[768,384]{1,0:T(8,128)(2,1)} %constant.66.clone.refs_0_, bf16[768,384]{1,0:T(8,128)(2,1)} %constant.67.clone.refs_1_, bf16[256,1024]{1,0:T(8,128)(2,1)} %get-tuple-element.74.refs_2_, bf16[128,1024]{1,0:T(8,128)(2,1)} %copy-done.22, ...), custom_call_target="tpu_custom_call" | custom-call | flops 5637144576 | bytes 49216 | tf_op jit(solution)/shard_map/pallas_call | solution.py:275
  106.4 6.6 %collective-permute-done.22 = bf16[64,1024]{1,0:T(8,128)(2,1)S(1)} collective-permute-done((bf16[64,1024]{1,0:T(8,128)(2,1)S(1)}, bf16[64,1024]{1,0:T(8,128)(2,1)S(1)}, u32[]{:S(2)}, u32[]{:S(2)}) %collective-permute-start.22) | collective-permute-done | bytes 131104 | tf_op jit(solution)/shard_map/ppermute | solution.py:376
  113.1 1.0 copy.16
  114.9 1.5 %pad_maximum_fusion = f32[512,1024]{1,0:T(8,128)} fusion(f32[512,512]{1,0:T(8,128)S(1)} %add_multiply_fusion, f32[512,512]{1,0:T(8,128)S(1)} %add_multiply_fusion.1), kind=kLoop, calls=%fused_computation | loop fusion | flops 524288 | bytes 4194304 | tf_op jit(solution)/shard_map/concatenate | solution.py:582
  (85 shorter events, 12.4 us)
Async XLA Ops:
  1.7 12.9 %collective-permute-start.4 = (bf16[256,1024]{1,0:T(8,128)(2,1)}, bf16[256,1024]{1,0:T(8,128)(2,1)S(1)}, u32[]{:S(2)}, u32[]{:S(2)}) collective-permute-start(bf16[256,1024]{1,0:T(8,128)(2,1)} %bitcast.27), channel_id=1, source_target_pairs={{2,4},{4,2},{8,14},{14,8},{18,20},{20,18},{24,30},{30,24},{3,5},{5... | collective-permute-start | bytes 1572872 | tf_op jit(solution)/shard_map/ppermute | solution.py:433
  2.4 11.6 %collective-permute-start = (bf16[128,1024]{1,0:T(8,128)(2,1)S(1)}, bf16[128,1024]{1,0:T(8,128)(2,1)S(1)}, u32[]{:S(2)}, u32[]{:S(2)}) collective-permute-start(bf16[128,1024]{1,0:T(8,128)(2,1)S(1)} %fusion), channel_id=1, source_target_pairs={{0,8},{8,16},{16,24},{1,9},{9,17},{17,25},{2,10},{10,18},{18,26},{... | collective-permute-start | bytes 786440 | tf_op jit(solution)/shard_map/ppermute | solution.py:411
  9.5 15.0 %collective-permute-start.2 = (bf16[256,1024]{1,0:T(8,128)(2,1)}, bf16[256,1024]{1,0:T(8,128)(2,1)S(1)}, u32[]{:S(2)}, u32[]{:S(2)}) collective-permute-start(bf16[256,1024]{1,0:T(8,128)(2,1)} %bitcast.28), channel_id=1, source_target_pairs={{0,0},{1,4},{2,2},{3,6},{4,1},{5,5},{6,3},{7,7},{8,8},{9,12},{10,1... | collective-permute-start | bytes 1572872 | tf_op jit(solution)/shard_map/ppermute | solution.py:420
  14.0 13.3 %collective-permute-start.3 = (bf16[256,1024]{1,0:T(8,128)(2,1)}, bf16[256,1024]{1,0:T(8,128)(2,1)S(1)}, u32[]{:S(2)}, u32[]{:S(2)}) collective-permute-start(bf16[256,1024]{1,0:T(8,128)(2,1)} %bitcast.29), channel_id=1, source_target_pairs={{0,4},{1,0},{2,6},{3,2},{4,5},{5,1},{6,7},{7,3},{8,12},{9,8},{10,1... | collective-permute-start | bytes 1572872 | tf_op jit(solution)/shard_map/ppermute | solution.py:420
  15.8 16.7 %collective-permute-start.5 = (bf16[256,1024]{1,0:T(8,128)(2,1)S(1)}, bf16[256,1024]{1,0:T(8,128)(2,1)S(1)}, u32[]{:S(2)}, u32[]{:S(2)}) collective-permute-start(bf16[256,1024]{1,0:T(8,128)(2,1)S(1)} %broadcast_select_fusion), channel_id=1, source_target_pairs={{0,0},{2,16},{4,12},{6,28},{8,24},{10,8},{12,20},{14,4},{16,2},{18... | collective-permute-start | bytes 1572872 | tf_op jit(solution)/shard_map/ppermute | solution.py:445
  27.3 8.5 %collective-permute-start.6 = (bf16[256,1024]{1,0:T(8,128)(2,1)S(1)}, bf16[256,1024]{1,0:T(8,128)(2,1)S(1)}, u32[]{:S(2)}, u32[]{:S(2)}) collective-permute-start(bf16[256,1024]{1,0:T(8,128)(2,1)S(1)} %collective-permute-done.2.first_mine), channel_id=1, source_target_pairs={{0,2},{1,3},{2,0},{3,1},{4,6},{5,7},{6,4},{7,5},{8,10},{9,11},{10,... | collective-permute-start | bytes 1572872 | tf_op jit(solution)/shard_map/ppermute | solution.py:486
  29.9 5.8 %collective-permute-start.7 = (bf16[256,1024]{1,0:T(8,128)(2,1)S(1)}, bf16[256,1024]{1,0:T(8,128)(2,1)S(1)}, u32[]{:S(2)}, u32[]{:S(2)}) collective-permute-start(bf16[256,1024]{1,0:T(8,128)(2,1)S(1)} %collective-permute-done.3.second_mine), channel_id=1, source_target_pairs={{0,2},{1,3},{2,0},{3,1},{4,6},{5,7},{6,4},{7,5},{8,10},{9,11},{10,... | collective-permute-start | bytes 1572872 | tf_op jit(solution)/shard_map/ppermute | solution.py:486
  30.0 15.8 %collective-permute-start.1 = (bf16[256,512]{1,0:T(8,128)(2,1)}, bf16[256,512]{1,0:T(8,128)(2,1)S(1)}, u32[]{:S(2)}, u32[]{:S(2)}) collective-permute-start(bf16[256,512]{1,0:T(8,128)(2,1)} %get-tuple-element.54.refs_4_), channel_id=1, source_target_pairs={{0,16},{16,24},{24,8},{8,0},{1,17},{17,25},{25,9},{9,1},{2,18},{18... | collective-permute-start | bytes 786440 | tf_op jit(solution)/shard_map/ppermute | solution.py:478
  35.4 15.4 %copy-start = (bf16[1024,256]{1,0:T(8,128)(2,1)S(1)}, bf16[1024,256]{1,0:T(8,128)(2,1)}, u32[]{:S(2)}) copy-start(bf16[1024,256]{1,0:T(8,128)(2,1)} %shard_map.146.refs_0_) | copy-start | bytes 1572868
  35.4 21.6 %copy-start.14 = (bf16[256,512]{1,0:T(8,128)(2,1)S(1)}, bf16[256,512]{1,0:T(8,128)(2,1)}, u32[]{:S(2)}) copy-start(bf16[256,512]{1,0:T(8,128)(2,1)} %get-tuple-element.72.refs_4_) | copy-start | bytes 786436
  35.4 15.7 %collective-permute-start.13 = (bf16[1024,256]{1,0:T(8,128)(2,1)}, bf16[1024,256]{1,0:T(8,128)(2,1)S(1)}, u32[]{:S(2)}, u32[]{:S(2)}) collective-permute-start(bf16[1024,256]{1,0:T(8,128)(2,1)} %shard_map.146.refs_0_), channel_id=1, source_target_pairs={{0,4},{2,6},{4,0},{6,2},{1,5},{3,7},{5,1},{7,3},{8,12},{10,14},{12... | collective-permute-start | bytes 1572872 | tf_op jit(solution)/shard_map/ppermute | solution.py:502
  43.7 16.8 %collective-permute-start.9 = (bf16[256,1024]{1,0:T(8,128)(2,1)}, bf16[256,1024]{1,0:T(8,128)(2,1)S(1)}, u32[]{:S(2)}, u32[]{:S(2)}) collective-permute-start(bf16[256,1024]{1,0:T(8,128)(2,1)} %get-tuple-element.64), channel_id=1, source_target_pairs={{0,1},{1,0},{2,3},{3,2},{4,5},{5,4},{6,7},{7,6},{8,9},{9,8},{10,11... | collective-permute-start | bytes 1572872 | tf_op jit(solution)/shard_map/ppermute | solution.py:376
  45.8 26.9 %copy-start.16 = (bf16[256,512]{1,0:T(8,128)(2,1)}, bf16[256,512]{1,0:T(8,128)(2,1)S(1)}, u32[]{:S(2)}) copy-start(bf16[256,512]{1,0:T(8,128)(2,1)S(1)} %collective-permute-done.1.refs_5_) | copy-start | bytes 786436
  45.8 11.2 %collective-permute-start.8 = (bf16[256,512]{1,0:T(8,128)(2,1)S(1)}, bf16[256,512]{1,0:T(8,128)(2,1)S(1)}, u32[]{:S(2)}, u32[]{:S(2)}) collective-permute-start(bf16[256,512]{1,0:T(8,128)(2,1)S(1)} %collective-permute-done.1.refs_5_), channel_id=1, source_target_pairs={{0,16},{16,24},{24,8},{8,0},{1,17},{17,25},{25,9},{9,1},{2,18},{18... | collective-permute-start | bytes 786440 | tf_op jit(solution)/shard_map/ppermute | solution.py:478
  50.8 21.4 %collective-permute-start.12 = (bf16[1024,256]{1,0:T(8,128)(2,1)S(1)}, bf16[1024,256]{1,0:T(8,128)(2,1)S(1)}, u32[]{:S(2)}, u32[]{:S(2)}) collective-permute-start(bf16[1024,256]{1,0:T(8,128)(2,1)S(1)} %copy-done), channel_id=1, source_target_pairs={{0,2},{2,0},{4,6},{6,4},{1,3},{3,1},{5,7},{7,5},{8,10},{10,8},{12,... | collective-permute-start | bytes 1572872 | tf_op jit(solution)/shard_map/ppermute | solution.py:502
  51.1 16.1 %copy-start.1 = (bf16[1024,256]{1,0:T(8,128)(2,1)}, bf16[1024,256]{1,0:T(8,128)(2,1)S(1)}, u32[]{:S(2)}) copy-start(bf16[1024,256]{1,0:T(8,128)(2,1)S(1)} %collective-permute-done.13.refs_2_) | copy-start | bytes 1572868
  57.0 15.7 %copy-start.18 = (bf16[256,512]{1,0:T(8,128)(2,1)}, bf16[256,512]{1,0:T(8,128)(2,1)S(1)}, u32[]{:S(2)}) copy-start(bf16[256,512]{1,0:T(8,128)(2,1)S(1)} %collective-permute-done.8.refs_6_) | copy-start | bytes 786436
  57.0 15.7 %collective-permute-start.14 = (bf16[1024,256]{1,0:T(8,128)(2,1)S(1)}, bf16[1024,256]{1,0:T(8,128)(2,1)S(1)}, u32[]{:S(2)}, u32[]{:S(2)}) collective-permute-start(bf16[1024,256]{1,0:T(8,128)(2,1)S(1)} %collective-permute-done.13.refs_2_), channel_id=1, source_target_pairs={{0,2},{2,0},{4,6},{6,4},{1,3},{3,1},{5,7},{7,5},{8,10},{10,8},{12,... | collective-permute-start | bytes 1572872 | tf_op jit(solution)/shard_map/ppermute | solution.py:502
  57.0 10.2 %collective-permute-start.10 = (bf16[256,512]{1,0:T(8,128)(2,1)S(1)}, bf16[256,512]{1,0:T(8,128)(2,1)S(1)}, u32[]{:S(2)}, u32[]{:S(2)}) collective-permute-start(bf16[256,512]{1,0:T(8,128)(2,1)S(1)} %copy-done.14), channel_id=1, source_target_pairs={{0,16},{16,24},{24,8},{8,0},{1,17},{17,25},{25,9},{9,1},{2,18},{18... | collective-permute-start | bytes 786440 | tf_op jit(solution)/shard_map/ppermute | solution.py:478
  60.5 12.2 %collective-permute-start.15 = (bf16[256,512]{1,0:T(8,128)(2,1)S(1)}, bf16[256,512]{1,0:T(8,128)(2,1)S(1)}, u32[]{:S(2)}, u32[]{:S(2)}) collective-permute-start(bf16[256,512]{1,0:T(8,128)(2,1)S(1)} %collective-permute-done.8.refs_6_), channel_id=1, source_target_pairs={{0,16},{16,24},{24,8},{8,0},{1,17},{17,25},{25,9},{9,1},{2,18},{18... | collective-permute-start | bytes 786440 | tf_op jit(solution)/shard_map/ppermute | solution.py:478
  67.2 13.5 %copy-start.13 = (f32[64,1024]{1,0:T(8,128)S(1)}, f32[64,1024]{1,0:T(8,128)}, u32[]{:S(2)}) copy-start(f32[64,1024]{1,0:T(8,128)} %get-tuple-element.84) | copy-start | bytes 786436
  67.2 23.6 %copy-start.21 = (bf16[128,1024]{1,0:T(8,128)(2,1)S(1)}, bf16[128,1024]{1,0:T(8,128)(2,1)}, u32[]{:S(2)}) copy-start(bf16[128,1024]{1,0:T(8,128)(2,1)} %get-tuple-element.83) | copy-start | bytes 786436
  67.2 25.1 %copy-start.15 = (bf16[256,512]{1,0:T(8,128)(2,1)}, bf16[256,512]{1,0:T(8,128)(2,1)S(1)}, u32[]{:S(2)}) copy-start(bf16[256,512]{1,0:T(8,128)(2,1)S(1)} %collective-permute-done.10.refs_5_) | copy-start | bytes 786436
  67.3 13.5 %collective-permute-start.16 = (bf16[256,512]{1,0:T(8,128)(2,1)S(1)}, bf16[256,512]{1,0:T(8,128)(2,1)S(1)}, u32[]{:S(2)}, u32[]{:S(2)}) collective-permute-start(bf16[256,512]{1,0:T(8,128)(2,1)S(1)} %collective-permute-done.10.refs_5_), channel_id=1, source_target_pairs={{0,16},{16,24},{24,8},{8,0},{1,17},{17,25},{25,9},{9,1},{2,18},{18... | collective-permute-start | bytes 786440 | tf_op jit(solution)/shard_map/ppermute | solution.py:478
  70.5 10.3 %collective-permute-start.11 = (bf16[64,1024]{1,0:T(8,128)(2,1)}, bf16[64,1024]{1,0:T(8,128)(2,1)S(1)}, u32[]{:S(2)}, u32[]{:S(2)}) collective-permute-start(bf16[64,1024]{1,0:T(8,128)(2,1)} %get-tuple-element.75), channel_id=1, source_target_pairs={{0,1},{1,0},{2,3},{3,2},{4,5},{5,4},{6,7},{7,6},{8,9},{9,8},{10,11... | collective-permute-start | bytes 393224 | tf_op jit(solution)/shard_map/ppermute | solution.py:376
  79.0 13.3 %collective-permute-start.20 = (bf16[512,512]{1,0:T(8,128)(2,1)}, bf16[512,512]{1,0:T(8,128)(2,1)S(1)}, u32[]{:S(2)}, u32[]{:S(2)}) collective-permute-start(bf16[512,512]{1,0:T(8,128)(2,1)} %get-tuple-element.86), channel_id=1, source_target_pairs={{0,1},{1,0},{2,3},{3,2},{4,5},{5,4},{6,7},{7,6},{8,9},{9,8},{10,11... | collective-permute-start | bytes 1572872 | tf_op jit(solution)/shard_map/ppermute | solution.py:376
  80.8 6.5 %collective-permute-start.18 = (bf16[64,1024]{1,0:T(8,128)(2,1)S(1)}, bf16[64,1024]{1,0:T(8,128)(2,1)S(1)}, u32[]{:S(2)}, u32[]{:S(2)}) collective-permute-start(bf16[64,1024]{1,0:T(8,128)(2,1)S(1)} %add_convert_fusion.2), channel_id=1, source_target_pairs={{0,8},{8,0},{16,24},{24,16},{1,9},{9,1},{17,25},{25,17},{2,10},{10... | collective-permute-start | bytes 393224 | tf_op jit(solution)/shard_map/ppermute | solution.py:376
  80.9 11.5 %collective-permute-start.21 = (bf16[256,512]{1,0:T(8,128)(2,1)S(1)}, bf16[256,512]{1,0:T(8,128)(2,1)S(1)}, u32[]{:S(2)}, u32[]{:S(2)}) collective-permute-start(bf16[256,512]{1,0:T(8,128)(2,1)S(1)} %collective-permute-done.16.refs_6_), channel_id=1, source_target_pairs={{0,16},{16,24},{24,8},{8,0},{1,17},{17,25},{25,9},{9,1},{2,18},{18... | collective-permute-start | bytes 786440 | tf_op jit(solution)/shard_map/ppermute | solution.py:478
  87.3 12.2 %collective-permute-start.19 = (bf16[64,1024]{1,0:T(8,128)(2,1)S(1)}, bf16[64,1024]{1,0:T(8,128)(2,1)S(1)}, u32[]{:S(2)}, u32[]{:S(2)}) collective-permute-start(bf16[64,1024]{1,0:T(8,128)(2,1)S(1)} %add_convert_fusion.1), channel_id=1, source_target_pairs={{0,16},{8,24},{16,0},{24,8},{1,17},{9,25},{17,1},{25,9},{2,18},{10... | collective-permute-start | bytes 393224 | tf_op jit(solution)/shard_map/ppermute | solution.py:376
  90.8 9.3 %collective-permute-start.17 = (bf16[128,1024]{1,0:T(8,128)(2,1)S(1)}, bf16[128,1024]{1,0:T(8,128)(2,1)S(1)}, u32[]{:S(2)}, u32[]{:S(2)}) collective-permute-start(bf16[128,1024]{1,0:T(8,128)(2,1)S(1)} %copy-done.21), channel_id=1, source_target_pairs={{8,0},{16,8},{24,16},{9,1},{17,9},{25,17},{10,2},{18,10},{26,18},{... | collective-permute-start | bytes 786440 | tf_op jit(solution)/shard_map/ppermute | solution.py:557
  97.8 16.9 %collective-permute-start.23 = (bf16[512,512]{1,0:T(8,128)(2,1)}, bf16[512,512]{1,0:T(8,128)(2,1)S(1)}, u32[]{:S(2)}, u32[]{:S(2)}) collective-permute-start(bf16[512,512]{1,0:T(8,128)(2,1)} %get-tuple-element.97), channel_id=1, source_target_pairs={{0,1},{1,0},{2,3},{3,2},{4,5},{5,4},{6,7},{7,6},{8,9},{9,8},{10,11... | collective-permute-start | bytes 1572872 | tf_op jit(solution)/shard_map/ppermute | solution.py:376
  99.6 13.4 %collective-permute-start.22 = (bf16[64,1024]{1,0:T(8,128)(2,1)S(1)}, bf16[64,1024]{1,0:T(8,128)(2,1)S(1)}, u32[]{:S(2)}, u32[]{:S(2)}) collective-permute-start(bf16[64,1024]{1,0:T(8,128)(2,1)S(1)} %add_convert_fusion), channel_id=1, source_target_pairs={{0,1},{1,0},{2,3},{3,2},{4,5},{5,4},{6,7},{7,6},{8,9},{9,8},{10,11... | collective-permute-start | bytes 393224 | tf_op jit(solution)/shard_map/ppermute | solution.py:376
  (15 other events, 58.4 us)

commit v20 on v12

--- a/solution.py
+++ b/solution.py
@@ -503,11 +503,10 @@
         sent_by = lambda value, flip: lax.ppermute(value, "tp", [(t, t ^ flip) for t in range(n_tp)])
         across = sent_by(moved, subs)
         cot_pieces = [moved, sent_by(moved, 1), across, sent_by(after(across, halves[0][2]), 1)]
-        halves[0][2], halves[1][1], own_part = lax.optimization_barrier(
-            (halves[0][2], halves[1][1], own_part)
-        )
         ring_step(halves[0])
+        halves[1][1], own_part = lax.optimization_barrier((halves[1][1], own_part))
         ring_step(halves[1])
+        halves[0][3], own_part = lax.optimization_barrier((halves[0][3], own_part))
     else:
         full = lax.all_gather(cot, "tp", axis=1, tiled=True)
         cot_all = lax.all_to_all(full, "seq", 1, 0, tiled=True)

time: 113 us -> 115 us (1.018)
  starting transfers between devices: 35.6 us -> 39 us
  waiting for transfers between devices: 27.9 us -> 26.1 us
    ppermute x6, starting transfers between devices: 14.4 us -> 17.2 us  [ring_step(): pieces.append(lax.ppermute(pieces[-1], 'seq', ring))]
    ppermute x7, waiting for transfers between devices: 7.8 us -> 6.18 us  [swap_pairs(): return lax.ppermute(value, axis, [(i, i ^ distance) for i in range(count)])]
  transfers between devices with their start and end apart: 24 -> 24, of which waited for: 10 -> 9; matrix products, arithmetic and copies ran while one was open for 5% -> 5% of each run, Pallas kernels for 31% -> 30%
where the time goes in v20:
time: 115 us
  starting transfers between devices  39 us (34%)
  Pallas kernels  34.9 us (30%)
  waiting for transfers between devices  26.1 us (23%)
  local copies, waits for them, and re-layouts  8.18 us (7%)
  other arithmetic  5.42 us (5%)
    ppermute x6, starting transfers between devices, ring_step(): pieces.append(lax.ppermute(pieces[-1], 'seq', ring))  17.2 us
    pallas_call x3, Pallas kernels, by_channel(): pl.pallas_call(kernel, in_specs=[pl.BlockSpec(memory_space=pl.ANY)] * (n_...  16.8 us
    pallas_call x3, Pallas kernels, local_call(): pl.pallas_call(kernel, in_specs=[pl.BlockSpec(memory_space=pltpu.SMEM)] +...  16 us
    ppermute x6, waiting for transfers between devices, ring_step(): pieces.append(lax.ppermute(pieces[-1], 'seq', ring))  12.3 us
    ppermute x1, starting transfers between devices, per_device(): prior = lax.ppermute(tail, 'seq', [(i, i + 1) for i in range(n_seq - 1)])  7.09 us
    unnamed x45, local copies, waits for them, and re-layouts  6.29 us
    ppermute x7, starting transfers between devices, swap_pairs(): return lax.ppermute(value, axis, [(i, i ^ distance) for i in range(count)])  6.25 us
    ppermute x7, waiting for transfers between devices, swap_pairs(): return lax.ppermute(value, axis, [(i, i ^ distance) for i in range(count)])  6.18 us
  transfers between devices with their start and end apart: 24, of which 9 were waited for; matrix products, arithmetic and copies ran while one was open for 5% of the time, Pallas kernels for 30%

profile of v20, /device:TPU:0, one launch (start us, length us, event | category | flops | bytes accessed | tf_op | source)
XLA Modules:
  0.0 114.6 jit_solution(7646488562137613404)
XLA Ops:
  0.6 1.1 fusion
  2.4 7.1 %collective-permute-start = (bf16[128,1024]{1,0:T(8,128)(2,1)S(1)}, bf16[128,1024]{1,0:T(8,128)(2,1)S(1)}, u32[]{:S(2)}, u32[]{:S(2)}) collective-permute-start(bf16[128,1024]{1,0:T(8,128)(2,1)S(1)} %fusion), channel_id=1, source_target_pairs={{0,8},{8,16},{16,24},{1,9},{9,17},{17,25},{2,10},{10,18},{18,26},{... | collective-permute-start | bytes 786440 | tf_op jit(solution)/shard_map/ppermute | solution.py:411
  9.5 1.7 %collective-permute-start.4 = (bf16[256,1024]{1,0:T(8,128)(2,1)}, bf16[256,1024]{1,0:T(8,128)(2,1)S(1)}, u32[]{:S(2)}, u32[]{:S(2)}) collective-permute-start(bf16[256,1024]{1,0:T(8,128)(2,1)} %bitcast.28), channel_id=1, source_target_pairs={{0,0},{1,4},{2,2},{3,6},{4,1},{5,5},{6,3},{7,7},{8,8},{9,12},{10,1... | collective-permute-start | bytes 1572872 | tf_op jit(solution)/shard_map/ppermute | solution.py:420
  11.2 2.8 %collective-permute-done.refs_2_.refs_6_ = bf16[128,1024]{1,0:T(8,128)(2,1)S(1)} collective-permute-done((bf16[128,1024]{1,0:T(8,128)(2,1)S(1)}, bf16[128,1024]{1,0:T(8,128)(2,1)S(1)}, u32[]{:S(2)}, u32[]{:S(2)}) %collective-permute-start) | collective-permute-done | bytes 262176 | tf_op jit(solution)/shard_map/ppermute | solution.py:411
  14.7 1.1 broadcast_select_fusion
  19.0 5.5 %shard_map.145 = (f32[256,1024]{1,0:T(8,128)}, bf16[256,512]{1,0:T(8,128)(2,1)}, bf16[256,512]{1,0:T(8,128)(2,1)}) custom-call(bf16[768,384]{1,0:T(8,128)(2,1)} %constant.66.clone.refs_0_, bf16[768,384]{1,0:T(8,128)(2,1)} %constant.67.clone.refs_1_, bf16[128,1024]{1,0:T(8,128)(2,1)} %copy-done.4, bf16[256,1024]{1,0:T(8,128)(2,1)} %bitcast.22, ...), custom_call_target="tpu_custom_call" | custom-call | flops 22020096 | bytes 57408 | tf_op jit(solution)/shard_map/pallas_call | solution.py:275
  24.6 2.7 %collective-permute-done.5.second_mine = bf16[256,1024]{1,0:T(8,128)(2,1)S(1)} collective-permute-done((bf16[256,1024]{1,0:T(8,128)(2,1)}, bf16[256,1024]{1,0:T(8,128)(2,1)S(1)}, u32[]{:S(2)}, u32[]{:S(2)}) %collective-permute-start.5) | collective-permute-done | bytes 524320 | tf_op jit(solution)/shard_map/ppermute | solution.py:420
  27.3 2.7 %collective-permute-start.6 = (bf16[256,1024]{1,0:T(8,128)(2,1)S(1)}, bf16[256,1024]{1,0:T(8,128)(2,1)S(1)}, u32[]{:S(2)}, u32[]{:S(2)}) collective-permute-start(bf16[256,1024]{1,0:T(8,128)(2,1)S(1)} %collective-permute-done.4.first_mine), channel_id=1, source_target_pairs={{0,2},{1,3},{2,0},{3,1},{4,6},{5,7},{6,4},{7,5},{8,10},{9,11},{10,... | collective-permute-start | bytes 1572872 | tf_op jit(solution)/shard_map/ppermute | solution.py:487
  30.1 6.8 %collective-permute-start.3 = (bf16[256,512]{1,0:T(8,128)(2,1)}, bf16[256,512]{1,0:T(8,128)(2,1)S(1)}, u32[]{:S(2)}, u32[]{:S(2)}) collective-permute-start(bf16[256,512]{1,0:T(8,128)(2,1)} %get-tuple-element.58.refs_4_), channel_id=1, source_target_pairs={{0,16},{16,24},{24,8},{8,0},{1,17},{17,25},{25,9},{9,1},{2,18},{18... | collective-permute-start | bytes 786440 | tf_op jit(solution)/shard_map/ppermute | solution.py:478
  36.9 2.1 %shard_map.146.refs_0_ = bf16[1024,256]{1,0:T(8,128)(2,1)} custom-call(bf16[256,1024]{1,0:T(8,128)(2,1)} %copy-done.12), custom_call_target="tpu_custom_call" | custom-call | bytes 16384 | tf_op jit(solution)/shard_map/pallas_call | solution.py:359
  40.6 6.4 %shard_map.147 = (bf16[256,1024]{1,0:T(8,128)(2,1)}, f32[256,1024]{1,0:T(8,128)}) custom-call(s32[3]{0:T(128)} %pad_add_fusion.place_ref, bf16[256,1024]{1,0:T(8,128)(2,1)} %copy-done.7, bf16[256,1024]{1,0:T(8,128)(2,1)} %copy-done.8, bf16[256,1024]{1,0:T(8,128)(2,1)} %copy-done.10, bf16[256,1024]{1,0:T(8,128)(2,1)} %copy-done.11, bf16[1024,2048]{1,0:T(8,128)(2,1)} %weight.1), custom_call_target="tpu_custom_call" | custom-call | flops 33554432 | bytes 122880 | tf_op jit(solution)/shard_map/pallas_call | solution.py:294
  47.0 2.0 %collective-permute-start.8 = (bf16[256,512]{1,0:T(8,128)(2,1)S(1)}, bf16[256,512]{1,0:T(8,128)(2,1)S(1)}, u32[]{:S(2)}, u32[]{:S(2)}) collective-permute-start(bf16[256,512]{1,0:T(8,128)(2,1)S(1)} %collective-permute-done.3.refs_5_), channel_id=1, source_target_pairs={{0,16},{16,24},{24,8},{8,0},{1,17},{17,25},{25,9},{9,1},{2,18},{18... | collective-permute-start | bytes 786440 | tf_op jit(solution)/shard_map/ppermute | solution.py:478
  49.1 1.9 %collective-permute-start.11 = (bf16[256,1024]{1,0:T(8,128)(2,1)}, bf16[256,1024]{1,0:T(8,128)(2,1)S(1)}, u32[]{:S(2)}, u32[]{:S(2)}) collective-permute-start(bf16[256,1024]{1,0:T(8,128)(2,1)} %get-tuple-element.68), channel_id=1, source_target_pairs={{0,1},{1,0},{2,3},{3,2},{4,5},{5,4},{6,7},{7,6},{8,9},{9,8},{10,11... | collective-permute-start | bytes 1572872 | tf_op jit(solution)/shard_map/ppermute | solution.py:376
  51.8 2.1 %collective-permute-done.16.refs_2_ = bf16[1024,256]{1,0:T(8,128)(2,1)S(1)} collective-permute-done((bf16[1024,256]{1,0:T(8,128)(2,1)}, bf16[1024,256]{1,0:T(8,128)(2,1)S(1)}, u32[]{:S(2)}, u32[]{:S(2)}) %collective-permute-start.16) | collective-permute-done | bytes 524320 | tf_op jit(solution)/shard_map/ppermute | solution.py:503
  53.9 2.2 %collective-permute-done.8.refs_6_ = bf16[256,512]{1,0:T(8,128)(2,1)S(1)} collective-permute-done((bf16[256,512]{1,0:T(8,128)(2,1)S(1)}, bf16[256,512]{1,0:T(8,128)(2,1)S(1)}, u32[]{:S(2)}, u32[]{:S(2)}) %collective-permute-start.8) | collective-permute-done | bytes 262176 | tf_op jit(solution)/shard_map/ppermute | solution.py:478
  56.6 2.7 %collective-permute-start.9 = (bf16[256,512]{1,0:T(8,128)(2,1)S(1)}, bf16[256,512]{1,0:T(8,128)(2,1)S(1)}, u32[]{:S(2)}, u32[]{:S(2)}) collective-permute-start(bf16[256,512]{1,0:T(8,128)(2,1)S(1)} %collective-permute-done.8.refs_6_), channel_id=1, source_target_pairs={{0,16},{16,24},{24,8},{8,0},{1,17},{17,25},{25,9},{9,1},{2,18},{18... | collective-permute-start | bytes 786440 | tf_op jit(solution)/shard_map/ppermute | solution.py:478
  59.2 2.5 %collective-permute-done.10.refs_5_ = bf16[256,512]{1,0:T(8,128)(2,1)S(1)} collective-permute-done((bf16[256,512]{1,0:T(8,128)(2,1)S(1)}, bf16[256,512]{1,0:T(8,128)(2,1)S(1)}, u32[]{:S(2)}, u32[]{:S(2)}) %collective-permute-start.10) | collective-permute-done | bytes 262176 | tf_op jit(solution)/shard_map/ppermute | solution.py:478
  61.7 1.5 %collective-permute-start.12 = (bf16[256,512]{1,0:T(8,128)(2,1)S(1)}, bf16[256,512]{1,0:T(8,128)(2,1)S(1)}, u32[]{:S(2)}, u32[]{:S(2)}) collective-permute-start(bf16[256,512]{1,0:T(8,128)(2,1)S(1)} %collective-permute-done.10.refs_5_), channel_id=1, source_target_pairs={{0,16},{16,24},{24,8},{8,0},{1,17},{17,25},{25,9},{9,1},{2,18},{18... | collective-permute-start | bytes 786440 | tf_op jit(solution)/shard_map/ppermute | solution.py:478
  63.2 4.1 %collective-permute-done.9.refs_7_ = bf16[256,512]{1,0:T(8,128)(2,1)S(1)} collective-permute-done((bf16[256,512]{1,0:T(8,128)(2,1)S(1)}, bf16[256,512]{1,0:T(8,128)(2,1)S(1)}, u32[]{:S(2)}, u32[]{:S(2)}) %collective-permute-start.9) | collective-permute-done | bytes 262176 | tf_op jit(solution)/shard_map/ppermute | solution.py:478
  68.2 5.8 %shard_map.148 = (bf16[256,1024]{1,0:T(8,128)(2,1)}, bf16[256,1024]{1,0:T(8,128)(2,1)}, bf16[128,1024]{1,0:T(8,128)(2,1)}, bf16[64,1024]{1,0:T(8,128)(2,1)}, f32[64,1024]{1,0:T(8,128)}) custom-call(bf16[768,384]{1,0:T(8,128)(2,1)} %constant.66.clone.refs_0_, bf16[768,384]{1,0:T(8,128)(2,1)} %constant.67.clone.refs_1_, ...), custom_call_target="tpu_custom_call" | custom-call | flops 20447232 | bytes 96320 | tf_op jit(solution)/shard_map/pallas_call | solution.py:275
  74.1 1.3 %collective-permute-start.13 = (bf16[128,1024]{1,0:T(8,128)(2,1)}, bf16[128,1024]{1,0:T(8,128)(2,1)S(1)}, u32[]{:S(2)}, u32[]{:S(2)}) collective-permute-start(bf16[128,1024]{1,0:T(8,128)(2,1)} %get-tuple-element.81), channel_id=1, source_target_pairs={{8,0},{16,8},{24,16},{9,1},{17,9},{25,17},{10,2},{18,10},{26,18},{... | collective-permute-start | bytes 786440 | tf_op jit(solution)/shard_map/ppermute | solution.py:539
  75.4 3.5 %collective-permute-start.19 = (bf16[256,512]{1,0:T(8,128)(2,1)S(1)}, bf16[256,512]{1,0:T(8,128)(2,1)S(1)}, u32[]{:S(2)}, u32[]{:S(2)}) collective-permute-start(bf16[256,512]{1,0:T(8,128)(2,1)S(1)} %collective-permute-done.12.refs_6_), channel_id=1, source_target_pairs={{0,16},{16,24},{24,8},{8,0},{1,17},{17,25},{25,9},{9,1},{2,18},{18... | collective-permute-start | bytes 786440 | tf_op jit(solution)/shard_map/ppermute | solution.py:478
  80.5 4.8 %shard_map.149 = (bf16[512,512]{1,0:T(8,128)(2,1)}, f32[512,512]{1,0:T(8,128)}) custom-call(s32[5]{0:T(128)} %pad_add_fusion.1.place_ref, bf16[1024,256]{1,0:T(8,128)(2,1)} %shard_map.146.refs_0_, bf16[1024,256]{1,0:T(8,128)(2,1)} %copy-done.2, bf16[1024,256]{1,0:T(8,128)(2,1)} %copy-done.1, bf16[1024,256]{1,0:T(8,128)(2,1)} %copy-done.3, ...), custom_call_target="tpu_custom_call" | custom-call | flops 16777216 | bytes 73728 | tf_op jit(solution)/shard_map/pallas_call | solution.py:294
  85.4 2.0 %collective-permute-start.20 = (bf16[512,512]{1,0:T(8,128)(2,1)}, bf16[512,512]{1,0:T(8,128)(2,1)S(1)}, u32[]{:S(2)}, u32[]{:S(2)}) collective-permute-start(bf16[512,512]{1,0:T(8,128)(2,1)} %get-tuple-element.96), channel_id=1, source_target_pairs={{0,1},{1,0},{2,3},{3,2},{4,5},{5,4},{6,7},{7,6},{8,9},{9,8},{10,11... | collective-permute-start | bytes 1572872 | tf_op jit(solution)/shard_map/ppermute | solution.py:376
  87.4 3.5 %collective-permute-done.19.refs_7_ = bf16[256,512]{1,0:T(8,128)(2,1)S(1)} collective-permute-done((bf16[256,512]{1,0:T(8,128)(2,1)S(1)}, bf16[256,512]{1,0:T(8,128)(2,1)S(1)}, u32[]{:S(2)}, u32[]{:S(2)}) %collective-permute-start.19) | collective-permute-done | bytes 262176 | tf_op jit(solution)/shard_map/ppermute | solution.py:478
  91.7 4.8 %shard_map.150 = (bf16[512,512]{1,0:T(8,128)(2,1)}, f32[512,512]{1,0:T(8,128)}) custom-call(s32[5]{0:T(128)} %pad_add_fusion.1.place_ref, bf16[1024,256]{1,0:T(8,128)(2,1)} %shard_map.146.refs_0_, bf16[1024,256]{1,0:T(8,128)(2,1)} %copy-done.2, bf16[1024,256]{1,0:T(8,128)(2,1)} %copy-done.1, bf16[1024,256]{1,0:T(8,128)(2,1)} %copy-done.3, ...), custom_call_target="tpu_custom_call" | custom-call | flops 16777216 | bytes 73728 | tf_op jit(solution)/shard_map/pallas_call | solution.py:294
  96.5 2.1 %collective-permute-start.23 = (bf16[512,512]{1,0:T(8,128)(2,1)}, bf16[512,512]{1,0:T(8,128)(2,1)S(1)}, u32[]{:S(2)}, u32[]{:S(2)}) collective-permute-start(bf16[512,512]{1,0:T(8,128)(2,1)} %get-tuple-element.101), channel_id=1, source_target_pairs={{0,1},{1,0},{2,3},{3,2},{4,5},{5,4},{6,7},{7,6},{8,9},{9,8},{10,11... | collective-permute-start | bytes 1572872 | tf_op jit(solution)/shard_map/ppermute | solution.py:376
  99.3 5.5 %shard_map.151 = (bf16[256,1024]{1,0:T(8,128)(2,1)}, bf16[256,1024]{1,0:T(8,128)(2,1)}) custom-call(bf16[768,384]{1,0:T(8,128)(2,1)} %constant.66.clone.refs_0_, bf16[768,384]{1,0:T(8,128)(2,1)} %constant.67.clone.refs_1_, bf16[256,1024]{1,0:T(8,128)(2,1)} %get-tuple-element.80.refs_2_, bf16[128,1024]{1,0:T(8,128)(2,1)} %copy-done.21, ...), custom_call_target="tpu_custom_call" | custom-call | flops 5637144576 | bytes 49216 | tf_op jit(solution)/shard_map/pallas_call | solution.py:275
  104.8 1.2 %collective-permute-done.21 = bf16[64,1024]{1,0:T(8,128)(2,1)S(1)} collective-permute-done((bf16[64,1024]{1,0:T(8,128)(2,1)S(1)}, bf16[64,1024]{1,0:T(8,128)(2,1)S(1)}, u32[]{:S(2)}, u32[]{:S(2)}) %collective-permute-start.21) | collective-permute-done | bytes 131104 | tf_op jit(solution)/shard_map/ppermute | solution.py:376
  106.3 5.0 %collective-permute-done.23 = bf16[512,512]{1,0:T(8,128)(2,1)S(1)} collective-permute-done((bf16[512,512]{1,0:T(8,128)(2,1)}, bf16[512,512]{1,0:T(8,128)(2,1)S(1)}, u32[]{:S(2)}, u32[]{:S(2)}) %collective-permute-start.23) | collective-permute-done | bytes 524320 | tf_op jit(solution)/shard_map/ppermute | solution.py:376
  111.4 1.5 %pad_maximum_fusion = f32[512,1024]{1,0:T(8,128)} fusion(f32[512,512]{1,0:T(8,128)S(1)} %add_multiply_fusion, f32[512,512]{1,0:T(8,128)S(1)} %add_multiply_fusion.1), kind=kLoop, calls=%fused_computation | loop fusion | flops 524288 | bytes 4194304 | tf_op jit(solution)/shard_map/concatenate | solution.py:582
  113.0 1.0 copy.16
  (83 shorter events, 12.7 us)
Async XLA Ops:
  1.7 12.9 %collective-permute-start.1 = (bf16[256,1024]{1,0:T(8,128)(2,1)}, bf16[256,1024]{1,0:T(8,128)(2,1)S(1)}, u32[]{:S(2)}, u32[]{:S(2)}) collective-permute-start(bf16[256,1024]{1,0:T(8,128)(2,1)} %bitcast.27), channel_id=1, source_target_pairs={{2,4},{4,2},{8,14},{14,8},{18,20},{20,18},{24,30},{30,24},{3,5},{5... | collective-permute-start | bytes 1572872 | tf_op jit(solution)/shard_map/ppermute | solution.py:433
  2.4 11.6 %collective-permute-start = (bf16[128,1024]{1,0:T(8,128)(2,1)S(1)}, bf16[128,1024]{1,0:T(8,128)(2,1)S(1)}, u32[]{:S(2)}, u32[]{:S(2)}) collective-permute-start(bf16[128,1024]{1,0:T(8,128)(2,1)S(1)} %fusion), channel_id=1, source_target_pairs={{0,8},{8,16},{16,24},{1,9},{9,17},{17,25},{2,10},{10,18},{18,26},{... | collective-permute-start | bytes 786440 | tf_op jit(solution)/shard_map/ppermute | solution.py:411
  9.5 15.0 %collective-permute-start.4 = (bf16[256,1024]{1,0:T(8,128)(2,1)}, bf16[256,1024]{1,0:T(8,128)(2,1)S(1)}, u32[]{:S(2)}, u32[]{:S(2)}) collective-permute-start(bf16[256,1024]{1,0:T(8,128)(2,1)} %bitcast.28), channel_id=1, source_target_pairs={{0,0},{1,4},{2,2},{3,6},{4,1},{5,5},{6,3},{7,7},{8,8},{9,12},{10,1... | collective-permute-start | bytes 1572872 | tf_op jit(solution)/shard_map/ppermute | solution.py:420
  14.0 13.3 %collective-permute-start.5 = (bf16[256,1024]{1,0:T(8,128)(2,1)}, bf16[256,1024]{1,0:T(8,128)(2,1)S(1)}, u32[]{:S(2)}, u32[]{:S(2)}) collective-permute-start(bf16[256,1024]{1,0:T(8,128)(2,1)} %bitcast.29), channel_id=1, source_target_pairs={{0,4},{1,0},{2,6},{3,2},{4,5},{5,1},{6,7},{7,3},{8,12},{9,8},{10,1... | collective-permute-start | bytes 1572872 | tf_op jit(solution)/shard_map/ppermute | solution.py:420
  15.8 14.3 %collective-permute-start.2 = (bf16[256,1024]{1,0:T(8,128)(2,1)S(1)}, bf16[256,1024]{1,0:T(8,128)(2,1)S(1)}, u32[]{:S(2)}, u32[]{:S(2)}) collective-permute-start(bf16[256,1024]{1,0:T(8,128)(2,1)S(1)} %broadcast_select_fusion), channel_id=1, source_target_pairs={{0,0},{2,16},{4,12},{6,28},{8,24},{10,8},{12,20},{14,4},{16,2},{18... | collective-permute-start | bytes 1572872 | tf_op jit(solution)/shard_map/ppermute | solution.py:445
  24.6 14.5 %copy-start.7 = (bf16[256,1024]{1,0:T(8,128)(2,1)}, bf16[256,1024]{1,0:T(8,128)(2,1)S(1)}, u32[]{:S(2)}) copy-start(bf16[256,1024]{1,0:T(8,128)(2,1)S(1)} %collective-permute-done.4.first_mine) | copy-start | bytes 1572868
  27.3 11.8 %collective-permute-start.6 = (bf16[256,1024]{1,0:T(8,128)(2,1)S(1)}, bf16[256,1024]{1,0:T(8,128)(2,1)S(1)}, u32[]{:S(2)}, u32[]{:S(2)}) collective-permute-start(bf16[256,1024]{1,0:T(8,128)(2,1)S(1)} %collective-permute-done.4.first_mine), channel_id=1, source_target_pairs={{0,2},{1,3},{2,0},{3,1},{4,6},{5,7},{6,4},{7,5},{8,10},{9,11},{10,... | collective-permute-start | bytes 1572872 | tf_op jit(solution)/shard_map/ppermute | solution.py:487
  30.0 9.1 %collective-permute-start.7 = (bf16[256,1024]{1,0:T(8,128)(2,1)S(1)}, bf16[256,1024]{1,0:T(8,128)(2,1)S(1)}, u32[]{:S(2)}, u32[]{:S(2)}) collective-permute-start(bf16[256,1024]{1,0:T(8,128)(2,1)S(1)} %collective-permute-done.5.second_mine), channel_id=1, source_target_pairs={{0,2},{1,3},{2,0},{3,1},{4,6},{5,7},{6,4},{7,5},{8,10},{9,11},{10,... | collective-permute-start | bytes 1572872 | tf_op jit(solution)/shard_map/ppermute | solution.py:487
  30.1 16.9 %collective-permute-start.3 = (bf16[256,512]{1,0:T(8,128)(2,1)}, bf16[256,512]{1,0:T(8,128)(2,1)S(1)}, u32[]{:S(2)}, u32[]{:S(2)}) collective-permute-start(bf16[256,512]{1,0:T(8,128)(2,1)} %get-tuple-element.58.refs_4_), channel_id=1, source_target_pairs={{0,16},{16,24},{24,8},{8,0},{1,17},{17,25},{25,9},{9,1},{2,18},{18... | collective-permute-start | bytes 786440 | tf_op jit(solution)/shard_map/ppermute | solution.py:478
  38.9 12.0 %copy-start.14 = (bf16[256,512]{1,0:T(8,128)(2,1)S(1)}, bf16[256,512]{1,0:T(8,128)(2,1)}, u32[]{:S(2)}) copy-start(bf16[256,512]{1,0:T(8,128)(2,1)} %get-tuple-element.70.refs_4_) | copy-start | bytes 786436
  38.9 12.8 %copy-start = (bf16[1024,256]{1,0:T(8,128)(2,1)S(1)}, bf16[1024,256]{1,0:T(8,128)(2,1)}, u32[]{:S(2)}) copy-start(bf16[1024,256]{1,0:T(8,128)(2,1)} %shard_map.146.refs_0_) | copy-start | bytes 1572868
  39.0 14.9 %collective-permute-start.16 = (bf16[1024,256]{1,0:T(8,128)(2,1)}, bf16[1024,256]{1,0:T(8,128)(2,1)S(1)}, u32[]{:S(2)}, u32[]{:S(2)}) collective-permute-start(bf16[1024,256]{1,0:T(8,128)(2,1)} %shard_map.146.refs_0_), channel_id=1, source_target_pairs={{0,4},{2,6},{4,0},{6,2},{1,5},{3,7},{5,1},{7,3},{8,12},{10,14},{12... | collective-permute-start | bytes 1572872 | tf_op jit(solution)/shard_map/ppermute | solution.py:503
  47.0 31.9 %copy-start.15 = (bf16[256,512]{1,0:T(8,128)(2,1)}, bf16[256,512]{1,0:T(8,128)(2,1)S(1)}, u32[]{:S(2)}) copy-start(bf16[256,512]{1,0:T(8,128)(2,1)S(1)} %collective-permute-done.3.refs_5_) | copy-start | bytes 786436
  47.0 9.1 %collective-permute-start.8 = (bf16[256,512]{1,0:T(8,128)(2,1)S(1)}, bf16[256,512]{1,0:T(8,128)(2,1)S(1)}, u32[]{:S(2)}, u32[]{:S(2)}) collective-permute-start(bf16[256,512]{1,0:T(8,128)(2,1)S(1)} %collective-permute-done.3.refs_5_), channel_id=1, source_target_pairs={{0,16},{16,24},{24,8},{8,0},{1,17},{17,25},{25,9},{9,1},{2,18},{18... | collective-permute-start | bytes 786440 | tf_op jit(solution)/shard_map/ppermute | solution.py:478
  49.1 18.3 %collective-permute-start.11 = (bf16[256,1024]{1,0:T(8,128)(2,1)}, bf16[256,1024]{1,0:T(8,128)(2,1)S(1)}, u32[]{:S(2)}, u32[]{:S(2)}) collective-permute-start(bf16[256,1024]{1,0:T(8,128)(2,1)} %get-tuple-element.68), channel_id=1, source_target_pairs={{0,1},{1,0},{2,3},{3,2},{4,5},{5,4},{6,7},{7,6},{8,9},{9,8},{10,11... | collective-permute-start | bytes 1572872 | tf_op jit(solution)/shard_map/ppermute | solution.py:376
  51.0 10.7 %collective-permute-start.10 = (bf16[256,512]{1,0:T(8,128)(2,1)S(1)}, bf16[256,512]{1,0:T(8,128)(2,1)S(1)}, u32[]{:S(2)}, u32[]{:S(2)}) collective-permute-start(bf16[256,512]{1,0:T(8,128)(2,1)S(1)} %copy-done.14), channel_id=1, source_target_pairs={{0,16},{16,24},{24,8},{8,0},{1,17},{17,25},{25,9},{9,1},{2,18},{18... | collective-permute-start | bytes 786440 | tf_op jit(solution)/shard_map/ppermute | solution.py:478
  51.8 27.1 %collective-permute-start.15 = (bf16[1024,256]{1,0:T(8,128)(2,1)S(1)}, bf16[1024,256]{1,0:T(8,128)(2,1)S(1)}, u32[]{:S(2)}, u32[]{:S(2)}) collective-permute-start(bf16[1024,256]{1,0:T(8,128)(2,1)S(1)} %copy-done), channel_id=1, source_target_pairs={{0,2},{2,0},{4,6},{6,4},{1,3},{3,1},{5,7},{7,5},{8,10},{10,8},{12,... | collective-permute-start | bytes 1572872 | tf_op jit(solution)/shard_map/ppermute | solution.py:503
  53.9 20.1 %copy-start.1 = (bf16[1024,256]{1,0:T(8,128)(2,1)}, bf16[1024,256]{1,0:T(8,128)(2,1)S(1)}, u32[]{:S(2)}) copy-start(bf16[1024,256]{1,0:T(8,128)(2,1)S(1)} %collective-permute-done.16.refs_2_) | copy-start | bytes 1572868
  56.1 22.8 %copy-start.17 = (bf16[256,512]{1,0:T(8,128)(2,1)}, bf16[256,512]{1,0:T(8,128)(2,1)S(1)}, u32[]{:S(2)}) copy-start(bf16[256,512]{1,0:T(8,128)(2,1)S(1)} %collective-permute-done.8.refs_6_) | copy-start | bytes 786436
  56.1 22.8 %collective-permute-start.17 = (bf16[1024,256]{1,0:T(8,128)(2,1)S(1)}, bf16[1024,256]{1,0:T(8,128)(2,1)S(1)}, u32[]{:S(2)}, u32[]{:S(2)}) collective-permute-start(bf16[1024,256]{1,0:T(8,128)(2,1)S(1)} %collective-permute-done.16.refs_2_), channel_id=1, source_target_pairs={{0,2},{2,0},{4,6},{6,4},{1,3},{3,1},{5,7},{7,5},{8,10},{10,8},{12,... | collective-permute-start | bytes 1572872 | tf_op jit(solution)/shard_map/ppermute | solution.py:503
  56.6 10.8 %collective-permute-start.9 = (bf16[256,512]{1,0:T(8,128)(2,1)S(1)}, bf16[256,512]{1,0:T(8,128)(2,1)S(1)}, u32[]{:S(2)}, u32[]{:S(2)}) collective-permute-start(bf16[256,512]{1,0:T(8,128)(2,1)S(1)} %collective-permute-done.8.refs_6_), channel_id=1, source_target_pairs={{0,16},{16,24},{24,8},{8,0},{1,17},{17,25},{25,9},{9,1},{2,18},{18... | collective-permute-start | bytes 786440 | tf_op jit(solution)/shard_map/ppermute | solution.py:478
  61.7 29.2 %copy-start.16 = (bf16[256,512]{1,0:T(8,128)(2,1)}, bf16[256,512]{1,0:T(8,128)(2,1)S(1)}, u32[]{:S(2)}) copy-start(bf16[256,512]{1,0:T(8,128)(2,1)S(1)} %collective-permute-done.10.refs_5_) | copy-start | bytes 786436
  61.7 12.4 %collective-permute-start.12 = (bf16[256,512]{1,0:T(8,128)(2,1)S(1)}, bf16[256,512]{1,0:T(8,128)(2,1)S(1)}, u32[]{:S(2)}, u32[]{:S(2)}) collective-permute-start(bf16[256,512]{1,0:T(8,128)(2,1)S(1)} %collective-permute-done.10.refs_5_), channel_id=1, source_target_pairs={{0,16},{16,24},{24,8},{8,0},{1,17},{17,25},{25,9},{9,1},{2,18},{18... | collective-permute-start | bytes 786440 | tf_op jit(solution)/shard_map/ppermute | solution.py:478
  74.0 11.3 %collective-permute-start.14 = (bf16[64,1024]{1,0:T(8,128)(2,1)}, bf16[64,1024]{1,0:T(8,128)(2,1)S(1)}, u32[]{:S(2)}, u32[]{:S(2)}) collective-permute-start(bf16[64,1024]{1,0:T(8,128)(2,1)} %get-tuple-element.83), channel_id=1, source_target_pairs={{0,1},{1,0},{2,3},{3,2},{4,5},{5,4},{6,7},{7,6},{8,9},{9,8},{10,11... | collective-permute-start | bytes 393224 | tf_op jit(solution)/shard_map/ppermute | solution.py:376
  74.1 16.8 %copy-start.18 = (bf16[256,512]{1,0:T(8,128)(2,1)}, bf16[256,512]{1,0:T(8,128)(2,1)S(1)}, u32[]{:S(2)}) copy-start(bf16[256,512]{1,0:T(8,128)(2,1)S(1)} %collective-permute-done.12.refs_6_) | copy-start | bytes 786436
  74.1 24.5 %collective-permute-start.13 = (bf16[128,1024]{1,0:T(8,128)(2,1)}, bf16[128,1024]{1,0:T(8,128)(2,1)S(1)}, u32[]{:S(2)}, u32[]{:S(2)}) collective-permute-start(bf16[128,1024]{1,0:T(8,128)(2,1)} %get-tuple-element.81), channel_id=1, source_target_pairs={{8,0},{16,8},{24,16},{9,1},{17,9},{25,17},{10,2},{18,10},{26,18},{... | collective-permute-start | bytes 786440 | tf_op jit(solution)/shard_map/ppermute | solution.py:539
  75.4 15.5 %collective-permute-start.19 = (bf16[256,512]{1,0:T(8,128)(2,1)S(1)}, bf16[256,512]{1,0:T(8,128)(2,1)S(1)}, u32[]{:S(2)}, u32[]{:S(2)}) collective-permute-start(bf16[256,512]{1,0:T(8,128)(2,1)S(1)} %collective-permute-done.12.refs_6_), channel_id=1, source_target_pairs={{0,16},{16,24},{24,8},{8,0},{1,17},{17,25},{25,9},{9,1},{2,18},{18... | collective-permute-start | bytes 786440 | tf_op jit(solution)/shard_map/ppermute | solution.py:478
  85.3 13.2 %collective-permute-start.18 = (bf16[64,1024]{1,0:T(8,128)(2,1)S(1)}, bf16[64,1024]{1,0:T(8,128)(2,1)S(1)}, u32[]{:S(2)}, u32[]{:S(2)}) collective-permute-start(bf16[64,1024]{1,0:T(8,128)(2,1)S(1)} %add_convert_fusion.1), channel_id=1, source_target_pairs={{0,8},{8,0},{16,24},{24,16},{1,9},{9,1},{17,25},{25,17},{2,10},{10... | collective-permute-start | bytes 393224 | tf_op jit(solution)/shard_map/ppermute | solution.py:376
  85.4 20.6 %collective-permute-start.20 = (bf16[512,512]{1,0:T(8,128)(2,1)}, bf16[512,512]{1,0:T(8,128)(2,1)S(1)}, u32[]{:S(2)}, u32[]{:S(2)}) collective-permute-start(bf16[512,512]{1,0:T(8,128)(2,1)} %get-tuple-element.96), channel_id=1, source_target_pairs={{0,1},{1,0},{2,3},{3,2},{4,5},{5,4},{6,7},{7,6},{8,9},{9,8},{10,11... | collective-permute-start | bytes 1572872 | tf_op jit(solution)/shard_map/ppermute | solution.py:376
  96.5 14.8 %collective-permute-start.23 = (bf16[512,512]{1,0:T(8,128)(2,1)}, bf16[512,512]{1,0:T(8,128)(2,1)S(1)}, u32[]{:S(2)}, u32[]{:S(2)}) collective-permute-start(bf16[512,512]{1,0:T(8,128)(2,1)} %get-tuple-element.101), channel_id=1, source_target_pairs={{0,1},{1,0},{2,3},{3,2},{4,5},{5,4},{6,7},{7,6},{8,9},{9,8},{10,11... | collective-permute-start | bytes 1572872 | tf_op jit(solution)/shard_map/ppermute | solution.py:376
  98.6 7.3 %collective-permute-start.21 = (bf16[64,1024]{1,0:T(8,128)(2,1)S(1)}, bf16[64,1024]{1,0:T(8,128)(2,1)S(1)}, u32[]{:S(2)}, u32[]{:S(2)}) collective-permute-start(bf16[64,1024]{1,0:T(8,128)(2,1)S(1)} %add_convert_fusion), channel_id=1, source_target_pairs={{0,16},{8,24},{16,0},{24,8},{1,17},{9,25},{17,1},{25,9},{2,18},{10... | collective-permute-start | bytes 393224 | tf_op jit(solution)/shard_map/ppermute | solution.py:376
  106.0 6.9 %collective-permute-start.22 = (bf16[64,1024]{1,0:T(8,128)(2,1)S(1)}, bf16[64,1024]{1,0:T(8,128)(2,1)S(1)}, u32[]{:S(2)}, u32[]{:S(2)}) collective-permute-start(bf16[64,1024]{1,0:T(8,128)(2,1)S(1)} %convert_add_fusion), channel_id=1, source_target_pairs={{0,1},{1,0},{2,3},{3,2},{4,5},{5,4},{6,7},{7,6},{8,9},{9,8},{10,11... | collective-permute-start | bytes 393224 | tf_op jit(solution)/shard_map/ppermute | solution.py:376
  (14 other events, 65.9 us)

commit v21 on v12

--- a/solution.py
+++ b/solution.py
@@ -13,7 +13,7 @@
 f32, bf16 = jnp.float32, jnp.bfloat16
 lanes = 512
 turn = 256
-vmem_bytes = 58 * 1024 * 1024
+vmem_bytes = 46 * 1024 * 1024
 
 
 def analysis_table(size, positions):

time: 113 us -> 109 us (0.965); the launches traced: 113 us -> 108 us
  Pallas kernels: 34.9 us -> 23 us
  starting transfers between devices: 35.6 us -> 44 us
  waiting for transfers between devices: 27.9 us -> 23.3 us
  other arithmetic: 5.48 us -> 6.96 us
  local copies, waits for them, and re-layouts: 8.05 us -> 9.27 us
    ppermute x6, starting transfers between devices: 14.4 us -> 20.9 us  [ring_step(): pieces.append(lax.ppermute(pieces[-1], 'seq', ring))]
    pallas_call x3, Pallas kernels: 16 us -> 10.6 us  [local_call(): pl.pallas_call(kernel, in_specs=[pl.BlockSpec(memory_space=pltpu.SMEM)] +...]
    ppermute x7, waiting for transfers between devices: 7.8 us -> 2.65 us  [swap_pairs(): return lax.ppermute(value, axis, [(i, i ^ distance) for i in range(count)])]
    pallas_call x3, Pallas kernels: 16.8 us -> 12.1 us  [by_channel(): pl.pallas_call(kernel, in_specs=[pl.BlockSpec(memory_space=pl.ANY)] * (n_...]
    ppermute x2, starting transfers between devices: 2.37 us -> 5.37 us  [per_device(): lax.ppermute(after(cot, prior) if turn else cot, ('tp', 'dp'), route)]
    ppermute x1, waiting for transfers between devices: 2.76 us -> 0.01 us  [per_device(): prior = lax.ppermute(tail, 'seq', [(i, i + 1) for i in range(n_seq - 1)])]
    ppermute x2, starting transfers between devices: 2.88 us -> 0.62 us  [per_device(): theirs = [lax.ppermute(r, ('tp', 'dp'), route) for r in rounds]]
    ppermute x3, waiting for transfers between devices: 2.1 us -> 3.96 us  [per_device(): lax.ppermute(value, 'tp', [(t, t ^ flip) for t in range(n_tp)])]
  transfers between devices with their start and end apart: 24 -> 24, of which waited for: 10 -> 9; matrix products, arithmetic and copies ran while one was open for 5% -> 6% of each run, Pallas kernels for 31% -> 21%
where the time goes in v21:
time: 109 us; the launch traced here: 108 us
  starting transfers between devices  44 us (40%)
  waiting for transfers between devices  23.3 us (21%)
  Pallas kernels  23 us (21%)
  local copies, waits for them, and re-layouts  9.27 us (9%)
  other arithmetic  6.96 us (6%)
    ppermute x6, starting transfers between devices, ring_step(): pieces.append(lax.ppermute(pieces[-1], 'seq', ring))  20.9 us
    ppermute x6, waiting for transfers between devices, ring_step(): pieces.append(lax.ppermute(pieces[-1], 'seq', ring))  13.1 us
    pallas_call x3, Pallas kernels, by_channel(): pl.pallas_call(kernel, in_specs=[pl.BlockSpec(memory_space=pl.ANY)] * (n_...  12.1 us
    pallas_call x3, Pallas kernels, local_call(): pl.pallas_call(kernel, in_specs=[pl.BlockSpec(memory_space=pltpu.SMEM)] +...  10.6 us
    unnamed x45, local copies, waits for them, and re-layouts  7.99 us
    ppermute x1, starting transfers between devices, per_device(): prior = lax.ppermute(tail, 'seq', [(i, i + 1) for i in range(n_seq - 1)])  7.09 us
    ppermute x7, starting transfers between devices, swap_pairs(): return lax.ppermute(value, axis, [(i, i ^ distance) for i in range(count)])  6.26 us
    ppermute x2, starting transfers between devices, per_device(): lax.ppermute(after(cot, prior) if turn else cot, ('tp', 'dp'), route)  5.37 us
  transfers between devices with their start and end apart: 24, of which 9 were waited for; matrix products, arithmetic and copies ran while one was open for 6% of the time, Pallas kernels for 21%

profile of v21, /device:TPU:0, one launch (start us, length us, event | category | flops | bytes accessed | tf_op | source)
XLA Modules:
  0.0 107.5 jit_solution(6663078059788947845)
XLA Ops:
  0.7 1.2 %fusion = bf16[128,1024]{1,0:T(8,128)(2,1)S(1)} fusion(bf16[1,256,1024]{2,1,0:T(8,128)(2,1)} %param.12, bf16[1,256,1024]{2,1,0:T(8,128)(2,1)} %param.11), kind=kLoop, calls=%fused_computation.6 | loop fusion | flops 524288 | bytes 786432 | tf_op jit(solution)/shard_map/convert_element_type | solution.py:409
  2.7 7.1 %collective-permute-start = (bf16[128,1024]{1,0:T(8,128)(2,1)S(1)}, bf16[128,1024]{1,0:T(8,128)(2,1)S(1)}, u32[]{:S(2)}, u32[]{:S(2)}) collective-permute-start(bf16[128,1024]{1,0:T(8,128)(2,1)S(1)} %fusion), channel_id=1, source_target_pairs={{0,8},{8,16},{16,24},{1,9},{9,17},{17,25},{2,10},{10,18},{18,26},{... | collective-permute-start | bytes 786440 | tf_op jit(solution)/shard_map/ppermute | solution.py:411
  9.8 5.4 %collective-permute-start.4 = (bf16[256,1024]{1,0:T(8,128)(2,1)}, bf16[256,1024]{1,0:T(8,128)(2,1)}, u32[]{:S(2)}, u32[]{:S(2)}) collective-permute-start(bf16[256,1024]{1,0:T(8,128)(2,1)} %bitcast.30), channel_id=1, source_target_pairs={{0,0},{1,4},{2,2},{3,6},{4,1},{5,5},{6,3},{7,7},{8,8},{9,12},{10,1... | collective-permute-start | bytes 1572872 | tf_op jit(solution)/shard_map/ppermute | solution.py:420
  15.1 1.9 %broadcast_select_fusion = bf16[256,1024]{1,0:T(8,128)(2,1)} fusion(bf16[256,1024]{1,0:T(8,128)(2,1)S(1)} %collective-permute-done.1, bf16[256,1024]{1,0:T(8,128)(2,1)} %bitcast.32, pred[]{:T(512)S(6)} %gt.3), kind=kLoop, calls=%fused_computation.5 | loop fusion | flops 262144 | bytes 1572865 | tf_op jit(solution)/shard_map/jit(_where)/select_n | solution.py:439
  17.1 1.7 %collective-permute-start.2 = (bf16[256,1024]{1,0:T(8,128)(2,1)}, bf16[256,1024]{1,0:T(8,128)(2,1)S(1)}, u32[]{:S(2)}, u32[]{:S(2)}) collective-permute-start(bf16[256,1024]{1,0:T(8,128)(2,1)} %broadcast_select_fusion), channel_id=1, source_target_pairs={{0,0},{2,16},{4,12},{6,28},{8,24},{10,8},{12,20},{14,4},{16,2},{18... | collective-permute-start | bytes 1572872 | tf_op jit(solution)/shard_map/ppermute | solution.py:445
  19.6 1.0 copy-done.5
  20.7 3.4 %shard_map.145 = (f32[256,1024]{1,0:T(8,128)S(1)}, bf16[256,512]{1,0:T(8,128)(2,1)S(1)}, bf16[256,512]{1,0:T(8,128)(2,1)S(1)}) custom-call(bf16[768,384]{1,0:T(8,128)(2,1)S(1)} %copy-done.3, bf16[768,384]{1,0:T(8,128)(2,1)S(1)} %copy-done.4, bf16[128,1024]{1,0:T(8,128)(2,1)S(1)} %collective-permute-done.refs_2_.refs_6_, bf16[256,1024]{1,0:T(8,128)(2,1)S(1)} %bitcast.22, ...), custom_call_target="tpu_custom_call" | custom-call | flops 22020096 | bytes 57408 | tf_op jit(solution)/shard_map/pallas_call | solution.py:275
  24.1 3.6 %collective-permute-done.5.second_mine = bf16[256,1024]{1,0:T(8,128)(2,1)} collective-permute-done((bf16[256,1024]{1,0:T(8,128)(2,1)}, bf16[256,1024]{1,0:T(8,128)(2,1)}, u32[]{:S(2)}, u32[]{:S(2)}) %collective-permute-start.5) | collective-permute-done | bytes 524320 | tf_op jit(solution)/shard_map/ppermute | solution.py:420
  28.4 9.8 %collective-permute-start.3 = (bf16[256,512]{1,0:T(8,128)(2,1)S(1)}, bf16[256,512]{1,0:T(8,128)(2,1)S(1)}, u32[]{:S(2)}, u32[]{:S(2)}) collective-permute-start(bf16[256,512]{1,0:T(8,128)(2,1)S(1)} %get-tuple-element.57.refs_4_), channel_id=1, source_target_pairs={{0,16},{16,24},{24,8},{8,0},{1,17},{17,25},{25,9},{9,1},{2,18},{18... | collective-permute-start | bytes 786440 | tf_op jit(solution)/shard_map/ppermute | solution.py:478
  38.5 4.8 %shard_map.147 = (bf16[256,1024]{1,0:T(8,128)(2,1)S(1)}, f32[256,1024]{1,0:T(8,128)S(1)}) custom-call(s32[3]{0:T(128)S(1)} %pad_add_fusion.place_ref, bf16[256,1024]{1,0:T(8,128)(2,1)} %collective-permute-done.4.first_mine, bf16[256,1024]{1,0:T(8,128)(2,1)} %collective-permute-done.5.second_mine, bf16[256,1024]{1,0:T(8,128)(2,1)S(1)} %collective-permute-done.6.first_theirs, ...), custom_call_target="tpu_custom_call" | custom-call | flops 33554432 | bytes 122880 | tf_op jit(solution)/shard_map/pallas_call | solution.py:294
  43.4 1.1 collective-permute-done.3.refs_5_
  44.4 3.4 %collective-permute-start.8 = (bf16[256,512]{1,0:T(8,128)(2,1)S(1)}, bf16[256,512]{1,0:T(8,128)(2,1)S(1)}, u32[]{:S(2)}, u32[]{:S(2)}) collective-permute-start(bf16[256,512]{1,0:T(8,128)(2,1)S(1)} %collective-permute-done.3.refs_5_), channel_id=1, source_target_pairs={{0,16},{16,24},{24,8},{8,0},{1,17},{17,25},{25,9},{9,1},{2,18},{18... | collective-permute-start | bytes 786440 | tf_op jit(solution)/shard_map/ppermute | solution.py:478
  48.6 4.0 %collective-permute-done.15.refs_2_ = bf16[1024,256]{1,0:T(8,128)(2,1)S(1)} collective-permute-done((bf16[1024,256]{1,0:T(8,128)(2,1)S(1)}, bf16[1024,256]{1,0:T(8,128)(2,1)S(1)}, u32[]{:S(2)}, u32[]{:S(2)}) %collective-permute-start.15) | collective-permute-done | bytes 524320 | tf_op jit(solution)/shard_map/ppermute | solution.py:503
  52.6 1.9 %collective-permute-done.8.refs_6_ = bf16[256,512]{1,0:T(8,128)(2,1)S(1)} collective-permute-done((bf16[256,512]{1,0:T(8,128)(2,1)S(1)}, bf16[256,512]{1,0:T(8,128)(2,1)S(1)}, u32[]{:S(2)}, u32[]{:S(2)}) %collective-permute-start.8) | collective-permute-done | bytes 262176 | tf_op jit(solution)/shard_map/ppermute | solution.py:478
  54.5 4.4 %collective-permute-done.9.refs_5_ = bf16[256,512]{1,0:T(8,128)(2,1)S(1)} collective-permute-done((bf16[256,512]{1,0:T(8,128)(2,1)S(1)}, bf16[256,512]{1,0:T(8,128)(2,1)S(1)}, u32[]{:S(2)}, u32[]{:S(2)}) %collective-permute-start.9) | collective-permute-done | bytes 262176 | tf_op jit(solution)/shard_map/ppermute | solution.py:478
  58.9 3.4 %collective-permute-start.11 = (bf16[256,512]{1,0:T(8,128)(2,1)S(1)}, bf16[256,512]{1,0:T(8,128)(2,1)}, u32[]{:S(2)}, u32[]{:S(2)}) collective-permute-start(bf16[256,512]{1,0:T(8,128)(2,1)S(1)} %collective-permute-done.9.refs_5_), channel_id=1, source_target_pairs={{0,16},{16,24},{24,8},{8,0},{1,17},{17,25},{25,9},{9,1},{2,18},{18... | collective-permute-start | bytes 786440 | tf_op jit(solution)/shard_map/ppermute | solution.py:478
  62.4 3.9 %shard_map.148 = (bf16[256,1024]{1,0:T(8,128)(2,1)}, bf16[256,1024]{1,0:T(8,128)(2,1)S(1)}, bf16[128,1024]{1,0:T(8,128)(2,1)}, bf16[64,1024]{1,0:T(8,128)(2,1)S(1)}, f32[64,1024]{1,0:T(8,128)S(1)}) custom-call(bf16[768,384]{1,0:T(8,128)(2,1)S(1)} %copy-done.3, bf16[768,384]{1,0:T(8,128)(2,1)S(1)} %copy-done.4, f32[256,1024]{1,0:T(8,128)S(1)} %get-tuple-element.71.refs_2_, ...), custom_call_target="tpu_custom_call" | custom-call | flops 20447232 | bytes 96320 | tf_op jit(solution)/shard_map/pallas_call | solution.py:275
  67.1 2.0 %collective-permute-done.11.refs_6_ = bf16[256,512]{1,0:T(8,128)(2,1)} collective-permute-done((bf16[256,512]{1,0:T(8,128)(2,1)S(1)}, bf16[256,512]{1,0:T(8,128)(2,1)}, u32[]{:S(2)}, u32[]{:S(2)}) %collective-permute-start.11) | collective-permute-done | bytes 262176 | tf_op jit(solution)/shard_map/ppermute | solution.py:478
  69.1 1.3 %collective-permute-start.12 = (bf16[128,1024]{1,0:T(8,128)(2,1)}, bf16[128,1024]{1,0:T(8,128)(2,1)}, u32[]{:S(2)}, u32[]{:S(2)}) collective-permute-start(bf16[128,1024]{1,0:T(8,128)(2,1)} %get-tuple-element.79), channel_id=1, source_target_pairs={{8,0},{16,8},{24,16},{9,1},{17,9},{25,17},{10,2},{18,10},{26,18},{... | collective-permute-start | bytes 786440 | tf_op jit(solution)/shard_map/ppermute | solution.py:540
  70.4 4.3 %collective-permute-start.19 = (bf16[256,512]{1,0:T(8,128)(2,1)}, bf16[256,512]{1,0:T(8,128)(2,1)}, u32[]{:S(2)}, u32[]{:S(2)}) collective-permute-start(bf16[256,512]{1,0:T(8,128)(2,1)} %collective-permute-done.11.refs_6_), channel_id=1, source_target_pairs={{0,16},{16,24},{24,8},{8,0},{1,17},{17,25},{25,9},{9,1},{2,18},{18... | collective-permute-start | bytes 786440 | tf_op jit(solution)/shard_map/ppermute | solution.py:478
  74.7 2.4 %shard_map.149 = (bf16[512,512]{1,0:T(8,128)(2,1)S(1)}, f32[512,512]{1,0:T(8,128)S(1)}) custom-call(s32[5]{0:T(128)S(1)} %pad_add_fusion.1.place_ref, bf16[1024,256]{1,0:T(8,128)(2,1)S(1)} %shard_map.146.refs_0_, bf16[1024,256]{1,0:T(8,128)(2,1)S(1)} %collective-permute-done.14.refs_1_, bf16[1024,256]{1,0:T(8,128)(2,1)S(1)} %collective-permute-done.15.refs_2_, ...), custom_call_target="tpu_custom_call" | custom-call | flops 16777216 | bytes 73728 | tf_op jit(solution)/shard_map/pallas_call | solution.py:294
  80.7 3.7 %collective-permute-done.19.refs_7_ = bf16[256,512]{1,0:T(8,128)(2,1)} collective-permute-done((bf16[256,512]{1,0:T(8,128)(2,1)}, bf16[256,512]{1,0:T(8,128)(2,1)}, u32[]{:S(2)}, u32[]{:S(2)}) %collective-permute-start.19) | collective-permute-done | bytes 262176 | tf_op jit(solution)/shard_map/ppermute | solution.py:478
  84.4 1.0 copy-done.7
  85.5 1.0 copy-done.9
  88.4 3.4 %shard_map.150 = (bf16[512,512]{1,0:T(8,128)(2,1)S(1)}, f32[512,512]{1,0:T(8,128)S(1)}) custom-call(s32[5]{0:T(128)S(1)} %pad_add_fusion.1.place_ref, bf16[1024,256]{1,0:T(8,128)(2,1)S(1)} %shard_map.146.refs_0_, bf16[1024,256]{1,0:T(8,128)(2,1)S(1)} %copy-done.7, bf16[1024,256]{1,0:T(8,128)(2,1)S(1)} %collective-permute-done.15.refs_2_, ...), custom_call_target="tpu_custom_call" | custom-call | flops 16777216 | bytes 73728 | tf_op jit(solution)/shard_map/pallas_call | solution.py:294
  92.6 1.0 add_convert_fusion
  93.7 4.8 %shard_map.151 = (bf16[256,1024]{1,0:T(8,128)(2,1)}, bf16[256,1024]{1,0:T(8,128)(2,1)}) custom-call(bf16[768,384]{1,0:T(8,128)(2,1)S(1)} %copy-done.3, bf16[768,384]{1,0:T(8,128)(2,1)S(1)} %copy-done.4, bf16[256,1024]{1,0:T(8,128)(2,1)S(1)} %copy-done.20, bf16[128,1024]{1,0:T(8,128)(2,1)} %collective-permute-done.12.refs_3_, ...), custom_call_target="tpu_custom_call" | custom-call | flops 5637144576 | bytes 49216 | tf_op jit(solution)/shard_map/pallas_call | solution.py:275
  98.5 1.0 collective-permute-done.21
  99.6 2.8 %collective-permute-start.22 = (bf16[64,1024]{1,0:T(8,128)(2,1)S(1)}, bf16[64,1024]{1,0:T(8,128)(2,1)S(1)}, u32[]{:S(2)}, u32[]{:S(2)}) collective-permute-start(bf16[64,1024]{1,0:T(8,128)(2,1)S(1)} %convert_add_fusion), channel_id=1, source_target_pairs={{0,1},{1,0},{2,3},{3,2},{4,5},{5,4},{6,7},{7,6},{8,9},{9,8},{10,11... | collective-permute-start | bytes 393224 | tf_op jit(solution)/shard_map/ppermute | solution.py:376
  102.5 1.6 %collective-permute-done.23 = bf16[512,512]{1,0:T(8,128)(2,1)S(1)} collective-permute-done((bf16[512,512]{1,0:T(8,128)(2,1)S(1)}, bf16[512,512]{1,0:T(8,128)(2,1)S(1)}, u32[]{:S(2)}, u32[]{:S(2)}) %collective-permute-start.23) | collective-permute-done | bytes 524320 | tf_op jit(solution)/shard_map/ppermute | solution.py:376
  104.4 1.5 %pad_maximum_fusion = f32[512,1024]{1,0:T(8,128)} fusion(f32[512,512]{1,0:T(8,128)S(1)} %add_multiply_fusion, f32[512,512]{1,0:T(8,128)S(1)} %add_multiply_fusion.1), kind=kLoop, calls=%fused_computation | loop fusion | flops 524288 | bytes 4194304 | tf_op jit(solution)/shard_map/concatenate | solution.py:583
  105.9 1.0 copy.16
  (83 shorter events, 11.7 us)
Async XLA Ops:
  0.6 19.0 %copy-start.3 = (bf16[768,384]{1,0:T(8,128)(2,1)S(1)}, bf16[768,384]{1,0:T(8,128)(2,1)}, u32[]{:S(2)}) copy-start(bf16[768,384]{1,0:T(8,128)(2,1)} %constant.66.clone.refs_0_) | copy-start | bytes 1769476
  0.6 18.9 %copy-start.4 = (bf16[768,384]{1,0:T(8,128)(2,1)S(1)}, bf16[768,384]{1,0:T(8,128)(2,1)}, u32[]{:S(2)}) copy-start(bf16[768,384]{1,0:T(8,128)(2,1)} %constant.67.clone.refs_1_) | copy-start | bytes 1769476
  0.7 18.9 %copy-start.1 = (bf16[1,256,1024]{2,1,0:T(8,128)(2,1)S(1)}, bf16[1,256,1024]{2,1,0:T(8,128)(2,1)}, u32[]{:S(2)}) copy-start(bf16[1,256,1024]{2,1,0:T(8,128)(2,1)} %param.12) | copy-start | bytes 1572868
  0.7 18.9 %copy-start.2 = (bf16[1,256,1024]{2,1,0:T(8,128)(2,1)S(1)}, bf16[1,256,1024]{2,1,0:T(8,128)(2,1)}, u32[]{:S(2)}) copy-start(bf16[1,256,1024]{2,1,0:T(8,128)(2,1)} %param.11) | copy-start | bytes 1572868
  0.7 18.9 %copy-start.12 = (bf16[1024,128]{1,0:T(8,128)(2,1)S(1)}, bf16[1024,128]{1,0:T(8,128)(2,1)}, u32[]{:S(2)}) copy-start(bf16[1024,128]{1,0:T(8,128)(2,1)} %refs_4_.1) | copy-start | bytes 786436
  0.7 18.9 %copy-start.18 = (f32[1024]{0:T(1024)S(1)}, f32[1024]{0:T(1024)}, u32[]{:S(2)}) copy-start(f32[1024]{0:T(1024)} %param.14) | copy-start | bytes 12292
  2.0 13.2 %collective-permute-start.1 = (bf16[256,1024]{1,0:T(8,128)(2,1)}, bf16[256,1024]{1,0:T(8,128)(2,1)S(1)}, u32[]{:S(2)}, u32[]{:S(2)}) collective-permute-start(bf16[256,1024]{1,0:T(8,128)(2,1)} %bitcast.29), channel_id=1, source_target_pairs={{2,4},{4,2},{8,14},{14,8},{18,20},{20,18},{24,30},{30,24},{3,5},{5... | collective-permute-start | bytes 1572872 | tf_op jit(solution)/shard_map/ppermute | solution.py:433
  2.7 12.5 %collective-permute-start = (bf16[128,1024]{1,0:T(8,128)(2,1)S(1)}, bf16[128,1024]{1,0:T(8,128)(2,1)S(1)}, u32[]{:S(2)}, u32[]{:S(2)}) collective-permute-start(bf16[128,1024]{1,0:T(8,128)(2,1)S(1)} %fusion), channel_id=1, source_target_pairs={{0,8},{8,16},{16,24},{1,9},{9,17},{17,25},{2,10},{10,18},{18,26},{... | collective-permute-start | bytes 786440 | tf_op jit(solution)/shard_map/ppermute | solution.py:411
  9.8 14.4 %collective-permute-start.4 = (bf16[256,1024]{1,0:T(8,128)(2,1)}, bf16[256,1024]{1,0:T(8,128)(2,1)}, u32[]{:S(2)}, u32[]{:S(2)}) collective-permute-start(bf16[256,1024]{1,0:T(8,128)(2,1)} %bitcast.30), channel_id=1, source_target_pairs={{0,0},{1,4},{2,2},{3,6},{4,1},{5,5},{6,3},{7,7},{8,8},{9,12},{10,1... | collective-permute-start | bytes 1572872 | tf_op jit(solution)/shard_map/ppermute | solution.py:420
  15.1 12.6 %collective-permute-start.5 = (bf16[256,1024]{1,0:T(8,128)(2,1)}, bf16[256,1024]{1,0:T(8,128)(2,1)}, u32[]{:S(2)}, u32[]{:S(2)}) collective-permute-start(bf16[256,1024]{1,0:T(8,128)(2,1)} %bitcast.31), channel_id=1, source_target_pairs={{0,4},{1,0},{2,6},{3,2},{4,5},{5,1},{6,7},{7,3},{8,12},{9,8},{10,1... | collective-permute-start | bytes 1572872 | tf_op jit(solution)/shard_map/ppermute | solution.py:420
  17.1 11.3 %collective-permute-start.2 = (bf16[256,1024]{1,0:T(8,128)(2,1)}, bf16[256,1024]{1,0:T(8,128)(2,1)S(1)}, u32[]{:S(2)}, u32[]{:S(2)}) collective-permute-start(bf16[256,1024]{1,0:T(8,128)(2,1)} %broadcast_select_fusion), channel_id=1, source_target_pairs={{0,0},{2,16},{4,12},{6,28},{8,24},{10,8},{12,20},{14,4},{16,2},{18... | collective-permute-start | bytes 1572872 | tf_op jit(solution)/shard_map/ppermute | solution.py:445
  20.7 17.8 %copy-start = (bf16[1024,2048]{1,0:T(8,128)(2,1)S(1)}, bf16[1024,2048]{1,0:T(8,128)(2,1)}, u32[]{:S(2)}) copy-start(bf16[1024,2048]{1,0:T(8,128)(2,1)} %weight.1) | copy-start | bytes 12582916
  24.1 24.5 %copy-start.14 = (bf16[256,512]{1,0:T(8,128)(2,1)}, bf16[256,512]{1,0:T(8,128)(2,1)S(1)}, u32[]{:S(2)}) copy-start(bf16[256,512]{1,0:T(8,128)(2,1)S(1)} %get-tuple-element.69.refs_4_) | copy-start | bytes 786436
  27.8 10.7 %collective-permute-start.6 = (bf16[256,1024]{1,0:T(8,128)(2,1)}, bf16[256,1024]{1,0:T(8,128)(2,1)S(1)}, u32[]{:S(2)}, u32[]{:S(2)}) collective-permute-start(bf16[256,1024]{1,0:T(8,128)(2,1)} %collective-permute-done.4.first_mine), channel_id=1, source_target_pairs={{0,2},{1,3},{2,0},{3,1},{4,6},{5,7},{6,4},{7,5},{8,10},{9,11},{10,... | collective-permute-start | bytes 1572872 | tf_op jit(solution)/shard_map/ppermute | solution.py:487
  28.3 10.2 %collective-permute-start.7 = (bf16[256,1024]{1,0:T(8,128)(2,1)}, bf16[256,1024]{1,0:T(8,128)(2,1)S(1)}, u32[]{:S(2)}, u32[]{:S(2)}) collective-permute-start(bf16[256,1024]{1,0:T(8,128)(2,1)} %collective-permute-done.5.second_mine), channel_id=1, source_target_pairs={{0,2},{1,3},{2,0},{3,1},{4,6},{5,7},{6,4},{7,5},{8,10},{9,11},{10,... | collective-permute-start | bytes 1572872 | tf_op jit(solution)/shard_map/ppermute | solution.py:487
  28.4 16.0 %collective-permute-start.3 = (bf16[256,512]{1,0:T(8,128)(2,1)S(1)}, bf16[256,512]{1,0:T(8,128)(2,1)S(1)}, u32[]{:S(2)}, u32[]{:S(2)}) collective-permute-start(bf16[256,512]{1,0:T(8,128)(2,1)S(1)} %get-tuple-element.57.refs_4_), channel_id=1, source_target_pairs={{0,16},{16,24},{24,8},{8,0},{1,17},{17,25},{25,9},{9,1},{2,18},{18... | collective-permute-start | bytes 786440 | tf_op jit(solution)/shard_map/ppermute | solution.py:478
  38.4 14.2 %collective-permute-start.15 = (bf16[1024,256]{1,0:T(8,128)(2,1)S(1)}, bf16[1024,256]{1,0:T(8,128)(2,1)S(1)}, u32[]{:S(2)}, u32[]{:S(2)}) collective-permute-start(bf16[1024,256]{1,0:T(8,128)(2,1)S(1)} %shard_map.146.refs_0_), channel_id=1, source_target_pairs={{0,4},{2,6},{4,0},{6,2},{1,5},{3,7},{5,1},{7,3},{8,12},{10,14},{12... | collective-permute-start | bytes 1572872 | tf_op jit(solution)/shard_map/ppermute | solution.py:503
  44.4 10.1 %collective-permute-start.8 = (bf16[256,512]{1,0:T(8,128)(2,1)S(1)}, bf16[256,512]{1,0:T(8,128)(2,1)S(1)}, u32[]{:S(2)}, u32[]{:S(2)}) collective-permute-start(bf16[256,512]{1,0:T(8,128)(2,1)S(1)} %collective-permute-done.3.refs_5_), channel_id=1, source_target_pairs={{0,16},{16,24},{24,8},{8,0},{1,17},{17,25},{25,9},{9,1},{2,18},{18... | collective-permute-start | bytes 786440 | tf_op jit(solution)/shard_map/ppermute | solution.py:478
  47.8 14.6 %collective-permute-start.10 = (bf16[256,1024]{1,0:T(8,128)(2,1)S(1)}, bf16[256,1024]{1,0:T(8,128)(2,1)S(1)}, u32[]{:S(2)}, u32[]{:S(2)}) collective-permute-start(bf16[256,1024]{1,0:T(8,128)(2,1)S(1)} %get-tuple-element.67), channel_id=1, source_target_pairs={{0,1},{1,0},{2,3},{3,2},{4,5},{5,4},{6,7},{7,6},{8,9},{9,8},{10,11... | collective-permute-start | bytes 1572872 | tf_op jit(solution)/shard_map/ppermute | solution.py:376
  48.6 10.3 %collective-permute-start.9 = (bf16[256,512]{1,0:T(8,128)(2,1)S(1)}, bf16[256,512]{1,0:T(8,128)(2,1)S(1)}, u32[]{:S(2)}, u32[]{:S(2)}) collective-permute-start(bf16[256,512]{1,0:T(8,128)(2,1)S(1)} %get-tuple-element.69.refs_4_), channel_id=1, source_target_pairs={{0,16},{16,24},{24,8},{8,0},{1,17},{17,25},{25,9},{9,1},{2,18},{18... | collective-permute-start | bytes 786440 | tf_op jit(solution)/shard_map/ppermute | solution.py:478
  48.6 21.7 %collective-permute-start.14 = (bf16[1024,256]{1,0:T(8,128)(2,1)S(1)}, bf16[1024,256]{1,0:T(8,128)(2,1)S(1)}, u32[]{:S(2)}, u32[]{:S(2)}) collective-permute-start(bf16[1024,256]{1,0:T(8,128)(2,1)S(1)} %shard_map.146.refs_0_), channel_id=1, source_target_pairs={{0,2},{2,0},{4,6},{6,4},{1,3},{3,1},{5,7},{7,5},{8,10},{10,8},{12,... | collective-permute-start | bytes 1572872 | tf_op jit(solution)/shard_map/ppermute | solution.py:503
  54.5 20.2 %collective-permute-start.16 = (bf16[1024,256]{1,0:T(8,128)(2,1)S(1)}, bf16[1024,256]{1,0:T(8,128)(2,1)S(1)}, u32[]{:S(2)}, u32[]{:S(2)}) collective-permute-start(bf16[1024,256]{1,0:T(8,128)(2,1)S(1)} %collective-permute-done.15.refs_2_), channel_id=1, source_target_pairs={{0,2},{2,0},{4,6},{6,4},{1,3},{3,1},{5,7},{7,5},{8,10},{10,8},{12,... | collective-permute-start | bytes 1572872 | tf_op jit(solution)/shard_map/ppermute | solution.py:503
  58.9 10.1 %collective-permute-start.11 = (bf16[256,512]{1,0:T(8,128)(2,1)S(1)}, bf16[256,512]{1,0:T(8,128)(2,1)}, u32[]{:S(2)}, u32[]{:S(2)}) collective-permute-start(bf16[256,512]{1,0:T(8,128)(2,1)S(1)} %collective-permute-done.9.refs_5_), channel_id=1, source_target_pairs={{0,16},{16,24},{24,8},{8,0},{1,17},{17,25},{25,9},{9,1},{2,18},{18... | collective-permute-start | bytes 786440 | tf_op jit(solution)/shard_map/ppermute | solution.py:478
  62.3 12.4 %collective-permute-start.17 = (bf16[256,512]{1,0:T(8,128)(2,1)S(1)}, bf16[256,512]{1,0:T(8,128)(2,1)S(1)}, u32[]{:S(2)}, u32[]{:S(2)}) collective-permute-start(bf16[256,512]{1,0:T(8,128)(2,1)S(1)} %collective-permute-done.8.refs_6_), channel_id=1, source_target_pairs={{0,16},{16,24},{24,8},{8,0},{1,17},{17,25},{25,9},{9,1},{2,18},{18... | collective-permute-start | bytes 786440 | tf_op jit(solution)/shard_map/ppermute | solution.py:478
  66.3 12.7 %collective-permute-start.13 = (bf16[64,1024]{1,0:T(8,128)(2,1)S(1)}, bf16[64,1024]{1,0:T(8,128)(2,1)S(1)}, u32[]{:S(2)}, u32[]{:S(2)}) collective-permute-start(bf16[64,1024]{1,0:T(8,128)(2,1)S(1)} %get-tuple-element.81), channel_id=1, source_target_pairs={{0,1},{1,0},{2,3},{3,2},{4,5},{5,4},{6,7},{7,6},{8,9},{9,8},{10,11... | collective-permute-start | bytes 393224 | tf_op jit(solution)/shard_map/ppermute | solution.py:376
  69.1 23.5 %collective-permute-start.12 = (bf16[128,1024]{1,0:T(8,128)(2,1)}, bf16[128,1024]{1,0:T(8,128)(2,1)}, u32[]{:S(2)}, u32[]{:S(2)}) collective-permute-start(bf16[128,1024]{1,0:T(8,128)(2,1)} %get-tuple-element.79), channel_id=1, source_target_pairs={{8,0},{16,8},{24,16},{9,1},{17,9},{25,17},{10,2},{18,10},{26,18},{... | collective-permute-start | bytes 786440 | tf_op jit(solution)/shard_map/ppermute | solution.py:540
  70.4 14.0 %collective-permute-start.19 = (bf16[256,512]{1,0:T(8,128)(2,1)}, bf16[256,512]{1,0:T(8,128)(2,1)}, u32[]{:S(2)}, u32[]{:S(2)}) collective-permute-start(bf16[256,512]{1,0:T(8,128)(2,1)} %collective-permute-done.11.refs_6_), channel_id=1, source_target_pairs={{0,16},{16,24},{24,8},{8,0},{1,17},{17,25},{25,9},{9,1},{2,18},{18... | collective-permute-start | bytes 786440 | tf_op jit(solution)/shard_map/ppermute | solution.py:478
  79.8 12.8 %collective-permute-start.18 = (bf16[64,1024]{1,0:T(8,128)(2,1)}, bf16[64,1024]{1,0:T(8,128)(2,1)}, u32[]{:S(2)}, u32[]{:S(2)}) collective-permute-start(bf16[64,1024]{1,0:T(8,128)(2,1)} %add_convert_fusion.1), channel_id=1, source_target_pairs={{0,8},{8,0},{16,24},{24,16},{1,9},{9,1},{17,25},{25,17},{2,10},{10... | collective-permute-start | bytes 393224 | tf_op jit(solution)/shard_map/ppermute | solution.py:376
  79.8 19.8 %collective-permute-start.20 = (bf16[512,512]{1,0:T(8,128)(2,1)}, bf16[512,512]{1,0:T(8,128)(2,1)S(1)}, u32[]{:S(2)}, u32[]{:S(2)}) collective-permute-start(bf16[512,512]{1,0:T(8,128)(2,1)} %copy-done.21), channel_id=1, source_target_pairs={{0,1},{1,0},{2,3},{3,2},{4,5},{5,4},{6,7},{7,6},{8,9},{9,8},{10,11... | collective-permute-start | bytes 1572872 | tf_op jit(solution)/shard_map/ppermute | solution.py:376
  91.8 12.4 %collective-permute-start.23 = (bf16[512,512]{1,0:T(8,128)(2,1)S(1)}, bf16[512,512]{1,0:T(8,128)(2,1)S(1)}, u32[]{:S(2)}, u32[]{:S(2)}) collective-permute-start(bf16[512,512]{1,0:T(8,128)(2,1)S(1)} %get-tuple-element.99), channel_id=1, source_target_pairs={{0,1},{1,0},{2,3},{3,2},{4,5},{5,4},{6,7},{7,6},{8,9},{9,8},{10,11... | collective-permute-start | bytes 1572872 | tf_op jit(solution)/shard_map/ppermute | solution.py:376
  93.6 5.9 %collective-permute-start.21 = (bf16[64,1024]{1,0:T(8,128)(2,1)S(1)}, bf16[64,1024]{1,0:T(8,128)(2,1)S(1)}, u32[]{:S(2)}, u32[]{:S(2)}) collective-permute-start(bf16[64,1024]{1,0:T(8,128)(2,1)S(1)} %add_convert_fusion), channel_id=1, source_target_pairs={{0,16},{8,24},{16,0},{24,8},{1,17},{9,25},{17,1},{25,9},{2,18},{10... | collective-permute-start | bytes 393224 | tf_op jit(solution)/shard_map/ppermute | solution.py:376
  99.6 6.3 %collective-permute-start.22 = (bf16[64,1024]{1,0:T(8,128)(2,1)S(1)}, bf16[64,1024]{1,0:T(8,128)(2,1)S(1)}, u32[]{:S(2)}, u32[]{:S(2)}) collective-permute-start(bf16[64,1024]{1,0:T(8,128)(2,1)S(1)} %convert_add_fusion), channel_id=1, source_target_pairs={{0,1},{1,0},{2,3},{3,2},{4,5},{5,4},{6,7},{7,6},{8,9},{9,8},{10,11... | collective-permute-start | bytes 393224 | tf_op jit(solution)/shard_map/ppermute | solution.py:376
  (14 other events, 59.5 us)

commit v22 on v21

--- a/solution.py
+++ b/solution.py
@@ -13,7 +13,7 @@
 f32, bf16 = jnp.float32, jnp.bfloat16
 lanes = 512
 turn = 256
-vmem_bytes = 46 * 1024 * 1024
+vmem_bytes = 20 * 1024 * 1024
 
 
 def analysis_table(size, positions):

time: 109 us -> 109 us (level)
  no operation moved by 1% of the time
where the time goes in v22:
time: 109 us; the launch traced here: 108 us
  starting transfers between devices  44 us (40%)
  waiting for transfers between devices  23.3 us (21%)
  Pallas kernels  23 us (21%)
  local copies, waits for them, and re-layouts  9.27 us (9%)
  other arithmetic  6.96 us (6%)
    ppermute x6, starting transfers between devices, ring_step(): pieces.append(lax.ppermute(pieces[-1], 'seq', ring))  20.9 us
    ppermute x6, waiting for transfers between devices, ring_step(): pieces.append(lax.ppermute(pieces[-1], 'seq', ring))  13.1 us
    pallas_call x3, Pallas kernels, by_channel(): pl.pallas_call(kernel, in_specs=[pl.BlockSpec(memory_space=pl.ANY)] * (n_...  12.1 us
    pallas_call x3, Pallas kernels, local_call(): pl.pallas_call(kernel, in_specs=[pl.BlockSpec(memory_space=pltpu.SMEM)] +...  10.6 us
    unnamed x45, local copies, waits for them, and re-layouts  7.99 us
    ppermute x1, starting transfers between devices, per_device(): prior = lax.ppermute(tail, 'seq', [(i, i + 1) for i in range(n_seq - 1)])  7.09 us
    ppermute x7, starting transfers between devices, swap_pairs(): return lax.ppermute(value, axis, [(i, i ^ distance) for i in range(count)])  6.26 us
    ppermute x2, starting transfers between devices, per_device(): lax.ppermute(after(cot, prior) if turn else cot, ('tp', 'dp'), route)  5.37 us
  transfers between devices with their start and end apart: 24, of which 9 were waited for; matrix products, arithmetic and copies ran while one was open for 6% of the time, Pallas kernels for 21%

profile of v22, /device:TPU:0, one launch (start us, length us, event | category | flops | bytes accessed | tf_op | source)
XLA Modules:
  0.0 107.5 jit_solution(7662809637756179930)
XLA Ops:
  0.7 1.2 %fusion = bf16[128,1024]{1,0:T(8,128)(2,1)S(1)} fusion(bf16[1,256,1024]{2,1,0:T(8,128)(2,1)} %param.12, bf16[1,256,1024]{2,1,0:T(8,128)(2,1)} %param.11), kind=kLoop, calls=%fused_computation.6 | loop fusion | flops 524288 | bytes 786432 | tf_op jit(solution)/shard_map/convert_element_type | solution.py:409
  2.7 7.1 %collective-permute-start = (bf16[128,1024]{1,0:T(8,128)(2,1)S(1)}, bf16[128,1024]{1,0:T(8,128)(2,1)S(1)}, u32[]{:S(2)}, u32[]{:S(2)}) collective-permute-start(bf16[128,1024]{1,0:T(8,128)(2,1)S(1)} %fusion), channel_id=1, source_target_pairs={{0,8},{8,16},{16,24},{1,9},{9,17},{17,25},{2,10},{10,18},{18,26},{... | collective-permute-start | bytes 786440 | tf_op jit(solution)/shard_map/ppermute | solution.py:411
  9.8 5.4 %collective-permute-start.4 = (bf16[256,1024]{1,0:T(8,128)(2,1)}, bf16[256,1024]{1,0:T(8,128)(2,1)}, u32[]{:S(2)}, u32[]{:S(2)}) collective-permute-start(bf16[256,1024]{1,0:T(8,128)(2,1)} %bitcast.30), channel_id=1, source_target_pairs={{0,0},{1,4},{2,2},{3,6},{4,1},{5,5},{6,3},{7,7},{8,8},{9,12},{10,1... | collective-permute-start | bytes 1572872 | tf_op jit(solution)/shard_map/ppermute | solution.py:420
  15.1 1.9 %broadcast_select_fusion = bf16[256,1024]{1,0:T(8,128)(2,1)} fusion(bf16[256,1024]{1,0:T(8,128)(2,1)S(1)} %collective-permute-done.1, bf16[256,1024]{1,0:T(8,128)(2,1)} %bitcast.32, pred[]{:T(512)S(6)} %gt.3), kind=kLoop, calls=%fused_computation.5 | loop fusion | flops 262144 | bytes 1572865 | tf_op jit(solution)/shard_map/jit(_where)/select_n | solution.py:439
  17.1 1.7 %collective-permute-start.2 = (bf16[256,1024]{1,0:T(8,128)(2,1)}, bf16[256,1024]{1,0:T(8,128)(2,1)S(1)}, u32[]{:S(2)}, u32[]{:S(2)}) collective-permute-start(bf16[256,1024]{1,0:T(8,128)(2,1)} %broadcast_select_fusion), channel_id=1, source_target_pairs={{0,0},{2,16},{4,12},{6,28},{8,24},{10,8},{12,20},{14,4},{16,2},{18... | collective-permute-start | bytes 1572872 | tf_op jit(solution)/shard_map/ppermute | solution.py:445
  19.6 1.0 copy-done.5
  20.7 3.4 %shard_map.145 = (f32[256,1024]{1,0:T(8,128)S(1)}, bf16[256,512]{1,0:T(8,128)(2,1)S(1)}, bf16[256,512]{1,0:T(8,128)(2,1)S(1)}) custom-call(bf16[768,384]{1,0:T(8,128)(2,1)S(1)} %copy-done.3, bf16[768,384]{1,0:T(8,128)(2,1)S(1)} %copy-done.4, bf16[128,1024]{1,0:T(8,128)(2,1)S(1)} %collective-permute-done.refs_2_.refs_6_, bf16[256,1024]{1,0:T(8,128)(2,1)S(1)} %bitcast.22, ...), custom_call_target="tpu_custom_call" | custom-call | flops 22020096 | bytes 57408 | tf_op jit(solution)/shard_map/pallas_call | solution.py:275
  24.1 3.6 %collective-permute-done.5.second_mine = bf16[256,1024]{1,0:T(8,128)(2,1)} collective-permute-done((bf16[256,1024]{1,0:T(8,128)(2,1)}, bf16[256,1024]{1,0:T(8,128)(2,1)}, u32[]{:S(2)}, u32[]{:S(2)}) %collective-permute-start.5) | collective-permute-done | bytes 524320 | tf_op jit(solution)/shard_map/ppermute | solution.py:420
  28.4 9.8 %collective-permute-start.3 = (bf16[256,512]{1,0:T(8,128)(2,1)S(1)}, bf16[256,512]{1,0:T(8,128)(2,1)S(1)}, u32[]{:S(2)}, u32[]{:S(2)}) collective-permute-start(bf16[256,512]{1,0:T(8,128)(2,1)S(1)} %get-tuple-element.57.refs_4_), channel_id=1, source_target_pairs={{0,16},{16,24},{24,8},{8,0},{1,17},{17,25},{25,9},{9,1},{2,18},{18... | collective-permute-start | bytes 786440 | tf_op jit(solution)/shard_map/ppermute | solution.py:478
  38.5 4.8 %shard_map.147 = (bf16[256,1024]{1,0:T(8,128)(2,1)S(1)}, f32[256,1024]{1,0:T(8,128)S(1)}) custom-call(s32[3]{0:T(128)S(1)} %pad_add_fusion.place_ref, bf16[256,1024]{1,0:T(8,128)(2,1)} %collective-permute-done.4.first_mine, bf16[256,1024]{1,0:T(8,128)(2,1)} %collective-permute-done.5.second_mine, bf16[256,1024]{1,0:T(8,128)(2,1)S(1)} %collective-permute-done.6.first_theirs, ...), custom_call_target="tpu_custom_call" | custom-call | flops 33554432 | bytes 122880 | tf_op jit(solution)/shard_map/pallas_call | solution.py:294
  43.4 1.1 collective-permute-done.3.refs_5_
  44.4 3.4 %collective-permute-start.8 = (bf16[256,512]{1,0:T(8,128)(2,1)S(1)}, bf16[256,512]{1,0:T(8,128)(2,1)S(1)}, u32[]{:S(2)}, u32[]{:S(2)}) collective-permute-start(bf16[256,512]{1,0:T(8,128)(2,1)S(1)} %collective-permute-done.3.refs_5_), channel_id=1, source_target_pairs={{0,16},{16,24},{24,8},{8,0},{1,17},{17,25},{25,9},{9,1},{2,18},{18... | collective-permute-start | bytes 786440 | tf_op jit(solution)/shard_map/ppermute | solution.py:478
  48.6 4.0 %collective-permute-done.15.refs_2_ = bf16[1024,256]{1,0:T(8,128)(2,1)S(1)} collective-permute-done((bf16[1024,256]{1,0:T(8,128)(2,1)S(1)}, bf16[1024,256]{1,0:T(8,128)(2,1)S(1)}, u32[]{:S(2)}, u32[]{:S(2)}) %collective-permute-start.15) | collective-permute-done | bytes 524320 | tf_op jit(solution)/shard_map/ppermute | solution.py:503
  52.6 1.9 %collective-permute-done.8.refs_6_ = bf16[256,512]{1,0:T(8,128)(2,1)S(1)} collective-permute-done((bf16[256,512]{1,0:T(8,128)(2,1)S(1)}, bf16[256,512]{1,0:T(8,128)(2,1)S(1)}, u32[]{:S(2)}, u32[]{:S(2)}) %collective-permute-start.8) | collective-permute-done | bytes 262176 | tf_op jit(solution)/shard_map/ppermute | solution.py:478
  54.5 4.4 %collective-permute-done.9.refs_5_ = bf16[256,512]{1,0:T(8,128)(2,1)S(1)} collective-permute-done((bf16[256,512]{1,0:T(8,128)(2,1)S(1)}, bf16[256,512]{1,0:T(8,128)(2,1)S(1)}, u32[]{:S(2)}, u32[]{:S(2)}) %collective-permute-start.9) | collective-permute-done | bytes 262176 | tf_op jit(solution)/shard_map/ppermute | solution.py:478
  58.9 3.4 %collective-permute-start.11 = (bf16[256,512]{1,0:T(8,128)(2,1)S(1)}, bf16[256,512]{1,0:T(8,128)(2,1)}, u32[]{:S(2)}, u32[]{:S(2)}) collective-permute-start(bf16[256,512]{1,0:T(8,128)(2,1)S(1)} %collective-permute-done.9.refs_5_), channel_id=1, source_target_pairs={{0,16},{16,24},{24,8},{8,0},{1,17},{17,25},{25,9},{9,1},{2,18},{18... | collective-permute-start | bytes 786440 | tf_op jit(solution)/shard_map/ppermute | solution.py:478
  62.4 3.9 %shard_map.148 = (bf16[256,1024]{1,0:T(8,128)(2,1)}, bf16[256,1024]{1,0:T(8,128)(2,1)S(1)}, bf16[128,1024]{1,0:T(8,128)(2,1)}, bf16[64,1024]{1,0:T(8,128)(2,1)S(1)}, f32[64,1024]{1,0:T(8,128)S(1)}) custom-call(bf16[768,384]{1,0:T(8,128)(2,1)S(1)} %copy-done.3, bf16[768,384]{1,0:T(8,128)(2,1)S(1)} %copy-done.4, f32[256,1024]{1,0:T(8,128)S(1)} %get-tuple-element.71.refs_2_, ...), custom_call_target="tpu_custom_call" | custom-call | flops 20447232 | bytes 96320 | tf_op jit(solution)/shard_map/pallas_call | solution.py:275
  67.1 2.0 %collective-permute-done.11.refs_6_ = bf16[256,512]{1,0:T(8,128)(2,1)} collective-permute-done((bf16[256,512]{1,0:T(8,128)(2,1)S(1)}, bf16[256,512]{1,0:T(8,128)(2,1)}, u32[]{:S(2)}, u32[]{:S(2)}) %collective-permute-start.11) | collective-permute-done | bytes 262176 | tf_op jit(solution)/shard_map/ppermute | solution.py:478
  69.1 1.3 %collective-permute-start.12 = (bf16[128,1024]{1,0:T(8,128)(2,1)}, bf16[128,1024]{1,0:T(8,128)(2,1)}, u32[]{:S(2)}, u32[]{:S(2)}) collective-permute-start(bf16[128,1024]{1,0:T(8,128)(2,1)} %get-tuple-element.79), channel_id=1, source_target_pairs={{8,0},{16,8},{24,16},{9,1},{17,9},{25,17},{10,2},{18,10},{26,18},{... | collective-permute-start | bytes 786440 | tf_op jit(solution)/shard_map/ppermute | solution.py:540
  70.4 4.3 %collective-permute-start.19 = (bf16[256,512]{1,0:T(8,128)(2,1)}, bf16[256,512]{1,0:T(8,128)(2,1)}, u32[]{:S(2)}, u32[]{:S(2)}) collective-permute-start(bf16[256,512]{1,0:T(8,128)(2,1)} %collective-permute-done.11.refs_6_), channel_id=1, source_target_pairs={{0,16},{16,24},{24,8},{8,0},{1,17},{17,25},{25,9},{9,1},{2,18},{18... | collective-permute-start | bytes 786440 | tf_op jit(solution)/shard_map/ppermute | solution.py:478
  74.7 2.4 %shard_map.149 = (bf16[512,512]{1,0:T(8,128)(2,1)S(1)}, f32[512,512]{1,0:T(8,128)S(1)}) custom-call(s32[5]{0:T(128)S(1)} %pad_add_fusion.1.place_ref, bf16[1024,256]{1,0:T(8,128)(2,1)S(1)} %shard_map.146.refs_0_, bf16[1024,256]{1,0:T(8,128)(2,1)S(1)} %collective-permute-done.14.refs_1_, bf16[1024,256]{1,0:T(8,128)(2,1)S(1)} %collective-permute-done.15.refs_2_, ...), custom_call_target="tpu_custom_call" | custom-call | flops 16777216 | bytes 73728 | tf_op jit(solution)/shard_map/pallas_call | solution.py:294
  80.7 3.7 %collective-permute-done.19.refs_7_ = bf16[256,512]{1,0:T(8,128)(2,1)} collective-permute-done((bf16[256,512]{1,0:T(8,128)(2,1)}, bf16[256,512]{1,0:T(8,128)(2,1)}, u32[]{:S(2)}, u32[]{:S(2)}) %collective-permute-start.19) | collective-permute-done | bytes 262176 | tf_op jit(solution)/shard_map/ppermute | solution.py:478
  84.4 1.0 copy-done.7
  85.5 1.0 copy-done.9
  88.4 3.4 %shard_map.150 = (bf16[512,512]{1,0:T(8,128)(2,1)S(1)}, f32[512,512]{1,0:T(8,128)S(1)}) custom-call(s32[5]{0:T(128)S(1)} %pad_add_fusion.1.place_ref, bf16[1024,256]{1,0:T(8,128)(2,1)S(1)} %shard_map.146.refs_0_, bf16[1024,256]{1,0:T(8,128)(2,1)S(1)} %copy-done.7, bf16[1024,256]{1,0:T(8,128)(2,1)S(1)} %collective-permute-done.15.refs_2_, ...), custom_call_target="tpu_custom_call" | custom-call | flops 16777216 | bytes 73728 | tf_op jit(solution)/shard_map/pallas_call | solution.py:294
  92.6 1.0 add_convert_fusion
  93.7 4.8 %shard_map.151 = (bf16[256,1024]{1,0:T(8,128)(2,1)}, bf16[256,1024]{1,0:T(8,128)(2,1)}) custom-call(bf16[768,384]{1,0:T(8,128)(2,1)S(1)} %copy-done.3, bf16[768,384]{1,0:T(8,128)(2,1)S(1)} %copy-done.4, bf16[256,1024]{1,0:T(8,128)(2,1)S(1)} %copy-done.20, bf16[128,1024]{1,0:T(8,128)(2,1)} %collective-permute-done.12.refs_3_, ...), custom_call_target="tpu_custom_call" | custom-call | flops 5637144576 | bytes 49216 | tf_op jit(solution)/shard_map/pallas_call | solution.py:275
  98.5 1.0 collective-permute-done.21
  99.6 2.8 %collective-permute-start.22 = (bf16[64,1024]{1,0:T(8,128)(2,1)S(1)}, bf16[64,1024]{1,0:T(8,128)(2,1)S(1)}, u32[]{:S(2)}, u32[]{:S(2)}) collective-permute-start(bf16[64,1024]{1,0:T(8,128)(2,1)S(1)} %convert_add_fusion), channel_id=1, source_target_pairs={{0,1},{1,0},{2,3},{3,2},{4,5},{5,4},{6,7},{7,6},{8,9},{9,8},{10,11... | collective-permute-start | bytes 393224 | tf_op jit(solution)/shard_map/ppermute | solution.py:376
  102.5 1.6 %collective-permute-done.23 = bf16[512,512]{1,0:T(8,128)(2,1)S(1)} collective-permute-done((bf16[512,512]{1,0:T(8,128)(2,1)S(1)}, bf16[512,512]{1,0:T(8,128)(2,1)S(1)}, u32[]{:S(2)}, u32[]{:S(2)}) %collective-permute-start.23) | collective-permute-done | bytes 524320 | tf_op jit(solution)/shard_map/ppermute | solution.py:376
  104.4 1.5 %pad_maximum_fusion = f32[512,1024]{1,0:T(8,128)} fusion(f32[512,512]{1,0:T(8,128)S(1)} %add_multiply_fusion, f32[512,512]{1,0:T(8,128)S(1)} %add_multiply_fusion.1), kind=kLoop, calls=%fused_computation | loop fusion | flops 524288 | bytes 4194304 | tf_op jit(solution)/shard_map/concatenate | solution.py:583
  105.9 1.0 copy.16
  (83 shorter events, 11.7 us)
Async XLA Ops:
  0.6 19.0 %copy-start.3 = (bf16[768,384]{1,0:T(8,128)(2,1)S(1)}, bf16[768,384]{1,0:T(8,128)(2,1)}, u32[]{:S(2)}) copy-start(bf16[768,384]{1,0:T(8,128)(2,1)} %constant.66.clone.refs_0_) | copy-start | bytes 1769476
  0.6 18.9 %copy-start.4 = (bf16[768,384]{1,0:T(8,128)(2,1)S(1)}, bf16[768,384]{1,0:T(8,128)(2,1)}, u32[]{:S(2)}) copy-start(bf16[768,384]{1,0:T(8,128)(2,1)} %constant.67.clone.refs_1_) | copy-start | bytes 1769476
  0.7 18.9 %copy-start.1 = (bf16[1,256,1024]{2,1,0:T(8,128)(2,1)S(1)}, bf16[1,256,1024]{2,1,0:T(8,128)(2,1)}, u32[]{:S(2)}) copy-start(bf16[1,256,1024]{2,1,0:T(8,128)(2,1)} %param.12) | copy-start | bytes 1572868
  0.7 18.9 %copy-start.2 = (bf16[1,256,1024]{2,1,0:T(8,128)(2,1)S(1)}, bf16[1,256,1024]{2,1,0:T(8,128)(2,1)}, u32[]{:S(2)}) copy-start(bf16[1,256,1024]{2,1,0:T(8,128)(2,1)} %param.11) | copy-start | bytes 1572868
  0.7 18.9 %copy-start.12 = (bf16[1024,128]{1,0:T(8,128)(2,1)S(1)}, bf16[1024,128]{1,0:T(8,128)(2,1)}, u32[]{:S(2)}) copy-start(bf16[1024,128]{1,0:T(8,128)(2,1)} %refs_4_.1) | copy-start | bytes 786436
  0.7 18.9 %copy-start.18 = (f32[1024]{0:T(1024)S(1)}, f32[1024]{0:T(1024)}, u32[]{:S(2)}) copy-start(f32[1024]{0:T(1024)} %param.14) | copy-start | bytes 12292
  2.0 13.2 %collective-permute-start.1 = (bf16[256,1024]{1,0:T(8,128)(2,1)}, bf16[256,1024]{1,0:T(8,128)(2,1)S(1)}, u32[]{:S(2)}, u32[]{:S(2)}) collective-permute-start(bf16[256,1024]{1,0:T(8,128)(2,1)} %bitcast.29), channel_id=1, source_target_pairs={{2,4},{4,2},{8,14},{14,8},{18,20},{20,18},{24,30},{30,24},{3,5},{5... | collective-permute-start | bytes 1572872 | tf_op jit(solution)/shard_map/ppermute | solution.py:433
  2.7 12.5 %collective-permute-start = (bf16[128,1024]{1,0:T(8,128)(2,1)S(1)}, bf16[128,1024]{1,0:T(8,128)(2,1)S(1)}, u32[]{:S(2)}, u32[]{:S(2)}) collective-permute-start(bf16[128,1024]{1,0:T(8,128)(2,1)S(1)} %fusion), channel_id=1, source_target_pairs={{0,8},{8,16},{16,24},{1,9},{9,17},{17,25},{2,10},{10,18},{18,26},{... | collective-permute-start | bytes 786440 | tf_op jit(solution)/shard_map/ppermute | solution.py:411
  9.8 14.4 %collective-permute-start.4 = (bf16[256,1024]{1,0:T(8,128)(2,1)}, bf16[256,1024]{1,0:T(8,128)(2,1)}, u32[]{:S(2)}, u32[]{:S(2)}) collective-permute-start(bf16[256,1024]{1,0:T(8,128)(2,1)} %bitcast.30), channel_id=1, source_target_pairs={{0,0},{1,4},{2,2},{3,6},{4,1},{5,5},{6,3},{7,7},{8,8},{9,12},{10,1... | collective-permute-start | bytes 1572872 | tf_op jit(solution)/shard_map/ppermute | solution.py:420
  15.1 12.6 %collective-permute-start.5 = (bf16[256,1024]{1,0:T(8,128)(2,1)}, bf16[256,1024]{1,0:T(8,128)(2,1)}, u32[]{:S(2)}, u32[]{:S(2)}) collective-permute-start(bf16[256,1024]{1,0:T(8,128)(2,1)} %bitcast.31), channel_id=1, source_target_pairs={{0,4},{1,0},{2,6},{3,2},{4,5},{5,1},{6,7},{7,3},{8,12},{9,8},{10,1... | collective-permute-start | bytes 1572872 | tf_op jit(solution)/shard_map/ppermute | solution.py:420
  17.1 11.3 %collective-permute-start.2 = (bf16[256,1024]{1,0:T(8,128)(2,1)}, bf16[256,1024]{1,0:T(8,128)(2,1)S(1)}, u32[]{:S(2)}, u32[]{:S(2)}) collective-permute-start(bf16[256,1024]{1,0:T(8,128)(2,1)} %broadcast_select_fusion), channel_id=1, source_target_pairs={{0,0},{2,16},{4,12},{6,28},{8,24},{10,8},{12,20},{14,4},{16,2},{18... | collective-permute-start | bytes 1572872 | tf_op jit(solution)/shard_map/ppermute | solution.py:445
  20.7 17.8 %copy-start = (bf16[1024,2048]{1,0:T(8,128)(2,1)S(1)}, bf16[1024,2048]{1,0:T(8,128)(2,1)}, u32[]{:S(2)}) copy-start(bf16[1024,2048]{1,0:T(8,128)(2,1)} %weight.1) | copy-start | bytes 12582916
  24.1 24.5 %copy-start.14 = (bf16[256,512]{1,0:T(8,128)(2,1)}, bf16[256,512]{1,0:T(8,128)(2,1)S(1)}, u32[]{:S(2)}) copy-start(bf16[256,512]{1,0:T(8,128)(2,1)S(1)} %get-tuple-element.69.refs_4_) | copy-start | bytes 786436
  27.8 10.7 %collective-permute-start.6 = (bf16[256,1024]{1,0:T(8,128)(2,1)}, bf16[256,1024]{1,0:T(8,128)(2,1)S(1)}, u32[]{:S(2)}, u32[]{:S(2)}) collective-permute-start(bf16[256,1024]{1,0:T(8,128)(2,1)} %collective-permute-done.4.first_mine), channel_id=1, source_target_pairs={{0,2},{1,3},{2,0},{3,1},{4,6},{5,7},{6,4},{7,5},{8,10},{9,11},{10,... | collective-permute-start | bytes 1572872 | tf_op jit(solution)/shard_map/ppermute | solution.py:487
  28.3 10.2 %collective-permute-start.7 = (bf16[256,1024]{1,0:T(8,128)(2,1)}, bf16[256,1024]{1,0:T(8,128)(2,1)S(1)}, u32[]{:S(2)}, u32[]{:S(2)}) collective-permute-start(bf16[256,1024]{1,0:T(8,128)(2,1)} %collective-permute-done.5.second_mine), channel_id=1, source_target_pairs={{0,2},{1,3},{2,0},{3,1},{4,6},{5,7},{6,4},{7,5},{8,10},{9,11},{10,... | collective-permute-start | bytes 1572872 | tf_op jit(solution)/shard_map/ppermute | solution.py:487
  28.4 16.0 %collective-permute-start.3 = (bf16[256,512]{1,0:T(8,128)(2,1)S(1)}, bf16[256,512]{1,0:T(8,128)(2,1)S(1)}, u32[]{:S(2)}, u32[]{:S(2)}) collective-permute-start(bf16[256,512]{1,0:T(8,128)(2,1)S(1)} %get-tuple-element.57.refs_4_), channel_id=1, source_target_pairs={{0,16},{16,24},{24,8},{8,0},{1,17},{17,25},{25,9},{9,1},{2,18},{18... | collective-permute-start | bytes 786440 | tf_op jit(solution)/shard_map/ppermute | solution.py:478
  38.4 14.2 %collective-permute-start.15 = (bf16[1024,256]{1,0:T(8,128)(2,1)S(1)}, bf16[1024,256]{1,0:T(8,128)(2,1)S(1)}, u32[]{:S(2)}, u32[]{:S(2)}) collective-permute-start(bf16[1024,256]{1,0:T(8,128)(2,1)S(1)} %shard_map.146.refs_0_), channel_id=1, source_target_pairs={{0,4},{2,6},{4,0},{6,2},{1,5},{3,7},{5,1},{7,3},{8,12},{10,14},{12... | collective-permute-start | bytes 1572872 | tf_op jit(solution)/shard_map/ppermute | solution.py:503
  44.4 10.1 %collective-permute-start.8 = (bf16[256,512]{1,0:T(8,128)(2,1)S(1)}, bf16[256,512]{1,0:T(8,128)(2,1)S(1)}, u32[]{:S(2)}, u32[]{:S(2)}) collective-permute-start(bf16[256,512]{1,0:T(8,128)(2,1)S(1)} %collective-permute-done.3.refs_5_), channel_id=1, source_target_pairs={{0,16},{16,24},{24,8},{8,0},{1,17},{17,25},{25,9},{9,1},{2,18},{18... | collective-permute-start | bytes 786440 | tf_op jit(solution)/shard_map/ppermute | solution.py:478
  47.8 14.6 %collective-permute-start.10 = (bf16[256,1024]{1,0:T(8,128)(2,1)S(1)}, bf16[256,1024]{1,0:T(8,128)(2,1)S(1)}, u32[]{:S(2)}, u32[]{:S(2)}) collective-permute-start(bf16[256,1024]{1,0:T(8,128)(2,1)S(1)} %get-tuple-element.67), channel_id=1, source_target_pairs={{0,1},{1,0},{2,3},{3,2},{4,5},{5,4},{6,7},{7,6},{8,9},{9,8},{10,11... | collective-permute-start | bytes 1572872 | tf_op jit(solution)/shard_map/ppermute | solution.py:376
  48.6 10.3 %collective-permute-start.9 = (bf16[256,512]{1,0:T(8,128)(2,1)S(1)}, bf16[256,512]{1,0:T(8,128)(2,1)S(1)}, u32[]{:S(2)}, u32[]{:S(2)}) collective-permute-start(bf16[256,512]{1,0:T(8,128)(2,1)S(1)} %get-tuple-element.69.refs_4_), channel_id=1, source_target_pairs={{0,16},{16,24},{24,8},{8,0},{1,17},{17,25},{25,9},{9,1},{2,18},{18... | collective-permute-start | bytes 786440 | tf_op jit(solution)/shard_map/ppermute | solution.py:478
  48.6 21.7 %collective-permute-start.14 = (bf16[1024,256]{1,0:T(8,128)(2,1)S(1)}, bf16[1024,256]{1,0:T(8,128)(2,1)S(1)}, u32[]{:S(2)}, u32[]{:S(2)}) collective-permute-start(bf16[1024,256]{1,0:T(8,128)(2,1)S(1)} %shard_map.146.refs_0_), channel_id=1, source_target_pairs={{0,2},{2,0},{4,6},{6,4},{1,3},{3,1},{5,7},{7,5},{8,10},{10,8},{12,... | collective-permute-start | bytes 1572872 | tf_op jit(solution)/shard_map/ppermute | solution.py:503
  54.5 20.2 %collective-permute-start.16 = (bf16[1024,256]{1,0:T(8,128)(2,1)S(1)}, bf16[1024,256]{1,0:T(8,128)(2,1)S(1)}, u32[]{:S(2)}, u32[]{:S(2)}) collective-permute-start(bf16[1024,256]{1,0:T(8,128)(2,1)S(1)} %collective-permute-done.15.refs_2_), channel_id=1, source_target_pairs={{0,2},{2,0},{4,6},{6,4},{1,3},{3,1},{5,7},{7,5},{8,10},{10,8},{12,... | collective-permute-start | bytes 1572872 | tf_op jit(solution)/shard_map/ppermute | solution.py:503
  58.9 10.1 %collective-permute-start.11 = (bf16[256,512]{1,0:T(8,128)(2,1)S(1)}, bf16[256,512]{1,0:T(8,128)(2,1)}, u32[]{:S(2)}, u32[]{:S(2)}) collective-permute-start(bf16[256,512]{1,0:T(8,128)(2,1)S(1)} %collective-permute-done.9.refs_5_), channel_id=1, source_target_pairs={{0,16},{16,24},{24,8},{8,0},{1,17},{17,25},{25,9},{9,1},{2,18},{18... | collective-permute-start | bytes 786440 | tf_op jit(solution)/shard_map/ppermute | solution.py:478
  62.3 12.4 %collective-permute-start.17 = (bf16[256,512]{1,0:T(8,128)(2,1)S(1)}, bf16[256,512]{1,0:T(8,128)(2,1)S(1)}, u32[]{:S(2)}, u32[]{:S(2)}) collective-permute-start(bf16[256,512]{1,0:T(8,128)(2,1)S(1)} %collective-permute-done.8.refs_6_), channel_id=1, source_target_pairs={{0,16},{16,24},{24,8},{8,0},{1,17},{17,25},{25,9},{9,1},{2,18},{18... | collective-permute-start | bytes 786440 | tf_op jit(solution)/shard_map/ppermute | solution.py:478
  66.3 12.7 %collective-permute-start.13 = (bf16[64,1024]{1,0:T(8,128)(2,1)S(1)}, bf16[64,1024]{1,0:T(8,128)(2,1)S(1)}, u32[]{:S(2)}, u32[]{:S(2)}) collective-permute-start(bf16[64,1024]{1,0:T(8,128)(2,1)S(1)} %get-tuple-element.81), channel_id=1, source_target_pairs={{0,1},{1,0},{2,3},{3,2},{4,5},{5,4},{6,7},{7,6},{8,9},{9,8},{10,11... | collective-permute-start | bytes 393224 | tf_op jit(solution)/shard_map/ppermute | solution.py:376
  69.1 23.5 %collective-permute-start.12 = (bf16[128,1024]{1,0:T(8,128)(2,1)}, bf16[128,1024]{1,0:T(8,128)(2,1)}, u32[]{:S(2)}, u32[]{:S(2)}) collective-permute-start(bf16[128,1024]{1,0:T(8,128)(2,1)} %get-tuple-element.79), channel_id=1, source_target_pairs={{8,0},{16,8},{24,16},{9,1},{17,9},{25,17},{10,2},{18,10},{26,18},{... | collective-permute-start | bytes 786440 | tf_op jit(solution)/shard_map/ppermute | solution.py:540
  70.4 14.0 %collective-permute-start.19 = (bf16[256,512]{1,0:T(8,128)(2,1)}, bf16[256,512]{1,0:T(8,128)(2,1)}, u32[]{:S(2)}, u32[]{:S(2)}) collective-permute-start(bf16[256,512]{1,0:T(8,128)(2,1)} %collective-permute-done.11.refs_6_), channel_id=1, source_target_pairs={{0,16},{16,24},{24,8},{8,0},{1,17},{17,25},{25,9},{9,1},{2,18},{18... | collective-permute-start | bytes 786440 | tf_op jit(solution)/shard_map/ppermute | solution.py:478
  79.8 12.8 %collective-permute-start.18 = (bf16[64,1024]{1,0:T(8,128)(2,1)}, bf16[64,1024]{1,0:T(8,128)(2,1)}, u32[]{:S(2)}, u32[]{:S(2)}) collective-permute-start(bf16[64,1024]{1,0:T(8,128)(2,1)} %add_convert_fusion.1), channel_id=1, source_target_pairs={{0,8},{8,0},{16,24},{24,16},{1,9},{9,1},{17,25},{25,17},{2,10},{10... | collective-permute-start | bytes 393224 | tf_op jit(solution)/shard_map/ppermute | solution.py:376
  79.8 19.8 %collective-permute-start.20 = (bf16[512,512]{1,0:T(8,128)(2,1)}, bf16[512,512]{1,0:T(8,128)(2,1)S(1)}, u32[]{:S(2)}, u32[]{:S(2)}) collective-permute-start(bf16[512,512]{1,0:T(8,128)(2,1)} %copy-done.21), channel_id=1, source_target_pairs={{0,1},{1,0},{2,3},{3,2},{4,5},{5,4},{6,7},{7,6},{8,9},{9,8},{10,11... | collective-permute-start | bytes 1572872 | tf_op jit(solution)/shard_map/ppermute | solution.py:376
  91.8 12.4 %collective-permute-start.23 = (bf16[512,512]{1,0:T(8,128)(2,1)S(1)}, bf16[512,512]{1,0:T(8,128)(2,1)S(1)}, u32[]{:S(2)}, u32[]{:S(2)}) collective-permute-start(bf16[512,512]{1,0:T(8,128)(2,1)S(1)} %get-tuple-element.99), channel_id=1, source_target_pairs={{0,1},{1,0},{2,3},{3,2},{4,5},{5,4},{6,7},{7,6},{8,9},{9,8},{10,11... | collective-permute-start | bytes 1572872 | tf_op jit(solution)/shard_map/ppermute | solution.py:376
  93.6 5.9 %collective-permute-start.21 = (bf16[64,1024]{1,0:T(8,128)(2,1)S(1)}, bf16[64,1024]{1,0:T(8,128)(2,1)S(1)}, u32[]{:S(2)}, u32[]{:S(2)}) collective-permute-start(bf16[64,1024]{1,0:T(8,128)(2,1)S(1)} %add_convert_fusion), channel_id=1, source_target_pairs={{0,16},{8,24},{16,0},{24,8},{1,17},{9,25},{17,1},{25,9},{2,18},{10... | collective-permute-start | bytes 393224 | tf_op jit(solution)/shard_map/ppermute | solution.py:376
  99.6 6.3 %collective-permute-start.22 = (bf16[64,1024]{1,0:T(8,128)(2,1)S(1)}, bf16[64,1024]{1,0:T(8,128)(2,1)S(1)}, u32[]{:S(2)}, u32[]{:S(2)}) collective-permute-start(bf16[64,1024]{1,0:T(8,128)(2,1)S(1)} %convert_add_fusion), channel_id=1, source_target_pairs={{0,1},{1,0},{2,3},{3,2},{4,5},{5,4},{6,7},{7,6},{8,9},{9,8},{10,11... | collective-permute-start | bytes 393224 | tf_op jit(solution)/shard_map/ppermute | solution.py:376
  (14 other events, 59.5 us)

commit v23 on v21

--- a/solution.py
+++ b/solution.py
@@ -477,7 +477,6 @@
         def ring_step(pieces):
             pieces.append(lax.ppermute(pieces[-1], "seq", ring))
 
-        halves[0][0], moved = lax.optimization_barrier((halves[0][0], moved))
         ring_step(halves[0])
         halves[1][0], *rounds = lax.optimization_barrier((halves[1][0], *rounds))
     else:

time: 109 us -> 111 us (1.018)
  starting transfers between devices: 44 us -> 47.7 us
  waiting for transfers between devices: 23.3 us -> 21.9 us
    ppermute x3, waiting for transfers between devices: 3.96 us -> 0.01 us  [per_device(): lax.ppermute(value, 'tp', [(t, t ^ flip) for t in range(n_tp)])]
    ppermute x3, starting transfers between devices: 0.08 us -> 2.94 us  [per_device(): lax.ppermute(value, 'tp', [(t, t ^ flip) for t in range(n_tp)])]
    ppermute x7, waiting for transfers between devices: 2.65 us -> 5.48 us  [swap_pairs(): return lax.ppermute(value, axis, [(i, i ^ distance) for i in range(count)])]
    ppermute x6, starting transfers between devices: 20.9 us -> 22.3 us  [ring_step(): pieces.append(lax.ppermute(pieces[-1], 'seq', ring))]
  transfers between devices with their start and end apart: 24 -> 24, of which waited for: 9 -> 8; matrix products, arithmetic and copies ran while one was open for 6% -> 6% of each run, Pallas kernels for 21% -> 21%
where the time goes in v23:
time: 111 us; the launch traced here: 110 us
  starting transfers between devices  47.7 us (43%)
  Pallas kernels  23 us (21%)
  waiting for transfers between devices  21.9 us (20%)
  local copies, waits for them, and re-layouts  9.27 us (8%)
  other arithmetic  6.96 us (6%)
    ppermute x6, starting transfers between devices, ring_step(): pieces.append(lax.ppermute(pieces[-1], 'seq', ring))  22.3 us
    ppermute x6, waiting for transfers between devices, ring_step(): pieces.append(lax.ppermute(pieces[-1], 'seq', ring))  12.7 us
    pallas_call x3, Pallas kernels, by_channel(): pl.pallas_call(kernel, in_specs=[pl.BlockSpec(memory_space=pl.ANY)] * (n_...  12.1 us
    pallas_call x3, Pallas kernels, local_call(): pl.pallas_call(kernel, in_specs=[pl.BlockSpec(memory_space=pltpu.SMEM)] +...  10.6 us
    unnamed x45, local copies, waits for them, and re-layouts  7.99 us
    ppermute x1, starting transfers between devices, per_device(): prior = lax.ppermute(tail, 'seq', [(i, i + 1) for i in range(n_seq - 1)])  7.09 us
    ppermute x7, starting transfers between devices, swap_pairs(): return lax.ppermute(value, axis, [(i, i ^ distance) for i in range(count)])  5.76 us
    ppermute x7, waiting for transfers between devices, swap_pairs(): return lax.ppermute(value, axis, [(i, i ^ distance) for i in range(count)])  5.48 us
  transfers between devices with their start and end apart: 24, of which 8 were waited for; matrix products, arithmetic and copies ran while one was open for 6% of the time, Pallas kernels for 21%

profile of v23, /device:TPU:0, one launch (start us, length us, event | category | flops | bytes accessed | tf_op | source)
XLA Modules:
  0.0 109.8 jit_solution(13068714822982111820)
XLA Ops:
  0.7 1.2 %fusion = bf16[128,1024]{1,0:T(8,128)(2,1)S(1)} fusion(bf16[1,256,1024]{2,1,0:T(8,128)(2,1)} %param.12, bf16[1,256,1024]{2,1,0:T(8,128)(2,1)} %param.11), kind=kLoop, calls=%fused_computation.6 | loop fusion | flops 524288 | bytes 786432 | tf_op jit(solution)/shard_map/convert_element_type | solution.py:409
  2.7 7.1 %collective-permute-start = (bf16[128,1024]{1,0:T(8,128)(2,1)S(1)}, bf16[128,1024]{1,0:T(8,128)(2,1)S(1)}, u32[]{:S(2)}, u32[]{:S(2)}) collective-permute-start(bf16[128,1024]{1,0:T(8,128)(2,1)S(1)} %fusion), channel_id=1, source_target_pairs={{0,8},{8,16},{16,24},{1,9},{9,17},{17,25},{2,10},{10,18},{18,26},{... | collective-permute-start | bytes 786440 | tf_op jit(solution)/shard_map/ppermute | solution.py:411
  9.8 5.4 %collective-permute-start.2 = (bf16[256,1024]{1,0:T(8,128)(2,1)}, bf16[256,1024]{1,0:T(8,128)(2,1)}, u32[]{:S(2)}, u32[]{:S(2)}) collective-permute-start(bf16[256,1024]{1,0:T(8,128)(2,1)} %bitcast.30), channel_id=1, source_target_pairs={{0,0},{1,4},{2,2},{3,6},{4,1},{5,5},{6,3},{7,7},{8,8},{9,12},{10,1... | collective-permute-start | bytes 1572872 | tf_op jit(solution)/shard_map/ppermute | solution.py:420
  15.1 1.9 %broadcast_select_fusion = bf16[256,1024]{1,0:T(8,128)(2,1)} fusion(bf16[256,1024]{1,0:T(8,128)(2,1)S(1)} %collective-permute-done.4, bf16[256,1024]{1,0:T(8,128)(2,1)} %bitcast.32, pred[]{:T(512)S(6)} %gt.3), kind=kLoop, calls=%fused_computation.5 | loop fusion | flops 262144 | bytes 1572865 | tf_op jit(solution)/shard_map/jit(_where)/select_n | solution.py:439
  17.1 1.7 %collective-permute-start.5 = (bf16[256,1024]{1,0:T(8,128)(2,1)}, bf16[256,1024]{1,0:T(8,128)(2,1)S(1)}, u32[]{:S(2)}, u32[]{:S(2)}) collective-permute-start(bf16[256,1024]{1,0:T(8,128)(2,1)} %broadcast_select_fusion), channel_id=1, source_target_pairs={{0,0},{2,16},{4,12},{6,28},{8,24},{10,8},{12,20},{14,4},{16,2},{18... | collective-permute-start | bytes 1572872 | tf_op jit(solution)/shard_map/ppermute | solution.py:445
  20.7 3.4 %shard_map.145 = (f32[256,1024]{1,0:T(8,128)S(1)}, bf16[256,512]{1,0:T(8,128)(2,1)S(1)}, bf16[256,512]{1,0:T(8,128)(2,1)S(1)}) custom-call(bf16[768,384]{1,0:T(8,128)(2,1)S(1)} %copy-done.3, bf16[768,384]{1,0:T(8,128)(2,1)S(1)} %copy-done.4, bf16[128,1024]{1,0:T(8,128)(2,1)S(1)} %collective-permute-done.refs_2_.refs_6_, bf16[256,1024]{1,0:T(8,128)(2,1)S(1)} %bitcast.22, ...), custom_call_target="tpu_custom_call" | custom-call | flops 22020096 | bytes 57408 | tf_op jit(solution)/shard_map/pallas_call | solution.py:275
  24.1 3.6 %collective-permute-done.3.second_mine = bf16[256,1024]{1,0:T(8,128)(2,1)} collective-permute-done((bf16[256,1024]{1,0:T(8,128)(2,1)}, bf16[256,1024]{1,0:T(8,128)(2,1)}, u32[]{:S(2)}, u32[]{:S(2)}) %collective-permute-start.3) | collective-permute-done | bytes 524320 | tf_op jit(solution)/shard_map/ppermute | solution.py:420
  28.4 4.5 %collective-permute-start.1 = (bf16[256,512]{1,0:T(8,128)(2,1)S(1)}, bf16[256,512]{1,0:T(8,128)(2,1)S(1)}, u32[]{:S(2)}, u32[]{:S(2)}) collective-permute-start(bf16[256,512]{1,0:T(8,128)(2,1)S(1)} %get-tuple-element.53.refs_4_), channel_id=1, source_target_pairs={{0,16},{16,24},{24,8},{8,0},{1,17},{17,25},{25,9},{9,1},{2,18},{18... | collective-permute-start | bytes 786440 | tf_op jit(solution)/shard_map/ppermute | solution.py:478
  33.1 1.0 collective-permute-start.15
  34.2 4.8 %shard_map.147 = (bf16[256,1024]{1,0:T(8,128)(2,1)S(1)}, f32[256,1024]{1,0:T(8,128)S(1)}) custom-call(s32[3]{0:T(128)S(1)} %pad_add_fusion.place_ref, bf16[256,1024]{1,0:T(8,128)(2,1)} %collective-permute-done.2.first_mine, bf16[256,1024]{1,0:T(8,128)(2,1)} %collective-permute-done.3.second_mine, bf16[256,1024]{1,0:T(8,128)(2,1)S(1)} %collective-permute-done.6.first_theirs, ...), custom_call_target="tpu_custom_call" | custom-call | flops 33554432 | bytes 122880 | tf_op jit(solution)/shard_map/pallas_call | solution.py:294
  39.0 1.3 %collective-permute-done.1.refs_5_ = bf16[256,512]{1,0:T(8,128)(2,1)S(1)} collective-permute-done((bf16[256,512]{1,0:T(8,128)(2,1)S(1)}, bf16[256,512]{1,0:T(8,128)(2,1)S(1)}, u32[]{:S(2)}, u32[]{:S(2)}) %collective-permute-start.1) | collective-permute-done | bytes 262176 | tf_op jit(solution)/shard_map/ppermute | solution.py:478
  40.4 5.9 %collective-permute-start.8 = (bf16[256,512]{1,0:T(8,128)(2,1)S(1)}, bf16[256,512]{1,0:T(8,128)(2,1)S(1)}, u32[]{:S(2)}, u32[]{:S(2)}) collective-permute-start(bf16[256,512]{1,0:T(8,128)(2,1)S(1)} %collective-permute-done.1.refs_5_), channel_id=1, source_target_pairs={{0,16},{16,24},{24,8},{8,0},{1,17},{17,25},{25,9},{9,1},{2,18},{18... | collective-permute-start | bytes 786440 | tf_op jit(solution)/shard_map/ppermute | solution.py:478
  47.1 4.1 %collective-permute-start.9 = (bf16[256,512]{1,0:T(8,128)(2,1)S(1)}, bf16[256,512]{1,0:T(8,128)(2,1)S(1)}, u32[]{:S(2)}, u32[]{:S(2)}) collective-permute-start(bf16[256,512]{1,0:T(8,128)(2,1)S(1)} %get-tuple-element.65.refs_4_), channel_id=1, source_target_pairs={{0,16},{16,24},{24,8},{8,0},{1,17},{17,25},{25,9},{9,1},{2,18},{18... | collective-permute-start | bytes 786440 | tf_op jit(solution)/shard_map/ppermute | solution.py:478
  51.3 1.6 %collective-permute-done.8.refs_6_ = bf16[256,512]{1,0:T(8,128)(2,1)S(1)} collective-permute-done((bf16[256,512]{1,0:T(8,128)(2,1)S(1)}, bf16[256,512]{1,0:T(8,128)(2,1)S(1)}, u32[]{:S(2)}, u32[]{:S(2)}) %collective-permute-start.8) | collective-permute-done | bytes 262176 | tf_op jit(solution)/shard_map/ppermute | solution.py:478
  52.9 1.9 %collective-permute-start.16 = (bf16[1024,256]{1,0:T(8,128)(2,1)S(1)}, bf16[1024,256]{1,0:T(8,128)(2,1)S(1)}, u32[]{:S(2)}, u32[]{:S(2)}) collective-permute-start(bf16[1024,256]{1,0:T(8,128)(2,1)S(1)} %collective-permute-done.15.refs_2_), channel_id=1, source_target_pairs={{0,2},{2,0},{4,6},{6,4},{1,3},{3,1},{5,7},{7,5},{8,10},{10,8},{12,... | collective-permute-start | bytes 1572872 | tf_op jit(solution)/shard_map/ppermute | solution.py:502
  54.8 3.3 %collective-permute-done.9.refs_5_ = bf16[256,512]{1,0:T(8,128)(2,1)S(1)} collective-permute-done((bf16[256,512]{1,0:T(8,128)(2,1)S(1)}, bf16[256,512]{1,0:T(8,128)(2,1)S(1)}, u32[]{:S(2)}, u32[]{:S(2)}) %collective-permute-start.9) | collective-permute-done | bytes 262176 | tf_op jit(solution)/shard_map/ppermute | solution.py:478
  58.1 3.4 %collective-permute-start.11 = (bf16[256,512]{1,0:T(8,128)(2,1)S(1)}, bf16[256,512]{1,0:T(8,128)(2,1)}, u32[]{:S(2)}, u32[]{:S(2)}) collective-permute-start(bf16[256,512]{1,0:T(8,128)(2,1)S(1)} %collective-permute-done.9.refs_5_), channel_id=1, source_target_pairs={{0,16},{16,24},{24,8},{8,0},{1,17},{17,25},{25,9},{9,1},{2,18},{18... | collective-permute-start | bytes 786440 | tf_op jit(solution)/shard_map/ppermute | solution.py:478
  61.5 3.9 %shard_map.148 = (bf16[256,1024]{1,0:T(8,128)(2,1)}, bf16[256,1024]{1,0:T(8,128)(2,1)S(1)}, bf16[128,1024]{1,0:T(8,128)(2,1)}, bf16[64,1024]{1,0:T(8,128)(2,1)S(1)}, f32[64,1024]{1,0:T(8,128)S(1)}) custom-call(bf16[768,384]{1,0:T(8,128)(2,1)S(1)} %copy-done.3, bf16[768,384]{1,0:T(8,128)(2,1)S(1)} %copy-done.4, f32[256,1024]{1,0:T(8,128)S(1)} %get-tuple-element.67.refs_2_, ...), custom_call_target="tpu_custom_call" | custom-call | flops 20447232 | bytes 96320 | tf_op jit(solution)/shard_map/pallas_call | solution.py:275
  66.4 1.8 %collective-permute-done.11.refs_6_ = bf16[256,512]{1,0:T(8,128)(2,1)} collective-permute-done((bf16[256,512]{1,0:T(8,128)(2,1)S(1)}, bf16[256,512]{1,0:T(8,128)(2,1)}, u32[]{:S(2)}, u32[]{:S(2)}) %collective-permute-start.11) | collective-permute-done | bytes 262176 | tf_op jit(solution)/shard_map/ppermute | solution.py:478
  68.2 1.3 %collective-permute-start.12 = (bf16[128,1024]{1,0:T(8,128)(2,1)}, bf16[128,1024]{1,0:T(8,128)(2,1)}, u32[]{:S(2)}, u32[]{:S(2)}) collective-permute-start(bf16[128,1024]{1,0:T(8,128)(2,1)} %get-tuple-element.75), channel_id=1, source_target_pairs={{8,0},{16,8},{24,16},{9,1},{17,9},{25,17},{10,2},{18,10},{26,18},{... | collective-permute-start | bytes 786440 | tf_op jit(solution)/shard_map/ppermute | solution.py:539
  69.5 4.3 %collective-permute-start.19 = (bf16[256,512]{1,0:T(8,128)(2,1)}, bf16[256,512]{1,0:T(8,128)(2,1)}, u32[]{:S(2)}, u32[]{:S(2)}) collective-permute-start(bf16[256,512]{1,0:T(8,128)(2,1)} %collective-permute-done.11.refs_6_), channel_id=1, source_target_pairs={{0,16},{16,24},{24,8},{8,0},{1,17},{17,25},{25,9},{9,1},{2,18},{18... | collective-permute-start | bytes 786440 | tf_op jit(solution)/shard_map/ppermute | solution.py:478
  73.9 2.4 %shard_map.149 = (bf16[512,512]{1,0:T(8,128)(2,1)S(1)}, f32[512,512]{1,0:T(8,128)S(1)}) custom-call(s32[5]{0:T(128)S(1)} %pad_add_fusion.1.place_ref, bf16[1024,256]{1,0:T(8,128)(2,1)S(1)} %shard_map.146.refs_0_, bf16[1024,256]{1,0:T(8,128)(2,1)S(1)} %collective-permute-done.14.refs_1_, bf16[1024,256]{1,0:T(8,128)(2,1)S(1)} %collective-permute-done.15.refs_2_, ...), custom_call_target="tpu_custom_call" | custom-call | flops 16777216 | bytes 73728 | tf_op jit(solution)/shard_map/pallas_call | solution.py:294
  78.9 1.7 %collective-permute-start.20 = (bf16[512,512]{1,0:T(8,128)(2,1)}, bf16[512,512]{1,0:T(8,128)(2,1)S(1)}, u32[]{:S(2)}, u32[]{:S(2)}) collective-permute-start(bf16[512,512]{1,0:T(8,128)(2,1)} %copy-done.21), channel_id=1, source_target_pairs={{0,1},{1,0},{2,3},{3,2},{4,5},{5,4},{6,7},{7,6},{8,9},{9,8},{10,11... | collective-permute-start | bytes 1572872 | tf_op jit(solution)/shard_map/ppermute | solution.py:376
  80.6 4.7 %collective-permute-done.19.refs_7_ = bf16[256,512]{1,0:T(8,128)(2,1)} collective-permute-done((bf16[256,512]{1,0:T(8,128)(2,1)}, bf16[256,512]{1,0:T(8,128)(2,1)}, u32[]{:S(2)}, u32[]{:S(2)}) %collective-permute-start.19) | collective-permute-done | bytes 262176 | tf_op jit(solution)/shard_map/ppermute | solution.py:478
  85.3 1.0 copy-done.7
  86.3 1.0 copy-done.9
  89.2 3.4 %shard_map.150 = (bf16[512,512]{1,0:T(8,128)(2,1)S(1)}, f32[512,512]{1,0:T(8,128)S(1)}) custom-call(s32[5]{0:T(128)S(1)} %pad_add_fusion.1.place_ref, bf16[1024,256]{1,0:T(8,128)(2,1)S(1)} %shard_map.146.refs_0_, bf16[1024,256]{1,0:T(8,128)(2,1)S(1)} %copy-done.7, bf16[1024,256]{1,0:T(8,128)(2,1)S(1)} %collective-permute-done.15.refs_2_, ...), custom_call_target="tpu_custom_call" | custom-call | flops 16777216 | bytes 73728 | tf_op jit(solution)/shard_map/pallas_call | solution.py:294
  92.6 1.6 %collective-permute-start.23 = (bf16[512,512]{1,0:T(8,128)(2,1)S(1)}, bf16[512,512]{1,0:T(8,128)(2,1)S(1)}, u32[]{:S(2)}, u32[]{:S(2)}) collective-permute-start(bf16[512,512]{1,0:T(8,128)(2,1)S(1)} %get-tuple-element.95), channel_id=1, source_target_pairs={{0,1},{1,0},{2,3},{3,2},{4,5},{5,4},{6,7},{7,6},{8,9},{9,8},{10,11... | collective-permute-start | bytes 1572872 | tf_op jit(solution)/shard_map/ppermute | solution.py:376
  95.3 4.8 %shard_map.151 = (bf16[256,1024]{1,0:T(8,128)(2,1)}, bf16[256,1024]{1,0:T(8,128)(2,1)}) custom-call(bf16[768,384]{1,0:T(8,128)(2,1)S(1)} %copy-done.3, bf16[768,384]{1,0:T(8,128)(2,1)S(1)} %copy-done.4, bf16[256,1024]{1,0:T(8,128)(2,1)S(1)} %copy-done.20, bf16[128,1024]{1,0:T(8,128)(2,1)} %collective-permute-done.12.refs_3_, ...), custom_call_target="tpu_custom_call" | custom-call | flops 5637144576 | bytes 49216 | tf_op jit(solution)/shard_map/pallas_call | solution.py:275
  100.2 2.4 %collective-permute-done.21 = bf16[64,1024]{1,0:T(8,128)(2,1)S(1)} collective-permute-done((bf16[64,1024]{1,0:T(8,128)(2,1)S(1)}, bf16[64,1024]{1,0:T(8,128)(2,1)S(1)}, u32[]{:S(2)}, u32[]{:S(2)}) %collective-permute-start.21) | collective-permute-done | bytes 131104 | tf_op jit(solution)/shard_map/ppermute | solution.py:376
  103.4 3.1 %collective-permute-done.23 = bf16[512,512]{1,0:T(8,128)(2,1)S(1)} collective-permute-done((bf16[512,512]{1,0:T(8,128)(2,1)S(1)}, bf16[512,512]{1,0:T(8,128)(2,1)S(1)}, u32[]{:S(2)}, u32[]{:S(2)}) %collective-permute-start.23) | collective-permute-done | bytes 524320 | tf_op jit(solution)/shard_map/ppermute | solution.py:376
  106.6 1.5 %pad_maximum_fusion = f32[512,1024]{1,0:T(8,128)} fusion(f32[512,512]{1,0:T(8,128)S(1)} %add_multiply_fusion, f32[512,512]{1,0:T(8,128)S(1)} %add_multiply_fusion.1), kind=kLoop, calls=%fused_computation | loop fusion | flops 524288 | bytes 4194304 | tf_op jit(solution)/shard_map/concatenate | solution.py:582
  (83 shorter events, 13.6 us)
Async XLA Ops:
  0.6 19.0 %copy-start.3 = (bf16[768,384]{1,0:T(8,128)(2,1)S(1)}, bf16[768,384]{1,0:T(8,128)(2,1)}, u32[]{:S(2)}) copy-start(bf16[768,384]{1,0:T(8,128)(2,1)} %constant.66.clone.refs_0_) | copy-start | bytes 1769476
  0.6 18.9 %copy-start.4 = (bf16[768,384]{1,0:T(8,128)(2,1)S(1)}, bf16[768,384]{1,0:T(8,128)(2,1)}, u32[]{:S(2)}) copy-start(bf16[768,384]{1,0:T(8,128)(2,1)} %constant.67.clone.refs_1_) | copy-start | bytes 1769476
  0.7 18.9 %copy-start.1 = (bf16[1,256,1024]{2,1,0:T(8,128)(2,1)S(1)}, bf16[1,256,1024]{2,1,0:T(8,128)(2,1)}, u32[]{:S(2)}) copy-start(bf16[1,256,1024]{2,1,0:T(8,128)(2,1)} %param.12) | copy-start | bytes 1572868
  0.7 18.9 %copy-start.2 = (bf16[1,256,1024]{2,1,0:T(8,128)(2,1)S(1)}, bf16[1,256,1024]{2,1,0:T(8,128)(2,1)}, u32[]{:S(2)}) copy-start(bf16[1,256,1024]{2,1,0:T(8,128)(2,1)} %param.11) | copy-start | bytes 1572868
  0.7 18.9 %copy-start.12 = (bf16[1024,128]{1,0:T(8,128)(2,1)S(1)}, bf16[1024,128]{1,0:T(8,128)(2,1)}, u32[]{:S(2)}) copy-start(bf16[1024,128]{1,0:T(8,128)(2,1)} %refs_4_.1) | copy-start | bytes 786436
  0.7 18.9 %copy-start.18 = (f32[1024]{0:T(1024)S(1)}, f32[1024]{0:T(1024)}, u32[]{:S(2)}) copy-start(f32[1024]{0:T(1024)} %param.14) | copy-start | bytes 12292
  2.0 13.2 %collective-permute-start.4 = (bf16[256,1024]{1,0:T(8,128)(2,1)}, bf16[256,1024]{1,0:T(8,128)(2,1)S(1)}, u32[]{:S(2)}, u32[]{:S(2)}) collective-permute-start(bf16[256,1024]{1,0:T(8,128)(2,1)} %bitcast.29), channel_id=1, source_target_pairs={{2,4},{4,2},{8,14},{14,8},{18,20},{20,18},{24,30},{30,24},{3,5},{5... | collective-permute-start | bytes 1572872 | tf_op jit(solution)/shard_map/ppermute | solution.py:433
  2.7 12.5 %collective-permute-start = (bf16[128,1024]{1,0:T(8,128)(2,1)S(1)}, bf16[128,1024]{1,0:T(8,128)(2,1)S(1)}, u32[]{:S(2)}, u32[]{:S(2)}) collective-permute-start(bf16[128,1024]{1,0:T(8,128)(2,1)S(1)} %fusion), channel_id=1, source_target_pairs={{0,8},{8,16},{16,24},{1,9},{9,17},{17,25},{2,10},{10,18},{18,26},{... | collective-permute-start | bytes 786440 | tf_op jit(solution)/shard_map/ppermute | solution.py:411
  9.8 14.4 %collective-permute-start.2 = (bf16[256,1024]{1,0:T(8,128)(2,1)}, bf16[256,1024]{1,0:T(8,128)(2,1)}, u32[]{:S(2)}, u32[]{:S(2)}) collective-permute-start(bf16[256,1024]{1,0:T(8,128)(2,1)} %bitcast.30), channel_id=1, source_target_pairs={{0,0},{1,4},{2,2},{3,6},{4,1},{5,5},{6,3},{7,7},{8,8},{9,12},{10,1... | collective-permute-start | bytes 1572872 | tf_op jit(solution)/shard_map/ppermute | solution.py:420
  15.1 12.6 %collective-permute-start.3 = (bf16[256,1024]{1,0:T(8,128)(2,1)}, bf16[256,1024]{1,0:T(8,128)(2,1)}, u32[]{:S(2)}, u32[]{:S(2)}) collective-permute-start(bf16[256,1024]{1,0:T(8,128)(2,1)} %bitcast.31), channel_id=1, source_target_pairs={{0,4},{1,0},{2,6},{3,2},{4,5},{5,1},{6,7},{7,3},{8,12},{9,8},{10,1... | collective-permute-start | bytes 1572872 | tf_op jit(solution)/shard_map/ppermute | solution.py:420
  17.1 15.8 %collective-permute-start.5 = (bf16[256,1024]{1,0:T(8,128)(2,1)}, bf16[256,1024]{1,0:T(8,128)(2,1)S(1)}, u32[]{:S(2)}, u32[]{:S(2)}) collective-permute-start(bf16[256,1024]{1,0:T(8,128)(2,1)} %broadcast_select_fusion), channel_id=1, source_target_pairs={{0,0},{2,16},{4,12},{6,28},{8,24},{10,8},{12,20},{14,4},{16,2},{18... | collective-permute-start | bytes 1572872 | tf_op jit(solution)/shard_map/ppermute | solution.py:445
  24.1 23.0 %copy-start.14 = (bf16[256,512]{1,0:T(8,128)(2,1)}, bf16[256,512]{1,0:T(8,128)(2,1)S(1)}, u32[]{:S(2)}) copy-start(bf16[256,512]{1,0:T(8,128)(2,1)S(1)} %get-tuple-element.65.refs_4_) | copy-start | bytes 786436
  27.8 6.4 %collective-permute-start.6 = (bf16[256,1024]{1,0:T(8,128)(2,1)}, bf16[256,1024]{1,0:T(8,128)(2,1)S(1)}, u32[]{:S(2)}, u32[]{:S(2)}) collective-permute-start(bf16[256,1024]{1,0:T(8,128)(2,1)} %collective-permute-done.2.first_mine), channel_id=1, source_target_pairs={{0,2},{1,3},{2,0},{3,1},{4,6},{5,7},{6,4},{7,5},{8,10},{9,11},{10,... | collective-permute-start | bytes 1572872 | tf_op jit(solution)/shard_map/ppermute | solution.py:486
  28.3 5.9 %collective-permute-start.7 = (bf16[256,1024]{1,0:T(8,128)(2,1)}, bf16[256,1024]{1,0:T(8,128)(2,1)S(1)}, u32[]{:S(2)}, u32[]{:S(2)}) collective-permute-start(bf16[256,1024]{1,0:T(8,128)(2,1)} %collective-permute-done.3.second_mine), channel_id=1, source_target_pairs={{0,2},{1,3},{2,0},{3,1},{4,6},{5,7},{6,4},{7,5},{8,10},{9,11},{10,... | collective-permute-start | bytes 1572872 | tf_op jit(solution)/shard_map/ppermute | solution.py:486
  28.4 12.0 %collective-permute-start.1 = (bf16[256,512]{1,0:T(8,128)(2,1)S(1)}, bf16[256,512]{1,0:T(8,128)(2,1)S(1)}, u32[]{:S(2)}, u32[]{:S(2)}) collective-permute-start(bf16[256,512]{1,0:T(8,128)(2,1)S(1)} %get-tuple-element.53.refs_4_), channel_id=1, source_target_pairs={{0,16},{16,24},{24,8},{8,0},{1,17},{17,25},{25,9},{9,1},{2,18},{18... | collective-permute-start | bytes 786440 | tf_op jit(solution)/shard_map/ppermute | solution.py:478
  33.1 18.2 %collective-permute-start.15 = (bf16[1024,256]{1,0:T(8,128)(2,1)S(1)}, bf16[1024,256]{1,0:T(8,128)(2,1)S(1)}, u32[]{:S(2)}, u32[]{:S(2)}) collective-permute-start(bf16[1024,256]{1,0:T(8,128)(2,1)S(1)} %shard_map.146.refs_0_), channel_id=1, source_target_pairs={{0,4},{2,6},{4,0},{6,2},{1,5},{3,7},{5,1},{7,3},{8,12},{10,14},{12... | collective-permute-start | bytes 1572872 | tf_op jit(solution)/shard_map/ppermute | solution.py:502
  40.4 12.5 %collective-permute-start.8 = (bf16[256,512]{1,0:T(8,128)(2,1)S(1)}, bf16[256,512]{1,0:T(8,128)(2,1)S(1)}, u32[]{:S(2)}, u32[]{:S(2)}) collective-permute-start(bf16[256,512]{1,0:T(8,128)(2,1)S(1)} %collective-permute-done.1.refs_5_), channel_id=1, source_target_pairs={{0,16},{16,24},{24,8},{8,0},{1,17},{17,25},{25,9},{9,1},{2,18},{18... | collective-permute-start | bytes 786440 | tf_op jit(solution)/shard_map/ppermute | solution.py:478
  46.3 15.2 %collective-permute-start.10 = (bf16[256,1024]{1,0:T(8,128)(2,1)S(1)}, bf16[256,1024]{1,0:T(8,128)(2,1)S(1)}, u32[]{:S(2)}, u32[]{:S(2)}) collective-permute-start(bf16[256,1024]{1,0:T(8,128)(2,1)S(1)} %get-tuple-element.63), channel_id=1, source_target_pairs={{0,1},{1,0},{2,3},{3,2},{4,5},{5,4},{6,7},{7,6},{8,9},{9,8},{10,11... | collective-permute-start | bytes 1572872 | tf_op jit(solution)/shard_map/ppermute | solution.py:376
  47.1 10.9 %collective-permute-start.9 = (bf16[256,512]{1,0:T(8,128)(2,1)S(1)}, bf16[256,512]{1,0:T(8,128)(2,1)S(1)}, u32[]{:S(2)}, u32[]{:S(2)}) collective-permute-start(bf16[256,512]{1,0:T(8,128)(2,1)S(1)} %get-tuple-element.65.refs_4_), channel_id=1, source_target_pairs={{0,16},{16,24},{24,8},{8,0},{1,17},{17,25},{25,9},{9,1},{2,18},{18... | collective-permute-start | bytes 786440 | tf_op jit(solution)/shard_map/ppermute | solution.py:478
  51.3 18.2 %collective-permute-start.14 = (bf16[1024,256]{1,0:T(8,128)(2,1)S(1)}, bf16[1024,256]{1,0:T(8,128)(2,1)S(1)}, u32[]{:S(2)}, u32[]{:S(2)}) collective-permute-start(bf16[1024,256]{1,0:T(8,128)(2,1)S(1)} %shard_map.146.refs_0_), channel_id=1, source_target_pairs={{0,2},{2,0},{4,6},{6,4},{1,3},{3,1},{5,7},{7,5},{8,10},{10,8},{12,... | collective-permute-start | bytes 1572872 | tf_op jit(solution)/shard_map/ppermute | solution.py:502
  52.9 20.9 %collective-permute-start.16 = (bf16[1024,256]{1,0:T(8,128)(2,1)S(1)}, bf16[1024,256]{1,0:T(8,128)(2,1)S(1)}, u32[]{:S(2)}, u32[]{:S(2)}) collective-permute-start(bf16[1024,256]{1,0:T(8,128)(2,1)S(1)} %collective-permute-done.15.refs_2_), channel_id=1, source_target_pairs={{0,2},{2,0},{4,6},{6,4},{1,3},{3,1},{5,7},{7,5},{8,10},{10,8},{12,... | collective-permute-start | bytes 1572872 | tf_op jit(solution)/shard_map/ppermute | solution.py:502
  58.1 10.1 %collective-permute-start.11 = (bf16[256,512]{1,0:T(8,128)(2,1)S(1)}, bf16[256,512]{1,0:T(8,128)(2,1)}, u32[]{:S(2)}, u32[]{:S(2)}) collective-permute-start(bf16[256,512]{1,0:T(8,128)(2,1)S(1)} %collective-permute-done.9.refs_5_), channel_id=1, source_target_pairs={{0,16},{16,24},{24,8},{8,0},{1,17},{17,25},{25,9},{9,1},{2,18},{18... | collective-permute-start | bytes 786440 | tf_op jit(solution)/shard_map/ppermute | solution.py:478
  61.5 12.4 %collective-permute-start.17 = (bf16[256,512]{1,0:T(8,128)(2,1)S(1)}, bf16[256,512]{1,0:T(8,128)(2,1)S(1)}, u32[]{:S(2)}, u32[]{:S(2)}) collective-permute-start(bf16[256,512]{1,0:T(8,128)(2,1)S(1)} %collective-permute-done.8.refs_6_), channel_id=1, source_target_pairs={{0,16},{16,24},{24,8},{8,0},{1,17},{17,25},{25,9},{9,1},{2,18},{18... | collective-permute-start | bytes 786440 | tf_op jit(solution)/shard_map/ppermute | solution.py:478
  65.4 12.6 %collective-permute-start.13 = (bf16[64,1024]{1,0:T(8,128)(2,1)S(1)}, bf16[64,1024]{1,0:T(8,128)(2,1)S(1)}, u32[]{:S(2)}, u32[]{:S(2)}) collective-permute-start(bf16[64,1024]{1,0:T(8,128)(2,1)S(1)} %get-tuple-element.77), channel_id=1, source_target_pairs={{0,1},{1,0},{2,3},{3,2},{4,5},{5,4},{6,7},{7,6},{8,9},{9,8},{10,11... | collective-permute-start | bytes 393224 | tf_op jit(solution)/shard_map/ppermute | solution.py:376
  68.2 26.0 %collective-permute-start.12 = (bf16[128,1024]{1,0:T(8,128)(2,1)}, bf16[128,1024]{1,0:T(8,128)(2,1)}, u32[]{:S(2)}, u32[]{:S(2)}) collective-permute-start(bf16[128,1024]{1,0:T(8,128)(2,1)} %get-tuple-element.75), channel_id=1, source_target_pairs={{8,0},{16,8},{24,16},{9,1},{17,9},{25,17},{10,2},{18,10},{26,18},{... | collective-permute-start | bytes 786440 | tf_op jit(solution)/shard_map/ppermute | solution.py:539
  69.5 15.8 %collective-permute-start.19 = (bf16[256,512]{1,0:T(8,128)(2,1)}, bf16[256,512]{1,0:T(8,128)(2,1)}, u32[]{:S(2)}, u32[]{:S(2)}) collective-permute-start(bf16[256,512]{1,0:T(8,128)(2,1)} %collective-permute-done.11.refs_6_), channel_id=1, source_target_pairs={{0,16},{16,24},{24,8},{8,0},{1,17},{17,25},{25,9},{9,1},{2,18},{18... | collective-permute-start | bytes 786440 | tf_op jit(solution)/shard_map/ppermute | solution.py:478
  78.0 17.3 %copy-start.13 = (bf16[1024,128]{1,0:T(8,128)(2,1)S(1)}, bf16[1024,128]{1,0:T(8,128)(2,1)}, u32[]{:S(2)}) copy-start(bf16[1024,128]{1,0:T(8,128)(2,1)} %refs_4_.1) | copy-start | bytes 786436
  78.9 15.3 %collective-permute-start.18 = (bf16[64,1024]{1,0:T(8,128)(2,1)}, bf16[64,1024]{1,0:T(8,128)(2,1)}, u32[]{:S(2)}, u32[]{:S(2)}) collective-permute-start(bf16[64,1024]{1,0:T(8,128)(2,1)} %add_convert_fusion.1), channel_id=1, source_target_pairs={{0,8},{8,0},{16,24},{24,16},{1,9},{9,1},{17,25},{25,17},{2,10},{10... | collective-permute-start | bytes 393224 | tf_op jit(solution)/shard_map/ppermute | solution.py:376
  78.9 23.7 %collective-permute-start.20 = (bf16[512,512]{1,0:T(8,128)(2,1)}, bf16[512,512]{1,0:T(8,128)(2,1)S(1)}, u32[]{:S(2)}, u32[]{:S(2)}) collective-permute-start(bf16[512,512]{1,0:T(8,128)(2,1)} %copy-done.21), channel_id=1, source_target_pairs={{0,1},{1,0},{2,3},{3,2},{4,5},{5,4},{6,7},{7,6},{8,9},{9,8},{10,11... | collective-permute-start | bytes 1572872 | tf_op jit(solution)/shard_map/ppermute | solution.py:376
  92.6 13.8 %collective-permute-start.23 = (bf16[512,512]{1,0:T(8,128)(2,1)S(1)}, bf16[512,512]{1,0:T(8,128)(2,1)S(1)}, u32[]{:S(2)}, u32[]{:S(2)}) collective-permute-start(bf16[512,512]{1,0:T(8,128)(2,1)S(1)} %get-tuple-element.95), channel_id=1, source_target_pairs={{0,1},{1,0},{2,3},{3,2},{4,5},{5,4},{6,7},{7,6},{8,9},{9,8},{10,11... | collective-permute-start | bytes 1572872 | tf_op jit(solution)/shard_map/ppermute | solution.py:376
  95.2 7.3 %collective-permute-start.21 = (bf16[64,1024]{1,0:T(8,128)(2,1)S(1)}, bf16[64,1024]{1,0:T(8,128)(2,1)S(1)}, u32[]{:S(2)}, u32[]{:S(2)}) collective-permute-start(bf16[64,1024]{1,0:T(8,128)(2,1)S(1)} %add_convert_fusion), channel_id=1, source_target_pairs={{0,16},{8,24},{16,0},{24,8},{1,17},{9,25},{17,1},{25,9},{2,18},{10... | collective-permute-start | bytes 393224 | tf_op jit(solution)/shard_map/ppermute | solution.py:376
  102.6 5.5 %collective-permute-start.22 = (bf16[64,1024]{1,0:T(8,128)(2,1)S(1)}, bf16[64,1024]{1,0:T(8,128)(2,1)S(1)}, u32[]{:S(2)}, u32[]{:S(2)}) collective-permute-start(bf16[64,1024]{1,0:T(8,128)(2,1)S(1)} %convert_add_fusion), channel_id=1, source_target_pairs={{0,1},{1,0},{2,3},{3,2},{4,5},{5,4},{6,7},{7,6},{8,9},{9,8},{10,11... | collective-permute-start | bytes 393224 | tf_op jit(solution)/shard_map/ppermute | solution.py:376
  (14 other events, 58.2 us)

commit v24 on v17

--- a/solution.py
+++ b/solution.py
@@ -13,7 +13,7 @@
 f32, bf16 = jnp.float32, jnp.bfloat16
 lanes = 512
 turn = 256
-vmem_bytes = 58 * 1024 * 1024
+vmem_bytes = 46 * 1024 * 1024
 
 
 def analysis_table(size, positions):
@@ -521,7 +521,7 @@
         ring_step()
         *last, own_part, other_part = lax.optimization_barrier((*ring_pieces[4:6], own_part, other_part))
         last = lax.ppermute(jnp.stack(last), "seq", ring)
-        moved_other = transposed(after(moved_other, across))
+        moved_other = transposed(after(moved_other, ring_pieces[2]))
         across_other = lax.ppermute(moved_other, "tp", opposite)
         cot_pieces = spread(moved, across, other_part) + spread(moved_other, across_other, own_part)
     else:

time: 117 us -> 111 us (0.949)
  Pallas kernels: 34.9 us -> 20.2 us
  waiting for transfers between devices: 29.2 us -> 38.8 us
    ppermute x8, waiting for transfers between devices: 11.3 us -> 21.2 us  [swap_pairs(): return lax.ppermute(value, axis, [(i, i ^ distance) for i in range(count)])]
    pallas_call x3, Pallas kernels: 16.9 us -> 10.7 us  [by_channel(): pl.pallas_call(kernel, in_specs=[pl.BlockSpec(memory_space=pltpu.SMEM)] *...]
    ppermute x1, starting transfers between devices: 6.23 us -> 0.08 us  [per_device(): across = lax.ppermute(moved, 'tp', opposite)]
    pallas_call x2, Pallas kernels: 13.8 us -> 7.88 us  [local_call(): pl.pallas_call(kernel, in_specs=[pl.BlockSpec(memory_space=pltpu.SMEM)] +...]
    ppermute x1, waiting for transfers between devices: 0.01 us -> 5.39 us  [per_device(): across = lax.ppermute(moved, 'tp', opposite)]
    ppermute x1, starting transfers between devices: 0.69 us -> 5.37 us  [per_device(): moved = lax.ppermute(held, ('seq', 'tp'), route)]
    ppermute x4, waiting for transfers between devices: 13 us -> 9.45 us  [ring_step(): ring_pieces.append(lax.ppermute(ring_pieces[-2], 'seq', ring))]
    ppermute x8, starting transfers between devices: 11.7 us -> 8.76 us  [swap_pairs(): return lax.ppermute(value, axis, [(i, i ^ distance) for i in range(count)])]
  transfers between devices with their start and end apart: 27 -> 27, of which waited for: 10 -> 10; matrix products, arithmetic and copies ran while one was open for 5% -> 4% of each run, Pallas kernels for 30% -> 18%
where the time goes in v24:
time: 111 us; the launch traced here: 110 us
  starting transfers between devices  39.6 us (36%)
  waiting for transfers between devices  38.8 us (35%)
  Pallas kernels  20.2 us (18%)
  other arithmetic  6.33 us (6%)
  local copies, waits for them, and re-layouts  4.3 us (4%)
    ppermute x8, waiting for transfers between devices, swap_pairs(): return lax.ppermute(value, axis, [(i, i ^ distance) for i in range(count)])  21.2 us
    pallas_call x3, Pallas kernels, by_channel(): pl.pallas_call(kernel, in_specs=[pl.BlockSpec(memory_space=pltpu.SMEM)] *...  10.7 us
    ppermute x4, waiting for transfers between devices, ring_step(): ring_pieces.append(lax.ppermute(ring_pieces[-2], 'seq', ring))  9.45 us
    ppermute x8, starting transfers between devices, swap_pairs(): return lax.ppermute(value, axis, [(i, i ^ distance) for i in range(count)])  8.76 us
    pallas_call x2, Pallas kernels, local_call(): pl.pallas_call(kernel, in_specs=[pl.BlockSpec(memory_space=pltpu.SMEM)] +...  7.88 us
    ppermute x1, starting transfers between devices, per_device(): prior = lax.ppermute(tail, 'seq', [(i, i + 1) for i in range(n_seq - 1)])  6.34 us
    ppermute x1, waiting for transfers between devices, per_device(): across = lax.ppermute(moved, 'tp', opposite)  5.39 us
    ppermute x1, starting transfers between devices, per_device(): moved = lax.ppermute(held, ('seq', 'tp'), route)  5.37 us
  transfers between devices with their start and end apart: 27, of which 10 were waited for; matrix products, arithmetic and copies ran while one was open for 4% of the time, Pallas kernels for 18%

profile of v24, /device:TPU:0, one launch (start us, length us, event | category | flops | bytes accessed | tf_op | source)
XLA Modules:
  0.0 110.2 jit_solution(2131776330452352486)
XLA Ops:
  0.7 1.2 %fusion.2 = bf16[128,1024]{1,0:T(8,128)(2,1)S(1)} fusion(bf16[1,256,1024]{2,1,0:T(8,128)(2,1)} %param.12, bf16[1,256,1024]{2,1,0:T(8,128)(2,1)} %param.11), kind=kLoop, calls=%fused_computation.8 | loop fusion | flops 524288 | bytes 786432 | tf_op jit(solution)/shard_map/convert_element_type | solution.py:417
  1.9 1.4 %collective-permute-start.2 = (bf16[256,1024]{1,0:T(8,128)(2,1)}, bf16[256,1024]{1,0:T(8,128)(2,1)}, u32[]{:S(2)}, u32[]{:S(2)}) collective-permute-start(bf16[256,1024]{1,0:T(8,128)(2,1)} %bitcast.33), channel_id=1, source_target_pairs={{2,4},{4,2},{8,14},{14,8},{18,20},{20,18},{24,30},{30,24},{3,5},{5... | collective-permute-start | bytes 1572872 | tf_op jit(solution)/shard_map/ppermute | solution.py:441
  3.4 6.3 %collective-permute-start = (bf16[128,1024]{1,0:T(8,128)(2,1)S(1)}, bf16[128,1024]{1,0:T(8,128)(2,1)S(1)}, u32[]{:S(2)}, u32[]{:S(2)}) collective-permute-start(bf16[128,1024]{1,0:T(8,128)(2,1)S(1)} %fusion.2), channel_id=1, source_target_pairs={{0,8},{8,16},{16,24},{1,9},{9,17},{17,25},{2,10},{10,18},{18,26},{... | collective-permute-start | bytes 786440 | tf_op jit(solution)/shard_map/ppermute | solution.py:419
  9.7 1.7 %collective-permute-start.6 = (bf16[256,1024]{1,0:T(8,128)(2,1)}, bf16[256,1024]{1,0:T(8,128)(2,1)S(1)}, u32[]{:S(2)}, u32[]{:S(2)}) collective-permute-start(bf16[256,1024]{1,0:T(8,128)(2,1)} %bitcast.34), channel_id=1, source_target_pairs={{0,0},{1,4},{2,2},{3,6},{4,1},{5,5},{6,3},{7,7},{8,8},{9,12},{10,1... | collective-permute-start | bytes 1572872 | tf_op jit(solution)/shard_map/ppermute | solution.py:428
  11.4 2.8 %collective-permute-done.refs_3_.refs_6_ = bf16[128,1024]{1,0:T(8,128)(2,1)S(1)} collective-permute-done((bf16[128,1024]{1,0:T(8,128)(2,1)S(1)}, bf16[128,1024]{1,0:T(8,128)(2,1)S(1)}, u32[]{:S(2)}, u32[]{:S(2)}) %collective-permute-start) | collective-permute-done | bytes 262176 | tf_op jit(solution)/shard_map/ppermute | solution.py:419
  14.2 2.1 %collective-permute-start.7 = (bf16[256,1024]{1,0:T(8,128)(2,1)}, bf16[256,1024]{1,0:T(8,128)(2,1)S(1)}, u32[]{:S(2)}, u32[]{:S(2)}) collective-permute-start(bf16[256,1024]{1,0:T(8,128)(2,1)} %bitcast.35), channel_id=1, source_target_pairs={{0,4},{1,0},{2,6},{3,2},{4,5},{5,1},{6,7},{7,3},{8,12},{9,8},{10,1... | collective-permute-start | bytes 1572872 | tf_op jit(solution)/shard_map/ppermute | solution.py:428
  16.3 1.9 %broadcast_select_fusion = bf16[256,1024]{1,0:T(8,128)(2,1)} fusion(bf16[256,1024]{1,0:T(8,128)(2,1)} %collective-permute-done.2, bf16[256,1024]{1,0:T(8,128)(2,1)} %bitcast.36, pred[]{:T(512)S(6)} %gt.3), kind=kLoop, calls=%fused_computation.7 | loop fusion | flops 262144 | bytes 1572865 | tf_op jit(solution)/shard_map/jit(_where)/select_n | solution.py:447
  18.2 5.4 %collective-permute-start.3 = (bf16[256,1024]{1,0:T(8,128)(2,1)}, bf16[256,1024]{1,0:T(8,128)(2,1)}, u32[]{:S(2)}, u32[]{:S(2)}) collective-permute-start(bf16[256,1024]{1,0:T(8,128)(2,1)} %broadcast_select_fusion), channel_id=1, source_target_pairs={{0,0},{2,16},{4,12},{6,28},{8,24},{10,8},{12,20},{14,4},{16,2},{18... | collective-permute-start | bytes 1572872 | tf_op jit(solution)/shard_map/ppermute | solution.py:453
  26.5 3.4 %shard_map.145 = (f32[256,1024]{1,0:T(8,128)S(1)}, bf16[256,512]{1,0:T(8,128)(2,1)S(1)}, bf16[256,512]{1,0:T(8,128)(2,1)S(1)}) custom-call(s32[1]{0:T(128)} %bitcast.refs_0_, bf16[768,384]{1,0:T(8,128)(2,1)S(1)} %copy-done.4, bf16[768,384]{1,0:T(8,128)(2,1)S(1)} %copy-done.3, bf16[128,1024]{1,0:T(8,128)(2,1)S(1)} %collective-permute-done.refs_3_.refs_6_, ...), custom_call_target="tpu_custom_call" | custom-call | flops 22020096 | bytes 57408 | tf_op jit(solution)/shard_map/pallas_call | solution.py:281
  30.6 6.8 %collective-permute-done.1.refs_9_ = bf16[256,512]{1,0:T(8,128)(2,1)S(1)} collective-permute-done((bf16[256,512]{1,0:T(8,128)(2,1)S(1)}, bf16[256,512]{1,0:T(8,128)(2,1)S(1)}, u32[]{:S(2)}, u32[]{:S(2)}) %collective-permute-start.1) | collective-permute-done | bytes 262176 | tf_op jit(solution)/shard_map/ppermute | solution.py:384
  38.0 1.3 %shard_map.146.refs_0_ = bf16[1024,256]{1,0:T(8,128)(2,1)S(1)} custom-call(bf16[256,1024]{1,0:T(8,128)(2,1)} %collective-permute-done.3.rows_in), custom_call_target="tpu_custom_call" | custom-call | bytes 16384 | tf_op jit(solution)/shard_map/pallas_call | solution.py:367
  39.4 2.1 %collective-permute-start.5 = (bf16[256,512]{1,0:T(8,128)(2,1)S(1)}, bf16[256,512]{1,0:T(8,128)(2,1)S(1)}, u32[]{:S(2)}, u32[]{:S(2)}) collective-permute-start(bf16[256,512]{1,0:T(8,128)(2,1)S(1)} %collective-permute-done.1.refs_9_), channel_id=1, source_target_pairs={{0,16},{16,24},{24,8},{8,0},{1,17},{17,25},{25,9},{9,1},{2,18},{18... | collective-permute-start | bytes 786440 | tf_op jit(solution)/shard_map/ppermute | solution.py:489
  41.6 3.8 %shard_map.147 = (bf16[256,1024]{1,0:T(8,128)(2,1)S(1)}, f32[256,1024]{1,0:T(8,128)S(1)}) custom-call(s32[3]{0:T(128)S(1)} %pad_add_fusion.place_ref, bf16[256,1024]{1,0:T(8,128)(2,1)S(1)} %collective-permute-done.6.first_mine, bf16[256,1024]{1,0:T(8,128)(2,1)S(1)} %collective-permute-done.7.second_mine, ...), custom_call_target="tpu_custom_call" | custom-call | flops 33554432 | bytes 122880 | tf_op jit(solution)/shard_map/pallas_call | solution.py:301
  45.4 4.5 %collective-permute-done.10.rows_in = bf16[256,1024]{1,0:T(8,128)(2,1)S(1)} collective-permute-done((bf16[256,1024]{1,0:T(8,128)(2,1)}, bf16[256,1024]{1,0:T(8,128)(2,1)S(1)}, u32[]{:S(2)}, u32[]{:S(2)}) %collective-permute-start.10) | collective-permute-done | bytes 524320 | tf_op jit(solution)/shard_map/ppermute | solution.py:384
  51.8 2.9 %collective-permute-start.12 = (bf16[256,512]{1,0:T(8,128)(2,1)S(1)}, bf16[256,512]{1,0:T(8,128)(2,1)S(1)}, u32[]{:S(2)}, u32[]{:S(2)}) collective-permute-start(bf16[256,512]{1,0:T(8,128)(2,1)S(1)} %collective-permute-done.5.refs_11_), channel_id=1, source_target_pairs={{0,16},{16,24},{24,8},{8,0},{1,17},{17,25},{25,9},{9,1},{2,18},{18... | collective-permute-start | bytes 786440 | tf_op jit(solution)/shard_map/ppermute | solution.py:489
  55.1 2.2 %collective-permute-start.21 = (bf16[1024,256]{1,0:T(8,128)(2,1)S(1)}, bf16[1024,256]{1,0:T(8,128)(2,1)S(1)}, u32[]{:S(2)}, u32[]{:S(2)}) collective-permute-start(bf16[1024,256]{1,0:T(8,128)(2,1)S(1)} %shard_map.149.refs_4_), channel_id=1, source_target_pairs={{0,4},{2,6},{4,0},{6,2},{1,5},{3,7},{5,1},{7,3},{8,12},{10,14},{12... | collective-permute-start | bytes 1572872 | tf_op jit(solution)/shard_map/ppermute | solution.py:525
  57.3 4.1 %collective-permute-done.12.refs_13_ = bf16[256,512]{1,0:T(8,128)(2,1)S(1)} collective-permute-done((bf16[256,512]{1,0:T(8,128)(2,1)S(1)}, bf16[256,512]{1,0:T(8,128)(2,1)S(1)}, u32[]{:S(2)}, u32[]{:S(2)}) %collective-permute-start.12) | collective-permute-done | bytes 262176 | tf_op jit(solution)/shard_map/ppermute | solution.py:489
  61.5 4.4 %collective-permute-done.11.refs_12_ = bf16[256,512]{1,0:T(8,128)(2,1)S(1)} collective-permute-done((bf16[256,512]{1,0:T(8,128)(2,1)S(1)}, bf16[256,512]{1,0:T(8,128)(2,1)S(1)}, u32[]{:S(2)}, u32[]{:S(2)}) %collective-permute-start.11) | collective-permute-done | bytes 262176 | tf_op jit(solution)/shard_map/ppermute | solution.py:489
  65.9 3.4 %collective-permute-start.14 = (bf16[2,256,512]{2,1,0:T(8,128)(2,1)S(1)}, bf16[2,256,512]{2,1,0:T(8,128)(2,1)S(1)}, u32[]{:S(2)}, u32[]{:S(2)}) collective-permute-start(bf16[2,256,512]{2,1,0:T(8,128)(2,1)S(1)} %pad_maximum_fusion.1), channel_id=1, source_target_pairs={{0,16},{16,24},{24,8},{8,0},{1,17},{17,25},{25,9},{9,1},{2,18},{18... | collective-permute-start | bytes 1572872 | tf_op jit(solution)/shard_map/ppermute | solution.py:523
  69.4 3.3 %shard_map.148 = (bf16[256,1024]{1,0:T(8,128)(2,1)}, bf16[256,1024]{1,0:T(8,128)(2,1)S(1)}, bf16[128,1024]{1,0:T(8,128)(2,1)S(1)}, bf16[64,1024]{1,0:T(8,128)(2,1)S(1)}, f32[64,1024]{1,0:T(8,128)S(1)}) custom-call(bf16[768,384]{1,0:T(8,128)(2,1)S(1)} %copy-done.4, bf16[768,384]{1,0:T(8,128)(2,1)S(1)} %copy-done.3, ...), custom_call_target="tpu_custom_call" | custom-call | flops 20447232 | bytes 96320 | tf_op jit(solution)/shard_map/pallas_call | solution.py:281
  74.3 5.4 %collective-permute-done.18.refs_2_ = bf16[1024,256]{1,0:T(8,128)(2,1)S(1)} collective-permute-done((bf16[1024,256]{1,0:T(8,128)(2,1)S(1)}, bf16[1024,256]{1,0:T(8,128)(2,1)S(1)}, u32[]{:S(2)}, u32[]{:S(2)}) %collective-permute-start.18) | collective-permute-done | bytes 524320 | tf_op jit(solution)/shard_map/ppermute | solution.py:519
  80.2 1.5 %collective-permute-start.24 = (bf16[128,1024]{1,0:T(8,128)(2,1)S(1)}, bf16[128,1024]{1,0:T(8,128)(2,1)S(1)}, u32[]{:S(2)}, u32[]{:S(2)}) collective-permute-start(bf16[128,1024]{1,0:T(8,128)(2,1)S(1)} %get-tuple-element.96), channel_id=1, source_target_pairs={{8,0},{16,8},{24,16},{9,1},{17,9},{25,17},{10,2},{18,10},{26,18},{... | collective-permute-start | bytes 786440 | tf_op jit(solution)/shard_map/ppermute | solution.py:556
  81.8 2.7 %collective-permute-start.16 = (bf16[64,1024]{1,0:T(8,128)(2,1)S(1)}, bf16[64,1024]{1,0:T(8,128)(2,1)S(1)}, u32[]{:S(2)}, u32[]{:S(2)}) collective-permute-start(bf16[64,1024]{1,0:T(8,128)(2,1)S(1)} %add_convert_fusion.2), channel_id=1, source_target_pairs={{0,8},{8,0},{16,24},{24,16},{1,9},{9,1},{17,25},{25,17},{2,10},{10... | collective-permute-start | bytes 393224 | tf_op jit(solution)/shard_map/ppermute | solution.py:384
  84.5 4.1 %shard_map.150 = (bf16[512,512]{1,0:T(8,128)(2,1)}, f32[512,512]{1,0:T(8,128)S(1)}) custom-call(s32[5]{0:T(128)S(1)} %pad_add_fusion.1.place_ref, bf16[1024,256]{1,0:T(8,128)(2,1)S(1)} %shard_map.146.refs_0_, bf16[1024,256]{1,0:T(8,128)(2,1)S(1)} %collective-permute-done.17.refs_1_, bf16[1024,256]{1,0:T(8,128)(2,1)S(1)} %collective-permute-done.18.refs_2_, ...), custom_call_target="tpu_custom_call" | custom-call | flops 33554432 | bytes 122880 | tf_op jit(solution)/shard_map/pallas_call | solution.py:301
  88.6 1.1 %collective-permute-start.26 = (bf16[512,512]{1,0:T(8,128)(2,1)}, bf16[512,512]{1,0:T(8,128)(2,1)}, u32[]{:S(2)}, u32[]{:S(2)}) collective-permute-start(bf16[512,512]{1,0:T(8,128)(2,1)} %get-tuple-element.103), channel_id=1, source_target_pairs={{0,1},{1,0},{2,3},{3,2},{4,5},{5,4},{6,7},{7,6},{8,9},{9,8},{10,11... | collective-permute-start | bytes 1572872 | tf_op jit(solution)/shard_map/ppermute | solution.py:384
  89.7 3.4 %collective-permute-done.16 = bf16[64,1024]{1,0:T(8,128)(2,1)S(1)} collective-permute-done((bf16[64,1024]{1,0:T(8,128)(2,1)S(1)}, bf16[64,1024]{1,0:T(8,128)(2,1)S(1)}, u32[]{:S(2)}, u32[]{:S(2)}) %collective-permute-start.16) | collective-permute-done | bytes 131104 | tf_op jit(solution)/shard_map/ppermute | solution.py:384
  94.1 4.0 %shard_map.151 = (bf16[256,1024]{1,0:T(8,128)(2,1)}, bf16[256,1024]{1,0:T(8,128)(2,1)}) custom-call(bf16[768,384]{1,0:T(8,128)(2,1)S(1)} %copy-done.4, bf16[768,384]{1,0:T(8,128)(2,1)S(1)} %copy-done.3, bf16[256,1024]{1,0:T(8,128)(2,1)S(1)} %get-tuple-element.95.refs_2_, bf16[128,1024]{1,0:T(8,128)(2,1)S(1)} %collective-permute-done.24.refs_3_, ...), custom_call_target="tpu_custom_call" | custom-call | flops 5637144576 | bytes 49216 | tf_op jit(solution)/shard_map/pallas_call | solution.py:281
  98.1 2.5 %collective-permute-done.23 = bf16[64,1024]{1,0:T(8,128)(2,1)S(1)} collective-permute-done((bf16[64,1024]{1,0:T(8,128)(2,1)S(1)}, bf16[64,1024]{1,0:T(8,128)(2,1)S(1)}, u32[]{:S(2)}, u32[]{:S(2)}) %collective-permute-start.23) | collective-permute-done | bytes 131104 | tf_op jit(solution)/shard_map/ppermute | solution.py:384
  100.6 1.1 %collective-permute-start.25 = (bf16[64,1024]{1,0:T(8,128)(2,1)S(1)}, bf16[64,1024]{1,0:T(8,128)(2,1)S(1)}, u32[]{:S(2)}, u32[]{:S(2)}) collective-permute-start(bf16[64,1024]{1,0:T(8,128)(2,1)S(1)} %add_convert_fusion), channel_id=1, source_target_pairs={{0,1},{1,0},{2,3},{3,2},{4,5},{5,4},{6,7},{7,6},{8,9},{9,8},{10,11... | collective-permute-start | bytes 393224 | tf_op jit(solution)/shard_map/ppermute | solution.py:384
  101.7 4.0 %collective-permute-done.25 = bf16[64,1024]{1,0:T(8,128)(2,1)S(1)} collective-permute-done((bf16[64,1024]{1,0:T(8,128)(2,1)S(1)}, bf16[64,1024]{1,0:T(8,128)(2,1)S(1)}, u32[]{:S(2)}, u32[]{:S(2)}) %collective-permute-start.25) | collective-permute-done | bytes 131104 | tf_op jit(solution)/shard_map/ppermute | solution.py:384
  107.4 1.3 %fusion.1 = (f32[512,512]{1,0:T(8,128)S(1)}, f32[512,512]{1,0:T(8,128)S(1)}) fusion(bf16[512,512]{1,0:T(8,128)(2,1)} %collective-permute-done.26, f32[512,512]{1,0:T(8,128)S(1)} %get-tuple-element.97, pred[]{:T(512)S(6)} %eq.40), kind=kLoop, calls=%fused_computation.3 | loop fusion | flops 1310720 | bytes 3670017 | tf_op jit(solution)/shard_map/jit(_where)/select_n | solution.py:599
  108.7 1.5 %pad_maximum_fusion = f32[512,1024]{1,0:T(8,128)} fusion(f32[512,512]{1,0:T(8,128)S(1)} %get-tuple-element.111, f32[512,512]{1,0:T(8,128)S(1)} %get-tuple-element.110), kind=kLoop, calls=%fused_computation | loop fusion | flops 524288 | bytes 4194304 | tf_op jit(solution)/shard_map/concatenate | solution.py:597
  (63 shorter events, 11.4 us)
Async XLA Ops:
  0.6 23.8 %copy-start.3 = (bf16[768,384]{1,0:T(8,128)(2,1)S(1)}, bf16[768,384]{1,0:T(8,128)(2,1)}, u32[]{:S(2)}) copy-start(bf16[768,384]{1,0:T(8,128)(2,1)} %constant.67.clone.refs_2_.refs_1_) | copy-start | bytes 1769476
  0.6 23.8 %copy-start.4 = (bf16[768,384]{1,0:T(8,128)(2,1)S(1)}, bf16[768,384]{1,0:T(8,128)(2,1)}, u32[]{:S(2)}) copy-start(bf16[768,384]{1,0:T(8,128)(2,1)} %constant.66.clone.refs_1_.refs_0_) | copy-start | bytes 1769476
  0.7 23.8 %copy-start.1 = (bf16[1,256,1024]{2,1,0:T(8,128)(2,1)S(1)}, bf16[1,256,1024]{2,1,0:T(8,128)(2,1)}, u32[]{:S(2)}) copy-start(bf16[1,256,1024]{2,1,0:T(8,128)(2,1)} %param.12) | copy-start | bytes 1572868
  0.7 23.8 %copy-start.2 = (bf16[1,256,1024]{2,1,0:T(8,128)(2,1)S(1)}, bf16[1,256,1024]{2,1,0:T(8,128)(2,1)}, u32[]{:S(2)}) copy-start(bf16[1,256,1024]{2,1,0:T(8,128)(2,1)} %param.11) | copy-start | bytes 1572868
  0.7 23.8 %copy-start.8 = (f32[1024]{0:T(1024)S(1)}, f32[1024]{0:T(1024)}, u32[]{:S(2)}) copy-start(f32[1024]{0:T(1024)} %param.14) | copy-start | bytes 12292
  1.9 14.4 %collective-permute-start.2 = (bf16[256,1024]{1,0:T(8,128)(2,1)}, bf16[256,1024]{1,0:T(8,128)(2,1)}, u32[]{:S(2)}, u32[]{:S(2)}) collective-permute-start(bf16[256,1024]{1,0:T(8,128)(2,1)} %bitcast.33), channel_id=1, source_target_pairs={{2,4},{4,2},{8,14},{14,8},{18,20},{20,18},{24,30},{30,24},{3,5},{5... | collective-permute-start | bytes 1572872 | tf_op jit(solution)/shard_map/ppermute | solution.py:441
  3.4 10.8 %collective-permute-start = (bf16[128,1024]{1,0:T(8,128)(2,1)S(1)}, bf16[128,1024]{1,0:T(8,128)(2,1)S(1)}, u32[]{:S(2)}, u32[]{:S(2)}) collective-permute-start(bf16[128,1024]{1,0:T(8,128)(2,1)S(1)} %fusion.2), channel_id=1, source_target_pairs={{0,8},{8,16},{16,24},{1,9},{9,17},{17,25},{2,10},{10,18},{18,26},{... | collective-permute-start | bytes 786440 | tf_op jit(solution)/shard_map/ppermute | solution.py:419
  9.7 20.3 %collective-permute-start.6 = (bf16[256,1024]{1,0:T(8,128)(2,1)}, bf16[256,1024]{1,0:T(8,128)(2,1)S(1)}, u32[]{:S(2)}, u32[]{:S(2)}) collective-permute-start(bf16[256,1024]{1,0:T(8,128)(2,1)} %bitcast.34), channel_id=1, source_target_pairs={{0,0},{1,4},{2,2},{3,6},{4,1},{5,5},{6,3},{7,7},{8,8},{9,12},{10,1... | collective-permute-start | bytes 1572872 | tf_op jit(solution)/shard_map/ppermute | solution.py:428
  14.2 15.8 %collective-permute-start.7 = (bf16[256,1024]{1,0:T(8,128)(2,1)}, bf16[256,1024]{1,0:T(8,128)(2,1)S(1)}, u32[]{:S(2)}, u32[]{:S(2)}) collective-permute-start(bf16[256,1024]{1,0:T(8,128)(2,1)} %bitcast.35), channel_id=1, source_target_pairs={{0,4},{1,0},{2,6},{3,2},{4,5},{5,1},{6,7},{7,3},{8,12},{9,8},{10,1... | collective-permute-start | bytes 1572872 | tf_op jit(solution)/shard_map/ppermute | solution.py:428
  18.2 19.2 %collective-permute-start.3 = (bf16[256,1024]{1,0:T(8,128)(2,1)}, bf16[256,1024]{1,0:T(8,128)(2,1)}, u32[]{:S(2)}, u32[]{:S(2)}) collective-permute-start(bf16[256,1024]{1,0:T(8,128)(2,1)} %broadcast_select_fusion), channel_id=1, source_target_pairs={{0,0},{2,16},{4,12},{6,28},{8,24},{10,8},{12,20},{14,4},{16,2},{18... | collective-permute-start | bytes 1572872 | tf_op jit(solution)/shard_map/ppermute | solution.py:453
  29.9 7.5 %collective-permute-start.1 = (bf16[256,512]{1,0:T(8,128)(2,1)S(1)}, bf16[256,512]{1,0:T(8,128)(2,1)S(1)}, u32[]{:S(2)}, u32[]{:S(2)}) collective-permute-start(bf16[256,512]{1,0:T(8,128)(2,1)S(1)} %get-tuple-element.58), channel_id=1, source_target_pairs={{0,1},{1,0},{2,3},{3,2},{4,5},{5,4},{6,7},{7,6},{8,9},{9,8},{10,11... | collective-permute-start | bytes 786440 | tf_op jit(solution)/shard_map/ppermute | solution.py:384
  30.0 11.5 %collective-permute-start.8 = (bf16[256,1024]{1,0:T(8,128)(2,1)S(1)}, bf16[256,1024]{1,0:T(8,128)(2,1)S(1)}, u32[]{:S(2)}, u32[]{:S(2)}) collective-permute-start(bf16[256,1024]{1,0:T(8,128)(2,1)S(1)} %collective-permute-done.6.first_mine), channel_id=1, source_target_pairs={{0,2},{1,3},{2,0},{3,1},{4,6},{5,7},{6,4},{7,5},{8,10},{9,11},{10,... | collective-permute-start | bytes 1572872 | tf_op jit(solution)/shard_map/ppermute | solution.py:495
  30.1 11.4 %collective-permute-start.9 = (bf16[256,1024]{1,0:T(8,128)(2,1)S(1)}, bf16[256,1024]{1,0:T(8,128)(2,1)S(1)}, u32[]{:S(2)}, u32[]{:S(2)}) collective-permute-start(bf16[256,1024]{1,0:T(8,128)(2,1)S(1)} %collective-permute-done.7.second_mine), channel_id=1, source_target_pairs={{0,2},{1,3},{2,0},{3,1},{4,6},{5,7},{6,4},{7,5},{8,10},{9,11},{10,... | collective-permute-start | bytes 1572872 | tf_op jit(solution)/shard_map/ppermute | solution.py:495
  37.5 12.4 %collective-permute-start.10 = (bf16[256,1024]{1,0:T(8,128)(2,1)}, bf16[256,1024]{1,0:T(8,128)(2,1)S(1)}, u32[]{:S(2)}, u32[]{:S(2)}) collective-permute-start(bf16[256,1024]{1,0:T(8,128)(2,1)} %collective-permute-done.3.rows_in), channel_id=1, source_target_pairs={{0,1},{1,0},{2,3},{3,2},{4,5},{5,4},{6,7},{7,6},{8,9},{9,8},{10,11... | collective-permute-start | bytes 1572872 | tf_op jit(solution)/shard_map/ppermute | solution.py:384
  39.3 11.6 %collective-permute-start.4 = (bf16[256,512]{1,0:T(8,128)(2,1)S(1)}, bf16[256,512]{1,0:T(8,128)(2,1)S(1)}, u32[]{:S(2)}, u32[]{:S(2)}) collective-permute-start(bf16[256,512]{1,0:T(8,128)(2,1)S(1)} %get-tuple-element.60.refs_8_), channel_id=1, source_target_pairs={{0,16},{16,24},{24,8},{8,0},{1,17},{17,25},{25,9},{9,1},{2,18},{18... | collective-permute-start | bytes 786440 | tf_op jit(solution)/shard_map/ppermute | solution.py:489
  39.4 12.4 %collective-permute-start.5 = (bf16[256,512]{1,0:T(8,128)(2,1)S(1)}, bf16[256,512]{1,0:T(8,128)(2,1)S(1)}, u32[]{:S(2)}, u32[]{:S(2)}) collective-permute-start(bf16[256,512]{1,0:T(8,128)(2,1)S(1)} %collective-permute-done.1.refs_9_), channel_id=1, source_target_pairs={{0,16},{16,24},{24,8},{8,0},{1,17},{17,25},{25,9},{9,1},{2,18},{18... | collective-permute-start | bytes 786440 | tf_op jit(solution)/shard_map/ppermute | solution.py:489
  49.8 16.1 %collective-permute-start.13 = (bf16[256,1024]{1,0:T(8,128)(2,1)S(1)}, bf16[256,1024]{1,0:T(8,128)(2,1)S(1)}, u32[]{:S(2)}, u32[]{:S(2)}) collective-permute-start(bf16[256,1024]{1,0:T(8,128)(2,1)S(1)} %get-tuple-element.70), channel_id=1, source_target_pairs={{0,1},{1,0},{2,3},{3,2},{4,5},{5,4},{6,7},{7,6},{8,9},{9,8},{10,11... | collective-permute-start | bytes 1572872 | tf_op jit(solution)/shard_map/ppermute | solution.py:384
  51.8 9.6 %collective-permute-start.12 = (bf16[256,512]{1,0:T(8,128)(2,1)S(1)}, bf16[256,512]{1,0:T(8,128)(2,1)S(1)}, u32[]{:S(2)}, u32[]{:S(2)}) collective-permute-start(bf16[256,512]{1,0:T(8,128)(2,1)S(1)} %collective-permute-done.5.refs_11_), channel_id=1, source_target_pairs={{0,16},{16,24},{24,8},{8,0},{1,17},{17,25},{25,9},{9,1},{2,18},{18... | collective-permute-start | bytes 786440 | tf_op jit(solution)/shard_map/ppermute | solution.py:489
  54.8 11.1 %collective-permute-start.11 = (bf16[256,512]{1,0:T(8,128)(2,1)S(1)}, bf16[256,512]{1,0:T(8,128)(2,1)S(1)}, u32[]{:S(2)}, u32[]{:S(2)}) collective-permute-start(bf16[256,512]{1,0:T(8,128)(2,1)S(1)} %collective-permute-done.4.refs_10_), channel_id=1, source_target_pairs={{0,16},{16,24},{24,8},{8,0},{1,17},{17,25},{25,9},{9,1},{2,18},{18... | collective-permute-start | bytes 786440 | tf_op jit(solution)/shard_map/ppermute | solution.py:489
  55.1 18.7 %collective-permute-start.21 = (bf16[1024,256]{1,0:T(8,128)(2,1)S(1)}, bf16[1024,256]{1,0:T(8,128)(2,1)S(1)}, u32[]{:S(2)}, u32[]{:S(2)}) collective-permute-start(bf16[1024,256]{1,0:T(8,128)(2,1)S(1)} %shard_map.149.refs_4_), channel_id=1, source_target_pairs={{0,4},{2,6},{4,0},{6,2},{1,5},{3,7},{5,1},{7,3},{8,12},{10,14},{12... | collective-permute-start | bytes 1572872 | tf_op jit(solution)/shard_map/ppermute | solution.py:525
  57.3 22.5 %collective-permute-start.18 = (bf16[1024,256]{1,0:T(8,128)(2,1)S(1)}, bf16[1024,256]{1,0:T(8,128)(2,1)S(1)}, u32[]{:S(2)}, u32[]{:S(2)}) collective-permute-start(bf16[1024,256]{1,0:T(8,128)(2,1)S(1)} %shard_map.146.refs_0_), channel_id=1, source_target_pairs={{0,4},{2,6},{4,0},{6,2},{1,5},{3,7},{5,1},{7,3},{8,12},{10,14},{12... | collective-permute-start | bytes 1572872 | tf_op jit(solution)/shard_map/ppermute | solution.py:519
  65.9 14.3 %collective-permute-start.14 = (bf16[2,256,512]{2,1,0:T(8,128)(2,1)S(1)}, bf16[2,256,512]{2,1,0:T(8,128)(2,1)S(1)}, u32[]{:S(2)}, u32[]{:S(2)}) collective-permute-start(bf16[2,256,512]{2,1,0:T(8,128)(2,1)S(1)} %pad_maximum_fusion.1), channel_id=1, source_target_pairs={{0,16},{16,24},{24,8},{8,0},{1,17},{17,25},{25,9},{9,1},{2,18},{18... | collective-permute-start | bytes 1572872 | tf_op jit(solution)/shard_map/ppermute | solution.py:523
  72.7 7.0 %collective-permute-start.15 = (bf16[64,1024]{1,0:T(8,128)(2,1)S(1)}, bf16[64,1024]{1,0:T(8,128)(2,1)S(1)}, u32[]{:S(2)}, u32[]{:S(2)}) collective-permute-start(bf16[64,1024]{1,0:T(8,128)(2,1)S(1)} %get-tuple-element.83), channel_id=1, source_target_pairs={{0,1},{1,0},{2,3},{3,2},{4,5},{5,4},{6,7},{7,6},{8,9},{9,8},{10,11... | collective-permute-start | bytes 393224 | tf_op jit(solution)/shard_map/ppermute | solution.py:384
  73.8 7.9 %collective-permute-start.17 = (bf16[1024,256]{1,0:T(8,128)(2,1)S(1)}, bf16[1024,256]{1,0:T(8,128)(2,1)S(1)}, u32[]{:S(2)}, u32[]{:S(2)}) collective-permute-start(bf16[1024,256]{1,0:T(8,128)(2,1)S(1)} %shard_map.146.refs_0_), channel_id=1, source_target_pairs={{0,2},{2,0},{4,6},{6,4},{1,3},{3,1},{5,7},{7,5},{8,10},{10,8},{12,... | collective-permute-start | bytes 1572872 | tf_op jit(solution)/shard_map/ppermute | solution.py:513
  73.8 10.7 %collective-permute-start.20 = (bf16[1024,256]{1,0:T(8,128)(2,1)S(1)}, bf16[1024,256]{1,0:T(8,128)(2,1)S(1)}, u32[]{:S(2)}, u32[]{:S(2)}) collective-permute-start(bf16[1024,256]{1,0:T(8,128)(2,1)S(1)} %shard_map.149.refs_4_), channel_id=1, source_target_pairs={{0,2},{2,0},{4,6},{6,4},{1,3},{3,1},{5,7},{7,5},{8,10},{10,8},{12,... | collective-permute-start | bytes 1572872 | tf_op jit(solution)/shard_map/ppermute | solution.py:513
  79.7 4.8 %collective-permute-start.19 = (bf16[1024,256]{1,0:T(8,128)(2,1)S(1)}, bf16[1024,256]{1,0:T(8,128)(2,1)S(1)}, u32[]{:S(2)}, u32[]{:S(2)}) collective-permute-start(bf16[1024,256]{1,0:T(8,128)(2,1)S(1)} %collective-permute-done.18.refs_2_), channel_id=1, source_target_pairs={{0,2},{2,0},{4,6},{6,4},{1,3},{3,1},{5,7},{7,5},{8,10},{10,8},{12,... | collective-permute-start | bytes 1572872 | tf_op jit(solution)/shard_map/ppermute | solution.py:515
  79.7 4.8 %collective-permute-start.22 = (bf16[1024,256]{1,0:T(8,128)(2,1)S(1)}, bf16[1024,256]{1,0:T(8,128)(2,1)S(1)}, u32[]{:S(2)}, u32[]{:S(2)}) collective-permute-start(bf16[1024,256]{1,0:T(8,128)(2,1)S(1)} %collective-permute-done.21.refs_6_), channel_id=1, source_target_pairs={{0,2},{2,0},{4,6},{6,4},{1,3},{3,1},{5,7},{7,5},{8,10},{10,8},{12,... | collective-permute-start | bytes 1572872 | tf_op jit(solution)/shard_map/ppermute | solution.py:515
  80.2 12.9 %collective-permute-start.24 = (bf16[128,1024]{1,0:T(8,128)(2,1)S(1)}, bf16[128,1024]{1,0:T(8,128)(2,1)S(1)}, u32[]{:S(2)}, u32[]{:S(2)}) collective-permute-start(bf16[128,1024]{1,0:T(8,128)(2,1)S(1)} %get-tuple-element.96), channel_id=1, source_target_pairs={{8,0},{16,8},{24,16},{9,1},{17,9},{25,17},{10,2},{18,10},{26,18},{... | collective-permute-start | bytes 786440 | tf_op jit(solution)/shard_map/ppermute | solution.py:556
  81.8 11.4 %collective-permute-start.16 = (bf16[64,1024]{1,0:T(8,128)(2,1)S(1)}, bf16[64,1024]{1,0:T(8,128)(2,1)S(1)}, u32[]{:S(2)}, u32[]{:S(2)}) collective-permute-start(bf16[64,1024]{1,0:T(8,128)(2,1)S(1)} %add_convert_fusion.2), channel_id=1, source_target_pairs={{0,8},{8,0},{16,24},{24,16},{1,9},{9,1},{17,25},{25,17},{2,10},{10... | collective-permute-start | bytes 393224 | tf_op jit(solution)/shard_map/ppermute | solution.py:384
  88.6 18.8 %collective-permute-start.26 = (bf16[512,512]{1,0:T(8,128)(2,1)}, bf16[512,512]{1,0:T(8,128)(2,1)}, u32[]{:S(2)}, u32[]{:S(2)}) collective-permute-start(bf16[512,512]{1,0:T(8,128)(2,1)} %get-tuple-element.103), channel_id=1, source_target_pairs={{0,1},{1,0},{2,3},{3,2},{4,5},{5,4},{6,7},{7,6},{8,9},{9,8},{10,11... | collective-permute-start | bytes 1572872 | tf_op jit(solution)/shard_map/ppermute | solution.py:384
  93.2 7.3 %collective-permute-start.23 = (bf16[64,1024]{1,0:T(8,128)(2,1)S(1)}, bf16[64,1024]{1,0:T(8,128)(2,1)S(1)}, u32[]{:S(2)}, u32[]{:S(2)}) collective-permute-start(bf16[64,1024]{1,0:T(8,128)(2,1)S(1)} %add_convert_fusion.1), channel_id=1, source_target_pairs={{0,16},{8,24},{16,0},{24,8},{1,17},{9,25},{17,1},{25,9},{2,18},{10... | collective-permute-start | bytes 393224 | tf_op jit(solution)/shard_map/ppermute | solution.py:384
  100.6 5.1 %collective-permute-start.25 = (bf16[64,1024]{1,0:T(8,128)(2,1)S(1)}, bf16[64,1024]{1,0:T(8,128)(2,1)S(1)}, u32[]{:S(2)}, u32[]{:S(2)}) collective-permute-start(bf16[64,1024]{1,0:T(8,128)(2,1)S(1)} %add_convert_fusion), channel_id=1, source_target_pairs={{0,1},{1,0},{2,3},{3,2},{4,5},{5,4},{6,7},{7,6},{8,9},{9,8},{10,11... | collective-permute-start | bytes 393224 | tf_op jit(solution)/shard_map/ppermute | solution.py:384
  (4 other events, 29.4 us)

commit v25 on v21

--- a/solution.py
+++ b/solution.py
@@ -537,8 +537,6 @@
         channels,
         unit * (2 * taps + 4 * length + 3 * taps),
     )
-    later = lax.ppermute(head, "seq", [(i + 1, i) for i in range(n_seq - 1)])
-
     def run_back(later):
         return by_channel(
             functools.partial(back_kernel, scale),
@@ -555,7 +553,8 @@
         ring_step(halves[1])
         first_sent, first_own = weight_sum(weight_place, cot_pieces, halves[0], rows)
         first_received = swap_pairs(first_sent, "dp", 1)
-        received, first_own = lax.optimization_barrier((received, first_own))
+        received, first_own, head = lax.optimization_barrier((received, first_own, head))
+    later = lax.ppermute(head, "seq", [(i + 1, i) for i in range(n_seq - 1)])
     lag_sum = own_lag + received.astype(f32)
     distance = 1
     while distance < n_seq:

time: 109 us -> 110 us (level)
  starting transfers between devices: 44 us -> 45.8 us
    ppermute x7, starting transfers between devices: 6.26 us -> 8.77 us  [swap_pairs(): return lax.ppermute(value, axis, [(i, i ^ distance) for i in range(count)])]
    ppermute x6, waiting for transfers between devices: 13.1 us -> 11.5 us  [ring_step(): pieces.append(lax.ppermute(pieces[-1], 'seq', ring))]
    ppermute x7, waiting for transfers between devices: 2.65 us -> 3.83 us  [swap_pairs(): return lax.ppermute(value, axis, [(i, i ^ distance) for i in range(count)])]
  transfers between devices with their start and end apart: 24 -> 24, of which waited for: 9 -> 8; matrix products, arithmetic and copies ran while one was open for 6% -> 6% of each run, Pallas kernels for 21% -> 21%
where the time goes in v25:
time: 110 us; the launch traced here: 109 us
  starting transfers between devices  45.8 us (42%)
  Pallas kernels  23 us (21%)
  waiting for transfers between devices  22.9 us (21%)
  local copies, waits for them, and re-layouts  9.27 us (8%)
  other arithmetic  6.96 us (6%)
    ppermute x6, starting transfers between devices, ring_step(): pieces.append(lax.ppermute(pieces[-1], 'seq', ring))  20 us
    pallas_call x3, Pallas kernels, by_channel(): pl.pallas_call(kernel, in_specs=[pl.BlockSpec(memory_space=pl.ANY)] * (n_...  12.1 us
    ppermute x6, waiting for transfers between devices, ring_step(): pieces.append(lax.ppermute(pieces[-1], 'seq', ring))  11.5 us
    pallas_call x3, Pallas kernels, local_call(): pl.pallas_call(kernel, in_specs=[pl.BlockSpec(memory_space=pltpu.SMEM)] +...  10.6 us
    ppermute x7, starting transfers between devices, swap_pairs(): return lax.ppermute(value, axis, [(i, i ^ distance) for i in range(count)])  8.77 us
    unnamed x45, local copies, waits for them, and re-layouts  7.98 us
    ppermute x1, starting transfers between devices, per_device(): prior = lax.ppermute(tail, 'seq', [(i, i + 1) for i in range(n_seq - 1)])  7.09 us
    ppermute x2, starting transfers between devices, per_device(): lax.ppermute(after(cot, prior) if turn else cot, ('tp', 'dp'), route)  5.37 us
  transfers between devices with their start and end apart: 24, of which 8 were waited for; matrix products, arithmetic and copies ran while one was open for 6% of the time, Pallas kernels for 21%

profile of v25, /device:TPU:0, one launch (start us, length us, event | category | flops | bytes accessed | tf_op | source)
XLA Modules:
  0.0 108.9 jit_solution(8520620770844525055)
XLA Ops:
  0.7 1.2 %fusion = bf16[128,1024]{1,0:T(8,128)(2,1)S(1)} fusion(bf16[1,256,1024]{2,1,0:T(8,128)(2,1)} %param.12, bf16[1,256,1024]{2,1,0:T(8,128)(2,1)} %param.11), kind=kLoop, calls=%fused_computation.6 | loop fusion | flops 524288 | bytes 786432 | tf_op jit(solution)/shard_map/convert_element_type | solution.py:409
  2.7 7.1 %collective-permute-start = (bf16[128,1024]{1,0:T(8,128)(2,1)S(1)}, bf16[128,1024]{1,0:T(8,128)(2,1)S(1)}, u32[]{:S(2)}, u32[]{:S(2)}) collective-permute-start(bf16[128,1024]{1,0:T(8,128)(2,1)S(1)} %fusion), channel_id=1, source_target_pairs={{0,8},{8,16},{16,24},{1,9},{9,17},{17,25},{2,10},{10,18},{18,26},{... | collective-permute-start | bytes 786440 | tf_op jit(solution)/shard_map/ppermute | solution.py:411
  9.8 5.4 %collective-permute-start.4 = (bf16[256,1024]{1,0:T(8,128)(2,1)}, bf16[256,1024]{1,0:T(8,128)(2,1)}, u32[]{:S(2)}, u32[]{:S(2)}) collective-permute-start(bf16[256,1024]{1,0:T(8,128)(2,1)} %bitcast.30), channel_id=1, source_target_pairs={{0,0},{1,4},{2,2},{3,6},{4,1},{5,5},{6,3},{7,7},{8,8},{9,12},{10,1... | collective-permute-start | bytes 1572872 | tf_op jit(solution)/shard_map/ppermute | solution.py:420
  15.1 1.9 %broadcast_select_fusion = bf16[256,1024]{1,0:T(8,128)(2,1)} fusion(bf16[256,1024]{1,0:T(8,128)(2,1)S(1)} %collective-permute-done.1, bf16[256,1024]{1,0:T(8,128)(2,1)} %bitcast.32, pred[]{:T(512)S(6)} %gt.3), kind=kLoop, calls=%fused_computation.5 | loop fusion | flops 262144 | bytes 1572865 | tf_op jit(solution)/shard_map/jit(_where)/select_n | solution.py:439
  17.1 1.7 %collective-permute-start.2 = (bf16[256,1024]{1,0:T(8,128)(2,1)}, bf16[256,1024]{1,0:T(8,128)(2,1)S(1)}, u32[]{:S(2)}, u32[]{:S(2)}) collective-permute-start(bf16[256,1024]{1,0:T(8,128)(2,1)} %broadcast_select_fusion), channel_id=1, source_target_pairs={{0,0},{2,16},{4,12},{6,28},{8,24},{10,8},{12,20},{14,4},{16,2},{18... | collective-permute-start | bytes 1572872 | tf_op jit(solution)/shard_map/ppermute | solution.py:445
  19.6 1.0 copy-done.5
  20.7 3.4 %shard_map.145 = (f32[256,1024]{1,0:T(8,128)S(1)}, bf16[256,512]{1,0:T(8,128)(2,1)S(1)}, bf16[256,512]{1,0:T(8,128)(2,1)S(1)}) custom-call(bf16[768,384]{1,0:T(8,128)(2,1)S(1)} %copy-done.3, bf16[768,384]{1,0:T(8,128)(2,1)S(1)} %copy-done.4, bf16[128,1024]{1,0:T(8,128)(2,1)S(1)} %collective-permute-done.refs_2_.refs_6_, bf16[256,1024]{1,0:T(8,128)(2,1)S(1)} %bitcast.22, ...), custom_call_target="tpu_custom_call" | custom-call | flops 22020096 | bytes 57408 | tf_op jit(solution)/shard_map/pallas_call | solution.py:275
  24.1 3.6 %collective-permute-done.5.second_mine = bf16[256,1024]{1,0:T(8,128)(2,1)} collective-permute-done((bf16[256,1024]{1,0:T(8,128)(2,1)}, bf16[256,1024]{1,0:T(8,128)(2,1)}, u32[]{:S(2)}, u32[]{:S(2)}) %collective-permute-start.5) | collective-permute-done | bytes 524320 | tf_op jit(solution)/shard_map/ppermute | solution.py:420
  28.4 9.8 %collective-permute-start.3 = (bf16[256,512]{1,0:T(8,128)(2,1)S(1)}, bf16[256,512]{1,0:T(8,128)(2,1)S(1)}, u32[]{:S(2)}, u32[]{:S(2)}) collective-permute-start(bf16[256,512]{1,0:T(8,128)(2,1)S(1)} %get-tuple-element.58.refs_4_), channel_id=1, source_target_pairs={{0,16},{16,24},{24,8},{8,0},{1,17},{17,25},{25,9},{9,1},{2,18},{18... | collective-permute-start | bytes 786440 | tf_op jit(solution)/shard_map/ppermute | solution.py:478
  38.5 4.8 %shard_map.147 = (bf16[256,1024]{1,0:T(8,128)(2,1)S(1)}, f32[256,1024]{1,0:T(8,128)S(1)}) custom-call(s32[3]{0:T(128)S(1)} %pad_add_fusion.place_ref, bf16[256,1024]{1,0:T(8,128)(2,1)} %collective-permute-done.4.first_mine, bf16[256,1024]{1,0:T(8,128)(2,1)} %collective-permute-done.5.second_mine, bf16[256,1024]{1,0:T(8,128)(2,1)S(1)} %collective-permute-done.6.first_theirs, ...), custom_call_target="tpu_custom_call" | custom-call | flops 33554432 | bytes 122880 | tf_op jit(solution)/shard_map/pallas_call | solution.py:294
  43.4 1.1 collective-permute-done.3.refs_5_
  44.4 3.4 %collective-permute-start.8 = (bf16[256,512]{1,0:T(8,128)(2,1)S(1)}, bf16[256,512]{1,0:T(8,128)(2,1)S(1)}, u32[]{:S(2)}, u32[]{:S(2)}) collective-permute-start(bf16[256,512]{1,0:T(8,128)(2,1)S(1)} %collective-permute-done.3.refs_5_), channel_id=1, source_target_pairs={{0,16},{16,24},{24,8},{8,0},{1,17},{17,25},{25,9},{9,1},{2,18},{18... | collective-permute-start | bytes 786440 | tf_op jit(solution)/shard_map/ppermute | solution.py:478
  48.6 4.0 %collective-permute-done.14.refs_2_ = bf16[1024,256]{1,0:T(8,128)(2,1)S(1)} collective-permute-done((bf16[1024,256]{1,0:T(8,128)(2,1)S(1)}, bf16[1024,256]{1,0:T(8,128)(2,1)S(1)}, u32[]{:S(2)}, u32[]{:S(2)}) %collective-permute-start.14) | collective-permute-done | bytes 524320 | tf_op jit(solution)/shard_map/ppermute | solution.py:503
  52.6 1.9 %collective-permute-done.8.refs_6_ = bf16[256,512]{1,0:T(8,128)(2,1)S(1)} collective-permute-done((bf16[256,512]{1,0:T(8,128)(2,1)S(1)}, bf16[256,512]{1,0:T(8,128)(2,1)S(1)}, u32[]{:S(2)}, u32[]{:S(2)}) %collective-permute-start.8) | collective-permute-done | bytes 262176 | tf_op jit(solution)/shard_map/ppermute | solution.py:478
  54.5 4.4 %collective-permute-done.9.refs_5_ = bf16[256,512]{1,0:T(8,128)(2,1)S(1)} collective-permute-done((bf16[256,512]{1,0:T(8,128)(2,1)S(1)}, bf16[256,512]{1,0:T(8,128)(2,1)S(1)}, u32[]{:S(2)}, u32[]{:S(2)}) %collective-permute-start.9) | collective-permute-done | bytes 262176 | tf_op jit(solution)/shard_map/ppermute | solution.py:478
  58.9 3.4 %collective-permute-start.11 = (bf16[256,512]{1,0:T(8,128)(2,1)S(1)}, bf16[256,512]{1,0:T(8,128)(2,1)}, u32[]{:S(2)}, u32[]{:S(2)}) collective-permute-start(bf16[256,512]{1,0:T(8,128)(2,1)S(1)} %collective-permute-done.9.refs_5_), channel_id=1, source_target_pairs={{0,16},{16,24},{24,8},{8,0},{1,17},{17,25},{25,9},{9,1},{2,18},{18... | collective-permute-start | bytes 786440 | tf_op jit(solution)/shard_map/ppermute | solution.py:478
  62.4 3.9 %shard_map.148 = (bf16[256,1024]{1,0:T(8,128)(2,1)}, bf16[256,1024]{1,0:T(8,128)(2,1)S(1)}, bf16[128,1024]{1,0:T(8,128)(2,1)}, bf16[64,1024]{1,0:T(8,128)(2,1)S(1)}, f32[64,1024]{1,0:T(8,128)S(1)}) custom-call(bf16[768,384]{1,0:T(8,128)(2,1)S(1)} %copy-done.3, bf16[768,384]{1,0:T(8,128)(2,1)S(1)} %copy-done.4, f32[256,1024]{1,0:T(8,128)S(1)} %get-tuple-element.72.refs_2_, ...), custom_call_target="tpu_custom_call" | custom-call | flops 20447232 | bytes 96320 | tf_op jit(solution)/shard_map/pallas_call | solution.py:275
  67.1 1.9 %collective-permute-done.11.refs_6_ = bf16[256,512]{1,0:T(8,128)(2,1)} collective-permute-done((bf16[256,512]{1,0:T(8,128)(2,1)S(1)}, bf16[256,512]{1,0:T(8,128)(2,1)}, u32[]{:S(2)}, u32[]{:S(2)}) %collective-permute-start.11) | collective-permute-done | bytes 262176 | tf_op jit(solution)/shard_map/ppermute | solution.py:478
  69.1 3.5 %collective-permute-start.19 = (bf16[256,512]{1,0:T(8,128)(2,1)}, bf16[256,512]{1,0:T(8,128)(2,1)}, u32[]{:S(2)}, u32[]{:S(2)}) collective-permute-start(bf16[256,512]{1,0:T(8,128)(2,1)} %collective-permute-done.11.refs_6_), channel_id=1, source_target_pairs={{0,16},{16,24},{24,8},{8,0},{1,17},{17,25},{25,9},{9,1},{2,18},{18... | collective-permute-start | bytes 786440 | tf_op jit(solution)/shard_map/ppermute | solution.py:478
  72.6 2.1 %collective-permute-done.16.refs_7_ = bf16[256,512]{1,0:T(8,128)(2,1)S(1)} collective-permute-done((bf16[256,512]{1,0:T(8,128)(2,1)S(1)}, bf16[256,512]{1,0:T(8,128)(2,1)S(1)}, u32[]{:S(2)}, u32[]{:S(2)}) %collective-permute-start.16) | collective-permute-done | bytes 262176 | tf_op jit(solution)/shard_map/ppermute | solution.py:478
  74.7 2.4 %shard_map.149 = (bf16[512,512]{1,0:T(8,128)(2,1)S(1)}, f32[512,512]{1,0:T(8,128)S(1)}) custom-call(s32[5]{0:T(128)S(1)} %pad_add_fusion.1.place_ref, bf16[1024,256]{1,0:T(8,128)(2,1)S(1)} %shard_map.146.refs_0_, bf16[1024,256]{1,0:T(8,128)(2,1)S(1)} %collective-permute-done.13.refs_1_, bf16[1024,256]{1,0:T(8,128)(2,1)S(1)} %collective-permute-done.14.refs_2_, ...), custom_call_target="tpu_custom_call" | custom-call | flops 16777216 | bytes 73728 | tf_op jit(solution)/shard_map/pallas_call | solution.py:294
  79.7 1.5 %collective-permute-start.17 = (bf16[128,1024]{1,0:T(8,128)(2,1)}, bf16[128,1024]{1,0:T(8,128)(2,1)}, u32[]{:S(2)}, u32[]{:S(2)}) collective-permute-start(bf16[128,1024]{1,0:T(8,128)(2,1)} %get-tuple-element.87), channel_id=1, source_target_pairs={{8,0},{16,8},{24,16},{9,1},{17,9},{25,17},{10,2},{18,10},{26,18},{... | collective-permute-start | bytes 786440 | tf_op jit(solution)/shard_map/ppermute | solution.py:557
  82.1 1.0 copy-done.7
  83.1 1.0 copy-done.9
  86.1 3.4 %shard_map.150 = (bf16[512,512]{1,0:T(8,128)(2,1)S(1)}, f32[512,512]{1,0:T(8,128)S(1)}) custom-call(s32[5]{0:T(128)S(1)} %pad_add_fusion.1.place_ref, bf16[1024,256]{1,0:T(8,128)(2,1)S(1)} %shard_map.146.refs_0_, bf16[1024,256]{1,0:T(8,128)(2,1)S(1)} %copy-done.7, bf16[1024,256]{1,0:T(8,128)(2,1)S(1)} %collective-permute-done.14.refs_2_, ...), custom_call_target="tpu_custom_call" | custom-call | flops 16777216 | bytes 73728 | tf_op jit(solution)/shard_map/pallas_call | solution.py:294
  89.5 1.2 %collective-permute-start.23 = (bf16[512,512]{1,0:T(8,128)(2,1)S(1)}, bf16[512,512]{1,0:T(8,128)(2,1)S(1)}, u32[]{:S(2)}, u32[]{:S(2)}) collective-permute-start(bf16[512,512]{1,0:T(8,128)(2,1)S(1)} %get-tuple-element.101), channel_id=1, source_target_pairs={{0,1},{1,0},{2,3},{3,2},{4,5},{5,4},{6,7},{7,6},{8,9},{9,8},{10,11... | collective-permute-start | bytes 1572872 | tf_op jit(solution)/shard_map/ppermute | solution.py:376
  90.7 1.0 add_convert_fusion
  91.7 4.1 %collective-permute-start.21 = (bf16[64,1024]{1,0:T(8,128)(2,1)S(1)}, bf16[64,1024]{1,0:T(8,128)(2,1)S(1)}, u32[]{:S(2)}, u32[]{:S(2)}) collective-permute-start(bf16[64,1024]{1,0:T(8,128)(2,1)S(1)} %add_convert_fusion), channel_id=1, source_target_pairs={{0,16},{8,24},{16,0},{24,8},{1,17},{9,25},{17,1},{25,9},{2,18},{10... | collective-permute-start | bytes 393224 | tf_op jit(solution)/shard_map/ppermute | solution.py:376
  95.8 4.8 %shard_map.151 = (bf16[256,1024]{1,0:T(8,128)(2,1)}, bf16[256,1024]{1,0:T(8,128)(2,1)}) custom-call(bf16[768,384]{1,0:T(8,128)(2,1)S(1)} %copy-done.3, bf16[768,384]{1,0:T(8,128)(2,1)S(1)} %copy-done.4, bf16[256,1024]{1,0:T(8,128)(2,1)S(1)} %copy-done.20, bf16[128,1024]{1,0:T(8,128)(2,1)} %collective-permute-done.17.refs_3_, ...), custom_call_target="tpu_custom_call" | custom-call | flops 5637144576 | bytes 49216 | tf_op jit(solution)/shard_map/pallas_call | solution.py:275
  101.8 3.8 %collective-permute-done.23 = bf16[512,512]{1,0:T(8,128)(2,1)S(1)} collective-permute-done((bf16[512,512]{1,0:T(8,128)(2,1)S(1)}, bf16[512,512]{1,0:T(8,128)(2,1)S(1)}, u32[]{:S(2)}, u32[]{:S(2)}) %collective-permute-start.23) | collective-permute-done | bytes 524320 | tf_op jit(solution)/shard_map/ppermute | solution.py:376
  105.8 1.5 %pad_maximum_fusion = f32[512,1024]{1,0:T(8,128)} fusion(f32[512,512]{1,0:T(8,128)S(1)} %add_multiply_fusion, f32[512,512]{1,0:T(8,128)S(1)} %add_multiply_fusion.1), kind=kLoop, calls=%fused_computation | loop fusion | flops 524288 | bytes 4194304 | tf_op jit(solution)/shard_map/concatenate | solution.py:582
  107.3 1.0 copy.16
  (83 shorter events, 11.7 us)
Async XLA Ops:
  0.6 19.0 %copy-start.3 = (bf16[768,384]{1,0:T(8,128)(2,1)S(1)}, bf16[768,384]{1,0:T(8,128)(2,1)}, u32[]{:S(2)}) copy-start(bf16[768,384]{1,0:T(8,128)(2,1)} %constant.66.clone.refs_0_) | copy-start | bytes 1769476
  0.6 18.9 %copy-start.4 = (bf16[768,384]{1,0:T(8,128)(2,1)S(1)}, bf16[768,384]{1,0:T(8,128)(2,1)}, u32[]{:S(2)}) copy-start(bf16[768,384]{1,0:T(8,128)(2,1)} %constant.67.clone.refs_1_) | copy-start | bytes 1769476
  0.7 18.9 %copy-start.1 = (bf16[1,256,1024]{2,1,0:T(8,128)(2,1)S(1)}, bf16[1,256,1024]{2,1,0:T(8,128)(2,1)}, u32[]{:S(2)}) copy-start(bf16[1,256,1024]{2,1,0:T(8,128)(2,1)} %param.12) | copy-start | bytes 1572868
  0.7 18.9 %copy-start.2 = (bf16[1,256,1024]{2,1,0:T(8,128)(2,1)S(1)}, bf16[1,256,1024]{2,1,0:T(8,128)(2,1)}, u32[]{:S(2)}) copy-start(bf16[1,256,1024]{2,1,0:T(8,128)(2,1)} %param.11) | copy-start | bytes 1572868
  0.7 18.9 %copy-start.12 = (bf16[1024,128]{1,0:T(8,128)(2,1)S(1)}, bf16[1024,128]{1,0:T(8,128)(2,1)}, u32[]{:S(2)}) copy-start(bf16[1024,128]{1,0:T(8,128)(2,1)} %refs_4_.1) | copy-start | bytes 786436
  0.7 18.9 %copy-start.18 = (f32[1024]{0:T(1024)S(1)}, f32[1024]{0:T(1024)}, u32[]{:S(2)}) copy-start(f32[1024]{0:T(1024)} %param.14) | copy-start | bytes 12292
  2.0 13.2 %collective-permute-start.1 = (bf16[256,1024]{1,0:T(8,128)(2,1)}, bf16[256,1024]{1,0:T(8,128)(2,1)S(1)}, u32[]{:S(2)}, u32[]{:S(2)}) collective-permute-start(bf16[256,1024]{1,0:T(8,128)(2,1)} %bitcast.29), channel_id=1, source_target_pairs={{2,4},{4,2},{8,14},{14,8},{18,20},{20,18},{24,30},{30,24},{3,5},{5... | collective-permute-start | bytes 1572872 | tf_op jit(solution)/shard_map/ppermute | solution.py:433
  2.7 12.5 %collective-permute-start = (bf16[128,1024]{1,0:T(8,128)(2,1)S(1)}, bf16[128,1024]{1,0:T(8,128)(2,1)S(1)}, u32[]{:S(2)}, u32[]{:S(2)}) collective-permute-start(bf16[128,1024]{1,0:T(8,128)(2,1)S(1)} %fusion), channel_id=1, source_target_pairs={{0,8},{8,16},{16,24},{1,9},{9,17},{17,25},{2,10},{10,18},{18,26},{... | collective-permute-start | bytes 786440 | tf_op jit(solution)/shard_map/ppermute | solution.py:411
  9.8 14.4 %collective-permute-start.4 = (bf16[256,1024]{1,0:T(8,128)(2,1)}, bf16[256,1024]{1,0:T(8,128)(2,1)}, u32[]{:S(2)}, u32[]{:S(2)}) collective-permute-start(bf16[256,1024]{1,0:T(8,128)(2,1)} %bitcast.30), channel_id=1, source_target_pairs={{0,0},{1,4},{2,2},{3,6},{4,1},{5,5},{6,3},{7,7},{8,8},{9,12},{10,1... | collective-permute-start | bytes 1572872 | tf_op jit(solution)/shard_map/ppermute | solution.py:420
  15.1 12.6 %collective-permute-start.5 = (bf16[256,1024]{1,0:T(8,128)(2,1)}, bf16[256,1024]{1,0:T(8,128)(2,1)}, u32[]{:S(2)}, u32[]{:S(2)}) collective-permute-start(bf16[256,1024]{1,0:T(8,128)(2,1)} %bitcast.31), channel_id=1, source_target_pairs={{0,4},{1,0},{2,6},{3,2},{4,5},{5,1},{6,7},{7,3},{8,12},{9,8},{10,1... | collective-permute-start | bytes 1572872 | tf_op jit(solution)/shard_map/ppermute | solution.py:420
  17.1 11.3 %collective-permute-start.2 = (bf16[256,1024]{1,0:T(8,128)(2,1)}, bf16[256,1024]{1,0:T(8,128)(2,1)S(1)}, u32[]{:S(2)}, u32[]{:S(2)}) collective-permute-start(bf16[256,1024]{1,0:T(8,128)(2,1)} %broadcast_select_fusion), channel_id=1, source_target_pairs={{0,0},{2,16},{4,12},{6,28},{8,24},{10,8},{12,20},{14,4},{16,2},{18... | collective-permute-start | bytes 1572872 | tf_op jit(solution)/shard_map/ppermute | solution.py:445
  20.7 17.8 %copy-start = (bf16[1024,2048]{1,0:T(8,128)(2,1)S(1)}, bf16[1024,2048]{1,0:T(8,128)(2,1)}, u32[]{:S(2)}) copy-start(bf16[1024,2048]{1,0:T(8,128)(2,1)} %weight.1) | copy-start | bytes 12582916
  24.1 24.5 %copy-start.14 = (bf16[256,512]{1,0:T(8,128)(2,1)}, bf16[256,512]{1,0:T(8,128)(2,1)S(1)}, u32[]{:S(2)}) copy-start(bf16[256,512]{1,0:T(8,128)(2,1)S(1)} %get-tuple-element.70.refs_4_) | copy-start | bytes 786436
  27.8 10.7 %collective-permute-start.6 = (bf16[256,1024]{1,0:T(8,128)(2,1)}, bf16[256,1024]{1,0:T(8,128)(2,1)S(1)}, u32[]{:S(2)}, u32[]{:S(2)}) collective-permute-start(bf16[256,1024]{1,0:T(8,128)(2,1)} %collective-permute-done.4.first_mine), channel_id=1, source_target_pairs={{0,2},{1,3},{2,0},{3,1},{4,6},{5,7},{6,4},{7,5},{8,10},{9,11},{10,... | collective-permute-start | bytes 1572872 | tf_op jit(solution)/shard_map/ppermute | solution.py:487
  28.3 10.2 %collective-permute-start.7 = (bf16[256,1024]{1,0:T(8,128)(2,1)}, bf16[256,1024]{1,0:T(8,128)(2,1)S(1)}, u32[]{:S(2)}, u32[]{:S(2)}) collective-permute-start(bf16[256,1024]{1,0:T(8,128)(2,1)} %collective-permute-done.5.second_mine), channel_id=1, source_target_pairs={{0,2},{1,3},{2,0},{3,1},{4,6},{5,7},{6,4},{7,5},{8,10},{9,11},{10,... | collective-permute-start | bytes 1572872 | tf_op jit(solution)/shard_map/ppermute | solution.py:487
  28.4 16.0 %collective-permute-start.3 = (bf16[256,512]{1,0:T(8,128)(2,1)S(1)}, bf16[256,512]{1,0:T(8,128)(2,1)S(1)}, u32[]{:S(2)}, u32[]{:S(2)}) collective-permute-start(bf16[256,512]{1,0:T(8,128)(2,1)S(1)} %get-tuple-element.58.refs_4_), channel_id=1, source_target_pairs={{0,16},{16,24},{24,8},{8,0},{1,17},{17,25},{25,9},{9,1},{2,18},{18... | collective-permute-start | bytes 786440 | tf_op jit(solution)/shard_map/ppermute | solution.py:478
  38.4 14.2 %collective-permute-start.14 = (bf16[1024,256]{1,0:T(8,128)(2,1)S(1)}, bf16[1024,256]{1,0:T(8,128)(2,1)S(1)}, u32[]{:S(2)}, u32[]{:S(2)}) collective-permute-start(bf16[1024,256]{1,0:T(8,128)(2,1)S(1)} %shard_map.146.refs_0_), channel_id=1, source_target_pairs={{0,4},{2,6},{4,0},{6,2},{1,5},{3,7},{5,1},{7,3},{8,12},{10,14},{12... | collective-permute-start | bytes 1572872 | tf_op jit(solution)/shard_map/ppermute | solution.py:503
  44.4 10.1 %collective-permute-start.8 = (bf16[256,512]{1,0:T(8,128)(2,1)S(1)}, bf16[256,512]{1,0:T(8,128)(2,1)S(1)}, u32[]{:S(2)}, u32[]{:S(2)}) collective-permute-start(bf16[256,512]{1,0:T(8,128)(2,1)S(1)} %collective-permute-done.3.refs_5_), channel_id=1, source_target_pairs={{0,16},{16,24},{24,8},{8,0},{1,17},{17,25},{25,9},{9,1},{2,18},{18... | collective-permute-start | bytes 786440 | tf_op jit(solution)/shard_map/ppermute | solution.py:478
  47.8 14.6 %collective-permute-start.10 = (bf16[256,1024]{1,0:T(8,128)(2,1)S(1)}, bf16[256,1024]{1,0:T(8,128)(2,1)S(1)}, u32[]{:S(2)}, u32[]{:S(2)}) collective-permute-start(bf16[256,1024]{1,0:T(8,128)(2,1)S(1)} %get-tuple-element.68), channel_id=1, source_target_pairs={{0,1},{1,0},{2,3},{3,2},{4,5},{5,4},{6,7},{7,6},{8,9},{9,8},{10,11... | collective-permute-start | bytes 1572872 | tf_op jit(solution)/shard_map/ppermute | solution.py:376
  48.6 10.3 %collective-permute-start.9 = (bf16[256,512]{1,0:T(8,128)(2,1)S(1)}, bf16[256,512]{1,0:T(8,128)(2,1)S(1)}, u32[]{:S(2)}, u32[]{:S(2)}) collective-permute-start(bf16[256,512]{1,0:T(8,128)(2,1)S(1)} %get-tuple-element.70.refs_4_), channel_id=1, source_target_pairs={{0,16},{16,24},{24,8},{8,0},{1,17},{17,25},{25,9},{9,1},{2,18},{18... | collective-permute-start | bytes 786440 | tf_op jit(solution)/shard_map/ppermute | solution.py:478
  48.6 23.9 %collective-permute-start.13 = (bf16[1024,256]{1,0:T(8,128)(2,1)S(1)}, bf16[1024,256]{1,0:T(8,128)(2,1)S(1)}, u32[]{:S(2)}, u32[]{:S(2)}) collective-permute-start(bf16[1024,256]{1,0:T(8,128)(2,1)S(1)} %shard_map.146.refs_0_), channel_id=1, source_target_pairs={{0,2},{2,0},{4,6},{6,4},{1,3},{3,1},{5,7},{7,5},{8,10},{10,8},{12,... | collective-permute-start | bytes 1572872 | tf_op jit(solution)/shard_map/ppermute | solution.py:503
  54.5 20.2 %collective-permute-start.15 = (bf16[1024,256]{1,0:T(8,128)(2,1)S(1)}, bf16[1024,256]{1,0:T(8,128)(2,1)S(1)}, u32[]{:S(2)}, u32[]{:S(2)}) collective-permute-start(bf16[1024,256]{1,0:T(8,128)(2,1)S(1)} %collective-permute-done.14.refs_2_), channel_id=1, source_target_pairs={{0,2},{2,0},{4,6},{6,4},{1,3},{3,1},{5,7},{7,5},{8,10},{10,8},{12,... | collective-permute-start | bytes 1572872 | tf_op jit(solution)/shard_map/ppermute | solution.py:503
  58.9 10.1 %collective-permute-start.11 = (bf16[256,512]{1,0:T(8,128)(2,1)S(1)}, bf16[256,512]{1,0:T(8,128)(2,1)}, u32[]{:S(2)}, u32[]{:S(2)}) collective-permute-start(bf16[256,512]{1,0:T(8,128)(2,1)S(1)} %collective-permute-done.9.refs_5_), channel_id=1, source_target_pairs={{0,16},{16,24},{24,8},{8,0},{1,17},{17,25},{25,9},{9,1},{2,18},{18... | collective-permute-start | bytes 786440 | tf_op jit(solution)/shard_map/ppermute | solution.py:478
  62.3 12.4 %collective-permute-start.16 = (bf16[256,512]{1,0:T(8,128)(2,1)S(1)}, bf16[256,512]{1,0:T(8,128)(2,1)S(1)}, u32[]{:S(2)}, u32[]{:S(2)}) collective-permute-start(bf16[256,512]{1,0:T(8,128)(2,1)S(1)} %collective-permute-done.8.refs_6_), channel_id=1, source_target_pairs={{0,16},{16,24},{24,8},{8,0},{1,17},{17,25},{25,9},{9,1},{2,18},{18... | collective-permute-start | bytes 786440 | tf_op jit(solution)/shard_map/ppermute | solution.py:478
  66.3 12.6 %collective-permute-start.12 = (bf16[64,1024]{1,0:T(8,128)(2,1)S(1)}, bf16[64,1024]{1,0:T(8,128)(2,1)S(1)}, u32[]{:S(2)}, u32[]{:S(2)}) collective-permute-start(bf16[64,1024]{1,0:T(8,128)(2,1)S(1)} %get-tuple-element.80), channel_id=1, source_target_pairs={{0,1},{1,0},{2,3},{3,2},{4,5},{5,4},{6,7},{7,6},{8,9},{9,8},{10,11... | collective-permute-start | bytes 393224 | tf_op jit(solution)/shard_map/ppermute | solution.py:376
  69.1 13.0 %collective-permute-start.19 = (bf16[256,512]{1,0:T(8,128)(2,1)}, bf16[256,512]{1,0:T(8,128)(2,1)}, u32[]{:S(2)}, u32[]{:S(2)}) collective-permute-start(bf16[256,512]{1,0:T(8,128)(2,1)} %collective-permute-done.11.refs_6_), channel_id=1, source_target_pairs={{0,16},{16,24},{24,8},{8,0},{1,17},{17,25},{25,9},{9,1},{2,18},{18... | collective-permute-start | bytes 786440 | tf_op jit(solution)/shard_map/ppermute | solution.py:478
  79.6 11.1 %collective-permute-start.18 = (bf16[64,1024]{1,0:T(8,128)(2,1)}, bf16[64,1024]{1,0:T(8,128)(2,1)}, u32[]{:S(2)}, u32[]{:S(2)}) collective-permute-start(bf16[64,1024]{1,0:T(8,128)(2,1)} %add_convert_fusion.1), channel_id=1, source_target_pairs={{0,8},{8,0},{16,24},{24,16},{1,9},{9,1},{17,25},{25,17},{2,10},{10... | collective-permute-start | bytes 393224 | tf_op jit(solution)/shard_map/ppermute | solution.py:376
  79.7 16.1 %collective-permute-start.17 = (bf16[128,1024]{1,0:T(8,128)(2,1)}, bf16[128,1024]{1,0:T(8,128)(2,1)}, u32[]{:S(2)}, u32[]{:S(2)}) collective-permute-start(bf16[128,1024]{1,0:T(8,128)(2,1)} %get-tuple-element.87), channel_id=1, source_target_pairs={{8,0},{16,8},{24,16},{9,1},{17,9},{25,17},{10,2},{18,10},{26,18},{... | collective-permute-start | bytes 786440 | tf_op jit(solution)/shard_map/ppermute | solution.py:557
  81.2 19.5 %collective-permute-start.20 = (bf16[512,512]{1,0:T(8,128)(2,1)}, bf16[512,512]{1,0:T(8,128)(2,1)S(1)}, u32[]{:S(2)}, u32[]{:S(2)}) collective-permute-start(bf16[512,512]{1,0:T(8,128)(2,1)} %copy-done.21), channel_id=1, source_target_pairs={{0,1},{1,0},{2,3},{3,2},{4,5},{5,4},{6,7},{7,6},{8,9},{9,8},{10,11... | collective-permute-start | bytes 1572872 | tf_op jit(solution)/shard_map/ppermute | solution.py:376
  89.5 16.1 %collective-permute-start.23 = (bf16[512,512]{1,0:T(8,128)(2,1)S(1)}, bf16[512,512]{1,0:T(8,128)(2,1)S(1)}, u32[]{:S(2)}, u32[]{:S(2)}) collective-permute-start(bf16[512,512]{1,0:T(8,128)(2,1)S(1)} %get-tuple-element.101), channel_id=1, source_target_pairs={{0,1},{1,0},{2,3},{3,2},{4,5},{5,4},{6,7},{7,6},{8,9},{9,8},{10,11... | collective-permute-start | bytes 1572872 | tf_op jit(solution)/shard_map/ppermute | solution.py:376
  91.7 8.9 %collective-permute-start.21 = (bf16[64,1024]{1,0:T(8,128)(2,1)S(1)}, bf16[64,1024]{1,0:T(8,128)(2,1)S(1)}, u32[]{:S(2)}, u32[]{:S(2)}) collective-permute-start(bf16[64,1024]{1,0:T(8,128)(2,1)S(1)} %add_convert_fusion), channel_id=1, source_target_pairs={{0,16},{8,24},{16,0},{24,8},{1,17},{9,25},{17,1},{25,9},{2,18},{10... | collective-permute-start | bytes 393224 | tf_op jit(solution)/shard_map/ppermute | solution.py:376
  100.7 6.5 %collective-permute-start.22 = (bf16[64,1024]{1,0:T(8,128)(2,1)S(1)}, bf16[64,1024]{1,0:T(8,128)(2,1)S(1)}, u32[]{:S(2)}, u32[]{:S(2)}) collective-permute-start(bf16[64,1024]{1,0:T(8,128)(2,1)S(1)} %convert_add_fusion), channel_id=1, source_target_pairs={{0,1},{1,0},{2,3},{3,2},{4,5},{5,4},{6,7},{7,6},{8,9},{9,8},{10,11... | collective-permute-start | bytes 393224 | tf_op jit(solution)/shard_map/ppermute | solution.py:376
  (14 other events, 67.2 us)
